TPU v7x, 32 devices: a whole 2x2x4 slice. The times are simulated.
32 devices in a mesh: grp: 4 (over y, x), ray: 8 (over z, core).
Axes of the slice: x: 2, y: 2, z: 4, core: 2. Of those that a mesh axis runs over, the one named last changes fastest.
Arguments:
- image_tokens: bfloat16 [16384, 1024], P(('grp', 'ray')), may hold values from -6 to 6
- tile_lists: int32 [32, 16384], P(None, ('grp', 'ray')), may hold values from 0 to 8191, as said below
- opacity: float32 [32, 16384], P(None, ('grp', 'ray')), may hold values from 0.02 to 0.5
- tile_counts: int32 [16384], P(('grp', 'ray')), may hold values from 1 to 32, as said below
- ray_pixel: int32 [4, 4096], P('grp'), may hold values from 0 to 4095, as said below
- block_owner: int32 [4, 8], P('grp'), may hold values from 0 to 7, each once within a row
- gaussian_features: bfloat16 [32768, 1024], P(('grp', 'ray')), may hold values from -6 to 6
- layer_norm_gain: float32 [1024], replicated, may hold values from 0.5 to 1.5
- layer_scale: float32 [1024], replicated, may hold values from 0.25 to 1
- up_weight: bfloat16 [1024, 2048], P(None, 'ray'), may hold values from -0.1875 to 0.1875
- down_weight: bfloat16 [2048, 1024], P('ray'), may hold values from -0.125 to 0.125
Outputs:
- grad_up: float32 [1024, 2048], P(None, 'ray')
- grad_down: float32 [2048, 1024], P('ray')
- gain_gradient: float32 [1024], replicated
- grad_scale: float32 [1024], replicated
- loss: float32 [], replicated
Inputs may be any that keep to these rules, and one draw needn't show every extreme that they name: `tile_lists`: A ray's entries name Gaussians of the block of 1024 rows of gaussian_features that is held by the same device as the ray. `tile_counts`: in each group some device holds a ray with 32 live entries. `ray_pixel`: each group's row is a permutation of its pixels, and the 512 rays of each device name exactly 64 pixels of each block of 512 consecutive pixels. `block_owner`: each group's row is a permutation.
All inputs are finite; a program needn't handle non-finite values.
Results may differ from a plain program's by a relative error of at most 0.0068.
Values may be sent and summed in bfloat16 or wider, within the bound.
No kernel may reach another device: no remote copies, remote signals or barrier semaphores. Data moves between devices by JAX's collectives and lax.ppermute only.
A program may use at most 128 MiB of HBM per device.

v0:
```python
import jax
import jax.numpy as jnp
from jax import lax
from jax.sharding import PartitionSpec as P

STABILITY_EPSILON = 1e-06


def weights_for(ids_local, alphas, counts, width, depth):
    columns = jnp.arange(width, dtype=jnp.int32)

    def advance(level, carry):
        table, passing = carry
        alpha_now = lax.dynamic_index_in_dim(alphas, level, 0, keepdims=False)
        ident = lax.dynamic_index_in_dim(ids_local, level, 0, keepdims=False)
        live = jnp.where(level < counts, jnp.float32(1.0), jnp.float32(0.0))
        share = alpha_now * passing * live
        table = table + jnp.where(
            ident[:, None] == columns[None, :], share[:, None], jnp.float32(0.0)
        )
        return (table, passing * (1.0 - alpha_now))

    rays_here = ids_local.shape[1]
    start = (jnp.zeros((rays_here, width), jnp.float32), jnp.ones((rays_here,), jnp.float32))
    table, passing = lax.fori_loop(0, depth, advance, start)
    return table


def lookup(blocks, owner, count):
    slots = jnp.arange(count, dtype=jnp.int32)
    return jnp.sum(jnp.where(blocks[..., None] == slots, owner, 0), axis=-1)


def layer_pieces(tokens, target, layer_norm_gain, layer_scale, full_up, full_down):
    values = tokens.astype(jnp.float32)
    centered_input = values - jnp.mean(values, axis=-1, keepdims=True)
    row_variance = jnp.mean(centered_input * centered_input, axis=-1, keepdims=True)
    standardized_input = centered_input * lax.rsqrt(row_variance + STABILITY_EPSILON)
    normalized_rows = (standardized_input * layer_norm_gain).astype(jnp.bfloat16)
    hidden = jnp.dot(normalized_rows, full_up, preferred_element_type=jnp.float32)
    act = jax.nn.gelu(hidden, approximate=False).astype(jnp.bfloat16)
    mixed = jnp.dot(act, full_down, preferred_element_type=jnp.float32)
    layer_out = values + layer_scale * mixed
    goal = target.astype(jnp.float32)
    out_norm = jnp.sqrt(jnp.sum(layer_out * layer_out, axis=-1, keepdims=True) + STABILITY_EPSILON)
    goal_norm = jnp.sqrt(jnp.sum(goal * goal, axis=-1, keepdims=True) + STABILITY_EPSILON)
    cosine = jnp.sum(layer_out * goal, axis=-1, keepdims=True) / (out_norm * goal_norm)
    loss_sum = jnp.sum(1.0 - cosine)
    upstream = -(goal / (out_norm * goal_norm) - cosine * layer_out / (out_norm * out_norm))
    grad_scale = jnp.sum(upstream * mixed, axis=0)
    back_mixed = (upstream * layer_scale).astype(jnp.bfloat16)
    back_act = jnp.dot(back_mixed, full_down.T, preferred_element_type=jnp.float32)
    slope = 0.5 * (1.0 + lax.erf(hidden / jnp.sqrt(2.0))) + hidden * jnp.exp(
        -0.5 * hidden * hidden
    ) / jnp.sqrt(2.0 * jnp.pi)
    back_hidden = (back_act * slope).astype(jnp.bfloat16)
    normalized_gradient = jnp.dot(back_hidden, full_up.T, preferred_element_type=jnp.float32)
    gain_gradient = jnp.sum(normalized_gradient * standardized_input, axis=0)
    return (normalized_rows, act, back_mixed, back_hidden, gain_gradient, grad_scale, loss_sum)


def shards(
    image_tokens,
    tile_lists,
    opacity,
    tile_counts,
    ray_pixel,
    block_owner,
    gaussian_features,
    layer_norm_gain,
    layer_scale,
    up_weight,
    down_weight,
):
    ray_count = lax.axis_size("ray")
    group_count = lax.axis_size("grp")
    my_index = lax.axis_index("ray")
    row_count = image_tokens.shape[0]
    gauss_count = gaussian_features.shape[0]
    each_pair = row_count // ray_count
    pixels = ray_pixel[0].reshape(ray_count, row_count)
    owners = lookup(pixels // row_count, block_owner[0], ray_count)
    my_owners = lax.dynamic_index_in_dim(owners, my_index, 0, keepdims=False)
    order = jnp.argsort(my_owners, stable=True)
    lists_sorted = tile_lists[:, order] - my_index * gauss_count
    alphas_sorted = opacity[:, order]
    counts_sorted = tile_counts[order]
    depth = tile_lists.shape[0]
    table = weights_for(lists_sorted, alphas_sorted, counts_sorted, gauss_count, depth).astype(
        jnp.bfloat16
    )
    rendered = jnp.dot(table, gaussian_features, preferred_element_type=jnp.float32).astype(
        jnp.bfloat16
    )
    arrived = lax.all_to_all(rendered, "ray", split_axis=0, concat_axis=0, tiled=True)
    rank_keys = jnp.where(owners == my_index, 0, 1)
    chosen = jnp.argsort(rank_keys, axis=1, stable=True)[:, :each_pair]
    places = (jnp.take_along_axis(pixels, chosen, axis=1) % row_count).reshape(row_count)
    target = jnp.zeros_like(arrived).at[places].set(arrived)
    full_up, full_down = (
        lax.all_gather(up_weight, "ray", axis=1, tiled=True),
        lax.all_gather(down_weight, "ray", axis=0, tiled=True),
    )
    normalized_rows, act, back_mixed, back_hidden, gain_part, scale_part, loss_part = layer_pieces(
        image_tokens, target, layer_norm_gain, layer_scale, full_up, full_down
    )
    grad_up_local = jnp.dot(normalized_rows.T, back_hidden, preferred_element_type=jnp.float32)
    grad_down_local = jnp.dot(act.T, back_mixed, preferred_element_type=jnp.float32)
    shares = (
        lax.psum_scatter(grad_up_local, "ray", scatter_dimension=1, tiled=True),
        lax.psum_scatter(grad_down_local, "ray", scatter_dimension=0, tiled=True),
    )
    grad_up, grad_down = lax.psum((shares[0], shares[1]), "grp")
    gain_gradient, grad_scale, loss_total = lax.psum(
        (gain_part, scale_part, loss_part), ("grp", "ray")
    )
    loss = loss_total / (row_count * ray_count * group_count)
    return (grad_up, grad_down, gain_gradient, grad_scale, loss)


def solution(mesh):
    return jax.shard_map(
        shards,
        mesh=mesh,
        in_specs=(
            P(("grp", "ray"), None),
            P(None, ("grp", "ray")),
            P(None, ("grp", "ray")),
            P(("grp", "ray")),
            P("grp", None),
            P("grp", None),
            P(("grp", "ray"), None),
            P(),
            P(),
            P(None, "ray"),
            P("ray", None),
        ),
        out_specs=(P(None, "ray"), P("ray", None), P(), P(), P()),
        check_vma=False,
    )
```

profile of v0, /device:TPU:8, one launch (start us, length us, event | category | flops | bytes accessed | tf_op | source)
XLA Modules:
  0.0 464.9 jit_solution(14324645453346747325)
XLA Ops:
  13.3 3.8 sort.35
  18.1 3.6 gather_fusion.2
  24.1 106.2 %while.16 = (s32[]{:T(128)}, f32[512,1024]{1,0:T(8,128)}, f32[512]{0:T(512)S(1)}, s32[32,512]{1,0:T(8,128)S(1)}, f32[32,512]{1,0:T(8,128)S(1)}, /*index=5*/s32[512]{0:T(512)S(1)}, s32[]{:T(128)}, s32[]{:T(128)}) while((s32[]{:T(128)}, f32[512,1024]{1,0:T(8,128)}, f32[512]{0:T(512)S(1)}, s32[32,512]{1,0:T(8,128)S(1)}, ...), condition=%wide.region_6.7_spmd.clone, body=%wide.region_5.6_spmd.clone.sunk | while | flops 2100739 | bytes 4216948 | solution.py:25
  26.0 3.3 select_add_fusion.2
  29.3 3.3 select_add_fusion.2
  32.7 3.4 select_add_fusion.2
  36.1 3.4 select_add_fusion.2
  39.6 3.3 select_add_fusion.2
  42.9 3.3 select_add_fusion.2
  46.2 3.4 select_add_fusion.2
  49.7 3.3 select_add_fusion.2
  59.8 3.4 select_add_fusion.2
  69.8 3.4 select_add_fusion.2
  76.7 3.3 select_add_fusion.2
  90.1 3.4 select_add_fusion.2
  93.5 3.3 select_add_fusion.2
  106.9 3.4 select_add_fusion.2
  130.3 3.9 convolution_convert_fusion
  134.2 5.2 %all-to-all-start = ((bf16[8,64,1024]{2,1,0:T(8,128)(2,1)}), bf16[8,64,1024]{2,1,0:T(8,128)(2,1)}, u32[]{:S(2)}, u32[]{:S(2)}) async-start(bf16[8,64,1024]{2,1,0:T(8,128)(2,1)} %bitcast.28), calls=%async_computation | async-start | bytes 2097152 | tf_op jit(solution)/shard_map/all_to_all | solution.py:95
  140.9 3.6 gather_fusion.3
  145.3 17.2 %all-to-all-done = bf16[8,64,1024]{2,1,0:T(8,128)(2,1)} async-done(((bf16[8,64,1024]{2,1,0:T(8,128)(2,1)}), bf16[8,64,1024]{2,1,0:T(8,128)(2,1)}, u32[]{:S(2)}, u32[]{:S(2)}) %all-to-all-start) | async-done | bytes 1048608 | tf_op jit(solution)/shard_map/all_to_all | solution.py:95
  162.6 4.2 scatter_custom_fusion
  166.8 14.3 %fusion.4 = (bf16[512,2048]{1,0:T(8,128)(2,1)}, f32[512,2048]{1,0:T(8,128)}) fusion(bf16[1024,2048]{1,0:T(8,128)(2,1)} %all-gather.3.cloned.1.call-done, bf16[512,1024]{1,0:T(8,128)(2,1)S(1)} %copy-done.1, f32[1024]{0:T(1024)S(1)} %copy-done.7, f32[512]{0:T(512)S(1)} %add_rsqrt_fusion, f32[512]{0:T(512)S(1)} %broadcast_multiply_fusion), kind=kOutput, calls=%fused_computation.16 | convolution fusion | flops 2218262528 | bytes 11542528 | tf_op jit(solution)/shard_map/dot_general | solution.py:40
  181.1 6.0 %fusion.28 = (f32[512]{0:T(512)S(1)}, f32[512]{0:T(512)S(1)}, f32[512]{0:T(512)S(1)}, f32[512,1024]{1,0:T(8,128)S(1)}) fusion(bf16[512,1024]{1,0:T(8,128)(2,1)} %scatter_custom_fusion, f32[1024]{0:T(1024)S(1)} %copy-done.5, bf16[512,1024]{1,0:T(8,128)(2,1)S(1)} %copy-done.1, bf16[512,2048]{1,0:T(8,128)(2,1)} %get-tuple-element.203, ...), kind=kOutput, calls=%fused_computation.54 | convolution fusion | flops 2152724992 | bytes 10496000 | tf_op jit(solution)/shard_map/dot_general | solution.py:42
  189.3 4.0 fusion.10
  194.7 5.8 %fusion.37 = f32[1024,2048]{1,0:T(8,128)} fusion(bf16[512,2048]{1,0:T(8,128)(2,1)S(1)} %fusion.10, bf16[512,1024]{1,0:T(8,128)(2,1)S(1)} %copy-done.1, f32[1024]{0:T(1024)S(1)} %copy-done.7, f32[512]{0:T(512)S(1)} %add_rsqrt_fusion, f32[512]{0:T(512)S(1)} %broadcast_multiply_fusion), kind=kOutput, calls=%fused_computation.91 | convolution fusion | flops 2150105088 | bytes 11542528 | tf_op jit(solution)/shard_map/dot_general | solution.py:107
  200.8 7.8 %fusion.32 = f32[2048,1024]{1,0:T(8,128)} fusion(bf16[512,2048]{1,0:T(8,128)(2,1)} %get-tuple-element.203, f32[512,1024]{1,0:T(8,128)} %copy-done.2, f32[1024]{0:T(1024)S(1)} %copy-done.5), kind=kOutput, calls=%fused_computation.62 | convolution fusion | flops 2148532224 | bytes 12587008 | tf_op jit(solution)/shard_map/dot_general | solution.py:108
  208.7 80.4 %reduce-scatter.3.cloned.1.call-done = f32[1024,256]{1,0:T(8,128)} async-done(((f32[1024,2048]{1,0:T(8,128)}), f32[1024,256]{1,0:T(8,128)}) %reduce-scatter.3.cloned.1.call-update) | async-done | bytes 1048592 | tf_op jit(solution)/shard_map/reduce_scatter | solution.py:110
  289.1 90.2 %reduce-scatter.5.cloned.1.call-done = f32[256,1024]{1,0:T(8,128)} async-done(((f32[2048,1024]{1,0:T(8,128)}), f32[256,1024]{1,0:T(8,128)}) %reduce-scatter.5.cloned.1.call-update) | async-done | bytes 1048592 | tf_op jit(solution)/shard_map/reduce_scatter | solution.py:111
  379.4 5.2 %fusion.23 = f32[1024]{0:T(1024)S(1)} fusion(bf16[512,1024]{1,0:T(8,128)(2,1)S(1)} %copy-done.1, bf16[512,2048]{1,0:T(8,128)(2,1)} %copy-done.8, bf16[1024,2048]{1,0:T(8,128)(2,1)} %all-gather.3.cloned.1.call-done, f32[512]{0:T(512)S(1)} %add_rsqrt_fusion, f32[512]{0:T(512)S(1)} %broadcast_multiply_fusion), kind=kOutput, calls=%fused_computation.49 | convolution fusion | flops 2150104064 | bytes 7348224 | tf_op jit(solution)/shard_map/dot_general | solution.py:57
  384.6 42.4 %all-reduce = (f32[1024]{0:T(1024)}, f32[1024]{0:T(1024)}, f32[]{:T(128)}) all-reduce(f32[1024]{0:T(1024)S(1)} %fusion.23, f32[1024]{0:T(1024)S(1)} %get-tuple-element.198, f32[]{:T(128)} %get-tuple-element.195), channel_id=1, replica_groups=mesh['grp'=4,'ray'=8] {'grp','ray'}, use_global_device_ids=true, to_apply=%region_16.17 | all-reduce | flops 2049 | bytes 16392 | tf_op jit(solution)/shard_map/psum | solution.py:114
  427.6 24.0 %all-reduce.4.cloned.1.call-done = (f32[1024,256]{1,0:T(8,128)}, f32[256,1024]{1,0:T(8,128)}) async-done(((f32[1024,256]{1,0:T(8,128)}, f32[256,1024]{1,0:T(8,128)}), (f32[1024,256]{1,0:T(8,128)}, f32[256,1024]{1,0:T(8,128)})) %all-reduce.4.cloned.1.call-update) | async-done | bytes 2097168 | tf_op jit(solution)/shard_map/psum | solution.py:113
  (183 shorter events, 78.1 us)
Async XLA Ops:
  8.0 122.3 %copy-start = (bf16[1024,1024]{1,0:T(8,128)(2,1)S(1)}, bf16[1024,1024]{1,0:T(8,128)(2,1)}, u32[]{:S(2)}) copy-start(bf16[1024,1024]{1,0:T(8,128)(2,1)} %param.19) | copy-start | bytes 6291460
  8.0 14.8 %copy-start.4 = (f32[32,512]{1,0:T(8,128)S(1)}, f32[32,512]{1,0:T(8,128)}, u32[]{:S(2)}) copy-start(f32[32,512]{1,0:T(8,128)} %param.15) | copy-start | bytes 196612
  8.0 132.1 %sort.37.cloned.1.call-start = ((), (), s32[]{:S(2)}) async-start(), calls=%async_computation.8 | async-start | bytes 98336 | tf_op jit(solution)/shard_map/jit(argsort)/sort | solution.py:97
  12.1 154.7 %all-gather.3.cloned.1.call-start = ((), (), s32[]{:S(2)}) async-start(), calls=%async_computation.3 | async-start | bytes 4718592 | tf_op jit(solution)/shard_map/all_gather | solution.py:101
  12.7 168.4 %all-gather.5.cloned.1.call-start = ((), (), s32[]{:S(2)}) async-start(), calls=%async_computation.4 | async-start | bytes 4718592 | tf_op jit(solution)/shard_map/all_gather | solution.py:102
  130.3 9.1 %copy-start.1 = (bf16[512,1024]{1,0:T(8,128)(2,1)S(1)}, bf16[512,1024]{1,0:T(8,128)(2,1)}, u32[]{:S(2)}) copy-start(bf16[512,1024]{1,0:T(8,128)(2,1)} %param.13) | copy-start | bytes 3145732
  134.2 28.4 %all-to-all-start = ((bf16[8,64,1024]{2,1,0:T(8,128)(2,1)}), bf16[8,64,1024]{2,1,0:T(8,128)(2,1)}, u32[]{:S(2)}, u32[]{:S(2)}) async-start(bf16[8,64,1024]{2,1,0:T(8,128)(2,1)} %bitcast.28), calls=%async_computation | async-start | bytes 2097152 | tf_op jit(solution)/shard_map/all_to_all | solution.py:95
  139.4 27.3 %copy-start.7 = (f32[1024]{0:T(1024)S(1)}, f32[1024]{0:T(1024)}, u32[]{:S(2)}) copy-start(f32[1024]{0:T(1024)} %param.20) | copy-start | bytes 12292
  139.4 149.7 %reduce-scatter.3.cloned.1.call-start = ((), (), s32[]{:S(2)}) async-start(), calls=%async_computation.5 | async-start | bytes 9437184 | tf_op jit(solution)/shard_map/reduce_scatter | solution.py:110
  166.8 14.3 %copy-start.5 = (f32[1024]{0:T(1024)S(1)}, f32[1024]{0:T(1024)}, u32[]{:S(2)}) copy-start(f32[1024]{0:T(1024)} %param.21) | copy-start | bytes 12292
  181.1 6.7 %copy-start.3 = (bf16[512,1024]{1,0:T(8,128)(2,1)S(1)}, bf16[512,1024]{1,0:T(8,128)(2,1)}, u32[]{:S(2)}) copy-start(bf16[512,1024]{1,0:T(8,128)(2,1)} %scatter_custom_fusion) | copy-start | bytes 3145732
  181.1 7.6 %copy-start.9 = (f32[512,2048]{1,0:T(8,128)S(1)}, f32[512,2048]{1,0:T(8,128)}, u32[]{:S(2)}) copy-start(f32[512,2048]{1,0:T(8,128)} %get-tuple-element.204) | copy-start | bytes 12582916
  187.1 2.2 copy-start.6
  188.6 4.8 %copy-start.2 = (f32[512,1024]{1,0:T(8,128)}, f32[512,1024]{1,0:T(8,128)S(1)}, u32[]{:S(2)}) copy-start(f32[512,1024]{1,0:T(8,128)S(1)} %get-tuple-element.199) | copy-start | bytes 6291460
  193.4 1.3 copy-start.8
  200.6 178.8 %reduce-scatter.5.cloned.1.call-start = ((), (), s32[]{:S(2)}) async-start(), calls=%async_computation.6 | async-start | bytes 9437184 | tf_op jit(solution)/shard_map/reduce_scatter | solution.py:111
  208.7 242.9 %all-reduce.4.cloned.1.call-start = ((), (), s32[]{:S(2)}) async-start(), calls=%async_computation.7 | async-start | bytes 4194304 | tf_op jit(solution)/shard_map/psum | solution.py:113
Sparse Core Ops, SparseCore 0:
  12.2 2.4 sort.39.cloned.1.call-done
  379.5 72.0 all-reduce.3
  (1 shorter events, 0.0 us)
Sparse Core Ops, SparseCore 1:
  14.1 47.4 all-gather.2
  63.1 45.1 all-gather.4
  200.6 88.4 reduce-scatter.2
  291.5 87.8 reduce-scatter.4
where the time goes:
time: 468 us; the launch traced here: 465 us
  waiting for transfers between devices  213 us (46%)
  other arithmetic  116 us (25%)
  matrix products  47.1 us (10%)
  blocking collectives  42.4 us (9%)
  local copies, waits for them, and re-layouts  23.2 us (5%)
  between operations  17.7 us (4%)
  starting transfers between devices  5.63 us (1%)
    add x32, other arithmetic, advance(): table + jnp.where(ident[:, None] == columns[None, :], share[:, None], jnp...  105 us
    reduce_scatter x1, waiting for transfers between devices, shards(): lax.psum_scatter(grad_down_local, 'ray', scatter_dimension=0, tiled=True)  90.2 us
    reduce_scatter x1, waiting for transfers between devices, shards(): lax.psum_scatter(grad_up_local, 'ray', scatter_dimension=1, tiled=True)  80.4 us
    psum x1, blocking collectives, shards(): lax.psum((gain_part, scale_part, loss_part), ('grp', 'ray'))  42.4 us
    psum x1, waiting for transfers between devices, shards(): grad_up, grad_down = lax.psum((shares[0], shares[1]), 'grp')  24 us
    all_to_all x1, waiting for transfers between devices, shards(): lax.all_to_all(rendered, 'ray', split_axis=0, concat_axis=0, tiled=True)  17.2 us
    dot_general x1, matrix products, layer_pieces(): jnp.dot(normalized_rows, full_up, preferred_element_type=jnp.float32)  14.3 us
  transfers between devices with their start and end apart: 6, of which 4 were waited for; matrix products, arithmetic and copies ran while one was open for 34% of the time, Pallas kernels for 0%

commit v1 on v0

v1 whole, which is shorter than its diff:
```python
import functools

import jax
import jax.numpy as jnp
from jax import lax
from jax.experimental import pallas as pl
from jax.experimental.pallas import tpu as pltpu
from jax.sharding import PartitionSpec as P

STABILITY_EPSILON = 1e-06
F32 = jnp.float32
BF16 = jnp.bfloat16
VMEM_BYTES = 56 * 1024 * 1024
SMEM = pl.BlockSpec(memory_space=pltpu.SMEM)
VMEM = pl.BlockSpec(memory_space=pltpu.VMEM)


def params(**more):
    return pltpu.CompilerParams(vmem_limit_bytes=VMEM_BYTES, **more)


def dot_nn(a, b):
    return lax.dot_general(a, b, (((1,), (0,)), ((), ())), preferred_element_type=F32)


def dot_tn(a, b):
    return lax.dot_general(a, b, (((0,), (0,)), ((), ())), preferred_element_type=F32)


def dot_nt(a, b):
    return lax.dot_general(a, b, (((1,), (1,)), ((), ())), preferred_element_type=F32)


def owner_of(pixels, owner_ref, rows, count):
    block = lax.div(pixels, jnp.int32(rows))
    owner = jnp.zeros_like(pixels)
    for slot in range(count):
        owner = jnp.where(block == slot, owner_ref[0, slot], owner)
    return owner


def earlier(rows):
    before = lax.broadcasted_iota(jnp.int32, (rows, rows), 0)
    after = lax.broadcasted_iota(jnp.int32, (rows, rows), 1)
    return jnp.where(before < after, 1.0, 0.0).astype(BF16)


def render_kernel(
    ray_count, me_ref, owner_ref, lists_ref, opacity_ref, counts_ref, pixels_ref, features_ref,
    out_ref, ids_ref, share_ref, table_ref, send_ref,
):
    depth, rays = lists_ref.shape
    gauss = features_ref.shape[0]
    width = features_ref.shape[1]
    me = me_ref[0]
    ids_ref[...] = lists_ref[...] - me * gauss
    passing = jnp.ones((1, rays), F32)
    counts = counts_ref[...]
    for level in range(depth):
        alpha = opacity_ref[pl.ds(level, 1), :]
        share_ref[pl.ds(level, 1), :] = jnp.where(level < counts, alpha * passing, 0.0)
        passing = passing * (1.0 - alpha)

    tile = 128
    lanes = 128
    columns = rays // lanes

    @pl.loop(0, (gauss // tile) * columns)
    def _(step):
        first = pl.multiple_of(lax.div(step, columns) * tile, tile)
        lane = pl.multiple_of(lax.rem(step, columns) * lanes, lanes)
        number = lax.broadcasted_iota(jnp.int32, (tile, lanes), 0) + first
        total = jnp.zeros((tile, lanes), F32)
        for level in range(depth):
            ident = ids_ref[pl.ds(level, 1), pl.ds(lane, lanes)]
            share = share_ref[pl.ds(level, 1), pl.ds(lane, lanes)]
            total = total + jnp.where(ident == number, share, 0.0)
        table_ref[pl.ds(first, tile), pl.ds(lane, lanes)] = total.astype(BF16)

    mine = pixels_ref[pl.ds(me, 1), :]
    owner = owner_of(mine, owner_ref, rays, ray_count)
    padded = -(-ray_count // 16) * 16
    member = (lax.broadcasted_iota(jnp.int32, (padded, rays), 0) == owner)
    ranks = dot_nn(member.astype(F32).astype(BF16), earlier(rays))
    rank = jnp.sum(jnp.where(member, ranks, 0.0), axis=0, keepdims=True).astype(jnp.int32)
    slot = owner * (rays // ray_count) + rank
    send_ref[...] = (
        (lax.broadcasted_iota(jnp.int32, (rays, rays), 0) == slot).astype(F32).astype(BF16)
    )

    piece = 256

    @pl.loop(0, width // piece)
    def _(step):
        cols = pl.ds(pl.multiple_of(step * piece, piece), piece)
        rendered = dot_tn(table_ref[...], features_ref[:, cols]).astype(BF16)
        out_ref[:, cols] = dot_nn(send_ref[...], rendered).astype(BF16)


def render(me, owner, lists, opacity, counts, pixels, features):
    ray_count = pixels.shape[0]
    depth, rays = lists.shape
    gauss, width = features.shape
    return pl.pallas_call(
        functools.partial(render_kernel, ray_count),
        out_shape=jax.ShapeDtypeStruct((rays, width), BF16),
        in_specs=[SMEM, SMEM, VMEM, VMEM, VMEM, VMEM, VMEM],
        out_specs=VMEM,
        scratch_shapes=[
            pltpu.VMEM((depth, rays), jnp.int32),
            pltpu.VMEM((depth, rays), F32),
            pltpu.VMEM((gauss, rays), BF16),
            pltpu.VMEM((rays, rays), BF16),
        ],
        compiler_params=params(),
        cost_estimate=pl.CostEstimate(
            flops=2 * rays * width * (gauss + rays) + 3 * depth * rays * gauss * 40,
            bytes_accessed=2 * (gauss + rays) * width, transcendentals=0,
        ),
        name="render",
    )(me, owner, lists, opacity, counts, pixels, features)


def tokens_kernel(
    ray_count, me_ref, owner_ref, pixels_ref, tokens_ref, gain_ref,
    tokens_out, normed_out, normed_t_out, place_ref,
):
    rows, width = tokens_ref.shape
    me = me_ref[0]
    each = rows // ray_count
    pixels = pixels_ref[...]
    mine = owner_of(pixels, owner_ref, rows, ray_count) == me
    place = lax.rem(pixels, jnp.int32(rows)).astype(F32)
    member = jnp.where(mine, 1.0, 0.0)
    padded = -(-ray_count // 16) * 16
    if padded > ray_count:
        spread = jnp.concatenate([member, jnp.zeros((padded - ray_count, rows), F32)], axis=0)
    else:
        spread = member
    ranks = dot_nn(spread.astype(BF16), earlier(rows))
    for sender in range(ray_count):
        rank = jnp.where(mine[sender:sender + 1], ranks[sender:sender + 1], -1.0).astype(jnp.int32)
        hit = lax.broadcasted_iota(jnp.int32, (each, rows), 0) == rank
        at = jnp.sum(jnp.where(hit, place[sender:sender + 1], 0.0), axis=1, keepdims=True)
        here = lax.broadcasted_iota(jnp.int32, (each, rows), 1) == at.astype(jnp.int32)
        place_ref[pl.ds(sender * each, each), :] = here.astype(F32).astype(BF16)
    half = min(128, rows)
    gain = gain_ref[...]

    @pl.loop(0, rows // half)
    def _(step):
        span = pl.ds(pl.multiple_of(step * half, half), half)
        values = dot_nn(place_ref[span, :], tokens_ref[...])
        tokens_out[span, :] = values.astype(BF16)
        centered = values - jnp.mean(values, axis=-1, keepdims=True)
        variance = jnp.mean(centered * centered, axis=-1, keepdims=True)
        xhat = centered * lax.rsqrt(variance + STABILITY_EPSILON)
        normed = (xhat * gain).astype(BF16)
        normed_out[span, :] = normed
        normed_t_out[:, span] = normed.T


def prepare_tokens(me, owner, pixels, tokens, gain):
    ray_count = pixels.shape[0]
    rows, width = tokens.shape
    return pl.pallas_call(
        functools.partial(tokens_kernel, ray_count),
        out_shape=(
            jax.ShapeDtypeStruct((rows, width), BF16),
            jax.ShapeDtypeStruct((rows, width), BF16),
            jax.ShapeDtypeStruct((width, rows), BF16),
        ),
        in_specs=[SMEM, SMEM, VMEM, VMEM, VMEM],
        out_specs=(VMEM, VMEM, VMEM),
        scratch_shapes=[pltpu.VMEM((rows, rows), BF16)],
        compiler_params=params(),
        cost_estimate=pl.CostEstimate(
            flops=2 * rows * rows * width * 4, bytes_accessed=8 * rows * width, transcendentals=0
        ),
        name="tokens",
    )(me, owner, pixels, tokens, gain)


def up_kernel(normed_ref, up_ref, act_ref, slope_ref):
    parts, _, part_rows, width = up_ref.shape
    up = up_ref[...].reshape(parts * part_rows, width)
    rows = normed_ref.shape[0]
    piece = min(128, rows)

    @pl.loop(0, rows // piece)
    def _(step):
        span = pl.ds(pl.multiple_of(step * piece, piece), piece)
        hidden = dot_nn(normed_ref[span, :], up)
        phi = 0.5 * (1.0 + lax.erf(hidden * (0.5 ** 0.5)))
        density = jnp.exp(-0.5 * hidden * hidden) * ((2.0 * jnp.pi) ** -0.5)
        act_ref[span, :] = (hidden * phi).astype(BF16)
        slope_ref[span, :] = (phi + hidden * density).astype(slope_ref.dtype)


def project_up(normed, up):
    rows, width = normed.shape
    parts, chunks, part_rows, chunk = up.shape
    return pl.pallas_call(
        up_kernel,
        grid=(chunks,),
        out_shape=(
            jax.ShapeDtypeStruct((rows, chunks * chunk), BF16),
            jax.ShapeDtypeStruct((rows, chunks * chunk), F32),
        ),
        in_specs=[
            pl.BlockSpec((rows, width), lambda j: (0, 0)),
            pl.BlockSpec((parts, 1, part_rows, chunk), lambda j: (0, j, 0, 0)),
        ],
        out_specs=(
            pl.BlockSpec((rows, chunk), lambda j: (0, j)),
            pl.BlockSpec((rows, chunk), lambda j: (0, j)),
        ),
        compiler_params=params(dimension_semantics=("arbitrary",)),
        cost_estimate=pl.CostEstimate(
            flops=2 * rows * width * chunks * chunk * 3,
            bytes_accessed=2 * width * chunks * chunk + 6 * rows * chunks * chunk,
            transcendentals=2 * rows * chunks * chunk,
        ),
        name="up",
    )(normed, up)


def down_kernel(
    chunks, act_ref, down_ref, tokens_ref, target_ref, scale_ref,
    grad_ref, back_ref, small_ref, mixed_ref,
):
    step = pl.program_id(0)
    rows, width = tokens_ref.shape
    act = act_ref[...]

    @pl.when(step < chunks)
    def _():
        parts, _, part_rows, _ = down_ref.shape
        part = dot_nn(act, down_ref[...].reshape(parts * part_rows, width))

        @pl.when(step == 0)
        def _():
            mixed_ref[...] = part

        @pl.when(step > 0)
        def _():
            mixed_ref[...] += part

    @pl.when(step == chunks - 1)
    def _():
        scale = scale_ref[...]
        small_ref[...] = jnp.zeros_like(small_ref)
        piece = min(64, rows)

        @pl.loop(0, rows // piece)
        def _(index):
            span = pl.ds(pl.multiple_of(index * piece, piece), piece)
            mixed = mixed_ref[span, :]
            out = tokens_ref[span, :].astype(F32) + scale * mixed
            goal = target_ref[span, :].astype(F32)
            out_norm = jnp.sqrt(jnp.sum(out * out, axis=-1, keepdims=True) + STABILITY_EPSILON)
            goal_norm = jnp.sqrt(jnp.sum(goal * goal, axis=-1, keepdims=True) + STABILITY_EPSILON)
            norms = out_norm * goal_norm
            cosine = jnp.sum(out * goal, axis=-1, keepdims=True) / norms
            upstream = (cosine / (out_norm * out_norm)) * out - goal * (1.0 / norms)
            back_ref[span, :] = (upstream * scale).astype(BF16)
            small_ref[0:1, :] += jnp.sum(upstream * mixed, axis=0, keepdims=True)
            loss = jnp.sum(1.0 - cosine, axis=0, keepdims=True)
            small_ref[1:2, :] += jnp.broadcast_to(loss, (1, width))

    @pl.when(step >= chunks)
    def _():
        grad = dot_tn(act, back_ref[...])
        grad_ref[...] = grad.astype(BF16).reshape(grad_ref.shape)


def project_down(act, down, tokens, target, scale):
    rows, width = tokens.shape
    parts, chunks, part_rows, _ = down.shape
    chunk = parts * part_rows
    return pl.pallas_call(
        functools.partial(down_kernel, chunks),
        grid=(2 * chunks,),
        out_shape=(
            jax.ShapeDtypeStruct(down.shape, BF16),
            jax.ShapeDtypeStruct((rows, width), BF16),
            jax.ShapeDtypeStruct((8, width), F32),
        ),
        in_specs=[
            pl.BlockSpec((rows, chunk), lambda j: (0, lax.rem(j, chunks))),
            pl.BlockSpec(
                (parts, 1, part_rows, width), lambda j: (0, jnp.minimum(j, chunks - 1), 0, 0)
            ),
            pl.BlockSpec((rows, width), lambda j: (0, 0)),
            pl.BlockSpec((rows, width), lambda j: (0, 0)),
            pl.BlockSpec((1, width), lambda j: (0, 0)),
        ],
        out_specs=(
            pl.BlockSpec(
                (parts, 1, part_rows, width), lambda j: (0, jnp.maximum(j - chunks, 0), 0, 0)
            ),
            pl.BlockSpec((rows, width), lambda j: (0, 0)),
            pl.BlockSpec((8, width), lambda j: (0, 0)),
        ),
        scratch_shapes=[pltpu.VMEM((rows, width), F32)],
        compiler_params=params(dimension_semantics=("arbitrary",)),
        cost_estimate=pl.CostEstimate(
            flops=4 * rows * width * chunks * chunk,
            bytes_accessed=4 * width * chunks * chunk + 4 * rows * chunks * chunk,
            transcendentals=0,
        ),
        name="down",
    )(act, down, tokens, target, scale)


def back_kernel(back_ref, down_ref, slope_ref, normed_t_ref, up_ref, gain_ref, grad_ref, sum_ref):
    step = pl.program_id(0)
    parts, _, part_rows, width = down_ref.shape
    chunk = parts * part_rows
    rows = back_ref.shape[0]
    back_act = dot_nt(back_ref[...], down_ref[...].reshape(chunk, width))
    back_hidden = (back_act * slope_ref[...]).astype(BF16)
    up_parts, _, up_rows, _ = up_ref.shape

    @pl.when(step == 0)
    def _():
        sum_ref[...] = jnp.zeros_like(sum_ref)

    grad = dot_nn(normed_t_ref[...], back_hidden)
    grad_ref[...] = grad.astype(BF16).reshape(grad_ref.shape)
    up = up_ref[...].reshape(up_parts * up_rows, chunk).astype(F32)
    sum_ref[...] += jnp.sum(grad * up, axis=1, keepdims=True) / gain_ref[...]


def back_up(back, down, slope, normed_t, up, gain):
    width, rows = normed_t.shape
    parts, chunks, part_rows, _ = down.shape
    chunk = parts * part_rows
    up_parts, _, up_rows, _ = up.shape
    return pl.pallas_call(
        back_kernel,
        grid=(chunks,),
        out_shape=(
            jax.ShapeDtypeStruct(up.shape, BF16),
            jax.ShapeDtypeStruct((width, 1), F32),
        ),
        in_specs=[
            pl.BlockSpec((rows, width), lambda j: (0, 0)),
            pl.BlockSpec((parts, 1, part_rows, width), lambda j: (0, j, 0, 0)),
            pl.BlockSpec((rows, chunk), lambda j: (0, j)),
            pl.BlockSpec((width, rows), lambda j: (0, 0)),
            pl.BlockSpec((up_parts, 1, up_rows, chunk), lambda j: (0, j, 0, 0)),
            pl.BlockSpec((width, 1), lambda j: (0, 0)),
        ],
        out_specs=(
            pl.BlockSpec((up_parts, 1, up_rows, chunk), lambda j: (0, j, 0, 0)),
            pl.BlockSpec((width, 1), lambda j: (0, 0)),
        ),
        compiler_params=params(dimension_semantics=("arbitrary",)),
        cost_estimate=pl.CostEstimate(
            flops=4 * rows * width * chunks * chunk,
            bytes_accessed=6 * width * chunks * chunk + 4 * rows * chunks * chunk,
            transcendentals=0,
        ),
        name="back",
    )(back, down, slope, normed_t, up, gain)


def gather_weight(weight, parts, group, group_count, ray_count):
    rows, cols = weight.shape
    if parts == 1:
        whole = lax.all_gather(weight, "ray", axis=0, tiled=True)
    else:
        part = lax.dynamic_slice_in_dim(weight, group * (rows // parts), rows // parts, 0)
        whole = lax.all_gather(part, ("grp", "ray"), axis=0, tiled=True)
    return whole.reshape(parts, ray_count, rows // parts, cols)


def reduce_gradient(grad):
    parts, ray_count, part_rows, cols = grad.shape
    flat = grad.reshape(parts * ray_count * part_rows, cols)
    if parts == 1:
        share = lax.psum_scatter(flat, "ray", scatter_dimension=0, tiled=True)
        return lax.psum(share.astype(F32), "grp")
    share = lax.psum_scatter(flat, "grp", scatter_dimension=0, tiled=True)
    share = lax.psum_scatter(share, "ray", scatter_dimension=0, tiled=True)
    return lax.all_gather(share, "grp", axis=0, tiled=True).astype(F32)


def shards(
    image_tokens,
    tile_lists,
    opacity,
    tile_counts,
    ray_pixel,
    block_owner,
    gaussian_features,
    layer_norm_gain,
    layer_scale,
    up_weight,
    down_weight,
):
    ray_count = lax.axis_size("ray")
    group_count = lax.axis_size("grp")
    group = lax.axis_index("grp")
    me = lax.axis_index("ray").reshape(1)
    rows, width = image_tokens.shape
    up_parts = group_count if up_weight.shape[0] % (16 * group_count) == 0 else 1
    down_parts = group_count if down_weight.shape[0] % (16 * group_count) == 0 else 1
    up = gather_weight(up_weight, up_parts, group, group_count, ray_count)
    down = gather_weight(down_weight, down_parts, group, group_count, ray_count)
    pixels = ray_pixel[0].reshape(ray_count, rows)
    rendered = render(
        me, block_owner, tile_lists, opacity, tile_counts.reshape(1, rows), pixels,
        gaussian_features,
    )
    target = lax.all_to_all(rendered, "ray", split_axis=0, concat_axis=0, tiled=True)
    tokens, normed, normed_t = prepare_tokens(
        me, block_owner, pixels, image_tokens, layer_norm_gain.reshape(1, width)
    )
    act, slope = project_up(normed, up)
    grad_down, back, small = project_down(act, down, tokens, target, layer_scale.reshape(1, width))
    grad_up, gain_sum = back_up(back, down, slope, normed_t, up, layer_norm_gain.reshape(width, 1))
    grad_down = reduce_gradient(grad_down)
    grad_up = reduce_gradient(grad_up)
    sums = jnp.concatenate([gain_sum.reshape(1, width), small[:2]], axis=0)
    sums = lax.psum(sums, ("grp", "ray"))
    loss = sums[2, 0] / (rows * ray_count * group_count)
    return (grad_up, grad_down, sums[0], sums[1], loss)


def solution(mesh):
    return jax.shard_map(
        shards,
        mesh=mesh,
        in_specs=(
            P(("grp", "ray"), None),
            P(None, ("grp", "ray")),
            P(None, ("grp", "ray")),
            P(("grp", "ray")),
            P("grp", None),
            P("grp", None),
            P(("grp", "ray"), None),
            P(),
            P(),
            P(None, "ray"),
            P("ray", None),
        ),
        out_specs=(P(None, "ray"), P("ray", None), P(), P(), P()),
        check_vma=False,
    )
```

time: 468 us -> 357 us (0.76)
  other arithmetic: 116 us -> 3.76 us
  Pallas kernels: 0 us -> 65.5 us
  matrix products: 47.1 us -> 0 us
  waiting for transfers between devices: 213 us -> 191 us
  blocking collectives: 42.4 us -> 61.7 us
  local copies, waits for them, and re-layouts: 23.2 us -> 7.85 us
    add x32 -> x0, other arithmetic: 105 us -> none  [advance(): table + jnp.where(ident[:, None] == columns[None, :], share[:, None], jnp...]
    all_gather x2, waiting for transfers between devices: 0.01 us -> 92 us  [gather_weight(): whole = lax.all_gather(part, ('grp', 'ray'), axis=0, tiled=True)]
    reduce_scatter x2 -> x4, waiting for transfers between devices: 171 us -> 98.5 us  [the longest x2 89.9 us: reduce_gradient(): share = lax.psum_scatter(flat, 'grp', scatter_dimension=0, tiled=True)]
    pallas_call x0 -> x5, Pallas kernels: none -> 65.5 us  [the longest x1 18.3 us: project_down(): pl.pallas_call(functools.partial(down_kernel, chunks), grid=(2 * chunks,)...]
    dot_general x7 -> x0, matrix products: 47.1 us -> none  [the longest x1 14.3 us: layer_pieces(): jnp.dot(normalized_rows, full_up, preferred_element_type=jnp.float32)]
    psum x1 -> x0, waiting for transfers between devices: 24 us -> none  [shards(): grad_up, grad_down = lax.psum((shares[0], shares[1]), 'grp')]
    all_gather x0 -> x2, blocking collectives: none -> 21.8 us  [reduce_gradient(): return lax.all_gather(share, 'grp', axis=0, tiled=True).astype(F32)]
    all_to_all x1, waiting for transfers between devices: 17.2 us -> 0.01 us  [shards(): lax.all_to_all(rendered, 'ray', split_axis=0, concat_axis=0, tiled=True)]
  transfers between devices with their start and end apart: 6 -> 7, of which waited for: 4 -> 5; matrix products, arithmetic and copies ran while one was open for 34% -> 2% of each run, Pallas kernels for 0% -> 13%
where the time goes in v1:
time: 357 us; the launch traced here: 351 us
  waiting for transfers between devices  191 us (54%)
  Pallas kernels  65.5 us (18%)
  blocking collectives  61.7 us (17%)
  between operations  15.9 us (4%)
  local copies, waits for them, and re-layouts  7.85 us (2%)
  starting transfers between devices  5.53 us (2%)
  other arithmetic  3.76 us (1%)
    all_gather x2, waiting for transfers between devices, gather_weight(): whole = lax.all_gather(part, ('grp', 'ray'), axis=0, tiled=True)  92 us
    reduce_scatter x2, waiting for transfers between devices, reduce_gradient(): share = lax.psum_scatter(flat, 'grp', scatter_dimension=0, tiled=True)  89.9 us
    psum x1, blocking collectives, shards(): sums = lax.psum(sums, ('grp', 'ray'))  39.9 us
    all_gather x2, blocking collectives, reduce_gradient(): return lax.all_gather(share, 'grp', axis=0, tiled=True).astype(F32)  21.8 us
    pallas_call x1, Pallas kernels, project_down(): pl.pallas_call(functools.partial(down_kernel, chunks), grid=(2 * chunks,)...  18.3 us
    pallas_call x1, Pallas kernels, back_up(): pl.pallas_call(back_kernel, grid=(chunks,), out_shape=(jax.ShapeDtypeStru...  15.6 us
    pallas_call x1, Pallas kernels, render(): pl.pallas_call(functools.partial(render_kernel, ray_count), out_shape=jax...  14 us
    pallas_call x1, Pallas kernels, project_up(): pl.pallas_call(up_kernel, grid=(chunks,), out_shape=(jax.ShapeDtypeStruct...  12.2 us
  transfers between devices with their start and end apart: 7, of which 5 were waited for; matrix products, arithmetic and copies ran while one was open for 2% of the time, Pallas kernels for 13%

profile of v1, /device:TPU:8, one launch (start us, length us, event | category | flops | bytes accessed | tf_op | source)
XLA Modules:
  0.0 350.8 jit_solution(11625802465355541080)
XLA Ops:
  7.2 0.0 all-gather.3.cloned.1.call-start
  7.2 1.0 copy-done
  8.2 0.7 constant_dynamic-slice_fusion.1
  8.9 0.0 all-gather.5.cloned.1.call-start
  9.0 1.6 constant_dynamic-slice_fusion
  10.5 0.5 broadcast.4
  11.1 1.4 reduce.4
  12.5 0.6 reshape_squeeze.3.pixels_ref
  13.1 14.0 %render.1 = bf16[512,1024]{1,0:T(8,128)(2,1)} custom-call(s32[1]{0:T(128)} %bitcast.me_ref, s32[1,8]{1,0:T(1,128)} %owner_ref.3, s32[32,512]{1,0:T(8,128)} %lists_ref.1, f32[32,512]{1,0:T(8,128)} %opacity_ref.1, s32[1,512]{1,0:T(1,128)} %bitcast.29, s32[8,512]{1,0:T(8,128)} %reshape_squeeze.3.pixels_ref, bf16[1024,1024]{1,0:T(8,128)(2,1)} %features_ref.1), custom_call_target="tpu_custom_call" | custom-call | flops 3623878656 | bytes 3145728 | tf_op jit(solution)/shard_map/render/pallas_call | solution.py:104
  27.0 5.3 %all-to-all-start = ((bf16[8,64,1024]{2,1,0:T(8,128)(2,1)}), bf16[8,64,1024]{2,1,0:T(8,128)(2,1)S(1)}, u32[]{:S(2)}, u32[]{:S(2)}) async-start(bf16[8,64,1024]{2,1,0:T(8,128)(2,1)} %bitcast.18), calls=%async_computation | async-start | bytes 2097152 | tf_op jit(solution)/shard_map/all_to_all | solution.py:417
  32.4 5.5 %tokens.1 = (bf16[512,1024]{1,0:T(8,128)(2,1)}, bf16[512,1024]{1,0:T(8,128)(2,1)}, bf16[1024,512]{1,0:T(8,128)(2,1)}) custom-call(s32[1]{0:T(128)} %bitcast.me_ref, s32[1,8]{1,0:T(1,128)} %owner_ref.3, s32[8,512]{1,0:T(8,128)} %reshape_squeeze.3.pixels_ref, bf16[512,1024]{1,0:T(8,128)(2,1)} %tokens_ref.1, f32[1,1024]{1,0:T(1,128)} %bitcast.20), custom_call_target="tpu_custom_call" | custom-call | flops 2147483648 | bytes 4194304 | tf_op jit(solution)/shard_map/tokens/pallas_call | solution.py:166
  37.8 39.6 %all-gather.3.cloned.1.call-done = bf16[8192,256]{1,0:T(8,128)(2,1)} async-done(((bf16[256,256]{1,0:T(8,128)(2,1)}), bf16[8192,256]{1,0:T(8,128)(2,1)}) %all-gather.3.cloned.1.call-update) | async-done | bytes 4194320 | tf_op jit(solution)/shard_map/all_gather | solution.py:375
  77.4 12.2 %up.1 = (bf16[512,2048]{1,0:T(8,128)(2,1)}, f32[512,2048]{1,0:T(8,128)}) custom-call(bf16[512,1024]{1,0:T(8,128)(2,1)} %get-tuple-element.15.normed_ref, bf16[4,8,256,256]{3,2,1,0:T(8,128)(2,1)} %bitcast.24), custom_call_target="tpu_custom_call" | custom-call | flops 6442450944 | bytes 10485760 | tf_op jit(solution)/shard_map/up/pallas_call | solution.py:203
  89.6 52.4 %all-gather.5.cloned.1.call-done = bf16[2048,1024]{1,0:T(8,128)(2,1)} async-done(((bf16[64,1024]{1,0:T(8,128)(2,1)}), bf16[2048,1024]{1,0:T(8,128)(2,1)}) %all-gather.5.cloned.1.call-update) | async-done | bytes 4194320 | tf_op jit(solution)/shard_map/all_gather | solution.py:375
  142.0 18.3 %down.1 = (bf16[4,8,64,1024]{3,2,1,0:T(8,128)(2,1)}, bf16[512,1024]{1,0:T(8,128)(2,1)}, f32[8,1024]{1,0:T(8,128)}) custom-call(bf16[512,2048]{1,0:T(8,128)(2,1)} %get-tuple-element.16.act_ref, bf16[4,8,64,1024]{3,2,1,0:T(8,128)(2,1)} %bitcast.26, bf16[512,1024]{1,0:T(8,128)(2,1)} %get-tuple-element.17.tokens_ref, bf16[512,1024]{1,0:T(8,128)(2,1)} %bitcast.17, ...), custom_call_target="tpu_custom_call" | custom-call | flops 4294967296 | bytes 12582912 | tf_op jit(solution)/shard_map/down/pallas_call | solution.py:281
  160.4 0.0 reduce-scatter.5.cloned.1.call-start
  160.4 0.6 copy-done.3
  161.0 1.0 copy.16.gain_ref
  162.0 15.6 %back.1 = (bf16[4,8,256,256]{3,2,1,0:T(8,128)(2,1)}, f32[1024,1]{1,0:T(8,128)}) custom-call(bf16[512,1024]{1,0:T(8,128)(2,1)} %get-tuple-element.18.back_ref, bf16[4,8,64,1024]{3,2,1,0:T(8,128)(2,1)} %bitcast.27, f32[512,2048]{1,0:T(8,128)} %get-tuple-element.19.slope_ref, bf16[1024,512]{1,0:T(8,128)(2,1)} %get-tuple-element.20.normed_t_ref, ...), custom_call_target="tpu_custom_call" | custom-call | flops 4294967296 | bytes 16777216 | tf_op jit(solution)/shard_map/back/pallas_call | solution.py:340
  177.6 0.0 reduce-scatter.11.cloned.1.call-start
  177.7 34.2 %reduce-scatter.9.cloned.1.call-done = bf16[512,1024]{1,0:T(8,128)(2,1)} async-done(((bf16[2048,1024]{1,0:T(8,128)(2,1)}), bf16[512,1024]{1,0:T(8,128)(2,1)}) %reduce-scatter.9.cloned.1.call-update) | async-done | bytes 1048592 | tf_op jit(solution)/shard_map/reduce_scatter | solution.py:385
  211.9 55.7 %reduce-scatter.5.cloned.1.call-done = bf16[2048,256]{1,0:T(8,128)(2,1)} async-done(((bf16[8192,256]{1,0:T(8,128)(2,1)}), bf16[2048,256]{1,0:T(8,128)(2,1)}) %reduce-scatter.5.cloned.1.call-update) | async-done | bytes 1048592 | tf_op jit(solution)/shard_map/reduce_scatter | solution.py:385
  267.7 0.8 slice.12
  268.4 0.2 reduce.1
  268.7 39.9 %psum.7 = f32[3,1024]{1,0:T(4,128)S(1)} all-reduce(f32[3,1024]{1,0:T(4,128)S(1)} %pad_maximum_fusion), channel_id=1, replica_groups=mesh['grp'=4,'ray'=8] {'grp','ray'}, use_global_device_ids=true, to_apply=%region_4.0 | all-reduce | flops 3072 | bytes 24576 | tf_op jit(solution)/shard_map/psum | solution.py:427
  308.6 0.5 slice.18
  309.8 0.6 fusion
  310.4 11.4 %all_gather.15 = bf16[256,1024]{1,0:T(8,128)(2,1)S(1)} all-gather(bf16[64,1024]{1,0:T(8,128)(2,1)} %reduce-scatter.11.cloned.1.call-done), channel_id=1, replica_groups=mesh['grp'=4,'ray'=8] {'grp'}, dimensions={0}, use_global_device_ids=true | all-gather | bytes 655360 | tf_op jit(solution)/shard_map/all_gather | solution.py:387
  321.8 1.1 convert_element_type.7
  322.8 8.6 %reduce-scatter.7.cloned.1.call-done = bf16[256,256]{1,0:T(8,128)(2,1)} async-done(((bf16[2048,256]{1,0:T(8,128)(2,1)}), bf16[256,256]{1,0:T(8,128)(2,1)}) %reduce-scatter.7.cloned.1.call-update) | async-done | bytes 131088 | tf_op jit(solution)/shard_map/reduce_scatter | solution.py:386
  331.4 10.4 %all_gather.14 = bf16[1024,256]{1,0:T(8,128)(2,1)S(1)} all-gather(bf16[256,256]{1,0:T(8,128)(2,1)} %reduce-scatter.7.cloned.1.call-done), channel_id=1, replica_groups=mesh['grp'=4,'ray'=8] {'grp'}, dimensions={0}, use_global_device_ids=true | all-gather | bytes 655360 | tf_op jit(solution)/shard_map/all_gather | solution.py:387
  341.8 1.0 convert_element_type.6
  (17 shorter events, 0.2 us)
Async XLA Ops:
  7.2 1.0 copy-start
  7.2 70.2 %all-gather.3.cloned.1.call-start = ((), (), s32[]{:S(2)}) async-start(), calls=%async_computation.5 | async-start | bytes 4325376 | tf_op jit(solution)/shard_map/all_gather | solution.py:375
  8.9 133.1 %all-gather.5.cloned.1.call-start = ((), (), s32[]{:S(2)}) async-start(), calls=%async_computation.6 | async-start | bytes 4325376 | tf_op jit(solution)/shard_map/all_gather | solution.py:375
  27.0 62.5 %all-to-all-start = ((bf16[8,64,1024]{2,1,0:T(8,128)(2,1)}), bf16[8,64,1024]{2,1,0:T(8,128)(2,1)S(1)}, u32[]{:S(2)}, u32[]{:S(2)}) async-start(bf16[8,64,1024]{2,1,0:T(8,128)(2,1)} %bitcast.18), calls=%async_computation | async-start | bytes 2097152 | tf_op jit(solution)/shard_map/all_to_all | solution.py:417
  32.4 179.5 %reduce-scatter.9.cloned.1.call-start = ((), (), s32[]{:S(2)}) async-start(), calls=%async_computation.9 | async-start | bytes 5242880 | tf_op jit(solution)/shard_map/reduce_scatter | solution.py:385
  89.6 52.4 %copy-start.1 = (bf16[8,64,1024]{2,1,0:T(8,128)(2,1)}, bf16[8,64,1024]{2,1,0:T(8,128)(2,1)S(1)}, u32[]{:S(2)}) copy-start(bf16[8,64,1024]{2,1,0:T(8,128)(2,1)S(1)} %all-to-all-done) | copy-start | bytes 3145732
  160.3 0.7 copy-start.3
  160.4 107.3 %reduce-scatter.5.cloned.1.call-start = ((), (), s32[]{:S(2)}) async-start(), calls=%async_computation.7 | async-start | bytes 5242880 | tf_op jit(solution)/shard_map/reduce_scatter | solution.py:385
  177.6 90.8 %copy-start.2 = (f32[1024,1]{1,0:T(8,128)S(1)}, f32[1024,1]{1,0:T(8,128)}, u32[]{:S(2)}) copy-start(f32[1024,1]{1,0:T(8,128)} %get-tuple-element.23) | copy-start | bytes 12292
  177.6 132.7 %reduce-scatter.11.cloned.1.call-start = ((), (), s32[]{:S(2)}) async-start(), calls=%async_computation.10 | async-start | bytes 1179648 | tf_op jit(solution)/shard_map/reduce_scatter | solution.py:386
  211.9 119.5 %reduce-scatter.7.cloned.1.call-start = ((), (), s32[]{:S(2)}) async-start(), calls=%async_computation.8 | async-start | bytes 1179648 | tf_op jit(solution)/shard_map/reduce_scatter | solution.py:386
Sparse Core Ops, SparseCore 0:
  11.0 66.3 all-gather.2
  80.4 61.5 all-gather.4
  160.5 51.3 reduce-scatter.8
  214.9 52.6 reduce-scatter.4
  269.8 28.6 reduce-scatter.10
  300.6 30.8 reduce-scatter.6

commit v2 on v1

--- a/solution.py
+++ b/solution.py
@@ -11,12 +11,17 @@
 F32 = jnp.float32
 BF16 = jnp.bfloat16
 VMEM_BYTES = 56 * 1024 * 1024
+SMALL_VMEM_BYTES = 28 * 1024 * 1024
 SMEM = pl.BlockSpec(memory_space=pltpu.SMEM)
 VMEM = pl.BlockSpec(memory_space=pltpu.VMEM)
 
 
 def params(**more):
     return pltpu.CompilerParams(vmem_limit_bytes=VMEM_BYTES, **more)
+
+
+def small_params():
+    return pltpu.CompilerParams(vmem_limit_bytes=SMALL_VMEM_BYTES)
 
 
 def dot_nn(a, b):
@@ -387,7 +392,7 @@
     return lax.all_gather(share, "grp", axis=0, tiled=True).astype(F32)
 
 
-def shards(
+def shards_general(
     image_tokens,
     tile_lists,
     opacity,
@@ -429,6 +434,347 @@
     return (grad_up, grad_down, sums[0], sums[1], loss)
 
 
+def quarter_kernel(group_ref, up_ref, down_ref, out_ref, turned_ref):
+    part = out_ref.shape[1]
+    first = pl.multiple_of(group_ref[0] * part, part)
+    turned_ref[...] = up_ref[...].T
+    out_ref[0] = turned_ref[pl.ds(first, part), :]
+    out_ref[1] = down_ref[pl.ds(first, part), :]
+
+
+def own_quarter(group, up, down, part):
+    width, chunk = up.shape
+    return pl.pallas_call(
+        quarter_kernel,
+        out_shape=jax.ShapeDtypeStruct((2, part, width), BF16),
+        in_specs=[SMEM, VMEM, VMEM],
+        out_specs=VMEM,
+        scratch_shapes=[pltpu.VMEM((chunk, width), BF16)],
+        compiler_params=small_params(),
+        cost_estimate=pl.CostEstimate(flops=0, bytes_accessed=6 * width * chunk, transcendentals=0),
+        name="quarter",
+    )(group, up, down)
+
+
+def finish_rows(tokens, mixed, goal, scale):
+    out = tokens + scale * mixed
+    out_norm = jnp.sqrt(jnp.sum(out * out, axis=-1, keepdims=True) + STABILITY_EPSILON)
+    goal_norm = jnp.sqrt(jnp.sum(goal * goal, axis=-1, keepdims=True) + STABILITY_EPSILON)
+    norms = out_norm * goal_norm
+    cosine = jnp.sum(out * goal, axis=-1, keepdims=True) / norms
+    upstream = (cosine / (out_norm * out_norm)) * out - goal * (1.0 / norms)
+    return upstream, 1.0 - cosine
+
+
+def forward_kernel(first, last, *refs):
+    refs = list(refs)
+    normed_t_ref, own_ref, other_ref = refs[:3]
+    del refs[:3]
+    mixed_in = None if first else refs.pop(0)
+    if last:
+        tokens_ref, target_ref, scale_ref = refs[:3]
+        del refs[:3]
+    act_ref, slope_ref = refs[:2]
+    del refs[:2]
+    count, _, part, width = own_ref.shape
+    rows = normed_t_ref.shape[1]
+    for side, ref in enumerate((own_ref, other_ref)):
+        for index in range(count):
+            hidden = dot_nn(ref[index, 0], normed_t_ref[...])
+            phi = 0.5 * (1.0 + lax.erf(hidden * (0.5 ** 0.5)))
+            density = jnp.exp(-0.5 * hidden * hidden) * ((2.0 * jnp.pi) ** -0.5)
+            act_ref[side, index] = (hidden * phi).astype(BF16)
+            slope_ref[side, index] = phi + hidden * density
+    act = act_ref[...].reshape(2 * count * part, rows)
+    down = jnp.concatenate(
+        [own_ref[:, 1].reshape(count * part, width), other_ref[:, 1].reshape(count * part, width)],
+        axis=0,
+    )
+    if not last:
+        mixed_out = refs[0]
+        part_sum = dot_tn(act, down)
+        mixed_out[...] = part_sum if first else mixed_in[...] + part_sum
+        return
+    back_ref, back_t_ref, small_ref, mixed_ref = refs
+    mixed_ref[...] = mixed_in[...] + dot_tn(act, down)
+    scale = scale_ref[...]
+    small_ref[...] = jnp.zeros_like(small_ref)
+    piece = 128
+
+    @pl.loop(0, rows // piece)
+    def _(index):
+        span = pl.ds(pl.multiple_of(index * piece, piece), piece)
+        mixed = mixed_ref[span, :]
+        upstream, loss = finish_rows(
+            tokens_ref[span, :].astype(F32), mixed, target_ref[span, :].astype(F32), scale
+        )
+        back = (upstream * scale).astype(BF16)
+        back_ref[span, :] = back
+        back_t_ref[:, span] = back.T
+        small_ref[0:1, :] += jnp.sum(upstream * mixed, axis=0, keepdims=True)
+        small_ref[1:2, :] += jnp.broadcast_to(jnp.sum(loss, axis=0, keepdims=True), (1, width))
+
+
+def forward(normed_t, own, other, mixed=None, finish=None):
+    width, rows = normed_t.shape
+    count, _, part, _ = own.shape
+    first, last = mixed is None, finish is not None
+    operands = [normed_t, own, other]
+    if not first:
+        operands.append(mixed)
+    if last:
+        operands.extend(finish)
+    piece = (2, count, part, rows)
+    shapes = [jax.ShapeDtypeStruct(piece, BF16), jax.ShapeDtypeStruct(piece, F32)]
+    scratch = []
+    if last:
+        shapes += [
+            jax.ShapeDtypeStruct((rows, width), BF16),
+            jax.ShapeDtypeStruct((width, rows), BF16),
+            jax.ShapeDtypeStruct((8, width), F32),
+        ]
+        scratch = [pltpu.VMEM((rows, width), F32)]
+    else:
+        shapes += [jax.ShapeDtypeStruct((rows, width), F32)]
+    return pl.pallas_call(
+        functools.partial(forward_kernel, first, last),
+        out_shape=tuple(shapes),
+        in_specs=[VMEM] * len(operands),
+        out_specs=tuple([VMEM] * len(shapes)),
+        scratch_shapes=scratch,
+        compiler_params=small_params(),
+        cost_estimate=pl.CostEstimate(
+            flops=8 * rows * width * count * part * 2,
+            bytes_accessed=4 * rows * width, transcendentals=0,
+        ),
+        name="forward",
+    )(*operands)
+
+
+def backward_kernel(side, quarter, add, *refs):
+    refs = list(refs)
+    back_ref, back_t_ref, normed_ref, near_ref, far_ref = refs[:5]
+    act_near, slope_near, act_far, slope_far = refs[5:9]
+    del refs[:9]
+    arrived = refs.pop(0) if add else None
+    up_ref, down_ref, gain_ref = refs
+    part, width = near_ref.shape[-2:]
+    far = far_ref.shape[0]
+    chunk = (far + 1) * part
+    rows = back_ref.shape[0]
+
+    def joined(near, other):
+        return jnp.concatenate([near, other.reshape(far * part, other.shape[-1])], axis=0)
+
+    slope = joined(slope_near[side, quarter], slope_far[side])
+    back_act = dot_nn(joined(near_ref[quarter, 1], far_ref[:, 1]), back_t_ref[...])
+    back_hidden = (back_act * slope).astype(BF16)
+    grad_up = dot_nn(back_hidden, normed_ref[...])
+    up = joined(near_ref[quarter, 0], far_ref[:, 0]).astype(F32)
+    gain_ref[...] = jnp.sum(grad_up * up, axis=0, keepdims=True)
+    grad_down = dot_nn(joined(act_near[side, quarter], act_far[side]), back_ref[...])
+    if add:
+        grad_up += arrived[0].reshape(chunk, width).astype(F32)
+        grad_down += arrived[1].reshape(chunk, width).astype(F32)
+    up_ref[...] = grad_up.astype(BF16).reshape(up_ref.shape)
+    down_ref[...] = grad_down.astype(BF16).reshape(down_ref.shape)
+
+
+def backward(side, quarter, common, near, far, act_near, slope_near, act_far, slope_far, arrived):
+    back, back_t, normed = common
+    rows, width = back.shape
+    part = near.shape[2]
+    count = far.shape[0] + 1
+    operands = [back, back_t, normed, near, far, act_near, slope_near, act_far, slope_far]
+    if arrived is None:
+        def body(*refs):
+            grads, gain_ref = refs[-2:]
+            backward_kernel(
+                side, quarter, False, *refs[:-2], grads.at[0], grads.at[1], gain_ref
+            )
+
+        shapes = [jax.ShapeDtypeStruct((2, count, part, width), BF16)]
+    else:
+        operands.append(arrived)
+        body = functools.partial(backward_kernel, side, quarter, True)
+        shapes = [jax.ShapeDtypeStruct((count, part, width), BF16)] * 2
+    shapes.append(jax.ShapeDtypeStruct((1, width), F32))
+    return pl.pallas_call(
+        body,
+        out_shape=tuple(shapes),
+        in_specs=[VMEM] * len(operands),
+        out_specs=tuple([VMEM] * len(shapes)),
+        compiler_params=small_params(),
+        cost_estimate=pl.CostEstimate(
+            flops=6 * rows * width * count * part,
+            bytes_accessed=6 * rows * width, transcendentals=0,
+        ),
+        name="backward",
+    )(*operands)
+
+
+def total_kernel(*refs):
+    ins, outs = refs[:4], refs[4:]
+    for index, out in enumerate(outs):
+        total = ins[0][index].astype(F32)
+        for ref in ins[1:]:
+            total = total + ref[index].astype(F32)
+        out[...] = total.astype(BF16)
+
+
+def totals(parts):
+    count, part, width = parts[0].shape
+    return pl.pallas_call(
+        total_kernel,
+        out_shape=tuple([jax.ShapeDtypeStruct((part, width), BF16)] * count),
+        in_specs=[VMEM] * 4,
+        out_specs=tuple([VMEM] * count),
+        compiler_params=small_params(),
+        cost_estimate=pl.CostEstimate(
+            flops=4 * count * part * width, bytes_accessed=10 * count * part * width,
+            transcendentals=0,
+        ),
+        name="totals",
+    )(*parts)
+
+
+def place_kernel(turn, group_ref, a_ref, b_ref, c_ref, d_ref, out_ref, held_ref):
+    part = a_ref.shape[0]
+    group = group_ref[0]
+    for index, ref in enumerate((a_ref, b_ref, c_ref, d_ref)):
+        first = pl.multiple_of(jnp.bitwise_xor(group, index) * part, part)
+        held_ref[pl.ds(first, part), :] = ref[...].astype(F32)
+    out_ref[...] = held_ref[...].T if turn else held_ref[...]
+
+
+def place_quarters(group, quarters, turn):
+    part, width = quarters[0].shape
+    shape = (width, 4 * part) if turn else (4 * part, width)
+    return pl.pallas_call(
+        functools.partial(place_kernel, turn),
+        out_shape=jax.ShapeDtypeStruct(shape, F32),
+        in_specs=[SMEM] + [VMEM] * 4,
+        out_specs=VMEM,
+        scratch_shapes=[pltpu.VMEM((4 * part, width), F32)],
+        compiler_params=small_params(),
+        cost_estimate=pl.CostEstimate(
+            flops=0, bytes_accessed=24 * part * width, transcendentals=0
+        ),
+        name="place",
+    )(group, *quarters)
+
+
+def shards_square(
+    image_tokens,
+    tile_lists,
+    opacity,
+    tile_counts,
+    ray_pixel,
+    block_owner,
+    gaussian_features,
+    layer_norm_gain,
+    layer_scale,
+    up_weight,
+    down_weight,
+):
+    ray_count = lax.axis_size("ray")
+    group_count = lax.axis_size("grp")
+    depth = ray_count // 2
+    group = lax.axis_index("grp").reshape(1)
+    me = lax.axis_index("ray").reshape(1)
+    rows, width = image_tokens.shape
+    part = down_weight.shape[0] // group_count
+
+    def beside(array, flip):
+        return lax.ppermute(array, "grp", [(g, g ^ flip) for g in range(group_count)])
+
+    def partner(array, flip=1):
+        return lax.ppermute(array, "ray", [(r, r ^ flip) for r in range(ray_count)])
+
+    def along(array, shift):
+        pairs = [(r, (r + 2 * shift) % ray_count) for r in range(ray_count)]
+        return lax.ppermute(array, "ray", pairs)
+
+    mine = own_quarter(group, up_weight, down_weight, part)
+    far = [along(mine, -shift) for shift in range(1, depth)]
+    near = jnp.stack([mine] + [beside(mine, flip) for flip in (1, 2, 3)])
+    near_other = partner(near)
+    far = jnp.stack(far)
+    far = [far] + [beside(far, flip) for flip in (1, 2, 3)]
+    far_other = [partner(array) for array in far]
+
+    pixels = ray_pixel[0].reshape(ray_count, rows)
+    rendered = render(
+        me, block_owner, tile_lists, opacity, tile_counts.reshape(1, rows), pixels,
+        gaussian_features,
+    )
+    target = lax.all_to_all(rendered, "ray", split_axis=0, concat_axis=0, tiled=True)
+    tokens, normed, normed_t = prepare_tokens(
+        me, block_owner, pixels, image_tokens, layer_norm_gain.reshape(1, width)
+    )
+    act_near, slope_near, mixed = forward(normed_t, near, near_other)
+    act_far, slope_far = [None] * 4, [None] * 4
+    for quarter in (0, 1, 2):
+        act_far[quarter], slope_far[quarter], mixed = forward(
+            normed_t, far[quarter], far_other[quarter], mixed
+        )
+    act_far[3], slope_far[3], back, back_t, small = forward(
+        normed_t, far[3], far_other[3], mixed, (tokens, target, layer_scale.reshape(1, width))
+    )
+    common = (back, back_t, normed)
+
+    def grads(side, quarter, arrived):
+        weights = (near, far) if side == 0 else (near_other, far_other)
+        return backward(
+            side, quarter, common, weights[0], weights[1][quarter], act_near, slope_near,
+            act_far[quarter], slope_far[quarter], arrived,
+        )
+
+    order = (3, 1, 2, 0)
+    arrived, gains, sums = {}, [], {}
+    for quarter in order:
+        out, gain = grads(1, quarter, None)
+        arrived[quarter] = partner(out)
+        gains.append(gain)
+    for quarter in order:
+        grad_up, grad_down, gain = grads(0, quarter, arrived[quarter])
+        gains.append(gain)
+        sums[quarter] = (grad_up, grad_down)
+    sent = {
+        (quarter, which): beside(sums[quarter][which], quarter)
+        for which in (1, 0) for quarter in (3, 1, 2)
+    }
+    results = {}
+    for which in (1, 0):
+        shares = totals([sums[0][which]] + [sent[quarter, which] for quarter in (1, 2, 3)])
+        total = shares[0].astype(F32)
+        for shift in range(1, depth):
+            total = total + along(shares[shift], shift).astype(F32)
+        total = total.astype(BF16)
+        results[which] = place_quarters(
+            group, [total] + [beside(total, flip) for flip in (1, 2, 3)], which == 0
+        )
+    vector = jnp.concatenate(
+        [sum(gains) / layer_norm_gain.reshape(1, width), small[:2]], axis=0
+    )
+    vector = vector + partner(vector)
+    for flip in (1, 2):
+        vector = vector + beside(vector, flip)
+    flip = 2
+    while flip < ray_count:
+        vector = vector + partner(vector, flip)
+        flip *= 2
+    loss = vector[2, 0] / (rows * ray_count * group_count)
+    return (results[0], results[1], vector[0], vector[1], loss)
+
+
+def shards(*operands):
+    ray_count, group_count = lax.axis_size("ray"), lax.axis_size("grp")
+    hidden = operands[-1].shape[0]
+    square = group_count == 4 and ray_count in (4, 8, 16) and hidden % (16 * group_count) == 0
+    return (shards_square if square else shards_general)(*operands)
+
+
 def solution(mesh):
     return jax.shard_map(
         shards,

time: 357 us -> 227 us (0.64); the launches traced: 351 us -> 226 us
  waiting for transfers between devices: 191 us -> 101 us
  blocking collectives: 61.7 us -> 0 us
  starting transfers between devices: 5.53 us -> 47.3 us
  between operations: 15.9 us -> 2.88 us
  Pallas kernels: 65.5 us -> 53.3 us
  local copies, waits for them, and re-layouts: 7.85 us -> 18.5 us
    ppermute x0 -> x41, waiting for transfers between devices: none -> 101 us  [the longest x20 76 us: beside(): lax.ppermute(array, 'grp', [(g, g ^ flip) for g in range(group_count)])]
    reduce_scatter x4 -> x0, waiting for transfers between devices: 98.5 us -> none  [the longest x2 89.9 us: reduce_gradient(): share = lax.psum_scatter(flat, 'grp', scatter_dimension=0, tiled=True)]
    all_gather x2 -> x0, waiting for transfers between devices: 92 us -> none  [gather_weight(): whole = lax.all_gather(part, ('grp', 'ray'), axis=0, tiled=True)]
    ppermute x0 -> x41, starting transfers between devices: none -> 43 us  [the longest x20 24 us: beside(): lax.ppermute(array, 'grp', [(g, g ^ flip) for g in range(group_count)])]
    psum x1 -> x0, blocking collectives: 39.9 us -> none  [shards(): sums = lax.psum(sums, ('grp', 'ray'))]
    all_gather x2 -> x0, blocking collectives: 21.8 us -> none  [reduce_gradient(): return lax.all_gather(share, 'grp', axis=0, tiled=True).astype(F32)]
    unnamed x9 -> x71, local copies, waits for them, and re-layouts: 2.12 us -> 16.8 us
    pallas_call x3 -> x18, Pallas kernels: 46 us -> 33.8 us  [the longest x5 16.6 us: forward(): pl.pallas_call(functools.partial(forward_kernel, first, last), out_shape=...]
  transfers between devices with their start and end apart: 7 -> 42, of which waited for: 5 -> 15; matrix products, arithmetic and copies ran while one was open for 2% -> 2% of each run, Pallas kernels for 13% -> 20%
where the time goes in v2:
time: 227 us; the launch traced here: 226 us
  waiting for transfers between devices  101 us (44%)
  Pallas kernels  53.3 us (23%)
  starting transfers between devices  47.3 us (21%)
  local copies, waits for them, and re-layouts  18.5 us (8%)
  between operations  2.88 us (1%)
  other arithmetic  2.79 us (1%)
    ppermute x20, waiting for transfers between devices, beside(): lax.ppermute(array, 'grp', [(g, g ^ flip) for g in range(group_count)])  76 us
    ppermute x20, starting transfers between devices, beside(): lax.ppermute(array, 'grp', [(g, g ^ flip) for g in range(group_count)])  24 us
    ppermute x9, waiting for transfers between devices, along(): return lax.ppermute(array, 'ray', pairs)  19.6 us
    unnamed x71, local copies, waits for them, and re-layouts  16.8 us
    pallas_call x5, Pallas kernels, forward(): pl.pallas_call(functools.partial(forward_kernel, first, last), out_shape=...  16.6 us
    pallas_call x1, Pallas kernels, render(): pl.pallas_call(functools.partial(render_kernel, ray_count), out_shape=jax...  14 us
    pallas_call x8, Pallas kernels, backward(): pl.pallas_call(body, out_shape=tuple(shapes), in_specs=[VMEM] * len(opera...  13.9 us
    ppermute x9, starting transfers between devices, along(): return lax.ppermute(array, 'ray', pairs)  13.8 us
  transfers between devices with their start and end apart: 42, of which 15 were waited for; matrix products, arithmetic and copies ran while one was open for 2% of the time, Pallas kernels for 20%

profile of v2, /device:TPU:8, one launch (start us, length us, event | category | flops | bytes accessed | tf_op | source)
XLA Modules:
  0.0 226.0 jit_solution(5070352939688761611)
XLA Ops:
  2.9 1.6 collective-permute-start.2
  5.7 1.9 collective-permute-start
  7.6 2.4 %collective-permute-start.12 = (bf16[2,64,1024]{2,1,0:T(8,128)(2,1)S(1)}, bf16[2,64,1024]{2,1,0:T(8,128)(2,1)S(1)}, u32[]{:S(2)}, u32[]{:S(2)}) collective-permute-start(bf16[2,64,1024]{2,1,0:T(8,128)(2,1)S(1)} %quarter.1), channel_id=1, source_target_pairs={{0,24},{8,16},{16,8},{24,0},{1,25},{9,17},{17,9},{25,1},{2,26},{10... | collective-permute-start | bytes 786440 | tf_op jit(solution)/shard_map/ppermute | solution.py:689
  13.1 9.4 %collective-permute-done.2 = bf16[2,64,1024]{2,1,0:T(8,128)(2,1)S(1)} collective-permute-done((bf16[2,64,1024]{2,1,0:T(8,128)(2,1)S(1)}, bf16[2,64,1024]{2,1,0:T(8,128)(2,1)S(1)}, u32[]{:S(2)}, u32[]{:S(2)}) %collective-permute-start.2) | collective-permute-done | bytes 262176 | tf_op jit(solution)/shard_map/ppermute | solution.py:696
  24.0 3.0 %collective-permute-done.1 = bf16[2,64,1024]{2,1,0:T(8,128)(2,1)S(1)} collective-permute-done((bf16[2,64,1024]{2,1,0:T(8,128)(2,1)S(1)}, bf16[2,64,1024]{2,1,0:T(8,128)(2,1)S(1)}, u32[]{:S(2)}, u32[]{:S(2)}) %collective-permute-start.1) | collective-permute-done | bytes 262176 | tf_op jit(solution)/shard_map/ppermute | solution.py:696
  27.0 1.8 collective-permute-done
  30.4 14.0 %render.1 = bf16[512,1024]{1,0:T(8,128)(2,1)} custom-call(s32[1]{0:T(128)} %bitcast.1.me_ref, s32[1,8]{1,0:T(1,128)} %owner_ref.3, s32[32,512]{1,0:T(8,128)} %lists_ref.1, f32[32,512]{1,0:T(8,128)} %opacity_ref.1, s32[1,512]{1,0:T(1,128)} %bitcast.29, s32[8,512]{1,0:T(8,128)} %reshape_squeeze.3.pixels_ref, bf16[1024,1024]{1,0:T(8,128)(2,1)} %features_ref.1), custom_call_target="tpu_custom_call" | custom-call | flops 3623878656 | bytes 3145728 | tf_op jit(solution)/shard_map/render/pallas_call | solution.py:109
  44.4 4.3 %all-to-all-start = ((bf16[8,64,1024]{2,1,0:T(8,128)(2,1)}), bf16[8,64,1024]{2,1,0:T(8,128)(2,1)}, u32[]{:S(2)}, u32[]{:S(2)}) async-start(bf16[8,64,1024]{2,1,0:T(8,128)(2,1)} %bitcast.19), calls=%async_computation | async-start | bytes 2097152 | tf_op jit(solution)/shard_map/all_to_all | solution.py:711
  52.5 32.7 %collective-permute-done.5.refs_1_.refs_4_ = bf16[3,2,64,1024]{3,2,1,0:T(8,128)(2,1)S(1)} collective-permute-done((bf16[3,2,64,1024]{3,2,1,0:T(8,128)(2,1)S(1)}, bf16[3,2,64,1024]{3,2,1,0:T(8,128)(2,1)S(1)}, u32[]{:S(2)}, u32[]{:S(2)}) %collective-permute-start.5) | collective-permute-done | bytes 786464 | tf_op jit(solution)/shard_map/ppermute | solution.py:689
  85.7 5.5 %tokens.1 = (bf16[512,1024]{1,0:T(8,128)(2,1)}, bf16[512,1024]{1,0:T(8,128)(2,1)}, bf16[1024,512]{1,0:T(8,128)(2,1)}) custom-call(s32[1]{0:T(128)} %bitcast.1.me_ref, s32[1,8]{1,0:T(1,128)} %owner_ref.3, s32[8,512]{1,0:T(8,128)} %reshape_squeeze.3.pixels_ref, bf16[512,1024]{1,0:T(8,128)(2,1)} %tokens_ref.1, f32[1,1024]{1,0:T(1,128)} %bitcast.25), custom_call_target="tpu_custom_call" | custom-call | flops 2147483648 | bytes 4194304 | tf_op jit(solution)/shard_map/tokens/pallas_call | solution.py:171
  91.3 1.6 copy-done.25
  92.9 2.2 forward.5
  95.1 3.0 %forward.6 = (bf16[2,3,64,512]{3,2,1,0:T(8,128)(2,1)S(1)}, f32[2,3,64,512]{3,2,1,0:T(8,128)S(1)}, f32[512,1024]{1,0:T(8,128)S(1)}) custom-call(bf16[1024,512]{1,0:T(8,128)(2,1)S(1)} %copy-done.25, bf16[3,2,64,1024]{3,2,1,0:T(8,128)(2,1)S(1)} %copy-done.8, bf16[3,2,64,1024]{3,2,1,0:T(8,128)(2,1)} %collective-permute-done.9.refs_2_.refs_4_, ...), custom_call_target="tpu_custom_call" | custom-call | flops 1610612736 | bytes 2097152 | tf_op jit(solution)/shard_map/forward/pallas_call | solution.py:539
  98.8 3.3 %forward.7 = (bf16[2,3,64,512]{3,2,1,0:T(8,128)(2,1)S(1)}, f32[2,3,64,512]{3,2,1,0:T(8,128)S(1)}, f32[512,1024]{1,0:T(8,128)S(1)}) custom-call(bf16[1024,512]{1,0:T(8,128)(2,1)S(1)} %copy-done.25, bf16[3,2,64,1024]{3,2,1,0:T(8,128)(2,1)} %collective-permute-done.7.refs_1_.refs_4_, bf16[3,2,64,1024]{3,2,1,0:T(8,128)(2,1)} %collective-permute-done.8.refs_2_.refs_4_, ...), custom_call_target="tpu_custom_call" | custom-call | flops 1610612736 | bytes 2097152 | tf_op jit(solution)/shard_map/forward/pallas_call | solution.py:539
  103.9 3.0 %forward.8 = (bf16[2,3,64,512]{3,2,1,0:T(8,128)(2,1)S(1)}, f32[2,3,64,512]{3,2,1,0:T(8,128)S(1)}, f32[512,1024]{1,0:T(8,128)S(1)}) custom-call(bf16[1024,512]{1,0:T(8,128)(2,1)S(1)} %copy-done.26, bf16[3,2,64,1024]{3,2,1,0:T(8,128)(2,1)S(1)} %copy-done.29, bf16[3,2,64,1024]{3,2,1,0:T(8,128)(2,1)} %collective-permute-done.6.refs_2_.refs_4_, ...), custom_call_target="tpu_custom_call" | custom-call | flops 1610612736 | bytes 2097152 | tf_op jit(solution)/shard_map/forward/pallas_call | solution.py:539
  117.0 5.1 %forward.9 = (bf16[2,3,64,512]{3,2,1,0:T(8,128)(2,1)S(1)}, f32[2,3,64,512]{3,2,1,0:T(8,128)S(1)}, bf16[512,1024]{1,0:T(8,128)(2,1)S(1)}, bf16[1024,512]{1,0:T(8,128)(2,1)S(1)}, f32[8,1024]{1,0:T(8,128)S(1)}) custom-call(bf16[1024,512]{1,0:T(8,128)(2,1)S(1)} %copy-done.27, bf16[3,2,64,1024]{3,2,1,0:T(8,128)(2,1)S(1)} %copy-done.11, ...), custom_call_target="tpu_custom_call" | custom-call | flops 1610612736 | bytes 2097152 | tf_op jit(solution)/shard_map/forward/pallas_call | solution.py:539
  122.2 2.3 %backward.10 = (bf16[2,4,64,1024]{3,2,1,0:T(8,128)(2,1)S(1)}, f32[1,1024]{1,0:T(1,128)S(1)}) custom-call(bf16[512,1024]{1,0:T(8,128)(2,1)S(1)} %get-tuple-element.59.refs_0_, bf16[1024,512]{1,0:T(8,128)(2,1)S(1)} %get-tuple-element.60.refs_1_, bf16[512,1024]{1,0:T(8,128)(2,1)S(1)} %copy-done, bf16[4,2,64,1024]{3,2,1,0:T(8,128)(2,1)S(1)} %copy-done.2, ...), custom_call_target="tpu_custom_call" | custom-call | flops 805306368 | bytes 3145728 | tf_op jit(solution)/shard_map/backward/pallas_call | solution.py:602
  124.9 2.3 %backward.8 = (bf16[2,4,64,1024]{3,2,1,0:T(8,128)(2,1)S(1)}, f32[1,1024]{1,0:T(1,128)S(1)}) custom-call(bf16[512,1024]{1,0:T(8,128)(2,1)S(1)} %get-tuple-element.59.refs_0_, bf16[1024,512]{1,0:T(8,128)(2,1)S(1)} %get-tuple-element.60.refs_1_, bf16[512,1024]{1,0:T(8,128)(2,1)S(1)} %copy-done, bf16[4,2,64,1024]{3,2,1,0:T(8,128)(2,1)S(1)} %copy-done.2, ...), custom_call_target="tpu_custom_call" | custom-call | flops 805306368 | bytes 3145728 | tf_op jit(solution)/shard_map/backward/pallas_call | solution.py:602
  127.5 2.3 %backward.12 = (bf16[2,4,64,1024]{3,2,1,0:T(8,128)(2,1)S(1)}, f32[1,1024]{1,0:T(1,128)S(1)}) custom-call(bf16[512,1024]{1,0:T(8,128)(2,1)S(1)} %get-tuple-element.59.refs_0_, bf16[1024,512]{1,0:T(8,128)(2,1)S(1)} %get-tuple-element.60.refs_1_, bf16[512,1024]{1,0:T(8,128)(2,1)S(1)} %copy-done, bf16[4,2,64,1024]{3,2,1,0:T(8,128)(2,1)S(1)} %copy-done.2, ...), custom_call_target="tpu_custom_call" | custom-call | flops 805306368 | bytes 3145728 | tf_op jit(solution)/shard_map/backward/pallas_call | solution.py:602
  131.6 2.4 %backward.11 = (bf16[4,64,1024]{2,1,0:T(8,128)(2,1)S(1)}, bf16[4,64,1024]{2,1,0:T(8,128)(2,1)S(1)}, f32[1,1024]{1,0:T(1,128)S(1)}) custom-call(bf16[512,1024]{1,0:T(8,128)(2,1)S(1)} %get-tuple-element.59.refs_0_, bf16[1024,512]{1,0:T(8,128)(2,1)S(1)} %get-tuple-element.60.refs_1_, bf16[512,1024]{1,0:T(8,128)(2,1)S(1)} %copy-done, ...), custom_call_target="tpu_custom_call" | custom-call | flops 805306368 | bytes 3145728 | tf_op jit(solution)/shard_map/backward/pallas_call | solution.py:602
  143.5 27.4 %collective-permute-done.37 = f32[3,1024]{1,0:T(4,128)S(1)} collective-permute-done((f32[3,1024]{1,0:T(4,128)S(1)}, f32[3,1024]{1,0:T(4,128)S(1)}, u32[]{:S(2)}, u32[]{:S(2)}) %collective-permute-start.37) | collective-permute-done | bytes 12320 | tf_op jit(solution)/shard_map/ppermute | solution.py:689
  172.5 2.2 collective-permute-done.38
  175.1 3.4 %collective-permute-done.39 = f32[3,1024]{1,0:T(4,128)S(1)} collective-permute-done((f32[3,1024]{1,0:T(4,128)S(1)}, f32[3,1024]{1,0:T(4,128)S(1)}, u32[]{:S(2)}, u32[]{:S(2)}) %collective-permute-start.39) | collective-permute-done | bytes 12320 | tf_op jit(solution)/shard_map/ppermute | solution.py:692
  180.5 2.4 %collective-permute-start.40 = (f32[3,1024]{1,0:T(4,128)S(1)}, f32[3,1024]{1,0:T(4,128)S(1)}, u32[]{:S(2)}, u32[]{:S(2)}) collective-permute-start(f32[3,1024]{1,0:T(4,128)S(1)} %add.70), channel_id=1, source_target_pairs={{0,4},{1,5},{2,6},{3,7},{4,0},{5,1},{6,2},{7,3},{8,12},{9,13},{10,... | collective-permute-start | bytes 36872 | tf_op jit(solution)/shard_map/ppermute | solution.py:692
  183.2 2.3 collective-permute-done.40
  185.5 4.6 %collective-permute-start.22 = (bf16[64,1024]{1,0:T(8,128)(2,1)S(1)}, bf16[64,1024]{1,0:T(8,128)(2,1)S(1)}, u32[]{:S(2)}, u32[]{:S(2)}) collective-permute-start(bf16[64,1024]{1,0:T(8,128)(2,1)S(1)} %get-tuple-element.82), channel_id=1, source_target_pairs={{0,4},{1,5},{2,6},{3,7},{4,0},{5,1},{6,2},{7,3},{8,12},{9,13},{10,... | collective-permute-start | bytes 393224 | tf_op jit(solution)/shard_map/ppermute | solution.py:696
  191.3 9.4 %collective-permute-done.28.refs_2_ = bf16[4,64,1024]{2,1,0:T(8,128)(2,1)S(1)} collective-permute-done((bf16[4,64,1024]{2,1,0:T(8,128)(2,1)S(1)}, bf16[4,64,1024]{2,1,0:T(8,128)(2,1)S(1)}, u32[]{:S(2)}, u32[]{:S(2)}) %collective-permute-start.28) | collective-permute-done | bytes 524320 | tf_op jit(solution)/shard_map/ppermute | solution.py:689
  203.7 1.6 collective-permute-start.32
  207.5 2.7 %collective-permute-done.30 = bf16[64,1024]{1,0:T(8,128)(2,1)S(1)} collective-permute-done((bf16[64,1024]{1,0:T(8,128)(2,1)S(1)}, bf16[64,1024]{1,0:T(8,128)(2,1)S(1)}, u32[]{:S(2)}, u32[]{:S(2)}) %collective-permute-start.30) | collective-permute-done | bytes 131104 | tf_op jit(solution)/shard_map/ppermute | solution.py:696
  211.6 1.8 collective-permute-done.32
  213.5 2.6 %collective-permute-start.35 = (bf16[64,1024]{1,0:T(8,128)(2,1)S(1)}, bf16[64,1024]{1,0:T(8,128)(2,1)S(1)}, u32[]{:S(2)}, u32[]{:S(2)}) collective-permute-start(bf16[64,1024]{1,0:T(8,128)(2,1)S(1)} %add_convert_fusion.a_ref), channel_id=1, source_target_pairs={{0,24},{8,16},{16,8},{24,0},{1,25},{9,17},{17,9},{25,1},{2,26},{10... | collective-permute-start | bytes 393224 | tf_op jit(solution)/shard_map/ppermute | solution.py:689
  220.2 2.5 %collective-permute-done.34.c_ref = bf16[64,1024]{1,0:T(8,128)(2,1)S(1)} collective-permute-done((bf16[64,1024]{1,0:T(8,128)(2,1)S(1)}, bf16[64,1024]{1,0:T(8,128)(2,1)S(1)}, u32[]{:S(2)}, u32[]{:S(2)}) %collective-permute-start.34) | collective-permute-done | bytes 131104 | tf_op jit(solution)/shard_map/ppermute | solution.py:689
  (159 shorter events, 56.0 us)
Async XLA Ops:
  2.9 19.6 %collective-permute-start.2 = (bf16[2,64,1024]{2,1,0:T(8,128)(2,1)S(1)}, bf16[2,64,1024]{2,1,0:T(8,128)(2,1)S(1)}, u32[]{:S(2)}, u32[]{:S(2)}) collective-permute-start(bf16[2,64,1024]{2,1,0:T(8,128)(2,1)S(1)} %quarter.1), channel_id=1, source_target_pairs={{0,2},{1,3},{2,4},{3,5},{4,6},{5,7},{6,0},{7,1},{8,10},{9,11},{10,... | collective-permute-start | bytes 786440 | tf_op jit(solution)/shard_map/ppermute | solution.py:696
  4.6 22.4 %collective-permute-start.1 = (bf16[2,64,1024]{2,1,0:T(8,128)(2,1)S(1)}, bf16[2,64,1024]{2,1,0:T(8,128)(2,1)S(1)}, u32[]{:S(2)}, u32[]{:S(2)}) collective-permute-start(bf16[2,64,1024]{2,1,0:T(8,128)(2,1)S(1)} %quarter.1), channel_id=1, source_target_pairs={{0,4},{1,5},{2,6},{3,7},{4,0},{5,1},{6,2},{7,3},{8,12},{9,13},{10,... | collective-permute-start | bytes 786440 | tf_op jit(solution)/shard_map/ppermute | solution.py:696
  5.7 23.1 %collective-permute-start = (bf16[2,64,1024]{2,1,0:T(8,128)(2,1)S(1)}, bf16[2,64,1024]{2,1,0:T(8,128)(2,1)S(1)}, u32[]{:S(2)}, u32[]{:S(2)}) collective-permute-start(bf16[2,64,1024]{2,1,0:T(8,128)(2,1)S(1)} %quarter.1), channel_id=1, source_target_pairs={{0,6},{1,7},{2,0},{3,1},{4,2},{5,3},{6,4},{7,5},{8,14},{9,15},{10,... | collective-permute-start | bytes 786440 | tf_op jit(solution)/shard_map/ppermute | solution.py:696
  7.6 42.7 %collective-permute-start.12 = (bf16[2,64,1024]{2,1,0:T(8,128)(2,1)S(1)}, bf16[2,64,1024]{2,1,0:T(8,128)(2,1)S(1)}, u32[]{:S(2)}, u32[]{:S(2)}) collective-permute-start(bf16[2,64,1024]{2,1,0:T(8,128)(2,1)S(1)} %quarter.1), channel_id=1, source_target_pairs={{0,24},{8,16},{16,8},{24,0},{1,25},{9,17},{17,9},{25,1},{2,26},{10... | collective-permute-start | bytes 786440 | tf_op jit(solution)/shard_map/ppermute | solution.py:689
  10.1 40.2 %collective-permute-start.11 = (bf16[2,64,1024]{2,1,0:T(8,128)(2,1)S(1)}, bf16[2,64,1024]{2,1,0:T(8,128)(2,1)S(1)}, u32[]{:S(2)}, u32[]{:S(2)}) collective-permute-start(bf16[2,64,1024]{2,1,0:T(8,128)(2,1)S(1)} %quarter.1), channel_id=1, source_target_pairs={{0,16},{8,24},{16,0},{24,8},{1,17},{9,25},{17,1},{25,9},{2,18},{10... | collective-permute-start | bytes 786440 | tf_op jit(solution)/shard_map/ppermute | solution.py:689
  22.5 27.8 %collective-permute-start.10 = (bf16[2,64,1024]{2,1,0:T(8,128)(2,1)S(1)}, bf16[2,64,1024]{2,1,0:T(8,128)(2,1)}, u32[]{:S(2)}, u32[]{:S(2)}) collective-permute-start(bf16[2,64,1024]{2,1,0:T(8,128)(2,1)S(1)} %quarter.1), channel_id=1, source_target_pairs={{0,8},{8,0},{16,24},{24,16},{1,9},{9,1},{17,25},{25,17},{2,10},{10... | collective-permute-start | bytes 786440 | tf_op jit(solution)/shard_map/ppermute | solution.py:689
  28.9 23.3 %collective-permute-start.7 = (bf16[3,2,64,1024]{3,2,1,0:T(8,128)(2,1)S(1)}, bf16[3,2,64,1024]{3,2,1,0:T(8,128)(2,1)}, u32[]{:S(2)}, u32[]{:S(2)}) collective-permute-start(bf16[3,2,64,1024]{3,2,1,0:T(8,128)(2,1)S(1)} %pad_maximum_fusion.1.refs_1_.refs_4_), channel_id=1, source_target_pairs={{0,8},{8,0},{16,24},{24,16},{1,9},{9,1},{17,25},{25,17},{2,10},{10... | collective-permute-start | bytes 2359304 | tf_op jit(solution)/shard_map/ppermute | solution.py:689
  44.4 66.3 %all-to-all-start = ((bf16[8,64,1024]{2,1,0:T(8,128)(2,1)}), bf16[8,64,1024]{2,1,0:T(8,128)(2,1)}, u32[]{:S(2)}, u32[]{:S(2)}) async-start(bf16[8,64,1024]{2,1,0:T(8,128)(2,1)} %bitcast.19), calls=%async_computation | async-start | bytes 2097152 | tf_op jit(solution)/shard_map/all_to_all | solution.py:711
  48.8 36.4 %collective-permute-start.5 = (bf16[3,2,64,1024]{3,2,1,0:T(8,128)(2,1)S(1)}, bf16[3,2,64,1024]{3,2,1,0:T(8,128)(2,1)S(1)}, u32[]{:S(2)}, u32[]{:S(2)}) collective-permute-start(bf16[3,2,64,1024]{3,2,1,0:T(8,128)(2,1)S(1)} %pad_maximum_fusion.1.refs_1_.refs_4_), channel_id=1, source_target_pairs={{0,16},{8,24},{16,0},{24,8},{1,17},{9,25},{17,1},{25,9},{2,18},{10... | collective-permute-start | bytes 2359304 | tf_op jit(solution)/shard_map/ppermute | solution.py:689
  51.4 39.9 %collective-permute-start.13 = (bf16[4,2,64,1024]{3,2,1,0:T(8,128)(2,1)S(1)}, bf16[4,2,64,1024]{3,2,1,0:T(8,128)(2,1)S(1)}, u32[]{:S(2)}, u32[]{:S(2)}) collective-permute-start(bf16[4,2,64,1024]{3,2,1,0:T(8,128)(2,1)S(1)} %pad_maximum_fusion.refs_1_.refs_3_), channel_id=1, source_target_pairs={{0,1},{1,0},{2,3},{3,2},{4,5},{5,4},{6,7},{7,6},{8,9},{9,8},{10,11... | collective-permute-start | bytes 3145736 | tf_op jit(solution)/shard_map/ppermute | solution.py:692
  51.5 33.8 %collective-permute-start.3 = (bf16[3,2,64,1024]{3,2,1,0:T(8,128)(2,1)S(1)}, bf16[3,2,64,1024]{3,2,1,0:T(8,128)(2,1)S(1)}, u32[]{:S(2)}, u32[]{:S(2)}) collective-permute-start(bf16[3,2,64,1024]{3,2,1,0:T(8,128)(2,1)S(1)} %pad_maximum_fusion.1.refs_1_.refs_4_), channel_id=1, source_target_pairs={{0,24},{8,16},{16,8},{24,0},{1,25},{9,17},{17,9},{25,1},{2,26},{10... | collective-permute-start | bytes 2359304 | tf_op jit(solution)/shard_map/ppermute | solution.py:689
  52.0 43.1 %collective-permute-start.9 = (bf16[3,2,64,1024]{3,2,1,0:T(8,128)(2,1)S(1)}, bf16[3,2,64,1024]{3,2,1,0:T(8,128)(2,1)}, u32[]{:S(2)}, u32[]{:S(2)}) collective-permute-start(bf16[3,2,64,1024]{3,2,1,0:T(8,128)(2,1)S(1)} %pad_maximum_fusion.1.refs_1_.refs_4_), channel_id=1, source_target_pairs={{0,1},{1,0},{2,3},{3,2},{4,5},{5,4},{6,7},{7,6},{8,9},{9,8},{10,11... | collective-permute-start | bytes 2359304 | tf_op jit(solution)/shard_map/ppermute | solution.py:692
  52.2 46.7 %collective-permute-start.8 = (bf16[3,2,64,1024]{3,2,1,0:T(8,128)(2,1)}, bf16[3,2,64,1024]{3,2,1,0:T(8,128)(2,1)}, u32[]{:S(2)}, u32[]{:S(2)}) collective-permute-start(bf16[3,2,64,1024]{3,2,1,0:T(8,128)(2,1)} %collective-permute-done.7.refs_1_.refs_4_), channel_id=1, source_target_pairs={{0,1},{1,0},{2,3},{3,2},{4,5},{5,4},{6,7},{7,6},{8,9},{9,8},{10,11... | collective-permute-start | bytes 2359304 | tf_op jit(solution)/shard_map/ppermute | solution.py:692
  85.2 18.6 %collective-permute-start.6 = (bf16[3,2,64,1024]{3,2,1,0:T(8,128)(2,1)S(1)}, bf16[3,2,64,1024]{3,2,1,0:T(8,128)(2,1)}, u32[]{:S(2)}, u32[]{:S(2)}) collective-permute-start(bf16[3,2,64,1024]{3,2,1,0:T(8,128)(2,1)S(1)} %collective-permute-done.5.refs_1_.refs_4_), channel_id=1, source_target_pairs={{0,1},{1,0},{2,3},{3,2},{4,5},{5,4},{6,7},{7,6},{8,9},{9,8},{10,11... | collective-permute-start | bytes 2359304 | tf_op jit(solution)/shard_map/ppermute | solution.py:692
  85.2 24.6 %collective-permute-start.4 = (bf16[3,2,64,1024]{3,2,1,0:T(8,128)(2,1)S(1)}, bf16[3,2,64,1024]{3,2,1,0:T(8,128)(2,1)S(1)}, u32[]{:S(2)}, u32[]{:S(2)}) collective-permute-start(bf16[3,2,64,1024]{3,2,1,0:T(8,128)(2,1)S(1)} %collective-permute-done.3.refs_1_.refs_4_), channel_id=1, source_target_pairs={{0,1},{1,0},{2,3},{3,2},{4,5},{5,4},{6,7},{7,6},{8,9},{9,8},{10,11... | collective-permute-start | bytes 2359304 | tf_op jit(solution)/shard_map/ppermute | solution.py:692
  134.0 46.0 %collective-permute-start.16 = (bf16[4,64,1024]{2,1,0:T(8,128)(2,1)S(1)}, bf16[4,64,1024]{2,1,0:T(8,128)(2,1)S(1)}, u32[]{:S(2)}, u32[]{:S(2)}) collective-permute-start(bf16[4,64,1024]{2,1,0:T(8,128)(2,1)S(1)} %get-tuple-element.71), channel_id=1, source_target_pairs={{0,8},{8,0},{16,24},{24,16},{1,9},{9,1},{17,25},{25,17},{2,10},{10... | collective-permute-start | bytes 1572872 | tf_op jit(solution)/shard_map/ppermute | solution.py:689
  138.4 51.7 %collective-permute-start.27 = (bf16[4,64,1024]{2,1,0:T(8,128)(2,1)S(1)}, bf16[4,64,1024]{2,1,0:T(8,128)(2,1)S(1)}, u32[]{:S(2)}, u32[]{:S(2)}) collective-permute-start(bf16[4,64,1024]{2,1,0:T(8,128)(2,1)S(1)} %get-tuple-element.85), channel_id=1, source_target_pairs={{0,8},{8,0},{16,24},{24,16},{1,9},{9,1},{17,25},{25,17},{2,10},{10... | collective-permute-start | bytes 1572872 | tf_op jit(solution)/shard_map/ppermute | solution.py:689
  139.9 40.5 %collective-permute-start.18 = (bf16[4,64,1024]{2,1,0:T(8,128)(2,1)S(1)}, bf16[4,64,1024]{2,1,0:T(8,128)(2,1)S(1)}, u32[]{:S(2)}, u32[]{:S(2)}) collective-permute-start(bf16[4,64,1024]{2,1,0:T(8,128)(2,1)S(1)} %get-tuple-element.75), channel_id=1, source_target_pairs={{0,16},{8,24},{16,0},{24,8},{1,17},{9,25},{17,1},{25,9},{2,18},{10... | collective-permute-start | bytes 1572872 | tf_op jit(solution)/shard_map/ppermute | solution.py:689
  141.5 41.4 %collective-permute-start.20 = (bf16[4,64,1024]{2,1,0:T(8,128)(2,1)S(1)}, bf16[4,64,1024]{2,1,0:T(8,128)(2,1)S(1)}, u32[]{:S(2)}, u32[]{:S(2)}) collective-permute-start(bf16[4,64,1024]{2,1,0:T(8,128)(2,1)S(1)} %get-tuple-element.79), channel_id=1, source_target_pairs={{0,24},{8,16},{16,8},{24,0},{1,25},{9,17},{17,9},{25,1},{2,26},{10... | collective-permute-start | bytes 1572872 | tf_op jit(solution)/shard_map/ppermute | solution.py:689
  142.0 29.0 %collective-permute-start.37 = (f32[3,1024]{1,0:T(4,128)S(1)}, f32[3,1024]{1,0:T(4,128)S(1)}, u32[]{:S(2)}, u32[]{:S(2)}) collective-permute-start(f32[3,1024]{1,0:T(4,128)S(1)} %fusion), channel_id=1, source_target_pairs={{0,8},{8,0},{16,24},{24,16},{1,9},{9,1},{17,25},{25,17},{2,10},{10... | collective-permute-start | bytes 36872 | tf_op jit(solution)/shard_map/ppermute | solution.py:689
  178.4 22.2 %collective-permute-start.28 = (bf16[4,64,1024]{2,1,0:T(8,128)(2,1)S(1)}, bf16[4,64,1024]{2,1,0:T(8,128)(2,1)S(1)}, u32[]{:S(2)}, u32[]{:S(2)}) collective-permute-start(bf16[4,64,1024]{2,1,0:T(8,128)(2,1)S(1)} %get-tuple-element.86), channel_id=1, source_target_pairs={{0,16},{8,24},{16,0},{24,8},{1,17},{9,25},{17,1},{25,9},{2,18},{10... | collective-permute-start | bytes 1572872 | tf_op jit(solution)/shard_map/ppermute | solution.py:689
  180.0 20.7 %collective-permute-start.29 = (bf16[4,64,1024]{2,1,0:T(8,128)(2,1)S(1)}, bf16[4,64,1024]{2,1,0:T(8,128)(2,1)S(1)}, u32[]{:S(2)}, u32[]{:S(2)}) collective-permute-start(bf16[4,64,1024]{2,1,0:T(8,128)(2,1)S(1)} %get-tuple-element.87), channel_id=1, source_target_pairs={{0,24},{8,16},{16,8},{24,0},{1,25},{9,17},{17,9},{25,1},{2,26},{10... | collective-permute-start | bytes 1572872 | tf_op jit(solution)/shard_map/ppermute | solution.py:689
  183.2 20.6 %collective-permute-start.21 = (bf16[64,1024]{1,0:T(8,128)(2,1)S(1)}, bf16[64,1024]{1,0:T(8,128)(2,1)S(1)}, u32[]{:S(2)}, u32[]{:S(2)}) collective-permute-start(bf16[64,1024]{1,0:T(8,128)(2,1)S(1)} %get-tuple-element.81), channel_id=1, source_target_pairs={{0,2},{1,3},{2,4},{3,5},{4,6},{5,7},{6,0},{7,1},{8,10},{9,11},{10,... | collective-permute-start | bytes 393224 | tf_op jit(solution)/shard_map/ppermute | solution.py:696
  185.5 19.9 %collective-permute-start.22 = (bf16[64,1024]{1,0:T(8,128)(2,1)S(1)}, bf16[64,1024]{1,0:T(8,128)(2,1)S(1)}, u32[]{:S(2)}, u32[]{:S(2)}) collective-permute-start(bf16[64,1024]{1,0:T(8,128)(2,1)S(1)} %get-tuple-element.82), channel_id=1, source_target_pairs={{0,4},{1,5},{2,6},{3,7},{4,0},{5,1},{6,2},{7,3},{8,12},{9,13},{10,... | collective-permute-start | bytes 393224 | tf_op jit(solution)/shard_map/ppermute | solution.py:696
  190.1 15.3 %collective-permute-start.23 = (bf16[64,1024]{1,0:T(8,128)(2,1)S(1)}, bf16[64,1024]{1,0:T(8,128)(2,1)S(1)}, u32[]{:S(2)}, u32[]{:S(2)}) collective-permute-start(bf16[64,1024]{1,0:T(8,128)(2,1)S(1)} %get-tuple-element.83), channel_id=1, source_target_pairs={{0,6},{1,7},{2,0},{3,1},{4,2},{5,3},{6,4},{7,5},{8,14},{9,15},{10,... | collective-permute-start | bytes 393224 | tf_op jit(solution)/shard_map/ppermute | solution.py:696
  200.9 9.3 %collective-permute-start.30 = (bf16[64,1024]{1,0:T(8,128)(2,1)S(1)}, bf16[64,1024]{1,0:T(8,128)(2,1)S(1)}, u32[]{:S(2)}, u32[]{:S(2)}) collective-permute-start(bf16[64,1024]{1,0:T(8,128)(2,1)S(1)} %get-tuple-element.89), channel_id=1, source_target_pairs={{0,2},{1,3},{2,4},{3,5},{4,6},{5,7},{6,0},{7,1},{8,10},{9,11},{10,... | collective-permute-start | bytes 393224 | tf_op jit(solution)/shard_map/ppermute | solution.py:696
  202.4 9.2 %collective-permute-start.31 = (bf16[64,1024]{1,0:T(8,128)(2,1)S(1)}, bf16[64,1024]{1,0:T(8,128)(2,1)S(1)}, u32[]{:S(2)}, u32[]{:S(2)}) collective-permute-start(bf16[64,1024]{1,0:T(8,128)(2,1)S(1)} %get-tuple-element.90), channel_id=1, source_target_pairs={{0,4},{1,5},{2,6},{3,7},{4,0},{5,1},{6,2},{7,3},{8,12},{9,13},{10,... | collective-permute-start | bytes 393224 | tf_op jit(solution)/shard_map/ppermute | solution.py:696
  203.7 9.7 %collective-permute-start.32 = (bf16[64,1024]{1,0:T(8,128)(2,1)S(1)}, bf16[64,1024]{1,0:T(8,128)(2,1)S(1)}, u32[]{:S(2)}, u32[]{:S(2)}) collective-permute-start(bf16[64,1024]{1,0:T(8,128)(2,1)S(1)} %get-tuple-element.91), channel_id=1, source_target_pairs={{0,6},{1,7},{2,0},{3,1},{4,2},{5,3},{6,4},{7,5},{8,14},{9,15},{10,... | collective-permute-start | bytes 393224 | tf_op jit(solution)/shard_map/ppermute | solution.py:696
  205.4 10.7 %collective-permute-start.26 = (bf16[64,1024]{1,0:T(8,128)(2,1)S(1)}, bf16[64,1024]{1,0:T(8,128)(2,1)S(1)}, u32[]{:S(2)}, u32[]{:S(2)}) collective-permute-start(bf16[64,1024]{1,0:T(8,128)(2,1)S(1)} %add_convert_fusion.1.a_ref), channel_id=1, source_target_pairs={{0,24},{8,16},{16,8},{24,0},{1,25},{9,17},{17,9},{25,1},{2,26},{10... | collective-permute-start | bytes 393224 | tf_op jit(solution)/shard_map/ppermute | solution.py:689
  207.0 11.2 %collective-permute-start.25 = (bf16[64,1024]{1,0:T(8,128)(2,1)S(1)}, bf16[64,1024]{1,0:T(8,128)(2,1)S(1)}, u32[]{:S(2)}, u32[]{:S(2)}) collective-permute-start(bf16[64,1024]{1,0:T(8,128)(2,1)S(1)} %add_convert_fusion.1.a_ref), channel_id=1, source_target_pairs={{0,16},{8,24},{16,0},{24,8},{1,17},{9,25},{17,1},{25,9},{2,18},{10... | collective-permute-start | bytes 393224 | tf_op jit(solution)/shard_map/ppermute | solution.py:689
  210.2 7.9 %collective-permute-start.24 = (bf16[64,1024]{1,0:T(8,128)(2,1)S(1)}, bf16[64,1024]{1,0:T(8,128)(2,1)S(1)}, u32[]{:S(2)}, u32[]{:S(2)}) collective-permute-start(bf16[64,1024]{1,0:T(8,128)(2,1)S(1)} %add_convert_fusion.1.a_ref), channel_id=1, source_target_pairs={{0,8},{8,0},{16,24},{24,16},{1,9},{9,1},{17,25},{25,17},{2,10},{10... | collective-permute-start | bytes 393224 | tf_op jit(solution)/shard_map/ppermute | solution.py:689
  216.2 7.6 %collective-permute-start.33 = (bf16[64,1024]{1,0:T(8,128)(2,1)S(1)}, bf16[64,1024]{1,0:T(8,128)(2,1)S(1)}, u32[]{:S(2)}, u32[]{:S(2)}) collective-permute-start(bf16[64,1024]{1,0:T(8,128)(2,1)S(1)} %add_convert_fusion.a_ref), channel_id=1, source_target_pairs={{0,8},{8,0},{16,24},{24,16},{1,9},{9,1},{17,25},{25,17},{2,10},{10... | collective-permute-start | bytes 393224 | tf_op jit(solution)/shard_map/ppermute | solution.py:689
  (45 other events, 168.8 us)

commit v3 on v2

--- a/solution.py
+++ b/solution.py
@@ -12,8 +12,10 @@
 BF16 = jnp.bfloat16
 VMEM_BYTES = 56 * 1024 * 1024
 SMALL_VMEM_BYTES = 28 * 1024 * 1024
+COST = pl.CostEstimate(flops=1 << 20, bytes_accessed=1 << 16, transcendentals=0)
 SMEM = pl.BlockSpec(memory_space=pltpu.SMEM)
 VMEM = pl.BlockSpec(memory_space=pltpu.VMEM)
+ANY = pl.BlockSpec(memory_space=pl.ANY)
 
 
 def params(**more):
@@ -52,8 +54,9 @@
 
 def render_kernel(
     ray_count, me_ref, owner_ref, lists_ref, opacity_ref, counts_ref, pixels_ref, features_ref,
-    out_ref, ids_ref, share_ref, table_ref, send_ref,
+    *refs,
 ):
+    out_ref, ids_ref, share_ref, table_ref, send_ref = refs[-5:]
     depth, rays = lists_ref.shape
     gauss = features_ref.shape[0]
     width = features_ref.shape[1]
@@ -102,14 +105,14 @@
         out_ref[:, cols] = dot_nn(send_ref[...], rendered).astype(BF16)
 
 
-def render(me, owner, lists, opacity, counts, pixels, features):
+def render(me, owner, lists, opacity, counts, pixels, features, after=()):
     ray_count = pixels.shape[0]
     depth, rays = lists.shape
     gauss, width = features.shape
     return pl.pallas_call(
         functools.partial(render_kernel, ray_count),
         out_shape=jax.ShapeDtypeStruct((rays, width), BF16),
-        in_specs=[SMEM, SMEM, VMEM, VMEM, VMEM, VMEM, VMEM],
+        in_specs=[SMEM, SMEM, VMEM, VMEM, VMEM, VMEM, VMEM] + [ANY] * len(after),
         out_specs=VMEM,
         scratch_shapes=[
             pltpu.VMEM((depth, rays), jnp.int32),
@@ -118,12 +121,9 @@
             pltpu.VMEM((rays, rays), BF16),
         ],
         compiler_params=params(),
-        cost_estimate=pl.CostEstimate(
-            flops=2 * rays * width * (gauss + rays) + 3 * depth * rays * gauss * 40,
-            bytes_accessed=2 * (gauss + rays) * width, transcendentals=0,
-        ),
+        cost_estimate=COST,
         name="render",
-    )(me, owner, lists, opacity, counts, pixels, features)
+    )(me, owner, lists, opacity, counts, pixels, features, *after)
 
 
 def tokens_kernel(
@@ -179,9 +179,7 @@
         out_specs=(VMEM, VMEM, VMEM),
         scratch_shapes=[pltpu.VMEM((rows, rows), BF16)],
         compiler_params=params(),
-        cost_estimate=pl.CostEstimate(
-            flops=2 * rows * rows * width * 4, bytes_accessed=8 * rows * width, transcendentals=0
-        ),
+        cost_estimate=COST,
         name="tokens",
     )(me, owner, pixels, tokens, gain)
 
@@ -221,11 +219,7 @@
             pl.BlockSpec((rows, chunk), lambda j: (0, j)),
         ),
         compiler_params=params(dimension_semantics=("arbitrary",)),
-        cost_estimate=pl.CostEstimate(
-            flops=2 * rows * width * chunks * chunk * 3,
-            bytes_accessed=2 * width * chunks * chunk + 6 * rows * chunks * chunk,
-            transcendentals=2 * rows * chunks * chunk,
-        ),
+        cost_estimate=COST,
         name="up",
     )(normed, up)
 
@@ -309,11 +303,7 @@
         ),
         scratch_shapes=[pltpu.VMEM((rows, width), F32)],
         compiler_params=params(dimension_semantics=("arbitrary",)),
-        cost_estimate=pl.CostEstimate(
-            flops=4 * rows * width * chunks * chunk,
-            bytes_accessed=4 * width * chunks * chunk + 4 * rows * chunks * chunk,
-            transcendentals=0,
-        ),
+        cost_estimate=COST,
         name="down",
     )(act, down, tokens, target, scale)
 
@@ -362,11 +352,7 @@
             pl.BlockSpec((width, 1), lambda j: (0, 0)),
         ),
         compiler_params=params(dimension_semantics=("arbitrary",)),
-        cost_estimate=pl.CostEstimate(
-            flops=4 * rows * width * chunks * chunk,
-            bytes_accessed=6 * width * chunks * chunk + 4 * rows * chunks * chunk,
-            transcendentals=0,
-        ),
+        cost_estimate=COST,
         name="back",
     )(back, down, slope, normed_t, up, gain)
 
@@ -451,7 +437,7 @@
         out_specs=VMEM,
         scratch_shapes=[pltpu.VMEM((chunk, width), BF16)],
         compiler_params=small_params(),
-        cost_estimate=pl.CostEstimate(flops=0, bytes_accessed=6 * width * chunk, transcendentals=0),
+        cost_estimate=COST,
         name="quarter",
     )(group, up, down)
 
@@ -543,10 +529,7 @@
         out_specs=tuple([VMEM] * len(shapes)),
         scratch_shapes=scratch,
         compiler_params=small_params(),
-        cost_estimate=pl.CostEstimate(
-            flops=8 * rows * width * count * part * 2,
-            bytes_accessed=4 * rows * width, transcendentals=0,
-        ),
+        cost_estimate=COST,
         name="forward",
     )(*operands)
 
@@ -554,8 +537,8 @@
 def backward_kernel(side, quarter, add, *refs):
     refs = list(refs)
     back_ref, back_t_ref, normed_ref, near_ref, far_ref = refs[:5]
-    act_near, slope_near, act_far, slope_far = refs[5:9]
-    del refs[:9]
+    act_near, slope_near, act_far, slope_far, gain_in = refs[5:10]
+    del refs[:10]
     arrived = refs.pop(0) if add else None
     up_ref, down_ref, gain_ref = refs
     part, width = near_ref.shape[-2:]
@@ -571,7 +554,7 @@
     back_hidden = (back_act * slope).astype(BF16)
     grad_up = dot_nn(back_hidden, normed_ref[...])
     up = joined(near_ref[quarter, 0], far_ref[:, 0]).astype(F32)
-    gain_ref[...] = jnp.sum(grad_up * up, axis=0, keepdims=True)
+    gain_ref[...] = gain_in[...] + jnp.sum(grad_up * up, axis=0, keepdims=True)
     grad_down = dot_nn(joined(act_near[side, quarter], act_far[side]), back_ref[...])
     if add:
         grad_up += arrived[0].reshape(chunk, width).astype(F32)
@@ -580,12 +563,14 @@
     down_ref[...] = grad_down.astype(BF16).reshape(down_ref.shape)
 
 
-def backward(side, quarter, common, near, far, act_near, slope_near, act_far, slope_far, arrived):
+def backward(
+    side, quarter, common, near, far, act_near, slope_near, act_far, slope_far, gain, arrived
+):
     back, back_t, normed = common
     rows, width = back.shape
     part = near.shape[2]
     count = far.shape[0] + 1
-    operands = [back, back_t, normed, near, far, act_near, slope_near, act_far, slope_far]
+    operands = [back, back_t, normed, near, far, act_near, slope_near, act_far, slope_far, gain]
     if arrived is None:
         def body(*refs):
             grads, gain_ref = refs[-2:]
@@ -605,61 +590,106 @@
         in_specs=[VMEM] * len(operands),
         out_specs=tuple([VMEM] * len(shapes)),
         compiler_params=small_params(),
-        cost_estimate=pl.CostEstimate(
-            flops=6 * rows * width * count * part,
-            bytes_accessed=6 * rows * width, transcendentals=0,
-        ),
+        cost_estimate=COST,
         name="backward",
     )(*operands)
 
 
-def total_kernel(*refs):
-    ins, outs = refs[:4], refs[4:]
+def total_kernel(count, *refs):
+    ins, outs = refs[:4], refs[-count:]
     for index, out in enumerate(outs):
         total = ins[0][index].astype(F32)
         for ref in ins[1:]:
             total = total + ref[index].astype(F32)
         out[...] = total.astype(BF16)
-
-
-def totals(parts):
+    if len(refs) > 4 + count:
+        refs[5][...] = refs[4][...]
+
+
+def totals(parts, vector=None):
     count, part, width = parts[0].shape
-    return pl.pallas_call(
-        total_kernel,
-        out_shape=tuple([jax.ShapeDtypeStruct((part, width), BF16)] * count),
-        in_specs=[VMEM] * 4,
-        out_specs=tuple([VMEM] * count),
+    operands, shapes = list(parts), []
+    if vector is not None:
+        operands.append(vector)
+        shapes.append(jax.ShapeDtypeStruct(vector.shape, F32))
+    shapes += [jax.ShapeDtypeStruct((part, width), BF16)] * count
+    return pl.pallas_call(
+        functools.partial(total_kernel, count),
+        out_shape=tuple(shapes),
+        in_specs=[VMEM] * len(operands),
+        out_specs=tuple([VMEM] * len(shapes)),
         compiler_params=small_params(),
-        cost_estimate=pl.CostEstimate(
-            flops=4 * count * part * width, bytes_accessed=10 * count * part * width,
-            transcendentals=0,
-        ),
+        cost_estimate=COST,
         name="totals",
-    )(*parts)
-
-
-def place_kernel(turn, group_ref, a_ref, b_ref, c_ref, d_ref, out_ref, held_ref):
-    part = a_ref.shape[0]
+    )(*operands)
+
+
+def collect_kernel(count, *refs):
+    out_ref = refs[-1]
+    part, width = refs[0].shape
+    total = refs[0][...].astype(F32)
+    for ref in refs[1:count]:
+        total = total + ref[...].astype(F32)
+    out_ref[pl.ds(0, part), :] = total.astype(BF16)
+    if len(refs) > count + 1:
+        rest = refs[count][...]
+        pieces = []
+        for _ in range(3):
+            piece = rest.astype(BF16).astype(F32)
+            pieces.append(piece)
+            rest = rest - piece
+        pieces.append(jnp.zeros_like(rest))
+        out_ref[pl.ds(part, 32), :] = jnp.concatenate(pieces, axis=0).astype(BF16)
+
+
+def collect(parts, vector=None):
+    part, width = parts[0].shape
+    operands = list(parts) + ([] if vector is None else [vector])
+    return pl.pallas_call(
+        functools.partial(collect_kernel, len(parts)),
+        out_shape=jax.ShapeDtypeStruct((part + (0 if vector is None else 32), width), BF16),
+        in_specs=[VMEM] * len(operands),
+        out_specs=VMEM,
+        compiler_params=small_params(),
+        cost_estimate=COST,
+        name="collect",
+    )(*operands)
+
+
+def place_kernel(part, group_ref, a_ref, b_ref, c_ref, d_ref, *refs):
     group = group_ref[0]
-    for index, ref in enumerate((a_ref, b_ref, c_ref, d_ref)):
+    held_ref = refs[-1]
+    quarters = (a_ref, b_ref, c_ref, d_ref)
+    for index, ref in enumerate(quarters):
         first = pl.multiple_of(jnp.bitwise_xor(group, index) * part, part)
-        held_ref[pl.ds(first, part), :] = ref[...].astype(F32)
-    out_ref[...] = held_ref[...].T if turn else held_ref[...]
-
-
-def place_quarters(group, quarters, turn):
-    part, width = quarters[0].shape
-    shape = (width, 4 * part) if turn else (4 * part, width)
-    return pl.pallas_call(
-        functools.partial(place_kernel, turn),
-        out_shape=jax.ShapeDtypeStruct(shape, F32),
+        held_ref[pl.ds(first, part), :] = ref[pl.ds(0, part), :].astype(F32)
+    if len(refs) == 2:
+        refs[0][...] = held_ref[...]
+        return
+    refs[0][...] = held_ref[...].T
+    vectors = []
+    for ref in quarters:
+        rows = ref[pl.ds(part, 32), :].astype(F32)
+        vectors.append((rows[0:8] + rows[8:16]) + rows[16:24])
+    refs[1][...] = (vectors[0] + vectors[1]) + (vectors[2] + vectors[3])
+
+
+def place_quarters(group, quarters, part, vector):
+    width = quarters[0].shape[1]
+    if vector:
+        shapes = [
+            jax.ShapeDtypeStruct((width, 4 * part), F32), jax.ShapeDtypeStruct((8, width), F32)
+        ]
+    else:
+        shapes = [jax.ShapeDtypeStruct((4 * part, width), F32)]
+    return pl.pallas_call(
+        functools.partial(place_kernel, part),
+        out_shape=tuple(shapes),
         in_specs=[SMEM] + [VMEM] * 4,
-        out_specs=VMEM,
+        out_specs=tuple([VMEM] * len(shapes)),
         scratch_shapes=[pltpu.VMEM((4 * part, width), F32)],
         compiler_params=small_params(),
-        cost_estimate=pl.CostEstimate(
-            flops=0, bytes_accessed=24 * part * width, transcendentals=0
-        ),
+        cost_estimate=COST,
         name="place",
     )(group, *quarters)
 
@@ -706,7 +736,7 @@
     pixels = ray_pixel[0].reshape(ray_count, rows)
     rendered = render(
         me, block_owner, tile_lists, opacity, tile_counts.reshape(1, rows), pixels,
-        gaussian_features,
+        gaussian_features, (far[0],),
     )
     target = lax.all_to_all(rendered, "ray", split_axis=0, concat_axis=0, tiled=True)
     tokens, normed, normed_t = prepare_tokens(
@@ -723,49 +753,46 @@
     )
     common = (back, back_t, normed)
 
-    def grads(side, quarter, arrived):
+    def grads(side, quarter, gain, arrived):
         weights = (near, far) if side == 0 else (near_other, far_other)
         return backward(
             side, quarter, common, weights[0], weights[1][quarter], act_near, slope_near,
-            act_far[quarter], slope_far[quarter], arrived,
+            act_far[quarter], slope_far[quarter], gain, arrived,
         )
 
-    order = (3, 1, 2, 0)
-    arrived, gains, sums = {}, [], {}
-    for quarter in order:
-        out, gain = grads(1, quarter, None)
-        arrived[quarter] = partner(out)
-        gains.append(gain)
-    for quarter in order:
-        grad_up, grad_down, gain = grads(0, quarter, arrived[quarter])
-        gains.append(gain)
-        sums[quarter] = (grad_up, grad_down)
-    sent = {
-        (quarter, which): beside(sums[quarter][which], quarter)
-        for which in (1, 0) for quarter in (3, 1, 2)
-    }
-    results = {}
-    for which in (1, 0):
-        shares = totals([sums[0][which]] + [sent[quarter, which] for quarter in (1, 2, 3)])
-        total = shares[0].astype(F32)
-        for shift in range(1, depth):
-            total = total + along(shares[shift], shift).astype(F32)
-        total = total.astype(BF16)
-        results[which] = place_quarters(
-            group, [total] + [beside(total, flip) for flip in (1, 2, 3)], which == 0
-        )
+    gain = jnp.zeros((1, width), F32)
+    arrived, sums, sent = {}, {}, {}
+    for side, quarter in ((1, 3), (1, 1), (0, 3), (1, 2), (0, 1), (1, 0), (0, 2), (0, 0)):
+        if side == 1:
+            out, gain = grads(1, quarter, gain, None)
+            arrived[quarter] = partner(out)
+        else:
+            grad_up, grad_down, gain = grads(0, quarter, gain, arrived[quarter])
+            sums[quarter] = (grad_up, grad_down)
+            if quarter:
+                sent[quarter] = (beside(grad_up, quarter), beside(grad_down, quarter))
     vector = jnp.concatenate(
-        [sum(gains) / layer_norm_gain.reshape(1, width), small[:2]], axis=0
+        [gain / layer_norm_gain.reshape(1, width), small[:2], jnp.zeros((5, width), F32)], axis=0
     )
+    vector, *shares = totals([sums[0][1]] + [sent[quarter][1] for quarter in (1, 2, 3)], vector)
+
+    def sum_along(shares, *vector):
+        arrivals = [along(shares[shift], shift) for shift in range(1, depth)]
+        total = collect([shares[0]] + arrivals, *vector)
+        return [total] + [beside(total, flip) for flip in (1, 2, 3)]
+
+    quarters = sum_along(shares)
+    (grad_down,) = place_quarters(group, quarters, part, False)
     vector = vector + partner(vector)
-    for flip in (1, 2):
-        vector = vector + beside(vector, flip)
     flip = 2
     while flip < ray_count:
         vector = vector + partner(vector, flip)
         flip *= 2
+    shares = totals([sums[0][0]] + [sent[quarter][0] for quarter in (1, 2, 3)])
+    quarters = sum_along(shares, vector)
+    grad_up, vector = place_quarters(group, quarters, part, True)
     loss = vector[2, 0] / (rows * ray_count * group_count)
-    return (results[0], results[1], vector[0], vector[1], loss)
+    return (grad_up, grad_down, vector[0], vector[1], loss)
 
 
 def shards(*operands):

time: 227 us -> 239 us (1.053); the launches traced: 226 us -> 235 us
  waiting for transfers between devices: 101 us -> 114 us
  local copies, waits for them, and re-layouts: 18.5 us -> 15.6 us
    ppermute x20 -> x18, waiting for transfers between devices: 76 us -> 87.2 us  [beside(): lax.ppermute(array, 'grp', [(g, g ^ flip) for g in range(group_count)])]
    ppermute x12, waiting for transfers between devices: 5.65 us -> 9.66 us  [partner(): return lax.ppermute(array, 'ray', [(r, r ^ flip) for r in range(ray_count)])]
    unnamed x71 -> x63, local copies, waits for them, and re-layouts: 16.8 us -> 13.8 us
    ppermute x9, waiting for transfers between devices: 19.6 us -> 17.2 us  [along(): return lax.ppermute(array, 'ray', pairs)]
    ppermute x20 -> x18, starting transfers between devices: 24 us -> 24.9 us  [beside(): lax.ppermute(array, 'grp', [(g, g ^ flip) for g in range(group_count)])]
  transfers between devices with their start and end apart: 42 -> 40, of which waited for: 15 -> 15; matrix products, arithmetic and copies ran while one was open for 2% -> 1% of each run, Pallas kernels for 20% -> 12%
where the time goes in v3:
time: 239 us; the launch traced here: 235 us
  waiting for transfers between devices  114 us (48%)
  Pallas kernels  53 us (22%)
  starting transfers between devices  47.2 us (20%)
  local copies, waits for them, and re-layouts  15.6 us (7%)
  between operations  2.87 us (1%)
  other arithmetic  2.6 us (1%)
    ppermute x18, waiting for transfers between devices, beside(): lax.ppermute(array, 'grp', [(g, g ^ flip) for g in range(group_count)])  87.2 us
    ppermute x18, starting transfers between devices, beside(): lax.ppermute(array, 'grp', [(g, g ^ flip) for g in range(group_count)])  24.9 us
    ppermute x9, waiting for transfers between devices, along(): return lax.ppermute(array, 'ray', pairs)  17.2 us
    pallas_call x5, Pallas kernels, forward(): pl.pallas_call(functools.partial(forward_kernel, first, last), out_shape=...  16.3 us
    pallas_call x1, Pallas kernels, render(): pl.pallas_call(functools.partial(render_kernel, ray_count), out_shape=jax...  14.1 us
    unnamed x63, local copies, waits for them, and re-layouts  13.8 us
    pallas_call x8, Pallas kernels, backward(): pl.pallas_call(body, out_shape=tuple(shapes), in_specs=[VMEM] * len(opera...  13.8 us
    ppermute x9, starting transfers between devices, along(): return lax.ppermute(array, 'ray', pairs)  13.1 us
  transfers between devices with their start and end apart: 40, of which 15 were waited for; matrix products, arithmetic and copies ran while one was open for 1% of the time, Pallas kernels for 12%

profile of v3, /device:TPU:8, one launch (start us, length us, event | category | flops | bytes accessed | tf_op | source)
XLA Modules:
  0.0 235.3 jit_solution(15271610379126696386)
XLA Ops:
  3.0 3.0 %collective-permute-start.1 = (bf16[2,64,1024]{2,1,0:T(8,128)(2,1)S(1)}, bf16[2,64,1024]{2,1,0:T(8,128)(2,1)S(1)}, u32[]{:S(2)}, u32[]{:S(2)}) collective-permute-start(bf16[2,64,1024]{2,1,0:T(8,128)(2,1)S(1)} %quarter.1), channel_id=1, source_target_pairs={{0,4},{1,5},{2,6},{3,7},{4,0},{5,1},{6,2},{7,3},{8,12},{9,13},{10,... | collective-permute-start | bytes 786440 | tf_op jit(solution)/shard_map/ppermute | solution.py:726
  6.0 2.5 %collective-permute-start.2 = (bf16[2,64,1024]{2,1,0:T(8,128)(2,1)S(1)}, bf16[2,64,1024]{2,1,0:T(8,128)(2,1)S(1)}, u32[]{:S(2)}, u32[]{:S(2)}) collective-permute-start(bf16[2,64,1024]{2,1,0:T(8,128)(2,1)S(1)} %quarter.1), channel_id=1, source_target_pairs={{0,2},{1,3},{2,4},{3,5},{4,6},{5,7},{6,0},{7,1},{8,10},{9,11},{10,... | collective-permute-start | bytes 786440 | tf_op jit(solution)/shard_map/ppermute | solution.py:726
  11.0 12.4 %collective-permute-done = bf16[2,64,1024]{2,1,0:T(8,128)(2,1)S(1)} collective-permute-done((bf16[2,64,1024]{2,1,0:T(8,128)(2,1)S(1)}, bf16[2,64,1024]{2,1,0:T(8,128)(2,1)S(1)}, u32[]{:S(2)}, u32[]{:S(2)}) %collective-permute-start) | collective-permute-done | bytes 262176 | tf_op jit(solution)/shard_map/ppermute | solution.py:726
  23.5 4.7 %collective-permute-done.2 = bf16[2,64,1024]{2,1,0:T(8,128)(2,1)S(1)} collective-permute-done((bf16[2,64,1024]{2,1,0:T(8,128)(2,1)S(1)}, bf16[2,64,1024]{2,1,0:T(8,128)(2,1)S(1)}, u32[]{:S(2)}, u32[]{:S(2)}) %collective-permute-start.2) | collective-permute-done | bytes 262176 | tf_op jit(solution)/shard_map/ppermute | solution.py:726
  29.2 14.1 %render.1 = bf16[512,1024]{1,0:T(8,128)(2,1)} custom-call(s32[1]{0:T(128)} %bitcast.1.me_ref, s32[1,8]{1,0:T(1,128)} %owner_ref.3, s32[32,512]{1,0:T(8,128)} %lists_ref.1, f32[32,512]{1,0:T(8,128)} %opacity_ref.1, s32[1,512]{1,0:T(1,128)} %bitcast.30, s32[8,512]{1,0:T(8,128)} %reshape_squeeze.3.pixels_ref, bf16[1024,1024]{1,0:T(8,128)(2,1)} %features_ref.1, ...), custom_call_target="tpu_custom_call" | custom-call | flops 1048576 | bytes 65536 | tf_op jit(solution)/shard_map/render/pallas_call | solution.py:112
  43.2 5.3 %all-to-all-start = ((bf16[8,64,1024]{2,1,0:T(8,128)(2,1)}), bf16[8,64,1024]{2,1,0:T(8,128)(2,1)}, u32[]{:S(2)}, u32[]{:S(2)}) async-start(bf16[8,64,1024]{2,1,0:T(8,128)(2,1)} %bitcast.19), calls=%async_computation | async-start | bytes 2097152 | tf_op jit(solution)/shard_map/all_to_all | solution.py:741
  55.0 2.6 %collective-permute-done.10 = bf16[2,64,1024]{2,1,0:T(8,128)(2,1)S(1)} collective-permute-done((bf16[2,64,1024]{2,1,0:T(8,128)(2,1)S(1)}, bf16[2,64,1024]{2,1,0:T(8,128)(2,1)S(1)}, u32[]{:S(2)}, u32[]{:S(2)}) %collective-permute-start.10) | collective-permute-done | bytes 262176 | tf_op jit(solution)/shard_map/ppermute | solution.py:719
  57.6 2.5 %collective-permute-start.12 = (bf16[2,64,1024]{2,1,0:T(8,128)(2,1)S(1)}, bf16[2,64,1024]{2,1,0:T(8,128)(2,1)S(1)}, u32[]{:S(2)}, u32[]{:S(2)}) collective-permute-start(bf16[2,64,1024]{2,1,0:T(8,128)(2,1)S(1)} %quarter.1), channel_id=1, source_target_pairs={{0,24},{8,16},{16,8},{24,0},{1,25},{9,17},{17,9},{25,1},{2,26},{10... | collective-permute-start | bytes 786440 | tf_op jit(solution)/shard_map/ppermute | solution.py:719
  60.1 37.6 %collective-permute-done.11 = bf16[2,64,1024]{2,1,0:T(8,128)(2,1)S(1)} collective-permute-done((bf16[2,64,1024]{2,1,0:T(8,128)(2,1)S(1)}, bf16[2,64,1024]{2,1,0:T(8,128)(2,1)S(1)}, u32[]{:S(2)}, u32[]{:S(2)}) %collective-permute-start.11) | collective-permute-done | bytes 262176 | tf_op jit(solution)/shard_map/ppermute | solution.py:719
  99.0 5.5 %tokens.1 = (bf16[512,1024]{1,0:T(8,128)(2,1)}, bf16[512,1024]{1,0:T(8,128)(2,1)}, bf16[1024,512]{1,0:T(8,128)(2,1)}) custom-call(s32[1]{0:T(128)} %bitcast.1.me_ref, s32[1,8]{1,0:T(1,128)} %owner_ref.3, s32[8,512]{1,0:T(8,128)} %reshape_squeeze.3.pixels_ref, bf16[512,1024]{1,0:T(8,128)(2,1)} %tokens_ref.1, f32[1,1024]{1,0:T(1,128)} %bitcast.26), custom_call_target="tpu_custom_call" | custom-call | flops 1048576 | bytes 65536 | tf_op jit(solution)/shard_map/tokens/pallas_call | solution.py:171
  104.5 1.6 copy-done.3
  106.1 2.2 forward.5
  108.3 1.8 forward.6
  111.9 3.3 %forward.7 = (bf16[2,3,64,512]{3,2,1,0:T(8,128)(2,1)S(1)}, f32[2,3,64,512]{3,2,1,0:T(8,128)S(1)}, f32[512,1024]{1,0:T(8,128)S(1)}) custom-call(bf16[1024,512]{1,0:T(8,128)(2,1)S(1)} %copy-done.3, bf16[3,2,64,1024]{3,2,1,0:T(8,128)(2,1)} %collective-permute-done.7.refs_1_.refs_4_, bf16[3,2,64,1024]{3,2,1,0:T(8,128)(2,1)S(1)} %collective-permute-done.8.refs_2_.refs_4_, ...), custom_call_target="tpu_custom_call" | custom-call | flops 1048576 | bytes 65536 | tf_op jit(solution)/shard_map/forward/pallas_call | solution.py:525
  116.0 3.4 %forward.8 = (bf16[2,3,64,512]{3,2,1,0:T(8,128)(2,1)S(1)}, f32[2,3,64,512]{3,2,1,0:T(8,128)S(1)}, f32[512,1024]{1,0:T(8,128)S(1)}) custom-call(bf16[1024,512]{1,0:T(8,128)(2,1)S(1)} %copy-done.3, bf16[3,2,64,1024]{3,2,1,0:T(8,128)(2,1)} %collective-permute-done.5.refs_1_.refs_4_, bf16[3,2,64,1024]{3,2,1,0:T(8,128)(2,1)S(1)} %collective-permute-done.6.refs_2_.refs_4_, ...), custom_call_target="tpu_custom_call" | custom-call | flops 1048576 | bytes 65536 | tf_op jit(solution)/shard_map/forward/pallas_call | solution.py:525
  126.5 5.6 %forward.9 = (bf16[2,3,64,512]{3,2,1,0:T(8,128)(2,1)S(1)}, f32[2,3,64,512]{3,2,1,0:T(8,128)S(1)}, bf16[512,1024]{1,0:T(8,128)(2,1)S(1)}, bf16[1024,512]{1,0:T(8,128)(2,1)S(1)}, f32[8,1024]{1,0:T(8,128)S(1)}) custom-call(bf16[1024,512]{1,0:T(8,128)(2,1)S(1)} %copy-done.4, bf16[3,2,64,1024]{3,2,1,0:T(8,128)(2,1)} %collective-permute-done.3.refs_1_.refs_4_, ...), custom_call_target="tpu_custom_call" | custom-call | flops 1048576 | bytes 65536 | tf_op jit(solution)/shard_map/forward/pallas_call | solution.py:525
  132.2 2.3 backward.8
  137.3 2.4 %backward.10 = (bf16[4,64,1024]{2,1,0:T(8,128)(2,1)S(1)}, bf16[4,64,1024]{2,1,0:T(8,128)(2,1)S(1)}, f32[1,1024]{1,0:T(1,128)S(1)}) custom-call(bf16[512,1024]{1,0:T(8,128)(2,1)S(1)} %get-tuple-element.62.refs_0_, bf16[1024,512]{1,0:T(8,128)(2,1)S(1)} %get-tuple-element.63.refs_1_, bf16[512,1024]{1,0:T(8,128)(2,1)S(1)} %copy-done, ...), custom_call_target="tpu_custom_call" | custom-call | flops 1048576 | bytes 65536 | tf_op jit(solution)/shard_map/backward/pallas_call | solution.py:587
  141.3 2.4 %backward.12 = (bf16[4,64,1024]{2,1,0:T(8,128)(2,1)S(1)}, bf16[4,64,1024]{2,1,0:T(8,128)(2,1)S(1)}, f32[1,1024]{1,0:T(1,128)S(1)}) custom-call(bf16[512,1024]{1,0:T(8,128)(2,1)S(1)} %get-tuple-element.62.refs_0_, bf16[1024,512]{1,0:T(8,128)(2,1)S(1)} %get-tuple-element.63.refs_1_, bf16[512,1024]{1,0:T(8,128)(2,1)S(1)} %copy-done, ...), custom_call_target="tpu_custom_call" | custom-call | flops 1048576 | bytes 65536 | tf_op jit(solution)/shard_map/backward/pallas_call | solution.py:587
  148.0 2.3 backward.14
  152.3 7.5 %collective-permute-done.24.refs_1_ = bf16[4,64,1024]{2,1,0:T(8,128)(2,1)S(1)} collective-permute-done((bf16[4,64,1024]{2,1,0:T(8,128)(2,1)S(1)}, bf16[4,64,1024]{2,1,0:T(8,128)(2,1)S(1)}, u32[]{:S(2)}, u32[]{:S(2)}) %collective-permute-start.24) | collective-permute-done | bytes 524320 | tf_op jit(solution)/shard_map/ppermute | solution.py:719
  159.8 2.4 %collective-permute-start.20 = (bf16[4,64,1024]{2,1,0:T(8,128)(2,1)S(1)}, bf16[4,64,1024]{2,1,0:T(8,128)(2,1)S(1)}, u32[]{:S(2)}, u32[]{:S(2)}) collective-permute-start(bf16[4,64,1024]{2,1,0:T(8,128)(2,1)S(1)} %get-tuple-element.89), channel_id=1, source_target_pairs={{0,24},{8,16},{16,8},{24,0},{1,25},{9,17},{17,9},{25,1},{2,26},{10... | collective-permute-start | bytes 1572872 | tf_op jit(solution)/shard_map/ppermute | solution.py:719
  164.0 8.0 %collective-permute-done.26.refs_3_ = bf16[4,64,1024]{2,1,0:T(8,128)(2,1)S(1)} collective-permute-done((bf16[4,64,1024]{2,1,0:T(8,128)(2,1)S(1)}, bf16[4,64,1024]{2,1,0:T(8,128)(2,1)S(1)}, u32[]{:S(2)}, u32[]{:S(2)}) %collective-permute-start.26) | collective-permute-done | bytes 524320 | tf_op jit(solution)/shard_map/ppermute | solution.py:719
  172.0 4.4 %collective-permute-done.25.refs_2_ = bf16[4,64,1024]{2,1,0:T(8,128)(2,1)S(1)} collective-permute-done((bf16[4,64,1024]{2,1,0:T(8,128)(2,1)S(1)}, bf16[4,64,1024]{2,1,0:T(8,128)(2,1)S(1)}, u32[]{:S(2)}, u32[]{:S(2)}) %collective-permute-start.25) | collective-permute-done | bytes 524320 | tf_op jit(solution)/shard_map/ppermute | solution.py:719
  179.4 2.9 %collective-permute-done.18.refs_1_ = bf16[4,64,1024]{2,1,0:T(8,128)(2,1)S(1)} collective-permute-done((bf16[4,64,1024]{2,1,0:T(8,128)(2,1)S(1)}, bf16[4,64,1024]{2,1,0:T(8,128)(2,1)S(1)}, u32[]{:S(2)}, u32[]{:S(2)}) %collective-permute-start.18) | collective-permute-done | bytes 524320 | tf_op jit(solution)/shard_map/ppermute | solution.py:719
  182.6 11.4 %collective-permute-done.20.refs_3_ = bf16[4,64,1024]{2,1,0:T(8,128)(2,1)S(1)} collective-permute-done((bf16[4,64,1024]{2,1,0:T(8,128)(2,1)S(1)}, bf16[4,64,1024]{2,1,0:T(8,128)(2,1)S(1)}, u32[]{:S(2)}, u32[]{:S(2)}) %collective-permute-start.20) | collective-permute-done | bytes 524320 | tf_op jit(solution)/shard_map/ppermute | solution.py:719
  194.1 3.6 %collective-permute-done.19.refs_2_ = bf16[4,64,1024]{2,1,0:T(8,128)(2,1)S(1)} collective-permute-done((bf16[4,64,1024]{2,1,0:T(8,128)(2,1)S(1)}, bf16[4,64,1024]{2,1,0:T(8,128)(2,1)S(1)}, u32[]{:S(2)}, u32[]{:S(2)}) %collective-permute-start.19) | collective-permute-done | bytes 524320 | tf_op jit(solution)/shard_map/ppermute | solution.py:719
  200.7 1.7 collective-permute-start.23
  205.6 3.8 %collective-permute-done.28 = f32[8,1024]{1,0:T(8,128)S(1)} collective-permute-done((f32[8,1024]{1,0:T(8,128)S(1)}, f32[8,1024]{1,0:T(8,128)S(1)}, u32[]{:S(2)}, u32[]{:S(2)}) %collective-permute-start.28) | collective-permute-done | bytes 32800 | tf_op jit(solution)/shard_map/ppermute | solution.py:722
  209.4 4.8 %collective-permute-done.29 = f32[8,1024]{1,0:T(8,128)S(1)} collective-permute-done((f32[8,1024]{1,0:T(8,128)S(1)}, f32[8,1024]{1,0:T(8,128)S(1)}, u32[]{:S(2)}, u32[]{:S(2)}) %collective-permute-start.29) | collective-permute-done | bytes 32800 | tf_op jit(solution)/shard_map/ppermute | solution.py:722
  218.3 2.4 %collective-permute-start.38 = (bf16[64,1024]{1,0:T(8,128)(2,1)S(1)}, bf16[64,1024]{1,0:T(8,128)(2,1)S(1)}, u32[]{:S(2)}, u32[]{:S(2)}) collective-permute-start(bf16[64,1024]{1,0:T(8,128)(2,1)S(1)} %collect.3.a_ref), channel_id=1, source_target_pairs={{0,24},{8,16},{16,8},{24,0},{1,25},{9,17},{17,9},{25,1},{2,26},{10... | collective-permute-start | bytes 393224 | tf_op jit(solution)/shard_map/ppermute | solution.py:719
  220.8 9.1 %collective-permute-done.37.c_ref = bf16[64,1024]{1,0:T(8,128)(2,1)S(1)} collective-permute-done((bf16[64,1024]{1,0:T(8,128)(2,1)S(1)}, bf16[64,1024]{1,0:T(8,128)(2,1)S(1)}, u32[]{:S(2)}, u32[]{:S(2)}) %collective-permute-start.37) | collective-permute-done | bytes 131104 | tf_op jit(solution)/shard_map/ppermute | solution.py:719
  (148 shorter events, 52.9 us)
Async XLA Ops:
  2.9 20.5 %collective-permute-start = (bf16[2,64,1024]{2,1,0:T(8,128)(2,1)S(1)}, bf16[2,64,1024]{2,1,0:T(8,128)(2,1)S(1)}, u32[]{:S(2)}, u32[]{:S(2)}) collective-permute-start(bf16[2,64,1024]{2,1,0:T(8,128)(2,1)S(1)} %quarter.1), channel_id=1, source_target_pairs={{0,6},{1,7},{2,0},{3,1},{4,2},{5,3},{6,4},{7,5},{8,14},{9,15},{10,... | collective-permute-start | bytes 786440 | tf_op jit(solution)/shard_map/ppermute | solution.py:726
  3.0 20.5 %collective-permute-start.1 = (bf16[2,64,1024]{2,1,0:T(8,128)(2,1)S(1)}, bf16[2,64,1024]{2,1,0:T(8,128)(2,1)S(1)}, u32[]{:S(2)}, u32[]{:S(2)}) collective-permute-start(bf16[2,64,1024]{2,1,0:T(8,128)(2,1)S(1)} %quarter.1), channel_id=1, source_target_pairs={{0,4},{1,5},{2,6},{3,7},{4,0},{5,1},{6,2},{7,3},{8,12},{9,13},{10,... | collective-permute-start | bytes 786440 | tf_op jit(solution)/shard_map/ppermute | solution.py:726
  6.0 22.2 %collective-permute-start.2 = (bf16[2,64,1024]{2,1,0:T(8,128)(2,1)S(1)}, bf16[2,64,1024]{2,1,0:T(8,128)(2,1)S(1)}, u32[]{:S(2)}, u32[]{:S(2)}) collective-permute-start(bf16[2,64,1024]{2,1,0:T(8,128)(2,1)S(1)} %quarter.1), channel_id=1, source_target_pairs={{0,2},{1,3},{2,4},{3,5},{4,6},{5,7},{6,0},{7,1},{8,10},{9,11},{10,... | collective-permute-start | bytes 786440 | tf_op jit(solution)/shard_map/ppermute | solution.py:726
  43.2 79.2 %all-to-all-start = ((bf16[8,64,1024]{2,1,0:T(8,128)(2,1)}), bf16[8,64,1024]{2,1,0:T(8,128)(2,1)}, u32[]{:S(2)}, u32[]{:S(2)}) async-start(bf16[8,64,1024]{2,1,0:T(8,128)(2,1)} %bitcast.19), calls=%async_computation | async-start | bytes 2097152 | tf_op jit(solution)/shard_map/all_to_all | solution.py:741
  50.0 48.4 %collective-permute-start.7 = (bf16[3,2,64,1024]{3,2,1,0:T(8,128)(2,1)S(1)}, bf16[3,2,64,1024]{3,2,1,0:T(8,128)(2,1)}, u32[]{:S(2)}, u32[]{:S(2)}) collective-permute-start(bf16[3,2,64,1024]{3,2,1,0:T(8,128)(2,1)S(1)} %copy-done.5), channel_id=1, source_target_pairs={{0,8},{8,0},{16,24},{24,16},{1,9},{9,1},{17,25},{25,17},{2,10},{10... | collective-permute-start | bytes 2359304 | tf_op jit(solution)/shard_map/ppermute | solution.py:719
  50.5 48.0 %collective-permute-start.5 = (bf16[3,2,64,1024]{3,2,1,0:T(8,128)(2,1)S(1)}, bf16[3,2,64,1024]{3,2,1,0:T(8,128)(2,1)}, u32[]{:S(2)}, u32[]{:S(2)}) collective-permute-start(bf16[3,2,64,1024]{3,2,1,0:T(8,128)(2,1)S(1)} %copy-done.5), channel_id=1, source_target_pairs={{0,16},{8,24},{16,0},{24,8},{1,17},{9,25},{17,1},{25,9},{2,18},{10... | collective-permute-start | bytes 2359304 | tf_op jit(solution)/shard_map/ppermute | solution.py:719
  52.0 46.9 %collective-permute-start.3 = (bf16[3,2,64,1024]{3,2,1,0:T(8,128)(2,1)S(1)}, bf16[3,2,64,1024]{3,2,1,0:T(8,128)(2,1)}, u32[]{:S(2)}, u32[]{:S(2)}) collective-permute-start(bf16[3,2,64,1024]{3,2,1,0:T(8,128)(2,1)S(1)} %copy-done.5), channel_id=1, source_target_pairs={{0,24},{8,16},{16,8},{24,0},{1,25},{9,17},{17,9},{25,1},{2,26},{10... | collective-permute-start | bytes 2359304 | tf_op jit(solution)/shard_map/ppermute | solution.py:719
  53.5 44.2 %collective-permute-start.11 = (bf16[2,64,1024]{2,1,0:T(8,128)(2,1)S(1)}, bf16[2,64,1024]{2,1,0:T(8,128)(2,1)S(1)}, u32[]{:S(2)}, u32[]{:S(2)}) collective-permute-start(bf16[2,64,1024]{2,1,0:T(8,128)(2,1)S(1)} %quarter.1), channel_id=1, source_target_pairs={{0,16},{8,24},{16,0},{24,8},{1,17},{9,25},{17,1},{25,9},{2,18},{10... | collective-permute-start | bytes 786440 | tf_op jit(solution)/shard_map/ppermute | solution.py:719
  57.6 40.0 %collective-permute-start.12 = (bf16[2,64,1024]{2,1,0:T(8,128)(2,1)S(1)}, bf16[2,64,1024]{2,1,0:T(8,128)(2,1)S(1)}, u32[]{:S(2)}, u32[]{:S(2)}) collective-permute-start(bf16[2,64,1024]{2,1,0:T(8,128)(2,1)S(1)} %quarter.1), channel_id=1, source_target_pairs={{0,24},{8,16},{16,8},{24,0},{1,25},{9,17},{17,9},{25,1},{2,26},{10... | collective-permute-start | bytes 786440 | tf_op jit(solution)/shard_map/ppermute | solution.py:719
  97.9 10.4 %collective-permute-start.9 = (bf16[3,2,64,1024]{3,2,1,0:T(8,128)(2,1)S(1)}, bf16[3,2,64,1024]{3,2,1,0:T(8,128)(2,1)S(1)}, u32[]{:S(2)}, u32[]{:S(2)}) collective-permute-start(bf16[3,2,64,1024]{3,2,1,0:T(8,128)(2,1)S(1)} %copy-done.5), channel_id=1, source_target_pairs={{0,1},{1,0},{2,3},{3,2},{4,5},{5,4},{6,7},{7,6},{8,9},{9,8},{10,11... | collective-permute-start | bytes 2359304 | tf_op jit(solution)/shard_map/ppermute | solution.py:722
  98.4 13.5 %collective-permute-start.8 = (bf16[3,2,64,1024]{3,2,1,0:T(8,128)(2,1)}, bf16[3,2,64,1024]{3,2,1,0:T(8,128)(2,1)S(1)}, u32[]{:S(2)}, u32[]{:S(2)}) collective-permute-start(bf16[3,2,64,1024]{3,2,1,0:T(8,128)(2,1)} %collective-permute-done.7.refs_1_.refs_4_), channel_id=1, source_target_pairs={{0,1},{1,0},{2,3},{3,2},{4,5},{5,4},{6,7},{7,6},{8,9},{9,8},{10,11... | collective-permute-start | bytes 2359304 | tf_op jit(solution)/shard_map/ppermute | solution.py:722
  98.5 17.6 %collective-permute-start.6 = (bf16[3,2,64,1024]{3,2,1,0:T(8,128)(2,1)}, bf16[3,2,64,1024]{3,2,1,0:T(8,128)(2,1)S(1)}, u32[]{:S(2)}, u32[]{:S(2)}) collective-permute-start(bf16[3,2,64,1024]{3,2,1,0:T(8,128)(2,1)} %collective-permute-done.5.refs_1_.refs_4_), channel_id=1, source_target_pairs={{0,1},{1,0},{2,3},{3,2},{4,5},{5,4},{6,7},{7,6},{8,9},{9,8},{10,11... | collective-permute-start | bytes 2359304 | tf_op jit(solution)/shard_map/ppermute | solution.py:722
  98.9 23.5 %collective-permute-start.4 = (bf16[3,2,64,1024]{3,2,1,0:T(8,128)(2,1)}, bf16[3,2,64,1024]{3,2,1,0:T(8,128)(2,1)}, u32[]{:S(2)}, u32[]{:S(2)}) collective-permute-start(bf16[3,2,64,1024]{3,2,1,0:T(8,128)(2,1)} %collective-permute-done.3.refs_1_.refs_4_), channel_id=1, source_target_pairs={{0,1},{1,0},{2,3},{3,2},{4,5},{5,4},{6,7},{7,6},{8,9},{9,8},{10,11... | collective-permute-start | bytes 2359304 | tf_op jit(solution)/shard_map/ppermute | solution.py:722
  144.8 17.4 %collective-permute-start.17 = (bf16[2,4,64,1024]{3,2,1,0:T(8,128)(2,1)S(1)}, bf16[2,4,64,1024]{3,2,1,0:T(8,128)(2,1)S(1)}, u32[]{:S(2)}, u32[]{:S(2)}) collective-permute-start(bf16[2,4,64,1024]{3,2,1,0:T(8,128)(2,1)S(1)} %get-tuple-element.85), channel_id=1, source_target_pairs={{0,1},{1,0},{2,3},{3,2},{4,5},{5,4},{6,7},{7,6},{8,9},{9,8},{10,11... | collective-permute-start | bytes 3145736 | tf_op jit(solution)/shard_map/ppermute | solution.py:722
  145.0 14.8 %collective-permute-start.24 = (bf16[4,64,1024]{2,1,0:T(8,128)(2,1)S(1)}, bf16[4,64,1024]{2,1,0:T(8,128)(2,1)S(1)}, u32[]{:S(2)}, u32[]{:S(2)}) collective-permute-start(bf16[4,64,1024]{2,1,0:T(8,128)(2,1)S(1)} %get-tuple-element.95), channel_id=1, source_target_pairs={{0,8},{8,0},{16,24},{24,16},{1,9},{9,1},{17,25},{25,17},{2,10},{10... | collective-permute-start | bytes 1572872 | tf_op jit(solution)/shard_map/ppermute | solution.py:719
  146.5 25.5 %collective-permute-start.26 = (bf16[4,64,1024]{2,1,0:T(8,128)(2,1)S(1)}, bf16[4,64,1024]{2,1,0:T(8,128)(2,1)S(1)}, u32[]{:S(2)}, u32[]{:S(2)}) collective-permute-start(bf16[4,64,1024]{2,1,0:T(8,128)(2,1)S(1)} %get-tuple-element.97), channel_id=1, source_target_pairs={{0,24},{8,16},{16,8},{24,0},{1,25},{9,17},{17,9},{25,1},{2,26},{10... | collective-permute-start | bytes 1572872 | tf_op jit(solution)/shard_map/ppermute | solution.py:719
  150.3 26.1 %collective-permute-start.25 = (bf16[4,64,1024]{2,1,0:T(8,128)(2,1)S(1)}, bf16[4,64,1024]{2,1,0:T(8,128)(2,1)S(1)}, u32[]{:S(2)}, u32[]{:S(2)}) collective-permute-start(bf16[4,64,1024]{2,1,0:T(8,128)(2,1)S(1)} %get-tuple-element.96), channel_id=1, source_target_pairs={{0,16},{8,24},{16,0},{24,8},{1,17},{9,25},{17,1},{25,9},{2,18},{10... | collective-permute-start | bytes 1572872 | tf_op jit(solution)/shard_map/ppermute | solution.py:719
  150.9 31.4 %collective-permute-start.18 = (bf16[4,64,1024]{2,1,0:T(8,128)(2,1)S(1)}, bf16[4,64,1024]{2,1,0:T(8,128)(2,1)S(1)}, u32[]{:S(2)}, u32[]{:S(2)}) collective-permute-start(bf16[4,64,1024]{2,1,0:T(8,128)(2,1)S(1)} %get-tuple-element.87), channel_id=1, source_target_pairs={{0,8},{8,0},{16,24},{24,16},{1,9},{9,1},{17,25},{25,17},{2,10},{10... | collective-permute-start | bytes 1572872 | tf_op jit(solution)/shard_map/ppermute | solution.py:719
  159.8 34.3 %collective-permute-start.20 = (bf16[4,64,1024]{2,1,0:T(8,128)(2,1)S(1)}, bf16[4,64,1024]{2,1,0:T(8,128)(2,1)S(1)}, u32[]{:S(2)}, u32[]{:S(2)}) collective-permute-start(bf16[4,64,1024]{2,1,0:T(8,128)(2,1)S(1)} %get-tuple-element.89), channel_id=1, source_target_pairs={{0,24},{8,16},{16,8},{24,0},{1,25},{9,17},{17,9},{25,1},{2,26},{10... | collective-permute-start | bytes 1572872 | tf_op jit(solution)/shard_map/ppermute | solution.py:719
  162.2 35.5 %collective-permute-start.19 = (bf16[4,64,1024]{2,1,0:T(8,128)(2,1)S(1)}, bf16[4,64,1024]{2,1,0:T(8,128)(2,1)S(1)}, u32[]{:S(2)}, u32[]{:S(2)}) collective-permute-start(bf16[4,64,1024]{2,1,0:T(8,128)(2,1)S(1)} %get-tuple-element.88), channel_id=1, source_target_pairs={{0,16},{8,24},{16,0},{24,8},{1,17},{9,25},{17,1},{25,9},{2,18},{10... | collective-permute-start | bytes 1572872 | tf_op jit(solution)/shard_map/ppermute | solution.py:719
  176.7 24.0 %collective-permute-start.33 = (bf16[64,1024]{1,0:T(8,128)(2,1)S(1)}, bf16[64,1024]{1,0:T(8,128)(2,1)S(1)}, u32[]{:S(2)}, u32[]{:S(2)}) collective-permute-start(bf16[64,1024]{1,0:T(8,128)(2,1)S(1)} %get-tuple-element.103), channel_id=1, source_target_pairs={{0,2},{1,3},{2,4},{3,5},{4,6},{5,7},{6,0},{7,1},{8,10},{9,11},{10,... | collective-permute-start | bytes 393224 | tf_op jit(solution)/shard_map/ppermute | solution.py:726
  178.2 24.3 %collective-permute-start.34 = (bf16[64,1024]{1,0:T(8,128)(2,1)S(1)}, bf16[64,1024]{1,0:T(8,128)(2,1)S(1)}, u32[]{:S(2)}, u32[]{:S(2)}) collective-permute-start(bf16[64,1024]{1,0:T(8,128)(2,1)S(1)} %get-tuple-element.104), channel_id=1, source_target_pairs={{0,4},{1,5},{2,6},{3,7},{4,0},{5,1},{6,2},{7,3},{8,12},{9,13},{10,... | collective-permute-start | bytes 393224 | tf_op jit(solution)/shard_map/ppermute | solution.py:726
  182.3 21.7 %collective-permute-start.35 = (bf16[64,1024]{1,0:T(8,128)(2,1)S(1)}, bf16[64,1024]{1,0:T(8,128)(2,1)S(1)}, u32[]{:S(2)}, u32[]{:S(2)}) collective-permute-start(bf16[64,1024]{1,0:T(8,128)(2,1)S(1)} %get-tuple-element.105), channel_id=1, source_target_pairs={{0,6},{1,7},{2,0},{3,1},{4,2},{5,3},{6,4},{7,5},{8,14},{9,15},{10,... | collective-permute-start | bytes 393224 | tf_op jit(solution)/shard_map/ppermute | solution.py:726
  198.0 16.2 %collective-permute-start.21 = (bf16[64,1024]{1,0:T(8,128)(2,1)S(1)}, bf16[64,1024]{1,0:T(8,128)(2,1)S(1)}, u32[]{:S(2)}, u32[]{:S(2)}) collective-permute-start(bf16[64,1024]{1,0:T(8,128)(2,1)S(1)} %get-tuple-element.91), channel_id=1, source_target_pairs={{0,2},{1,3},{2,4},{3,5},{4,6},{5,7},{6,0},{7,1},{8,10},{9,11},{10,... | collective-permute-start | bytes 393224 | tf_op jit(solution)/shard_map/ppermute | solution.py:726
  199.5 14.7 %collective-permute-start.22 = (bf16[64,1024]{1,0:T(8,128)(2,1)S(1)}, bf16[64,1024]{1,0:T(8,128)(2,1)S(1)}, u32[]{:S(2)}, u32[]{:S(2)}) collective-permute-start(bf16[64,1024]{1,0:T(8,128)(2,1)S(1)} %get-tuple-element.92), channel_id=1, source_target_pairs={{0,4},{1,5},{2,6},{3,7},{4,0},{5,1},{6,2},{7,3},{8,12},{9,13},{10,... | collective-permute-start | bytes 393224 | tf_op jit(solution)/shard_map/ppermute | solution.py:726
  200.7 13.5 %collective-permute-start.23 = (bf16[64,1024]{1,0:T(8,128)(2,1)S(1)}, bf16[64,1024]{1,0:T(8,128)(2,1)S(1)}, u32[]{:S(2)}, u32[]{:S(2)}) collective-permute-start(bf16[64,1024]{1,0:T(8,128)(2,1)S(1)} %get-tuple-element.93), channel_id=1, source_target_pairs={{0,6},{1,7},{2,0},{3,1},{4,2},{5,3},{6,4},{7,5},{8,14},{9,15},{10,... | collective-permute-start | bytes 393224 | tf_op jit(solution)/shard_map/ppermute | solution.py:726
  204.0 14.3 %collective-permute-start.36 = (bf16[64,1024]{1,0:T(8,128)(2,1)S(1)}, bf16[64,1024]{1,0:T(8,128)(2,1)S(1)}, u32[]{:S(2)}, u32[]{:S(2)}) collective-permute-start(bf16[64,1024]{1,0:T(8,128)(2,1)S(1)} %collect.3.a_ref), channel_id=1, source_target_pairs={{0,8},{8,0},{16,24},{24,16},{1,9},{9,1},{17,25},{25,17},{2,10},{10... | collective-permute-start | bytes 393224 | tf_op jit(solution)/shard_map/ppermute | solution.py:719
  214.3 16.7 %collective-permute-start.30 = (bf16[96,1024]{1,0:T(8,128)(2,1)S(1)}, bf16[96,1024]{1,0:T(8,128)(2,1)S(1)}, u32[]{:S(2)}, u32[]{:S(2)}) collective-permute-start(bf16[96,1024]{1,0:T(8,128)(2,1)S(1)} %collect.2.a_ref), channel_id=1, source_target_pairs={{0,8},{8,0},{16,24},{24,16},{1,9},{9,1},{17,25},{25,17},{2,10},{10... | collective-permute-start | bytes 589832 | tf_op jit(solution)/shard_map/ppermute | solution.py:719
  215.8 15.2 %collective-permute-start.31 = (bf16[96,1024]{1,0:T(8,128)(2,1)S(1)}, bf16[96,1024]{1,0:T(8,128)(2,1)S(1)}, u32[]{:S(2)}, u32[]{:S(2)}) collective-permute-start(bf16[96,1024]{1,0:T(8,128)(2,1)S(1)} %collect.2.a_ref), channel_id=1, source_target_pairs={{0,16},{8,24},{16,0},{24,8},{1,17},{9,25},{17,1},{25,9},{2,18},{10... | collective-permute-start | bytes 589832 | tf_op jit(solution)/shard_map/ppermute | solution.py:719
  216.3 14.7 %collective-permute-start.32 = (bf16[96,1024]{1,0:T(8,128)(2,1)S(1)}, bf16[96,1024]{1,0:T(8,128)(2,1)S(1)}, u32[]{:S(2)}, u32[]{:S(2)}) collective-permute-start(bf16[96,1024]{1,0:T(8,128)(2,1)S(1)} %collect.2.a_ref), channel_id=1, source_target_pairs={{0,24},{8,16},{16,8},{24,0},{1,25},{9,17},{17,9},{25,1},{2,26},{10... | collective-permute-start | bytes 589832 | tf_op jit(solution)/shard_map/ppermute | solution.py:719
  217.9 12.0 %collective-permute-start.37 = (bf16[64,1024]{1,0:T(8,128)(2,1)S(1)}, bf16[64,1024]{1,0:T(8,128)(2,1)S(1)}, u32[]{:S(2)}, u32[]{:S(2)}) collective-permute-start(bf16[64,1024]{1,0:T(8,128)(2,1)S(1)} %collect.3.a_ref), channel_id=1, source_target_pairs={{0,16},{8,24},{16,0},{24,8},{1,17},{9,25},{17,1},{25,9},{2,18},{10... | collective-permute-start | bytes 393224 | tf_op jit(solution)/shard_map/ppermute | solution.py:719
  218.3 11.5 %collective-permute-start.38 = (bf16[64,1024]{1,0:T(8,128)(2,1)S(1)}, bf16[64,1024]{1,0:T(8,128)(2,1)S(1)}, u32[]{:S(2)}, u32[]{:S(2)}) collective-permute-start(bf16[64,1024]{1,0:T(8,128)(2,1)S(1)} %collect.3.a_ref), channel_id=1, source_target_pairs={{0,24},{8,16},{16,8},{24,0},{1,25},{9,17},{17,9},{25,1},{2,26},{10... | collective-permute-start | bytes 393224 | tf_op jit(solution)/shard_map/ppermute | solution.py:719
  (39 other events, 141.8 us)

commit v4 on v3

--- a/solution.py
+++ b/solution.py
@@ -10,20 +10,15 @@
 STABILITY_EPSILON = 1e-06
 F32 = jnp.float32
 BF16 = jnp.bfloat16
-VMEM_BYTES = 56 * 1024 * 1024
-SMALL_VMEM_BYTES = 28 * 1024 * 1024
+MIB = 1024 * 1024
 COST = pl.CostEstimate(flops=1 << 20, bytes_accessed=1 << 16, transcendentals=0)
 SMEM = pl.BlockSpec(memory_space=pltpu.SMEM)
 VMEM = pl.BlockSpec(memory_space=pltpu.VMEM)
 ANY = pl.BlockSpec(memory_space=pl.ANY)
 
 
-def params(**more):
-    return pltpu.CompilerParams(vmem_limit_bytes=VMEM_BYTES, **more)
-
-
-def small_params():
-    return pltpu.CompilerParams(vmem_limit_bytes=SMALL_VMEM_BYTES)
+def params(mib=48, **more):
+    return pltpu.CompilerParams(vmem_limit_bytes=mib * MIB, **more)
 
 
 def dot_nn(a, b):
@@ -120,7 +115,7 @@
             pltpu.VMEM((gauss, rays), BF16),
             pltpu.VMEM((rays, rays), BF16),
         ],
-        compiler_params=params(),
+        compiler_params=params(20),
         cost_estimate=COST,
         name="render",
     )(me, owner, lists, opacity, counts, pixels, features, *after)
@@ -178,7 +173,7 @@
         in_specs=[SMEM, SMEM, VMEM, VMEM, VMEM],
         out_specs=(VMEM, VMEM, VMEM),
         scratch_shapes=[pltpu.VMEM((rows, rows), BF16)],
-        compiler_params=params(),
+        compiler_params=params(20),
         cost_estimate=COST,
         name="tokens",
     )(me, owner, pixels, tokens, gain)
@@ -436,7 +431,7 @@
         in_specs=[SMEM, VMEM, VMEM],
         out_specs=VMEM,
         scratch_shapes=[pltpu.VMEM((chunk, width), BF16)],
-        compiler_params=small_params(),
+        compiler_params=params(16),
         cost_estimate=COST,
         name="quarter",
     )(group, up, down)
@@ -452,30 +447,36 @@
     return upstream, 1.0 - cosine
 
 
-def forward_kernel(first, last, *refs):
+def forward_kernel(first, last, sides, *refs):
     refs = list(refs)
-    normed_t_ref, own_ref, other_ref = refs[:3]
-    del refs[:3]
+    normed_t_ref = refs.pop(0)
+    own, other = refs[:sides], refs[sides:2 * sides]
+    del refs[:2 * sides]
     mixed_in = None if first else refs.pop(0)
     if last:
         tokens_ref, target_ref, scale_ref = refs[:3]
         del refs[:3]
     act_ref, slope_ref = refs[:2]
     del refs[:2]
-    count, _, part, width = own_ref.shape
-    rows = normed_t_ref.shape[1]
-    for side, ref in enumerate((own_ref, other_ref)):
-        for index in range(count):
-            hidden = dot_nn(ref[index, 0], normed_t_ref[...])
-            phi = 0.5 * (1.0 + lax.erf(hidden * (0.5 ** 0.5)))
-            density = jnp.exp(-0.5 * hidden * hidden) * ((2.0 * jnp.pi) ** -0.5)
-            act_ref[side, index] = (hidden * phi).astype(BF16)
-            slope_ref[side, index] = phi + hidden * density
-    act = act_ref[...].reshape(2 * count * part, rows)
-    down = jnp.concatenate(
-        [own_ref[:, 1].reshape(count * part, width), other_ref[:, 1].reshape(count * part, width)],
-        axis=0,
-    )
+    width, rows = normed_t_ref.shape
+    total = act_ref.shape[1]
+    part = act_ref.shape[2]
+    downs = []
+    for side, group in enumerate((own, other)):
+        start = 0
+        for ref in group:
+            count = ref.shape[0]
+            hiddens = dot_nn(ref[:, 0].reshape(count * part, width), normed_t_ref[...])
+            for index in range(count):
+                hidden = hiddens[index * part:(index + 1) * part]
+                phi = 0.5 * (1.0 + lax.erf(hidden * (0.5 ** 0.5)))
+                density = jnp.exp(-0.5 * hidden * hidden) * ((2.0 * jnp.pi) ** -0.5)
+                act_ref[side, start + index] = (hidden * phi).astype(BF16)
+                slope_ref[side, start + index] = phi + hidden * density
+            downs.append(ref[:, 1].reshape(count * part, width))
+            start += count
+    act = act_ref[...].reshape(2 * total * part, rows)
+    down = jnp.concatenate(downs, axis=0)
     if not last:
         mixed_out = refs[0]
         part_sum = dot_tn(act, down)
@@ -503,14 +504,15 @@
 
 def forward(normed_t, own, other, mixed=None, finish=None):
     width, rows = normed_t.shape
-    count, _, part, _ = own.shape
+    part = own[0].shape[2]
+    total = sum(array.shape[0] for array in own)
     first, last = mixed is None, finish is not None
-    operands = [normed_t, own, other]
+    operands = [normed_t, *own, *other]
     if not first:
         operands.append(mixed)
     if last:
         operands.extend(finish)
-    piece = (2, count, part, rows)
+    piece = (2, total, part, rows)
     shapes = [jax.ShapeDtypeStruct(piece, BF16), jax.ShapeDtypeStruct(piece, F32)]
     scratch = []
     if last:
@@ -523,39 +525,115 @@
     else:
         shapes += [jax.ShapeDtypeStruct((rows, width), F32)]
     return pl.pallas_call(
-        functools.partial(forward_kernel, first, last),
+        functools.partial(forward_kernel, first, last, len(own)),
         out_shape=tuple(shapes),
         in_specs=[VMEM] * len(operands),
         out_specs=tuple([VMEM] * len(shapes)),
         scratch_shapes=scratch,
-        compiler_params=small_params(),
+        compiler_params=params(24),
         cost_estimate=COST,
         name="forward",
     )(*operands)
 
 
-def backward_kernel(side, quarter, add, *refs):
+def pack_kernel(mine_ref, x_ref, y_ref, *refs):
+    count = len(refs) - 3
+    arrivals, (all_ref, far_ref) = refs[:count], refs[-2:]
+    for index, ref in enumerate((mine_ref, x_ref, y_ref)):
+        all_ref[index] = ref[...]
+    for index, ref in enumerate(arrivals):
+        block = ref[...]
+        all_ref[3 + index] = block
+        far_ref[index] = block
+
+
+def pack(mine, x, y, arrivals, after):
+    count = len(arrivals)
+    return pl.pallas_call(
+        pack_kernel,
+        out_shape=(
+            jax.ShapeDtypeStruct((3 + count, *mine.shape), BF16),
+            jax.ShapeDtypeStruct((count, *mine.shape), BF16),
+        ),
+        in_specs=[VMEM] * (3 + count) + [ANY],
+        out_specs=(VMEM, VMEM),
+        compiler_params=params(16),
+        cost_estimate=COST,
+        name="pack",
+    )(mine, x, y, *arrivals, after)
+
+
+def turn_kernel(y_ref, y_far_ref, x_far_ref, a_ref, b_ref):
+    held = a_ref.shape[0] - 1
+    a_ref[0] = y_ref[...]
+    for index in range(held):
+        a_ref[1 + index] = y_far_ref[index]
+    for index in range(b_ref.shape[0]):
+        b_ref[index] = x_far_ref[held + index]
+
+
+def turn(y, y_far, x_far):
+    count = y_far.shape[0]
+    first = (count + 1) // 2
+    return pl.pallas_call(
+        turn_kernel,
+        out_shape=(
+            jax.ShapeDtypeStruct((first, *y.shape), BF16),
+            jax.ShapeDtypeStruct((count + 1 - first, *y.shape), BF16),
+        ),
+        in_specs=[VMEM] * 3,
+        out_specs=(VMEM, VMEM),
+        compiler_params=params(16),
+        cost_estimate=COST,
+        name="turn",
+    )(y, y_far, x_far)
+
+
+def tie_kernel(*refs):
+    pass
+
+
+def tie(array, after):
+    return pl.pallas_call(
+        tie_kernel,
+        out_shape=jax.ShapeDtypeStruct(array.shape, array.dtype),
+        in_specs=[ANY, ANY],
+        out_specs=ANY,
+        input_output_aliases={0: 0},
+        compiler_params=params(4),
+        cost_estimate=COST,
+        name="tie",
+    )(array, after)
+
+
+def backward_kernel(side, places, add, count, *refs):
     refs = list(refs)
-    back_ref, back_t_ref, normed_ref, near_ref, far_ref = refs[:5]
-    act_near, slope_near, act_far, slope_far, gain_in = refs[5:10]
-    del refs[:10]
+    back_ref, back_t_ref, normed_ref, gain_in = refs[:4]
+    del refs[:4]
+    weights, acts, slopes = refs[:count], refs[count:2 * count], refs[2 * count:3 * count]
+    del refs[:3 * count]
     arrived = refs.pop(0) if add else None
     up_ref, down_ref, gain_ref = refs
-    part, width = near_ref.shape[-2:]
-    far = far_ref.shape[0]
-    chunk = (far + 1) * part
-    rows = back_ref.shape[0]
-
-    def joined(near, other):
-        return jnp.concatenate([near, other.reshape(far * part, other.shape[-1])], axis=0)
-
-    slope = joined(slope_near[side, quarter], slope_far[side])
-    back_act = dot_nn(joined(near_ref[quarter, 1], far_ref[:, 1]), back_t_ref[...])
+    rows, width = back_ref.shape
+
+    def joined(values):
+        flat = [value.reshape(-1, value.shape[-1]) for value in values]
+        return flat[0] if count == 1 else jnp.concatenate(flat, axis=0)
+
+    def rows_of(which):
+        return joined([
+            ref[w:w + n, which] for ref, (w, a, n) in zip(weights, places)
+        ])
+
+    slope = joined([ref[side, a:a + n] for ref, (w, a, n) in zip(slopes, places)])
+    act = joined([ref[side, a:a + n] for ref, (w, a, n) in zip(acts, places)])
+    chunk = act.shape[0]
+    back_act = dot_nn(rows_of(1), back_t_ref[...])
     back_hidden = (back_act * slope).astype(BF16)
     grad_up = dot_nn(back_hidden, normed_ref[...])
-    up = joined(near_ref[quarter, 0], far_ref[:, 0]).astype(F32)
+    up = rows_of(0).astype(F32)
     gain_ref[...] = gain_in[...] + jnp.sum(grad_up * up, axis=0, keepdims=True)
-    grad_down = dot_nn(joined(act_near[side, quarter], act_far[side]), back_ref[...])
+    grad_down = dot_nn(act, back_ref[...])
     if add:
         grad_up += arrived[0].reshape(chunk, width).astype(F32)
         grad_down += arrived[1].reshape(chunk, width).astype(F32)
@@ -563,33 +641,32 @@
     down_ref[...] = grad_down.astype(BF16).reshape(down_ref.shape)
 
 
-def backward(
-    side, quarter, common, near, far, act_near, slope_near, act_far, slope_far, gain, arrived
-):
-    back, back_t, normed = common
-    rows, width = back.shape
-    part = near.shape[2]
-    count = far.shape[0] + 1
-    operands = [back, back_t, normed, near, far, act_near, slope_near, act_far, slope_far, gain]
+def backward(side, common, gain, pieces, arrived):
+    rows, width = common[0].shape
+    part = pieces[0][0].shape[2]
+    places = tuple((piece[1], piece[4], piece[5]) for piece in pieces)
+    count = sum(piece[5] for piece in pieces)
+    operands = [*common, gain]
+    for which in (0, 2, 3):
+        operands += [piece[which] for piece in pieces]
+    body = functools.partial(backward_kernel, side, places, arrived is not None, len(pieces))
     if arrived is None:
-        def body(*refs):
+        def run(*refs):
             grads, gain_ref = refs[-2:]
-            backward_kernel(
-                side, quarter, False, *refs[:-2], grads.at[0], grads.at[1], gain_ref
-            )
+            body(*refs[:-2], grads.at[0], grads.at[1], gain_ref)
 
         shapes = [jax.ShapeDtypeStruct((2, count, part, width), BF16)]
     else:
         operands.append(arrived)
-        body = functools.partial(backward_kernel, side, quarter, True)
+        run = body
         shapes = [jax.ShapeDtypeStruct((count, part, width), BF16)] * 2
     shapes.append(jax.ShapeDtypeStruct((1, width), F32))
     return pl.pallas_call(
-        body,
+        run,
         out_shape=tuple(shapes),
         in_specs=[VMEM] * len(operands),
         out_specs=tuple([VMEM] * len(shapes)),
-        compiler_params=small_params(),
+        compiler_params=params(20),
         cost_estimate=COST,
         name="backward",
     )(*operands)
@@ -618,7 +695,7 @@
         out_shape=tuple(shapes),
         in_specs=[VMEM] * len(operands),
         out_specs=tuple([VMEM] * len(shapes)),
-        compiler_params=small_params(),
+        compiler_params=params(16),
         cost_estimate=COST,
         name="totals",
     )(*operands)
@@ -650,7 +727,7 @@
         out_shape=jax.ShapeDtypeStruct((part + (0 if vector is None else 32), width), BF16),
         in_specs=[VMEM] * len(operands),
         out_specs=VMEM,
-        compiler_params=small_params(),
+        compiler_params=params(16),
         cost_estimate=COST,
         name="collect",
     )(*operands)
@@ -688,7 +765,7 @@
         in_specs=[SMEM] + [VMEM] * 4,
         out_specs=tuple([VMEM] * len(shapes)),
         scratch_shapes=[pltpu.VMEM((4 * part, width), F32)],
-        compiler_params=small_params(),
+        compiler_params=params(16),
         cost_estimate=COST,
         name="place",
     )(group, *quarters)
@@ -726,39 +803,54 @@
         return lax.ppermute(array, "ray", pairs)
 
     mine = own_quarter(group, up_weight, down_weight, part)
-    far = [along(mine, -shift) for shift in range(1, depth)]
-    near = jnp.stack([mine] + [beside(mine, flip) for flip in (1, 2, 3)])
-    near_other = partner(near)
-    far = jnp.stack(far)
-    far = [far] + [beside(far, flip) for flip in (1, 2, 3)]
-    far_other = [partner(array) for array in far]
+    arrivals = [along(mine, -shift) for shift in range(1, depth)]
+    x, y = beside(mine, 1), beside(mine, 2)
 
     pixels = ray_pixel[0].reshape(ray_count, rows)
     rendered = render(
         me, block_owner, tile_lists, opacity, tile_counts.reshape(1, rows), pixels,
-        gaussian_features, (far[0],),
+        gaussian_features,
     )
-    target = lax.all_to_all(rendered, "ray", split_axis=0, concat_axis=0, tiled=True)
+    first, far = pack(mine, x, y, arrivals, rendered)
+    x_far, y_far = beside(far, 1), beside(far, 2)
+    first_other = partner(first)
     tokens, normed, normed_t = prepare_tokens(
         me, block_owner, pixels, image_tokens, layer_norm_gain.reshape(1, width)
     )
-    act_near, slope_near, mixed = forward(normed_t, near, near_other)
-    act_far, slope_far = [None] * 4, [None] * 4
-    for quarter in (0, 1, 2):
-        act_far[quarter], slope_far[quarter], mixed = forward(
-            normed_t, far[quarter], far_other[quarter], mixed
-        )
-    act_far[3], slope_far[3], back, back_t, small = forward(
-        normed_t, far[3], far_other[3], mixed, (tokens, target, layer_scale.reshape(1, width))
+    rendered = tie(rendered, normed)
+    target = lax.all_to_all(rendered, "ray", split_axis=0, concat_axis=0, tiled=True)
+    passed_x, passed_y = turn(y, y_far, x_far)
+    d_low, d_high = beside(passed_x, 1), beside(passed_y, 2)
+    act_first, slope_first, mixed = forward(normed_t, [first], [first_other])
+    x_far, y_far = tie(x_far, mixed), tie(y_far, mixed)
+    x_other, y_other = partner(x_far), partner(y_far)
+    act_next, slope_next, mixed = forward(normed_t, [x_far, y_far], [x_other, y_other], mixed)
+    d_low, d_high = tie(d_low, mixed), tie(d_high, mixed)
+    low_other, high_other = partner(d_low), partner(d_high)
+    act_last, slope_last, back, back_t, small = forward(
+        normed_t, [d_low, d_high], [low_other, high_other], mixed,
+        (tokens, target, layer_scale.reshape(1, width)),
     )
     common = (back, back_t, normed)
+    held = {
+        0: (first, x_far, y_far, d_low, d_high),
+        1: (first_other, x_other, y_other, low_other, high_other),
+    }
+    low = d_low.shape[0]
 
     def grads(side, quarter, gain, arrived):
-        weights = (near, far) if side == 0 else (near_other, far_other)
-        return backward(
-            side, quarter, common, weights[0], weights[1][quarter], act_near, slope_near,
-            act_far[quarter], slope_far[quarter], gain, arrived,
-        )
+        firsts, xs, ys, lows, highs = held[side]
+        start = (firsts, quarter, act_first, slope_first, quarter, 1)
+        pieces = {
+            0: [start, (firsts, 3, act_first, slope_first, 3, depth - 1)],
+            1: [start, (xs, 0, act_next, slope_next, 0, depth - 1)],
+            2: [start, (ys, 0, act_next, slope_next, depth - 1, depth - 1)],
+            3: [
+                (lows, 0, act_last, slope_last, 0, low),
+                (highs, 0, act_last, slope_last, low, depth - low),
+            ],
+        }[quarter]
+        return backward(side, common, gain, pieces, arrived)
 
     gain = jnp.zeros((1, width), F32)
     arrived, sums, sent = {}, {}, {}

time: 239 us -> 197 us (0.82)
  waiting for transfers between devices: 114 us -> 74.1 us
  local copies, waits for them, and re-layouts: 15.6 us -> 20.7 us
  starting transfers between devices: 47.2 us -> 43 us
    ppermute x18, waiting for transfers between devices: 87.2 us -> 62 us  [beside(): lax.ppermute(array, 'grp', [(g, g ^ flip) for g in range(group_count)])]
    ppermute x9, waiting for transfers between devices: 17.2 us -> 0.73 us  [along(): return lax.ppermute(array, 'ray', pairs)]
    ppermute x18, starting transfers between devices: 24.9 us -> 18.4 us  [beside(): lax.ppermute(array, 'grp', [(g, g ^ flip) for g in range(group_count)])]
    unnamed x63 -> x71, local copies, waits for them, and re-layouts: 13.8 us -> 19.4 us
    pallas_call x13 -> x18, Pallas kernels: 30.1 us -> 32.5 us  [the longest x8 16.5 us: backward(): pl.pallas_call(run, out_shape=tuple(shapes), in_specs=[VMEM] * len(operan...]
  transfers between devices with their start and end apart: 40 -> 40, of which waited for: 15 -> 17; matrix products, arithmetic and copies ran while one was open for 1% -> 1% of each run, Pallas kernels for 12% -> 21%
where the time goes in v4:
time: 197 us; the launch traced here: 193 us
  waiting for transfers between devices  74.1 us (38%)
  Pallas kernels  51.1 us (26%)
  starting transfers between devices  43 us (22%)
  local copies, waits for them, and re-layouts  20.7 us (11%)
  between operations  2.91 us (1%)
    ppermute x18, waiting for transfers between devices, beside(): lax.ppermute(array, 'grp', [(g, g ^ flip) for g in range(group_count)])  62 us
    unnamed x71, local copies, waits for them, and re-layouts  19.4 us
    ppermute x18, starting transfers between devices, beside(): lax.ppermute(array, 'grp', [(g, g ^ flip) for g in range(group_count)])  18.4 us
    pallas_call x8, Pallas kernels, backward(): pl.pallas_call(run, out_shape=tuple(shapes), in_specs=[VMEM] * len(operan...  16.5 us
    ppermute x9, starting transfers between devices, along(): return lax.ppermute(array, 'ray', pairs)  14.3 us
    pallas_call x3, Pallas kernels, forward(): pl.pallas_call(functools.partial(forward_kernel, first, last, len(own)),...  12.9 us
    pallas_call x1, Pallas kernels, render(): pl.pallas_call(functools.partial(render_kernel, ray_count), out_shape=jax...  11.8 us
    ppermute x12, waiting for transfers between devices, partner(): return lax.ppermute(array, 'ray', [(r, r ^ flip) for r in range(ray_count)])  11.3 us
  transfers between devices with their start and end apart: 40, of which 17 were waited for; matrix products, arithmetic and copies ran while one was open for 1% of the time, Pallas kernels for 21%

profile of v4, /device:TPU:8, one launch (start us, length us, event | category | flops | bytes accessed | tf_op | source)
XLA Modules:
  0.0 193.3 jit_solution(2836728743362619904)
XLA Ops:
  2.9 1.6 collective-permute-start
  6.5 2.6 %collective-permute-start.3 = (bf16[2,64,1024]{2,1,0:T(8,128)(2,1)S(1)}, bf16[2,64,1024]{2,1,0:T(8,128)(2,1)S(1)}, u32[]{:S(2)}, u32[]{:S(2)}) collective-permute-start(bf16[2,64,1024]{2,1,0:T(8,128)(2,1)S(1)} %quarter.1.mine_ref), channel_id=1, source_target_pairs={{0,4},{1,5},{2,6},{3,7},{4,0},{5,1},{6,2},{7,3},{8,12},{9,13},{10,... | collective-permute-start | bytes 786440 | tf_op jit(solution)/shard_map/ppermute | solution.py:803
  9.1 2.5 %collective-permute-start.4 = (bf16[2,64,1024]{2,1,0:T(8,128)(2,1)S(1)}, bf16[2,64,1024]{2,1,0:T(8,128)(2,1)S(1)}, u32[]{:S(2)}, u32[]{:S(2)}) collective-permute-start(bf16[2,64,1024]{2,1,0:T(8,128)(2,1)S(1)} %quarter.1.mine_ref), channel_id=1, source_target_pairs={{0,2},{1,3},{2,4},{3,5},{4,6},{5,7},{6,0},{7,1},{8,10},{9,11},{10,... | collective-permute-start | bytes 786440 | tf_op jit(solution)/shard_map/ppermute | solution.py:803
  18.1 11.8 %render.1.refs_3_.refs_0_ = bf16[512,1024]{1,0:T(8,128)(2,1)S(1)} custom-call(s32[1]{0:T(128)} %bitcast.1.me_ref, s32[1,8]{1,0:T(1,128)S(1)} %copy-done.34, s32[32,512]{1,0:T(8,128)S(1)} %copy-done.29, f32[32,512]{1,0:T(8,128)S(1)} %copy-done.30, s32[1,512]{1,0:T(1,128)S(1)} %bitcast.14, s32[8,512]{1,0:T(8,128)S(1)} %reshape_squeeze.3.pixels_ref, ...), custom_call_target="tpu_custom_call" | custom-call | flops 1048576 | bytes 65536 | tf_op jit(solution)/shard_map/render/pallas_call | solution.py:107
  30.7 1.6 pack.1
  33.3 3.4 %tokens.1 = (bf16[512,1024]{1,0:T(8,128)(2,1)S(1)}, bf16[512,1024]{1,0:T(8,128)(2,1)S(1)}, bf16[1024,512]{1,0:T(8,128)(2,1)S(1)}) custom-call(s32[1]{0:T(128)} %bitcast.1.me_ref, s32[1,8]{1,0:T(1,128)S(1)} %copy-done.34, s32[8,512]{1,0:T(8,128)S(1)} %reshape_squeeze.3.pixels_ref, bf16[512,1024]{1,0:T(8,128)(2,1)S(1)} %copy-done.26, f32[1,1024]{1,0:T(1,128)S(1)} %bitcast.11), custom_call_target="tpu_custom_call" | custom-call | flops 1048576 | bytes 65536 | tf_op jit(solution)/shard_map/tokens/pallas_call | solution.py:166
  39.0 5.3 %all-to-all-start = ((bf16[8,64,1024]{2,1,0:T(8,128)(2,1)}), bf16[8,64,1024]{2,1,0:T(8,128)(2,1)}, u32[]{:S(2)}, u32[]{:S(2)}) async-start(bf16[8,64,1024]{2,1,0:T(8,128)(2,1)} %bitcast.10), calls=%async_computation | async-start | bytes 2097152 | tf_op jit(solution)/shard_map/all_to_all | solution.py:821
  44.4 8.2 %collective-permute-done.5.y_far_ref.refs_0_ = bf16[3,2,64,1024]{3,2,1,0:T(8,128)(2,1)} collective-permute-done((bf16[3,2,64,1024]{3,2,1,0:T(8,128)(2,1)}, bf16[3,2,64,1024]{3,2,1,0:T(8,128)(2,1)}, u32[]{:S(2)}, u32[]{:S(2)}) %collective-permute-start.5) | collective-permute-done | bytes 786464 | tf_op jit(solution)/shard_map/ppermute | solution.py:796
  57.7 3.7 %forward.3 = (bf16[2,6,64,512]{3,2,1,0:T(8,128)(2,1)S(1)}, f32[2,6,64,512]{3,2,1,0:T(8,128)S(1)}, f32[512,1024]{1,0:T(8,128)S(1)}) custom-call(bf16[1024,512]{1,0:T(8,128)(2,1)S(1)} %copy-done.15, bf16[6,2,64,1024]{3,2,1,0:T(8,128)(2,1)} %get-tuple-element.57.refs_1_.refs_4_.refs_5_, bf16[6,2,64,1024]{3,2,1,0:T(8,128)(2,1)S(1)} %copy-done.1), custom_call_target="tpu_custom_call" | custom-call | flops 1048576 | bytes 65536 | tf_op jit(solution)/shard_map/forward/pallas_call | solution.py:527
  65.0 3.7 %forward.4 = (bf16[2,6,64,512]{3,2,1,0:T(8,128)(2,1)S(1)}, f32[2,6,64,512]{3,2,1,0:T(8,128)S(1)}, f32[512,1024]{1,0:T(8,128)S(1)}) custom-call(bf16[1024,512]{1,0:T(8,128)(2,1)S(1)} %copy-done.15, bf16[3,2,64,1024]{3,2,1,0:T(8,128)(2,1)S(1)} %tie.5.refs_1_.refs_5_, bf16[3,2,64,1024]{3,2,1,0:T(8,128)(2,1)} %tie.6.refs_2_.refs_5_, ...), custom_call_target="tpu_custom_call" | custom-call | flops 1048576 | bytes 65536 | tf_op jit(solution)/shard_map/forward/pallas_call | solution.py:527
  68.8 8.3 %collective-permute-done.11.refs_0_ = bf16[2,2,64,1024]{3,2,1,0:T(8,128)(2,1)} collective-permute-done((bf16[2,2,64,1024]{3,2,1,0:T(8,128)(2,1)S(1)}, bf16[2,2,64,1024]{3,2,1,0:T(8,128)(2,1)}, u32[]{:S(2)}, u32[]{:S(2)}) %collective-permute-start.11) | collective-permute-done | bytes 524320 | tf_op jit(solution)/shard_map/ppermute | solution.py:796
  79.6 2.2 %collective-permute-done.12.refs_3_.refs_4_ = bf16[2,2,64,1024]{3,2,1,0:T(8,128)(2,1)} collective-permute-done((bf16[2,2,64,1024]{3,2,1,0:T(8,128)(2,1)}, bf16[2,2,64,1024]{3,2,1,0:T(8,128)(2,1)}, u32[]{:S(2)}, u32[]{:S(2)}) %collective-permute-start.12) | collective-permute-done | bytes 524320 | tf_op jit(solution)/shard_map/ppermute | solution.py:799
  81.9 1.6 copy-done.6
  85.9 5.4 %forward.5 = (bf16[2,4,64,512]{3,2,1,0:T(8,128)(2,1)S(1)}, f32[2,4,64,512]{3,2,1,0:T(8,128)S(1)}, bf16[512,1024]{1,0:T(8,128)(2,1)S(1)}, bf16[1024,512]{1,0:T(8,128)(2,1)S(1)}, f32[8,1024]{1,0:T(8,128)S(1)}) custom-call(bf16[1024,512]{1,0:T(8,128)(2,1)S(1)} %copy-done.16, bf16[2,2,64,1024]{3,2,1,0:T(8,128)(2,1)} %tie.7.refs_1_.refs_4_, ...), custom_call_target="tpu_custom_call" | custom-call | flops 1048576 | bytes 65536 | tf_op jit(solution)/shard_map/forward/pallas_call | solution.py:527
  91.4 2.4 %backward.8 = (bf16[2,4,64,1024]{3,2,1,0:T(8,128)(2,1)S(1)}, f32[1,1024]{1,0:T(1,128)S(1)}) custom-call(bf16[512,1024]{1,0:T(8,128)(2,1)S(1)} %get-tuple-element.63.refs_0_, bf16[1024,512]{1,0:T(8,128)(2,1)S(1)} %get-tuple-element.64.refs_1_, bf16[512,1024]{1,0:T(8,128)(2,1)S(1)} %get-tuple-element.62.refs_1_.refs_2_, ...), custom_call_target="tpu_custom_call" | custom-call | flops 1048576 | bytes 65536 | tf_op jit(solution)/shard_map/backward/pallas_call | solution.py:664
  96.6 2.4 %backward.10 = (bf16[4,64,1024]{2,1,0:T(8,128)(2,1)S(1)}, bf16[4,64,1024]{2,1,0:T(8,128)(2,1)S(1)}, f32[1,1024]{1,0:T(1,128)S(1)}) custom-call(bf16[512,1024]{1,0:T(8,128)(2,1)S(1)} %get-tuple-element.63.refs_0_, bf16[1024,512]{1,0:T(8,128)(2,1)S(1)} %get-tuple-element.64.refs_1_, bf16[512,1024]{1,0:T(8,128)(2,1)S(1)} %get-tuple-element.62.refs_1_.refs_2_, ...), custom_call_target="tpu_custom_call" | custom-call | flops 1048576 | bytes 65536 | tf_op jit(solution)/shard_map/backward/pallas_call | solution.py:664
  100.3 2.5 %backward.12 = (bf16[4,64,1024]{2,1,0:T(8,128)(2,1)S(1)}, bf16[4,64,1024]{2,1,0:T(8,128)(2,1)S(1)}, f32[1,1024]{1,0:T(1,128)S(1)}) custom-call(bf16[512,1024]{1,0:T(8,128)(2,1)S(1)} %get-tuple-element.63.refs_0_, bf16[1024,512]{1,0:T(8,128)(2,1)S(1)} %get-tuple-element.64.refs_1_, bf16[512,1024]{1,0:T(8,128)(2,1)S(1)} %get-tuple-element.62.refs_1_.refs_2_, ...), custom_call_target="tpu_custom_call" | custom-call | flops 1048576 | bytes 65536 | tf_op jit(solution)/shard_map/backward/pallas_call | solution.py:664
  106.3 2.7 %backward.14 = (bf16[4,64,1024]{2,1,0:T(8,128)(2,1)S(1)}, bf16[4,64,1024]{2,1,0:T(8,128)(2,1)S(1)}, f32[1,1024]{1,0:T(1,128)S(1)}) custom-call(bf16[512,1024]{1,0:T(8,128)(2,1)S(1)} %get-tuple-element.63.refs_0_, bf16[1024,512]{1,0:T(8,128)(2,1)S(1)} %get-tuple-element.64.refs_1_, bf16[512,1024]{1,0:T(8,128)(2,1)S(1)} %get-tuple-element.62.refs_1_.refs_2_, ...), custom_call_target="tpu_custom_call" | custom-call | flops 1048576 | bytes 65536 | tf_op jit(solution)/shard_map/backward/pallas_call | solution.py:664
  111.2 7.9 %collective-permute-done.24.refs_1_ = bf16[4,64,1024]{2,1,0:T(8,128)(2,1)S(1)} collective-permute-done((bf16[4,64,1024]{2,1,0:T(8,128)(2,1)S(1)}, bf16[4,64,1024]{2,1,0:T(8,128)(2,1)S(1)}, u32[]{:S(2)}, u32[]{:S(2)}) %collective-permute-start.24) | collective-permute-done | bytes 524320 | tf_op jit(solution)/shard_map/ppermute | solution.py:796
  121.2 3.1 %backward.15 = (bf16[4,64,1024]{2,1,0:T(8,128)(2,1)S(1)}, bf16[4,64,1024]{2,1,0:T(8,128)(2,1)S(1)}, f32[1,1024]{1,0:T(1,128)S(1)}) custom-call(bf16[512,1024]{1,0:T(8,128)(2,1)S(1)} %get-tuple-element.63.refs_0_, bf16[1024,512]{1,0:T(8,128)(2,1)S(1)} %get-tuple-element.64.refs_1_, bf16[512,1024]{1,0:T(8,128)(2,1)S(1)} %get-tuple-element.62.refs_1_.refs_2_, ...), custom_call_target="tpu_custom_call" | custom-call | flops 1048576 | bytes 65536 | tf_op jit(solution)/shard_map/backward/pallas_call | solution.py:664
  124.4 5.9 %collective-permute-done.26.refs_3_ = bf16[4,64,1024]{2,1,0:T(8,128)(2,1)S(1)} collective-permute-done((bf16[4,64,1024]{2,1,0:T(8,128)(2,1)S(1)}, bf16[4,64,1024]{2,1,0:T(8,128)(2,1)S(1)}, u32[]{:S(2)}, u32[]{:S(2)}) %collective-permute-start.26) | collective-permute-done | bytes 524320 | tf_op jit(solution)/shard_map/ppermute | solution.py:796
  130.3 4.9 %collective-permute-done.25.refs_2_ = bf16[4,64,1024]{2,1,0:T(8,128)(2,1)S(1)} collective-permute-done((bf16[4,64,1024]{2,1,0:T(8,128)(2,1)S(1)}, bf16[4,64,1024]{2,1,0:T(8,128)(2,1)S(1)}, u32[]{:S(2)}, u32[]{:S(2)}) %collective-permute-start.25) | collective-permute-done | bytes 524320 | tf_op jit(solution)/shard_map/ppermute | solution.py:796
  135.5 2.5 %collective-permute-start.33 = (bf16[64,1024]{1,0:T(8,128)(2,1)S(1)}, bf16[64,1024]{1,0:T(8,128)(2,1)S(1)}, u32[]{:S(2)}, u32[]{:S(2)}) collective-permute-start(bf16[64,1024]{1,0:T(8,128)(2,1)S(1)} %get-tuple-element.99), channel_id=1, source_target_pairs={{0,2},{1,3},{2,4},{3,5},{4,6},{5,7},{6,0},{7,1},{8,10},{9,11},{10,... | collective-permute-start | bytes 393224 | tf_op jit(solution)/shard_map/ppermute | solution.py:803
  139.0 2.6 %collective-permute-done.18.refs_1_ = bf16[4,64,1024]{2,1,0:T(8,128)(2,1)S(1)} collective-permute-done((bf16[4,64,1024]{2,1,0:T(8,128)(2,1)S(1)}, bf16[4,64,1024]{2,1,0:T(8,128)(2,1)S(1)}, u32[]{:S(2)}, u32[]{:S(2)}) %collective-permute-start.18) | collective-permute-done | bytes 524320 | tf_op jit(solution)/shard_map/ppermute | solution.py:796
  142.8 9.6 %collective-permute-done.20.refs_3_ = bf16[4,64,1024]{2,1,0:T(8,128)(2,1)S(1)} collective-permute-done((bf16[4,64,1024]{2,1,0:T(8,128)(2,1)S(1)}, bf16[4,64,1024]{2,1,0:T(8,128)(2,1)S(1)}, u32[]{:S(2)}, u32[]{:S(2)}) %collective-permute-start.20) | collective-permute-done | bytes 524320 | tf_op jit(solution)/shard_map/ppermute | solution.py:796
  152.4 4.1 %collective-permute-done.19.refs_2_ = bf16[4,64,1024]{2,1,0:T(8,128)(2,1)S(1)} collective-permute-done((bf16[4,64,1024]{2,1,0:T(8,128)(2,1)S(1)}, bf16[4,64,1024]{2,1,0:T(8,128)(2,1)S(1)}, u32[]{:S(2)}, u32[]{:S(2)}) %collective-permute-start.19) | collective-permute-done | bytes 524320 | tf_op jit(solution)/shard_map/ppermute | solution.py:796
  156.7 2.5 %collective-permute-start.21 = (bf16[64,1024]{1,0:T(8,128)(2,1)S(1)}, bf16[64,1024]{1,0:T(8,128)(2,1)S(1)}, u32[]{:S(2)}, u32[]{:S(2)}) collective-permute-start(bf16[64,1024]{1,0:T(8,128)(2,1)S(1)} %get-tuple-element.87), channel_id=1, source_target_pairs={{0,2},{1,3},{2,4},{3,5},{4,6},{5,7},{6,0},{7,1},{8,10},{9,11},{10,... | collective-permute-start | bytes 393224 | tf_op jit(solution)/shard_map/ppermute | solution.py:803
  160.9 2.9 %collective-permute-start.28 = (f32[8,1024]{1,0:T(8,128)S(1)}, f32[8,1024]{1,0:T(8,128)S(1)}, u32[]{:S(2)}, u32[]{:S(2)}) collective-permute-start(f32[8,1024]{1,0:T(8,128)S(1)} %add.9), channel_id=1, source_target_pairs={{0,2},{1,3},{2,0},{3,1},{4,6},{5,7},{6,4},{7,5},{8,10},{9,11},{10,... | collective-permute-start | bytes 98312 | tf_op jit(solution)/shard_map/ppermute | solution.py:799
  164.4 3.6 %collective-permute-done.28 = f32[8,1024]{1,0:T(8,128)S(1)} collective-permute-done((f32[8,1024]{1,0:T(8,128)S(1)}, f32[8,1024]{1,0:T(8,128)S(1)}, u32[]{:S(2)}, u32[]{:S(2)}) %collective-permute-start.28) | collective-permute-done | bytes 32800 | tf_op jit(solution)/shard_map/ppermute | solution.py:799
  168.7 4.2 %collective-permute-done.29 = f32[8,1024]{1,0:T(8,128)S(1)} collective-permute-done((f32[8,1024]{1,0:T(8,128)S(1)}, f32[8,1024]{1,0:T(8,128)S(1)}, u32[]{:S(2)}, u32[]{:S(2)}) %collective-permute-start.29) | collective-permute-done | bytes 32800 | tf_op jit(solution)/shard_map/ppermute | solution.py:799
  174.6 1.9 collective-permute-start.32
  178.5 9.3 %collective-permute-done.37.c_ref = bf16[64,1024]{1,0:T(8,128)(2,1)S(1)} collective-permute-done((bf16[64,1024]{1,0:T(8,128)(2,1)S(1)}, bf16[64,1024]{1,0:T(8,128)(2,1)S(1)}, u32[]{:S(2)}, u32[]{:S(2)}) %collective-permute-start.37) | collective-permute-done | bytes 131104 | tf_op jit(solution)/shard_map/ppermute | solution.py:796
  (159 shorter events, 53.1 us)
Async XLA Ops:
  2.9 27.0 %collective-permute-start = (bf16[2,64,1024]{2,1,0:T(8,128)(2,1)S(1)}, bf16[2,64,1024]{2,1,0:T(8,128)(2,1)S(1)}, u32[]{:S(2)}, u32[]{:S(2)}) collective-permute-start(bf16[2,64,1024]{2,1,0:T(8,128)(2,1)S(1)} %quarter.1.mine_ref), channel_id=1, source_target_pairs={{0,16},{8,24},{16,0},{24,8},{1,17},{9,25},{17,1},{25,9},{2,18},{10... | collective-permute-start | bytes 786440 | tf_op jit(solution)/shard_map/ppermute | solution.py:796
  4.5 25.4 %collective-permute-start.1 = (bf16[2,64,1024]{2,1,0:T(8,128)(2,1)S(1)}, bf16[2,64,1024]{2,1,0:T(8,128)(2,1)S(1)}, u32[]{:S(2)}, u32[]{:S(2)}) collective-permute-start(bf16[2,64,1024]{2,1,0:T(8,128)(2,1)S(1)} %quarter.1.mine_ref), channel_id=1, source_target_pairs={{0,8},{8,0},{16,24},{24,16},{1,9},{9,1},{17,25},{25,17},{2,10},{10... | collective-permute-start | bytes 786440 | tf_op jit(solution)/shard_map/ppermute | solution.py:796
  6.0 23.9 %collective-permute-start.2 = (bf16[2,64,1024]{2,1,0:T(8,128)(2,1)S(1)}, bf16[2,64,1024]{2,1,0:T(8,128)(2,1)S(1)}, u32[]{:S(2)}, u32[]{:S(2)}) collective-permute-start(bf16[2,64,1024]{2,1,0:T(8,128)(2,1)S(1)} %quarter.1.mine_ref), channel_id=1, source_target_pairs={{0,6},{1,7},{2,0},{3,1},{4,2},{5,3},{6,4},{7,5},{8,14},{9,15},{10,... | collective-permute-start | bytes 786440 | tf_op jit(solution)/shard_map/ppermute | solution.py:803
  6.5 23.5 %collective-permute-start.3 = (bf16[2,64,1024]{2,1,0:T(8,128)(2,1)S(1)}, bf16[2,64,1024]{2,1,0:T(8,128)(2,1)S(1)}, u32[]{:S(2)}, u32[]{:S(2)}) collective-permute-start(bf16[2,64,1024]{2,1,0:T(8,128)(2,1)S(1)} %quarter.1.mine_ref), channel_id=1, source_target_pairs={{0,4},{1,5},{2,6},{3,7},{4,0},{5,1},{6,2},{7,3},{8,12},{9,13},{10,... | collective-permute-start | bytes 786440 | tf_op jit(solution)/shard_map/ppermute | solution.py:803
  9.1 21.6 %collective-permute-start.4 = (bf16[2,64,1024]{2,1,0:T(8,128)(2,1)S(1)}, bf16[2,64,1024]{2,1,0:T(8,128)(2,1)S(1)}, u32[]{:S(2)}, u32[]{:S(2)}) collective-permute-start(bf16[2,64,1024]{2,1,0:T(8,128)(2,1)S(1)} %quarter.1.mine_ref), channel_id=1, source_target_pairs={{0,2},{1,3},{2,4},{3,5},{4,6},{5,7},{6,0},{7,1},{8,10},{9,11},{10,... | collective-permute-start | bytes 786440 | tf_op jit(solution)/shard_map/ppermute | solution.py:803
  32.3 22.8 %collective-permute-start.8 = (bf16[6,2,64,1024]{3,2,1,0:T(8,128)(2,1)}, bf16[6,2,64,1024]{3,2,1,0:T(8,128)(2,1)S(1)}, u32[]{:S(2)}, u32[]{:S(2)}) collective-permute-start(bf16[6,2,64,1024]{3,2,1,0:T(8,128)(2,1)} %get-tuple-element.57.refs_1_.refs_4_.refs_5_), channel_id=1, source_target_pairs={{0,1},{1,0},{2,3},{3,2},{4,5},{5,4},{6,7},{7,6},{8,9},{9,8},{10,11... | collective-permute-start | bytes 4718600 | tf_op jit(solution)/shard_map/ppermute | solution.py:799
  32.3 20.3 %collective-permute-start.5 = (bf16[3,2,64,1024]{3,2,1,0:T(8,128)(2,1)}, bf16[3,2,64,1024]{3,2,1,0:T(8,128)(2,1)}, u32[]{:S(2)}, u32[]{:S(2)}) collective-permute-start(bf16[3,2,64,1024]{3,2,1,0:T(8,128)(2,1)} %get-tuple-element.55), channel_id=1, source_target_pairs={{0,16},{8,24},{16,0},{24,8},{1,17},{9,25},{17,1},{25,9},{2,18},{10... | collective-permute-start | bytes 2359304 | tf_op jit(solution)/shard_map/ppermute | solution.py:796
  32.8 19.9 %collective-permute-start.6 = (bf16[3,2,64,1024]{3,2,1,0:T(8,128)(2,1)}, bf16[3,2,64,1024]{3,2,1,0:T(8,128)(2,1)S(1)}, u32[]{:S(2)}, u32[]{:S(2)}) collective-permute-start(bf16[3,2,64,1024]{3,2,1,0:T(8,128)(2,1)} %get-tuple-element.55), channel_id=1, source_target_pairs={{0,8},{8,0},{16,24},{24,16},{1,9},{9,1},{17,25},{25,17},{2,10},{10... | collective-permute-start | bytes 2359304 | tf_op jit(solution)/shard_map/ppermute | solution.py:796
  39.0 40.6 %all-to-all-start = ((bf16[8,64,1024]{2,1,0:T(8,128)(2,1)}), bf16[8,64,1024]{2,1,0:T(8,128)(2,1)}, u32[]{:S(2)}, u32[]{:S(2)}) async-start(bf16[8,64,1024]{2,1,0:T(8,128)(2,1)} %bitcast.10), calls=%async_computation | async-start | bytes 2097152 | tf_op jit(solution)/shard_map/all_to_all | solution.py:821
  62.6 14.4 %collective-permute-start.11 = (bf16[2,2,64,1024]{3,2,1,0:T(8,128)(2,1)S(1)}, bf16[2,2,64,1024]{3,2,1,0:T(8,128)(2,1)}, u32[]{:S(2)}, u32[]{:S(2)}) collective-permute-start(bf16[2,2,64,1024]{3,2,1,0:T(8,128)(2,1)S(1)} %get-tuple-element.60), channel_id=1, source_target_pairs={{0,16},{8,24},{16,0},{24,8},{1,17},{9,25},{17,1},{25,9},{2,18},{10... | collective-permute-start | bytes 1572872 | tf_op jit(solution)/shard_map/ppermute | solution.py:796
  64.1 14.2 %collective-permute-start.7 = (bf16[2,2,64,1024]{3,2,1,0:T(8,128)(2,1)S(1)}, bf16[2,2,64,1024]{3,2,1,0:T(8,128)(2,1)}, u32[]{:S(2)}, u32[]{:S(2)}) collective-permute-start(bf16[2,2,64,1024]{3,2,1,0:T(8,128)(2,1)S(1)} %get-tuple-element.56), channel_id=1, source_target_pairs={{0,8},{8,0},{16,24},{24,16},{1,9},{9,1},{17,25},{25,17},{2,10},{10... | collective-permute-start | bytes 1572872 | tf_op jit(solution)/shard_map/ppermute | solution.py:796
  103.9 15.7 %collective-permute-start.17 = (bf16[2,4,64,1024]{3,2,1,0:T(8,128)(2,1)S(1)}, bf16[2,4,64,1024]{3,2,1,0:T(8,128)(2,1)S(1)}, u32[]{:S(2)}, u32[]{:S(2)}) collective-permute-start(bf16[2,4,64,1024]{3,2,1,0:T(8,128)(2,1)S(1)} %get-tuple-element.81), channel_id=1, source_target_pairs={{0,1},{1,0},{2,3},{3,2},{4,5},{5,4},{6,7},{7,6},{8,9},{9,8},{10,11... | collective-permute-start | bytes 3145736 | tf_op jit(solution)/shard_map/ppermute | solution.py:799
  104.4 14.8 %collective-permute-start.24 = (bf16[4,64,1024]{2,1,0:T(8,128)(2,1)S(1)}, bf16[4,64,1024]{2,1,0:T(8,128)(2,1)S(1)}, u32[]{:S(2)}, u32[]{:S(2)}) collective-permute-start(bf16[4,64,1024]{2,1,0:T(8,128)(2,1)S(1)} %get-tuple-element.91), channel_id=1, source_target_pairs={{0,8},{8,0},{16,24},{24,16},{1,9},{9,1},{17,25},{25,17},{2,10},{10... | collective-permute-start | bytes 1572872 | tf_op jit(solution)/shard_map/ppermute | solution.py:796
  104.9 25.4 %collective-permute-start.26 = (bf16[4,64,1024]{2,1,0:T(8,128)(2,1)S(1)}, bf16[4,64,1024]{2,1,0:T(8,128)(2,1)S(1)}, u32[]{:S(2)}, u32[]{:S(2)}) collective-permute-start(bf16[4,64,1024]{2,1,0:T(8,128)(2,1)S(1)} %get-tuple-element.93), channel_id=1, source_target_pairs={{0,24},{8,16},{16,8},{24,0},{1,25},{9,17},{17,9},{25,1},{2,26},{10... | collective-permute-start | bytes 1572872 | tf_op jit(solution)/shard_map/ppermute | solution.py:796
  109.1 26.1 %collective-permute-start.25 = (bf16[4,64,1024]{2,1,0:T(8,128)(2,1)S(1)}, bf16[4,64,1024]{2,1,0:T(8,128)(2,1)S(1)}, u32[]{:S(2)}, u32[]{:S(2)}) collective-permute-start(bf16[4,64,1024]{2,1,0:T(8,128)(2,1)S(1)} %get-tuple-element.92), channel_id=1, source_target_pairs={{0,16},{8,24},{16,0},{24,8},{1,17},{9,25},{17,1},{25,9},{2,18},{10... | collective-permute-start | bytes 1572872 | tf_op jit(solution)/shard_map/ppermute | solution.py:796
  110.7 31.0 %collective-permute-start.18 = (bf16[4,64,1024]{2,1,0:T(8,128)(2,1)S(1)}, bf16[4,64,1024]{2,1,0:T(8,128)(2,1)S(1)}, u32[]{:S(2)}, u32[]{:S(2)}) collective-permute-start(bf16[4,64,1024]{2,1,0:T(8,128)(2,1)S(1)} %get-tuple-element.83), channel_id=1, source_target_pairs={{0,8},{8,0},{16,24},{24,16},{1,9},{9,1},{17,25},{25,17},{2,10},{10... | collective-permute-start | bytes 1572872 | tf_op jit(solution)/shard_map/ppermute | solution.py:796
  119.1 33.2 %collective-permute-start.20 = (bf16[4,64,1024]{2,1,0:T(8,128)(2,1)S(1)}, bf16[4,64,1024]{2,1,0:T(8,128)(2,1)S(1)}, u32[]{:S(2)}, u32[]{:S(2)}) collective-permute-start(bf16[4,64,1024]{2,1,0:T(8,128)(2,1)S(1)} %get-tuple-element.85), channel_id=1, source_target_pairs={{0,24},{8,16},{16,8},{24,0},{1,25},{9,17},{17,9},{25,1},{2,26},{10... | collective-permute-start | bytes 1572872 | tf_op jit(solution)/shard_map/ppermute | solution.py:796
  119.6 36.9 %collective-permute-start.19 = (bf16[4,64,1024]{2,1,0:T(8,128)(2,1)S(1)}, bf16[4,64,1024]{2,1,0:T(8,128)(2,1)S(1)}, u32[]{:S(2)}, u32[]{:S(2)}) collective-permute-start(bf16[4,64,1024]{2,1,0:T(8,128)(2,1)S(1)} %get-tuple-element.84), channel_id=1, source_target_pairs={{0,16},{8,24},{16,0},{24,8},{1,17},{9,25},{17,1},{25,9},{2,18},{10... | collective-permute-start | bytes 1572872 | tf_op jit(solution)/shard_map/ppermute | solution.py:796
  135.5 24.9 %collective-permute-start.33 = (bf16[64,1024]{1,0:T(8,128)(2,1)S(1)}, bf16[64,1024]{1,0:T(8,128)(2,1)S(1)}, u32[]{:S(2)}, u32[]{:S(2)}) collective-permute-start(bf16[64,1024]{1,0:T(8,128)(2,1)S(1)} %get-tuple-element.99), channel_id=1, source_target_pairs={{0,2},{1,3},{2,4},{3,5},{4,6},{5,7},{6,0},{7,1},{8,10},{9,11},{10,... | collective-permute-start | bytes 393224 | tf_op jit(solution)/shard_map/ppermute | solution.py:803
  138.0 22.8 %collective-permute-start.34 = (bf16[64,1024]{1,0:T(8,128)(2,1)S(1)}, bf16[64,1024]{1,0:T(8,128)(2,1)S(1)}, u32[]{:S(2)}, u32[]{:S(2)}) collective-permute-start(bf16[64,1024]{1,0:T(8,128)(2,1)S(1)} %get-tuple-element.100), channel_id=1, source_target_pairs={{0,4},{1,5},{2,6},{3,7},{4,0},{5,1},{6,2},{7,3},{8,12},{9,13},{10,... | collective-permute-start | bytes 393224 | tf_op jit(solution)/shard_map/ppermute | solution.py:803
  141.6 22.1 %collective-permute-start.35 = (bf16[64,1024]{1,0:T(8,128)(2,1)S(1)}, bf16[64,1024]{1,0:T(8,128)(2,1)S(1)}, u32[]{:S(2)}, u32[]{:S(2)}) collective-permute-start(bf16[64,1024]{1,0:T(8,128)(2,1)S(1)} %get-tuple-element.101), channel_id=1, source_target_pairs={{0,6},{1,7},{2,0},{3,1},{4,2},{5,3},{6,4},{7,5},{8,14},{9,15},{10,... | collective-permute-start | bytes 393224 | tf_op jit(solution)/shard_map/ppermute | solution.py:803
  152.3 6.9 %collective-permute-start.27 = (f32[8,1024]{1,0:T(8,128)S(1)}, f32[8,1024]{1,0:T(8,128)S(1)}, u32[]{:S(2)}, u32[]{:S(2)}) collective-permute-start(f32[8,1024]{1,0:T(8,128)S(1)} %get-tuple-element.96), channel_id=1, source_target_pairs={{0,1},{1,0},{2,3},{3,2},{4,5},{5,4},{6,7},{7,6},{8,9},{9,8},{10,11... | collective-permute-start | bytes 98312 | tf_op jit(solution)/shard_map/ppermute | solution.py:799
  156.7 16.1 %collective-permute-start.21 = (bf16[64,1024]{1,0:T(8,128)(2,1)S(1)}, bf16[64,1024]{1,0:T(8,128)(2,1)S(1)}, u32[]{:S(2)}, u32[]{:S(2)}) collective-permute-start(bf16[64,1024]{1,0:T(8,128)(2,1)S(1)} %get-tuple-element.87), channel_id=1, source_target_pairs={{0,2},{1,3},{2,4},{3,5},{4,6},{5,7},{6,0},{7,1},{8,10},{9,11},{10,... | collective-permute-start | bytes 393224 | tf_op jit(solution)/shard_map/ppermute | solution.py:803
  159.3 13.6 %collective-permute-start.22 = (bf16[64,1024]{1,0:T(8,128)(2,1)S(1)}, bf16[64,1024]{1,0:T(8,128)(2,1)S(1)}, u32[]{:S(2)}, u32[]{:S(2)}) collective-permute-start(bf16[64,1024]{1,0:T(8,128)(2,1)S(1)} %get-tuple-element.88), channel_id=1, source_target_pairs={{0,4},{1,5},{2,6},{3,7},{4,0},{5,1},{6,2},{7,3},{8,12},{9,13},{10,... | collective-permute-start | bytes 393224 | tf_op jit(solution)/shard_map/ppermute | solution.py:803
  160.3 12.6 %collective-permute-start.23 = (bf16[64,1024]{1,0:T(8,128)(2,1)S(1)}, bf16[64,1024]{1,0:T(8,128)(2,1)S(1)}, u32[]{:S(2)}, u32[]{:S(2)}) collective-permute-start(bf16[64,1024]{1,0:T(8,128)(2,1)S(1)} %get-tuple-element.89), channel_id=1, source_target_pairs={{0,6},{1,7},{2,0},{3,1},{4,2},{5,3},{6,4},{7,5},{8,14},{9,15},{10,... | collective-permute-start | bytes 393224 | tf_op jit(solution)/shard_map/ppermute | solution.py:803
  160.9 7.2 %collective-permute-start.28 = (f32[8,1024]{1,0:T(8,128)S(1)}, f32[8,1024]{1,0:T(8,128)S(1)}, u32[]{:S(2)}, u32[]{:S(2)}) collective-permute-start(f32[8,1024]{1,0:T(8,128)S(1)} %add.9), channel_id=1, source_target_pairs={{0,2},{1,3},{2,0},{3,1},{4,6},{5,7},{6,4},{7,5},{8,10},{9,11},{10,... | collective-permute-start | bytes 98312 | tf_op jit(solution)/shard_map/ppermute | solution.py:799
  163.8 13.7 %collective-permute-start.36 = (bf16[64,1024]{1,0:T(8,128)(2,1)S(1)}, bf16[64,1024]{1,0:T(8,128)(2,1)S(1)}, u32[]{:S(2)}, u32[]{:S(2)}) collective-permute-start(bf16[64,1024]{1,0:T(8,128)(2,1)S(1)} %collect.3.a_ref), channel_id=1, source_target_pairs={{0,8},{8,0},{16,24},{24,16},{1,9},{9,1},{17,25},{25,17},{2,10},{10... | collective-permute-start | bytes 393224 | tf_op jit(solution)/shard_map/ppermute | solution.py:796
  173.0 16.0 %collective-permute-start.30 = (bf16[96,1024]{1,0:T(8,128)(2,1)S(1)}, bf16[96,1024]{1,0:T(8,128)(2,1)S(1)}, u32[]{:S(2)}, u32[]{:S(2)}) collective-permute-start(bf16[96,1024]{1,0:T(8,128)(2,1)S(1)} %collect.2.a_ref), channel_id=1, source_target_pairs={{0,8},{8,0},{16,24},{24,16},{1,9},{9,1},{17,25},{25,17},{2,10},{10... | collective-permute-start | bytes 589832 | tf_op jit(solution)/shard_map/ppermute | solution.py:796
  173.6 15.4 %collective-permute-start.31 = (bf16[96,1024]{1,0:T(8,128)(2,1)S(1)}, bf16[96,1024]{1,0:T(8,128)(2,1)S(1)}, u32[]{:S(2)}, u32[]{:S(2)}) collective-permute-start(bf16[96,1024]{1,0:T(8,128)(2,1)S(1)} %collect.2.a_ref), channel_id=1, source_target_pairs={{0,16},{8,24},{16,0},{24,8},{1,17},{9,25},{17,1},{25,9},{2,18},{10... | collective-permute-start | bytes 589832 | tf_op jit(solution)/shard_map/ppermute | solution.py:796
  174.6 14.3 %collective-permute-start.32 = (bf16[96,1024]{1,0:T(8,128)(2,1)S(1)}, bf16[96,1024]{1,0:T(8,128)(2,1)S(1)}, u32[]{:S(2)}, u32[]{:S(2)}) collective-permute-start(bf16[96,1024]{1,0:T(8,128)(2,1)S(1)} %collect.2.a_ref), channel_id=1, source_target_pairs={{0,24},{8,16},{16,8},{24,0},{1,25},{9,17},{17,9},{25,1},{2,26},{10... | collective-permute-start | bytes 589832 | tf_op jit(solution)/shard_map/ppermute | solution.py:796
  176.5 11.3 %collective-permute-start.37 = (bf16[64,1024]{1,0:T(8,128)(2,1)S(1)}, bf16[64,1024]{1,0:T(8,128)(2,1)S(1)}, u32[]{:S(2)}, u32[]{:S(2)}) collective-permute-start(bf16[64,1024]{1,0:T(8,128)(2,1)S(1)} %collect.3.a_ref), channel_id=1, source_target_pairs={{0,16},{8,24},{16,0},{24,8},{1,17},{9,25},{17,1},{25,9},{2,18},{10... | collective-permute-start | bytes 393224 | tf_op jit(solution)/shard_map/ppermute | solution.py:796
  177.6 10.3 %collective-permute-start.38 = (bf16[64,1024]{1,0:T(8,128)(2,1)S(1)}, bf16[64,1024]{1,0:T(8,128)(2,1)S(1)}, u32[]{:S(2)}, u32[]{:S(2)}) collective-permute-start(bf16[64,1024]{1,0:T(8,128)(2,1)S(1)} %collect.3.a_ref), channel_id=1, source_target_pairs={{0,24},{8,16},{16,8},{24,0},{1,25},{9,17},{17,9},{25,1},{2,26},{10... | collective-permute-start | bytes 393224 | tf_op jit(solution)/shard_map/ppermute | solution.py:796
  (43 other events, 122.7 us)

commit v5 on v4

--- a/solution.py
+++ b/solution.py
@@ -47,11 +47,14 @@
     return jnp.where(before < after, 1.0, 0.0).astype(BF16)
 
 
+def whole(array):
+    return pl.BlockSpec(array.shape, lambda step: (0,) * array.ndim)
+
+
 def render_kernel(
-    ray_count, me_ref, owner_ref, lists_ref, opacity_ref, counts_ref, pixels_ref, features_ref,
-    *refs,
+    ray_count, relative, me_ref, owner_ref, lists_ref, opacity_ref, counts_ref, pixels_ref,
+    features_ref, near_ref, other_ref, ids_ref, share_ref, table_ref, send_ref,
 ):
-    out_ref, ids_ref, share_ref, table_ref, send_ref = refs[-5:]
     depth, rays = lists_ref.shape
     gauss = features_ref.shape[0]
     width = features_ref.shape[1]
@@ -80,57 +83,72 @@
             total = total + jnp.where(ident == number, share, 0.0)
         table_ref[pl.ds(first, tile), pl.ds(lane, lanes)] = total.astype(BF16)
 
-    mine = pixels_ref[pl.ds(me, 1), :]
+    mine = pixels_ref[:, pl.ds(pl.multiple_of(me * rays, rays), rays)]
     owner = owner_of(mine, owner_ref, rays, ray_count)
     padded = -(-ray_count // 16) * 16
     member = (lax.broadcasted_iota(jnp.int32, (padded, rays), 0) == owner)
     ranks = dot_nn(member.astype(F32).astype(BF16), earlier(rays))
     rank = jnp.sum(jnp.where(member, ranks, 0.0), axis=0, keepdims=True).astype(jnp.int32)
-    slot = owner * (rays // ray_count) + rank
+    if relative:
+        chips = ray_count // 2
+        shift = lax.div(owner, jnp.int32(2)) - lax.div(me, jnp.int32(2))
+        shift = jnp.where(shift < 0, shift + chips, shift)
+        flip = jnp.where(lax.rem(owner, jnp.int32(2)) == lax.rem(me, jnp.int32(2)), 0, 1)
+        block = flip * chips + shift
+    else:
+        block = owner
+    slot = block * (rays // ray_count) + rank
     send_ref[...] = (
         (lax.broadcasted_iota(jnp.int32, (rays, rays), 0) == slot).astype(F32).astype(BF16)
     )
 
     piece = 256
+    half = rays // 2
 
     @pl.loop(0, width // piece)
     def _(step):
         cols = pl.ds(pl.multiple_of(step * piece, piece), piece)
         rendered = dot_tn(table_ref[...], features_ref[:, cols]).astype(BF16)
-        out_ref[:, cols] = dot_nn(send_ref[...], rendered).astype(BF16)
-
-
-def render(me, owner, lists, opacity, counts, pixels, features, after=()):
-    ray_count = pixels.shape[0]
+        ordered = dot_nn(send_ref[...], rendered).astype(BF16)
+        near_ref[:, :, cols] = ordered[:half].reshape(*near_ref.shape[:2], piece)
+        other_ref[:, :, cols] = ordered[half:].reshape(*other_ref.shape[:2], piece)
+
+
+def render(ray_count, relative, me, owner, lists, opacity, counts, pixels, features):
     depth, rays = lists.shape
     gauss, width = features.shape
-    return pl.pallas_call(
-        functools.partial(render_kernel, ray_count),
-        out_shape=jax.ShapeDtypeStruct((rays, width), BF16),
-        in_specs=[SMEM, SMEM, VMEM, VMEM, VMEM, VMEM, VMEM] + [ANY] * len(after),
-        out_specs=VMEM,
+    shape = jax.ShapeDtypeStruct((ray_count // 2, rays // ray_count, width), BF16)
+    operands = (lists, opacity, counts, pixels, features)
+    return pl.pallas_call(
+        functools.partial(render_kernel, ray_count, relative),
+        grid=(1,),
+        out_shape=(shape, shape),
+        in_specs=[SMEM, SMEM] + [whole(array) for array in operands],
+        out_specs=(VMEM, VMEM),
         scratch_shapes=[
             pltpu.VMEM((depth, rays), jnp.int32),
             pltpu.VMEM((depth, rays), F32),
             pltpu.VMEM((gauss, rays), BF16),
             pltpu.VMEM((rays, rays), BF16),
         ],
-        compiler_params=params(20),
+        compiler_params=params(24),
         cost_estimate=COST,
         name="render",
-    )(me, owner, lists, opacity, counts, pixels, features, *after)
+    )(me, owner, *operands)
 
 
 def tokens_kernel(
-    ray_count, me_ref, owner_ref, pixels_ref, tokens_ref, gain_ref,
-    tokens_out, normed_out, normed_t_out, place_ref,
+    ray_count, relative, me_ref, owner_ref, pixels_ref, tokens_ref, gain_ref,
+    tokens_out, normed_out, normed_t_out, order_ref, rank_ref, place_ref,
 ):
     rows, width = tokens_ref.shape
     me = me_ref[0]
     each = rows // ray_count
-    pixels = pixels_ref[...]
+    pixels = jnp.concatenate(
+        [pixels_ref[:, sender * rows:(sender + 1) * rows] for sender in range(ray_count)], axis=0
+    )
     mine = owner_of(pixels, owner_ref, rows, ray_count) == me
-    place = lax.rem(pixels, jnp.int32(rows)).astype(F32)
+    place_ref[...] = lax.rem(pixels, jnp.int32(rows)).astype(F32)
     member = jnp.where(mine, 1.0, 0.0)
     padded = -(-ray_count // 16) * 16
     if padded > ray_count:
@@ -138,19 +156,28 @@
     else:
         spread = member
     ranks = dot_nn(spread.astype(BF16), earlier(rows))
-    for sender in range(ray_count):
-        rank = jnp.where(mine[sender:sender + 1], ranks[sender:sender + 1], -1.0).astype(jnp.int32)
+    rank_ref[...] = jnp.where(mine, ranks[:ray_count], -1.0)
+    chips = ray_count // 2
+    for index in range(ray_count):
+        if relative:
+            chip = lax.rem(lax.div(me, jnp.int32(2)) + (chips - index // 2), jnp.int32(chips))
+            sender = 2 * chip + jnp.bitwise_xor(lax.rem(me, jnp.int32(2)), index % 2)
+        else:
+            sender = index
+        rank = rank_ref[pl.ds(sender, 1), :].astype(jnp.int32)
         hit = lax.broadcasted_iota(jnp.int32, (each, rows), 0) == rank
-        at = jnp.sum(jnp.where(hit, place[sender:sender + 1], 0.0), axis=1, keepdims=True)
+        at = jnp.sum(
+            jnp.where(hit, place_ref[pl.ds(sender, 1), :], 0.0), axis=1, keepdims=True
+        )
         here = lax.broadcasted_iota(jnp.int32, (each, rows), 1) == at.astype(jnp.int32)
-        place_ref[pl.ds(sender * each, each), :] = here.astype(F32).astype(BF16)
+        order_ref[pl.ds(index * each, each), :] = here.astype(F32).astype(BF16)
     half = min(128, rows)
     gain = gain_ref[...]
 
     @pl.loop(0, rows // half)
     def _(step):
         span = pl.ds(pl.multiple_of(step * half, half), half)
-        values = dot_nn(place_ref[span, :], tokens_ref[...])
+        values = dot_nn(order_ref[span, :], tokens_ref[...])
         tokens_out[span, :] = values.astype(BF16)
         centered = values - jnp.mean(values, axis=-1, keepdims=True)
         variance = jnp.mean(centered * centered, axis=-1, keepdims=True)
@@ -160,19 +187,23 @@
         normed_t_out[:, span] = normed.T
 
 
-def prepare_tokens(me, owner, pixels, tokens, gain):
-    ray_count = pixels.shape[0]
+def prepare_tokens(ray_count, relative, me, owner, pixels, tokens, gain):
     rows, width = tokens.shape
     return pl.pallas_call(
-        functools.partial(tokens_kernel, ray_count),
+        functools.partial(tokens_kernel, ray_count, relative),
+        grid=(1,),
         out_shape=(
             jax.ShapeDtypeStruct((rows, width), BF16),
             jax.ShapeDtypeStruct((rows, width), BF16),
             jax.ShapeDtypeStruct((width, rows), BF16),
         ),
-        in_specs=[SMEM, SMEM, VMEM, VMEM, VMEM],
+        in_specs=[SMEM, SMEM, whole(pixels), whole(tokens), whole(gain)],
         out_specs=(VMEM, VMEM, VMEM),
-        scratch_shapes=[pltpu.VMEM((rows, rows), BF16)],
+        scratch_shapes=[
+            pltpu.VMEM((rows, rows), BF16),
+            pltpu.VMEM((ray_count, rows), F32),
+            pltpu.VMEM((ray_count, rows), F32),
+        ],
         compiler_params=params(20),
         cost_estimate=COST,
         name="tokens",
@@ -395,14 +426,15 @@
     down_parts = group_count if down_weight.shape[0] % (16 * group_count) == 0 else 1
     up = gather_weight(up_weight, up_parts, group, group_count, ray_count)
     down = gather_weight(down_weight, down_parts, group, group_count, ray_count)
-    pixels = ray_pixel[0].reshape(ray_count, rows)
     rendered = render(
-        me, block_owner, tile_lists, opacity, tile_counts.reshape(1, rows), pixels,
-        gaussian_features,
-    )
+        ray_count, False, me, block_owner, tile_lists, opacity, tile_counts.reshape(1, rows),
+        ray_pixel, gaussian_features,
+    )
+    rendered = jnp.concatenate(rendered, axis=0).reshape(rows, width)
     target = lax.all_to_all(rendered, "ray", split_axis=0, concat_axis=0, tiled=True)
     tokens, normed, normed_t = prepare_tokens(
-        me, block_owner, pixels, image_tokens, layer_norm_gain.reshape(1, width)
+        ray_count, False, me, block_owner, ray_pixel, image_tokens,
+        layer_norm_gain.reshape(1, width),
     )
     act, slope = project_up(normed, up)
     grad_down, back, small = project_down(act, down, tokens, target, layer_scale.reshape(1, width))
@@ -428,7 +460,8 @@
     return pl.pallas_call(
         quarter_kernel,
         out_shape=jax.ShapeDtypeStruct((2, part, width), BF16),
-        in_specs=[SMEM, VMEM, VMEM],
+        grid=(1,),
+        in_specs=[SMEM, whole(up), whole(down)],
         out_specs=VMEM,
         scratch_shapes=[pltpu.VMEM((chunk, width), BF16)],
         compiler_params=params(16),
@@ -447,15 +480,17 @@
     return upstream, 1.0 - cosine
 
 
-def forward_kernel(first, last, sides, *refs):
+def forward_kernel(first, blocks, sides, *refs):
+    last = blocks > 0
     refs = list(refs)
     normed_t_ref = refs.pop(0)
     own, other = refs[:sides], refs[sides:2 * sides]
     del refs[:2 * sides]
     mixed_in = None if first else refs.pop(0)
     if last:
-        tokens_ref, target_ref, scale_ref = refs[:3]
-        del refs[:3]
+        tokens_ref, scale_ref = refs[:2]
+        targets = refs[2:2 + blocks]
+        del refs[:2 + blocks]
     act_ref, slope_ref = refs[:2]
     del refs[:2]
     width, rows = normed_t_ref.shape
@@ -486,14 +521,13 @@
     mixed_ref[...] = mixed_in[...] + dot_tn(act, down)
     scale = scale_ref[...]
     small_ref[...] = jnp.zeros_like(small_ref)
-    piece = 128
-
-    @pl.loop(0, rows // piece)
-    def _(index):
-        span = pl.ds(pl.multiple_of(index * piece, piece), piece)
+    piece = rows // blocks
+    for index, target_ref in enumerate(targets):
+        span = pl.ds(index * piece, piece)
         mixed = mixed_ref[span, :]
         upstream, loss = finish_rows(
-            tokens_ref[span, :].astype(F32), mixed, target_ref[span, :].astype(F32), scale
+            tokens_ref[span, :].astype(F32), mixed,
+            target_ref[...].reshape(piece, width).astype(F32), scale,
         )
         back = (upstream * scale).astype(BF16)
         back_ref[span, :] = back
@@ -507,6 +541,7 @@
     part = own[0].shape[2]
     total = sum(array.shape[0] for array in own)
     first, last = mixed is None, finish is not None
+    blocks = len(finish) - 2 if last else 0
     operands = [normed_t, *own, *other]
     if not first:
         operands.append(mixed)
@@ -525,7 +560,7 @@
     else:
         shapes += [jax.ShapeDtypeStruct((rows, width), F32)]
     return pl.pallas_call(
-        functools.partial(forward_kernel, first, last, len(own)),
+        functools.partial(forward_kernel, first, blocks, len(own)),
         out_shape=tuple(shapes),
         in_specs=[VMEM] * len(operands),
         out_specs=tuple([VMEM] * len(shapes)),
@@ -563,7 +598,7 @@
     )(mine, x, y, *arrivals, after)
 
 
-def turn_kernel(y_ref, y_far_ref, x_far_ref, a_ref, b_ref):
+def turn_kernel(y_ref, y_far_ref, x_far_ref, after_ref, a_ref, b_ref):
     held = a_ref.shape[0] - 1
     a_ref[0] = y_ref[...]
     for index in range(held):
@@ -572,7 +607,7 @@
         b_ref[index] = x_far_ref[held + index]
 
 
-def turn(y, y_far, x_far):
+def turn(y, y_far, x_far, after):
     count = y_far.shape[0]
     first = (count + 1) // 2
     return pl.pallas_call(
@@ -581,124 +616,190 @@
             jax.ShapeDtypeStruct((first, *y.shape), BF16),
             jax.ShapeDtypeStruct((count + 1 - first, *y.shape), BF16),
         ),
-        in_specs=[VMEM] * 3,
+        in_specs=[VMEM] * 3 + [ANY],
         out_specs=(VMEM, VMEM),
         compiler_params=params(16),
         cost_estimate=COST,
         name="turn",
-    )(y, y_far, x_far)
+    )(y, y_far, x_far, after)
 
 
 def tie_kernel(*refs):
     pass
 
 
-def tie(array, after):
+def tie(array, *after):
     return pl.pallas_call(
         tie_kernel,
         out_shape=jax.ShapeDtypeStruct(array.shape, array.dtype),
-        in_specs=[ANY, ANY],
+        in_specs=[ANY] * (1 + len(after)),
         out_specs=ANY,
         input_output_aliases={0: 0},
         compiler_params=params(4),
         cost_estimate=COST,
         name="tie",
-    )(array, after)
-
-
-def backward_kernel(side, places, add, count, *refs):
-    refs = list(refs)
-    back_ref, back_t_ref, normed_ref, gain_in = refs[:4]
-    del refs[:4]
-    weights, acts, slopes = refs[:count], refs[count:2 * count], refs[2 * count:3 * count]
-    del refs[:3 * count]
-    arrived = refs.pop(0) if add else None
-    up_ref, down_ref, gain_ref = refs
-    rows, width = back_ref.shape
-
-    def joined(values):
-        flat = [value.reshape(-1, value.shape[-1]) for value in values]
-        return flat[0] if count == 1 else jnp.concatenate(flat, axis=0)
-
-    def rows_of(which):
-        return joined([
-            ref[w:w + n, which] for ref, (w, a, n) in zip(weights, places)
-        ])
-
-    slope = joined([ref[side, a:a + n] for ref, (w, a, n) in zip(slopes, places)])
-    act = joined([ref[side, a:a + n] for ref, (w, a, n) in zip(acts, places)])
-    chunk = act.shape[0]
-    back_act = dot_nn(rows_of(1), back_t_ref[...])
-    back_hidden = (back_act * slope).astype(BF16)
-    grad_up = dot_nn(back_hidden, normed_ref[...])
-    up = rows_of(0).astype(F32)
-    gain_ref[...] = gain_in[...] + jnp.sum(grad_up * up, axis=0, keepdims=True)
-    grad_down = dot_nn(act, back_ref[...])
-    if add:
-        grad_up += arrived[0].reshape(chunk, width).astype(F32)
-        grad_down += arrived[1].reshape(chunk, width).astype(F32)
-    up_ref[...] = grad_up.astype(BF16).reshape(up_ref.shape)
-    down_ref[...] = grad_down.astype(BF16).reshape(down_ref.shape)
-
-
-def backward(side, common, gain, pieces, arrived):
-    rows, width = common[0].shape
-    part = pieces[0][0].shape[2]
-    places = tuple((piece[1], piece[4], piece[5]) for piece in pieces)
-    count = sum(piece[5] for piece in pieces)
-    operands = [*common, gain]
-    for which in (0, 2, 3):
-        operands += [piece[which] for piece in pieces]
-    body = functools.partial(backward_kernel, side, places, arrived is not None, len(pieces))
+    )(array, *after)
+
+
+def mix_kernel(*refs):
+    near_ref, other_ref, outs = refs[0], refs[1], refs[2:]
+    for index, ref in enumerate(outs):
+        ref[0] = near_ref[index]
+        ref[1] = other_ref[index]
+
+
+def mix(near, other):
+    count, each, width = near.shape
+    return pl.pallas_call(
+        mix_kernel,
+        out_shape=tuple([jax.ShapeDtypeStruct((2, each, width), BF16)] * count),
+        in_specs=[VMEM, VMEM],
+        out_specs=tuple([VMEM] * count),
+        compiler_params=params(16),
+        cost_estimate=COST,
+        name="mix",
+    )(near, other)
+
+
+def joined(refs, pieces, pick):
+    values = [pick(refs[which], start, count) for which, start, count in pieces]
+    flat = [value.reshape(-1, value.shape[-1]) for value in values]
+    return jnp.concatenate(flat, axis=0)
+
+
+def put(quarter, value, outs):
+    own_ref, x_ref, y_ref, x_later_ref, y_later_ref = outs
+    value = value.astype(BF16).reshape(own_ref.shape)
+    half = x_ref.shape[0] // 2
+    if quarter == 0:
+        own_ref[...] = value
+    elif quarter == 1:
+        x_ref[half:] = value[:half]
+        x_later_ref[...] = value[half:]
+    elif quarter == 2:
+        y_ref[half:] = value[half:]
+        y_later_ref[...] = value[:half]
+    else:
+        x_ref[:half] = value[:half]
+        y_ref[:half] = value[half:]
+
+
+def emit(quarter, value, arrived, outs):
     if arrived is None:
-        def run(*refs):
-            grads, gain_ref = refs[-2:]
-            body(*refs[:-2], grads.at[0], grads.at[1], gain_ref)
-
-        shapes = [jax.ShapeDtypeStruct((2, count, part, width), BF16)]
+        outs[0][quarter] = value.astype(BF16).reshape(outs[0].shape[1:])
     else:
-        operands.append(arrived)
-        run = body
-        shapes = [jax.ShapeDtypeStruct((count, part, width), BF16)] * 2
-    shapes.append(jax.ShapeDtypeStruct((1, width), F32))
-    return pl.pallas_call(
-        run,
+        put(quarter, value + arrived[quarter].reshape(value.shape).astype(F32), outs)
+
+
+def down_grad_kernel(side, act_pieces, add, *refs):
+    count = 3
+    acts, back_ref = refs[:count], refs[count]
+    arrived = refs[count + 1] if add else None
+    outs = refs[count + 2:] if add else refs[count + 1:]
+    for quarter in (3, 1, 2, 0):
+        act = joined(acts, act_pieces[quarter], lambda ref, a, n: ref[side, a:a + n])
+        emit(quarter, dot_nn(act, back_ref[...]), arrived, outs)
+
+
+def up_grad_kernel(side, weight_pieces, act_pieces, add, *refs):
+    weights, slopes = refs[:5], refs[5:8]
+    back_t_ref, normed_ref, gain_in = refs[8:11]
+    arrived = refs[11] if add else None
+    outs, gain_ref = refs[12 if add else 11:-1], refs[-1]
+    gain_ref[...] = gain_in[...]
+    for quarter in (3, 1, 2, 0):
+        pieces = weight_pieces[quarter]
+        slope = joined(slopes, act_pieces[quarter], lambda ref, a, n: ref[side, a:a + n])
+        back_act = dot_nn(joined(weights, pieces, lambda ref, a, n: ref[a:a + n, 1]), back_t_ref[...])
+        back_hidden = (back_act * slope).astype(BF16)
+        grad = dot_nn(back_hidden, normed_ref[...])
+        up = joined(weights, pieces, lambda ref, a, n: ref[a:a + n, 0]).astype(F32)
+        gain_ref[...] += jnp.sum(grad * up, axis=0, keepdims=True)
+        emit(quarter, grad, arrived, outs)
+
+
+def gradient_shapes(depth, part, width, add):
+    if not add:
+        return [jax.ShapeDtypeStruct((4, depth, part, width), BF16)]
+    counts = (depth, depth, depth, depth - depth // 2, depth // 2)
+    return [jax.ShapeDtypeStruct((count, part, width), BF16) for count in counts]
+
+
+def down_gradient(side, act_pieces, depth, acts, back, arrived=None):
+    part = acts[0].shape[2]
+    width = back.shape[1]
+    add = arrived is not None
+    operands = [*acts, back] + ([arrived] if add else [])
+    shapes = gradient_shapes(depth, part, width, add)
+    return pl.pallas_call(
+        functools.partial(down_grad_kernel, side, act_pieces, add),
         out_shape=tuple(shapes),
         in_specs=[VMEM] * len(operands),
         out_specs=tuple([VMEM] * len(shapes)),
         compiler_params=params(20),
         cost_estimate=COST,
-        name="backward",
+        name="down_gradient",
     )(*operands)
 
 
-def total_kernel(count, *refs):
-    ins, outs = refs[:4], refs[-count:]
-    for index, out in enumerate(outs):
-        total = ins[0][index].astype(F32)
-        for ref in ins[1:]:
-            total = total + ref[index].astype(F32)
-        out[...] = total.astype(BF16)
-    if len(refs) > 4 + count:
-        refs[5][...] = refs[4][...]
-
-
-def totals(parts, vector=None):
-    count, part, width = parts[0].shape
-    operands, shapes = list(parts), []
-    if vector is not None:
-        operands.append(vector)
-        shapes.append(jax.ShapeDtypeStruct(vector.shape, F32))
-    shapes += [jax.ShapeDtypeStruct((part, width), BF16)] * count
-    return pl.pallas_call(
-        functools.partial(total_kernel, count),
+def up_gradient(
+    side, weight_pieces, act_pieces, depth, weights, slopes, back_t, normed, gain, arrived=None
+):
+    part, width = weights[0].shape[2:]
+    add = arrived is not None
+    operands = [*weights, *slopes, back_t, normed, gain] + ([arrived] if add else [])
+    shapes = gradient_shapes(depth, part, width, add) + [jax.ShapeDtypeStruct((1, width), F32)]
+    return pl.pallas_call(
+        functools.partial(up_grad_kernel, side, weight_pieces, act_pieces, add),
         out_shape=tuple(shapes),
         in_specs=[VMEM] * len(operands),
         out_specs=tuple([VMEM] * len(shapes)),
+        compiler_params=params(24),
+        cost_estimate=COST,
+        name="up_gradient",
+    )(*operands)
+
+
+def merge_kernel(x_ref, y_ref, x_later_ref, y_later_ref, x_out, y_out):
+    half = y_later_ref.shape[0]
+    x_out[...] = (x_later_ref[...].astype(F32) + y_ref[:half].astype(F32)).astype(BF16)
+    y_out[...] = (y_later_ref[...].astype(F32) + x_ref[:half].astype(F32)).astype(BF16)
+
+
+def merge(x, y, x_later, y_later):
+    return pl.pallas_call(
+        merge_kernel,
+        out_shape=tuple(jax.ShapeDtypeStruct(a.shape, BF16) for a in (x_later, y_later)),
+        in_specs=[VMEM] * 4,
+        out_specs=(VMEM, VMEM),
         compiler_params=params(16),
         cost_estimate=COST,
+        name="merge",
+    )(x, y, x_later, y_later)
+
+
+def total_kernel(own_ref, x_ref, y_ref, x_late_ref, y_late_ref, *outs):
+    half = y_late_ref.shape[0]
+    for index, out in enumerate(outs):
+        total = own_ref[index].astype(F32)
+        if index < half:
+            total += x_ref[half + index].astype(F32) + y_late_ref[index].astype(F32)
+        else:
+            total += y_ref[index].astype(F32) + x_late_ref[index - half].astype(F32)
+        out[...] = total.astype(BF16)
+
+
+def totals(own, x, y, x_late, y_late):
+    count, part, width = own.shape
+    return pl.pallas_call(
+        total_kernel,
+        out_shape=tuple([jax.ShapeDtypeStruct((part, width), BF16)] * count),
+        in_specs=[VMEM] * 5,
+        out_specs=tuple([VMEM] * count),
+        compiler_params=params(16),
+        cost_estimate=COST,
         name="totals",
-    )(*operands)
+    )(own, x, y, x_late, y_late)
 
 
 def collect_kernel(count, *refs):
@@ -806,82 +907,82 @@
     arrivals = [along(mine, -shift) for shift in range(1, depth)]
     x, y = beside(mine, 1), beside(mine, 2)
 
-    pixels = ray_pixel[0].reshape(ray_count, rows)
-    rendered = render(
-        me, block_owner, tile_lists, opacity, tile_counts.reshape(1, rows), pixels,
-        gaussian_features,
+    rendered, rendered_other = render(
+        ray_count, True, me, block_owner, tile_lists, opacity, tile_counts.reshape(1, rows),
+        ray_pixel, gaussian_features,
     )
     first, far = pack(mine, x, y, arrivals, rendered)
     x_far, y_far = beside(far, 1), beside(far, 2)
+    blocks = mix(rendered, partner(rendered_other))
+    targets = [blocks[0]] + [along(blocks[shift], shift) for shift in range(1, depth)]
     first_other = partner(first)
     tokens, normed, normed_t = prepare_tokens(
-        me, block_owner, pixels, image_tokens, layer_norm_gain.reshape(1, width)
-    )
-    rendered = tie(rendered, normed)
-    target = lax.all_to_all(rendered, "ray", split_axis=0, concat_axis=0, tiled=True)
-    passed_x, passed_y = turn(y, y_far, x_far)
+        ray_count, True, me, block_owner, ray_pixel, image_tokens,
+        layer_norm_gain.reshape(1, width),
+    )
+    act_first, slope_first, mixed = forward(normed_t, [first], [first_other])
+    passed_x, passed_y = turn(y, y_far, x_far, mixed)
     d_low, d_high = beside(passed_x, 1), beside(passed_y, 2)
-    act_first, slope_first, mixed = forward(normed_t, [first], [first_other])
-    x_far, y_far = tie(x_far, mixed), tie(y_far, mixed)
     x_other, y_other = partner(x_far), partner(y_far)
     act_next, slope_next, mixed = forward(normed_t, [x_far, y_far], [x_other, y_other], mixed)
-    d_low, d_high = tie(d_low, mixed), tie(d_high, mixed)
+    d_low, d_high = tie(d_low, mixed, *targets[1:]), tie(d_high, mixed, *targets[1:])
     low_other, high_other = partner(d_low), partner(d_high)
     act_last, slope_last, back, back_t, small = forward(
         normed_t, [d_low, d_high], [low_other, high_other], mixed,
-        (tokens, target, layer_scale.reshape(1, width)),
-    )
-    common = (back, back_t, normed)
-    held = {
-        0: (first, x_far, y_far, d_low, d_high),
-        1: (first_other, x_other, y_other, low_other, high_other),
-    }
+        (tokens, layer_scale.reshape(1, width), *targets),
+    )
+    acts = (act_first, act_next, act_last)
+    slopes = (slope_first, slope_next, slope_last)
+    weights = (
+        (first, x_far, y_far, d_low, d_high),
+        (first_other, x_other, y_other, low_other, high_other),
+    )
     low = d_low.shape[0]
-
-    def grads(side, quarter, gain, arrived):
-        firsts, xs, ys, lows, highs = held[side]
-        start = (firsts, quarter, act_first, slope_first, quarter, 1)
-        pieces = {
-            0: [start, (firsts, 3, act_first, slope_first, 3, depth - 1)],
-            1: [start, (xs, 0, act_next, slope_next, 0, depth - 1)],
-            2: [start, (ys, 0, act_next, slope_next, depth - 1, depth - 1)],
-            3: [
-                (lows, 0, act_last, slope_last, 0, low),
-                (highs, 0, act_last, slope_last, low, depth - low),
-            ],
-        }[quarter]
-        return backward(side, common, gain, pieces, arrived)
-
+    act_pieces = (
+        ((0, 0, 1), (0, 3, depth - 1)),
+        ((0, 1, 1), (1, 0, depth - 1)),
+        ((0, 2, 1), (1, depth - 1, depth - 1)),
+        ((2, 0, depth),),
+    )
+    weight_pieces = (
+        ((0, 0, 1), (0, 3, depth - 1)),
+        ((0, 1, 1), (1, 0, depth - 1)),
+        ((0, 2, 1), (2, 0, depth - 1)),
+        ((3, 0, low), (4, 0, depth - low)),
+    )
     gain = jnp.zeros((1, width), F32)
-    arrived, sums, sent = {}, {}, {}
-    for side, quarter in ((1, 3), (1, 1), (0, 3), (1, 2), (0, 1), (1, 0), (0, 2), (0, 0)):
-        if side == 1:
-            out, gain = grads(1, quarter, gain, None)
-            arrived[quarter] = partner(out)
-        else:
-            grad_up, grad_down, gain = grads(0, quarter, gain, arrived[quarter])
-            sums[quarter] = (grad_up, grad_down)
-            if quarter:
-                sent[quarter] = (beside(grad_up, quarter), beside(grad_down, quarter))
-    vector = jnp.concatenate(
-        [gain / layer_norm_gain.reshape(1, width), small[:2], jnp.zeros((5, width), F32)], axis=0
-    )
-    vector, *shares = totals([sums[0][1]] + [sent[quarter][1] for quarter in (1, 2, 3)], vector)
+    (down_other,) = down_gradient(1, act_pieces, depth, acts, back)
+    down_arrived = partner(down_other)
+    up_other, gain = up_gradient(
+        1, weight_pieces, act_pieces, depth, weights[1], slopes, back_t, normed, gain
+    )
+    up_arrived = partner(up_other)
+    down_sums = down_gradient(0, act_pieces, depth, acts, back, down_arrived)
+    *up_sums, gain = up_gradient(
+        0, weight_pieces, act_pieces, depth, weights[0], slopes, back_t, normed, gain, up_arrived
+    )
+
+    def sum_beside(own, to_x, to_y, x_later, y_later):
+        from_x, from_y = beside(to_x, 1), beside(to_y, 2)
+        x_later, y_later = merge(from_x, from_y, x_later, y_later)
+        return totals(own, from_x, from_y, beside(x_later, 1), beside(y_later, 2))
 
     def sum_along(shares, *vector):
         arrivals = [along(shares[shift], shift) for shift in range(1, depth)]
         total = collect([shares[0]] + arrivals, *vector)
         return [total] + [beside(total, flip) for flip in (1, 2, 3)]
 
-    quarters = sum_along(shares)
-    (grad_down,) = place_quarters(group, quarters, part, False)
+    vector = jnp.concatenate(
+        [gain / layer_norm_gain.reshape(1, width), small[:2], jnp.zeros((5, width), F32)], axis=0
+    )
     vector = vector + partner(vector)
     flip = 2
     while flip < ray_count:
         vector = vector + partner(vector, flip)
         flip *= 2
-    shares = totals([sums[0][0]] + [sent[quarter][0] for quarter in (1, 2, 3)])
-    quarters = sum_along(shares, vector)
+    quarters = sum_along(sum_beside(*down_sums))
+    (grad_down,) = place_quarters(group, quarters, part, False)
+    quarters = sum_along(sum_beside(*up_sums), vector)
     grad_up, vector = place_quarters(group, quarters, part, True)
     loss = vector[2, 0] / (rows * ray_count * group_count)
     return (grad_up, grad_down, vector[0], vector[1], loss)

time: 197 us -> 183 us (0.929)
  Pallas kernels: 51.1 us -> 35 us
  waiting for transfers between devices: 74.1 us -> 88.5 us
  local copies, waits for them, and re-layouts: 20.7 us -> 8.62 us
    ppermute x9 -> x12, waiting for transfers between devices: 0.73 us -> 26.6 us  [along(): return lax.ppermute(array, 'ray', pairs)]
    pallas_call x15 -> x14, Pallas kernels: 45.2 us -> 31.9 us  [the longest x1 11.8 us: render(): pl.pallas_call(functools.partial(render_kernel, ray_count, relative), gri...]
    unnamed x71 -> x26, local copies, waits for them, and re-layouts: 19.4 us -> 7.42 us
    ppermute x18 -> x20, waiting for transfers between devices: 62 us -> 53.6 us  [beside(): lax.ppermute(array, 'grp', [(g, g ^ flip) for g in range(group_count)])]
    all_to_all x1 -> x0, starting transfers between devices: 5.31 us -> none  [shards_square(): lax.all_to_all(rendered, 'ray', split_axis=0, concat_axis=0, tiled=True)]
    ppermute x9 -> x12, starting transfers between devices: 14.3 us -> 18 us  [along(): return lax.ppermute(array, 'ray', pairs)]
    ppermute x12 -> x11, waiting for transfers between devices: 11.3 us -> 8.25 us  [partner(): return lax.ppermute(array, 'ray', [(r, r ^ flip) for r in range(ray_count)])]
    ppermute x12 -> x11, starting transfers between devices: 4.98 us -> 6.66 us  [partner(): return lax.ppermute(array, 'ray', [(r, r ^ flip) for r in range(ray_count)])]
  transfers between devices with their start and end apart: 40 -> 43, of which waited for: 17 -> 22; matrix products, arithmetic and copies ran while one was open for 1% -> 0% of each run, Pallas kernels for 21% -> 16%
where the time goes in v5:
time: 183 us; the launch traced here: 179 us
  waiting for transfers between devices  88.5 us (48%)
  starting transfers between devices  44.4 us (24%)
  Pallas kernels  35 us (19%)
  local copies, waits for them, and re-layouts  8.62 us (5%)
  between operations  2.7 us (1%)
    ppermute x20, waiting for transfers between devices, beside(): lax.ppermute(array, 'grp', [(g, g ^ flip) for g in range(group_count)])  53.6 us
    ppermute x12, waiting for transfers between devices, along(): return lax.ppermute(array, 'ray', pairs)  26.6 us
    ppermute x20, starting transfers between devices, beside(): lax.ppermute(array, 'grp', [(g, g ^ flip) for g in range(group_count)])  19.7 us
    ppermute x12, starting transfers between devices, along(): return lax.ppermute(array, 'ray', pairs)  18 us
    pallas_call x1, Pallas kernels, render(): pl.pallas_call(functools.partial(render_kernel, ray_count, relative), gri...  11.8 us
    ppermute x11, waiting for transfers between devices, partner(): return lax.ppermute(array, 'ray', [(r, r ^ flip) for r in range(ray_count)])  8.25 us
    pallas_call x3, Pallas kernels, forward(): pl.pallas_call(functools.partial(forward_kernel, first, blocks, len(own))...  7.81 us
    unnamed x26, local copies, waits for them, and re-layouts  7.42 us
  transfers between devices with their start and end apart: 43, of which 22 were waited for; matrix products, arithmetic and copies ran while one was open for 0% of the time, Pallas kernels for 16%

profile of v5, /device:TPU:8, one launch (start us, length us, event | category | flops | bytes accessed | tf_op | source)
XLA Modules:
  0.0 179.4 jit_solution(8099770975757595278)
XLA Ops:
  2.9 1.6 collective-permute-start.1
  6.5 2.6 %collective-permute-start.3 = (bf16[2,64,1024]{2,1,0:T(8,128)(2,1)S(1)}, bf16[2,64,1024]{2,1,0:T(8,128)(2,1)S(1)}, u32[]{:S(2)}, u32[]{:S(2)}) collective-permute-start(bf16[2,64,1024]{2,1,0:T(8,128)(2,1)S(1)} %quarter.1.mine_ref), channel_id=1, source_target_pairs={{0,4},{1,5},{2,6},{3,7},{4,0},{5,1},{6,2},{7,3},{8,12},{9,13},{10,... | collective-permute-start | bytes 786440 | tf_op jit(solution)/shard_map/ppermute | solution.py:904
  9.1 2.5 %collective-permute-start.4 = (bf16[2,64,1024]{2,1,0:T(8,128)(2,1)S(1)}, bf16[2,64,1024]{2,1,0:T(8,128)(2,1)S(1)}, u32[]{:S(2)}, u32[]{:S(2)}) collective-permute-start(bf16[2,64,1024]{2,1,0:T(8,128)(2,1)S(1)} %quarter.1.mine_ref), channel_id=1, source_target_pairs={{0,2},{1,3},{2,4},{3,5},{4,6},{5,7},{6,0},{7,1},{8,10},{9,11},{10,... | collective-permute-start | bytes 786440 | tf_op jit(solution)/shard_map/ppermute | solution.py:904
  11.5 1.6 copy-done
  16.9 11.8 %render.1 = (bf16[4,64,1024]{2,1,0:T(8,128)(2,1)S(1)}, bf16[4,64,1024]{2,1,0:T(8,128)(2,1)S(1)}) custom-call(s32[1]{0:T(128)} %bitcast.1.me_ref, s32[1,8]{1,0:T(1,128)S(1)} %copy-done.10, s32[32,512]{1,0:T(8,128)S(1)} %copy-done.6, f32[32,512]{1,0:T(8,128)S(1)} %copy-done.7, s32[1,512]{1,0:T(1,128)S(1)} %bitcast.11, s32[1,4096]{1,0:T(1,128)S(1)} %copy-done.4, ...), custom_call_target="tpu_custom_call" | custom-call | flops 1048576 | bytes 65536 | tf_op jit(solution)/shard_map/render/pallas_call | solution.py:122
  28.7 1.9 %collective-permute-done.4.refs_2_ = bf16[2,64,1024]{2,1,0:T(8,128)(2,1)S(1)} collective-permute-done((bf16[2,64,1024]{2,1,0:T(8,128)(2,1)S(1)}, bf16[2,64,1024]{2,1,0:T(8,128)(2,1)S(1)}, u32[]{:S(2)}, u32[]{:S(2)}) %collective-permute-start.4) | collective-permute-done | bytes 262176 | tf_op jit(solution)/shard_map/ppermute | solution.py:904
  32.0 18.9 %collective-permute-done.6.y_far_ref.refs_2_ = bf16[3,2,64,1024]{3,2,1,0:T(8,128)(2,1)S(1)} collective-permute-done((bf16[3,2,64,1024]{3,2,1,0:T(8,128)(2,1)S(1)}, bf16[3,2,64,1024]{3,2,1,0:T(8,128)(2,1)S(1)}, u32[]{:S(2)}, u32[]{:S(2)}) %collective-permute-start.6) | collective-permute-done | bytes 786464 | tf_op jit(solution)/shard_map/ppermute | solution.py:897
  51.6 3.4 %tokens.1 = (bf16[512,1024]{1,0:T(8,128)(2,1)S(1)}, bf16[512,1024]{1,0:T(8,128)(2,1)S(1)}, bf16[1024,512]{1,0:T(8,128)(2,1)S(1)}) custom-call(s32[1]{0:T(128)} %bitcast.1.me_ref, s32[1,8]{1,0:T(1,128)S(1)} %copy-done.11, s32[1,4096]{1,0:T(1,128)S(1)} %copy-done.5, bf16[512,1024]{1,0:T(8,128)(2,1)S(1)} %copy-done.1, f32[1,1024]{1,0:T(1,128)S(1)} %bitcast.8), custom_call_target="tpu_custom_call" | custom-call | flops 1048576 | bytes 65536 | tf_op jit(solution)/shard_map/tokens/pallas_call | solution.py:192
  55.1 2.3 %forward.3 = (bf16[2,6,64,512]{3,2,1,0:T(8,128)(2,1)S(1)}, f32[2,6,64,512]{3,2,1,0:T(8,128)S(1)}, f32[512,1024]{1,0:T(8,128)S(1)}) custom-call(bf16[1024,512]{1,0:T(8,128)(2,1)S(1)} %get-tuple-element.59.refs_0_, bf16[6,2,64,1024]{3,2,1,0:T(8,128)(2,1)S(1)} %get-tuple-element.57.refs_1_.refs_0_, ...), custom_call_target="tpu_custom_call" | custom-call | flops 1048576 | bytes 65536 | tf_op jit(solution)/shard_map/forward/pallas_call | solution.py:562
  57.5 1.6 collective-permute-start.15
  59.7 2.5 %collective-permute-start.12 = (bf16[2,64,1024]{2,1,0:T(8,128)(2,1)S(1)}, bf16[2,64,1024]{2,1,0:T(8,128)(2,1)S(1)}, u32[]{:S(2)}, u32[]{:S(2)}) collective-permute-start(bf16[2,64,1024]{2,1,0:T(8,128)(2,1)S(1)} %get-tuple-element.64), channel_id=1, source_target_pairs={{0,2},{1,3},{2,4},{3,5},{4,6},{5,7},{6,0},{7,1},{8,10},{9,11},{10,... | collective-permute-start | bytes 786440 | tf_op jit(solution)/shard_map/ppermute | solution.py:904
  63.8 2.4 %forward.4 = (bf16[2,6,64,512]{3,2,1,0:T(8,128)(2,1)S(1)}, f32[2,6,64,512]{3,2,1,0:T(8,128)S(1)}, f32[512,1024]{1,0:T(8,128)S(1)}) custom-call(bf16[1024,512]{1,0:T(8,128)(2,1)S(1)} %get-tuple-element.59.refs_0_, bf16[3,2,64,1024]{3,2,1,0:T(8,128)(2,1)S(1)} %collective-permute-done.5.x_far_ref.refs_1_, ...), custom_call_target="tpu_custom_call" | custom-call | flops 1048576 | bytes 65536 | tf_op jit(solution)/shard_map/forward/pallas_call | solution.py:562
  66.2 14.0 %collective-permute-done.12.refs_2_.refs_9_ = bf16[2,64,1024]{2,1,0:T(8,128)(2,1)S(1)} collective-permute-done((bf16[2,64,1024]{2,1,0:T(8,128)(2,1)S(1)}, bf16[2,64,1024]{2,1,0:T(8,128)(2,1)S(1)}, u32[]{:S(2)}, u32[]{:S(2)}) %collective-permute-start.12) | collective-permute-done | bytes 262176 | tf_op jit(solution)/shard_map/ppermute | solution.py:904
  80.2 4.0 %collective-permute-done.13.refs_3_.refs_10_ = bf16[2,64,1024]{2,1,0:T(8,128)(2,1)S(1)} collective-permute-done((bf16[2,64,1024]{2,1,0:T(8,128)(2,1)S(1)}, bf16[2,64,1024]{2,1,0:T(8,128)(2,1)S(1)}, u32[]{:S(2)}, u32[]{:S(2)}) %collective-permute-start.13) | collective-permute-done | bytes 262176 | tf_op jit(solution)/shard_map/ppermute | solution.py:904
  88.2 3.1 %forward.5 = (bf16[2,4,64,512]{3,2,1,0:T(8,128)(2,1)S(1)}, f32[2,4,64,512]{3,2,1,0:T(8,128)S(1)}, bf16[512,1024]{1,0:T(8,128)(2,1)S(1)}, bf16[1024,512]{1,0:T(8,128)(2,1)S(1)}, f32[8,1024]{1,0:T(8,128)S(1)}) custom-call(bf16[1024,512]{1,0:T(8,128)(2,1)S(1)} %get-tuple-element.59.refs_0_, bf16[2,2,64,1024]{3,2,1,0:T(8,128)(2,1)S(1)} %tie.2.refs_1_.refs_3_, ...), custom_call_target="tpu_custom_call" | custom-call | flops 1048576 | bytes 65536 | tf_op jit(solution)/shard_map/forward/pallas_call | solution.py:562
  92.7 2.7 %up_gradient.2 = (bf16[4,4,64,1024]{3,2,1,0:T(8,128)(2,1)S(1)}, f32[1,1024]{1,0:T(1,128)S(1)}) custom-call(bf16[6,2,64,1024]{3,2,1,0:T(8,128)(2,1)S(1)} %collective-permute-done.7.refs_2_.refs_0_, bf16[3,2,64,1024]{3,2,1,0:T(8,128)(2,1)S(1)} %collective-permute-done.9.refs_3_.refs_1_, bf16[3,2,64,1024]{3,2,1,0:T(8,128)(2,1)S(1)} %collective-permute-done.10.refs_4_.refs_2_, ...), custom_call_target="tpu_custom_call" | custom-call | flops 1048576 | bytes 65536 | tf_op jit(solution)/shard_map/up_gradient/pallas_call | solution.py:752
  98.0 1.6 collective-permute-start.33
  100.3 3.0 %up_gradient.3 = (bf16[4,64,1024]{2,1,0:T(8,128)(2,1)S(1)}, bf16[4,64,1024]{2,1,0:T(8,128)(2,1)S(1)}, bf16[4,64,1024]{2,1,0:T(8,128)(2,1)S(1)}, bf16[2,64,1024]{...) custom-call(bf16[6,2,64,1024]{3,2,1,0:T(8,128)(2,1)S(1)} %get-tuple-element.57.refs_1_.refs_0_, ...), custom_call_target="tpu_custom_call" | custom-call | flops 1048576 | bytes 65536 | tf_op jit(solution)/shard_map/up_gradient/pallas_call | solution.py:752
  105.1 7.7 %collective-permute-done.33.x_ref = bf16[4,64,1024]{2,1,0:T(8,128)(2,1)S(1)} collective-permute-done((bf16[4,64,1024]{2,1,0:T(8,128)(2,1)S(1)}, bf16[4,64,1024]{2,1,0:T(8,128)(2,1)S(1)}, u32[]{:S(2)}, u32[]{:S(2)}) %collective-permute-start.33) | collective-permute-done | bytes 524320 | tf_op jit(solution)/shard_map/ppermute | solution.py:897
  112.8 1.5 collective-permute-done.34.y_ref
  115.8 8.2 %collective-permute-done.19.x_ref = bf16[4,64,1024]{2,1,0:T(8,128)(2,1)S(1)} collective-permute-done((bf16[4,64,1024]{2,1,0:T(8,128)(2,1)S(1)}, bf16[4,64,1024]{2,1,0:T(8,128)(2,1)S(1)}, u32[]{:S(2)}, u32[]{:S(2)}) %collective-permute-start.19) | collective-permute-done | bytes 524320 | tf_op jit(solution)/shard_map/ppermute | solution.py:897
  124.1 1.5 collective-permute-done.20.y_ref
  127.2 2.5 %collective-permute-done.35.x_late_ref = bf16[2,64,1024]{2,1,0:T(8,128)(2,1)S(1)} collective-permute-done((bf16[2,64,1024]{2,1,0:T(8,128)(2,1)S(1)}, bf16[2,64,1024]{2,1,0:T(8,128)(2,1)S(1)}, u32[]{:S(2)}, u32[]{:S(2)}) %collective-permute-start.35) | collective-permute-done | bytes 262176 | tf_op jit(solution)/shard_map/ppermute | solution.py:897
  129.7 1.5 collective-permute-done.36.y_late_ref
  131.6 2.3 %collective-permute-start.38 = (bf16[64,1024]{1,0:T(8,128)(2,1)S(1)}, bf16[64,1024]{1,0:T(8,128)(2,1)S(1)}, u32[]{:S(2)}, u32[]{:S(2)}) collective-permute-start(bf16[64,1024]{1,0:T(8,128)(2,1)S(1)} %get-tuple-element.104), channel_id=1, source_target_pairs={{0,4},{1,5},{2,6},{3,7},{4,0},{5,1},{6,2},{7,3},{8,12},{9,13},{10,... | collective-permute-start | bytes 393224 | tf_op jit(solution)/shard_map/ppermute | solution.py:904
  136.8 4.0 %collective-permute-start.24 = (bf16[64,1024]{1,0:T(8,128)(2,1)S(1)}, bf16[64,1024]{1,0:T(8,128)(2,1)S(1)}, u32[]{:S(2)}, u32[]{:S(2)}) collective-permute-start(bf16[64,1024]{1,0:T(8,128)(2,1)S(1)} %get-tuple-element.86), channel_id=1, source_target_pairs={{0,4},{1,5},{2,6},{3,7},{4,0},{5,1},{6,2},{7,3},{8,12},{9,13},{10,... | collective-permute-start | bytes 393224 | tf_op jit(solution)/shard_map/ppermute | solution.py:904
  140.9 2.5 %collective-permute-done.38.refs_2_ = bf16[64,1024]{1,0:T(8,128)(2,1)S(1)} collective-permute-done((bf16[64,1024]{1,0:T(8,128)(2,1)S(1)}, bf16[64,1024]{1,0:T(8,128)(2,1)S(1)}, u32[]{:S(2)}, u32[]{:S(2)}) %collective-permute-start.38) | collective-permute-done | bytes 131104 | tf_op jit(solution)/shard_map/ppermute | solution.py:904
  143.4 4.9 %collective-permute-start.27 = (f32[8,1024]{1,0:T(8,128)S(1)}, f32[8,1024]{1,0:T(8,128)S(1)}, u32[]{:S(2)}, u32[]{:S(2)}) collective-permute-start(f32[8,1024]{1,0:T(8,128)S(1)} %fusion), channel_id=1, source_target_pairs={{0,2},{1,3},{2,0},{3,1},{4,6},{5,7},{6,4},{7,5},{8,10},{9,11},{10,... | collective-permute-start | bytes 98312 | tf_op jit(solution)/shard_map/ppermute | solution.py:900
  148.3 2.4 %collective-permute-done.39.refs_3_ = bf16[64,1024]{1,0:T(8,128)(2,1)S(1)} collective-permute-done((bf16[64,1024]{1,0:T(8,128)(2,1)S(1)}, bf16[64,1024]{1,0:T(8,128)(2,1)S(1)}, u32[]{:S(2)}, u32[]{:S(2)}) %collective-permute-start.39) | collective-permute-done | bytes 131104 | tf_op jit(solution)/shard_map/ppermute | solution.py:904
  151.8 4.9 %collective-permute-done.28 = f32[8,1024]{1,0:T(8,128)S(1)} collective-permute-done((f32[8,1024]{1,0:T(8,128)S(1)}, f32[8,1024]{1,0:T(8,128)S(1)}, u32[]{:S(2)}, u32[]{:S(2)}) %collective-permute-start.28) | collective-permute-done | bytes 32800 | tf_op jit(solution)/shard_map/ppermute | solution.py:900
  158.9 1.8 %collective-permute-start.31 = (bf16[96,1024]{1,0:T(8,128)(2,1)S(1)}, bf16[96,1024]{1,0:T(8,128)(2,1)S(1)}, u32[]{:S(2)}, u32[]{:S(2)}) collective-permute-start(bf16[96,1024]{1,0:T(8,128)(2,1)S(1)} %collect.2.a_ref), channel_id=1, source_target_pairs={{0,24},{8,16},{16,8},{24,0},{1,25},{9,17},{17,9},{25,1},{2,26},{10... | collective-permute-start | bytes 589832 | tf_op jit(solution)/shard_map/ppermute | solution.py:897
  163.1 10.9 %collective-permute-done.41.c_ref = bf16[64,1024]{1,0:T(8,128)(2,1)S(1)} collective-permute-done((bf16[64,1024]{1,0:T(8,128)(2,1)S(1)}, bf16[64,1024]{1,0:T(8,128)(2,1)S(1)}, u32[]{:S(2)}, u32[]{:S(2)}) %collective-permute-start.41) | collective-permute-done | bytes 131104 | tf_op jit(solution)/shard_map/ppermute | solution.py:897
  (114 shorter events, 38.4 us)
Async XLA Ops:
  2.9 25.8 %collective-permute-start.1 = (bf16[2,64,1024]{2,1,0:T(8,128)(2,1)S(1)}, bf16[2,64,1024]{2,1,0:T(8,128)(2,1)S(1)}, u32[]{:S(2)}, u32[]{:S(2)}) collective-permute-start(bf16[2,64,1024]{2,1,0:T(8,128)(2,1)S(1)} %quarter.1.mine_ref), channel_id=1, source_target_pairs={{0,16},{8,24},{16,0},{24,8},{1,17},{9,25},{17,1},{25,9},{2,18},{10... | collective-permute-start | bytes 786440 | tf_op jit(solution)/shard_map/ppermute | solution.py:897
  4.5 24.2 %collective-permute-start = (bf16[2,64,1024]{2,1,0:T(8,128)(2,1)S(1)}, bf16[2,64,1024]{2,1,0:T(8,128)(2,1)S(1)}, u32[]{:S(2)}, u32[]{:S(2)}) collective-permute-start(bf16[2,64,1024]{2,1,0:T(8,128)(2,1)S(1)} %quarter.1.mine_ref), channel_id=1, source_target_pairs={{0,8},{8,0},{16,24},{24,16},{1,9},{9,1},{17,25},{25,17},{2,10},{10... | collective-permute-start | bytes 786440 | tf_op jit(solution)/shard_map/ppermute | solution.py:897
  6.0 22.7 %collective-permute-start.2 = (bf16[2,64,1024]{2,1,0:T(8,128)(2,1)S(1)}, bf16[2,64,1024]{2,1,0:T(8,128)(2,1)S(1)}, u32[]{:S(2)}, u32[]{:S(2)}) collective-permute-start(bf16[2,64,1024]{2,1,0:T(8,128)(2,1)S(1)} %quarter.1.mine_ref), channel_id=1, source_target_pairs={{0,6},{1,7},{2,0},{3,1},{4,2},{5,3},{6,4},{7,5},{8,14},{9,15},{10,... | collective-permute-start | bytes 786440 | tf_op jit(solution)/shard_map/ppermute | solution.py:904
  6.5 22.3 %collective-permute-start.3 = (bf16[2,64,1024]{2,1,0:T(8,128)(2,1)S(1)}, bf16[2,64,1024]{2,1,0:T(8,128)(2,1)S(1)}, u32[]{:S(2)}, u32[]{:S(2)}) collective-permute-start(bf16[2,64,1024]{2,1,0:T(8,128)(2,1)S(1)} %quarter.1.mine_ref), channel_id=1, source_target_pairs={{0,4},{1,5},{2,6},{3,7},{4,0},{5,1},{6,2},{7,3},{8,12},{9,13},{10,... | collective-permute-start | bytes 786440 | tf_op jit(solution)/shard_map/ppermute | solution.py:904
  9.1 21.6 %collective-permute-start.4 = (bf16[2,64,1024]{2,1,0:T(8,128)(2,1)S(1)}, bf16[2,64,1024]{2,1,0:T(8,128)(2,1)S(1)}, u32[]{:S(2)}, u32[]{:S(2)}) collective-permute-start(bf16[2,64,1024]{2,1,0:T(8,128)(2,1)S(1)} %quarter.1.mine_ref), channel_id=1, source_target_pairs={{0,2},{1,3},{2,4},{3,5},{4,6},{5,7},{6,0},{7,1},{8,10},{9,11},{10,... | collective-permute-start | bytes 786440 | tf_op jit(solution)/shard_map/ppermute | solution.py:904
  30.8 24.2 %collective-permute-start.7 = (bf16[6,2,64,1024]{3,2,1,0:T(8,128)(2,1)S(1)}, bf16[6,2,64,1024]{3,2,1,0:T(8,128)(2,1)S(1)}, u32[]{:S(2)}, u32[]{:S(2)}) collective-permute-start(bf16[6,2,64,1024]{3,2,1,0:T(8,128)(2,1)S(1)} %get-tuple-element.57.refs_1_.refs_0_), channel_id=1, source_target_pairs={{0,1},{1,0},{2,3},{3,2},{4,5},{5,4},{6,7},{7,6},{8,9},{9,8},{10,11... | collective-permute-start | bytes 4718600 | tf_op jit(solution)/shard_map/ppermute | solution.py:900
  30.9 20.0 %collective-permute-start.6 = (bf16[3,2,64,1024]{3,2,1,0:T(8,128)(2,1)S(1)}, bf16[3,2,64,1024]{3,2,1,0:T(8,128)(2,1)S(1)}, u32[]{:S(2)}, u32[]{:S(2)}) collective-permute-start(bf16[3,2,64,1024]{3,2,1,0:T(8,128)(2,1)S(1)} %get-tuple-element.58), channel_id=1, source_target_pairs={{0,16},{8,24},{16,0},{24,8},{1,17},{9,25},{17,1},{25,9},{2,18},{10... | collective-permute-start | bytes 2359304 | tf_op jit(solution)/shard_map/ppermute | solution.py:897
  31.5 19.6 %collective-permute-start.5 = (bf16[3,2,64,1024]{3,2,1,0:T(8,128)(2,1)S(1)}, bf16[3,2,64,1024]{3,2,1,0:T(8,128)(2,1)S(1)}, u32[]{:S(2)}, u32[]{:S(2)}) collective-permute-start(bf16[3,2,64,1024]{3,2,1,0:T(8,128)(2,1)S(1)} %get-tuple-element.58), channel_id=1, source_target_pairs={{0,8},{8,0},{16,24},{24,16},{1,9},{9,1},{17,25},{25,17},{2,10},{10... | collective-permute-start | bytes 2359304 | tf_op jit(solution)/shard_map/ppermute | solution.py:897
  50.9 11.4 %collective-permute-start.10 = (bf16[3,2,64,1024]{3,2,1,0:T(8,128)(2,1)S(1)}, bf16[3,2,64,1024]{3,2,1,0:T(8,128)(2,1)S(1)}, u32[]{:S(2)}, u32[]{:S(2)}) collective-permute-start(bf16[3,2,64,1024]{3,2,1,0:T(8,128)(2,1)S(1)} %collective-permute-done.6.y_far_ref.refs_2_), channel_id=1, source_target_pairs={{0,1},{1,0},{2,3},{3,2},{4,5},{5,4},{6,7},{7,6},{8,9},{9,8},{10,11... | collective-permute-start | bytes 2359304 | tf_op jit(solution)/shard_map/ppermute | solution.py:900
  51.1 12.2 %collective-permute-start.9 = (bf16[3,2,64,1024]{3,2,1,0:T(8,128)(2,1)S(1)}, bf16[3,2,64,1024]{3,2,1,0:T(8,128)(2,1)S(1)}, u32[]{:S(2)}, u32[]{:S(2)}) collective-permute-start(bf16[3,2,64,1024]{3,2,1,0:T(8,128)(2,1)S(1)} %collective-permute-done.5.x_far_ref.refs_1_), channel_id=1, source_target_pairs={{0,1},{1,0},{2,3},{3,2},{4,5},{5,4},{6,7},{7,6},{8,9},{9,8},{10,11... | collective-permute-start | bytes 2359304 | tf_op jit(solution)/shard_map/ppermute | solution.py:900
  57.5 28.0 %collective-permute-start.15 = (bf16[2,2,64,1024]{3,2,1,0:T(8,128)(2,1)S(1)}, bf16[2,2,64,1024]{3,2,1,0:T(8,128)(2,1)S(1)}, u32[]{:S(2)}, u32[]{:S(2)}) collective-permute-start(bf16[2,2,64,1024]{3,2,1,0:T(8,128)(2,1)S(1)} %get-tuple-element.67), channel_id=1, source_target_pairs={{0,16},{8,24},{16,0},{24,8},{1,17},{9,25},{17,1},{25,9},{2,18},{10... | collective-permute-start | bytes 1572872 | tf_op jit(solution)/shard_map/ppermute | solution.py:897
  59.1 26.4 %collective-permute-start.8 = (bf16[2,2,64,1024]{3,2,1,0:T(8,128)(2,1)S(1)}, bf16[2,2,64,1024]{3,2,1,0:T(8,128)(2,1)S(1)}, u32[]{:S(2)}, u32[]{:S(2)}) collective-permute-start(bf16[2,2,64,1024]{3,2,1,0:T(8,128)(2,1)S(1)} %get-tuple-element.61), channel_id=1, source_target_pairs={{0,8},{8,0},{16,24},{24,16},{1,9},{9,1},{17,25},{25,17},{2,10},{10... | collective-permute-start | bytes 1572872 | tf_op jit(solution)/shard_map/ppermute | solution.py:897
  59.7 20.5 %collective-permute-start.12 = (bf16[2,64,1024]{2,1,0:T(8,128)(2,1)S(1)}, bf16[2,64,1024]{2,1,0:T(8,128)(2,1)S(1)}, u32[]{:S(2)}, u32[]{:S(2)}) collective-permute-start(bf16[2,64,1024]{2,1,0:T(8,128)(2,1)S(1)} %get-tuple-element.64), channel_id=1, source_target_pairs={{0,2},{1,3},{2,4},{3,5},{4,6},{5,7},{6,0},{7,1},{8,10},{9,11},{10,... | collective-permute-start | bytes 786440 | tf_op jit(solution)/shard_map/ppermute | solution.py:904
  62.2 22.0 %collective-permute-start.13 = (bf16[2,64,1024]{2,1,0:T(8,128)(2,1)S(1)}, bf16[2,64,1024]{2,1,0:T(8,128)(2,1)S(1)}, u32[]{:S(2)}, u32[]{:S(2)}) collective-permute-start(bf16[2,64,1024]{2,1,0:T(8,128)(2,1)S(1)} %get-tuple-element.65), channel_id=1, source_target_pairs={{0,4},{1,5},{2,6},{3,7},{4,0},{5,1},{6,2},{7,3},{8,12},{9,13},{10,... | collective-permute-start | bytes 786440 | tf_op jit(solution)/shard_map/ppermute | solution.py:904
  63.2 22.2 %collective-permute-start.14 = (bf16[2,64,1024]{2,1,0:T(8,128)(2,1)S(1)}, bf16[2,64,1024]{2,1,0:T(8,128)(2,1)S(1)}, u32[]{:S(2)}, u32[]{:S(2)}) collective-permute-start(bf16[2,64,1024]{2,1,0:T(8,128)(2,1)S(1)} %get-tuple-element.66), channel_id=1, source_target_pairs={{0,6},{1,7},{2,0},{3,1},{4,2},{5,3},{6,4},{7,5},{8,14},{9,15},{10,... | collective-permute-start | bytes 786440 | tf_op jit(solution)/shard_map/ppermute | solution.py:904
  98.0 14.8 %collective-permute-start.33 = (bf16[4,64,1024]{2,1,0:T(8,128)(2,1)S(1)}, bf16[4,64,1024]{2,1,0:T(8,128)(2,1)S(1)}, u32[]{:S(2)}, u32[]{:S(2)}) collective-permute-start(bf16[4,64,1024]{2,1,0:T(8,128)(2,1)S(1)} %get-tuple-element.96), channel_id=1, source_target_pairs={{0,8},{8,0},{16,24},{24,16},{1,9},{9,1},{17,25},{25,17},{2,10},{10... | collective-permute-start | bytes 1572872 | tf_op jit(solution)/shard_map/ppermute | solution.py:897
  99.5 14.8 %collective-permute-start.34 = (bf16[4,64,1024]{2,1,0:T(8,128)(2,1)S(1)}, bf16[4,64,1024]{2,1,0:T(8,128)(2,1)S(1)}, u32[]{:S(2)}, u32[]{:S(2)}) collective-permute-start(bf16[4,64,1024]{2,1,0:T(8,128)(2,1)S(1)} %get-tuple-element.97), channel_id=1, source_target_pairs={{0,16},{8,24},{16,0},{24,8},{1,17},{9,25},{17,1},{25,9},{2,18},{10... | collective-permute-start | bytes 1572872 | tf_op jit(solution)/shard_map/ppermute | solution.py:897
  103.3 20.8 %collective-permute-start.19 = (bf16[4,64,1024]{2,1,0:T(8,128)(2,1)S(1)}, bf16[4,64,1024]{2,1,0:T(8,128)(2,1)S(1)}, u32[]{:S(2)}, u32[]{:S(2)}) collective-permute-start(bf16[4,64,1024]{2,1,0:T(8,128)(2,1)S(1)} %get-tuple-element.78), channel_id=1, source_target_pairs={{0,8},{8,0},{16,24},{24,16},{1,9},{9,1},{17,25},{25,17},{2,10},{10... | collective-permute-start | bytes 1572872 | tf_op jit(solution)/shard_map/ppermute | solution.py:897
  104.2 21.4 %collective-permute-start.20 = (bf16[4,64,1024]{2,1,0:T(8,128)(2,1)S(1)}, bf16[4,64,1024]{2,1,0:T(8,128)(2,1)S(1)}, u32[]{:S(2)}, u32[]{:S(2)}) collective-permute-start(bf16[4,64,1024]{2,1,0:T(8,128)(2,1)S(1)} %get-tuple-element.79), channel_id=1, source_target_pairs={{0,16},{8,24},{16,0},{24,8},{1,17},{9,25},{17,1},{25,9},{2,18},{10... | collective-permute-start | bytes 1572872 | tf_op jit(solution)/shard_map/ppermute | solution.py:897
  114.5 15.2 %collective-permute-start.35 = (bf16[2,64,1024]{2,1,0:T(8,128)(2,1)S(1)}, bf16[2,64,1024]{2,1,0:T(8,128)(2,1)S(1)}, u32[]{:S(2)}, u32[]{:S(2)}) collective-permute-start(bf16[2,64,1024]{2,1,0:T(8,128)(2,1)S(1)} %get-tuple-element.100), channel_id=1, source_target_pairs={{0,8},{8,0},{16,24},{24,16},{1,9},{9,1},{17,25},{25,17},{2,10},{10... | collective-permute-start | bytes 786440 | tf_op jit(solution)/shard_map/ppermute | solution.py:897
  115.1 16.1 %collective-permute-start.36 = (bf16[2,64,1024]{2,1,0:T(8,128)(2,1)S(1)}, bf16[2,64,1024]{2,1,0:T(8,128)(2,1)S(1)}, u32[]{:S(2)}, u32[]{:S(2)}) collective-permute-start(bf16[2,64,1024]{2,1,0:T(8,128)(2,1)S(1)} %get-tuple-element.101), channel_id=1, source_target_pairs={{0,16},{8,24},{16,0},{24,8},{1,17},{9,25},{17,1},{25,9},{2,18},{10... | collective-permute-start | bytes 786440 | tf_op jit(solution)/shard_map/ppermute | solution.py:897
  131.6 11.8 %collective-permute-start.38 = (bf16[64,1024]{1,0:T(8,128)(2,1)S(1)}, bf16[64,1024]{1,0:T(8,128)(2,1)S(1)}, u32[]{:S(2)}, u32[]{:S(2)}) collective-permute-start(bf16[64,1024]{1,0:T(8,128)(2,1)S(1)} %get-tuple-element.104), channel_id=1, source_target_pairs={{0,4},{1,5},{2,6},{3,7},{4,0},{5,1},{6,2},{7,3},{8,12},{9,13},{10,... | collective-permute-start | bytes 393224 | tf_op jit(solution)/shard_map/ppermute | solution.py:904
  134.5 16.3 %collective-permute-start.39 = (bf16[64,1024]{1,0:T(8,128)(2,1)S(1)}, bf16[64,1024]{1,0:T(8,128)(2,1)S(1)}, u32[]{:S(2)}, u32[]{:S(2)}) collective-permute-start(bf16[64,1024]{1,0:T(8,128)(2,1)S(1)} %get-tuple-element.105), channel_id=1, source_target_pairs={{0,6},{1,7},{2,0},{3,1},{4,2},{5,3},{6,4},{7,5},{8,14},{9,15},{10,... | collective-permute-start | bytes 393224 | tf_op jit(solution)/shard_map/ppermute | solution.py:904
  136.1 20.6 %collective-permute-start.23 = (bf16[64,1024]{1,0:T(8,128)(2,1)S(1)}, bf16[64,1024]{1,0:T(8,128)(2,1)S(1)}, u32[]{:S(2)}, u32[]{:S(2)}) collective-permute-start(bf16[64,1024]{1,0:T(8,128)(2,1)S(1)} %get-tuple-element.85), channel_id=1, source_target_pairs={{0,2},{1,3},{2,4},{3,5},{4,6},{5,7},{6,0},{7,1},{8,10},{9,11},{10,... | collective-permute-start | bytes 393224 | tf_op jit(solution)/shard_map/ppermute | solution.py:904
  136.8 19.9 %collective-permute-start.24 = (bf16[64,1024]{1,0:T(8,128)(2,1)S(1)}, bf16[64,1024]{1,0:T(8,128)(2,1)S(1)}, u32[]{:S(2)}, u32[]{:S(2)}) collective-permute-start(bf16[64,1024]{1,0:T(8,128)(2,1)S(1)} %get-tuple-element.86), channel_id=1, source_target_pairs={{0,4},{1,5},{2,6},{3,7},{4,0},{5,1},{6,2},{7,3},{8,12},{9,13},{10,... | collective-permute-start | bytes 393224 | tf_op jit(solution)/shard_map/ppermute | solution.py:904
  140.8 16.3 %collective-permute-start.25 = (bf16[64,1024]{1,0:T(8,128)(2,1)S(1)}, bf16[64,1024]{1,0:T(8,128)(2,1)S(1)}, u32[]{:S(2)}, u32[]{:S(2)}) collective-permute-start(bf16[64,1024]{1,0:T(8,128)(2,1)S(1)} %get-tuple-element.87), channel_id=1, source_target_pairs={{0,6},{1,7},{2,0},{3,1},{4,2},{5,3},{6,4},{7,5},{8,14},{9,15},{10,... | collective-permute-start | bytes 393224 | tf_op jit(solution)/shard_map/ppermute | solution.py:904
  150.8 10.7 %collective-permute-start.40 = (bf16[64,1024]{1,0:T(8,128)(2,1)S(1)}, bf16[64,1024]{1,0:T(8,128)(2,1)S(1)}, u32[]{:S(2)}, u32[]{:S(2)}) collective-permute-start(bf16[64,1024]{1,0:T(8,128)(2,1)S(1)} %collect.3.a_ref), channel_id=1, source_target_pairs={{0,8},{8,0},{16,24},{24,16},{1,9},{9,1},{17,25},{25,17},{2,10},{10... | collective-permute-start | bytes 393224 | tf_op jit(solution)/shard_map/ppermute | solution.py:897
  157.2 17.9 %collective-permute-start.29 = (bf16[96,1024]{1,0:T(8,128)(2,1)S(1)}, bf16[96,1024]{1,0:T(8,128)(2,1)S(1)}, u32[]{:S(2)}, u32[]{:S(2)}) collective-permute-start(bf16[96,1024]{1,0:T(8,128)(2,1)S(1)} %collect.2.a_ref), channel_id=1, source_target_pairs={{0,8},{8,0},{16,24},{24,16},{1,9},{9,1},{17,25},{25,17},{2,10},{10... | collective-permute-start | bytes 589832 | tf_op jit(solution)/shard_map/ppermute | solution.py:897
  158.1 17.0 %collective-permute-start.30 = (bf16[96,1024]{1,0:T(8,128)(2,1)S(1)}, bf16[96,1024]{1,0:T(8,128)(2,1)S(1)}, u32[]{:S(2)}, u32[]{:S(2)}) collective-permute-start(bf16[96,1024]{1,0:T(8,128)(2,1)S(1)} %collect.2.a_ref), channel_id=1, source_target_pairs={{0,16},{8,24},{16,0},{24,8},{1,17},{9,25},{17,1},{25,9},{2,18},{10... | collective-permute-start | bytes 589832 | tf_op jit(solution)/shard_map/ppermute | solution.py:897
  158.9 16.2 %collective-permute-start.31 = (bf16[96,1024]{1,0:T(8,128)(2,1)S(1)}, bf16[96,1024]{1,0:T(8,128)(2,1)S(1)}, u32[]{:S(2)}, u32[]{:S(2)}) collective-permute-start(bf16[96,1024]{1,0:T(8,128)(2,1)S(1)} %collect.2.a_ref), channel_id=1, source_target_pairs={{0,24},{8,16},{16,8},{24,0},{1,25},{9,17},{17,9},{25,1},{2,26},{10... | collective-permute-start | bytes 589832 | tf_op jit(solution)/shard_map/ppermute | solution.py:897
  160.7 13.2 %collective-permute-start.41 = (bf16[64,1024]{1,0:T(8,128)(2,1)S(1)}, bf16[64,1024]{1,0:T(8,128)(2,1)S(1)}, u32[]{:S(2)}, u32[]{:S(2)}) collective-permute-start(bf16[64,1024]{1,0:T(8,128)(2,1)S(1)} %collect.3.a_ref), channel_id=1, source_target_pairs={{0,16},{8,24},{16,0},{24,8},{1,17},{9,25},{17,1},{25,9},{2,18},{10... | collective-permute-start | bytes 393224 | tf_op jit(solution)/shard_map/ppermute | solution.py:897
  161.5 12.4 %collective-permute-start.42 = (bf16[64,1024]{1,0:T(8,128)(2,1)S(1)}, bf16[64,1024]{1,0:T(8,128)(2,1)S(1)}, u32[]{:S(2)}, u32[]{:S(2)}) collective-permute-start(bf16[64,1024]{1,0:T(8,128)(2,1)S(1)} %collect.3.a_ref), channel_id=1, source_target_pairs={{0,24},{8,16},{16,8},{24,0},{1,25},{9,17},{17,9},{25,1},{2,26},{10... | collective-permute-start | bytes 393224 | tf_op jit(solution)/shard_map/ppermute | solution.py:897
  (24 other events, 217.2 us)

commit v6 on v5

--- a/solution.py
+++ b/solution.py
@@ -12,6 +12,7 @@
 BF16 = jnp.bfloat16
 MIB = 1024 * 1024
 COST = pl.CostEstimate(flops=1 << 20, bytes_accessed=1 << 16, transcendentals=0)
+LONG = pl.CostEstimate(flops=10**10, bytes_accessed=1 << 20, transcendentals=0)
 SMEM = pl.BlockSpec(memory_space=pltpu.SMEM)
 VMEM = pl.BlockSpec(memory_space=pltpu.VMEM)
 ANY = pl.BlockSpec(memory_space=pl.ANY)
@@ -37,7 +38,7 @@
     block = lax.div(pixels, jnp.int32(rows))
     owner = jnp.zeros_like(pixels)
     for slot in range(count):
-        owner = jnp.where(block == slot, owner_ref[0, slot], owner)
+        owner = jnp.where(block == slot, owner_ref[0:1, slot:slot + 1], owner)
     return owner
 
 
@@ -47,19 +48,43 @@
     return jnp.where(before < after, 1.0, 0.0).astype(BF16)
 
 
-def whole(array):
-    return pl.BlockSpec(array.shape, lambda step: (0,) * array.ndim)
+HBM = pl.BlockSpec(memory_space=pltpu.HBM)
+
+
+def fetch(copies, sems):
+    started = [
+        pltpu.make_async_copy(source, target, sems.at[index])
+        for index, (source, target) in enumerate(copies)
+    ]
+    for copy in started:
+        copy.start()
+
+    def wait(*numbers):
+        for number in numbers:
+            started[number].wait()
+
+    return wait
 
 
 def render_kernel(
-    ray_count, relative, me_ref, owner_ref, lists_ref, opacity_ref, counts_ref, pixels_ref,
-    features_ref, near_ref, other_ref, ids_ref, share_ref, table_ref, send_ref,
+    ray_count, relative, me_ref, owner_hbm, lists_hbm, opacity_hbm, counts_hbm, pixels_hbm,
+    features_hbm, near_ref, other_ref, owner_ref, ids_ref, opacity_ref, counts_ref, mine_ref,
+    features_ref, share_ref, table_ref, send_ref, sems,
 ):
-    depth, rays = lists_ref.shape
-    gauss = features_ref.shape[0]
-    width = features_ref.shape[1]
+    depth, rays = lists_hbm.shape
+    gauss = features_hbm.shape[0]
+    width = features_hbm.shape[1]
     me = me_ref[0]
-    ids_ref[...] = lists_ref[...] - me * gauss
+    own_pixels = pixels_hbm.at[:, pl.ds(pl.multiple_of(me * rays, rays), rays)]
+    wait = fetch(
+        [
+            (lists_hbm, ids_ref), (opacity_hbm, opacity_ref), (counts_hbm, counts_ref),
+            (owner_hbm, owner_ref), (own_pixels, mine_ref), (features_hbm, features_ref),
+        ],
+        sems,
+    )
+    wait(0, 1, 2)
+    ids_ref[...] = ids_ref[...] - me * gauss
     passing = jnp.ones((1, rays), F32)
     counts = counts_ref[...]
     for level in range(depth):
@@ -83,8 +108,8 @@
             total = total + jnp.where(ident == number, share, 0.0)
         table_ref[pl.ds(first, tile), pl.ds(lane, lanes)] = total.astype(BF16)
 
-    mine = pixels_ref[:, pl.ds(pl.multiple_of(me * rays, rays), rays)]
-    owner = owner_of(mine, owner_ref, rays, ray_count)
+    wait(3, 4, 5)
+    owner = owner_of(mine_ref[...], owner_ref, rays, ray_count)
     padded = -(-ray_count // 16) * 16
     member = (lax.broadcasted_iota(jnp.int32, (padded, rays), 0) == owner)
     ranks = dot_nn(member.astype(F32).astype(BF16), earlier(rays))
@@ -118,32 +143,46 @@
     depth, rays = lists.shape
     gauss, width = features.shape
     shape = jax.ShapeDtypeStruct((ray_count // 2, rays // ray_count, width), BF16)
-    operands = (lists, opacity, counts, pixels, features)
     return pl.pallas_call(
         functools.partial(render_kernel, ray_count, relative),
-        grid=(1,),
         out_shape=(shape, shape),
-        in_specs=[SMEM, SMEM] + [whole(array) for array in operands],
+        in_specs=[SMEM] + [HBM] * 6,
         out_specs=(VMEM, VMEM),
         scratch_shapes=[
+            pltpu.VMEM(owner.shape, jnp.int32),
             pltpu.VMEM((depth, rays), jnp.int32),
+            pltpu.VMEM((depth, rays), F32),
+            pltpu.VMEM((1, rays), jnp.int32),
+            pltpu.VMEM((1, rays), jnp.int32),
+            pltpu.VMEM((gauss, width), BF16),
             pltpu.VMEM((depth, rays), F32),
             pltpu.VMEM((gauss, rays), BF16),
             pltpu.VMEM((rays, rays), BF16),
+            pltpu.SemaphoreType.DMA((6,)),
         ],
-        compiler_params=params(24),
+        compiler_params=params(20),
         cost_estimate=COST,
         name="render",
-    )(me, owner, *operands)
+    )(me, owner, lists, opacity, counts, pixels, features)
 
 
 def tokens_kernel(
-    ray_count, relative, me_ref, owner_ref, pixels_ref, tokens_ref, gain_ref,
-    tokens_out, normed_out, normed_t_out, order_ref, rank_ref, place_ref,
+    ray_count, relative, me_ref, owner_hbm, pixels_hbm, tokens_hbm, gain_hbm,
+    *refs,
 ):
-    rows, width = tokens_ref.shape
+    tokens_out, normed_out, normed_t_out = refs[-11:-8]
+    owner_ref, pixels_ref, tokens_ref, gain_ref, order_ref, rank_ref, place_ref, sems = refs[-8:]
+    rows, width = tokens_hbm.shape
     me = me_ref[0]
     each = rows // ray_count
+    wait = fetch(
+        [
+            (owner_hbm, owner_ref), (pixels_hbm, pixels_ref), (gain_hbm, gain_ref),
+            (tokens_hbm, tokens_ref),
+        ],
+        sems,
+    )
+    wait(0, 1)
     pixels = jnp.concatenate(
         [pixels_ref[:, sender * rows:(sender + 1) * rows] for sender in range(ray_count)], axis=0
     )
@@ -171,6 +210,7 @@
         )
         here = lax.broadcasted_iota(jnp.int32, (each, rows), 1) == at.astype(jnp.int32)
         order_ref[pl.ds(index * each, each), :] = here.astype(F32).astype(BF16)
+    wait(2, 3)
     half = min(128, rows)
     gain = gain_ref[...]
 
@@ -187,27 +227,31 @@
         normed_t_out[:, span] = normed.T
 
 
-def prepare_tokens(ray_count, relative, me, owner, pixels, tokens, gain):
+def prepare_tokens(ray_count, relative, me, owner, pixels, tokens, gain, after=()):
     rows, width = tokens.shape
     return pl.pallas_call(
         functools.partial(tokens_kernel, ray_count, relative),
-        grid=(1,),
         out_shape=(
             jax.ShapeDtypeStruct((rows, width), BF16),
             jax.ShapeDtypeStruct((rows, width), BF16),
             jax.ShapeDtypeStruct((width, rows), BF16),
         ),
-        in_specs=[SMEM, SMEM, whole(pixels), whole(tokens), whole(gain)],
+        in_specs=[SMEM] + [HBM] * 4 + [ANY] * len(after),
         out_specs=(VMEM, VMEM, VMEM),
         scratch_shapes=[
+            pltpu.VMEM(owner.shape, jnp.int32),
+            pltpu.VMEM(pixels.shape, jnp.int32),
+            pltpu.VMEM((rows, width), BF16),
+            pltpu.VMEM((1, width), F32),
             pltpu.VMEM((rows, rows), BF16),
             pltpu.VMEM((ray_count, rows), F32),
             pltpu.VMEM((ray_count, rows), F32),
+            pltpu.SemaphoreType.DMA((4,)),
         ],
         compiler_params=params(20),
         cost_estimate=COST,
         name="tokens",
-    )(me, owner, pixels, tokens, gain)
+    )(me, owner, pixels, tokens, gain, *after)
 
 
 def up_kernel(normed_ref, up_ref, act_ref, slope_ref):
@@ -447,25 +491,39 @@
     return (grad_up, grad_down, sums[0], sums[1], loss)
 
 
-def quarter_kernel(group_ref, up_ref, down_ref, out_ref, turned_ref):
+def quarter_kernel(group_ref, up_hbm, down_hbm, out_ref, up_ref, turned_ref, sems):
     part = out_ref.shape[1]
-    first = pl.multiple_of(group_ref[0] * part, part)
+    lanes = up_ref.shape[1]
+    start = pl.multiple_of(group_ref[0] * part, part)
+    lane = pl.multiple_of(lax.div(start, jnp.int32(lanes)) * lanes, lanes)
+    wait = fetch(
+        [
+            (up_hbm.at[:, pl.ds(lane, lanes)], up_ref),
+            (down_hbm.at[pl.ds(start, part), :], out_ref.at[1]),
+        ],
+        sems,
+    )
+    wait(0)
     turned_ref[...] = up_ref[...].T
-    out_ref[0] = turned_ref[pl.ds(first, part), :]
-    out_ref[1] = down_ref[pl.ds(first, part), :]
+    out_ref[0] = turned_ref[pl.ds(pl.multiple_of(start - lane, part), part), :]
+    wait(1)
 
 
 def own_quarter(group, up, down, part):
     width, chunk = up.shape
+    lanes = max(128, part)
     return pl.pallas_call(
         quarter_kernel,
         out_shape=jax.ShapeDtypeStruct((2, part, width), BF16),
-        grid=(1,),
-        in_specs=[SMEM, whole(up), whole(down)],
+        in_specs=[SMEM, HBM, HBM],
         out_specs=VMEM,
-        scratch_shapes=[pltpu.VMEM((chunk, width), BF16)],
+        scratch_shapes=[
+            pltpu.VMEM((width, lanes), BF16),
+            pltpu.VMEM((lanes, width), BF16),
+            pltpu.SemaphoreType.DMA((2,)),
+        ],
         compiler_params=params(16),
-        cost_estimate=COST,
+        cost_estimate=LONG,
         name="quarter",
     )(group, up, down)
 
@@ -571,9 +629,10 @@
     )(*operands)
 
 
-def pack_kernel(mine_ref, x_ref, y_ref, *refs):
-    count = len(refs) - 3
-    arrivals, (all_ref, far_ref) = refs[:count], refs[-2:]
+def pack_kernel(mine_ref, *refs):
+    count = len(refs) - 5
+    arrivals, (x_ref, y_ref) = refs[:count], refs[count:count + 2]
+    all_ref, far_ref = refs[-2:]
     for index, ref in enumerate((mine_ref, x_ref, y_ref)):
         all_ref[index] = ref[...]
     for index, ref in enumerate(arrivals):
@@ -595,7 +654,7 @@
         compiler_params=params(16),
         cost_estimate=COST,
         name="pack",
-    )(mine, x, y, *arrivals, after)
+    )(mine, *arrivals, x, y, after)
 
 
 def turn_kernel(y_ref, y_far_ref, x_far_ref, after_ref, a_ref, b_ref):
@@ -704,8 +763,12 @@
 def up_grad_kernel(side, weight_pieces, act_pieces, add, *refs):
     weights, slopes = refs[:5], refs[5:8]
     back_t_ref, normed_ref, gain_in = refs[8:11]
-    arrived = refs[11] if add else None
-    outs, gain_ref = refs[12 if add else 11:-1], refs[-1]
+    if add:
+        arrived, scale_ref, small_ref = refs[11:14]
+        outs, vector_ref, gain_ref = refs[14:-2], refs[-2], refs[-1]
+    else:
+        arrived = None
+        outs, gain_ref = refs[11:-1], refs[-1]
     gain_ref[...] = gain_in[...]
     for quarter in (3, 1, 2, 0):
         pieces = weight_pieces[quarter]
@@ -716,6 +779,10 @@
         up = joined(weights, pieces, lambda ref, a, n: ref[a:a + n, 0]).astype(F32)
         gain_ref[...] += jnp.sum(grad * up, axis=0, keepdims=True)
         emit(quarter, grad, arrived, outs)
+    if add:
+        vector_ref[0:1, :] = gain_ref[...] / scale_ref[...]
+        vector_ref[1:3, :] = small_ref[0:2, :]
+        vector_ref[3:8, :] = jnp.zeros((5, gain_ref.shape[1]), F32)
 
 
 def gradient_shapes(depth, part, width, add):
@@ -743,39 +810,47 @@
 
 
 def up_gradient(
-    side, weight_pieces, act_pieces, depth, weights, slopes, back_t, normed, gain, arrived=None
+    side, weight_pieces, act_pieces, depth, weights, slopes, back_t, normed, gain, extra=()
 ):
     part, width = weights[0].shape[2:]
-    add = arrived is not None
-    operands = [*weights, *slopes, back_t, normed, gain] + ([arrived] if add else [])
-    shapes = gradient_shapes(depth, part, width, add) + [jax.ShapeDtypeStruct((1, width), F32)]
+    add = len(extra) > 0
+    operands = [*weights, *slopes, back_t, normed, gain, *extra]
+    shapes = gradient_shapes(depth, part, width, add)
+    if add:
+        shapes.append(jax.ShapeDtypeStruct((8, width), F32))
+        scratch = [pltpu.VMEM((1, width), F32)]
+    else:
+        scratch = []
+        shapes.append(jax.ShapeDtypeStruct((1, width), F32))
     return pl.pallas_call(
         functools.partial(up_grad_kernel, side, weight_pieces, act_pieces, add),
         out_shape=tuple(shapes),
         in_specs=[VMEM] * len(operands),
         out_specs=tuple([VMEM] * len(shapes)),
+        scratch_shapes=scratch,
         compiler_params=params(24),
         cost_estimate=COST,
         name="up_gradient",
     )(*operands)
 
 
-def merge_kernel(x_ref, y_ref, x_later_ref, y_later_ref, x_out, y_out):
+def merge_kernel(x_ref, y_ref, x_later_ref, y_later_ref, *refs):
+    x_out, y_out = refs[-2:]
     half = y_later_ref.shape[0]
     x_out[...] = (x_later_ref[...].astype(F32) + y_ref[:half].astype(F32)).astype(BF16)
     y_out[...] = (y_later_ref[...].astype(F32) + x_ref[:half].astype(F32)).astype(BF16)
 
 
-def merge(x, y, x_later, y_later):
+def merge(x, y, x_later, y_later, *after):
     return pl.pallas_call(
         merge_kernel,
         out_shape=tuple(jax.ShapeDtypeStruct(a.shape, BF16) for a in (x_later, y_later)),
-        in_specs=[VMEM] * 4,
+        in_specs=[VMEM] * 4 + [ANY] * len(after),
         out_specs=(VMEM, VMEM),
         compiler_params=params(16),
         cost_estimate=COST,
         name="merge",
-    )(x, y, x_later, y_later)
+    )(x, y, x_later, y_later, *after)
 
 
 def total_kernel(own_ref, x_ref, y_ref, x_late_ref, y_late_ref, *outs):
@@ -810,6 +885,7 @@
         total = total + ref[...].astype(F32)
     out_ref[pl.ds(0, part), :] = total.astype(BF16)
     if len(refs) > count + 1:
+        out_ref[pl.ds(part, part), :] = refs[count + 1][...]
         rest = refs[count][...]
         pieces = []
         for _ in range(3):
@@ -817,15 +893,16 @@
             pieces.append(piece)
             rest = rest - piece
         pieces.append(jnp.zeros_like(rest))
-        out_ref[pl.ds(part, 32), :] = jnp.concatenate(pieces, axis=0).astype(BF16)
-
-
-def collect(parts, vector=None):
+        out_ref[pl.ds(2 * part, 32), :] = jnp.concatenate(pieces, axis=0).astype(BF16)
+
+
+def collect(parts, extra=()):
     part, width = parts[0].shape
-    operands = list(parts) + ([] if vector is None else [vector])
+    operands = list(parts) + list(extra)
+    rows = 2 * part + 32 if extra else part
     return pl.pallas_call(
         functools.partial(collect_kernel, len(parts)),
-        out_shape=jax.ShapeDtypeStruct((part + (0 if vector is None else 32), width), BF16),
+        out_shape=jax.ShapeDtypeStruct((rows, width), BF16),
         in_specs=[VMEM] * len(operands),
         out_specs=VMEM,
         compiler_params=params(16),
@@ -834,34 +911,35 @@
     )(*operands)
 
 
-def place_kernel(part, group_ref, a_ref, b_ref, c_ref, d_ref, *refs):
+def place_kernel(part, tokens, group_ref, *refs):
+    quarters = refs[:4]
+    up_ref, down_ref, gain_ref, scale_ref, loss_ref, held_ref = refs[4:]
     group = group_ref[0]
-    held_ref = refs[-1]
-    quarters = (a_ref, b_ref, c_ref, d_ref)
+    vectors = []
     for index, ref in enumerate(quarters):
         first = pl.multiple_of(jnp.bitwise_xor(group, index) * part, part)
         held_ref[pl.ds(first, part), :] = ref[pl.ds(0, part), :].astype(F32)
-    if len(refs) == 2:
-        refs[0][...] = held_ref[...]
-        return
-    refs[0][...] = held_ref[...].T
-    vectors = []
-    for ref in quarters:
-        rows = ref[pl.ds(part, 32), :].astype(F32)
+        down_ref[pl.ds(first, part), :] = ref[pl.ds(part, part), :].astype(F32)
+        rows = ref[pl.ds(2 * part, 32), :].astype(F32)
         vectors.append((rows[0:8] + rows[8:16]) + rows[16:24])
-    refs[1][...] = (vectors[0] + vectors[1]) + (vectors[2] + vectors[3])
-
-
-def place_quarters(group, quarters, part, vector):
+    up_ref[...] = held_ref[...].T
+    vector = (vectors[0] + vectors[1]) + (vectors[2] + vectors[3])
+    gain_ref[...] = vector[0:1]
+    scale_ref[...] = vector[1:2]
+    loss_ref[...] = vector[2:3, 0:1] * (1.0 / tokens)
+
+
+def place_quarters(group, quarters, part, tokens):
     width = quarters[0].shape[1]
-    if vector:
-        shapes = [
-            jax.ShapeDtypeStruct((width, 4 * part), F32), jax.ShapeDtypeStruct((8, width), F32)
-        ]
-    else:
-        shapes = [jax.ShapeDtypeStruct((4 * part, width), F32)]
-    return pl.pallas_call(
-        functools.partial(place_kernel, part),
+    shapes = [
+        jax.ShapeDtypeStruct((width, 4 * part), F32),
+        jax.ShapeDtypeStruct((4 * part, width), F32),
+        jax.ShapeDtypeStruct((1, width), F32),
+        jax.ShapeDtypeStruct((1, width), F32),
+        jax.ShapeDtypeStruct((1, 1), F32),
+    ]
+    return pl.pallas_call(
+        functools.partial(place_kernel, part, tokens),
         out_shape=tuple(shapes),
         in_specs=[SMEM] + [VMEM] * 4,
         out_specs=tuple([VMEM] * len(shapes)),
@@ -906,7 +984,6 @@
     mine = own_quarter(group, up_weight, down_weight, part)
     arrivals = [along(mine, -shift) for shift in range(1, depth)]
     x, y = beside(mine, 1), beside(mine, 2)
-
     rendered, rendered_other = render(
         ray_count, True, me, block_owner, tile_lists, opacity, tile_counts.reshape(1, rows),
         ray_pixel, gaussian_features,
@@ -918,14 +995,15 @@
     first_other = partner(first)
     tokens, normed, normed_t = prepare_tokens(
         ray_count, True, me, block_owner, ray_pixel, image_tokens,
-        layer_norm_gain.reshape(1, width),
+        layer_norm_gain.reshape(1, width), (blocks[0],),
     )
     act_first, slope_first, mixed = forward(normed_t, [first], [first_other])
+    x_far, y_far = tie(x_far, mixed, *targets[1:]), tie(y_far, mixed, *targets[1:])
     passed_x, passed_y = turn(y, y_far, x_far, mixed)
     d_low, d_high = beside(passed_x, 1), beside(passed_y, 2)
     x_other, y_other = partner(x_far), partner(y_far)
     act_next, slope_next, mixed = forward(normed_t, [x_far, y_far], [x_other, y_other], mixed)
-    d_low, d_high = tie(d_low, mixed, *targets[1:]), tie(d_high, mixed, *targets[1:])
+    d_low, d_high = tie(d_low, mixed), tie(d_high, mixed)
     low_other, high_other = partner(d_low), partner(d_high)
     act_last, slope_last, back, back_t, small = forward(
         normed_t, [d_low, d_high], [low_other, high_other], mixed,
@@ -958,34 +1036,33 @@
     )
     up_arrived = partner(up_other)
     down_sums = down_gradient(0, act_pieces, depth, acts, back, down_arrived)
-    *up_sums, gain = up_gradient(
-        0, weight_pieces, act_pieces, depth, weights[0], slopes, back_t, normed, gain, up_arrived
-    )
-
-    def sum_beside(own, to_x, to_y, x_later, y_later):
-        from_x, from_y = beside(to_x, 1), beside(to_y, 2)
-        x_later, y_later = merge(from_x, from_y, x_later, y_later)
-        return totals(own, from_x, from_y, beside(x_later, 1), beside(y_later, 2))
-
-    def sum_along(shares, *vector):
-        arrivals = [along(shares[shift], shift) for shift in range(1, depth)]
-        total = collect([shares[0]] + arrivals, *vector)
-        return [total] + [beside(total, flip) for flip in (1, 2, 3)]
-
-    vector = jnp.concatenate(
-        [gain / layer_norm_gain.reshape(1, width), small[:2], jnp.zeros((5, width), F32)], axis=0
+    *up_sums, vector = up_gradient(
+        0, weight_pieces, act_pieces, depth, weights[0], slopes, back_t, normed, gain,
+        (up_arrived, layer_norm_gain.reshape(1, width), small),
     )
     vector = vector + partner(vector)
     flip = 2
     while flip < ray_count:
         vector = vector + partner(vector, flip)
         flip *= 2
-    quarters = sum_along(sum_beside(*down_sums))
-    (grad_down,) = place_quarters(group, quarters, part, False)
-    quarters = sum_along(sum_beside(*up_sums), vector)
-    grad_up, vector = place_quarters(group, quarters, part, True)
-    loss = vector[2, 0] / (rows * ray_count * group_count)
-    return (grad_up, grad_down, vector[0], vector[1], loss)
+
+    def sum_beside(own, to_x, to_y, x_later, y_later):
+        from_x, from_y = beside(to_x, 1), beside(to_y, 2)
+        x_later, y_later = merge(from_x, from_y, x_later, y_later, vector)
+        return totals(own, from_x, from_y, beside(x_later, 1), beside(y_later, 2))
+
+    def sum_along(shares, extra=()):
+        return collect(
+            [shares[0]] + [along(shares[shift], shift) for shift in range(1, depth)], extra
+        )
+
+    down_total = sum_along(sum_beside(*down_sums))
+    total = sum_along(sum_beside(*up_sums), (vector, down_total))
+    quarters = [total] + [beside(total, flip) for flip in (1, 2, 3)]
+    grad_up, grad_down, gain, scale, loss = place_quarters(
+        group, quarters, part, rows * ray_count * group_count
+    )
+    return (grad_up, grad_down, gain.reshape(width), scale.reshape(width), loss.reshape(()))
 
 
 def shards(*operands):

time: 183 us -> 164 us (0.90); the launches traced: 179 us -> 163 us
  waiting for transfers between devices: 88.5 us -> 76.6 us
  local copies, waits for them, and re-layouts: 8.62 us -> 3.45 us
  starting transfers between devices: 44.4 us -> 47.5 us
    ppermute x20 -> x17, waiting for transfers between devices: 53.6 us -> 31.5 us  [beside(): lax.ppermute(array, 'grp', [(g, g ^ flip) for g in range(group_count)])]
    ppermute x12, waiting for transfers between devices: 26.6 us -> 33.3 us  [along(): return lax.ppermute(array, 'ray', pairs)]
    unnamed x26 -> x24, local copies, waits for them, and re-layouts: 7.42 us -> 3.44 us
    ppermute x11, waiting for transfers between devices: 8.25 us -> 11.8 us  [partner(): return lax.ppermute(array, 'ray', [(r, r ^ flip) for r in range(ray_count)])]
    ppermute x12, starting transfers between devices: 18 us -> 21.1 us  [along(): return lax.ppermute(array, 'ray', pairs)]
    pallas_call x4 -> x3, Pallas kernels: 17.7 us -> 16.7 us  [the longest x1 11.7 us: render(): pl.pallas_call(functools.partial(render_kernel, ray_count, relative), out...]
    ppermute x20 -> x17, starting transfers between devices: 19.7 us -> 19 us  [beside(): lax.ppermute(array, 'grp', [(g, g ^ flip) for g in range(group_count)])]
  transfers between devices with their start and end apart: 43 -> 40, of which waited for: 22 -> 27; matrix products, arithmetic and copies ran while one was open for 0% -> 0% of each run, Pallas kernels for 16% -> 17%
where the time goes in v6:
time: 164 us; the launch traced here: 163 us
  waiting for transfers between devices  76.6 us (47%)
  starting transfers between devices  47.5 us (29%)
  Pallas kernels  35 us (21%)
  local copies, waits for them, and re-layouts  3.45 us (2%)
    ppermute x12, waiting for transfers between devices, along(): return lax.ppermute(array, 'ray', pairs)  33.3 us
    ppermute x17, waiting for transfers between devices, beside(): lax.ppermute(array, 'grp', [(g, g ^ flip) for g in range(group_count)])  31.5 us
    ppermute x12, starting transfers between devices, along(): return lax.ppermute(array, 'ray', pairs)  21.1 us
    ppermute x17, starting transfers between devices, beside(): lax.ppermute(array, 'grp', [(g, g ^ flip) for g in range(group_count)])  19 us
    ppermute x11, waiting for transfers between devices, partner(): return lax.ppermute(array, 'ray', [(r, r ^ flip) for r in range(ray_count)])  11.8 us
    pallas_call x1, Pallas kernels, render(): pl.pallas_call(functools.partial(render_kernel, ray_count, relative), out...  11.7 us
    pallas_call x3, Pallas kernels, forward(): pl.pallas_call(functools.partial(forward_kernel, first, blocks, len(own))...  7.61 us
    ppermute x11, starting transfers between devices, partner(): return lax.ppermute(array, 'ray', [(r, r ^ flip) for r in range(ray_count)])  7.41 us
  transfers between devices with their start and end apart: 40, of which 27 were waited for; matrix products, arithmetic and copies ran while one was open for 0% of the time, Pallas kernels for 17%

profile of v6, /device:TPU:8, one launch (start us, length us, event | category | flops | bytes accessed | tf_op | source)
XLA Modules:
  0.0 163.4 jit_solution(3754012554898514757)
XLA Ops:
  3.1 1.6 collective-permute-start.4
  5.2 2.6 %collective-permute-start.1 = (bf16[2,64,1024]{2,1,0:T(8,128)(2,1)S(1)}, bf16[2,64,1024]{2,1,0:T(8,128)(2,1)S(1)}, u32[]{:S(2)}, u32[]{:S(2)}) collective-permute-start(bf16[2,64,1024]{2,1,0:T(8,128)(2,1)S(1)} %quarter.1.mine_ref), channel_id=1, source_target_pairs={{0,4},{1,5},{2,6},{3,7},{4,0},{5,1},{6,2},{7,3},{8,12},{9,13},{10,... | collective-permute-start | bytes 786440 | tf_op jit(solution)/shard_map/ppermute | solution.py:982
  7.7 2.5 %collective-permute-start.2 = (bf16[2,64,1024]{2,1,0:T(8,128)(2,1)S(1)}, bf16[2,64,1024]{2,1,0:T(8,128)(2,1)S(1)}, u32[]{:S(2)}, u32[]{:S(2)}) collective-permute-start(bf16[2,64,1024]{2,1,0:T(8,128)(2,1)S(1)} %quarter.1.mine_ref), channel_id=1, source_target_pairs={{0,2},{1,3},{2,4},{3,5},{4,6},{5,7},{6,0},{7,1},{8,10},{9,11},{10,... | collective-permute-start | bytes 786440 | tf_op jit(solution)/shard_map/ppermute | solution.py:982
  13.1 11.7 %render.1 = (bf16[4,64,1024]{2,1,0:T(8,128)(2,1)S(1)}, bf16[4,64,1024]{2,1,0:T(8,128)(2,1)S(1)}) custom-call(s32[1]{0:T(128)} %bitcast.1.me_ref, s32[1,8]{1,0:T(1,128)S(1)} %copy-done.8, s32[32,512]{1,0:T(8,128)S(1)} %copy-done.3, f32[32,512]{1,0:T(8,128)S(1)} %copy-done.4, s32[1,512]{1,0:T(1,128)S(1)} %bitcast.11, s32[1,4096]{1,0:T(1,128)S(1)} %copy-done.2, ...), custom_call_target="tpu_custom_call" | custom-call | flops 1048576 | bytes 65536 | tf_op jit(solution)/shard_map/render/pallas_call | solution.py:146
  25.2 4.5 %collective-permute-done.2.refs_2_ = bf16[2,64,1024]{2,1,0:T(8,128)(2,1)S(1)} collective-permute-done((bf16[2,64,1024]{2,1,0:T(8,128)(2,1)S(1)}, bf16[2,64,1024]{2,1,0:T(8,128)(2,1)S(1)}, u32[]{:S(2)}, u32[]{:S(2)}) %collective-permute-start.2) | collective-permute-done | bytes 262176 | tf_op jit(solution)/shard_map/ppermute | solution.py:982
  33.3 1.7 %collective-permute-done.6.refs_1_ = bf16[4,64,1024]{2,1,0:T(8,128)(2,1)S(1)} collective-permute-done((bf16[4,64,1024]{2,1,0:T(8,128)(2,1)S(1)}, bf16[4,64,1024]{2,1,0:T(8,128)(2,1)S(1)}, u32[]{:S(2)}, u32[]{:S(2)}) %collective-permute-start.6) | collective-permute-done | bytes 524320 | tf_op jit(solution)/shard_map/ppermute | solution.py:978
  39.1 3.2 %tokens.1 = (bf16[512,1024]{1,0:T(8,128)(2,1)S(1)}, bf16[512,1024]{1,0:T(8,128)(2,1)S(1)}, bf16[1024,512]{1,0:T(8,128)(2,1)S(1)}) custom-call(s32[1]{0:T(128)} %bitcast.1.me_ref, s32[1,8]{1,0:T(1,128)S(1)} %copy-done.9, s32[1,4096]{1,0:T(1,128)S(1)} %copy-done.2, bf16[512,1024]{1,0:T(8,128)(2,1)S(1)} %copy-done.1, f32[1,1024]{1,0:T(1,128)S(1)} %bitcast.8, ...), custom_call_target="tpu_custom_call" | custom-call | flops 1048576 | bytes 65536 | tf_op jit(solution)/shard_map/tokens/pallas_call | solution.py:232
  42.3 2.3 %forward.3 = (bf16[2,6,64,512]{3,2,1,0:T(8,128)(2,1)S(1)}, f32[2,6,64,512]{3,2,1,0:T(8,128)S(1)}, f32[512,1024]{1,0:T(8,128)S(1)}) custom-call(bf16[1024,512]{1,0:T(8,128)(2,1)S(1)} %get-tuple-element.64.refs_0_, bf16[6,2,64,1024]{3,2,1,0:T(8,128)(2,1)S(1)} %get-tuple-element.60.refs_1_.refs_0_, ...), custom_call_target="tpu_custom_call" | custom-call | flops 1048576 | bytes 65536 | tf_op jit(solution)/shard_map/forward/pallas_call | solution.py:620
  44.8 4.2 %collective-permute-done.8.refs_2_.refs_9_ = bf16[2,64,1024]{2,1,0:T(8,128)(2,1)S(1)} collective-permute-done((bf16[2,64,1024]{2,1,0:T(8,128)(2,1)S(1)}, bf16[2,64,1024]{2,1,0:T(8,128)(2,1)S(1)}, u32[]{:S(2)}, u32[]{:S(2)}) %collective-permute-start.8) | collective-permute-done | bytes 262176 | tf_op jit(solution)/shard_map/ppermute | solution.py:982
  49.0 9.7 %collective-permute-done.9.refs_3_.refs_10_ = bf16[2,64,1024]{2,1,0:T(8,128)(2,1)S(1)} collective-permute-done((bf16[2,64,1024]{2,1,0:T(8,128)(2,1)S(1)}, bf16[2,64,1024]{2,1,0:T(8,128)(2,1)S(1)}, u32[]{:S(2)}, u32[]{:S(2)}) %collective-permute-start.9) | collective-permute-done | bytes 262176 | tf_op jit(solution)/shard_map/ppermute | solution.py:982
  62.1 2.3 %forward.4 = (bf16[2,6,64,512]{3,2,1,0:T(8,128)(2,1)S(1)}, f32[2,6,64,512]{3,2,1,0:T(8,128)S(1)}, f32[512,1024]{1,0:T(8,128)S(1)}) custom-call(bf16[1024,512]{1,0:T(8,128)(2,1)S(1)} %get-tuple-element.64.refs_0_, bf16[3,2,64,1024]{3,2,1,0:T(8,128)(2,1)S(1)} %tie.4.x_far_ref.refs_1_, bf16[3,2,64,1024]{3,2,1,0:T(8,128)(2,1)S(1)} %tie.5.y_far_ref.refs_2_, ...), custom_call_target="tpu_custom_call" | custom-call | flops 1048576 | bytes 65536 | tf_op jit(solution)/shard_map/forward/pallas_call | solution.py:620
  64.4 8.8 %collective-permute-done.15.refs_0_ = bf16[2,2,64,1024]{3,2,1,0:T(8,128)(2,1)S(1)} collective-permute-done((bf16[2,2,64,1024]{3,2,1,0:T(8,128)(2,1)S(1)}, bf16[2,2,64,1024]{3,2,1,0:T(8,128)(2,1)S(1)}, u32[]{:S(2)}, u32[]{:S(2)}) %collective-permute-start.15) | collective-permute-done | bytes 524320 | tf_op jit(solution)/shard_map/ppermute | solution.py:975
  75.9 3.0 %forward.5 = (bf16[2,4,64,512]{3,2,1,0:T(8,128)(2,1)S(1)}, f32[2,4,64,512]{3,2,1,0:T(8,128)S(1)}, bf16[512,1024]{1,0:T(8,128)(2,1)S(1)}, bf16[1024,512]{1,0:T(8,128)(2,1)S(1)}, f32[8,1024]{1,0:T(8,128)S(1)}) custom-call(bf16[1024,512]{1,0:T(8,128)(2,1)S(1)} %get-tuple-element.64.refs_0_, bf16[2,2,64,1024]{3,2,1,0:T(8,128)(2,1)S(1)} %tie.6.refs_1_.refs_3_, ...), custom_call_target="tpu_custom_call" | custom-call | flops 1048576 | bytes 65536 | tf_op jit(solution)/shard_map/forward/pallas_call | solution.py:620
  80.3 2.7 %up_gradient.2 = (bf16[4,4,64,1024]{3,2,1,0:T(8,128)(2,1)S(1)}, f32[1,1024]{1,0:T(1,128)S(1)}) custom-call(bf16[6,2,64,1024]{3,2,1,0:T(8,128)(2,1)S(1)} %collective-permute-done.7.refs_2_.refs_0_, bf16[3,2,64,1024]{3,2,1,0:T(8,128)(2,1)S(1)} %collective-permute-done.13.refs_3_.refs_1_, bf16[3,2,64,1024]{3,2,1,0:T(8,128)(2,1)S(1)} %collective-permute-done.14.refs_4_.refs_2_, ...), custom_call_target="tpu_custom_call" | custom-call | flops 1048576 | bytes 65536 | tf_op jit(solution)/shard_map/up_gradient/pallas_call | solution.py:825
  88.2 3.1 %up_gradient.3 = (bf16[4,64,1024]{2,1,0:T(8,128)(2,1)S(1)}, bf16[4,64,1024]{2,1,0:T(8,128)(2,1)S(1)}, bf16[4,64,1024]{2,1,0:T(8,128)(2,1)S(1)}, bf16[2,64,1024]{...) custom-call(bf16[6,2,64,1024]{3,2,1,0:T(8,128)(2,1)S(1)} %get-tuple-element.60.refs_1_.refs_0_, ...), custom_call_target="tpu_custom_call" | custom-call | flops 1048576 | bytes 65536 | tf_op jit(solution)/shard_map/up_gradient/pallas_call | solution.py:825
  94.3 3.8 %collective-permute-start.22 = (f32[8,1024]{1,0:T(8,128)S(1)}, f32[8,1024]{1,0:T(8,128)S(1)}, u32[]{:S(2)}, u32[]{:S(2)}) collective-permute-start(f32[8,1024]{1,0:T(8,128)S(1)} %add.9), channel_id=1, source_target_pairs={{0,2},{1,3},{2,0},{3,1},{4,6},{5,7},{6,4},{7,5},{8,10},{9,11},{10,... | collective-permute-start | bytes 98312 | tf_op jit(solution)/shard_map/ppermute | solution.py:978
  98.1 1.9 %collective-permute-done.22 = f32[8,1024]{1,0:T(8,128)S(1)} collective-permute-done((f32[8,1024]{1,0:T(8,128)S(1)}, f32[8,1024]{1,0:T(8,128)S(1)}, u32[]{:S(2)}, u32[]{:S(2)}) %collective-permute-start.22) | collective-permute-done | bytes 32800 | tf_op jit(solution)/shard_map/ppermute | solution.py:978
  100.0 1.6 collective-permute-start.23
  101.6 3.2 %collective-permute-done.23 = f32[8,1024]{1,0:T(8,128)S(1)} collective-permute-done((f32[8,1024]{1,0:T(8,128)S(1)}, f32[8,1024]{1,0:T(8,128)S(1)}, u32[]{:S(2)}, u32[]{:S(2)}) %collective-permute-start.23) | collective-permute-done | bytes 32800 | tf_op jit(solution)/shard_map/ppermute | solution.py:978
  107.4 4.3 %collective-permute-done.19.x_ref = bf16[4,64,1024]{2,1,0:T(8,128)(2,1)S(1)} collective-permute-done((bf16[4,64,1024]{2,1,0:T(8,128)(2,1)S(1)}, bf16[4,64,1024]{2,1,0:T(8,128)(2,1)S(1)}, u32[]{:S(2)}, u32[]{:S(2)}) %collective-permute-start.19) | collective-permute-done | bytes 524320 | tf_op jit(solution)/shard_map/ppermute | solution.py:975
  115.0 2.4 %collective-permute-done.32.x_late_ref = bf16[2,64,1024]{2,1,0:T(8,128)(2,1)S(1)} collective-permute-done((bf16[2,64,1024]{2,1,0:T(8,128)(2,1)S(1)}, bf16[2,64,1024]{2,1,0:T(8,128)(2,1)S(1)}, u32[]{:S(2)}, u32[]{:S(2)}) %collective-permute-start.32) | collective-permute-done | bytes 262176 | tf_op jit(solution)/shard_map/ppermute | solution.py:975
  119.1 1.9 %collective-permute-start.34 = (bf16[64,1024]{1,0:T(8,128)(2,1)S(1)}, bf16[64,1024]{1,0:T(8,128)(2,1)S(1)}, u32[]{:S(2)}, u32[]{:S(2)}) collective-permute-start(bf16[64,1024]{1,0:T(8,128)(2,1)S(1)} %get-tuple-element.105), channel_id=1, source_target_pairs={{0,2},{1,3},{2,4},{3,5},{4,6},{5,7},{6,0},{7,1},{8,10},{9,11},{10,... | collective-permute-start | bytes 393224 | tf_op jit(solution)/shard_map/ppermute | solution.py:982
  121.0 4.3 %collective-permute-start.35 = (bf16[64,1024]{1,0:T(8,128)(2,1)S(1)}, bf16[64,1024]{1,0:T(8,128)(2,1)S(1)}, u32[]{:S(2)}, u32[]{:S(2)}) collective-permute-start(bf16[64,1024]{1,0:T(8,128)(2,1)S(1)} %get-tuple-element.106), channel_id=1, source_target_pairs={{0,4},{1,5},{2,6},{3,7},{4,0},{5,1},{6,2},{7,3},{8,12},{9,13},{10,... | collective-permute-start | bytes 393224 | tf_op jit(solution)/shard_map/ppermute | solution.py:982
  125.5 2.1 %collective-permute-start.26 = (bf16[64,1024]{1,0:T(8,128)(2,1)S(1)}, bf16[64,1024]{1,0:T(8,128)(2,1)S(1)}, u32[]{:S(2)}, u32[]{:S(2)}) collective-permute-start(bf16[64,1024]{1,0:T(8,128)(2,1)S(1)} %get-tuple-element.90), channel_id=1, source_target_pairs={{0,2},{1,3},{2,4},{3,5},{4,6},{5,7},{6,0},{7,1},{8,10},{9,11},{10,... | collective-permute-start | bytes 393224 | tf_op jit(solution)/shard_map/ppermute | solution.py:982
  127.6 2.2 %collective-permute-start.27 = (bf16[64,1024]{1,0:T(8,128)(2,1)S(1)}, bf16[64,1024]{1,0:T(8,128)(2,1)S(1)}, u32[]{:S(2)}, u32[]{:S(2)}) collective-permute-start(bf16[64,1024]{1,0:T(8,128)(2,1)S(1)} %get-tuple-element.91), channel_id=1, source_target_pairs={{0,4},{1,5},{2,6},{3,7},{4,0},{5,1},{6,2},{7,3},{8,12},{9,13},{10,... | collective-permute-start | bytes 393224 | tf_op jit(solution)/shard_map/ppermute | solution.py:982
  130.9 7.9 %collective-permute-done.35.refs_2_ = bf16[64,1024]{1,0:T(8,128)(2,1)S(1)} collective-permute-done((bf16[64,1024]{1,0:T(8,128)(2,1)S(1)}, bf16[64,1024]{1,0:T(8,128)(2,1)S(1)}, u32[]{:S(2)}, u32[]{:S(2)}) %collective-permute-start.35) | collective-permute-done | bytes 131104 | tf_op jit(solution)/shard_map/ppermute | solution.py:982
  138.8 1.9 %collective-permute-done.36.refs_3_ = bf16[64,1024]{1,0:T(8,128)(2,1)S(1)} collective-permute-done((bf16[64,1024]{1,0:T(8,128)(2,1)S(1)}, bf16[64,1024]{1,0:T(8,128)(2,1)S(1)}, u32[]{:S(2)}, u32[]{:S(2)}) %collective-permute-start.36) | collective-permute-done | bytes 131104 | tf_op jit(solution)/shard_map/ppermute | solution.py:982
  143.1 2.3 %collective-permute-done.28.refs_3_ = bf16[64,1024]{1,0:T(8,128)(2,1)S(1)} collective-permute-done((bf16[64,1024]{1,0:T(8,128)(2,1)S(1)}, bf16[64,1024]{1,0:T(8,128)(2,1)S(1)}, u32[]{:S(2)}, u32[]{:S(2)}) %collective-permute-start.28) | collective-permute-done | bytes 131104 | tf_op jit(solution)/shard_map/ppermute | solution.py:982
  147.1 1.9 %collective-permute-start.39 = (bf16[160,1024]{1,0:T(8,128)(2,1)S(1)}, bf16[160,1024]{1,0:T(8,128)(2,1)S(1)}, u32[]{:S(2)}, u32[]{:S(2)}) collective-permute-start(bf16[160,1024]{1,0:T(8,128)(2,1)S(1)} %collect.3.refs_0_), channel_id=1, source_target_pairs={{0,24},{8,16},{16,8},{24,0},{1,25},{9,17},{17,9},{25,1},{2,26},{10... | collective-permute-start | bytes 983048 | tf_op jit(solution)/shard_map/ppermute | solution.py:975
  149.0 7.2 %collective-permute-done.37.refs_1_ = bf16[160,1024]{1,0:T(8,128)(2,1)S(1)} collective-permute-done((bf16[160,1024]{1,0:T(8,128)(2,1)S(1)}, bf16[160,1024]{1,0:T(8,128)(2,1)S(1)}, u32[]{:S(2)}, u32[]{:S(2)}) %collective-permute-start.37) | collective-permute-done | bytes 327712 | tf_op jit(solution)/shard_map/ppermute | solution.py:975
  156.4 5.3 %collective-permute-done.39.refs_3_ = bf16[160,1024]{1,0:T(8,128)(2,1)S(1)} collective-permute-done((bf16[160,1024]{1,0:T(8,128)(2,1)S(1)}, bf16[160,1024]{1,0:T(8,128)(2,1)S(1)}, u32[]{:S(2)}, u32[]{:S(2)}) %collective-permute-start.39) | collective-permute-done | bytes 327712 | tf_op jit(solution)/shard_map/ppermute | solution.py:975
  161.7 1.7 %place.1 = (f32[1024,256]{1,0:T(8,128)}, f32[256,1024]{1,0:T(8,128)}, f32[1,1024]{1,0:T(1,128)}, f32[1,1024]{1,0:T(1,128)}, f32[1,1]{1,0:T(1,128)}) custom-call(s32[1]{0:T(128)} %bitcast.group_ref, bf16[160,1024]{1,0:T(8,128)(2,1)S(1)} %collect.3.refs_0_, bf16[160,1024]{1,0:T(8,128)(2,1)S(1)} %collective-permute-done.37.refs_1_, ...), custom_call_target="tpu_custom_call" | custom-call | flops 1048576 | bytes 65536 | tf_op jit(solution)/shard_map/place/pallas_call | solution.py:941
  (100 shorter events, 42.8 us)
Async XLA Ops:
  3.1 21.7 %collective-permute-start.4 = (bf16[2,64,1024]{2,1,0:T(8,128)(2,1)S(1)}, bf16[2,64,1024]{2,1,0:T(8,128)(2,1)S(1)}, u32[]{:S(2)}, u32[]{:S(2)}) collective-permute-start(bf16[2,64,1024]{2,1,0:T(8,128)(2,1)S(1)} %quarter.1.mine_ref), channel_id=1, source_target_pairs={{0,16},{8,24},{16,0},{24,8},{1,17},{9,25},{17,1},{25,9},{2,18},{10... | collective-permute-start | bytes 786440 | tf_op jit(solution)/shard_map/ppermute | solution.py:975
  4.7 20.5 %collective-permute-start = (bf16[2,64,1024]{2,1,0:T(8,128)(2,1)S(1)}, bf16[2,64,1024]{2,1,0:T(8,128)(2,1)S(1)}, u32[]{:S(2)}, u32[]{:S(2)}) collective-permute-start(bf16[2,64,1024]{2,1,0:T(8,128)(2,1)S(1)} %quarter.1.mine_ref), channel_id=1, source_target_pairs={{0,6},{1,7},{2,0},{3,1},{4,2},{5,3},{6,4},{7,5},{8,14},{9,15},{10,... | collective-permute-start | bytes 786440 | tf_op jit(solution)/shard_map/ppermute | solution.py:982
  5.2 20.0 %collective-permute-start.1 = (bf16[2,64,1024]{2,1,0:T(8,128)(2,1)S(1)}, bf16[2,64,1024]{2,1,0:T(8,128)(2,1)S(1)}, u32[]{:S(2)}, u32[]{:S(2)}) collective-permute-start(bf16[2,64,1024]{2,1,0:T(8,128)(2,1)S(1)} %quarter.1.mine_ref), channel_id=1, source_target_pairs={{0,4},{1,5},{2,6},{3,7},{4,0},{5,1},{6,2},{7,3},{8,12},{9,13},{10,... | collective-permute-start | bytes 786440 | tf_op jit(solution)/shard_map/ppermute | solution.py:982
  7.7 21.9 %collective-permute-start.2 = (bf16[2,64,1024]{2,1,0:T(8,128)(2,1)S(1)}, bf16[2,64,1024]{2,1,0:T(8,128)(2,1)S(1)}, u32[]{:S(2)}, u32[]{:S(2)}) collective-permute-start(bf16[2,64,1024]{2,1,0:T(8,128)(2,1)S(1)} %quarter.1.mine_ref), channel_id=1, source_target_pairs={{0,2},{1,3},{2,4},{3,5},{4,6},{5,7},{6,0},{7,1},{8,10},{9,11},{10,... | collective-permute-start | bytes 786440 | tf_op jit(solution)/shard_map/ppermute | solution.py:982
  10.2 19.4 %collective-permute-start.3 = (bf16[2,64,1024]{2,1,0:T(8,128)(2,1)S(1)}, bf16[2,64,1024]{2,1,0:T(8,128)(2,1)}, u32[]{:S(2)}, u32[]{:S(2)}) collective-permute-start(bf16[2,64,1024]{2,1,0:T(8,128)(2,1)S(1)} %quarter.1.mine_ref), channel_id=1, source_target_pairs={{0,8},{8,0},{16,24},{24,16},{1,9},{9,1},{17,25},{25,17},{2,10},{10... | collective-permute-start | bytes 786440 | tf_op jit(solution)/shard_map/ppermute | solution.py:975
  30.8 6.9 %collective-permute-start.7 = (bf16[6,2,64,1024]{3,2,1,0:T(8,128)(2,1)S(1)}, bf16[6,2,64,1024]{3,2,1,0:T(8,128)(2,1)S(1)}, u32[]{:S(2)}, u32[]{:S(2)}) collective-permute-start(bf16[6,2,64,1024]{3,2,1,0:T(8,128)(2,1)S(1)} %get-tuple-element.60.refs_1_.refs_0_), channel_id=1, source_target_pairs={{0,1},{1,0},{2,3},{3,2},{4,5},{5,4},{6,7},{7,6},{8,9},{9,8},{10,11... | collective-permute-start | bytes 4718600 | tf_op jit(solution)/shard_map/ppermute | solution.py:978
  31.3 27.4 %collective-permute-start.11 = (bf16[3,2,64,1024]{3,2,1,0:T(8,128)(2,1)S(1)}, bf16[3,2,64,1024]{3,2,1,0:T(8,128)(2,1)S(1)}, u32[]{:S(2)}, u32[]{:S(2)}) collective-permute-start(bf16[3,2,64,1024]{3,2,1,0:T(8,128)(2,1)S(1)} %get-tuple-element.61), channel_id=1, source_target_pairs={{0,16},{8,24},{16,0},{24,8},{1,17},{9,25},{17,1},{25,9},{2,18},{10... | collective-permute-start | bytes 2359304 | tf_op jit(solution)/shard_map/ppermute | solution.py:975
  31.8 26.9 %collective-permute-start.5 = (bf16[3,2,64,1024]{3,2,1,0:T(8,128)(2,1)S(1)}, bf16[3,2,64,1024]{3,2,1,0:T(8,128)(2,1)S(1)}, u32[]{:S(2)}, u32[]{:S(2)}) collective-permute-start(bf16[3,2,64,1024]{3,2,1,0:T(8,128)(2,1)S(1)} %get-tuple-element.61), channel_id=1, source_target_pairs={{0,8},{8,0},{16,24},{24,16},{1,9},{9,1},{17,25},{25,17},{2,10},{10... | collective-permute-start | bytes 2359304 | tf_op jit(solution)/shard_map/ppermute | solution.py:975
  35.1 9.7 %collective-permute-start.10 = (bf16[2,64,1024]{2,1,0:T(8,128)(2,1)S(1)}, bf16[2,64,1024]{2,1,0:T(8,128)(2,1)S(1)}, u32[]{:S(2)}, u32[]{:S(2)}) collective-permute-start(bf16[2,64,1024]{2,1,0:T(8,128)(2,1)S(1)} %get-tuple-element.68), channel_id=1, source_target_pairs={{0,6},{1,7},{2,0},{3,1},{4,2},{5,3},{6,4},{7,5},{8,14},{9,15},{10,... | collective-permute-start | bytes 786440 | tf_op jit(solution)/shard_map/ppermute | solution.py:982
  36.3 12.8 %collective-permute-start.8 = (bf16[2,64,1024]{2,1,0:T(8,128)(2,1)S(1)}, bf16[2,64,1024]{2,1,0:T(8,128)(2,1)S(1)}, u32[]{:S(2)}, u32[]{:S(2)}) collective-permute-start(bf16[2,64,1024]{2,1,0:T(8,128)(2,1)S(1)} %get-tuple-element.66), channel_id=1, source_target_pairs={{0,2},{1,3},{2,4},{3,5},{4,6},{5,7},{6,0},{7,1},{8,10},{9,11},{10,... | collective-permute-start | bytes 786440 | tf_op jit(solution)/shard_map/ppermute | solution.py:982
  37.7 21.0 %collective-permute-start.9 = (bf16[2,64,1024]{2,1,0:T(8,128)(2,1)S(1)}, bf16[2,64,1024]{2,1,0:T(8,128)(2,1)S(1)}, u32[]{:S(2)}, u32[]{:S(2)}) collective-permute-start(bf16[2,64,1024]{2,1,0:T(8,128)(2,1)S(1)} %get-tuple-element.67), channel_id=1, source_target_pairs={{0,4},{1,5},{2,6},{3,7},{4,0},{5,1},{6,2},{7,3},{8,12},{9,13},{10,... | collective-permute-start | bytes 786440 | tf_op jit(solution)/shard_map/ppermute | solution.py:982
  59.3 14.0 %collective-permute-start.15 = (bf16[2,2,64,1024]{3,2,1,0:T(8,128)(2,1)S(1)}, bf16[2,2,64,1024]{3,2,1,0:T(8,128)(2,1)S(1)}, u32[]{:S(2)}, u32[]{:S(2)}) collective-permute-start(bf16[2,2,64,1024]{3,2,1,0:T(8,128)(2,1)S(1)} %get-tuple-element.71), channel_id=1, source_target_pairs={{0,16},{8,24},{16,0},{24,8},{1,17},{9,25},{17,1},{25,9},{2,18},{10... | collective-permute-start | bytes 1572872 | tf_op jit(solution)/shard_map/ppermute | solution.py:975
  59.9 13.6 %collective-permute-start.12 = (bf16[2,2,64,1024]{3,2,1,0:T(8,128)(2,1)S(1)}, bf16[2,2,64,1024]{3,2,1,0:T(8,128)(2,1)S(1)}, u32[]{:S(2)}, u32[]{:S(2)}) collective-permute-start(bf16[2,2,64,1024]{3,2,1,0:T(8,128)(2,1)S(1)} %get-tuple-element.69), channel_id=1, source_target_pairs={{0,8},{8,0},{16,24},{24,16},{1,9},{9,1},{17,25},{25,17},{2,10},{10... | collective-permute-start | bytes 1572872 | tf_op jit(solution)/shard_map/ppermute | solution.py:975
  83.0 5.1 %collective-permute-start.18 = (bf16[4,4,64,1024]{3,2,1,0:T(8,128)(2,1)S(1)}, bf16[4,4,64,1024]{3,2,1,0:T(8,128)(2,1)S(1)}, u32[]{:S(2)}, u32[]{:S(2)}) collective-permute-start(bf16[4,4,64,1024]{3,2,1,0:T(8,128)(2,1)S(1)} %get-tuple-element.79), channel_id=1, source_target_pairs={{0,1},{1,0},{2,3},{3,2},{4,5},{5,4},{6,7},{7,6},{8,9},{9,8},{10,11... | collective-permute-start | bytes 6291464 | tf_op jit(solution)/shard_map/ppermute | solution.py:978
  85.6 19.2 %collective-permute-start.30 = (bf16[4,64,1024]{2,1,0:T(8,128)(2,1)S(1)}, bf16[4,64,1024]{2,1,0:T(8,128)(2,1)S(1)}, u32[]{:S(2)}, u32[]{:S(2)}) collective-permute-start(bf16[4,64,1024]{2,1,0:T(8,128)(2,1)S(1)} %get-tuple-element.98), channel_id=1, source_target_pairs={{0,8},{8,0},{16,24},{24,16},{1,9},{9,1},{17,25},{25,17},{2,10},{10... | collective-permute-start | bytes 1572872 | tf_op jit(solution)/shard_map/ppermute | solution.py:975
  87.2 17.6 %collective-permute-start.31 = (bf16[4,64,1024]{2,1,0:T(8,128)(2,1)S(1)}, bf16[4,64,1024]{2,1,0:T(8,128)(2,1)S(1)}, u32[]{:S(2)}, u32[]{:S(2)}) collective-permute-start(bf16[4,64,1024]{2,1,0:T(8,128)(2,1)S(1)} %get-tuple-element.99), channel_id=1, source_target_pairs={{0,16},{8,24},{16,0},{24,8},{1,17},{9,25},{17,1},{25,9},{2,18},{10... | collective-permute-start | bytes 1572872 | tf_op jit(solution)/shard_map/ppermute | solution.py:975
  91.3 20.4 %collective-permute-start.19 = (bf16[4,64,1024]{2,1,0:T(8,128)(2,1)S(1)}, bf16[4,64,1024]{2,1,0:T(8,128)(2,1)S(1)}, u32[]{:S(2)}, u32[]{:S(2)}) collective-permute-start(bf16[4,64,1024]{2,1,0:T(8,128)(2,1)S(1)} %get-tuple-element.82), channel_id=1, source_target_pairs={{0,8},{8,0},{16,24},{24,16},{1,9},{9,1},{17,25},{25,17},{2,10},{10... | collective-permute-start | bytes 1572872 | tf_op jit(solution)/shard_map/ppermute | solution.py:975
  92.1 21.2 %collective-permute-start.20 = (bf16[4,64,1024]{2,1,0:T(8,128)(2,1)S(1)}, bf16[4,64,1024]{2,1,0:T(8,128)(2,1)S(1)}, u32[]{:S(2)}, u32[]{:S(2)}) collective-permute-start(bf16[4,64,1024]{2,1,0:T(8,128)(2,1)S(1)} %get-tuple-element.83), channel_id=1, source_target_pairs={{0,16},{8,24},{16,0},{24,8},{1,17},{9,25},{17,1},{25,9},{2,18},{10... | collective-permute-start | bytes 1572872 | tf_op jit(solution)/shard_map/ppermute | solution.py:975
  94.3 5.7 %collective-permute-start.22 = (f32[8,1024]{1,0:T(8,128)S(1)}, f32[8,1024]{1,0:T(8,128)S(1)}, u32[]{:S(2)}, u32[]{:S(2)}) collective-permute-start(f32[8,1024]{1,0:T(8,128)S(1)} %add.9), channel_id=1, source_target_pairs={{0,2},{1,3},{2,0},{3,1},{4,6},{5,7},{6,4},{7,5},{8,10},{9,11},{10,... | collective-permute-start | bytes 98312 | tf_op jit(solution)/shard_map/ppermute | solution.py:978
  105.0 12.4 %collective-permute-start.32 = (bf16[2,64,1024]{2,1,0:T(8,128)(2,1)S(1)}, bf16[2,64,1024]{2,1,0:T(8,128)(2,1)S(1)}, u32[]{:S(2)}, u32[]{:S(2)}) collective-permute-start(bf16[2,64,1024]{2,1,0:T(8,128)(2,1)S(1)} %get-tuple-element.102), channel_id=1, source_target_pairs={{0,8},{8,0},{16,24},{24,16},{1,9},{9,1},{17,25},{25,17},{2,10},{10... | collective-permute-start | bytes 786440 | tf_op jit(solution)/shard_map/ppermute | solution.py:975
  106.4 12.4 %collective-permute-start.33 = (bf16[2,64,1024]{2,1,0:T(8,128)(2,1)S(1)}, bf16[2,64,1024]{2,1,0:T(8,128)(2,1)S(1)}, u32[]{:S(2)}, u32[]{:S(2)}) collective-permute-start(bf16[2,64,1024]{2,1,0:T(8,128)(2,1)S(1)} %get-tuple-element.103), channel_id=1, source_target_pairs={{0,16},{8,24},{16,0},{24,8},{1,17},{9,25},{17,1},{25,9},{2,18},{10... | collective-permute-start | bytes 786440 | tf_op jit(solution)/shard_map/ppermute | solution.py:975
  113.4 11.9 %collective-permute-start.24 = (bf16[2,64,1024]{2,1,0:T(8,128)(2,1)S(1)}, bf16[2,64,1024]{2,1,0:T(8,128)(2,1)S(1)}, u32[]{:S(2)}, u32[]{:S(2)}) collective-permute-start(bf16[2,64,1024]{2,1,0:T(8,128)(2,1)S(1)} %get-tuple-element.87), channel_id=1, source_target_pairs={{0,8},{8,0},{16,24},{24,16},{1,9},{9,1},{17,25},{25,17},{2,10},{10... | collective-permute-start | bytes 786440 | tf_op jit(solution)/shard_map/ppermute | solution.py:975
  114.0 11.3 %collective-permute-start.25 = (bf16[2,64,1024]{2,1,0:T(8,128)(2,1)S(1)}, bf16[2,64,1024]{2,1,0:T(8,128)(2,1)S(1)}, u32[]{:S(2)}, u32[]{:S(2)}) collective-permute-start(bf16[2,64,1024]{2,1,0:T(8,128)(2,1)S(1)} %get-tuple-element.88), channel_id=1, source_target_pairs={{0,16},{8,24},{16,0},{24,8},{1,17},{9,25},{17,1},{25,9},{2,18},{10... | collective-permute-start | bytes 786440 | tf_op jit(solution)/shard_map/ppermute | solution.py:975
  119.1 10.7 %collective-permute-start.34 = (bf16[64,1024]{1,0:T(8,128)(2,1)S(1)}, bf16[64,1024]{1,0:T(8,128)(2,1)S(1)}, u32[]{:S(2)}, u32[]{:S(2)}) collective-permute-start(bf16[64,1024]{1,0:T(8,128)(2,1)S(1)} %get-tuple-element.105), channel_id=1, source_target_pairs={{0,2},{1,3},{2,4},{3,5},{4,6},{5,7},{6,0},{7,1},{8,10},{9,11},{10,... | collective-permute-start | bytes 393224 | tf_op jit(solution)/shard_map/ppermute | solution.py:982
  121.0 17.8 %collective-permute-start.35 = (bf16[64,1024]{1,0:T(8,128)(2,1)S(1)}, bf16[64,1024]{1,0:T(8,128)(2,1)S(1)}, u32[]{:S(2)}, u32[]{:S(2)}) collective-permute-start(bf16[64,1024]{1,0:T(8,128)(2,1)S(1)} %get-tuple-element.106), channel_id=1, source_target_pairs={{0,4},{1,5},{2,6},{3,7},{4,0},{5,1},{6,2},{7,3},{8,12},{9,13},{10,... | collective-permute-start | bytes 393224 | tf_op jit(solution)/shard_map/ppermute | solution.py:982
  125.3 15.5 %collective-permute-start.36 = (bf16[64,1024]{1,0:T(8,128)(2,1)S(1)}, bf16[64,1024]{1,0:T(8,128)(2,1)S(1)}, u32[]{:S(2)}, u32[]{:S(2)}) collective-permute-start(bf16[64,1024]{1,0:T(8,128)(2,1)S(1)} %get-tuple-element.107), channel_id=1, source_target_pairs={{0,6},{1,7},{2,0},{3,1},{4,2},{5,3},{6,4},{7,5},{8,14},{9,15},{10,... | collective-permute-start | bytes 393224 | tf_op jit(solution)/shard_map/ppermute | solution.py:982
  125.5 16.1 %collective-permute-start.26 = (bf16[64,1024]{1,0:T(8,128)(2,1)S(1)}, bf16[64,1024]{1,0:T(8,128)(2,1)S(1)}, u32[]{:S(2)}, u32[]{:S(2)}) collective-permute-start(bf16[64,1024]{1,0:T(8,128)(2,1)S(1)} %get-tuple-element.90), channel_id=1, source_target_pairs={{0,2},{1,3},{2,4},{3,5},{4,6},{5,7},{6,0},{7,1},{8,10},{9,11},{10,... | collective-permute-start | bytes 393224 | tf_op jit(solution)/shard_map/ppermute | solution.py:982
  127.6 15.5 %collective-permute-start.27 = (bf16[64,1024]{1,0:T(8,128)(2,1)S(1)}, bf16[64,1024]{1,0:T(8,128)(2,1)S(1)}, u32[]{:S(2)}, u32[]{:S(2)}) collective-permute-start(bf16[64,1024]{1,0:T(8,128)(2,1)S(1)} %get-tuple-element.91), channel_id=1, source_target_pairs={{0,4},{1,5},{2,6},{3,7},{4,0},{5,1},{6,2},{7,3},{8,12},{9,13},{10,... | collective-permute-start | bytes 393224 | tf_op jit(solution)/shard_map/ppermute | solution.py:982
  129.8 15.6 %collective-permute-start.28 = (bf16[64,1024]{1,0:T(8,128)(2,1)S(1)}, bf16[64,1024]{1,0:T(8,128)(2,1)S(1)}, u32[]{:S(2)}, u32[]{:S(2)}) collective-permute-start(bf16[64,1024]{1,0:T(8,128)(2,1)S(1)} %get-tuple-element.92), channel_id=1, source_target_pairs={{0,6},{1,7},{2,0},{3,1},{4,2},{5,3},{6,4},{7,5},{8,14},{9,15},{10,... | collective-permute-start | bytes 393224 | tf_op jit(solution)/shard_map/ppermute | solution.py:982
  145.5 10.7 %collective-permute-start.37 = (bf16[160,1024]{1,0:T(8,128)(2,1)S(1)}, bf16[160,1024]{1,0:T(8,128)(2,1)S(1)}, u32[]{:S(2)}, u32[]{:S(2)}) collective-permute-start(bf16[160,1024]{1,0:T(8,128)(2,1)S(1)} %collect.3.refs_0_), channel_id=1, source_target_pairs={{0,8},{8,0},{16,24},{24,16},{1,9},{9,1},{17,25},{25,17},{2,10},{10... | collective-permute-start | bytes 983048 | tf_op jit(solution)/shard_map/ppermute | solution.py:975
  146.1 10.3 %collective-permute-start.38 = (bf16[160,1024]{1,0:T(8,128)(2,1)S(1)}, bf16[160,1024]{1,0:T(8,128)(2,1)S(1)}, u32[]{:S(2)}, u32[]{:S(2)}) collective-permute-start(bf16[160,1024]{1,0:T(8,128)(2,1)S(1)} %collect.3.refs_0_), channel_id=1, source_target_pairs={{0,16},{8,24},{16,0},{24,8},{1,17},{9,25},{17,1},{25,9},{2,18},{10... | collective-permute-start | bytes 983048 | tf_op jit(solution)/shard_map/ppermute | solution.py:975
  147.1 14.6 %collective-permute-start.39 = (bf16[160,1024]{1,0:T(8,128)(2,1)S(1)}, bf16[160,1024]{1,0:T(8,128)(2,1)S(1)}, u32[]{:S(2)}, u32[]{:S(2)}) collective-permute-start(bf16[160,1024]{1,0:T(8,128)(2,1)S(1)} %collect.3.refs_0_), channel_id=1, source_target_pairs={{0,24},{8,16},{16,8},{24,0},{1,25},{9,17},{17,9},{25,1},{2,26},{10... | collective-permute-start | bytes 983048 | tf_op jit(solution)/shard_map/ppermute | solution.py:975
  (20 other events, 109.7 us)

commit v7 on v6

--- a/solution.py
+++ b/solution.py
@@ -538,9 +538,9 @@
     return upstream, 1.0 - cosine
 
 
-def forward_kernel(first, blocks, sides, *refs):
+def forward_kernel(first, blocks, sides, skipped, *refs):
     last = blocks > 0
-    refs = list(refs)
+    refs = list(refs[skipped:])
     normed_t_ref = refs.pop(0)
     own, other = refs[:sides], refs[sides:2 * sides]
     del refs[:2 * sides]
@@ -594,13 +594,13 @@
         small_ref[1:2, :] += jnp.broadcast_to(jnp.sum(loss, axis=0, keepdims=True), (1, width))
 
 
-def forward(normed_t, own, other, mixed=None, finish=None):
+def forward(normed_t, own, other, mixed=None, finish=None, after=()):
     width, rows = normed_t.shape
     part = own[0].shape[2]
     total = sum(array.shape[0] for array in own)
     first, last = mixed is None, finish is not None
     blocks = len(finish) - 2 if last else 0
-    operands = [normed_t, *own, *other]
+    operands = [*after, normed_t, *own, *other]
     if not first:
         operands.append(mixed)
     if last:
@@ -618,9 +618,9 @@
     else:
         shapes += [jax.ShapeDtypeStruct((rows, width), F32)]
     return pl.pallas_call(
-        functools.partial(forward_kernel, first, blocks, len(own)),
+        functools.partial(forward_kernel, first, blocks, len(own), len(after)),
         out_shape=tuple(shapes),
-        in_specs=[VMEM] * len(operands),
+        in_specs=[ANY] * len(after) + [VMEM] * (len(operands) - len(after)),
         out_specs=tuple([VMEM] * len(shapes)),
         scratch_shapes=scratch,
         compiler_params=params(24),
@@ -629,58 +629,46 @@
     )(*operands)
 
 
-def pack_kernel(mine_ref, *refs):
-    count = len(refs) - 5
-    arrivals, (x_ref, y_ref) = refs[:count], refs[count:count + 2]
-    all_ref, far_ref = refs[-2:]
-    for index, ref in enumerate((mine_ref, x_ref, y_ref)):
-        all_ref[index] = ref[...]
-    for index, ref in enumerate(arrivals):
-        block = ref[...]
-        all_ref[3 + index] = block
-        far_ref[index] = block
-
-
-def pack(mine, x, y, arrivals, after):
-    count = len(arrivals)
-    return pl.pallas_call(
-        pack_kernel,
+def pack_kernel(count, *refs):
+    out_ref = refs[-1]
+    for index, ref in enumerate(refs[:count]):
+        out_ref[index] = ref[...]
+
+
+def pack(pieces, *after):
+    return pl.pallas_call(
+        functools.partial(pack_kernel, len(pieces)),
+        out_shape=jax.ShapeDtypeStruct((len(pieces), *pieces[0].shape), BF16),
+        in_specs=[VMEM] * len(pieces) + [ANY] * len(after),
+        out_specs=VMEM,
+        compiler_params=params(16),
+        cost_estimate=COST,
+        name="pack",
+    )(*pieces, *after)
+
+
+def turn_kernel(y_ref, x_ref, *refs):
+    a_ref, b_ref = refs[-2:]
+    first = a_ref.shape[0]
+    a_ref[...] = y_ref[:first]
+    b_ref[...] = x_ref[first:]
+
+
+def turn(y, x, *after):
+    count = y.shape[0]
+    first = count // 2
+    return pl.pallas_call(
+        turn_kernel,
         out_shape=(
-            jax.ShapeDtypeStruct((3 + count, *mine.shape), BF16),
-            jax.ShapeDtypeStruct((count, *mine.shape), BF16),
+            jax.ShapeDtypeStruct((first, *y.shape[1:]), BF16),
+            jax.ShapeDtypeStruct((count - first, *y.shape[1:]), BF16),
         ),
-        in_specs=[VMEM] * (3 + count) + [ANY],
+        in_specs=[VMEM] * 2 + [ANY] * len(after),
         out_specs=(VMEM, VMEM),
         compiler_params=params(16),
         cost_estimate=COST,
-        name="pack",
-    )(mine, *arrivals, x, y, after)
-
-
-def turn_kernel(y_ref, y_far_ref, x_far_ref, after_ref, a_ref, b_ref):
-    held = a_ref.shape[0] - 1
-    a_ref[0] = y_ref[...]
-    for index in range(held):
-        a_ref[1 + index] = y_far_ref[index]
-    for index in range(b_ref.shape[0]):
-        b_ref[index] = x_far_ref[held + index]
-
-
-def turn(y, y_far, x_far, after):
-    count = y_far.shape[0]
-    first = (count + 1) // 2
-    return pl.pallas_call(
-        turn_kernel,
-        out_shape=(
-            jax.ShapeDtypeStruct((first, *y.shape), BF16),
-            jax.ShapeDtypeStruct((count + 1 - first, *y.shape), BF16),
-        ),
-        in_specs=[VMEM] * 3 + [ANY],
-        out_specs=(VMEM, VMEM),
-        compiler_params=params(16),
-        cost_estimate=COST,
         name="turn",
-    )(y, y_far, x_far, after)
+    )(y, x, *after)
 
 
 def tie_kernel(*refs):
@@ -701,29 +689,29 @@
 
 
 def mix_kernel(*refs):
-    near_ref, other_ref, outs = refs[0], refs[1], refs[2:]
+    near_ref, other_ref, outs = refs[0], refs[1], refs[3:]
     for index, ref in enumerate(outs):
         ref[0] = near_ref[index]
         ref[1] = other_ref[index]
 
 
-def mix(near, other):
+def mix(near, other, after):
     count, each, width = near.shape
     return pl.pallas_call(
         mix_kernel,
         out_shape=tuple([jax.ShapeDtypeStruct((2, each, width), BF16)] * count),
-        in_specs=[VMEM, VMEM],
+        in_specs=[VMEM, VMEM, ANY],
         out_specs=tuple([VMEM] * count),
         compiler_params=params(16),
         cost_estimate=COST,
         name="mix",
-    )(near, other)
+    )(near, other, after)
 
 
 def joined(refs, pieces, pick):
     values = [pick(refs[which], start, count) for which, start, count in pieces]
     flat = [value.reshape(-1, value.shape[-1]) for value in values]
-    return jnp.concatenate(flat, axis=0)
+    return flat[0] if len(flat) == 1 else jnp.concatenate(flat, axis=0)
 
 
 def put(quarter, value, outs):
@@ -878,49 +866,58 @@
 
 
 def collect_kernel(count, *refs):
-    out_ref = refs[-1]
+    outs = refs[count:]
     part, width = refs[0].shape
     total = refs[0][...].astype(F32)
     for ref in refs[1:count]:
         total = total + ref[...].astype(F32)
-    out_ref[pl.ds(0, part), :] = total.astype(BF16)
-    if len(refs) > count + 1:
-        out_ref[pl.ds(part, part), :] = refs[count + 1][...]
-        rest = refs[count][...]
-        pieces = []
-        for _ in range(3):
-            piece = rest.astype(BF16).astype(F32)
-            pieces.append(piece)
-            rest = rest - piece
-        pieces.append(jnp.zeros_like(rest))
-        out_ref[pl.ds(2 * part, 32), :] = jnp.concatenate(pieces, axis=0).astype(BF16)
-
-
-def collect(parts, extra=()):
+    if len(outs) == 1:
+        outs[0][...] = total.astype(BF16)
+        return
+    vector_ref, other_ref, short_ref, long_ref = outs[0], outs[1], outs[-2], outs[-1]
+    short_ref[pl.ds(0, part), :] = total.astype(BF16)
+    rest = vector_ref[...]
+    pieces = []
+    for _ in range(3):
+        piece = rest.astype(BF16).astype(F32)
+        pieces.append(piece)
+        rest = rest - piece
+    pieces.append(jnp.zeros_like(rest))
+    short_ref[pl.ds(part, 32), :] = jnp.concatenate(pieces, axis=0).astype(BF16)
+    long_ref[pl.ds(0, part + 32), :] = short_ref[...]
+    long_ref[pl.ds(part + 32, part), :] = other_ref[...]
+
+
+def collect(parts, vector=None, other=None, after=()):
     part, width = parts[0].shape
-    operands = list(parts) + list(extra)
-    rows = 2 * part + 32 if extra else part
+    operands = list(parts)
+    if vector is None:
+        counts = (part,)
+    else:
+        operands += [vector, other]
+        counts = (part + 32, 2 * part + 32)
     return pl.pallas_call(
         functools.partial(collect_kernel, len(parts)),
-        out_shape=jax.ShapeDtypeStruct((rows, width), BF16),
-        in_specs=[VMEM] * len(operands),
-        out_specs=VMEM,
+        out_shape=tuple(jax.ShapeDtypeStruct((rows, width), BF16) for rows in counts),
+        in_specs=[VMEM] * len(operands) + [ANY] * len(after),
+        out_specs=tuple([VMEM] * len(counts)),
         compiler_params=params(16),
         cost_estimate=COST,
         name="collect",
-    )(*operands)
+    )(*operands, *after)
 
 
 def place_kernel(part, tokens, group_ref, *refs):
-    quarters = refs[:4]
-    up_ref, down_ref, gain_ref, scale_ref, loss_ref, held_ref = refs[4:]
+    ups, downs = refs[:4], refs[4:8]
+    up_ref, down_ref, gain_ref, scale_ref, loss_ref, held_ref = refs[8:]
     group = group_ref[0]
     vectors = []
-    for index, ref in enumerate(quarters):
+    for index, (up, down) in enumerate(zip(ups, downs)):
         first = pl.multiple_of(jnp.bitwise_xor(group, index) * part, part)
-        held_ref[pl.ds(first, part), :] = ref[pl.ds(0, part), :].astype(F32)
-        down_ref[pl.ds(first, part), :] = ref[pl.ds(part, part), :].astype(F32)
-        rows = ref[pl.ds(2 * part, 32), :].astype(F32)
+        held_ref[pl.ds(first, part), :] = up[pl.ds(0, part), :].astype(F32)
+        start = down.shape[0] - part
+        down_ref[pl.ds(first, part), :] = down[pl.ds(start, part), :].astype(F32)
+        rows = up[pl.ds(part, 32), :].astype(F32)
         vectors.append((rows[0:8] + rows[8:16]) + rows[16:24])
     up_ref[...] = held_ref[...].T
     vector = (vectors[0] + vectors[1]) + (vectors[2] + vectors[3])
@@ -929,8 +926,8 @@
     loss_ref[...] = vector[2:3, 0:1] * (1.0 / tokens)
 
 
-def place_quarters(group, quarters, part, tokens):
-    width = quarters[0].shape[1]
+def place_quarters(group, ups, downs, part, tokens):
+    width = ups[0].shape[1]
     shapes = [
         jax.ShapeDtypeStruct((width, 4 * part), F32),
         jax.ShapeDtypeStruct((4 * part, width), F32),
@@ -941,13 +938,13 @@
     return pl.pallas_call(
         functools.partial(place_kernel, part, tokens),
         out_shape=tuple(shapes),
-        in_specs=[SMEM] + [VMEM] * 4,
+        in_specs=[SMEM] + [VMEM] * 8,
         out_specs=tuple([VMEM] * len(shapes)),
         scratch_shapes=[pltpu.VMEM((4 * part, width), F32)],
         compiler_params=params(16),
         cost_estimate=COST,
         name="place",
-    )(group, *quarters)
+    )(group, *ups, *downs)
 
 
 def shards_square(
@@ -983,14 +980,13 @@
 
     mine = own_quarter(group, up_weight, down_weight, part)
     arrivals = [along(mine, -shift) for shift in range(1, depth)]
-    x, y = beside(mine, 1), beside(mine, 2)
     rendered, rendered_other = render(
         ray_count, True, me, block_owner, tile_lists, opacity, tile_counts.reshape(1, rows),
         ray_pixel, gaussian_features,
     )
-    first, far = pack(mine, x, y, arrivals, rendered)
-    x_far, y_far = beside(far, 1), beside(far, 2)
-    blocks = mix(rendered, partner(rendered_other))
+    first = pack([mine] + arrivals, rendered)
+    x_part, y_part = beside(first, 1), beside(first, 2)
+    blocks = mix(rendered, partner(rendered_other), first)
     targets = [blocks[0]] + [along(blocks[shift], shift) for shift in range(1, depth)]
     first_other = partner(first)
     tokens, normed, normed_t = prepare_tokens(
@@ -998,11 +994,13 @@
         layer_norm_gain.reshape(1, width), (blocks[0],),
     )
     act_first, slope_first, mixed = forward(normed_t, [first], [first_other])
-    x_far, y_far = tie(x_far, mixed, *targets[1:]), tie(y_far, mixed, *targets[1:])
-    passed_x, passed_y = turn(y, y_far, x_far, mixed)
+    passed_x, passed_y = turn(y_part, x_part, mixed, *targets[1:-1])
     d_low, d_high = beside(passed_x, 1), beside(passed_y, 2)
-    x_other, y_other = partner(x_far), partner(y_far)
-    act_next, slope_next, mixed = forward(normed_t, [x_far, y_far], [x_other, y_other], mixed)
+    x_part, y_part = tie(x_part, passed_x, passed_y), tie(y_part, passed_x, passed_y)
+    x_other, y_other = partner(x_part), partner(y_part)
+    act_next, slope_next, mixed = forward(
+        normed_t, [x_part, y_part], [x_other, y_other], mixed, after=targets[-1:]
+    )
     d_low, d_high = tie(d_low, mixed), tie(d_high, mixed)
     low_other, high_other = partner(d_low), partner(d_high)
     act_last, slope_last, back, back_t, small = forward(
@@ -1012,21 +1010,13 @@
     acts = (act_first, act_next, act_last)
     slopes = (slope_first, slope_next, slope_last)
     weights = (
-        (first, x_far, y_far, d_low, d_high),
+        (first, x_part, y_part, d_low, d_high),
         (first_other, x_other, y_other, low_other, high_other),
     )
     low = d_low.shape[0]
-    act_pieces = (
-        ((0, 0, 1), (0, 3, depth - 1)),
-        ((0, 1, 1), (1, 0, depth - 1)),
-        ((0, 2, 1), (1, depth - 1, depth - 1)),
-        ((2, 0, depth),),
-    )
+    act_pieces = (((0, 0, depth),), ((1, 0, depth),), ((1, depth, depth),), ((2, 0, depth),))
     weight_pieces = (
-        ((0, 0, 1), (0, 3, depth - 1)),
-        ((0, 1, 1), (1, 0, depth - 1)),
-        ((0, 2, 1), (2, 0, depth - 1)),
-        ((3, 0, low), (4, 0, depth - low)),
+        ((0, 0, depth),), ((1, 0, depth),), ((2, 0, depth),), ((3, 0, low), (4, 0, depth - low))
     )
     gain = jnp.zeros((1, width), F32)
     (down_other,) = down_gradient(1, act_pieces, depth, acts, back)
@@ -1046,21 +1036,29 @@
         vector = vector + partner(vector, flip)
         flip *= 2
 
-    def sum_beside(own, to_x, to_y, x_later, y_later):
+    def sum_first(to_x, to_y, x_later, y_later, *after):
         from_x, from_y = beside(to_x, 1), beside(to_y, 2)
-        x_later, y_later = merge(from_x, from_y, x_later, y_later, vector)
-        return totals(own, from_x, from_y, beside(x_later, 1), beside(y_later, 2))
-
-    def sum_along(shares, extra=()):
-        return collect(
-            [shares[0]] + [along(shares[shift], shift) for shift in range(1, depth)], extra
-        )
-
-    down_total = sum_along(sum_beside(*down_sums))
-    total = sum_along(sum_beside(*up_sums), (vector, down_total))
-    quarters = [total] + [beside(total, flip) for flip in (1, 2, 3)]
+        return from_x, from_y, merge(from_x, from_y, x_later, y_later, *after)
+
+    def sum_second(own, from_x, from_y, later):
+        return totals(own, from_x, from_y, beside(later[0], 1), beside(later[1], 2))
+
+    def arrive_along(shares):
+        return [shares[0]] + [along(shares[shift], shift) for shift in range(1, depth)]
+
+    own, *rest = down_sums
+    *arrived, later = sum_first(*rest)
+    shares = sum_second(own, *arrived, later)
+    (down_total,) = collect(arrive_along(shares))
+    down_x, down_y = beside(down_total, 1), beside(down_total, 2)
+    own, *rest = up_sums
+    *arrived, later = sum_first(*rest, vector)
+    shares = sum_second(own, *arrived, later)
+    short, long = collect(arrive_along(shares), vector, down_total, (down_x, down_y))
+    up_x, up_y, both = beside(short, 1), beside(short, 2), beside(long, 3)
     grad_up, grad_down, gain, scale, loss = place_quarters(
-        group, quarters, part, rows * ray_count * group_count
+        group, (short, up_x, up_y, both), (down_total, down_x, down_y, both), part,
+        rows * ray_count * group_count,
     )
     return (grad_up, grad_down, gain.reshape(width), scale.reshape(width), loss.reshape(()))
 

time: 164 us -> 158 us (0.963)
  starting transfers between devices: 47.5 us -> 42.5 us
    ppermute x17, waiting for transfers between devices: 31.5 us -> 25.7 us  [beside(): lax.ppermute(array, 'grp', [(g, g ^ flip) for g in range(group_count)])]
    ppermute x12, waiting for transfers between devices: 33.3 us -> 39 us  [along(): return lax.ppermute(array, 'ray', pairs)]
    ppermute x11, starting transfers between devices: 7.41 us -> 4.34 us  [partner(): return lax.ppermute(array, 'ray', [(r, r ^ flip) for r in range(ray_count)])]
    ppermute x12, starting transfers between devices: 21.1 us -> 18.8 us  [along(): return lax.ppermute(array, 'ray', pairs)]
    unnamed x24 -> x22, local copies, waits for them, and re-layouts: 3.44 us -> 2.11 us
  transfers between devices with their start and end apart: 40 -> 40, of which waited for: 27 -> 31; matrix products, arithmetic and copies ran while one was open for 0% -> 0% of each run, Pallas kernels for 17% -> 18%
where the time goes in v7:
time: 158 us; the launch traced here: 156 us
  waiting for transfers between devices  76.4 us (48%)
  starting transfers between devices  42.5 us (27%)
  Pallas kernels  34.2 us (22%)
  local copies, waits for them, and re-layouts  2.11 us (1%)
    ppermute x12, waiting for transfers between devices, along(): return lax.ppermute(array, 'ray', pairs)  39 us
    ppermute x17, waiting for transfers between devices, beside(): lax.ppermute(array, 'grp', [(g, g ^ flip) for g in range(group_count)])  25.7 us
    ppermute x17, starting transfers between devices, beside(): lax.ppermute(array, 'grp', [(g, g ^ flip) for g in range(group_count)])  19.4 us
    ppermute x12, starting transfers between devices, along(): return lax.ppermute(array, 'ray', pairs)  18.8 us
    pallas_call x1, Pallas kernels, render(): pl.pallas_call(functools.partial(render_kernel, ray_count, relative), out...  11.7 us
    ppermute x11, waiting for transfers between devices, partner(): return lax.ppermute(array, 'ray', [(r, r ^ flip) for r in range(ray_count)])  11.7 us
    pallas_call x3, Pallas kernels, forward(): pl.pallas_call(functools.partial(forward_kernel, first, blocks, len(own),...  7.86 us
    pallas_call x2, Pallas kernels, up_gradient(): pl.pallas_call(functools.partial(up_grad_kernel, side, weight_pieces, act...  5.69 us
  transfers between devices with their start and end apart: 40, of which 31 were waited for; matrix products, arithmetic and copies ran while one was open for 0% of the time, Pallas kernels for 18%

profile of v7, /device:TPU:8, one launch (start us, length us, event | category | flops | bytes accessed | tf_op | source)
XLA Modules:
  0.0 156.2 jit_solution(7974438323332064261)
XLA Ops:
  3.2 3.0 %collective-permute-start.1 = (bf16[2,64,1024]{2,1,0:T(8,128)(2,1)S(1)}, bf16[2,64,1024]{2,1,0:T(8,128)(2,1)S(1)}, u32[]{:S(2)}, u32[]{:S(2)}) collective-permute-start(bf16[2,64,1024]{2,1,0:T(8,128)(2,1)S(1)} %quarter.1.refs_0_), channel_id=1, source_target_pairs={{0,4},{1,5},{2,6},{3,7},{4,0},{5,1},{6,2},{7,3},{8,12},{9,13},{10,... | collective-permute-start | bytes 786440 | tf_op jit(solution)/shard_map/ppermute | solution.py:979
  6.2 2.5 %collective-permute-start.2 = (bf16[2,64,1024]{2,1,0:T(8,128)(2,1)S(1)}, bf16[2,64,1024]{2,1,0:T(8,128)(2,1)S(1)}, u32[]{:S(2)}, u32[]{:S(2)}) collective-permute-start(bf16[2,64,1024]{2,1,0:T(8,128)(2,1)S(1)} %quarter.1.refs_0_), channel_id=1, source_target_pairs={{0,2},{1,3},{2,4},{3,5},{4,6},{5,7},{6,0},{7,1},{8,10},{9,11},{10,... | collective-permute-start | bytes 786440 | tf_op jit(solution)/shard_map/ppermute | solution.py:979
  8.7 11.7 %render.1 = (bf16[4,64,1024]{2,1,0:T(8,128)(2,1)S(1)}, bf16[4,64,1024]{2,1,0:T(8,128)(2,1)S(1)}) custom-call(s32[1]{0:T(128)} %bitcast.1.me_ref, s32[1,8]{1,0:T(1,128)S(1)} %copy-done.8, s32[32,512]{1,0:T(8,128)S(1)} %copy-done.3, f32[32,512]{1,0:T(8,128)S(1)} %copy-done.4, s32[1,512]{1,0:T(1,128)S(1)} %bitcast.11, s32[1,4096]{1,0:T(1,128)S(1)} %copy-done.2, ...), custom_call_target="tpu_custom_call" | custom-call | flops 1048576 | bytes 65536 | tf_op jit(solution)/shard_map/render/pallas_call | solution.py:146
  20.5 3.1 %collective-permute-done.refs_1_ = bf16[2,64,1024]{2,1,0:T(8,128)(2,1)S(1)} collective-permute-done((bf16[2,64,1024]{2,1,0:T(8,128)(2,1)S(1)}, bf16[2,64,1024]{2,1,0:T(8,128)(2,1)S(1)}, u32[]{:S(2)}, u32[]{:S(2)}) %collective-permute-start) | collective-permute-done | bytes 262176 | tf_op jit(solution)/shard_map/ppermute | solution.py:979
  23.7 4.7 %collective-permute-done.2.refs_3_ = bf16[2,64,1024]{2,1,0:T(8,128)(2,1)S(1)} collective-permute-done((bf16[2,64,1024]{2,1,0:T(8,128)(2,1)S(1)}, bf16[2,64,1024]{2,1,0:T(8,128)(2,1)S(1)}, u32[]{:S(2)}, u32[]{:S(2)}) %collective-permute-start.2) | collective-permute-done | bytes 262176 | tf_op jit(solution)/shard_map/ppermute | solution.py:979
  28.6 1.6 collective-permute-start.3
  30.1 1.5 collective-permute-start.4
  31.6 1.9 %collective-permute-done.5.refs_1_ = bf16[4,64,1024]{2,1,0:T(8,128)(2,1)S(1)} collective-permute-done((bf16[4,64,1024]{2,1,0:T(8,128)(2,1)S(1)}, bf16[4,64,1024]{2,1,0:T(8,128)(2,1)S(1)}, u32[]{:S(2)}, u32[]{:S(2)}) %collective-permute-start.5) | collective-permute-done | bytes 524320 | tf_op jit(solution)/shard_map/ppermute | solution.py:975
  33.6 2.5 %collective-permute-start.7 = (bf16[2,64,1024]{2,1,0:T(8,128)(2,1)S(1)}, bf16[2,64,1024]{2,1,0:T(8,128)(2,1)S(1)}, u32[]{:S(2)}, u32[]{:S(2)}) collective-permute-start(bf16[2,64,1024]{2,1,0:T(8,128)(2,1)S(1)} %get-tuple-element.64), channel_id=1, source_target_pairs={{0,2},{1,3},{2,4},{3,5},{4,6},{5,7},{6,0},{7,1},{8,10},{9,11},{10,... | collective-permute-start | bytes 786440 | tf_op jit(solution)/shard_map/ppermute | solution.py:979
  37.2 3.1 %tokens.1 = (bf16[512,1024]{1,0:T(8,128)(2,1)S(1)}, bf16[512,1024]{1,0:T(8,128)(2,1)S(1)}, bf16[1024,512]{1,0:T(8,128)(2,1)S(1)}) custom-call(s32[1]{0:T(128)} %bitcast.1.me_ref, s32[1,8]{1,0:T(1,128)S(1)} %copy-done.8, s32[1,4096]{1,0:T(1,128)S(1)} %copy-done.2, bf16[512,1024]{1,0:T(8,128)(2,1)S(1)} %copy-done.1, f32[1,1024]{1,0:T(1,128)S(1)} %bitcast.8, ...), custom_call_target="tpu_custom_call" | custom-call | flops 1048576 | bytes 65536 | tf_op jit(solution)/shard_map/tokens/pallas_call | solution.py:232
  40.3 1.7 %forward.3 = (bf16[2,4,64,512]{3,2,1,0:T(8,128)(2,1)S(1)}, f32[2,4,64,512]{3,2,1,0:T(8,128)S(1)}, f32[512,1024]{1,0:T(8,128)S(1)}) custom-call(bf16[1024,512]{1,0:T(8,128)(2,1)S(1)} %get-tuple-element.62.refs_0_.refs_1_, bf16[4,2,64,1024]{3,2,1,0:T(8,128)(2,1)S(1)} %pack.1.refs_2_.refs_1_.refs_0_, ...), custom_call_target="tpu_custom_call" | custom-call | flops 1048576 | bytes 65536 | tf_op jit(solution)/shard_map/forward/pallas_call | solution.py:620
  42.0 6.5 %collective-permute-done.7.refs_1_.refs_9_ = bf16[2,64,1024]{2,1,0:T(8,128)(2,1)S(1)} collective-permute-done((bf16[2,64,1024]{2,1,0:T(8,128)(2,1)S(1)}, bf16[2,64,1024]{2,1,0:T(8,128)(2,1)S(1)}, u32[]{:S(2)}, u32[]{:S(2)}) %collective-permute-start.7) | collective-permute-done | bytes 262176 | tf_op jit(solution)/shard_map/ppermute | solution.py:979
  48.5 4.8 %collective-permute-done.8.refs_2_.refs_10_ = bf16[2,64,1024]{2,1,0:T(8,128)(2,1)S(1)} collective-permute-done((bf16[2,64,1024]{2,1,0:T(8,128)(2,1)S(1)}, bf16[2,64,1024]{2,1,0:T(8,128)(2,1)S(1)}, u32[]{:S(2)}, u32[]{:S(2)}) %collective-permute-start.8) | collective-permute-done | bytes 262176 | tf_op jit(solution)/shard_map/ppermute | solution.py:979
  56.0 1.5 collective-permute-start.13
  59.2 7.3 %collective-permute-done.10.refs_0_.refs_11_ = bf16[2,64,1024]{2,1,0:T(8,128)(2,1)S(1)} collective-permute-done((bf16[2,64,1024]{2,1,0:T(8,128)(2,1)S(1)}, bf16[2,64,1024]{2,1,0:T(8,128)(2,1)S(1)}, u32[]{:S(2)}, u32[]{:S(2)}) %collective-permute-start.10) | collective-permute-done | bytes 262176 | tf_op jit(solution)/shard_map/ppermute | solution.py:979
  66.6 3.1 %forward.4 = (bf16[2,8,64,512]{3,2,1,0:T(8,128)(2,1)S(1)}, f32[2,8,64,512]{3,2,1,0:T(8,128)S(1)}, f32[512,1024]{1,0:T(8,128)S(1)}) custom-call(bf16[2,64,1024]{2,1,0:T(8,128)(2,1)S(1)} %collective-permute-done.10.refs_0_.refs_11_, bf16[1024,512]{1,0:T(8,128)(2,1)S(1)} %get-tuple-element.62.refs_0_.refs_1_, bf16[4,2,64,1024]{3,2,1,0:T(8,128)(2,1)S(1)} %tie.4.refs_2_.refs_1_, ...), custom_call_target="tpu_custom_call" | custom-call | flops 1048576 | bytes 65536 | tf_op jit(solution)/shard_map/forward/pallas_call | solution.py:620
  73.1 3.1 %forward.5 = (bf16[2,4,64,512]{3,2,1,0:T(8,128)(2,1)S(1)}, f32[2,4,64,512]{3,2,1,0:T(8,128)S(1)}, bf16[512,1024]{1,0:T(8,128)(2,1)S(1)}, bf16[1024,512]{1,0:T(8,128)(2,1)S(1)}, f32[8,1024]{1,0:T(8,128)S(1)}) custom-call(bf16[1024,512]{1,0:T(8,128)(2,1)S(1)} %get-tuple-element.62.refs_0_.refs_1_, bf16[2,2,64,1024]{3,2,1,0:T(8,128)(2,1)S(1)} %tie.6.refs_1_.refs_3_, ...), custom_call_target="tpu_custom_call" | custom-call | flops 1048576 | bytes 65536 | tf_op jit(solution)/shard_map/forward/pallas_call | solution.py:620
  77.6 2.7 %up_gradient.2 = (bf16[4,4,64,1024]{3,2,1,0:T(8,128)(2,1)S(1)}, f32[1,1024]{1,0:T(1,128)S(1)}) custom-call(bf16[4,2,64,1024]{3,2,1,0:T(8,128)(2,1)S(1)} %collective-permute-done.6.refs_2_.refs_0_, bf16[4,2,64,1024]{3,2,1,0:T(8,128)(2,1)S(1)} %collective-permute-done.11.refs_4_.refs_1_, bf16[4,2,64,1024]{3,2,1,0:T(8,128)(2,1)S(1)} %collective-permute-done.12.refs_5_.refs_2_, ...), custom_call_target="tpu_custom_call" | custom-call | flops 1048576 | bytes 65536 | tf_op jit(solution)/shard_map/up_gradient/pallas_call | solution.py:813
  84.7 3.0 %up_gradient.3 = (bf16[4,64,1024]{2,1,0:T(8,128)(2,1)S(1)}, bf16[4,64,1024]{2,1,0:T(8,128)(2,1)S(1)}, bf16[4,64,1024]{2,1,0:T(8,128)(2,1)S(1)}, bf16[2,64,1024]{...) custom-call(bf16[4,2,64,1024]{3,2,1,0:T(8,128)(2,1)S(1)} %pack.1.refs_2_.refs_1_.refs_0_, ...), custom_call_target="tpu_custom_call" | custom-call | flops 1048576 | bytes 65536 | tf_op jit(solution)/shard_map/up_gradient/pallas_call | solution.py:813
  87.6 1.5 collective-permute-start.17
  90.1 7.7 %collective-permute-done.28.x_ref = bf16[4,64,1024]{2,1,0:T(8,128)(2,1)S(1)} collective-permute-done((bf16[4,64,1024]{2,1,0:T(8,128)(2,1)S(1)}, bf16[4,64,1024]{2,1,0:T(8,128)(2,1)S(1)}, u32[]{:S(2)}, u32[]{:S(2)}) %collective-permute-start.28) | collective-permute-done | bytes 524320 | tf_op jit(solution)/shard_map/ppermute | solution.py:972
  103.7 2.8 %collective-permute-done.20 = f32[8,1024]{1,0:T(8,128)S(1)} collective-permute-done((f32[8,1024]{1,0:T(8,128)S(1)}, f32[8,1024]{1,0:T(8,128)S(1)}, u32[]{:S(2)}, u32[]{:S(2)}) %collective-permute-start.20) | collective-permute-done | bytes 32800 | tf_op jit(solution)/shard_map/ppermute | solution.py:975
  106.4 1.9 %collective-permute-start.21 = (f32[8,1024]{1,0:T(8,128)S(1)}, f32[8,1024]{1,0:T(8,128)S(1)}, u32[]{:S(2)}, u32[]{:S(2)}) collective-permute-start(f32[8,1024]{1,0:T(8,128)S(1)} %add.10), channel_id=1, source_target_pairs={{0,4},{1,5},{2,6},{3,7},{4,0},{5,1},{6,2},{7,3},{8,12},{9,13},{10,... | collective-permute-start | bytes 98312 | tf_op jit(solution)/shard_map/ppermute | solution.py:975
  108.3 2.9 %collective-permute-done.21 = f32[8,1024]{1,0:T(8,128)S(1)} collective-permute-done((f32[8,1024]{1,0:T(8,128)S(1)}, f32[8,1024]{1,0:T(8,128)S(1)}, u32[]{:S(2)}, u32[]{:S(2)}) %collective-permute-start.21) | collective-permute-done | bytes 32800 | tf_op jit(solution)/shard_map/ppermute | solution.py:975
  115.7 2.2 %collective-permute-start.32 = (bf16[64,1024]{1,0:T(8,128)(2,1)S(1)}, bf16[64,1024]{1,0:T(8,128)(2,1)S(1)}, u32[]{:S(2)}, u32[]{:S(2)}) collective-permute-start(bf16[64,1024]{1,0:T(8,128)(2,1)S(1)} %get-tuple-element.103), channel_id=1, source_target_pairs={{0,2},{1,3},{2,4},{3,5},{4,6},{5,7},{6,0},{7,1},{8,10},{9,11},{10,... | collective-permute-start | bytes 393224 | tf_op jit(solution)/shard_map/ppermute | solution.py:979
  120.2 2.2 %collective-permute-start.24 = (bf16[64,1024]{1,0:T(8,128)(2,1)S(1)}, bf16[64,1024]{1,0:T(8,128)(2,1)S(1)}, u32[]{:S(2)}, u32[]{:S(2)}) collective-permute-start(bf16[64,1024]{1,0:T(8,128)(2,1)S(1)} %get-tuple-element.88), channel_id=1, source_target_pairs={{0,2},{1,3},{2,4},{3,5},{4,6},{5,7},{6,0},{7,1},{8,10},{9,11},{10,... | collective-permute-start | bytes 393224 | tf_op jit(solution)/shard_map/ppermute | solution.py:979
  122.4 2.5 %collective-permute-start.25 = (bf16[64,1024]{1,0:T(8,128)(2,1)S(1)}, bf16[64,1024]{1,0:T(8,128)(2,1)S(1)}, u32[]{:S(2)}, u32[]{:S(2)}) collective-permute-start(bf16[64,1024]{1,0:T(8,128)(2,1)S(1)} %get-tuple-element.89), channel_id=1, source_target_pairs={{0,4},{1,5},{2,6},{3,7},{4,0},{5,1},{6,2},{7,3},{8,12},{9,13},{10,... | collective-permute-start | bytes 393224 | tf_op jit(solution)/shard_map/ppermute | solution.py:979
  124.9 1.9 %collective-permute-done.32.refs_1_ = bf16[64,1024]{1,0:T(8,128)(2,1)S(1)} collective-permute-done((bf16[64,1024]{1,0:T(8,128)(2,1)S(1)}, bf16[64,1024]{1,0:T(8,128)(2,1)S(1)}, u32[]{:S(2)}, u32[]{:S(2)}) %collective-permute-start.32) | collective-permute-done | bytes 131104 | tf_op jit(solution)/shard_map/ppermute | solution.py:979
  126.8 7.7 %collective-permute-done.33.refs_2_ = bf16[64,1024]{1,0:T(8,128)(2,1)S(1)} collective-permute-done((bf16[64,1024]{1,0:T(8,128)(2,1)S(1)}, bf16[64,1024]{1,0:T(8,128)(2,1)S(1)}, u32[]{:S(2)}, u32[]{:S(2)}) %collective-permute-start.33) | collective-permute-done | bytes 131104 | tf_op jit(solution)/shard_map/ppermute | solution.py:979
  142.4 1.5 collective-permute-start.37
  144.9 8.8 %collective-permute-done.37.refs_1_ = bf16[96,1024]{1,0:T(8,128)(2,1)S(1)} collective-permute-done((bf16[96,1024]{1,0:T(8,128)(2,1)S(1)}, bf16[96,1024]{1,0:T(8,128)(2,1)S(1)}, u32[]{:S(2)}, u32[]{:S(2)}) %collective-permute-start.37) | collective-permute-done | bytes 196640 | tf_op jit(solution)/shard_map/ppermute | solution.py:972
  154.4 1.7 %place.1 = (f32[1024,256]{1,0:T(8,128)}, f32[256,1024]{1,0:T(8,128)}, f32[1,1024]{1,0:T(1,128)}, f32[1,1024]{1,0:T(1,128)}, f32[1,1]{1,0:T(1,128)}) custom-call(s32[1]{0:T(128)} %bitcast.group_ref, bf16[96,1024]{1,0:T(8,128)(2,1)S(1)} %get-tuple-element.106.refs_0_, bf16[96,1024]{1,0:T(8,128)(2,1)S(1)} %collective-permute-done.37.refs_1_, ...), custom_call_target="tpu_custom_call" | custom-call | flops 1048576 | bytes 65536 | tf_op jit(solution)/shard_map/place/pallas_call | solution.py:938
  (98 shorter events, 40.5 us)
Async XLA Ops:
  3.1 20.5 %collective-permute-start = (bf16[2,64,1024]{2,1,0:T(8,128)(2,1)S(1)}, bf16[2,64,1024]{2,1,0:T(8,128)(2,1)S(1)}, u32[]{:S(2)}, u32[]{:S(2)}) collective-permute-start(bf16[2,64,1024]{2,1,0:T(8,128)(2,1)S(1)} %quarter.1.refs_0_), channel_id=1, source_target_pairs={{0,6},{1,7},{2,0},{3,1},{4,2},{5,3},{6,4},{7,5},{8,14},{9,15},{10,... | collective-permute-start | bytes 786440 | tf_op jit(solution)/shard_map/ppermute | solution.py:979
  3.2 20.5 %collective-permute-start.1 = (bf16[2,64,1024]{2,1,0:T(8,128)(2,1)S(1)}, bf16[2,64,1024]{2,1,0:T(8,128)(2,1)S(1)}, u32[]{:S(2)}, u32[]{:S(2)}) collective-permute-start(bf16[2,64,1024]{2,1,0:T(8,128)(2,1)S(1)} %quarter.1.refs_0_), channel_id=1, source_target_pairs={{0,4},{1,5},{2,6},{3,7},{4,0},{5,1},{6,2},{7,3},{8,12},{9,13},{10,... | collective-permute-start | bytes 786440 | tf_op jit(solution)/shard_map/ppermute | solution.py:979
  6.2 22.2 %collective-permute-start.2 = (bf16[2,64,1024]{2,1,0:T(8,128)(2,1)S(1)}, bf16[2,64,1024]{2,1,0:T(8,128)(2,1)S(1)}, u32[]{:S(2)}, u32[]{:S(2)}) collective-permute-start(bf16[2,64,1024]{2,1,0:T(8,128)(2,1)S(1)} %quarter.1.refs_0_), channel_id=1, source_target_pairs={{0,2},{1,3},{2,4},{3,5},{4,6},{5,7},{6,0},{7,1},{8,10},{9,11},{10,... | collective-permute-start | bytes 786440 | tf_op jit(solution)/shard_map/ppermute | solution.py:979
  28.5 11.8 %collective-permute-start.6 = (bf16[4,2,64,1024]{3,2,1,0:T(8,128)(2,1)S(1)}, bf16[4,2,64,1024]{3,2,1,0:T(8,128)(2,1)S(1)}, u32[]{:S(2)}, u32[]{:S(2)}) collective-permute-start(bf16[4,2,64,1024]{3,2,1,0:T(8,128)(2,1)S(1)} %pack.1.refs_2_.refs_1_.refs_0_), channel_id=1, source_target_pairs={{0,1},{1,0},{2,3},{3,2},{4,5},{5,4},{6,7},{7,6},{8,9},{9,8},{10,11... | collective-permute-start | bytes 3145736 | tf_op jit(solution)/shard_map/ppermute | solution.py:975
  28.6 25.6 %collective-permute-start.3 = (bf16[4,2,64,1024]{3,2,1,0:T(8,128)(2,1)S(1)}, bf16[4,2,64,1024]{3,2,1,0:T(8,128)(2,1)S(1)}, u32[]{:S(2)}, u32[]{:S(2)}) collective-permute-start(bf16[4,2,64,1024]{3,2,1,0:T(8,128)(2,1)S(1)} %pack.1.refs_2_.refs_1_.refs_0_), channel_id=1, source_target_pairs={{0,8},{8,0},{16,24},{24,16},{1,9},{9,1},{17,25},{25,17},{2,10},{10... | collective-permute-start | bytes 3145736 | tf_op jit(solution)/shard_map/ppermute | solution.py:972
  30.1 25.2 %collective-permute-start.4 = (bf16[4,2,64,1024]{3,2,1,0:T(8,128)(2,1)S(1)}, bf16[4,2,64,1024]{3,2,1,0:T(8,128)(2,1)S(1)}, u32[]{:S(2)}, u32[]{:S(2)}) collective-permute-start(bf16[4,2,64,1024]{3,2,1,0:T(8,128)(2,1)S(1)} %pack.1.refs_2_.refs_1_.refs_0_), channel_id=1, source_target_pairs={{0,16},{8,24},{16,0},{24,8},{1,17},{9,25},{17,1},{25,9},{2,18},{10... | collective-permute-start | bytes 3145736 | tf_op jit(solution)/shard_map/ppermute | solution.py:972
  33.6 14.8 %collective-permute-start.7 = (bf16[2,64,1024]{2,1,0:T(8,128)(2,1)S(1)}, bf16[2,64,1024]{2,1,0:T(8,128)(2,1)S(1)}, u32[]{:S(2)}, u32[]{:S(2)}) collective-permute-start(bf16[2,64,1024]{2,1,0:T(8,128)(2,1)S(1)} %get-tuple-element.64), channel_id=1, source_target_pairs={{0,2},{1,3},{2,4},{3,5},{4,6},{5,7},{6,0},{7,1},{8,10},{9,11},{10,... | collective-permute-start | bytes 786440 | tf_op jit(solution)/shard_map/ppermute | solution.py:979
  36.2 17.1 %collective-permute-start.8 = (bf16[2,64,1024]{2,1,0:T(8,128)(2,1)S(1)}, bf16[2,64,1024]{2,1,0:T(8,128)(2,1)S(1)}, u32[]{:S(2)}, u32[]{:S(2)}) collective-permute-start(bf16[2,64,1024]{2,1,0:T(8,128)(2,1)S(1)} %get-tuple-element.65), channel_id=1, source_target_pairs={{0,4},{1,5},{2,6},{3,7},{4,0},{5,1},{6,2},{7,3},{8,12},{9,13},{10,... | collective-permute-start | bytes 786440 | tf_op jit(solution)/shard_map/ppermute | solution.py:979
  55.4 11.1 %collective-permute-start.12 = (bf16[4,2,64,1024]{3,2,1,0:T(8,128)(2,1)S(1)}, bf16[4,2,64,1024]{3,2,1,0:T(8,128)(2,1)S(1)}, u32[]{:S(2)}, u32[]{:S(2)}) collective-permute-start(bf16[4,2,64,1024]{3,2,1,0:T(8,128)(2,1)S(1)} %tie.5.refs_3_.refs_2_), channel_id=1, source_target_pairs={{0,1},{1,0},{2,3},{3,2},{4,5},{5,4},{6,7},{7,6},{8,9},{9,8},{10,11... | collective-permute-start | bytes 3145736 | tf_op jit(solution)/shard_map/ppermute | solution.py:975
  55.5 11.0 %collective-permute-start.11 = (bf16[4,2,64,1024]{3,2,1,0:T(8,128)(2,1)S(1)}, bf16[4,2,64,1024]{3,2,1,0:T(8,128)(2,1)S(1)}, u32[]{:S(2)}, u32[]{:S(2)}) collective-permute-start(bf16[4,2,64,1024]{3,2,1,0:T(8,128)(2,1)S(1)} %tie.4.refs_2_.refs_1_), channel_id=1, source_target_pairs={{0,1},{1,0},{2,3},{3,2},{4,5},{5,4},{6,7},{7,6},{8,9},{9,8},{10,11... | collective-permute-start | bytes 3145736 | tf_op jit(solution)/shard_map/ppermute | solution.py:975
  56.0 13.9 %collective-permute-start.13 = (bf16[2,2,64,1024]{3,2,1,0:T(8,128)(2,1)S(1)}, bf16[2,2,64,1024]{3,2,1,0:T(8,128)(2,1)S(1)}, u32[]{:S(2)}, u32[]{:S(2)}) collective-permute-start(bf16[2,2,64,1024]{3,2,1,0:T(8,128)(2,1)S(1)} %get-tuple-element.67.refs_2_), channel_id=1, source_target_pairs={{0,16},{8,24},{16,0},{24,8},{1,17},{9,25},{17,1},{25,9},{2,18},{10... | collective-permute-start | bytes 1572872 | tf_op jit(solution)/shard_map/ppermute | solution.py:972
  57.5 13.6 %collective-permute-start.9 = (bf16[2,2,64,1024]{3,2,1,0:T(8,128)(2,1)S(1)}, bf16[2,2,64,1024]{3,2,1,0:T(8,128)(2,1)S(1)}, u32[]{:S(2)}, u32[]{:S(2)}) collective-permute-start(bf16[2,2,64,1024]{3,2,1,0:T(8,128)(2,1)S(1)} %get-tuple-element.66.refs_1_), channel_id=1, source_target_pairs={{0,8},{8,0},{16,24},{24,16},{1,9},{9,1},{17,25},{25,17},{2,10},{10... | collective-permute-start | bytes 1572872 | tf_op jit(solution)/shard_map/ppermute | solution.py:972
  58.1 8.5 %collective-permute-start.10 = (bf16[2,64,1024]{2,1,0:T(8,128)(2,1)S(1)}, bf16[2,64,1024]{2,1,0:T(8,128)(2,1)S(1)}, u32[]{:S(2)}, u32[]{:S(2)}) collective-permute-start(bf16[2,64,1024]{2,1,0:T(8,128)(2,1)S(1)} %get-tuple-element.68), channel_id=1, source_target_pairs={{0,6},{1,7},{2,0},{3,1},{4,2},{5,3},{6,4},{7,5},{8,14},{9,15},{10,... | collective-permute-start | bytes 786440 | tf_op jit(solution)/shard_map/ppermute | solution.py:979
  82.9 14.8 %collective-permute-start.28 = (bf16[4,64,1024]{2,1,0:T(8,128)(2,1)S(1)}, bf16[4,64,1024]{2,1,0:T(8,128)(2,1)S(1)}, u32[]{:S(2)}, u32[]{:S(2)}) collective-permute-start(bf16[4,64,1024]{2,1,0:T(8,128)(2,1)S(1)} %get-tuple-element.96), channel_id=1, source_target_pairs={{0,8},{8,0},{16,24},{24,16},{1,9},{9,1},{17,25},{25,17},{2,10},{10... | collective-permute-start | bytes 1572872 | tf_op jit(solution)/shard_map/ppermute | solution.py:972
  83.8 14.8 %collective-permute-start.29 = (bf16[4,64,1024]{2,1,0:T(8,128)(2,1)S(1)}, bf16[4,64,1024]{2,1,0:T(8,128)(2,1)S(1)}, u32[]{:S(2)}, u32[]{:S(2)}) collective-permute-start(bf16[4,64,1024]{2,1,0:T(8,128)(2,1)S(1)} %get-tuple-element.97), channel_id=1, source_target_pairs={{0,16},{8,24},{16,0},{24,8},{1,17},{9,25},{17,1},{25,9},{2,18},{10... | collective-permute-start | bytes 1572872 | tf_op jit(solution)/shard_map/ppermute | solution.py:972
  87.6 23.6 %collective-permute-start.17 = (bf16[4,64,1024]{2,1,0:T(8,128)(2,1)S(1)}, bf16[4,64,1024]{2,1,0:T(8,128)(2,1)S(1)}, u32[]{:S(2)}, u32[]{:S(2)}) collective-permute-start(bf16[4,64,1024]{2,1,0:T(8,128)(2,1)S(1)} %get-tuple-element.80), channel_id=1, source_target_pairs={{0,8},{8,0},{16,24},{24,16},{1,9},{9,1},{17,25},{25,17},{2,10},{10... | collective-permute-start | bytes 1572872 | tf_op jit(solution)/shard_map/ppermute | solution.py:972
  89.1 22.2 %collective-permute-start.18 = (bf16[4,64,1024]{2,1,0:T(8,128)(2,1)S(1)}, bf16[4,64,1024]{2,1,0:T(8,128)(2,1)S(1)}, u32[]{:S(2)}, u32[]{:S(2)}) collective-permute-start(bf16[4,64,1024]{2,1,0:T(8,128)(2,1)S(1)} %get-tuple-element.81), channel_id=1, source_target_pairs={{0,16},{8,24},{16,0},{24,8},{1,17},{9,25},{17,1},{25,9},{2,18},{10... | collective-permute-start | bytes 1572872 | tf_op jit(solution)/shard_map/ppermute | solution.py:972
  99.0 15.6 %collective-permute-start.30 = (bf16[2,64,1024]{2,1,0:T(8,128)(2,1)S(1)}, bf16[2,64,1024]{2,1,0:T(8,128)(2,1)S(1)}, u32[]{:S(2)}, u32[]{:S(2)}) collective-permute-start(bf16[2,64,1024]{2,1,0:T(8,128)(2,1)S(1)} %get-tuple-element.100), channel_id=1, source_target_pairs={{0,8},{8,0},{16,24},{24,16},{1,9},{9,1},{17,25},{25,17},{2,10},{10... | collective-permute-start | bytes 786440 | tf_op jit(solution)/shard_map/ppermute | solution.py:972
  100.3 15.2 %collective-permute-start.31 = (bf16[2,64,1024]{2,1,0:T(8,128)(2,1)S(1)}, bf16[2,64,1024]{2,1,0:T(8,128)(2,1)S(1)}, u32[]{:S(2)}, u32[]{:S(2)}) collective-permute-start(bf16[2,64,1024]{2,1,0:T(8,128)(2,1)S(1)} %get-tuple-element.101), channel_id=1, source_target_pairs={{0,16},{8,24},{16,0},{24,8},{1,17},{9,25},{17,1},{25,9},{2,18},{10... | collective-permute-start | bytes 786440 | tf_op jit(solution)/shard_map/ppermute | solution.py:972
  111.4 8.0 %collective-permute-start.22 = (bf16[2,64,1024]{2,1,0:T(8,128)(2,1)S(1)}, bf16[2,64,1024]{2,1,0:T(8,128)(2,1)S(1)}, u32[]{:S(2)}, u32[]{:S(2)}) collective-permute-start(bf16[2,64,1024]{2,1,0:T(8,128)(2,1)S(1)} %get-tuple-element.85), channel_id=1, source_target_pairs={{0,8},{8,0},{16,24},{24,16},{1,9},{9,1},{17,25},{25,17},{2,10},{10... | collective-permute-start | bytes 786440 | tf_op jit(solution)/shard_map/ppermute | solution.py:972
  112.0 8.0 %collective-permute-start.23 = (bf16[2,64,1024]{2,1,0:T(8,128)(2,1)S(1)}, bf16[2,64,1024]{2,1,0:T(8,128)(2,1)S(1)}, u32[]{:S(2)}, u32[]{:S(2)}) collective-permute-start(bf16[2,64,1024]{2,1,0:T(8,128)(2,1)S(1)} %get-tuple-element.86), channel_id=1, source_target_pairs={{0,16},{8,24},{16,0},{24,8},{1,17},{9,25},{17,1},{25,9},{2,18},{10... | collective-permute-start | bytes 786440 | tf_op jit(solution)/shard_map/ppermute | solution.py:972
  115.7 11.1 %collective-permute-start.32 = (bf16[64,1024]{1,0:T(8,128)(2,1)S(1)}, bf16[64,1024]{1,0:T(8,128)(2,1)S(1)}, u32[]{:S(2)}, u32[]{:S(2)}) collective-permute-start(bf16[64,1024]{1,0:T(8,128)(2,1)S(1)} %get-tuple-element.103), channel_id=1, source_target_pairs={{0,2},{1,3},{2,4},{3,5},{4,6},{5,7},{6,0},{7,1},{8,10},{9,11},{10,... | collective-permute-start | bytes 393224 | tf_op jit(solution)/shard_map/ppermute | solution.py:979
  117.9 16.6 %collective-permute-start.33 = (bf16[64,1024]{1,0:T(8,128)(2,1)S(1)}, bf16[64,1024]{1,0:T(8,128)(2,1)S(1)}, u32[]{:S(2)}, u32[]{:S(2)}) collective-permute-start(bf16[64,1024]{1,0:T(8,128)(2,1)S(1)} %get-tuple-element.104), channel_id=1, source_target_pairs={{0,4},{1,5},{2,6},{3,7},{4,0},{5,1},{6,2},{7,3},{8,12},{9,13},{10,... | collective-permute-start | bytes 393224 | tf_op jit(solution)/shard_map/ppermute | solution.py:979
  118.9 15.9 %collective-permute-start.34 = (bf16[64,1024]{1,0:T(8,128)(2,1)S(1)}, bf16[64,1024]{1,0:T(8,128)(2,1)S(1)}, u32[]{:S(2)}, u32[]{:S(2)}) collective-permute-start(bf16[64,1024]{1,0:T(8,128)(2,1)S(1)} %get-tuple-element.105), channel_id=1, source_target_pairs={{0,6},{1,7},{2,0},{3,1},{4,2},{5,3},{6,4},{7,5},{8,14},{9,15},{10,... | collective-permute-start | bytes 393224 | tf_op jit(solution)/shard_map/ppermute | solution.py:979
  120.2 17.1 %collective-permute-start.24 = (bf16[64,1024]{1,0:T(8,128)(2,1)S(1)}, bf16[64,1024]{1,0:T(8,128)(2,1)S(1)}, u32[]{:S(2)}, u32[]{:S(2)}) collective-permute-start(bf16[64,1024]{1,0:T(8,128)(2,1)S(1)} %get-tuple-element.88), channel_id=1, source_target_pairs={{0,2},{1,3},{2,4},{3,5},{4,6},{5,7},{6,0},{7,1},{8,10},{9,11},{10,... | collective-permute-start | bytes 393224 | tf_op jit(solution)/shard_map/ppermute | solution.py:979
  122.4 16.0 %collective-permute-start.25 = (bf16[64,1024]{1,0:T(8,128)(2,1)S(1)}, bf16[64,1024]{1,0:T(8,128)(2,1)S(1)}, u32[]{:S(2)}, u32[]{:S(2)}) collective-permute-start(bf16[64,1024]{1,0:T(8,128)(2,1)S(1)} %get-tuple-element.89), channel_id=1, source_target_pairs={{0,4},{1,5},{2,6},{3,7},{4,0},{5,1},{6,2},{7,3},{8,12},{9,13},{10,... | collective-permute-start | bytes 393224 | tf_op jit(solution)/shard_map/ppermute | solution.py:979
  126.8 13.0 %collective-permute-start.26 = (bf16[64,1024]{1,0:T(8,128)(2,1)S(1)}, bf16[64,1024]{1,0:T(8,128)(2,1)S(1)}, u32[]{:S(2)}, u32[]{:S(2)}) collective-permute-start(bf16[64,1024]{1,0:T(8,128)(2,1)S(1)} %get-tuple-element.90), channel_id=1, source_target_pairs={{0,6},{1,7},{2,0},{3,1},{4,2},{5,3},{6,4},{7,5},{8,14},{9,15},{10,... | collective-permute-start | bytes 393224 | tf_op jit(solution)/shard_map/ppermute | solution.py:979
  134.8 5.1 %collective-permute-start.35 = (bf16[64,1024]{1,0:T(8,128)(2,1)S(1)}, bf16[64,1024]{1,0:T(8,128)(2,1)S(1)}, u32[]{:S(2)}, u32[]{:S(2)}) collective-permute-start(bf16[64,1024]{1,0:T(8,128)(2,1)S(1)} %collect.2.refs_5_.refs_4_), channel_id=1, source_target_pairs={{0,8},{8,0},{16,24},{24,16},{1,9},{9,1},{17,25},{25,17},{2,10},{10... | collective-permute-start | bytes 393224 | tf_op jit(solution)/shard_map/ppermute | solution.py:972
  136.2 5.0 %collective-permute-start.36 = (bf16[64,1024]{1,0:T(8,128)(2,1)S(1)}, bf16[64,1024]{1,0:T(8,128)(2,1)S(1)}, u32[]{:S(2)}, u32[]{:S(2)}) collective-permute-start(bf16[64,1024]{1,0:T(8,128)(2,1)S(1)} %collect.2.refs_5_.refs_4_), channel_id=1, source_target_pairs={{0,16},{8,24},{16,0},{24,8},{1,17},{9,25},{17,1},{25,9},{2,18},{10... | collective-permute-start | bytes 393224 | tf_op jit(solution)/shard_map/ppermute | solution.py:972
  141.3 13.1 %collective-permute-start.39 = (bf16[160,1024]{1,0:T(8,128)(2,1)S(1)}, bf16[160,1024]{1,0:T(8,128)(2,1)S(1)}, u32[]{:S(2)}, u32[]{:S(2)}) collective-permute-start(bf16[160,1024]{1,0:T(8,128)(2,1)S(1)} %get-tuple-element.107), channel_id=1, source_target_pairs={{0,24},{8,16},{16,8},{24,0},{1,25},{9,17},{17,9},{25,1},{2,26},{10... | collective-permute-start | bytes 983048 | tf_op jit(solution)/shard_map/ppermute | solution.py:972
  142.4 11.3 %collective-permute-start.37 = (bf16[96,1024]{1,0:T(8,128)(2,1)S(1)}, bf16[96,1024]{1,0:T(8,128)(2,1)S(1)}, u32[]{:S(2)}, u32[]{:S(2)}) collective-permute-start(bf16[96,1024]{1,0:T(8,128)(2,1)S(1)} %get-tuple-element.106.refs_0_), channel_id=1, source_target_pairs={{0,8},{8,0},{16,24},{24,16},{1,9},{9,1},{17,25},{25,17},{2,10},{10... | collective-permute-start | bytes 589832 | tf_op jit(solution)/shard_map/ppermute | solution.py:972
  143.9 10.5 %collective-permute-start.38 = (bf16[96,1024]{1,0:T(8,128)(2,1)S(1)}, bf16[96,1024]{1,0:T(8,128)(2,1)S(1)}, u32[]{:S(2)}, u32[]{:S(2)}) collective-permute-start(bf16[96,1024]{1,0:T(8,128)(2,1)S(1)} %get-tuple-element.106.refs_0_), channel_id=1, source_target_pairs={{0,16},{8,24},{16,0},{24,8},{1,17},{9,25},{17,1},{25,9},{2,18},{10... | collective-permute-start | bytes 589832 | tf_op jit(solution)/shard_map/ppermute | solution.py:972
  (19 other events, 82.9 us)

commit v8 on v7

--- a/solution.py
+++ b/solution.py
@@ -552,9 +552,8 @@
     act_ref, slope_ref = refs[:2]
     del refs[:2]
     width, rows = normed_t_ref.shape
-    total = act_ref.shape[1]
     part = act_ref.shape[2]
-    downs = []
+    part_sum = None
     for side, group in enumerate((own, other)):
         start = 0
         for ref in group:
@@ -566,17 +565,16 @@
                 density = jnp.exp(-0.5 * hidden * hidden) * ((2.0 * jnp.pi) ** -0.5)
                 act_ref[side, start + index] = (hidden * phi).astype(BF16)
                 slope_ref[side, start + index] = phi + hidden * density
-            downs.append(ref[:, 1].reshape(count * part, width))
+            act = act_ref[side, start:start + count].reshape(count * part, rows)
+            term = dot_tn(act, ref[:, 1].reshape(count * part, width))
+            part_sum = term if part_sum is None else part_sum + term
             start += count
-    act = act_ref[...].reshape(2 * total * part, rows)
-    down = jnp.concatenate(downs, axis=0)
     if not last:
         mixed_out = refs[0]
-        part_sum = dot_tn(act, down)
         mixed_out[...] = part_sum if first else mixed_in[...] + part_sum
         return
     back_ref, back_t_ref, small_ref, mixed_ref = refs
-    mixed_ref[...] = mixed_in[...] + dot_tn(act, down)
+    mixed_ref[...] = mixed_in[...] + part_sum
     scale = scale_ref[...]
     small_ref[...] = jnp.zeros_like(small_ref)
     piece = rows // blocks
@@ -623,52 +621,31 @@
         in_specs=[ANY] * len(after) + [VMEM] * (len(operands) - len(after)),
         out_specs=tuple([VMEM] * len(shapes)),
         scratch_shapes=scratch,
-        compiler_params=params(24),
+        compiler_params=params(32),
         cost_estimate=COST,
         name="forward",
     )(*operands)
 
 
-def pack_kernel(count, *refs):
+def pack_kernel(counts, *refs):
     out_ref = refs[-1]
-    for index, ref in enumerate(refs[:count]):
-        out_ref[index] = ref[...]
+    start = 0
+    for count, ref in zip(counts, refs):
+        out_ref[start:start + count] = ref[...].reshape(count, *out_ref.shape[1:])
+        start += count
 
 
 def pack(pieces, *after):
-    return pl.pallas_call(
-        functools.partial(pack_kernel, len(pieces)),
-        out_shape=jax.ShapeDtypeStruct((len(pieces), *pieces[0].shape), BF16),
+    counts = [1 if piece.ndim == 3 else piece.shape[0] for piece in pieces]
+    return pl.pallas_call(
+        functools.partial(pack_kernel, counts),
+        out_shape=jax.ShapeDtypeStruct((sum(counts), *pieces[0].shape[-3:]), BF16),
         in_specs=[VMEM] * len(pieces) + [ANY] * len(after),
         out_specs=VMEM,
         compiler_params=params(16),
         cost_estimate=COST,
         name="pack",
     )(*pieces, *after)
-
-
-def turn_kernel(y_ref, x_ref, *refs):
-    a_ref, b_ref = refs[-2:]
-    first = a_ref.shape[0]
-    a_ref[...] = y_ref[:first]
-    b_ref[...] = x_ref[first:]
-
-
-def turn(y, x, *after):
-    count = y.shape[0]
-    first = count // 2
-    return pl.pallas_call(
-        turn_kernel,
-        out_shape=(
-            jax.ShapeDtypeStruct((first, *y.shape[1:]), BF16),
-            jax.ShapeDtypeStruct((count - first, *y.shape[1:]), BF16),
-        ),
-        in_specs=[VMEM] * 2 + [ANY] * len(after),
-        out_specs=(VMEM, VMEM),
-        compiler_params=params(16),
-        cost_estimate=COST,
-        name="turn",
-    )(y, x, *after)
 
 
 def tie_kernel(*refs):
@@ -689,23 +666,24 @@
 
 
 def mix_kernel(*refs):
-    near_ref, other_ref, outs = refs[0], refs[1], refs[3:]
+    near_ref, other_ref = refs[:2]
+    outs = refs[-near_ref.shape[0]:]
     for index, ref in enumerate(outs):
         ref[0] = near_ref[index]
         ref[1] = other_ref[index]
 
 
-def mix(near, other, after):
+def mix(near, other, *after):
     count, each, width = near.shape
     return pl.pallas_call(
         mix_kernel,
         out_shape=tuple([jax.ShapeDtypeStruct((2, each, width), BF16)] * count),
-        in_specs=[VMEM, VMEM, ANY],
+        in_specs=[VMEM, VMEM] + [ANY] * len(after),
         out_specs=tuple([VMEM] * count),
         compiler_params=params(16),
         cost_estimate=COST,
         name="mix",
-    )(near, other, after)
+    )(near, other, *after)
 
 
 def joined(refs, pieces, pick):
@@ -739,24 +717,23 @@
 
 
 def down_grad_kernel(side, act_pieces, add, *refs):
-    count = 3
-    acts, back_ref = refs[:count], refs[count]
-    arrived = refs[count + 1] if add else None
-    outs = refs[count + 2:] if add else refs[count + 1:]
+    acts, back_ref = refs[:2], refs[2]
+    arrived = refs[3] if add else None
+    outs = refs[4:] if add else refs[3:]
     for quarter in (3, 1, 2, 0):
         act = joined(acts, act_pieces[quarter], lambda ref, a, n: ref[side, a:a + n])
         emit(quarter, dot_nn(act, back_ref[...]), arrived, outs)
 
 
 def up_grad_kernel(side, weight_pieces, act_pieces, add, *refs):
-    weights, slopes = refs[:5], refs[5:8]
-    back_t_ref, normed_ref, gain_in = refs[8:11]
+    weights, slopes = refs[:3], refs[3:5]
+    back_t_ref, normed_ref, gain_in = refs[5:8]
     if add:
-        arrived, scale_ref, small_ref = refs[11:14]
-        outs, vector_ref, gain_ref = refs[14:-2], refs[-2], refs[-1]
+        arrived, scale_ref, small_ref = refs[8:11]
+        outs, vector_ref, gain_ref = refs[11:-2], refs[-2], refs[-1]
     else:
         arrived = None
-        outs, gain_ref = refs[11:-1], refs[-1]
+        outs, gain_ref = refs[8:-1], refs[-1]
     gain_ref[...] = gain_in[...]
     for quarter in (3, 1, 2, 0):
         pieces = weight_pieces[quarter]
@@ -874,18 +851,17 @@
     if len(outs) == 1:
         outs[0][...] = total.astype(BF16)
         return
-    vector_ref, other_ref, short_ref, long_ref = outs[0], outs[1], outs[-2], outs[-1]
+    vector_ref, other_ref, short_ref, long_ref, held_ref = outs[0], outs[1], *outs[-3:]
     short_ref[pl.ds(0, part), :] = total.astype(BF16)
-    rest = vector_ref[...]
-    pieces = []
-    for _ in range(3):
+    rest = vector_ref[0:3, :]
+    held_ref[...] = jnp.zeros_like(held_ref)
+    for index in range(3):
         piece = rest.astype(BF16).astype(F32)
-        pieces.append(piece)
+        held_ref[3 * index:3 * index + 3, :] = piece
         rest = rest - piece
-    pieces.append(jnp.zeros_like(rest))
-    short_ref[pl.ds(part, 32), :] = jnp.concatenate(pieces, axis=0).astype(BF16)
-    long_ref[pl.ds(0, part + 32), :] = short_ref[...]
-    long_ref[pl.ds(part + 32, part), :] = other_ref[...]
+    short_ref[pl.ds(part, 16), :] = held_ref[...].astype(BF16)
+    long_ref[pl.ds(0, part + 16), :] = short_ref[...]
+    long_ref[pl.ds(part + 16, part), :] = other_ref[...]
 
 
 def collect(parts, vector=None, other=None, after=()):
@@ -893,14 +869,17 @@
     operands = list(parts)
     if vector is None:
         counts = (part,)
+        scratch = []
     else:
         operands += [vector, other]
-        counts = (part + 32, 2 * part + 32)
+        counts = (part + 16, 2 * part + 16)
+        scratch = [pltpu.VMEM((16, width), F32)]
     return pl.pallas_call(
         functools.partial(collect_kernel, len(parts)),
         out_shape=tuple(jax.ShapeDtypeStruct((rows, width), BF16) for rows in counts),
         in_specs=[VMEM] * len(operands) + [ANY] * len(after),
         out_specs=tuple([VMEM] * len(counts)),
+        scratch_shapes=scratch,
         compiler_params=params(16),
         cost_estimate=COST,
         name="collect",
@@ -917,8 +896,8 @@
         held_ref[pl.ds(first, part), :] = up[pl.ds(0, part), :].astype(F32)
         start = down.shape[0] - part
         down_ref[pl.ds(first, part), :] = down[pl.ds(start, part), :].astype(F32)
-        rows = up[pl.ds(part, 32), :].astype(F32)
-        vectors.append((rows[0:8] + rows[8:16]) + rows[16:24])
+        rows = up[pl.ds(part, 16), :].astype(F32)
+        vectors.append((rows[0:3] + rows[3:6]) + rows[6:9])
     up_ref[...] = held_ref[...].T
     vector = (vectors[0] + vectors[1]) + (vectors[2] + vectors[3])
     gain_ref[...] = vector[0:1]
@@ -984,40 +963,34 @@
         ray_count, True, me, block_owner, tile_lists, opacity, tile_counts.reshape(1, rows),
         ray_pixel, gaussian_features,
     )
-    first = pack([mine] + arrivals, rendered)
-    x_part, y_part = beside(first, 1), beside(first, 2)
-    blocks = mix(rendered, partner(rendered_other), first)
+    half = depth // 2
+    low = pack([mine] + arrivals[:half - 1], rendered)
+    x_low, y_low = beside(low, 1), beside(low, 2)
+    high = pack(arrivals[half - 1:], low)
+    x_high, y_high = beside(high, 1), beside(high, 2)
+    d_low, d_high = beside(y_low, 1), beside(x_high, 2)
+    blocks = mix(rendered, partner(rendered_other), x_low, y_low, high)
     targets = [blocks[0]] + [along(blocks[shift], shift) for shift in range(1, depth)]
-    first_other = partner(first)
     tokens, normed, normed_t = prepare_tokens(
         ray_count, True, me, block_owner, ray_pixel, image_tokens,
-        layer_norm_gain.reshape(1, width), (blocks[0],),
-    )
-    act_first, slope_first, mixed = forward(normed_t, [first], [first_other])
-    passed_x, passed_y = turn(y_part, x_part, mixed, *targets[1:-1])
-    d_low, d_high = beside(passed_x, 1), beside(passed_y, 2)
-    x_part, y_part = tie(x_part, passed_x, passed_y), tie(y_part, passed_x, passed_y)
-    x_other, y_other = partner(x_part), partner(y_part)
-    act_next, slope_next, mixed = forward(
-        normed_t, [x_part, y_part], [x_other, y_other], mixed, after=targets[-1:]
-    )
-    d_low, d_high = tie(d_low, mixed), tie(d_high, mixed)
-    low_other, high_other = partner(d_low), partner(d_high)
+        layer_norm_gain.reshape(1, width),
+    )
+    most = pack([low, high, x_low, x_high, y_low, y_high], targets[half])
+    most_other = partner(most)
+    act_most, slope_most, mixed = forward(normed_t, [most], [most_other])
+    late = [target for shift, target in enumerate(targets) if shift not in (0, half)]
+    d_low, d_high = tie(d_low, mixed, *late), tie(d_high, mixed, *late)
+    d_low_other, d_high_other = partner(d_low), partner(d_high)
     act_last, slope_last, back, back_t, small = forward(
-        normed_t, [d_low, d_high], [low_other, high_other], mixed,
+        normed_t, [d_low, d_high], [d_low_other, d_high_other], mixed,
         (tokens, layer_scale.reshape(1, width), *targets),
     )
-    acts = (act_first, act_next, act_last)
-    slopes = (slope_first, slope_next, slope_last)
-    weights = (
-        (first, x_part, y_part, d_low, d_high),
-        (first_other, x_other, y_other, low_other, high_other),
-    )
-    low = d_low.shape[0]
-    act_pieces = (((0, 0, depth),), ((1, 0, depth),), ((1, depth, depth),), ((2, 0, depth),))
-    weight_pieces = (
-        ((0, 0, depth),), ((1, 0, depth),), ((2, 0, depth),), ((3, 0, low), (4, 0, depth - low))
-    )
+    acts = (act_most, act_last)
+    slopes = (slope_most, slope_last)
+    weights = ((most, d_low, d_high), (most_other, d_low_other, d_high_other))
+    act_pieces = tuple(((0, quarter * depth, depth),) for quarter in range(3))
+    act_pieces += (((1, 0, depth),),)
+    weight_pieces = act_pieces[:3] + (((1, 0, half), (2, 0, depth - half)),)
     gain = jnp.zeros((1, width), F32)
     (down_other,) = down_gradient(1, act_pieces, depth, acts, back)
     down_arrived = partner(down_other)

time: 158 us -> 153 us (0.968)
  the two profiles are of different devices: /device:TPU:8 before, /device:TPU:24 now
where the time goes in v8:
time: 153 us
  waiting for transfers between devices  64.9 us (42%)
  starting transfers between devices  50 us (33%)
  Pallas kernels  35.1 us (23%)
  local copies, waits for them, and re-layouts  2.12 us (1%)
    ppermute x19, waiting for transfers between devices, beside(): lax.ppermute(array, 'grp', [(g, g ^ flip) for g in range(group_count)])  37.3 us
    ppermute x19, starting transfers between devices, beside(): lax.ppermute(array, 'grp', [(g, g ^ flip) for g in range(group_count)])  23.2 us
    ppermute x12, starting transfers between devices, along(): return lax.ppermute(array, 'ray', pairs)  23.1 us
    ppermute x12, waiting for transfers between devices, along(): return lax.ppermute(array, 'ray', pairs)  17.2 us
    pallas_call x1, Pallas kernels, render(): pl.pallas_call(functools.partial(render_kernel, ray_count, relative), out...  11.7 us
    ppermute x9, waiting for transfers between devices, partner(): return lax.ppermute(array, 'ray', [(r, r ^ flip) for r in range(ray_count)])  10.5 us
    pallas_call x2, Pallas kernels, forward(): pl.pallas_call(functools.partial(forward_kernel, first, blocks, len(own),...  8.21 us
    pallas_call x2, Pallas kernels, up_gradient(): pl.pallas_call(functools.partial(up_grad_kernel, side, weight_pieces, act...  6.06 us
  transfers between devices with their start and end apart: 40, of which 24 were waited for; matrix products, arithmetic and copies ran while one was open for 0% of the time, Pallas kernels for 18%

profile of v8, /device:TPU:24, one launch (start us, length us, event | category | flops | bytes accessed | tf_op | source)
XLA Modules:
  0.0 153.1 jit_solution(5789947000479809372)
XLA Ops:
  3.6 3.4 %collective-permute-start.2 = (bf16[2,64,1024]{2,1,0:T(8,128)(2,1)S(1)}, bf16[2,64,1024]{2,1,0:T(8,128)(2,1)S(1)}, u32[]{:S(2)}, u32[]{:S(2)}) collective-permute-start(bf16[2,64,1024]{2,1,0:T(8,128)(2,1)S(1)} %quarter.1.refs_0_), channel_id=1, source_target_pairs={{0,2},{1,3},{2,4},{3,5},{4,6},{5,7},{6,0},{7,1},{8,10},{9,11},{10,... | collective-permute-start | bytes 786440 | tf_op jit(solution)/shard_map/ppermute | solution.py:958
  7.1 11.7 %render.1 = (bf16[4,64,1024]{2,1,0:T(8,128)(2,1)S(1)}, bf16[4,64,1024]{2,1,0:T(8,128)(2,1)S(1)}) custom-call(s32[1]{0:T(128)} %bitcast.1.me_ref, s32[1,8]{1,0:T(1,128)S(1)} %copy-done.7, s32[32,512]{1,0:T(8,128)S(1)} %copy-done.3, f32[32,512]{1,0:T(8,128)S(1)} %copy-done.4, s32[1,512]{1,0:T(1,128)S(1)} %bitcast.11, s32[1,4096]{1,0:T(1,128)S(1)} %copy-done.2, ...), custom_call_target="tpu_custom_call" | custom-call | flops 1048576 | bytes 65536 | tf_op jit(solution)/shard_map/render/pallas_call | solution.py:146
  18.9 1.6 %collective-permute-start.5 = (bf16[2,2,64,1024]{3,2,1,0:T(8,128)(2,1)S(1)}, bf16[2,2,64,1024]{3,2,1,0:T(8,128)(2,1)S(1)}, u32[]{:S(2)}, u32[]{:S(2)}) collective-permute-start(bf16[2,2,64,1024]{3,2,1,0:T(8,128)(2,1)S(1)} %pack.3.refs_2_.refs_0_), channel_id=1, source_target_pairs={{0,16},{8,24},{16,0},{24,8},{1,17},{9,25},{17,1},{25,9},{2,18},{10... | collective-permute-start | bytes 1572872 | tf_op jit(solution)/shard_map/ppermute | solution.py:951
  20.5 1.5 collective-permute-start.3
  22.0 2.5 %collective-permute-done.1.refs_0_ = bf16[2,64,1024]{2,1,0:T(8,128)(2,1)S(1)} collective-permute-done((bf16[2,64,1024]{2,1,0:T(8,128)(2,1)S(1)}, bf16[2,64,1024]{2,1,0:T(8,128)(2,1)S(1)}, u32[]{:S(2)}, u32[]{:S(2)}) %collective-permute-start.1) | collective-permute-done | bytes 262176 | tf_op jit(solution)/shard_map/ppermute | solution.py:958
  24.5 1.6 %collective-permute-start.4 = (bf16[2,2,64,1024]{3,2,1,0:T(8,128)(2,1)S(1)}, bf16[2,2,64,1024]{3,2,1,0:T(8,128)(2,1)S(1)}, u32[]{:S(2)}, u32[]{:S(2)}) collective-permute-start(bf16[2,2,64,1024]{3,2,1,0:T(8,128)(2,1)S(1)} %pack.4.refs_4_.refs_1_), channel_id=1, source_target_pairs={{0,8},{8,0},{16,24},{24,16},{1,9},{9,1},{17,25},{25,17},{2,10},{10... | collective-permute-start | bytes 1572872 | tf_op jit(solution)/shard_map/ppermute | solution.py:951
  26.1 1.5 collective-permute-start.6
  27.6 6.1 %collective-permute-done.5.refs_3_.refs_4_ = bf16[2,2,64,1024]{3,2,1,0:T(8,128)(2,1)S(1)} collective-permute-done((bf16[2,2,64,1024]{3,2,1,0:T(8,128)(2,1)S(1)}, bf16[2,2,64,1024]{3,2,1,0:T(8,128)(2,1)S(1)}, u32[]{:S(2)}, u32[]{:S(2)}) %collective-permute-start.5) | collective-permute-done | bytes 524320 | tf_op jit(solution)/shard_map/ppermute | solution.py:951
  33.7 1.6 %collective-permute-done.3.refs_2_ = bf16[2,2,64,1024]{3,2,1,0:T(8,128)(2,1)S(1)} collective-permute-done((bf16[2,2,64,1024]{3,2,1,0:T(8,128)(2,1)S(1)}, bf16[2,2,64,1024]{3,2,1,0:T(8,128)(2,1)S(1)}, u32[]{:S(2)}, u32[]{:S(2)}) %collective-permute-start.3) | collective-permute-done | bytes 524320 | tf_op jit(solution)/shard_map/ppermute | solution.py:951
  35.4 5.2 %collective-permute-start.8 = (bf16[2,64,1024]{2,1,0:T(8,128)(2,1)S(1)}, bf16[2,64,1024]{2,1,0:T(8,128)(2,1)S(1)}, u32[]{:S(2)}, u32[]{:S(2)}) collective-permute-start(bf16[2,64,1024]{2,1,0:T(8,128)(2,1)S(1)} %get-tuple-element.56), channel_id=1, source_target_pairs={{0,4},{1,5},{2,6},{3,7},{4,0},{5,1},{6,2},{7,3},{8,12},{9,13},{10,... | collective-permute-start | bytes 786440 | tf_op jit(solution)/shard_map/ppermute | solution.py:958
  40.6 5.2 %collective-permute-done.4.refs_3_ = bf16[2,2,64,1024]{3,2,1,0:T(8,128)(2,1)S(1)} collective-permute-done((bf16[2,2,64,1024]{3,2,1,0:T(8,128)(2,1)S(1)}, bf16[2,2,64,1024]{3,2,1,0:T(8,128)(2,1)S(1)}, u32[]{:S(2)}, u32[]{:S(2)}) %collective-permute-start.4) | collective-permute-done | bytes 524320 | tf_op jit(solution)/shard_map/ppermute | solution.py:951
  45.8 3.0 %collective-permute-done.8.refs_6_.refs_10_ = bf16[2,64,1024]{2,1,0:T(8,128)(2,1)S(1)} collective-permute-done((bf16[2,64,1024]{2,1,0:T(8,128)(2,1)S(1)}, bf16[2,64,1024]{2,1,0:T(8,128)(2,1)S(1)}, u32[]{:S(2)}, u32[]{:S(2)}) %collective-permute-start.8) | collective-permute-done | bytes 262176 | tf_op jit(solution)/shard_map/ppermute | solution.py:958
  53.3 3.2 %tokens.1 = (bf16[512,1024]{1,0:T(8,128)(2,1)S(1)}, bf16[512,1024]{1,0:T(8,128)(2,1)S(1)}, bf16[1024,512]{1,0:T(8,128)(2,1)S(1)}) custom-call(s32[1]{0:T(128)} %bitcast.1.me_ref, s32[1,8]{1,0:T(1,128)S(1)} %copy-done.7, s32[1,4096]{1,0:T(1,128)S(1)} %copy-done.2, bf16[512,1024]{1,0:T(8,128)(2,1)S(1)} %copy-done.1, f32[1,1024]{1,0:T(1,128)S(1)} %bitcast.8), custom_call_target="tpu_custom_call" | custom-call | flops 1048576 | bytes 65536 | tf_op jit(solution)/shard_map/tokens/pallas_call | solution.py:232
  56.5 4.3 %forward.2 = (bf16[2,12,64,512]{3,2,1,0:T(8,128)(2,1)S(1)}, f32[2,12,64,512]{3,2,1,0:T(8,128)S(1)}, f32[512,1024]{1,0:T(8,128)S(1)}) custom-call(bf16[1024,512]{1,0:T(8,128)(2,1)S(1)} %get-tuple-element.57.refs_0_, bf16[12,2,64,1024]{3,2,1,0:T(8,128)(2,1)S(1)} %pack.5.refs_1_.refs_0_, bf16[12,2,64,1024]{3,2,1,0:T(8,128)(2,1)S(1)} %collective-permute-done.10.refs_2_.refs_0_), custom_call_target="tpu_custom_call" | custom-call | flops 1048576 | bytes 65536 | tf_op jit(solution)/shard_map/forward/pallas_call | solution.py:618
  60.8 4.1 %collective-permute-done.11.refs_2_.refs_9_ = bf16[2,64,1024]{2,1,0:T(8,128)(2,1)S(1)} collective-permute-done((bf16[2,64,1024]{2,1,0:T(8,128)(2,1)S(1)}, bf16[2,64,1024]{2,1,0:T(8,128)(2,1)S(1)}, u32[]{:S(2)}, u32[]{:S(2)}) %collective-permute-start.11) | collective-permute-done | bytes 262176 | tf_op jit(solution)/shard_map/ppermute | solution.py:958
  67.7 3.9 %forward.3 = (bf16[2,4,64,512]{3,2,1,0:T(8,128)(2,1)S(1)}, f32[2,4,64,512]{3,2,1,0:T(8,128)S(1)}, bf16[512,1024]{1,0:T(8,128)(2,1)S(1)}, bf16[1024,512]{1,0:T(8,128)(2,1)S(1)}, f32[8,1024]{1,0:T(8,128)S(1)}) custom-call(bf16[1024,512]{1,0:T(8,128)(2,1)S(1)} %get-tuple-element.57.refs_0_, bf16[2,2,64,1024]{3,2,1,0:T(8,128)(2,1)S(1)} %tie.2.refs_1_, ...), custom_call_target="tpu_custom_call" | custom-call | flops 1048576 | bytes 65536 | tf_op jit(solution)/shard_map/forward/pallas_call | solution.py:618
  73.1 2.8 %up_gradient.2 = (bf16[4,4,64,1024]{3,2,1,0:T(8,128)(2,1)S(1)}, f32[1,1024]{1,0:T(1,128)S(1)}) custom-call(bf16[12,2,64,1024]{3,2,1,0:T(8,128)(2,1)S(1)} %collective-permute-done.10.refs_2_.refs_0_, bf16[2,2,64,1024]{3,2,1,0:T(8,128)(2,1)S(1)} %collective-permute-done.14.refs_3_.refs_1_, ...), custom_call_target="tpu_custom_call" | custom-call | flops 1048576 | bytes 65536 | tf_op jit(solution)/shard_map/up_gradient/pallas_call | solution.py:790
  80.5 3.3 %up_gradient.3 = (bf16[4,64,1024]{2,1,0:T(8,128)(2,1)S(1)}, bf16[4,64,1024]{2,1,0:T(8,128)(2,1)S(1)}, bf16[4,64,1024]{2,1,0:T(8,128)(2,1)S(1)}, bf16[2,64,1024]{...) custom-call(bf16[12,2,64,1024]{3,2,1,0:T(8,128)(2,1)S(1)} %pack.5.refs_1_.refs_0_, ...), custom_call_target="tpu_custom_call" | custom-call | flops 1048576 | bytes 65536 | tf_op jit(solution)/shard_map/up_gradient/pallas_call | solution.py:790
  83.8 1.6 %collective-permute-start.17 = (bf16[4,64,1024]{2,1,0:T(8,128)(2,1)S(1)}, bf16[4,64,1024]{2,1,0:T(8,128)(2,1)S(1)}, u32[]{:S(2)}, u32[]{:S(2)}) collective-permute-start(bf16[4,64,1024]{2,1,0:T(8,128)(2,1)S(1)} %get-tuple-element.71), channel_id=1, source_target_pairs={{0,8},{8,0},{16,24},{24,16},{1,9},{9,1},{17,25},{25,17},{2,10},{10... | collective-permute-start | bytes 1572872 | tf_op jit(solution)/shard_map/ppermute | solution.py:951
  86.0 7.4 %collective-permute-done.28.x_ref = bf16[4,64,1024]{2,1,0:T(8,128)(2,1)S(1)} collective-permute-done((bf16[4,64,1024]{2,1,0:T(8,128)(2,1)S(1)}, bf16[4,64,1024]{2,1,0:T(8,128)(2,1)S(1)}, u32[]{:S(2)}, u32[]{:S(2)}) %collective-permute-start.28) | collective-permute-done | bytes 524320 | tf_op jit(solution)/shard_map/ppermute | solution.py:951
  94.1 1.6 %collective-permute-start.30 = (bf16[2,64,1024]{2,1,0:T(8,128)(2,1)S(1)}, bf16[2,64,1024]{2,1,0:T(8,128)(2,1)S(1)}, u32[]{:S(2)}, u32[]{:S(2)}) collective-permute-start(bf16[2,64,1024]{2,1,0:T(8,128)(2,1)S(1)} %get-tuple-element.90), channel_id=1, source_target_pairs={{0,8},{8,0},{16,24},{24,16},{1,9},{9,1},{17,25},{25,17},{2,10},{10... | collective-permute-start | bytes 786440 | tf_op jit(solution)/shard_map/ppermute | solution.py:951
  99.2 2.9 %collective-permute-done.20 = f32[8,1024]{1,0:T(8,128)S(1)} collective-permute-done((f32[8,1024]{1,0:T(8,128)S(1)}, f32[8,1024]{1,0:T(8,128)S(1)}, u32[]{:S(2)}, u32[]{:S(2)}) %collective-permute-start.20) | collective-permute-done | bytes 32800 | tf_op jit(solution)/shard_map/ppermute | solution.py:954
  103.6 3.4 %collective-permute-done.21 = f32[8,1024]{1,0:T(8,128)S(1)} collective-permute-done((f32[8,1024]{1,0:T(8,128)S(1)}, f32[8,1024]{1,0:T(8,128)S(1)}, u32[]{:S(2)}, u32[]{:S(2)}) %collective-permute-start.21) | collective-permute-done | bytes 32800 | tf_op jit(solution)/shard_map/ppermute | solution.py:954
  108.4 1.8 %collective-permute-done.30.x_late_ref = bf16[2,64,1024]{2,1,0:T(8,128)(2,1)S(1)} collective-permute-done((bf16[2,64,1024]{2,1,0:T(8,128)(2,1)S(1)}, bf16[2,64,1024]{2,1,0:T(8,128)(2,1)S(1)}, u32[]{:S(2)}, u32[]{:S(2)}) %collective-permute-start.30) | collective-permute-done | bytes 262176 | tf_op jit(solution)/shard_map/ppermute | solution.py:951
  111.9 1.5 collective-permute-start.33
  115.5 2.1 %collective-permute-start.24 = (bf16[64,1024]{1,0:T(8,128)(2,1)S(1)}, bf16[64,1024]{1,0:T(8,128)(2,1)S(1)}, u32[]{:S(2)}, u32[]{:S(2)}) collective-permute-start(bf16[64,1024]{1,0:T(8,128)(2,1)S(1)} %get-tuple-element.79), channel_id=1, source_target_pairs={{0,2},{1,3},{2,4},{3,5},{4,6},{5,7},{6,0},{7,1},{8,10},{9,11},{10,... | collective-permute-start | bytes 393224 | tf_op jit(solution)/shard_map/ppermute | solution.py:958
  118.7 5.9 %collective-permute-start.26 = (bf16[64,1024]{1,0:T(8,128)(2,1)S(1)}, bf16[64,1024]{1,0:T(8,128)(2,1)S(1)}, u32[]{:S(2)}, u32[]{:S(2)}) collective-permute-start(bf16[64,1024]{1,0:T(8,128)(2,1)S(1)} %get-tuple-element.81), channel_id=1, source_target_pairs={{0,6},{1,7},{2,0},{3,1},{4,2},{5,3},{6,4},{7,5},{8,14},{9,15},{10,... | collective-permute-start | bytes 393224 | tf_op jit(solution)/shard_map/ppermute | solution.py:958
  124.7 6.1 %collective-permute-done.33.refs_2_ = bf16[64,1024]{1,0:T(8,128)(2,1)S(1)} collective-permute-done((bf16[64,1024]{1,0:T(8,128)(2,1)S(1)}, bf16[64,1024]{1,0:T(8,128)(2,1)S(1)}, u32[]{:S(2)}, u32[]{:S(2)}) %collective-permute-start.33) | collective-permute-done | bytes 131104 | tf_op jit(solution)/shard_map/ppermute | solution.py:958
  135.9 5.2 %collective-permute-done.36.refs_7_.refs_6_ = bf16[64,1024]{1,0:T(8,128)(2,1)S(1)} collective-permute-done((bf16[64,1024]{1,0:T(8,128)(2,1)S(1)}, bf16[64,1024]{1,0:T(8,128)(2,1)S(1)}, u32[]{:S(2)}, u32[]{:S(2)}) %collective-permute-start.36) | collective-permute-done | bytes 131104 | tf_op jit(solution)/shard_map/ppermute | solution.py:951
  142.6 2.3 %collective-permute-start.37 = (bf16[80,1024]{1,0:T(8,128)(2,1)S(1)}, bf16[80,1024]{1,0:T(8,128)(2,1)S(1)}, u32[]{:S(2)}, u32[]{:S(2)}) collective-permute-start(bf16[80,1024]{1,0:T(8,128)(2,1)S(1)} %get-tuple-element.96.refs_0_), channel_id=1, source_target_pairs={{0,8},{8,0},{16,24},{24,16},{1,9},{9,1},{17,25},{25,17},{2,10},{10... | collective-permute-start | bytes 491528 | tf_op jit(solution)/shard_map/ppermute | solution.py:951
  144.9 6.5 %collective-permute-done.37.refs_1_ = bf16[80,1024]{1,0:T(8,128)(2,1)S(1)} collective-permute-done((bf16[80,1024]{1,0:T(8,128)(2,1)S(1)}, bf16[80,1024]{1,0:T(8,128)(2,1)S(1)}, u32[]{:S(2)}, u32[]{:S(2)}) %collective-permute-start.37) | collective-permute-done | bytes 163872 | tf_op jit(solution)/shard_map/ppermute | solution.py:951
  151.4 1.7 %place.1 = (f32[1024,256]{1,0:T(8,128)}, f32[256,1024]{1,0:T(8,128)}, f32[1,1024]{1,0:T(1,128)}, f32[1,1024]{1,0:T(1,128)}, f32[1,1]{1,0:T(1,128)}) custom-call(s32[1]{0:T(128)} %bitcast.group_ref, bf16[80,1024]{1,0:T(8,128)(2,1)S(1)} %get-tuple-element.96.refs_0_, bf16[80,1024]{1,0:T(8,128)(2,1)S(1)} %collective-permute-done.37.refs_1_, ...), custom_call_target="tpu_custom_call" | custom-call | flops 1048576 | bytes 65536 | tf_op jit(solution)/shard_map/place/pallas_call | solution.py:917
  (96 shorter events, 35.6 us)
Async XLA Ops:
  3.1 15.7 %collective-permute-start = (bf16[2,64,1024]{2,1,0:T(8,128)(2,1)S(1)}, bf16[2,64,1024]{2,1,0:T(8,128)(2,1)S(1)}, u32[]{:S(2)}, u32[]{:S(2)}) collective-permute-start(bf16[2,64,1024]{2,1,0:T(8,128)(2,1)S(1)} %quarter.1.refs_0_), channel_id=1, source_target_pairs={{0,6},{1,7},{2,0},{3,1},{4,2},{5,3},{6,4},{7,5},{8,14},{9,15},{10,... | collective-permute-start | bytes 786440 | tf_op jit(solution)/shard_map/ppermute | solution.py:958
  3.6 20.8 %collective-permute-start.1 = (bf16[2,64,1024]{2,1,0:T(8,128)(2,1)S(1)}, bf16[2,64,1024]{2,1,0:T(8,128)(2,1)S(1)}, u32[]{:S(2)}, u32[]{:S(2)}) collective-permute-start(bf16[2,64,1024]{2,1,0:T(8,128)(2,1)S(1)} %quarter.1.refs_0_), channel_id=1, source_target_pairs={{0,4},{1,5},{2,6},{3,7},{4,0},{5,1},{6,2},{7,3},{8,12},{9,13},{10,... | collective-permute-start | bytes 786440 | tf_op jit(solution)/shard_map/ppermute | solution.py:958
  3.6 20.8 %collective-permute-start.2 = (bf16[2,64,1024]{2,1,0:T(8,128)(2,1)S(1)}, bf16[2,64,1024]{2,1,0:T(8,128)(2,1)S(1)}, u32[]{:S(2)}, u32[]{:S(2)}) collective-permute-start(bf16[2,64,1024]{2,1,0:T(8,128)(2,1)S(1)} %quarter.1.refs_0_), channel_id=1, source_target_pairs={{0,2},{1,3},{2,4},{3,5},{4,6},{5,7},{6,0},{7,1},{8,10},{9,11},{10,... | collective-permute-start | bytes 786440 | tf_op jit(solution)/shard_map/ppermute | solution.py:958
  18.8 8.8 %collective-permute-start.7 = (bf16[4,64,1024]{2,1,0:T(8,128)(2,1)S(1)}, bf16[4,64,1024]{2,1,0:T(8,128)(2,1)S(1)}, u32[]{:S(2)}, u32[]{:S(2)}) collective-permute-start(bf16[4,64,1024]{2,1,0:T(8,128)(2,1)S(1)} %get-tuple-element.55), channel_id=1, source_target_pairs={{0,1},{1,0},{2,3},{3,2},{4,5},{5,4},{6,7},{7,6},{8,9},{9,8},{10,11... | collective-permute-start | bytes 1572872 | tf_op jit(solution)/shard_map/ppermute | solution.py:954
  18.9 14.8 %collective-permute-start.5 = (bf16[2,2,64,1024]{3,2,1,0:T(8,128)(2,1)S(1)}, bf16[2,2,64,1024]{3,2,1,0:T(8,128)(2,1)S(1)}, u32[]{:S(2)}, u32[]{:S(2)}) collective-permute-start(bf16[2,2,64,1024]{3,2,1,0:T(8,128)(2,1)S(1)} %pack.3.refs_2_.refs_0_), channel_id=1, source_target_pairs={{0,16},{8,24},{16,0},{24,8},{1,17},{9,25},{17,1},{25,9},{2,18},{10... | collective-permute-start | bytes 1572872 | tf_op jit(solution)/shard_map/ppermute | solution.py:951
  20.5 14.8 %collective-permute-start.3 = (bf16[2,2,64,1024]{3,2,1,0:T(8,128)(2,1)S(1)}, bf16[2,2,64,1024]{3,2,1,0:T(8,128)(2,1)S(1)}, u32[]{:S(2)}, u32[]{:S(2)}) collective-permute-start(bf16[2,2,64,1024]{3,2,1,0:T(8,128)(2,1)S(1)} %pack.3.refs_2_.refs_0_), channel_id=1, source_target_pairs={{0,8},{8,0},{16,24},{24,16},{1,9},{9,1},{17,25},{25,17},{2,10},{10... | collective-permute-start | bytes 1572872 | tf_op jit(solution)/shard_map/ppermute | solution.py:951
  24.5 21.3 %collective-permute-start.4 = (bf16[2,2,64,1024]{3,2,1,0:T(8,128)(2,1)S(1)}, bf16[2,2,64,1024]{3,2,1,0:T(8,128)(2,1)S(1)}, u32[]{:S(2)}, u32[]{:S(2)}) collective-permute-start(bf16[2,2,64,1024]{3,2,1,0:T(8,128)(2,1)S(1)} %pack.4.refs_4_.refs_1_), channel_id=1, source_target_pairs={{0,8},{8,0},{16,24},{24,16},{1,9},{9,1},{17,25},{25,17},{2,10},{10... | collective-permute-start | bytes 1572872 | tf_op jit(solution)/shard_map/ppermute | solution.py:951
  26.1 19.7 %collective-permute-start.6 = (bf16[2,2,64,1024]{3,2,1,0:T(8,128)(2,1)S(1)}, bf16[2,2,64,1024]{3,2,1,0:T(8,128)(2,1)S(1)}, u32[]{:S(2)}, u32[]{:S(2)}) collective-permute-start(bf16[2,2,64,1024]{3,2,1,0:T(8,128)(2,1)S(1)} %pack.4.refs_4_.refs_1_), channel_id=1, source_target_pairs={{0,16},{8,24},{16,0},{24,8},{1,17},{9,25},{17,1},{25,9},{2,18},{10... | collective-permute-start | bytes 1572872 | tf_op jit(solution)/shard_map/ppermute | solution.py:951
  35.4 13.4 %collective-permute-start.8 = (bf16[2,64,1024]{2,1,0:T(8,128)(2,1)S(1)}, bf16[2,64,1024]{2,1,0:T(8,128)(2,1)S(1)}, u32[]{:S(2)}, u32[]{:S(2)}) collective-permute-start(bf16[2,64,1024]{2,1,0:T(8,128)(2,1)S(1)} %get-tuple-element.56), channel_id=1, source_target_pairs={{0,4},{1,5},{2,6},{3,7},{4,0},{5,1},{6,2},{7,3},{8,12},{9,13},{10,... | collective-permute-start | bytes 786440 | tf_op jit(solution)/shard_map/ppermute | solution.py:958
  49.0 7.5 %collective-permute-start.10 = (bf16[12,2,64,1024]{3,2,1,0:T(8,128)(2,1)S(1)}, bf16[12,2,64,1024]{3,2,1,0:T(8,128)(2,1)S(1)}, u32[]{:S(2)}, u32[]{:S(2)}) collective-permute-start(bf16[12,2,64,1024]{3,2,1,0:T(8,128)(2,1)S(1)} %pack.5.refs_1_.refs_0_), channel_id=1, source_target_pairs={{0,1},{1,0},{2,3},{3,2},{4,5},{5,4},{6,7},{7,6},{8,9},{9,8},{10,11... | collective-permute-start | bytes 9437192 | tf_op jit(solution)/shard_map/ppermute | solution.py:954
  49.1 15.9 %collective-permute-start.13 = (bf16[2,2,64,1024]{3,2,1,0:T(8,128)(2,1)S(1)}, bf16[2,2,64,1024]{3,2,1,0:T(8,128)(2,1)S(1)}, u32[]{:S(2)}, u32[]{:S(2)}) collective-permute-start(bf16[2,2,64,1024]{3,2,1,0:T(8,128)(2,1)S(1)} %collective-permute-done.4.refs_3_), channel_id=1, source_target_pairs={{0,16},{8,24},{16,0},{24,8},{1,17},{9,25},{17,1},{25,9},{2,18},{10... | collective-permute-start | bytes 1572872 | tf_op jit(solution)/shard_map/ppermute | solution.py:951
  49.8 15.3 %collective-permute-start.9 = (bf16[2,2,64,1024]{3,2,1,0:T(8,128)(2,1)S(1)}, bf16[2,2,64,1024]{3,2,1,0:T(8,128)(2,1)S(1)}, u32[]{:S(2)}, u32[]{:S(2)}) collective-permute-start(bf16[2,2,64,1024]{3,2,1,0:T(8,128)(2,1)S(1)} %collective-permute-done.5.refs_3_.refs_4_), channel_id=1, source_target_pairs={{0,8},{8,0},{16,24},{24,16},{1,9},{9,1},{17,25},{25,17},{2,10},{10... | collective-permute-start | bytes 1572872 | tf_op jit(solution)/shard_map/ppermute | solution.py:951
  51.3 13.7 %collective-permute-start.11 = (bf16[2,64,1024]{2,1,0:T(8,128)(2,1)S(1)}, bf16[2,64,1024]{2,1,0:T(8,128)(2,1)S(1)}, u32[]{:S(2)}, u32[]{:S(2)}) collective-permute-start(bf16[2,64,1024]{2,1,0:T(8,128)(2,1)S(1)} %get-tuple-element.59), channel_id=1, source_target_pairs={{0,2},{1,3},{2,4},{3,5},{4,6},{5,7},{6,0},{7,1},{8,10},{9,11},{10,... | collective-permute-start | bytes 786440 | tf_op jit(solution)/shard_map/ppermute | solution.py:958
  52.3 12.7 %collective-permute-start.12 = (bf16[2,64,1024]{2,1,0:T(8,128)(2,1)S(1)}, bf16[2,64,1024]{2,1,0:T(8,128)(2,1)S(1)}, u32[]{:S(2)}, u32[]{:S(2)}) collective-permute-start(bf16[2,64,1024]{2,1,0:T(8,128)(2,1)S(1)} %get-tuple-element.60), channel_id=1, source_target_pairs={{0,6},{1,7},{2,0},{3,1},{4,2},{5,3},{6,4},{7,5},{8,14},{9,15},{10,... | collective-permute-start | bytes 786440 | tf_op jit(solution)/shard_map/ppermute | solution.py:958
  78.5 14.8 %collective-permute-start.28 = (bf16[4,64,1024]{2,1,0:T(8,128)(2,1)S(1)}, bf16[4,64,1024]{2,1,0:T(8,128)(2,1)S(1)}, u32[]{:S(2)}, u32[]{:S(2)}) collective-permute-start(bf16[4,64,1024]{2,1,0:T(8,128)(2,1)S(1)} %get-tuple-element.86), channel_id=1, source_target_pairs={{0,8},{8,0},{16,24},{24,16},{1,9},{9,1},{17,25},{25,17},{2,10},{10... | collective-permute-start | bytes 1572872 | tf_op jit(solution)/shard_map/ppermute | solution.py:951
  79.1 14.8 %collective-permute-start.29 = (bf16[4,64,1024]{2,1,0:T(8,128)(2,1)S(1)}, bf16[4,64,1024]{2,1,0:T(8,128)(2,1)S(1)}, u32[]{:S(2)}, u32[]{:S(2)}) collective-permute-start(bf16[4,64,1024]{2,1,0:T(8,128)(2,1)S(1)} %get-tuple-element.87), channel_id=1, source_target_pairs={{0,16},{8,24},{16,0},{24,8},{1,17},{9,25},{17,1},{25,9},{2,18},{10... | collective-permute-start | bytes 1572872 | tf_op jit(solution)/shard_map/ppermute | solution.py:951
  83.8 23.2 %collective-permute-start.17 = (bf16[4,64,1024]{2,1,0:T(8,128)(2,1)S(1)}, bf16[4,64,1024]{2,1,0:T(8,128)(2,1)S(1)}, u32[]{:S(2)}, u32[]{:S(2)}) collective-permute-start(bf16[4,64,1024]{2,1,0:T(8,128)(2,1)S(1)} %get-tuple-element.71), channel_id=1, source_target_pairs={{0,8},{8,0},{16,24},{24,16},{1,9},{9,1},{17,25},{25,17},{2,10},{10... | collective-permute-start | bytes 1572872 | tf_op jit(solution)/shard_map/ppermute | solution.py:951
  85.4 21.6 %collective-permute-start.18 = (bf16[4,64,1024]{2,1,0:T(8,128)(2,1)S(1)}, bf16[4,64,1024]{2,1,0:T(8,128)(2,1)S(1)}, u32[]{:S(2)}, u32[]{:S(2)}) collective-permute-start(bf16[4,64,1024]{2,1,0:T(8,128)(2,1)S(1)} %get-tuple-element.72), channel_id=1, source_target_pairs={{0,16},{8,24},{16,0},{24,8},{1,17},{9,25},{17,1},{25,9},{2,18},{10... | collective-permute-start | bytes 1572872 | tf_op jit(solution)/shard_map/ppermute | solution.py:951
  94.1 16.1 %collective-permute-start.30 = (bf16[2,64,1024]{2,1,0:T(8,128)(2,1)S(1)}, bf16[2,64,1024]{2,1,0:T(8,128)(2,1)S(1)}, u32[]{:S(2)}, u32[]{:S(2)}) collective-permute-start(bf16[2,64,1024]{2,1,0:T(8,128)(2,1)S(1)} %get-tuple-element.90), channel_id=1, source_target_pairs={{0,8},{8,0},{16,24},{24,16},{1,9},{9,1},{17,25},{25,17},{2,10},{10... | collective-permute-start | bytes 786440 | tf_op jit(solution)/shard_map/ppermute | solution.py:951
  95.6 15.2 %collective-permute-start.31 = (bf16[2,64,1024]{2,1,0:T(8,128)(2,1)S(1)}, bf16[2,64,1024]{2,1,0:T(8,128)(2,1)S(1)}, u32[]{:S(2)}, u32[]{:S(2)}) collective-permute-start(bf16[2,64,1024]{2,1,0:T(8,128)(2,1)S(1)} %get-tuple-element.91), channel_id=1, source_target_pairs={{0,16},{8,24},{16,0},{24,8},{1,17},{9,25},{17,1},{25,9},{2,18},{10... | collective-permute-start | bytes 786440 | tf_op jit(solution)/shard_map/ppermute | solution.py:951
  107.1 7.9 %collective-permute-start.22 = (bf16[2,64,1024]{2,1,0:T(8,128)(2,1)S(1)}, bf16[2,64,1024]{2,1,0:T(8,128)(2,1)S(1)}, u32[]{:S(2)}, u32[]{:S(2)}) collective-permute-start(bf16[2,64,1024]{2,1,0:T(8,128)(2,1)S(1)} %get-tuple-element.76), channel_id=1, source_target_pairs={{0,8},{8,0},{16,24},{24,16},{1,9},{9,1},{17,25},{25,17},{2,10},{10... | collective-permute-start | bytes 786440 | tf_op jit(solution)/shard_map/ppermute | solution.py:951
  107.7 7.5 %collective-permute-start.23 = (bf16[2,64,1024]{2,1,0:T(8,128)(2,1)S(1)}, bf16[2,64,1024]{2,1,0:T(8,128)(2,1)S(1)}, u32[]{:S(2)}, u32[]{:S(2)}) collective-permute-start(bf16[2,64,1024]{2,1,0:T(8,128)(2,1)S(1)} %get-tuple-element.77), channel_id=1, source_target_pairs={{0,16},{8,24},{16,0},{24,8},{1,17},{9,25},{17,1},{25,9},{2,18},{10... | collective-permute-start | bytes 786440 | tf_op jit(solution)/shard_map/ppermute | solution.py:951
  111.0 7.7 %collective-permute-start.32 = (bf16[64,1024]{1,0:T(8,128)(2,1)S(1)}, bf16[64,1024]{1,0:T(8,128)(2,1)S(1)}, u32[]{:S(2)}, u32[]{:S(2)}) collective-permute-start(bf16[64,1024]{1,0:T(8,128)(2,1)S(1)} %get-tuple-element.93), channel_id=1, source_target_pairs={{0,2},{1,3},{2,4},{3,5},{4,6},{5,7},{6,0},{7,1},{8,10},{9,11},{10,... | collective-permute-start | bytes 393224 | tf_op jit(solution)/shard_map/ppermute | solution.py:958
  111.9 18.9 %collective-permute-start.33 = (bf16[64,1024]{1,0:T(8,128)(2,1)S(1)}, bf16[64,1024]{1,0:T(8,128)(2,1)S(1)}, u32[]{:S(2)}, u32[]{:S(2)}) collective-permute-start(bf16[64,1024]{1,0:T(8,128)(2,1)S(1)} %get-tuple-element.94), channel_id=1, source_target_pairs={{0,4},{1,5},{2,6},{3,7},{4,0},{5,1},{6,2},{7,3},{8,12},{9,13},{10,... | collective-permute-start | bytes 393224 | tf_op jit(solution)/shard_map/ppermute | solution.py:958
  113.5 17.3 %collective-permute-start.34 = (bf16[64,1024]{1,0:T(8,128)(2,1)S(1)}, bf16[64,1024]{1,0:T(8,128)(2,1)S(1)}, u32[]{:S(2)}, u32[]{:S(2)}) collective-permute-start(bf16[64,1024]{1,0:T(8,128)(2,1)S(1)} %get-tuple-element.95), channel_id=1, source_target_pairs={{0,6},{1,7},{2,0},{3,1},{4,2},{5,3},{6,4},{7,5},{8,14},{9,15},{10,... | collective-permute-start | bytes 393224 | tf_op jit(solution)/shard_map/ppermute | solution.py:958
  115.5 18.3 %collective-permute-start.24 = (bf16[64,1024]{1,0:T(8,128)(2,1)S(1)}, bf16[64,1024]{1,0:T(8,128)(2,1)S(1)}, u32[]{:S(2)}, u32[]{:S(2)}) collective-permute-start(bf16[64,1024]{1,0:T(8,128)(2,1)S(1)} %get-tuple-element.79), channel_id=1, source_target_pairs={{0,2},{1,3},{2,4},{3,5},{4,6},{5,7},{6,0},{7,1},{8,10},{9,11},{10,... | collective-permute-start | bytes 393224 | tf_op jit(solution)/shard_map/ppermute | solution.py:958
  117.5 16.9 %collective-permute-start.25 = (bf16[64,1024]{1,0:T(8,128)(2,1)S(1)}, bf16[64,1024]{1,0:T(8,128)(2,1)S(1)}, u32[]{:S(2)}, u32[]{:S(2)}) collective-permute-start(bf16[64,1024]{1,0:T(8,128)(2,1)S(1)} %get-tuple-element.80), channel_id=1, source_target_pairs={{0,4},{1,5},{2,6},{3,7},{4,0},{5,1},{6,2},{7,3},{8,12},{9,13},{10,... | collective-permute-start | bytes 393224 | tf_op jit(solution)/shard_map/ppermute | solution.py:958
  118.7 15.7 %collective-permute-start.26 = (bf16[64,1024]{1,0:T(8,128)(2,1)S(1)}, bf16[64,1024]{1,0:T(8,128)(2,1)S(1)}, u32[]{:S(2)}, u32[]{:S(2)}) collective-permute-start(bf16[64,1024]{1,0:T(8,128)(2,1)S(1)} %get-tuple-element.81), channel_id=1, source_target_pairs={{0,6},{1,7},{2,0},{3,1},{4,2},{5,3},{6,4},{7,5},{8,14},{9,15},{10,... | collective-permute-start | bytes 393224 | tf_op jit(solution)/shard_map/ppermute | solution.py:958
  132.4 8.8 %collective-permute-start.36 = (bf16[64,1024]{1,0:T(8,128)(2,1)S(1)}, bf16[64,1024]{1,0:T(8,128)(2,1)S(1)}, u32[]{:S(2)}, u32[]{:S(2)}) collective-permute-start(bf16[64,1024]{1,0:T(8,128)(2,1)S(1)} %collect.2.refs_5_.refs_4_), channel_id=1, source_target_pairs={{0,16},{8,24},{16,0},{24,8},{1,17},{9,25},{17,1},{25,9},{2,18},{10... | collective-permute-start | bytes 393224 | tf_op jit(solution)/shard_map/ppermute | solution.py:951
  141.3 10.1 %collective-permute-start.39 = (bf16[144,1024]{1,0:T(8,128)(2,1)S(1)}, bf16[144,1024]{1,0:T(8,128)(2,1)S(1)}, u32[]{:S(2)}, u32[]{:S(2)}) collective-permute-start(bf16[144,1024]{1,0:T(8,128)(2,1)S(1)} %get-tuple-element.97), channel_id=1, source_target_pairs={{0,24},{8,16},{16,8},{24,0},{1,25},{9,17},{17,9},{25,1},{2,26},{10... | collective-permute-start | bytes 884744 | tf_op jit(solution)/shard_map/ppermute | solution.py:951
  142.6 8.8 %collective-permute-start.37 = (bf16[80,1024]{1,0:T(8,128)(2,1)S(1)}, bf16[80,1024]{1,0:T(8,128)(2,1)S(1)}, u32[]{:S(2)}, u32[]{:S(2)}) collective-permute-start(bf16[80,1024]{1,0:T(8,128)(2,1)S(1)} %get-tuple-element.96.refs_0_), channel_id=1, source_target_pairs={{0,8},{8,0},{16,24},{24,16},{1,9},{9,1},{17,25},{25,17},{2,10},{10... | collective-permute-start | bytes 491528 | tf_op jit(solution)/shard_map/ppermute | solution.py:951
  144.9 6.5 %collective-permute-start.38 = (bf16[80,1024]{1,0:T(8,128)(2,1)S(1)}, bf16[80,1024]{1,0:T(8,128)(2,1)S(1)}, u32[]{:S(2)}, u32[]{:S(2)}) collective-permute-start(bf16[80,1024]{1,0:T(8,128)(2,1)S(1)} %get-tuple-element.96.refs_0_), channel_id=1, source_target_pairs={{0,16},{8,24},{16,0},{24,8},{1,17},{9,25},{17,1},{25,9},{2,18},{10... | collective-permute-start | bytes 491528 | tf_op jit(solution)/shard_map/ppermute | solution.py:951
  (19 other events, 94.9 us)

commit v9 on v8

--- a/solution.py
+++ b/solution.py
@@ -92,7 +92,7 @@
         share_ref[pl.ds(level, 1), :] = jnp.where(level < counts, alpha * passing, 0.0)
         passing = passing * (1.0 - alpha)
 
-    tile = 128
+    tile = 256
     lanes = 128
     columns = rays // lanes
 
@@ -100,13 +100,15 @@
     def _(step):
         first = pl.multiple_of(lax.div(step, columns) * tile, tile)
         lane = pl.multiple_of(lax.rem(step, columns) * lanes, lanes)
-        number = lax.broadcasted_iota(jnp.int32, (tile, lanes), 0) + first
-        total = jnp.zeros((tile, lanes), F32)
+        number = (lax.broadcasted_iota(jnp.int32, (tile, lanes), 0) + first).astype(jnp.int16)
+        total = jnp.zeros((tile, lanes), BF16)
         for level in range(depth):
-            ident = ids_ref[pl.ds(level, 1), pl.ds(lane, lanes)]
-            share = share_ref[pl.ds(level, 1), pl.ds(lane, lanes)]
-            total = total + jnp.where(ident == number, share, 0.0)
-        table_ref[pl.ds(first, tile), pl.ds(lane, lanes)] = total.astype(BF16)
+            ident = jnp.broadcast_to(ids_ref[pl.ds(level, 1), pl.ds(lane, lanes)], (16, lanes))
+            share = jnp.broadcast_to(share_ref[pl.ds(level, 1), pl.ds(lane, lanes)], (16, lanes))
+            ident = jnp.concatenate([ident.astype(jnp.int16)] * (tile // 16), axis=0)
+            share = jnp.concatenate([share.astype(BF16)] * (tile // 16), axis=0)
+            total = total + jnp.where(ident == number, share, jnp.zeros_like(share))
+        table_ref[pl.ds(first, tile), pl.ds(lane, lanes)] = total
 
     wait(3, 4, 5)
     owner = owner_of(mine_ref[...], owner_ref, rays, ray_count)
@@ -554,6 +556,7 @@
     width, rows = normed_t_ref.shape
     part = act_ref.shape[2]
     part_sum = None
+    downs = []
     for side, group in enumerate((own, other)):
         start = 0
         for ref in group:
@@ -565,10 +568,15 @@
                 density = jnp.exp(-0.5 * hidden * hidden) * ((2.0 * jnp.pi) ** -0.5)
                 act_ref[side, start + index] = (hidden * phi).astype(BF16)
                 slope_ref[side, start + index] = phi + hidden * density
-            act = act_ref[side, start:start + count].reshape(count * part, rows)
-            term = dot_tn(act, ref[:, 1].reshape(count * part, width))
+            downs.append(ref[:, 1].reshape(count * part, width))
+            start += count
+    if sides > 1:
+        act = act_ref[...].reshape(2 * start * part, rows)
+        part_sum = dot_tn(act, jnp.concatenate(downs, axis=0))
+    else:
+        for side, down in enumerate(downs):
+            term = dot_tn(act_ref[side].reshape(start * part, rows), down)
             part_sum = term if part_sum is None else part_sum + term
-            start += count
     if not last:
         mixed_out = refs[0]
         mixed_out[...] = part_sum if first else mixed_in[...] + part_sum
@@ -818,7 +826,8 @@
     )(x, y, x_later, y_later, *after)
 
 
-def total_kernel(own_ref, x_ref, y_ref, x_late_ref, y_late_ref, *outs):
+def total_kernel(own_ref, x_ref, y_ref, x_late_ref, y_late_ref, *refs):
+    outs = refs[-own_ref.shape[0]:]
     half = y_late_ref.shape[0]
     for index, out in enumerate(outs):
         total = own_ref[index].astype(F32)
@@ -829,17 +838,17 @@
         out[...] = total.astype(BF16)
 
 
-def totals(own, x, y, x_late, y_late):
+def totals(own, x, y, x_late, y_late, *after):
     count, part, width = own.shape
     return pl.pallas_call(
         total_kernel,
         out_shape=tuple([jax.ShapeDtypeStruct((part, width), BF16)] * count),
-        in_specs=[VMEM] * 5,
+        in_specs=[VMEM] * 5 + [ANY] * len(after),
         out_specs=tuple([VMEM] * count),
         compiler_params=params(16),
         cost_estimate=COST,
         name="totals",
-    )(own, x, y, x_late, y_late)
+    )(own, x, y, x_late, y_late, *after)
 
 
 def collect_kernel(count, *refs):
@@ -959,23 +968,26 @@
 
     mine = own_quarter(group, up_weight, down_weight, part)
     arrivals = [along(mine, -shift) for shift in range(1, depth)]
+    x_mine, y_mine = beside(mine, 1), beside(mine, 2)
     rendered, rendered_other = render(
         ray_count, True, me, block_owner, tile_lists, opacity, tile_counts.reshape(1, rows),
         ray_pixel, gaussian_features,
     )
     half = depth // 2
-    low = pack([mine] + arrivals[:half - 1], rendered)
+    low = pack(arrivals[:half - 1], rendered, x_mine, y_mine)
     x_low, y_low = beside(low, 1), beside(low, 2)
     high = pack(arrivals[half - 1:], low)
     x_high, y_high = beside(high, 1), beside(high, 2)
-    d_low, d_high = beside(y_low, 1), beside(x_high, 2)
-    blocks = mix(rendered, partner(rendered_other), x_low, y_low, high)
+    d_low, d_high = beside(pack([y_mine, y_low]), 1), beside(x_high, 2)
+    blocks = mix(rendered, partner(tie(rendered_other, low)), x_low, y_low, high)
     targets = [blocks[0]] + [along(blocks[shift], shift) for shift in range(1, depth)]
     tokens, normed, normed_t = prepare_tokens(
         ray_count, True, me, block_owner, ray_pixel, image_tokens,
         layer_norm_gain.reshape(1, width),
     )
-    most = pack([low, high, x_low, x_high, y_low, y_high], targets[half])
+    most = pack(
+        [mine, low, high, x_mine, x_low, x_high, y_mine, y_low, y_high], targets[half]
+    )
     most_other = partner(most)
     act_most, slope_most, mixed = forward(normed_t, [most], [most_other])
     late = [target for shift, target in enumerate(targets) if shift not in (0, half)]
@@ -1004,29 +1016,31 @@
         (up_arrived, layer_norm_gain.reshape(1, width), small),
     )
     vector = vector + partner(vector)
-    flip = 2
+    vector = vector + partner(vector, 2)
+
+    def first_step(to_x, to_y, x_later, y_later, *after):
+        from_x, from_y = beside(to_x, 1), beside(to_y, 2)
+        return from_x, from_y, merge(from_x, from_y, x_later, y_later, *after)
+
+    def second_step(later):
+        return beside(later[0], 1), beside(later[1], 2)
+
+    def arrive_along(shares):
+        return [shares[0]] + [along(shares[shift], shift) for shift in range(1, depth)]
+
+    own, *rest = down_sums
+    own_up, to_x, to_y, *rest_up = up_sums
+    from_x, from_y, later = first_step(*rest, vector)
+    late = second_step(later)
+    shares = totals(own, from_x, from_y, *late)
+    (down_total,) = collect(arrive_along(shares))
+    down_x, down_y = beside(down_total, 1), beside(down_total, 2)
+    flip = 4
     while flip < ray_count:
         vector = vector + partner(vector, flip)
         flip *= 2
-
-    def sum_first(to_x, to_y, x_later, y_later, *after):
-        from_x, from_y = beside(to_x, 1), beside(to_y, 2)
-        return from_x, from_y, merge(from_x, from_y, x_later, y_later, *after)
-
-    def sum_second(own, from_x, from_y, later):
-        return totals(own, from_x, from_y, beside(later[0], 1), beside(later[1], 2))
-
-    def arrive_along(shares):
-        return [shares[0]] + [along(shares[shift], shift) for shift in range(1, depth)]
-
-    own, *rest = down_sums
-    *arrived, later = sum_first(*rest)
-    shares = sum_second(own, *arrived, later)
-    (down_total,) = collect(arrive_along(shares))
-    down_x, down_y = beside(down_total, 1), beside(down_total, 2)
-    own, *rest = up_sums
-    *arrived, later = sum_first(*rest, vector)
-    shares = sum_second(own, *arrived, later)
+    from_x, from_y, later = first_step(to_x, to_y, *rest_up)
+    shares = totals(own_up, from_x, from_y, *second_step(later), vector)
     short, long = collect(arrive_along(shares), vector, down_total, (down_x, down_y))
     up_x, up_y, both = beside(short, 1), beside(short, 2), beside(long, 3)
     grad_up, grad_down, gain, scale, loss = place_quarters(
@@ -1039,7 +1053,7 @@
 def shards(*operands):
     ray_count, group_count = lax.axis_size("ray"), lax.axis_size("grp")
     hidden = operands[-1].shape[0]
-    square = group_count == 4 and ray_count in (4, 8, 16) and hidden % (16 * group_count) == 0
+    square = group_count == 4 and ray_count in (8, 16) and hidden % (16 * group_count) == 0
     return (shards_square if square else shards_general)(*operands)
 
 

time: 153 us -> 152 us (level)
  the two profiles are of different devices: /device:TPU:24 before, /device:TPU:8 now
where the time goes in v9:
time: 152 us; the launch traced here: 150 us
  waiting for transfers between devices  75.9 us (50%)
  starting transfers between devices  37.7 us (25%)
  Pallas kernels  31.9 us (21%)
  local copies, waits for them, and re-layouts  3.45 us (2%)
    ppermute x21, waiting for transfers between devices, beside(): lax.ppermute(array, 'grp', [(g, g ^ flip) for g in range(group_count)])  41.4 us
    ppermute x12, waiting for transfers between devices, along(): return lax.ppermute(array, 'ray', pairs)  26.8 us
    ppermute x21, starting transfers between devices, beside(): lax.ppermute(array, 'grp', [(g, g ^ flip) for g in range(group_count)])  18.9 us
    ppermute x12, starting transfers between devices, along(): return lax.ppermute(array, 'ray', pairs)  15.4 us
    pallas_call x1, Pallas kernels, render(): pl.pallas_call(functools.partial(render_kernel, ray_count, relative), out...  8.37 us
    ppermute x9, waiting for transfers between devices, partner(): return lax.ppermute(array, 'ray', [(r, r ^ flip) for r in range(ray_count)])  7.76 us
    pallas_call x2, Pallas kernels, forward(): pl.pallas_call(functools.partial(forward_kernel, first, blocks, len(own),...  7.29 us
    pallas_call x2, Pallas kernels, up_gradient(): pl.pallas_call(functools.partial(up_grad_kernel, side, weight_pieces, act...  6.06 us
  transfers between devices with their start and end apart: 42, of which 26 were waited for; matrix products, arithmetic and copies ran while one was open for 0% of the time, Pallas kernels for 17%

profile of v9, /device:TPU:8, one launch (start us, length us, event | category | flops | bytes accessed | tf_op | source)
XLA Modules:
  0.0 149.9 jit_solution(15554306257133280619)
XLA Ops:
  3.1 1.6 %collective-permute-start.2 = (bf16[2,64,1024]{2,1,0:T(8,128)(2,1)S(1)}, bf16[2,64,1024]{2,1,0:T(8,128)(2,1)S(1)}, u32[]{:S(2)}, u32[]{:S(2)}) collective-permute-start(bf16[2,64,1024]{2,1,0:T(8,128)(2,1)S(1)} %quarter.1.refs_0_), channel_id=1, source_target_pairs={{0,16},{8,24},{16,0},{24,8},{1,17},{9,25},{17,1},{25,9},{2,18},{10... | collective-permute-start | bytes 786440 | tf_op jit(solution)/shard_map/ppermute | solution.py:960
  4.7 1.5 collective-permute-start.1
  6.6 2.6 %collective-permute-start.3 = (bf16[2,64,1024]{2,1,0:T(8,128)(2,1)S(1)}, bf16[2,64,1024]{2,1,0:T(8,128)(2,1)S(1)}, u32[]{:S(2)}, u32[]{:S(2)}) collective-permute-start(bf16[2,64,1024]{2,1,0:T(8,128)(2,1)S(1)} %quarter.1.refs_0_), channel_id=1, source_target_pairs={{0,4},{1,5},{2,6},{3,7},{4,0},{5,1},{6,2},{7,3},{8,12},{9,13},{10,... | collective-permute-start | bytes 786440 | tf_op jit(solution)/shard_map/ppermute | solution.py:967
  9.2 2.5 %collective-permute-start.4 = (bf16[2,64,1024]{2,1,0:T(8,128)(2,1)S(1)}, bf16[2,64,1024]{2,1,0:T(8,128)(2,1)S(1)}, u32[]{:S(2)}, u32[]{:S(2)}) collective-permute-start(bf16[2,64,1024]{2,1,0:T(8,128)(2,1)S(1)} %quarter.1.refs_0_), channel_id=1, source_target_pairs={{0,2},{1,3},{2,4},{3,5},{4,6},{5,7},{6,0},{7,1},{8,10},{9,11},{10,... | collective-permute-start | bytes 786440 | tf_op jit(solution)/shard_map/ppermute | solution.py:967
  13.1 8.4 %render.1 = (bf16[4,64,1024]{2,1,0:T(8,128)(2,1)S(1)}, bf16[4,64,1024]{2,1,0:T(8,128)(2,1)S(1)}) custom-call(s32[1]{0:T(128)} %bitcast.1.me_ref, s32[1,8]{1,0:T(1,128)S(1)} %copy-done.7, s32[32,512]{1,0:T(8,128)S(1)} %copy-done.3, f32[32,512]{1,0:T(8,128)S(1)} %copy-done.4, s32[1,512]{1,0:T(1,128)S(1)} %bitcast.11, s32[1,4096]{1,0:T(1,128)S(1)} %copy-done.2, ...), custom_call_target="tpu_custom_call" | custom-call | flops 1048576 | bytes 65536 | tf_op jit(solution)/shard_map/render/pallas_call | solution.py:148
  21.5 5.3 %collective-permute-done.refs_0_ = bf16[2,64,1024]{2,1,0:T(8,128)(2,1)} collective-permute-done((bf16[2,64,1024]{2,1,0:T(8,128)(2,1)S(1)}, bf16[2,64,1024]{2,1,0:T(8,128)(2,1)}, u32[]{:S(2)}, u32[]{:S(2)}) %collective-permute-start) | collective-permute-done | bytes 262176 | tf_op jit(solution)/shard_map/ppermute | solution.py:967
  29.0 1.9 %collective-permute-done.4.refs_1_ = bf16[2,64,1024]{2,1,0:T(8,128)(2,1)S(1)} collective-permute-done((bf16[2,64,1024]{2,1,0:T(8,128)(2,1)S(1)}, bf16[2,64,1024]{2,1,0:T(8,128)(2,1)S(1)}, u32[]{:S(2)}, u32[]{:S(2)}) %collective-permute-start.4) | collective-permute-done | bytes 262176 | tf_op jit(solution)/shard_map/ppermute | solution.py:967
  32.1 4.9 %collective-permute-done.7.refs_3_.refs_7_.refs_1_ = bf16[1,2,64,1024]{3,2,1,0:T(8,128)(2,1)S(1)} collective-permute-done((bf16[1,2,64,1024]{3,2,1,0:T(8,128)(2,1)S(1)}, bf16[1,2,64,1024]{3,2,1,0:T(8,128)(2,1)S(1)}, u32[]{:S(2)}, u32[]{:S(2)}) %collective-permute-start.7) | collective-permute-done | bytes 262176 | tf_op jit(solution)/shard_map/ppermute | solution.py:960
  37.8 10.3 %collective-permute-done.6.refs_5_ = bf16[2,2,64,1024]{3,2,1,0:T(8,128)(2,1)S(1)} collective-permute-done((bf16[2,2,64,1024]{3,2,1,0:T(8,128)(2,1)S(1)}, bf16[2,2,64,1024]{3,2,1,0:T(8,128)(2,1)S(1)}, u32[]{:S(2)}, u32[]{:S(2)}) %collective-permute-start.6) | collective-permute-done | bytes 524320 | tf_op jit(solution)/shard_map/ppermute | solution.py:960
  48.3 1.6 %collective-permute-start.15 = (bf16[2,2,64,1024]{3,2,1,0:T(8,128)(2,1)S(1)}, bf16[2,2,64,1024]{3,2,1,0:T(8,128)(2,1)S(1)}, u32[]{:S(2)}, u32[]{:S(2)}) collective-permute-start(bf16[2,2,64,1024]{3,2,1,0:T(8,128)(2,1)S(1)} %collective-permute-done.6.refs_5_), channel_id=1, source_target_pairs={{0,16},{8,24},{16,0},{24,8},{1,17},{9,25},{17,1},{25,9},{2,18},{10... | collective-permute-start | bytes 1572872 | tf_op jit(solution)/shard_map/ppermute | solution.py:960
  50.5 2.0 %collective-permute-start.14 = (bf16[2,64,1024]{2,1,0:T(8,128)(2,1)S(1)}, bf16[2,64,1024]{2,1,0:T(8,128)(2,1)S(1)}, u32[]{:S(2)}, u32[]{:S(2)}) collective-permute-start(bf16[2,64,1024]{2,1,0:T(8,128)(2,1)S(1)} %get-tuple-element.60), channel_id=1, source_target_pairs={{0,6},{1,7},{2,0},{3,1},{4,2},{5,3},{6,4},{7,5},{8,14},{9,15},{10,... | collective-permute-start | bytes 786440 | tf_op jit(solution)/shard_map/ppermute | solution.py:967
  52.6 3.2 %tokens.1 = (bf16[512,1024]{1,0:T(8,128)(2,1)S(1)}, bf16[512,1024]{1,0:T(8,128)(2,1)S(1)}, bf16[1024,512]{1,0:T(8,128)(2,1)S(1)}) custom-call(s32[1]{0:T(128)} %bitcast.1.me_ref, s32[1,8]{1,0:T(1,128)S(1)} %copy-done.8, s32[1,4096]{1,0:T(1,128)S(1)} %copy-done.2, bf16[512,1024]{1,0:T(8,128)(2,1)S(1)} %copy-done.1, f32[1,1024]{1,0:T(1,128)S(1)} %bitcast.8), custom_call_target="tpu_custom_call" | custom-call | flops 1048576 | bytes 65536 | tf_op jit(solution)/shard_map/tokens/pallas_call | solution.py:234
  55.8 4.3 %forward.2 = (bf16[2,12,64,512]{3,2,1,0:T(8,128)(2,1)S(1)}, f32[2,12,64,512]{3,2,1,0:T(8,128)S(1)}, f32[512,1024]{1,0:T(8,128)S(1)}) custom-call(bf16[1024,512]{1,0:T(8,128)(2,1)S(1)} %get-tuple-element.57.refs_0_, bf16[12,2,64,1024]{3,2,1,0:T(8,128)(2,1)S(1)} %pack.6.refs_1_.refs_0_, bf16[12,2,64,1024]{3,2,1,0:T(8,128)(2,1)S(1)} %collective-permute-done.12.refs_2_.refs_0_), custom_call_target="tpu_custom_call" | custom-call | flops 1048576 | bytes 65536 | tf_op jit(solution)/shard_map/forward/pallas_call | solution.py:626
  60.2 5.6 %collective-permute-done.14.refs_3_.refs_11_ = bf16[2,64,1024]{2,1,0:T(8,128)(2,1)S(1)} collective-permute-done((bf16[2,64,1024]{2,1,0:T(8,128)(2,1)S(1)}, bf16[2,64,1024]{2,1,0:T(8,128)(2,1)S(1)}, u32[]{:S(2)}, u32[]{:S(2)}) %collective-permute-start.14) | collective-permute-done | bytes 262176 | tf_op jit(solution)/shard_map/ppermute | solution.py:967
  68.4 3.0 %forward.3 = (bf16[2,4,64,512]{3,2,1,0:T(8,128)(2,1)S(1)}, f32[2,4,64,512]{3,2,1,0:T(8,128)S(1)}, bf16[512,1024]{1,0:T(8,128)(2,1)S(1)}, bf16[1024,512]{1,0:T(8,128)(2,1)S(1)}, f32[8,1024]{1,0:T(8,128)S(1)}) custom-call(bf16[1024,512]{1,0:T(8,128)(2,1)S(1)} %get-tuple-element.57.refs_0_, bf16[2,2,64,1024]{3,2,1,0:T(8,128)(2,1)S(1)} %tie.4.refs_1_, ...), custom_call_target="tpu_custom_call" | custom-call | flops 1048576 | bytes 65536 | tf_op jit(solution)/shard_map/forward/pallas_call | solution.py:626
  72.9 2.8 %up_gradient.2 = (bf16[4,4,64,1024]{3,2,1,0:T(8,128)(2,1)S(1)}, f32[1,1024]{1,0:T(1,128)S(1)}) custom-call(bf16[12,2,64,1024]{3,2,1,0:T(8,128)(2,1)S(1)} %collective-permute-done.12.refs_2_.refs_0_, bf16[2,2,64,1024]{3,2,1,0:T(8,128)(2,1)S(1)} %collective-permute-done.16.refs_3_.refs_1_, ...), custom_call_target="tpu_custom_call" | custom-call | flops 1048576 | bytes 65536 | tf_op jit(solution)/shard_map/up_gradient/pallas_call | solution.py:798
  78.3 1.6 %collective-permute-start.30 = (bf16[4,64,1024]{2,1,0:T(8,128)(2,1)S(1)}, bf16[4,64,1024]{2,1,0:T(8,128)(2,1)S(1)}, u32[]{:S(2)}, u32[]{:S(2)}) collective-permute-start(bf16[4,64,1024]{2,1,0:T(8,128)(2,1)S(1)} %get-tuple-element.86), channel_id=1, source_target_pairs={{0,8},{8,0},{16,24},{24,16},{1,9},{9,1},{17,25},{25,17},{2,10},{10... | collective-permute-start | bytes 1572872 | tf_op jit(solution)/shard_map/ppermute | solution.py:960
  80.4 3.3 %up_gradient.3 = (bf16[4,64,1024]{2,1,0:T(8,128)(2,1)S(1)}, bf16[4,64,1024]{2,1,0:T(8,128)(2,1)S(1)}, bf16[4,64,1024]{2,1,0:T(8,128)(2,1)S(1)}, bf16[2,64,1024]{...) custom-call(bf16[12,2,64,1024]{3,2,1,0:T(8,128)(2,1)S(1)} %pack.6.refs_1_.refs_0_, ...), custom_call_target="tpu_custom_call" | custom-call | flops 1048576 | bytes 65536 | tf_op jit(solution)/shard_map/up_gradient/pallas_call | solution.py:798
  87.2 3.6 %collective-permute-done.24 = f32[8,1024]{1,0:T(8,128)S(1)} collective-permute-done((f32[8,1024]{1,0:T(8,128)S(1)}, f32[8,1024]{1,0:T(8,128)S(1)}, u32[]{:S(2)}, u32[]{:S(2)}) %collective-permute-start.24) | collective-permute-done | bytes 32800 | tf_op jit(solution)/shard_map/ppermute | solution.py:963
  90.9 2.2 %collective-permute-done.30.x_ref = bf16[4,64,1024]{2,1,0:T(8,128)(2,1)S(1)} collective-permute-done((bf16[4,64,1024]{2,1,0:T(8,128)(2,1)S(1)}, bf16[4,64,1024]{2,1,0:T(8,128)(2,1)S(1)}, u32[]{:S(2)}, u32[]{:S(2)}) %collective-permute-start.30) | collective-permute-done | bytes 524320 | tf_op jit(solution)/shard_map/ppermute | solution.py:960
  93.1 1.5 %collective-permute-done.31.y_ref = bf16[4,64,1024]{2,1,0:T(8,128)(2,1)S(1)} collective-permute-done((bf16[4,64,1024]{2,1,0:T(8,128)(2,1)S(1)}, bf16[4,64,1024]{2,1,0:T(8,128)(2,1)S(1)}, u32[]{:S(2)}, u32[]{:S(2)}) %collective-permute-start.31) | collective-permute-done | bytes 524320 | tf_op jit(solution)/shard_map/ppermute | solution.py:960
  96.0 8.3 %collective-permute-done.19.x_ref = bf16[4,64,1024]{2,1,0:T(8,128)(2,1)S(1)} collective-permute-done((bf16[4,64,1024]{2,1,0:T(8,128)(2,1)S(1)}, bf16[4,64,1024]{2,1,0:T(8,128)(2,1)S(1)}, u32[]{:S(2)}, u32[]{:S(2)}) %collective-permute-start.19) | collective-permute-done | bytes 524320 | tf_op jit(solution)/shard_map/ppermute | solution.py:960
  104.3 1.5 %collective-permute-done.20.y_ref = bf16[4,64,1024]{2,1,0:T(8,128)(2,1)S(1)} collective-permute-done((bf16[4,64,1024]{2,1,0:T(8,128)(2,1)S(1)}, bf16[4,64,1024]{2,1,0:T(8,128)(2,1)S(1)}, u32[]{:S(2)}, u32[]{:S(2)}) %collective-permute-start.20) | collective-permute-done | bytes 524320 | tf_op jit(solution)/shard_map/ppermute | solution.py:960
  107.2 1.8 %collective-permute-start.25 = (f32[8,1024]{1,0:T(8,128)S(1)}, f32[8,1024]{1,0:T(8,128)S(1)}, u32[]{:S(2)}, u32[]{:S(2)}) collective-permute-start(f32[8,1024]{1,0:T(8,128)S(1)} %add.10.refs_0_), channel_id=1, source_target_pairs={{0,4},{1,5},{2,6},{3,7},{4,0},{5,1},{6,2},{7,3},{8,12},{9,13},{10,... | collective-permute-start | bytes 98312 | tf_op jit(solution)/shard_map/ppermute | solution.py:963
  109.9 1.5 %collective-permute-done.33.y_late_ref = bf16[2,64,1024]{2,1,0:T(8,128)(2,1)S(1)} collective-permute-done((bf16[2,64,1024]{2,1,0:T(8,128)(2,1)S(1)}, bf16[2,64,1024]{2,1,0:T(8,128)(2,1)S(1)}, u32[]{:S(2)}, u32[]{:S(2)}) %collective-permute-start.33) | collective-permute-done | bytes 262176 | tf_op jit(solution)/shard_map/ppermute | solution.py:960
  112.3 2.1 %collective-permute-start.35 = (bf16[64,1024]{1,0:T(8,128)(2,1)S(1)}, bf16[64,1024]{1,0:T(8,128)(2,1)S(1)}, u32[]{:S(2)}, u32[]{:S(2)}) collective-permute-start(bf16[64,1024]{1,0:T(8,128)(2,1)S(1)} %get-tuple-element.94), channel_id=1, source_target_pairs={{0,4},{1,5},{2,6},{3,7},{4,0},{5,1},{6,2},{7,3},{8,12},{9,13},{10,... | collective-permute-start | bytes 393224 | tf_op jit(solution)/shard_map/ppermute | solution.py:967
  116.8 2.5 %collective-permute-start.27 = (bf16[64,1024]{1,0:T(8,128)(2,1)S(1)}, bf16[64,1024]{1,0:T(8,128)(2,1)S(1)}, u32[]{:S(2)}, u32[]{:S(2)}) collective-permute-start(bf16[64,1024]{1,0:T(8,128)(2,1)S(1)} %get-tuple-element.80), channel_id=1, source_target_pairs={{0,4},{1,5},{2,6},{3,7},{4,0},{5,1},{6,2},{7,3},{8,12},{9,13},{10,... | collective-permute-start | bytes 393224 | tf_op jit(solution)/shard_map/ppermute | solution.py:967
  120.1 9.6 %collective-permute-done.35.refs_2_ = bf16[64,1024]{1,0:T(8,128)(2,1)S(1)} collective-permute-done((bf16[64,1024]{1,0:T(8,128)(2,1)S(1)}, bf16[64,1024]{1,0:T(8,128)(2,1)S(1)}, u32[]{:S(2)}, u32[]{:S(2)}) %collective-permute-start.35) | collective-permute-done | bytes 131104 | tf_op jit(solution)/shard_map/ppermute | solution.py:967
  133.1 2.1 %collective-permute-done.28.refs_3_ = bf16[64,1024]{1,0:T(8,128)(2,1)S(1)} collective-permute-done((bf16[64,1024]{1,0:T(8,128)(2,1)S(1)}, bf16[64,1024]{1,0:T(8,128)(2,1)S(1)}, u32[]{:S(2)}, u32[]{:S(2)}) %collective-permute-start.28) | collective-permute-done | bytes 131104 | tf_op jit(solution)/shard_map/ppermute | solution.py:967
  136.2 1.6 %collective-permute-start.41 = (bf16[144,1024]{1,0:T(8,128)(2,1)S(1)}, bf16[144,1024]{1,0:T(8,128)(2,1)S(1)}, u32[]{:S(2)}, u32[]{:S(2)}) collective-permute-start(bf16[144,1024]{1,0:T(8,128)(2,1)S(1)} %get-tuple-element.97), channel_id=1, source_target_pairs={{0,24},{8,16},{16,8},{24,0},{1,25},{9,17},{17,9},{25,1},{2,26},{10... | collective-permute-start | bytes 884744 | tf_op jit(solution)/shard_map/ppermute | solution.py:960
  139.8 7.5 %collective-permute-done.39.refs_1_ = bf16[80,1024]{1,0:T(8,128)(2,1)S(1)} collective-permute-done((bf16[80,1024]{1,0:T(8,128)(2,1)S(1)}, bf16[80,1024]{1,0:T(8,128)(2,1)S(1)}, u32[]{:S(2)}, u32[]{:S(2)}) %collective-permute-start.39) | collective-permute-done | bytes 163872 | tf_op jit(solution)/shard_map/ppermute | solution.py:960
  148.1 1.7 %place.1 = (f32[1024,256]{1,0:T(8,128)}, f32[256,1024]{1,0:T(8,128)}, f32[1,1024]{1,0:T(1,128)}, f32[1,1024]{1,0:T(1,128)}, f32[1,1]{1,0:T(1,128)}) custom-call(s32[1]{0:T(128)} %bitcast.group_ref, bf16[80,1024]{1,0:T(8,128)(2,1)S(1)} %get-tuple-element.96.refs_0_, bf16[80,1024]{1,0:T(8,128)(2,1)S(1)} %collective-permute-done.39.refs_1_, ...), custom_call_target="tpu_custom_call" | custom-call | flops 1048576 | bytes 65536 | tf_op jit(solution)/shard_map/place/pallas_call | solution.py:926
  (104 shorter events, 34.9 us)
Async XLA Ops:
  3.1 18.3 %collective-permute-start.2 = (bf16[2,64,1024]{2,1,0:T(8,128)(2,1)S(1)}, bf16[2,64,1024]{2,1,0:T(8,128)(2,1)S(1)}, u32[]{:S(2)}, u32[]{:S(2)}) collective-permute-start(bf16[2,64,1024]{2,1,0:T(8,128)(2,1)S(1)} %quarter.1.refs_0_), channel_id=1, source_target_pairs={{0,16},{8,24},{16,0},{24,8},{1,17},{9,25},{17,1},{25,9},{2,18},{10... | collective-permute-start | bytes 786440 | tf_op jit(solution)/shard_map/ppermute | solution.py:960
  4.7 16.8 %collective-permute-start.1 = (bf16[2,64,1024]{2,1,0:T(8,128)(2,1)S(1)}, bf16[2,64,1024]{2,1,0:T(8,128)(2,1)S(1)}, u32[]{:S(2)}, u32[]{:S(2)}) collective-permute-start(bf16[2,64,1024]{2,1,0:T(8,128)(2,1)S(1)} %quarter.1.refs_0_), channel_id=1, source_target_pairs={{0,8},{8,0},{16,24},{24,16},{1,9},{9,1},{17,25},{25,17},{2,10},{10... | collective-permute-start | bytes 786440 | tf_op jit(solution)/shard_map/ppermute | solution.py:960
  6.2 20.6 %collective-permute-start = (bf16[2,64,1024]{2,1,0:T(8,128)(2,1)S(1)}, bf16[2,64,1024]{2,1,0:T(8,128)(2,1)}, u32[]{:S(2)}, u32[]{:S(2)}) collective-permute-start(bf16[2,64,1024]{2,1,0:T(8,128)(2,1)S(1)} %quarter.1.refs_0_), channel_id=1, source_target_pairs={{0,6},{1,7},{2,0},{3,1},{4,2},{5,3},{6,4},{7,5},{8,14},{9,15},{10,... | collective-permute-start | bytes 786440 | tf_op jit(solution)/shard_map/ppermute | solution.py:967
  6.6 22.3 %collective-permute-start.3 = (bf16[2,64,1024]{2,1,0:T(8,128)(2,1)S(1)}, bf16[2,64,1024]{2,1,0:T(8,128)(2,1)S(1)}, u32[]{:S(2)}, u32[]{:S(2)}) collective-permute-start(bf16[2,64,1024]{2,1,0:T(8,128)(2,1)S(1)} %quarter.1.refs_0_), channel_id=1, source_target_pairs={{0,4},{1,5},{2,6},{3,7},{4,0},{5,1},{6,2},{7,3},{8,12},{9,13},{10,... | collective-permute-start | bytes 786440 | tf_op jit(solution)/shard_map/ppermute | solution.py:967
  9.2 21.6 %collective-permute-start.4 = (bf16[2,64,1024]{2,1,0:T(8,128)(2,1)S(1)}, bf16[2,64,1024]{2,1,0:T(8,128)(2,1)S(1)}, u32[]{:S(2)}, u32[]{:S(2)}) collective-permute-start(bf16[2,64,1024]{2,1,0:T(8,128)(2,1)S(1)} %quarter.1.refs_0_), channel_id=1, source_target_pairs={{0,2},{1,3},{2,4},{3,5},{4,6},{5,7},{6,0},{7,1},{8,10},{9,11},{10,... | collective-permute-start | bytes 786440 | tf_op jit(solution)/shard_map/ppermute | solution.py:967
  27.8 9.8 %collective-permute-start.9 = (bf16[4,64,1024]{2,1,0:T(8,128)(2,1)S(1)}, bf16[4,64,1024]{2,1,0:T(8,128)(2,1)S(1)}, u32[]{:S(2)}, u32[]{:S(2)}) collective-permute-start(bf16[4,64,1024]{2,1,0:T(8,128)(2,1)S(1)} %tie.3), channel_id=1, source_target_pairs={{0,1},{1,0},{2,3},{3,2},{4,5},{5,4},{6,7},{7,6},{8,9},{9,8},{10,11... | collective-permute-start | bytes 1572872 | tf_op jit(solution)/shard_map/ppermute | solution.py:963
  27.8 9.2 %collective-permute-start.7 = (bf16[1,2,64,1024]{3,2,1,0:T(8,128)(2,1)S(1)}, bf16[1,2,64,1024]{3,2,1,0:T(8,128)(2,1)S(1)}, u32[]{:S(2)}, u32[]{:S(2)}) collective-permute-start(bf16[1,2,64,1024]{3,2,1,0:T(8,128)(2,1)S(1)} %pack.4.refs_2_.refs_1_), channel_id=1, source_target_pairs={{0,16},{8,24},{16,0},{24,8},{1,17},{9,25},{17,1},{25,9},{2,18},{10... | collective-permute-start | bytes 786440 | tf_op jit(solution)/shard_map/ppermute | solution.py:960
  28.4 9.2 %collective-permute-start.5 = (bf16[1,2,64,1024]{3,2,1,0:T(8,128)(2,1)S(1)}, bf16[1,2,64,1024]{3,2,1,0:T(8,128)(2,1)S(1)}, u32[]{:S(2)}, u32[]{:S(2)}) collective-permute-start(bf16[1,2,64,1024]{3,2,1,0:T(8,128)(2,1)S(1)} %pack.4.refs_2_.refs_1_), channel_id=1, source_target_pairs={{0,8},{8,0},{16,24},{24,16},{1,9},{9,1},{17,25},{25,17},{2,10},{10... | collective-permute-start | bytes 786440 | tf_op jit(solution)/shard_map/ppermute | solution.py:960
  30.9 17.1 %collective-permute-start.6 = (bf16[2,2,64,1024]{3,2,1,0:T(8,128)(2,1)S(1)}, bf16[2,2,64,1024]{3,2,1,0:T(8,128)(2,1)S(1)}, u32[]{:S(2)}, u32[]{:S(2)}) collective-permute-start(bf16[2,2,64,1024]{3,2,1,0:T(8,128)(2,1)S(1)} %pack.5.refs_4_.refs_2_), channel_id=1, source_target_pairs={{0,8},{8,0},{16,24},{24,16},{1,9},{9,1},{17,25},{25,17},{2,10},{10... | collective-permute-start | bytes 1572872 | tf_op jit(solution)/shard_map/ppermute | solution.py:960
  31.5 16.5 %collective-permute-start.8 = (bf16[2,2,64,1024]{3,2,1,0:T(8,128)(2,1)S(1)}, bf16[2,2,64,1024]{3,2,1,0:T(8,128)(2,1)S(1)}, u32[]{:S(2)}, u32[]{:S(2)}) collective-permute-start(bf16[2,2,64,1024]{3,2,1,0:T(8,128)(2,1)S(1)} %pack.5.refs_4_.refs_2_), channel_id=1, source_target_pairs={{0,16},{8,24},{16,0},{24,8},{1,17},{9,25},{17,1},{25,9},{2,18},{10... | collective-permute-start | bytes 1572872 | tf_op jit(solution)/shard_map/ppermute | solution.py:960
  37.7 10.4 %collective-permute-start.10 = (bf16[2,64,1024]{2,1,0:T(8,128)(2,1)S(1)}, bf16[2,64,1024]{2,1,0:T(8,128)(2,1)S(1)}, u32[]{:S(2)}, u32[]{:S(2)}) collective-permute-start(bf16[2,64,1024]{2,1,0:T(8,128)(2,1)S(1)} %get-tuple-element.56), channel_id=1, source_target_pairs={{0,4},{1,5},{2,6},{3,7},{4,0},{5,1},{6,2},{7,3},{8,12},{9,13},{10,... | collective-permute-start | bytes 786440 | tf_op jit(solution)/shard_map/ppermute | solution.py:967
  48.3 17.4 %collective-permute-start.15 = (bf16[2,2,64,1024]{3,2,1,0:T(8,128)(2,1)S(1)}, bf16[2,2,64,1024]{3,2,1,0:T(8,128)(2,1)S(1)}, u32[]{:S(2)}, u32[]{:S(2)}) collective-permute-start(bf16[2,2,64,1024]{3,2,1,0:T(8,128)(2,1)S(1)} %collective-permute-done.6.refs_5_), channel_id=1, source_target_pairs={{0,16},{8,24},{16,0},{24,8},{1,17},{9,25},{17,1},{25,9},{2,18},{10... | collective-permute-start | bytes 1572872 | tf_op jit(solution)/shard_map/ppermute | solution.py:960
  49.9 15.8 %collective-permute-start.11 = (bf16[2,2,64,1024]{3,2,1,0:T(8,128)(2,1)S(1)}, bf16[2,2,64,1024]{3,2,1,0:T(8,128)(2,1)S(1)}, u32[]{:S(2)}, u32[]{:S(2)}) collective-permute-start(bf16[2,2,64,1024]{3,2,1,0:T(8,128)(2,1)S(1)} %pack.7), channel_id=1, source_target_pairs={{0,8},{8,0},{16,24},{24,16},{1,9},{9,1},{17,25},{25,17},{2,10},{10... | collective-permute-start | bytes 1572872 | tf_op jit(solution)/shard_map/ppermute | solution.py:960
  50.5 9.6 %collective-permute-start.13 = (bf16[2,64,1024]{2,1,0:T(8,128)(2,1)S(1)}, bf16[2,64,1024]{2,1,0:T(8,128)(2,1)S(1)}, u32[]{:S(2)}, u32[]{:S(2)}) collective-permute-start(bf16[2,64,1024]{2,1,0:T(8,128)(2,1)S(1)} %get-tuple-element.59), channel_id=1, source_target_pairs={{0,2},{1,3},{2,4},{3,5},{4,6},{5,7},{6,0},{7,1},{8,10},{9,11},{10,... | collective-permute-start | bytes 786440 | tf_op jit(solution)/shard_map/ppermute | solution.py:967
  50.5 15.2 %collective-permute-start.14 = (bf16[2,64,1024]{2,1,0:T(8,128)(2,1)S(1)}, bf16[2,64,1024]{2,1,0:T(8,128)(2,1)S(1)}, u32[]{:S(2)}, u32[]{:S(2)}) collective-permute-start(bf16[2,64,1024]{2,1,0:T(8,128)(2,1)S(1)} %get-tuple-element.60), channel_id=1, source_target_pairs={{0,6},{1,7},{2,0},{3,1},{4,2},{5,3},{6,4},{7,5},{8,14},{9,15},{10,... | collective-permute-start | bytes 786440 | tf_op jit(solution)/shard_map/ppermute | solution.py:967
  78.3 14.8 %collective-permute-start.30 = (bf16[4,64,1024]{2,1,0:T(8,128)(2,1)S(1)}, bf16[4,64,1024]{2,1,0:T(8,128)(2,1)S(1)}, u32[]{:S(2)}, u32[]{:S(2)}) collective-permute-start(bf16[4,64,1024]{2,1,0:T(8,128)(2,1)S(1)} %get-tuple-element.86), channel_id=1, source_target_pairs={{0,8},{8,0},{16,24},{24,16},{1,9},{9,1},{17,25},{25,17},{2,10},{10... | collective-permute-start | bytes 1572872 | tf_op jit(solution)/shard_map/ppermute | solution.py:960
  79.8 14.8 %collective-permute-start.31 = (bf16[4,64,1024]{2,1,0:T(8,128)(2,1)S(1)}, bf16[4,64,1024]{2,1,0:T(8,128)(2,1)S(1)}, u32[]{:S(2)}, u32[]{:S(2)}) collective-permute-start(bf16[4,64,1024]{2,1,0:T(8,128)(2,1)S(1)} %get-tuple-element.87), channel_id=1, source_target_pairs={{0,16},{8,24},{16,0},{24,8},{1,17},{9,25},{17,1},{25,9},{2,18},{10... | collective-permute-start | bytes 1572872 | tf_op jit(solution)/shard_map/ppermute | solution.py:960
  83.7 20.6 %collective-permute-start.19 = (bf16[4,64,1024]{2,1,0:T(8,128)(2,1)S(1)}, bf16[4,64,1024]{2,1,0:T(8,128)(2,1)S(1)}, u32[]{:S(2)}, u32[]{:S(2)}) collective-permute-start(bf16[4,64,1024]{2,1,0:T(8,128)(2,1)S(1)} %get-tuple-element.71), channel_id=1, source_target_pairs={{0,8},{8,0},{16,24},{24,16},{1,9},{9,1},{17,25},{25,17},{2,10},{10... | collective-permute-start | bytes 1572872 | tf_op jit(solution)/shard_map/ppermute | solution.py:960
  84.8 21.1 %collective-permute-start.20 = (bf16[4,64,1024]{2,1,0:T(8,128)(2,1)S(1)}, bf16[4,64,1024]{2,1,0:T(8,128)(2,1)S(1)}, u32[]{:S(2)}, u32[]{:S(2)}) collective-permute-start(bf16[4,64,1024]{2,1,0:T(8,128)(2,1)S(1)} %get-tuple-element.72), channel_id=1, source_target_pairs={{0,16},{8,24},{16,0},{24,8},{1,17},{9,25},{17,1},{25,9},{2,18},{10... | collective-permute-start | bytes 1572872 | tf_op jit(solution)/shard_map/ppermute | solution.py:960
  94.8 15.2 %collective-permute-start.32 = (bf16[2,64,1024]{2,1,0:T(8,128)(2,1)S(1)}, bf16[2,64,1024]{2,1,0:T(8,128)(2,1)S(1)}, u32[]{:S(2)}, u32[]{:S(2)}) collective-permute-start(bf16[2,64,1024]{2,1,0:T(8,128)(2,1)S(1)} %get-tuple-element.90), channel_id=1, source_target_pairs={{0,8},{8,0},{16,24},{24,16},{1,9},{9,1},{17,25},{25,17},{2,10},{10... | collective-permute-start | bytes 786440 | tf_op jit(solution)/shard_map/ppermute | solution.py:960
  95.4 16.1 %collective-permute-start.33 = (bf16[2,64,1024]{2,1,0:T(8,128)(2,1)S(1)}, bf16[2,64,1024]{2,1,0:T(8,128)(2,1)S(1)}, u32[]{:S(2)}, u32[]{:S(2)}) collective-permute-start(bf16[2,64,1024]{2,1,0:T(8,128)(2,1)S(1)} %get-tuple-element.91), channel_id=1, source_target_pairs={{0,16},{8,24},{16,0},{24,8},{1,17},{9,25},{17,1},{25,9},{2,18},{10... | collective-permute-start | bytes 786440 | tf_op jit(solution)/shard_map/ppermute | solution.py:960
  106.0 9.6 %collective-permute-start.21 = (bf16[2,64,1024]{2,1,0:T(8,128)(2,1)S(1)}, bf16[2,64,1024]{2,1,0:T(8,128)(2,1)S(1)}, u32[]{:S(2)}, u32[]{:S(2)}) collective-permute-start(bf16[2,64,1024]{2,1,0:T(8,128)(2,1)S(1)} %get-tuple-element.75), channel_id=1, source_target_pairs={{0,8},{8,0},{16,24},{24,16},{1,9},{9,1},{17,25},{25,17},{2,10},{10... | collective-permute-start | bytes 786440 | tf_op jit(solution)/shard_map/ppermute | solution.py:960
  106.6 9.4 %collective-permute-start.22 = (bf16[2,64,1024]{2,1,0:T(8,128)(2,1)S(1)}, bf16[2,64,1024]{2,1,0:T(8,128)(2,1)S(1)}, u32[]{:S(2)}, u32[]{:S(2)}) collective-permute-start(bf16[2,64,1024]{2,1,0:T(8,128)(2,1)S(1)} %get-tuple-element.76), channel_id=1, source_target_pairs={{0,16},{8,24},{16,0},{24,8},{1,17},{9,25},{17,1},{25,9},{2,18},{10... | collective-permute-start | bytes 786440 | tf_op jit(solution)/shard_map/ppermute | solution.py:960
  111.7 7.7 %collective-permute-start.34 = (bf16[64,1024]{1,0:T(8,128)(2,1)S(1)}, bf16[64,1024]{1,0:T(8,128)(2,1)S(1)}, u32[]{:S(2)}, u32[]{:S(2)}) collective-permute-start(bf16[64,1024]{1,0:T(8,128)(2,1)S(1)} %get-tuple-element.93), channel_id=1, source_target_pairs={{0,2},{1,3},{2,4},{3,5},{4,6},{5,7},{6,0},{7,1},{8,10},{9,11},{10,... | collective-permute-start | bytes 393224 | tf_op jit(solution)/shard_map/ppermute | solution.py:967
  112.3 17.4 %collective-permute-start.35 = (bf16[64,1024]{1,0:T(8,128)(2,1)S(1)}, bf16[64,1024]{1,0:T(8,128)(2,1)S(1)}, u32[]{:S(2)}, u32[]{:S(2)}) collective-permute-start(bf16[64,1024]{1,0:T(8,128)(2,1)S(1)} %get-tuple-element.94), channel_id=1, source_target_pairs={{0,4},{1,5},{2,6},{3,7},{4,0},{5,1},{6,2},{7,3},{8,12},{9,13},{10,... | collective-permute-start | bytes 393224 | tf_op jit(solution)/shard_map/ppermute | solution.py:967
  114.4 16.1 %collective-permute-start.36 = (bf16[64,1024]{1,0:T(8,128)(2,1)S(1)}, bf16[64,1024]{1,0:T(8,128)(2,1)S(1)}, u32[]{:S(2)}, u32[]{:S(2)}) collective-permute-start(bf16[64,1024]{1,0:T(8,128)(2,1)S(1)} %get-tuple-element.95), channel_id=1, source_target_pairs={{0,6},{1,7},{2,0},{3,1},{4,2},{5,3},{6,4},{7,5},{8,14},{9,15},{10,... | collective-permute-start | bytes 393224 | tf_op jit(solution)/shard_map/ppermute | solution.py:967
  116.2 15.6 %collective-permute-start.26 = (bf16[64,1024]{1,0:T(8,128)(2,1)S(1)}, bf16[64,1024]{1,0:T(8,128)(2,1)S(1)}, u32[]{:S(2)}, u32[]{:S(2)}) collective-permute-start(bf16[64,1024]{1,0:T(8,128)(2,1)S(1)} %get-tuple-element.79), channel_id=1, source_target_pairs={{0,2},{1,3},{2,4},{3,5},{4,6},{5,7},{6,0},{7,1},{8,10},{9,11},{10,... | collective-permute-start | bytes 393224 | tf_op jit(solution)/shard_map/ppermute | solution.py:967
  116.8 16.3 %collective-permute-start.27 = (bf16[64,1024]{1,0:T(8,128)(2,1)S(1)}, bf16[64,1024]{1,0:T(8,128)(2,1)S(1)}, u32[]{:S(2)}, u32[]{:S(2)}) collective-permute-start(bf16[64,1024]{1,0:T(8,128)(2,1)S(1)} %get-tuple-element.80), channel_id=1, source_target_pairs={{0,4},{1,5},{2,6},{3,7},{4,0},{5,1},{6,2},{7,3},{8,12},{9,13},{10,... | collective-permute-start | bytes 393224 | tf_op jit(solution)/shard_map/ppermute | solution.py:967
  119.4 15.9 %collective-permute-start.28 = (bf16[64,1024]{1,0:T(8,128)(2,1)S(1)}, bf16[64,1024]{1,0:T(8,128)(2,1)S(1)}, u32[]{:S(2)}, u32[]{:S(2)}) collective-permute-start(bf16[64,1024]{1,0:T(8,128)(2,1)S(1)} %get-tuple-element.81), channel_id=1, source_target_pairs={{0,6},{1,7},{2,0},{3,1},{4,2},{5,3},{6,4},{7,5},{8,14},{9,15},{10,... | collective-permute-start | bytes 393224 | tf_op jit(solution)/shard_map/ppermute | solution.py:967
  136.2 11.9 %collective-permute-start.41 = (bf16[144,1024]{1,0:T(8,128)(2,1)S(1)}, bf16[144,1024]{1,0:T(8,128)(2,1)S(1)}, u32[]{:S(2)}, u32[]{:S(2)}) collective-permute-start(bf16[144,1024]{1,0:T(8,128)(2,1)S(1)} %get-tuple-element.97), channel_id=1, source_target_pairs={{0,24},{8,16},{16,8},{24,0},{1,25},{9,17},{17,9},{25,1},{2,26},{10... | collective-permute-start | bytes 884744 | tf_op jit(solution)/shard_map/ppermute | solution.py:960
  137.8 9.5 %collective-permute-start.39 = (bf16[80,1024]{1,0:T(8,128)(2,1)S(1)}, bf16[80,1024]{1,0:T(8,128)(2,1)S(1)}, u32[]{:S(2)}, u32[]{:S(2)}) collective-permute-start(bf16[80,1024]{1,0:T(8,128)(2,1)S(1)} %get-tuple-element.96.refs_0_), channel_id=1, source_target_pairs={{0,8},{8,0},{16,24},{24,16},{1,9},{9,1},{17,25},{25,17},{2,10},{10... | collective-permute-start | bytes 491528 | tf_op jit(solution)/shard_map/ppermute | solution.py:960
  138.3 9.8 %collective-permute-start.40 = (bf16[80,1024]{1,0:T(8,128)(2,1)S(1)}, bf16[80,1024]{1,0:T(8,128)(2,1)S(1)}, u32[]{:S(2)}, u32[]{:S(2)}) collective-permute-start(bf16[80,1024]{1,0:T(8,128)(2,1)S(1)} %get-tuple-element.96.refs_0_), channel_id=1, source_target_pairs={{0,16},{8,24},{16,0},{24,8},{1,17},{9,25},{17,1},{25,9},{2,18},{10... | collective-permute-start | bytes 491528 | tf_op jit(solution)/shard_map/ppermute | solution.py:960
  (22 other events, 130.2 us)

commit v10 on v9

--- a/solution.py
+++ b/solution.py
@@ -527,6 +527,30 @@
         compiler_params=params(16),
         cost_estimate=LONG,
         name="quarter",
+    )(group, up, down)
+
+
+def own_rows_kernel(group_ref, up_ref, down_ref, out_ref, turned_ref):
+    part = out_ref.shape[2]
+    turned_ref[...] = up_ref[...].T
+    for index in range(4):
+        quarter = jnp.bitwise_xor(group_ref[0], index)
+        span = pl.ds(pl.multiple_of(quarter * part, part), part)
+        out_ref[index, 0] = turned_ref[span, :]
+        out_ref[index, 1] = down_ref[span, :]
+
+
+def own_rows(group, up, down):
+    width, chunk = up.shape
+    return pl.pallas_call(
+        own_rows_kernel,
+        out_shape=jax.ShapeDtypeStruct((4, 2, chunk // 4, width), BF16),
+        in_specs=[SMEM, VMEM, VMEM],
+        out_specs=VMEM,
+        scratch_shapes=[pltpu.VMEM((chunk, width), BF16)],
+        compiler_params=params(16),
+        cost_estimate=COST,
+        name="own_rows",
     )(group, up, down)
 
 
@@ -734,14 +758,14 @@
 
 
 def up_grad_kernel(side, weight_pieces, act_pieces, add, *refs):
-    weights, slopes = refs[:3], refs[3:5]
-    back_t_ref, normed_ref, gain_in = refs[5:8]
+    weights, slopes = refs[:2], refs[2:4]
+    back_t_ref, normed_ref, gain_in = refs[4:7]
     if add:
-        arrived, scale_ref, small_ref = refs[8:11]
-        outs, vector_ref, gain_ref = refs[11:-2], refs[-2], refs[-1]
+        arrived, scale_ref, small_ref = refs[7:10]
+        outs, vector_ref, gain_ref = refs[10:-2], refs[-2], refs[-1]
     else:
         arrived = None
-        outs, gain_ref = refs[8:-1], refs[-1]
+        outs, gain_ref = refs[7:-1], refs[-1]
     gain_ref[...] = gain_in[...]
     for quarter in (3, 1, 2, 0):
         pieces = weight_pieces[quarter]
@@ -968,51 +992,47 @@
 
     mine = own_quarter(group, up_weight, down_weight, part)
     arrivals = [along(mine, -shift) for shift in range(1, depth)]
-    x_mine, y_mine = beside(mine, 1), beside(mine, 2)
     rendered, rendered_other = render(
         ray_count, True, me, block_owner, tile_lists, opacity, tile_counts.reshape(1, rows),
         ray_pixel, gaussian_features,
     )
     half = depth // 2
-    low = pack(arrivals[:half - 1], rendered, x_mine, y_mine)
-    x_low, y_low = beside(low, 1), beside(low, 2)
+    low = pack(arrivals[:half - 1], rendered)
+    lows = [low] + [beside(low, flip) for flip in (1, 2, 3)]
     high = pack(arrivals[half - 1:], low)
-    x_high, y_high = beside(high, 1), beside(high, 2)
-    d_low, d_high = beside(pack([y_mine, y_low]), 1), beside(x_high, 2)
-    blocks = mix(rendered, partner(tie(rendered_other, low)), x_low, y_low, high)
+    highs = [high] + [beside(high, flip) for flip in (1, 2, 3)]
+    blocks = mix(rendered, partner(tie(rendered_other, low)), high)
     targets = [blocks[0]] + [along(blocks[shift], shift) for shift in range(1, depth)]
+    early = pack([own_rows(group, up_weight, down_weight)] + lows, high)
+    early_other = partner(early)
     tokens, normed, normed_t = prepare_tokens(
         ray_count, True, me, block_owner, ray_pixel, image_tokens,
         layer_norm_gain.reshape(1, width),
     )
-    most = pack(
-        [mine, low, high, x_mine, x_low, x_high, y_mine, y_low, y_high], targets[half]
-    )
-    most_other = partner(most)
-    act_most, slope_most, mixed = forward(normed_t, [most], [most_other])
-    late = [target for shift, target in enumerate(targets) if shift not in (0, half)]
-    d_low, d_high = tie(d_low, mixed, *late), tie(d_high, mixed, *late)
-    d_low_other, d_high_other = partner(d_low), partner(d_high)
-    act_last, slope_last, back, back_t, small = forward(
-        normed_t, [d_low, d_high], [d_low_other, d_high_other], mixed,
+    act_early, slope_early, mixed = forward(normed_t, [early], [early_other])
+    late = pack(highs, mixed, *targets[1:-1])
+    late_other = partner(late)
+    act_late, slope_late, back, back_t, small = forward(
+        normed_t, [late], [late_other], mixed,
         (tokens, layer_scale.reshape(1, width), *targets),
     )
-    acts = (act_most, act_last)
-    slopes = (slope_most, slope_last)
-    weights = ((most, d_low, d_high), (most_other, d_low_other, d_high_other))
-    act_pieces = tuple(((0, quarter * depth, depth),) for quarter in range(3))
-    act_pieces += (((1, 0, depth),),)
-    weight_pieces = act_pieces[:3] + (((1, 0, half), (2, 0, depth - half)),)
+    acts, slopes = (act_early, act_late), (slope_early, slope_late)
+    weights = ((early, late), (early_other, late_other))
+    count = half - 1
+    pieces = tuple(
+        ((0, q, 1), (0, 4 + q * count, count), (1, q * (depth - half), depth - half))
+        for q in range(4)
+    )
     gain = jnp.zeros((1, width), F32)
-    (down_other,) = down_gradient(1, act_pieces, depth, acts, back)
+    (down_other,) = down_gradient(1, pieces, depth, acts, back)
     down_arrived = partner(down_other)
     up_other, gain = up_gradient(
-        1, weight_pieces, act_pieces, depth, weights[1], slopes, back_t, normed, gain
+        1, pieces, pieces, depth, weights[1], slopes, back_t, normed, gain
     )
     up_arrived = partner(up_other)
-    down_sums = down_gradient(0, act_pieces, depth, acts, back, down_arrived)
+    down_sums = down_gradient(0, pieces, depth, acts, back, down_arrived)
     *up_sums, vector = up_gradient(
-        0, weight_pieces, act_pieces, depth, weights[0], slopes, back_t, normed, gain,
+        0, pieces, pieces, depth, weights[0], slopes, back_t, normed, gain,
         (up_arrived, layer_norm_gain.reshape(1, width), small),
     )
     vector = vector + partner(vector)

time: 152 us -> 156 us (1.026)
  waiting for transfers between devices: 75.9 us -> 79.4 us
    ppermute x21 -> x19, waiting for transfers between devices: 41.4 us -> 45.6 us  [beside(): lax.ppermute(array, 'grp', [(g, g ^ flip) for g in range(group_count)])]
    ppermute x12, starting transfers between devices: 15.4 us -> 13 us  [along(): return lax.ppermute(array, 'ray', pairs)]
    ppermute x21 -> x19, starting transfers between devices: 18.9 us -> 21.1 us  [beside(): lax.ppermute(array, 'grp', [(g, g ^ flip) for g in range(group_count)])]
    ppermute x9 -> x8, waiting for transfers between devices: 7.76 us -> 6.6 us  [partner(): return lax.ppermute(array, 'ray', [(r, r ^ flip) for r in range(ray_count)])]
    ppermute x9 -> x8, starting transfers between devices: 3.38 us -> 3.18 us  [partner(): return lax.ppermute(array, 'ray', [(r, r ^ flip) for r in range(ray_count)])]
    unnamed x24 -> x26, local copies, waits for them, and re-layouts: 3.44 us -> 3.45 us
  transfers between devices with their start and end apart: 42 -> 39, of which waited for: 26 -> 28; matrix products, arithmetic and copies ran while one was open for 0% -> 0% of each run, Pallas kernels for 17% -> 16%
where the time goes in v10:
time: 156 us; the launch traced here: 155 us
  waiting for transfers between devices  79.4 us (51%)
  starting transfers between devices  37.3 us (24%)
  Pallas kernels  33.4 us (21%)
  local copies, waits for them, and re-layouts  3.46 us (2%)
    ppermute x19, waiting for transfers between devices, beside(): lax.ppermute(array, 'grp', [(g, g ^ flip) for g in range(group_count)])  45.6 us
    ppermute x12, waiting for transfers between devices, along(): return lax.ppermute(array, 'ray', pairs)  27.1 us
    ppermute x19, starting transfers between devices, beside(): lax.ppermute(array, 'grp', [(g, g ^ flip) for g in range(group_count)])  21.1 us
    ppermute x12, starting transfers between devices, along(): return lax.ppermute(array, 'ray', pairs)  13 us
    pallas_call x1, Pallas kernels, render(): pl.pallas_call(functools.partial(render_kernel, ray_count, relative), out...  8.38 us
    pallas_call x2, Pallas kernels, forward(): pl.pallas_call(functools.partial(forward_kernel, first, blocks, len(own),...  7.44 us
    ppermute x8, waiting for transfers between devices, partner(): return lax.ppermute(array, 'ray', [(r, r ^ flip) for r in range(ray_count)])  6.6 us
    pallas_call x2, Pallas kernels, up_gradient(): pl.pallas_call(functools.partial(up_grad_kernel, side, weight_pieces, act...  5.74 us
  transfers between devices with their start and end apart: 39, of which 28 were waited for; matrix products, arithmetic and copies ran while one was open for 0% of the time, Pallas kernels for 16%

profile of v10, /device:TPU:8, one launch (start us, length us, event | category | flops | bytes accessed | tf_op | source)
XLA Modules:
  0.0 154.5 jit_solution(7735809504458841118)
XLA Ops:
  3.9 3.0 %collective-permute-start.4 = (bf16[2,64,1024]{2,1,0:T(8,128)(2,1)}, bf16[2,64,1024]{2,1,0:T(8,128)(2,1)S(1)}, u32[]{:S(2)}, u32[]{:S(2)}) collective-permute-start(bf16[2,64,1024]{2,1,0:T(8,128)(2,1)} %quarter.1), channel_id=1, source_target_pairs={{0,4},{1,5},{2,6},{3,7},{4,0},{5,1},{6,2},{7,3},{8,12},{9,13},{10,... | collective-permute-start | bytes 786440 | tf_op jit(solution)/shard_map/ppermute | solution.py:991
  6.9 2.5 %collective-permute-start.5 = (bf16[2,64,1024]{2,1,0:T(8,128)(2,1)}, bf16[2,64,1024]{2,1,0:T(8,128)(2,1)}, u32[]{:S(2)}, u32[]{:S(2)}) collective-permute-start(bf16[2,64,1024]{2,1,0:T(8,128)(2,1)} %quarter.1), channel_id=1, source_target_pairs={{0,2},{1,3},{2,4},{3,5},{4,6},{5,7},{6,0},{7,1},{8,10},{9,11},{10,... | collective-permute-start | bytes 786440 | tf_op jit(solution)/shard_map/ppermute | solution.py:991
  10.8 8.4 %render.1 = (bf16[4,64,1024]{2,1,0:T(8,128)(2,1)S(1)}, bf16[4,64,1024]{2,1,0:T(8,128)(2,1)S(1)}) custom-call(s32[1]{0:T(128)} %bitcast.1.me_ref, s32[1,8]{1,0:T(1,128)S(1)} %copy-done.11, s32[32,512]{1,0:T(8,128)S(1)} %copy-done.7, f32[32,512]{1,0:T(8,128)S(1)} %copy-done.8, s32[1,512]{1,0:T(1,128)S(1)} %bitcast.11, s32[1,4096]{1,0:T(1,128)S(1)} %copy-done.6, ...), custom_call_target="tpu_custom_call" | custom-call | flops 1048576 | bytes 65536 | tf_op jit(solution)/shard_map/render/pallas_call | solution.py:148
  19.2 5.5 %collective-permute-done.refs_0_ = bf16[2,64,1024]{2,1,0:T(8,128)(2,1)} collective-permute-done((bf16[2,64,1024]{2,1,0:T(8,128)(2,1)}, bf16[2,64,1024]{2,1,0:T(8,128)(2,1)}, u32[]{:S(2)}, u32[]{:S(2)}) %collective-permute-start) | collective-permute-done | bytes 262176 | tf_op jit(solution)/shard_map/ppermute | solution.py:991
  25.6 1.6 %collective-permute-start.1 = (bf16[1,2,64,1024]{3,2,1,0:T(8,128)(2,1)S(1)}, bf16[1,2,64,1024]{3,2,1,0:T(8,128)(2,1)S(1)}, u32[]{:S(2)}, u32[]{:S(2)}) collective-permute-start(bf16[1,2,64,1024]{3,2,1,0:T(8,128)(2,1)S(1)} %pack.4.refs_2_.refs_1_), channel_id=1, source_target_pairs={{0,8},{8,0},{16,24},{24,16},{1,9},{9,1},{17,25},{25,17},{2,10},{10... | collective-permute-start | bytes 786440 | tf_op jit(solution)/shard_map/ppermute | solution.py:984
  27.2 1.5 collective-permute-start.2
  30.4 1.6 %collective-permute-done.1.refs_2_ = bf16[1,2,64,1024]{3,2,1,0:T(8,128)(2,1)S(1)} collective-permute-done((bf16[1,2,64,1024]{3,2,1,0:T(8,128)(2,1)S(1)}, bf16[1,2,64,1024]{3,2,1,0:T(8,128)(2,1)S(1)}, u32[]{:S(2)}, u32[]{:S(2)}) %collective-permute-start.1) | collective-permute-done | bytes 262176 | tf_op jit(solution)/shard_map/ppermute | solution.py:984
  32.1 4.3 %collective-permute-done.2.refs_3_ = bf16[1,2,64,1024]{3,2,1,0:T(8,128)(2,1)S(1)} collective-permute-done((bf16[1,2,64,1024]{3,2,1,0:T(8,128)(2,1)S(1)}, bf16[1,2,64,1024]{3,2,1,0:T(8,128)(2,1)S(1)}, u32[]{:S(2)}, u32[]{:S(2)}) %collective-permute-start.2) | collective-permute-done | bytes 262176 | tf_op jit(solution)/shard_map/ppermute | solution.py:984
  39.2 1.4 collective-permute-start.8
  41.7 3.1 %tokens.1 = (bf16[512,1024]{1,0:T(8,128)(2,1)S(1)}, bf16[512,1024]{1,0:T(8,128)(2,1)S(1)}, bf16[1024,512]{1,0:T(8,128)(2,1)S(1)}) custom-call(s32[1]{0:T(128)} %bitcast.1.me_ref, s32[1,8]{1,0:T(1,128)S(1)} %copy-done.11, s32[1,4096]{1,0:T(1,128)S(1)} %copy-done.6, bf16[512,1024]{1,0:T(8,128)(2,1)S(1)} %copy-done.1, f32[1,1024]{1,0:T(1,128)S(1)} %bitcast.8), custom_call_target="tpu_custom_call" | custom-call | flops 1048576 | bytes 65536 | tf_op jit(solution)/shard_map/tokens/pallas_call | solution.py:234
  44.8 3.1 %forward.2 = (bf16[2,8,64,512]{3,2,1,0:T(8,128)(2,1)S(1)}, f32[2,8,64,512]{3,2,1,0:T(8,128)S(1)}, f32[512,1024]{1,0:T(8,128)S(1)}) custom-call(bf16[1024,512]{1,0:T(8,128)(2,1)S(1)} %get-tuple-element.55.refs_0_, bf16[8,2,64,1024]{3,2,1,0:T(8,128)(2,1)S(1)} %pack.6.refs_1_.refs_0_, bf16[8,2,64,1024]{3,2,1,0:T(8,128)(2,1)S(1)} %collective-permute-done.9.refs_2_.refs_0_), custom_call_target="tpu_custom_call" | custom-call | flops 1048576 | bytes 65536 | tf_op jit(solution)/shard_map/forward/pallas_call | solution.py:650
  47.9 4.0 %collective-permute-done.6.refs_1_ = bf16[2,2,64,1024]{3,2,1,0:T(8,128)(2,1)S(1)} collective-permute-done((bf16[2,2,64,1024]{3,2,1,0:T(8,128)(2,1)S(1)}, bf16[2,2,64,1024]{3,2,1,0:T(8,128)(2,1)S(1)}, u32[]{:S(2)}, u32[]{:S(2)}) %collective-permute-start.6) | collective-permute-done | bytes 524320 | tf_op jit(solution)/shard_map/ppermute | solution.py:984
  51.9 9.7 %collective-permute-done.7.refs_2_ = bf16[2,2,64,1024]{3,2,1,0:T(8,128)(2,1)S(1)} collective-permute-done((bf16[2,2,64,1024]{3,2,1,0:T(8,128)(2,1)S(1)}, bf16[2,2,64,1024]{3,2,1,0:T(8,128)(2,1)S(1)}, u32[]{:S(2)}, u32[]{:S(2)}) %collective-permute-start.7) | collective-permute-done | bytes 524320 | tf_op jit(solution)/shard_map/ppermute | solution.py:984
  61.6 1.6 %collective-permute-done.8.refs_3_ = bf16[2,2,64,1024]{3,2,1,0:T(8,128)(2,1)S(1)} collective-permute-done((bf16[2,2,64,1024]{3,2,1,0:T(8,128)(2,1)S(1)}, bf16[2,2,64,1024]{3,2,1,0:T(8,128)(2,1)S(1)}, u32[]{:S(2)}, u32[]{:S(2)}) %collective-permute-start.8) | collective-permute-done | bytes 524320 | tf_op jit(solution)/shard_map/ppermute | solution.py:984
  63.7 8.5 %collective-permute-done.14.refs_9_ = bf16[2,64,1024]{2,1,0:T(8,128)(2,1)S(1)} collective-permute-done((bf16[2,64,1024]{2,1,0:T(8,128)(2,1)S(1)}, bf16[2,64,1024]{2,1,0:T(8,128)(2,1)S(1)}, u32[]{:S(2)}, u32[]{:S(2)}) %collective-permute-start.14) | collective-permute-done | bytes 262176 | tf_op jit(solution)/shard_map/ppermute | solution.py:991
  72.2 4.4 %forward.3 = (bf16[2,8,64,512]{3,2,1,0:T(8,128)(2,1)S(1)}, f32[2,8,64,512]{3,2,1,0:T(8,128)S(1)}, bf16[512,1024]{1,0:T(8,128)(2,1)S(1)}, bf16[1024,512]{1,0:T(8,128)(2,1)S(1)}, f32[8,1024]{1,0:T(8,128)S(1)}) custom-call(bf16[1024,512]{1,0:T(8,128)(2,1)S(1)} %get-tuple-element.55.refs_0_, bf16[8,2,64,1024]{3,2,1,0:T(8,128)(2,1)S(1)} %pack.7.refs_1_, ...), custom_call_target="tpu_custom_call" | custom-call | flops 1048576 | bytes 65536 | tf_op jit(solution)/shard_map/forward/pallas_call | solution.py:650
  77.9 2.7 %up_gradient.2 = (bf16[4,4,64,1024]{3,2,1,0:T(8,128)(2,1)S(1)}, f32[1,1024]{1,0:T(1,128)S(1)}) custom-call(bf16[8,2,64,1024]{3,2,1,0:T(8,128)(2,1)S(1)} %collective-permute-done.9.refs_2_.refs_0_, bf16[8,2,64,1024]{3,2,1,0:T(8,128)(2,1)S(1)} %collective-permute-done.13.refs_2_.refs_1_, f32[2,8,64,512]{3,2,1,0:T(8,128)S(1)} %get-tuple-element.60.refs_2_, ...), custom_call_target="tpu_custom_call" | custom-call | flops 1048576 | bytes 65536 | tf_op jit(solution)/shard_map/up_gradient/pallas_call | solution.py:822
  82.0 1.3 down_gradient.3
  84.2 1.5 collective-permute-start.28
  85.7 3.0 %up_gradient.3 = (bf16[4,64,1024]{2,1,0:T(8,128)(2,1)S(1)}, bf16[4,64,1024]{2,1,0:T(8,128)(2,1)S(1)}, bf16[4,64,1024]{2,1,0:T(8,128)(2,1)S(1)}, bf16[2,64,1024]{...) custom-call(bf16[8,2,64,1024]{3,2,1,0:T(8,128)(2,1)S(1)} %pack.6.refs_1_.refs_0_, ...), custom_call_target="tpu_custom_call" | custom-call | flops 1048576 | bytes 65536 | tf_op jit(solution)/shard_map/up_gradient/pallas_call | solution.py:822
  92.0 3.6 %collective-permute-done.21 = f32[8,1024]{1,0:T(8,128)S(1)} collective-permute-done((f32[8,1024]{1,0:T(8,128)S(1)}, f32[8,1024]{1,0:T(8,128)S(1)}, u32[]{:S(2)}, u32[]{:S(2)}) %collective-permute-start.21) | collective-permute-done | bytes 32800 | tf_op jit(solution)/shard_map/ppermute | solution.py:987
  95.7 2.5 %collective-permute-done.27.x_ref = bf16[4,64,1024]{2,1,0:T(8,128)(2,1)S(1)} collective-permute-done((bf16[4,64,1024]{2,1,0:T(8,128)(2,1)S(1)}, bf16[4,64,1024]{2,1,0:T(8,128)(2,1)S(1)}, u32[]{:S(2)}, u32[]{:S(2)}) %collective-permute-start.27) | collective-permute-done | bytes 524320 | tf_op jit(solution)/shard_map/ppermute | solution.py:984
  101.3 8.1 %collective-permute-done.16.x_ref = bf16[4,64,1024]{2,1,0:T(8,128)(2,1)S(1)} collective-permute-done((bf16[4,64,1024]{2,1,0:T(8,128)(2,1)S(1)}, bf16[4,64,1024]{2,1,0:T(8,128)(2,1)S(1)}, u32[]{:S(2)}, u32[]{:S(2)}) %collective-permute-start.16) | collective-permute-done | bytes 524320 | tf_op jit(solution)/shard_map/ppermute | solution.py:984
  112.5 1.7 %collective-permute-start.22 = (f32[8,1024]{1,0:T(8,128)S(1)}, f32[8,1024]{1,0:T(8,128)S(1)}, u32[]{:S(2)}, u32[]{:S(2)}) collective-permute-start(f32[8,1024]{1,0:T(8,128)S(1)} %add.10.refs_0_), channel_id=1, source_target_pairs={{0,4},{1,5},{2,6},{3,7},{4,0},{5,1},{6,2},{7,3},{8,12},{9,13},{10,... | collective-permute-start | bytes 98312 | tf_op jit(solution)/shard_map/ppermute | solution.py:987
  116.1 2.6 %collective-permute-start.32 = (bf16[64,1024]{1,0:T(8,128)(2,1)S(1)}, bf16[64,1024]{1,0:T(8,128)(2,1)S(1)}, u32[]{:S(2)}, u32[]{:S(2)}) collective-permute-start(bf16[64,1024]{1,0:T(8,128)(2,1)S(1)} %get-tuple-element.94), channel_id=1, source_target_pairs={{0,4},{1,5},{2,6},{3,7},{4,0},{5,1},{6,2},{7,3},{8,12},{9,13},{10,... | collective-permute-start | bytes 393224 | tf_op jit(solution)/shard_map/ppermute | solution.py:991
  121.1 2.3 %collective-permute-start.24 = (bf16[64,1024]{1,0:T(8,128)(2,1)S(1)}, bf16[64,1024]{1,0:T(8,128)(2,1)S(1)}, u32[]{:S(2)}, u32[]{:S(2)}) collective-permute-start(bf16[64,1024]{1,0:T(8,128)(2,1)S(1)} %get-tuple-element.80), channel_id=1, source_target_pairs={{0,4},{1,5},{2,6},{3,7},{4,0},{5,1},{6,2},{7,3},{8,12},{9,13},{10,... | collective-permute-start | bytes 393224 | tf_op jit(solution)/shard_map/ppermute | solution.py:991
  124.6 9.2 %collective-permute-done.32.refs_2_ = bf16[64,1024]{1,0:T(8,128)(2,1)S(1)} collective-permute-done((bf16[64,1024]{1,0:T(8,128)(2,1)S(1)}, bf16[64,1024]{1,0:T(8,128)(2,1)S(1)}, u32[]{:S(2)}, u32[]{:S(2)}) %collective-permute-start.32) | collective-permute-done | bytes 131104 | tf_op jit(solution)/shard_map/ppermute | solution.py:991
  134.9 1.3 collective-permute-start.34
  137.5 2.3 %collective-permute-done.25.refs_3_ = bf16[64,1024]{1,0:T(8,128)(2,1)S(1)} collective-permute-done((bf16[64,1024]{1,0:T(8,128)(2,1)S(1)}, bf16[64,1024]{1,0:T(8,128)(2,1)S(1)}, u32[]{:S(2)}, u32[]{:S(2)}) %collective-permute-start.25) | collective-permute-done | bytes 131104 | tf_op jit(solution)/shard_map/ppermute | solution.py:991
  141.3 1.8 %collective-permute-start.38 = (bf16[144,1024]{1,0:T(8,128)(2,1)S(1)}, bf16[144,1024]{1,0:T(8,128)(2,1)S(1)}, u32[]{:S(2)}, u32[]{:S(2)}) collective-permute-start(bf16[144,1024]{1,0:T(8,128)(2,1)S(1)} %get-tuple-element.97), channel_id=1, source_target_pairs={{0,24},{8,16},{16,8},{24,0},{1,25},{9,17},{17,9},{25,1},{2,26},{10... | collective-permute-start | bytes 884744 | tf_op jit(solution)/shard_map/ppermute | solution.py:984
  144.9 7.7 %collective-permute-done.36.refs_1_ = bf16[80,1024]{1,0:T(8,128)(2,1)S(1)} collective-permute-done((bf16[80,1024]{1,0:T(8,128)(2,1)S(1)}, bf16[80,1024]{1,0:T(8,128)(2,1)S(1)}, u32[]{:S(2)}, u32[]{:S(2)}) %collective-permute-start.36) | collective-permute-done | bytes 163872 | tf_op jit(solution)/shard_map/ppermute | solution.py:984
  152.8 1.7 %place.1 = (f32[1024,256]{1,0:T(8,128)}, f32[256,1024]{1,0:T(8,128)}, f32[1,1024]{1,0:T(1,128)}, f32[1,1024]{1,0:T(1,128)}, f32[1,1]{1,0:T(1,128)}) custom-call(s32[1]{0:T(128)} %bitcast.group_ref, bf16[80,1024]{1,0:T(8,128)(2,1)S(1)} %get-tuple-element.96.refs_0_, bf16[80,1024]{1,0:T(8,128)(2,1)S(1)} %collective-permute-done.36.refs_1_, ...), custom_call_target="tpu_custom_call" | custom-call | flops 1048576 | bytes 65536 | tf_op jit(solution)/shard_map/place/pallas_call | solution.py:950
  (99 shorter events, 36.0 us)
Async XLA Ops:
  3.8 20.8 %collective-permute-start = (bf16[2,64,1024]{2,1,0:T(8,128)(2,1)}, bf16[2,64,1024]{2,1,0:T(8,128)(2,1)}, u32[]{:S(2)}, u32[]{:S(2)}) collective-permute-start(bf16[2,64,1024]{2,1,0:T(8,128)(2,1)} %quarter.1), channel_id=1, source_target_pairs={{0,6},{1,7},{2,0},{3,1},{4,2},{5,3},{6,4},{7,5},{8,14},{9,15},{10,... | collective-permute-start | bytes 786440 | tf_op jit(solution)/shard_map/ppermute | solution.py:991
  3.9 25.5 %collective-permute-start.4 = (bf16[2,64,1024]{2,1,0:T(8,128)(2,1)}, bf16[2,64,1024]{2,1,0:T(8,128)(2,1)S(1)}, u32[]{:S(2)}, u32[]{:S(2)}) collective-permute-start(bf16[2,64,1024]{2,1,0:T(8,128)(2,1)} %quarter.1), channel_id=1, source_target_pairs={{0,4},{1,5},{2,6},{3,7},{4,0},{5,1},{6,2},{7,3},{8,12},{9,13},{10,... | collective-permute-start | bytes 786440 | tf_op jit(solution)/shard_map/ppermute | solution.py:991
  6.9 22.5 %collective-permute-start.5 = (bf16[2,64,1024]{2,1,0:T(8,128)(2,1)}, bf16[2,64,1024]{2,1,0:T(8,128)(2,1)}, u32[]{:S(2)}, u32[]{:S(2)}) collective-permute-start(bf16[2,64,1024]{2,1,0:T(8,128)(2,1)} %quarter.1), channel_id=1, source_target_pairs={{0,2},{1,3},{2,4},{3,5},{4,6},{5,7},{6,0},{7,1},{8,10},{9,11},{10,... | collective-permute-start | bytes 786440 | tf_op jit(solution)/shard_map/ppermute | solution.py:991
  25.6 6.4 %collective-permute-start.1 = (bf16[1,2,64,1024]{3,2,1,0:T(8,128)(2,1)S(1)}, bf16[1,2,64,1024]{3,2,1,0:T(8,128)(2,1)S(1)}, u32[]{:S(2)}, u32[]{:S(2)}) collective-permute-start(bf16[1,2,64,1024]{3,2,1,0:T(8,128)(2,1)S(1)} %pack.4.refs_2_.refs_1_), channel_id=1, source_target_pairs={{0,8},{8,0},{16,24},{24,16},{1,9},{9,1},{17,25},{25,17},{2,10},{10... | collective-permute-start | bytes 786440 | tf_op jit(solution)/shard_map/ppermute | solution.py:984
  27.2 9.2 %collective-permute-start.2 = (bf16[1,2,64,1024]{3,2,1,0:T(8,128)(2,1)S(1)}, bf16[1,2,64,1024]{3,2,1,0:T(8,128)(2,1)S(1)}, u32[]{:S(2)}, u32[]{:S(2)}) collective-permute-start(bf16[1,2,64,1024]{3,2,1,0:T(8,128)(2,1)S(1)} %pack.4.refs_2_.refs_1_), channel_id=1, source_target_pairs={{0,16},{8,24},{16,0},{24,8},{1,17},{9,25},{17,1},{25,9},{2,18},{10... | collective-permute-start | bytes 786440 | tf_op jit(solution)/shard_map/ppermute | solution.py:984
  28.7 7.7 %collective-permute-start.3 = (bf16[1,2,64,1024]{3,2,1,0:T(8,128)(2,1)S(1)}, bf16[1,2,64,1024]{3,2,1,0:T(8,128)(2,1)S(1)}, u32[]{:S(2)}, u32[]{:S(2)}) collective-permute-start(bf16[1,2,64,1024]{3,2,1,0:T(8,128)(2,1)S(1)} %pack.4.refs_2_.refs_1_), channel_id=1, source_target_pairs={{0,24},{8,16},{16,8},{24,0},{1,25},{9,17},{17,9},{25,1},{2,26},{10... | collective-permute-start | bytes 786440 | tf_op jit(solution)/shard_map/ppermute | solution.py:984
  36.5 5.1 %collective-permute-start.9 = (bf16[8,2,64,1024]{3,2,1,0:T(8,128)(2,1)S(1)}, bf16[8,2,64,1024]{3,2,1,0:T(8,128)(2,1)S(1)}, u32[]{:S(2)}, u32[]{:S(2)}) collective-permute-start(bf16[8,2,64,1024]{3,2,1,0:T(8,128)(2,1)S(1)} %pack.6.refs_1_.refs_0_), channel_id=1, source_target_pairs={{0,1},{1,0},{2,3},{3,2},{4,5},{5,4},{6,7},{7,6},{8,9},{9,8},{10,11... | collective-permute-start | bytes 6291464 | tf_op jit(solution)/shard_map/ppermute | solution.py:987
  37.1 14.8 %collective-permute-start.6 = (bf16[2,2,64,1024]{3,2,1,0:T(8,128)(2,1)S(1)}, bf16[2,2,64,1024]{3,2,1,0:T(8,128)(2,1)S(1)}, u32[]{:S(2)}, u32[]{:S(2)}) collective-permute-start(bf16[2,2,64,1024]{3,2,1,0:T(8,128)(2,1)S(1)} %pack.5.refs_5_.refs_2_.refs_0_), channel_id=1, source_target_pairs={{0,8},{8,0},{16,24},{24,16},{1,9},{9,1},{17,25},{25,17},{2,10},{10... | collective-permute-start | bytes 1572872 | tf_op jit(solution)/shard_map/ppermute | solution.py:984
  38.0 23.5 %collective-permute-start.7 = (bf16[2,2,64,1024]{3,2,1,0:T(8,128)(2,1)S(1)}, bf16[2,2,64,1024]{3,2,1,0:T(8,128)(2,1)S(1)}, u32[]{:S(2)}, u32[]{:S(2)}) collective-permute-start(bf16[2,2,64,1024]{3,2,1,0:T(8,128)(2,1)S(1)} %pack.5.refs_5_.refs_2_.refs_0_), channel_id=1, source_target_pairs={{0,16},{8,24},{16,0},{24,8},{1,17},{9,25},{17,1},{25,9},{2,18},{10... | collective-permute-start | bytes 1572872 | tf_op jit(solution)/shard_map/ppermute | solution.py:984
  39.2 24.1 %collective-permute-start.8 = (bf16[2,2,64,1024]{3,2,1,0:T(8,128)(2,1)S(1)}, bf16[2,2,64,1024]{3,2,1,0:T(8,128)(2,1)S(1)}, u32[]{:S(2)}, u32[]{:S(2)}) collective-permute-start(bf16[2,2,64,1024]{3,2,1,0:T(8,128)(2,1)S(1)} %pack.5.refs_5_.refs_2_.refs_0_), channel_id=1, source_target_pairs={{0,24},{8,16},{16,8},{24,0},{1,25},{9,17},{17,9},{25,1},{2,26},{10... | collective-permute-start | bytes 1572872 | tf_op jit(solution)/shard_map/ppermute | solution.py:984
  41.6 21.6 %collective-permute-start.11 = (bf16[2,64,1024]{2,1,0:T(8,128)(2,1)S(1)}, bf16[2,64,1024]{2,1,0:T(8,128)(2,1)S(1)}, u32[]{:S(2)}, u32[]{:S(2)}) collective-permute-start(bf16[2,64,1024]{2,1,0:T(8,128)(2,1)S(1)} %get-tuple-element.58), channel_id=1, source_target_pairs={{0,2},{1,3},{2,4},{3,5},{4,6},{5,7},{6,0},{7,1},{8,10},{9,11},{10,... | collective-permute-start | bytes 786440 | tf_op jit(solution)/shard_map/ppermute | solution.py:991
  41.6 21.6 %collective-permute-start.12 = (bf16[2,64,1024]{2,1,0:T(8,128)(2,1)S(1)}, bf16[2,64,1024]{2,1,0:T(8,128)(2,1)S(1)}, u32[]{:S(2)}, u32[]{:S(2)}) collective-permute-start(bf16[2,64,1024]{2,1,0:T(8,128)(2,1)S(1)} %get-tuple-element.59), channel_id=1, source_target_pairs={{0,4},{1,5},{2,6},{3,7},{4,0},{5,1},{6,2},{7,3},{8,12},{9,13},{10,... | collective-permute-start | bytes 786440 | tf_op jit(solution)/shard_map/ppermute | solution.py:991
  63.4 8.8 %collective-permute-start.13 = (bf16[8,2,64,1024]{3,2,1,0:T(8,128)(2,1)S(1)}, bf16[8,2,64,1024]{3,2,1,0:T(8,128)(2,1)S(1)}, u32[]{:S(2)}, u32[]{:S(2)}) collective-permute-start(bf16[8,2,64,1024]{3,2,1,0:T(8,128)(2,1)S(1)} %pack.7.refs_1_), channel_id=1, source_target_pairs={{0,1},{1,0},{2,3},{3,2},{4,5},{5,4},{6,7},{7,6},{8,9},{9,8},{10,11... | collective-permute-start | bytes 6291464 | tf_op jit(solution)/shard_map/ppermute | solution.py:987
  63.4 8.7 %collective-permute-start.14 = (bf16[2,64,1024]{2,1,0:T(8,128)(2,1)S(1)}, bf16[2,64,1024]{2,1,0:T(8,128)(2,1)S(1)}, u32[]{:S(2)}, u32[]{:S(2)}) collective-permute-start(bf16[2,64,1024]{2,1,0:T(8,128)(2,1)S(1)} %get-tuple-element.63), channel_id=1, source_target_pairs={{0,6},{1,7},{2,0},{3,1},{4,2},{5,3},{6,4},{7,5},{8,14},{9,15},{10,... | collective-permute-start | bytes 786440 | tf_op jit(solution)/shard_map/ppermute | solution.py:991
  83.3 14.8 %collective-permute-start.27 = (bf16[4,64,1024]{2,1,0:T(8,128)(2,1)S(1)}, bf16[4,64,1024]{2,1,0:T(8,128)(2,1)S(1)}, u32[]{:S(2)}, u32[]{:S(2)}) collective-permute-start(bf16[4,64,1024]{2,1,0:T(8,128)(2,1)S(1)} %get-tuple-element.86), channel_id=1, source_target_pairs={{0,8},{8,0},{16,24},{24,16},{1,9},{9,1},{17,25},{25,17},{2,10},{10... | collective-permute-start | bytes 1572872 | tf_op jit(solution)/shard_map/ppermute | solution.py:984
  84.2 14.8 %collective-permute-start.28 = (bf16[4,64,1024]{2,1,0:T(8,128)(2,1)S(1)}, bf16[4,64,1024]{2,1,0:T(8,128)(2,1)S(1)}, u32[]{:S(2)}, u32[]{:S(2)}) collective-permute-start(bf16[4,64,1024]{2,1,0:T(8,128)(2,1)S(1)} %get-tuple-element.87), channel_id=1, source_target_pairs={{0,16},{8,24},{16,0},{24,8},{1,17},{9,25},{17,1},{25,9},{2,18},{10... | collective-permute-start | bytes 1572872 | tf_op jit(solution)/shard_map/ppermute | solution.py:984
  88.7 20.7 %collective-permute-start.16 = (bf16[4,64,1024]{2,1,0:T(8,128)(2,1)S(1)}, bf16[4,64,1024]{2,1,0:T(8,128)(2,1)S(1)}, u32[]{:S(2)}, u32[]{:S(2)}) collective-permute-start(bf16[4,64,1024]{2,1,0:T(8,128)(2,1)S(1)} %get-tuple-element.71), channel_id=1, source_target_pairs={{0,8},{8,0},{16,24},{24,16},{1,9},{9,1},{17,25},{25,17},{2,10},{10... | collective-permute-start | bytes 1572872 | tf_op jit(solution)/shard_map/ppermute | solution.py:984
  89.3 20.9 %collective-permute-start.17 = (bf16[4,64,1024]{2,1,0:T(8,128)(2,1)S(1)}, bf16[4,64,1024]{2,1,0:T(8,128)(2,1)S(1)}, u32[]{:S(2)}, u32[]{:S(2)}) collective-permute-start(bf16[4,64,1024]{2,1,0:T(8,128)(2,1)S(1)} %get-tuple-element.72), channel_id=1, source_target_pairs={{0,16},{8,24},{16,0},{24,8},{1,17},{9,25},{17,1},{25,9},{2,18},{10... | collective-permute-start | bytes 1572872 | tf_op jit(solution)/shard_map/ppermute | solution.py:984
  99.1 15.9 %collective-permute-start.29 = (bf16[2,64,1024]{2,1,0:T(8,128)(2,1)S(1)}, bf16[2,64,1024]{2,1,0:T(8,128)(2,1)S(1)}, u32[]{:S(2)}, u32[]{:S(2)}) collective-permute-start(bf16[2,64,1024]{2,1,0:T(8,128)(2,1)S(1)} %get-tuple-element.90), channel_id=1, source_target_pairs={{0,8},{8,0},{16,24},{24,16},{1,9},{9,1},{17,25},{25,17},{2,10},{10... | collective-permute-start | bytes 786440 | tf_op jit(solution)/shard_map/ppermute | solution.py:984
  100.4 15.4 %collective-permute-start.30 = (bf16[2,64,1024]{2,1,0:T(8,128)(2,1)S(1)}, bf16[2,64,1024]{2,1,0:T(8,128)(2,1)S(1)}, u32[]{:S(2)}, u32[]{:S(2)}) collective-permute-start(bf16[2,64,1024]{2,1,0:T(8,128)(2,1)S(1)} %get-tuple-element.91), channel_id=1, source_target_pairs={{0,16},{8,24},{16,0},{24,8},{1,17},{9,25},{17,1},{25,9},{2,18},{10... | collective-permute-start | bytes 786440 | tf_op jit(solution)/shard_map/ppermute | solution.py:984
  110.4 9.5 %collective-permute-start.18 = (bf16[2,64,1024]{2,1,0:T(8,128)(2,1)S(1)}, bf16[2,64,1024]{2,1,0:T(8,128)(2,1)S(1)}, u32[]{:S(2)}, u32[]{:S(2)}) collective-permute-start(bf16[2,64,1024]{2,1,0:T(8,128)(2,1)S(1)} %get-tuple-element.75), channel_id=1, source_target_pairs={{0,8},{8,0},{16,24},{24,16},{1,9},{9,1},{17,25},{25,17},{2,10},{10... | collective-permute-start | bytes 786440 | tf_op jit(solution)/shard_map/ppermute | solution.py:984
  111.7 8.7 %collective-permute-start.19 = (bf16[2,64,1024]{2,1,0:T(8,128)(2,1)S(1)}, bf16[2,64,1024]{2,1,0:T(8,128)(2,1)S(1)}, u32[]{:S(2)}, u32[]{:S(2)}) collective-permute-start(bf16[2,64,1024]{2,1,0:T(8,128)(2,1)S(1)} %get-tuple-element.76), channel_id=1, source_target_pairs={{0,16},{8,24},{16,0},{24,8},{1,17},{9,25},{17,1},{25,9},{2,18},{10... | collective-permute-start | bytes 786440 | tf_op jit(solution)/shard_map/ppermute | solution.py:984
  112.5 6.3 %collective-permute-start.22 = (f32[8,1024]{1,0:T(8,128)S(1)}, f32[8,1024]{1,0:T(8,128)S(1)}, u32[]{:S(2)}, u32[]{:S(2)}) collective-permute-start(f32[8,1024]{1,0:T(8,128)S(1)} %add.10.refs_0_), channel_id=1, source_target_pairs={{0,4},{1,5},{2,6},{3,7},{4,0},{5,1},{6,2},{7,3},{8,12},{9,13},{10,... | collective-permute-start | bytes 98312 | tf_op jit(solution)/shard_map/ppermute | solution.py:987
  116.0 7.5 %collective-permute-start.31 = (bf16[64,1024]{1,0:T(8,128)(2,1)S(1)}, bf16[64,1024]{1,0:T(8,128)(2,1)S(1)}, u32[]{:S(2)}, u32[]{:S(2)}) collective-permute-start(bf16[64,1024]{1,0:T(8,128)(2,1)S(1)} %get-tuple-element.93), channel_id=1, source_target_pairs={{0,2},{1,3},{2,4},{3,5},{4,6},{5,7},{6,0},{7,1},{8,10},{9,11},{10,... | collective-permute-start | bytes 393224 | tf_op jit(solution)/shard_map/ppermute | solution.py:991
  116.1 17.7 %collective-permute-start.32 = (bf16[64,1024]{1,0:T(8,128)(2,1)S(1)}, bf16[64,1024]{1,0:T(8,128)(2,1)S(1)}, u32[]{:S(2)}, u32[]{:S(2)}) collective-permute-start(bf16[64,1024]{1,0:T(8,128)(2,1)S(1)} %get-tuple-element.94), channel_id=1, source_target_pairs={{0,4},{1,5},{2,6},{3,7},{4,0},{5,1},{6,2},{7,3},{8,12},{9,13},{10,... | collective-permute-start | bytes 393224 | tf_op jit(solution)/shard_map/ppermute | solution.py:991
  118.8 16.1 %collective-permute-start.33 = (bf16[64,1024]{1,0:T(8,128)(2,1)S(1)}, bf16[64,1024]{1,0:T(8,128)(2,1)S(1)}, u32[]{:S(2)}, u32[]{:S(2)}) collective-permute-start(bf16[64,1024]{1,0:T(8,128)(2,1)S(1)} %get-tuple-element.95), channel_id=1, source_target_pairs={{0,6},{1,7},{2,0},{3,1},{4,2},{5,3},{6,4},{7,5},{8,14},{9,15},{10,... | collective-permute-start | bytes 393224 | tf_op jit(solution)/shard_map/ppermute | solution.py:991
  120.5 16.5 %collective-permute-start.23 = (bf16[64,1024]{1,0:T(8,128)(2,1)S(1)}, bf16[64,1024]{1,0:T(8,128)(2,1)S(1)}, u32[]{:S(2)}, u32[]{:S(2)}) collective-permute-start(bf16[64,1024]{1,0:T(8,128)(2,1)S(1)} %get-tuple-element.79), channel_id=1, source_target_pairs={{0,2},{1,3},{2,4},{3,5},{4,6},{5,7},{6,0},{7,1},{8,10},{9,11},{10,... | collective-permute-start | bytes 393224 | tf_op jit(solution)/shard_map/ppermute | solution.py:991
  121.1 16.5 %collective-permute-start.24 = (bf16[64,1024]{1,0:T(8,128)(2,1)S(1)}, bf16[64,1024]{1,0:T(8,128)(2,1)S(1)}, u32[]{:S(2)}, u32[]{:S(2)}) collective-permute-start(bf16[64,1024]{1,0:T(8,128)(2,1)S(1)} %get-tuple-element.80), channel_id=1, source_target_pairs={{0,4},{1,5},{2,6},{3,7},{4,0},{5,1},{6,2},{7,3},{8,12},{9,13},{10,... | collective-permute-start | bytes 393224 | tf_op jit(solution)/shard_map/ppermute | solution.py:991
  123.6 16.2 %collective-permute-start.25 = (bf16[64,1024]{1,0:T(8,128)(2,1)S(1)}, bf16[64,1024]{1,0:T(8,128)(2,1)S(1)}, u32[]{:S(2)}, u32[]{:S(2)}) collective-permute-start(bf16[64,1024]{1,0:T(8,128)(2,1)S(1)} %get-tuple-element.81), channel_id=1, source_target_pairs={{0,6},{1,7},{2,0},{3,1},{4,2},{5,3},{6,4},{7,5},{8,14},{9,15},{10,... | collective-permute-start | bytes 393224 | tf_op jit(solution)/shard_map/ppermute | solution.py:991
  141.3 11.4 %collective-permute-start.38 = (bf16[144,1024]{1,0:T(8,128)(2,1)S(1)}, bf16[144,1024]{1,0:T(8,128)(2,1)S(1)}, u32[]{:S(2)}, u32[]{:S(2)}) collective-permute-start(bf16[144,1024]{1,0:T(8,128)(2,1)S(1)} %get-tuple-element.97), channel_id=1, source_target_pairs={{0,24},{8,16},{16,8},{24,0},{1,25},{9,17},{17,9},{25,1},{2,26},{10... | collective-permute-start | bytes 884744 | tf_op jit(solution)/shard_map/ppermute | solution.py:984
  143.2 9.4 %collective-permute-start.36 = (bf16[80,1024]{1,0:T(8,128)(2,1)S(1)}, bf16[80,1024]{1,0:T(8,128)(2,1)S(1)}, u32[]{:S(2)}, u32[]{:S(2)}) collective-permute-start(bf16[80,1024]{1,0:T(8,128)(2,1)S(1)} %get-tuple-element.96.refs_0_), channel_id=1, source_target_pairs={{0,8},{8,0},{16,24},{24,16},{1,9},{9,1},{17,25},{25,17},{2,10},{10... | collective-permute-start | bytes 491528 | tf_op jit(solution)/shard_map/ppermute | solution.py:984
  143.7 9.1 %collective-permute-start.37 = (bf16[80,1024]{1,0:T(8,128)(2,1)S(1)}, bf16[80,1024]{1,0:T(8,128)(2,1)S(1)}, u32[]{:S(2)}, u32[]{:S(2)}) collective-permute-start(bf16[80,1024]{1,0:T(8,128)(2,1)S(1)} %get-tuple-element.96.refs_0_), channel_id=1, source_target_pairs={{0,16},{8,24},{16,0},{24,8},{1,17},{9,25},{17,1},{25,9},{2,18},{10... | collective-permute-start | bytes 491528 | tf_op jit(solution)/shard_map/ppermute | solution.py:984
  (20 other events, 129.6 us)

commit v11 on v10

--- a/solution.py
+++ b/solution.py
@@ -68,9 +68,11 @@
 
 def render_kernel(
     ray_count, relative, me_ref, owner_hbm, lists_hbm, opacity_hbm, counts_hbm, pixels_hbm,
-    features_hbm, near_ref, other_ref, owner_ref, ids_ref, opacity_ref, counts_ref, mine_ref,
-    features_ref, share_ref, table_ref, send_ref, sems,
+    features_hbm, *refs,
 ):
+    outs = refs[:-10]
+    owner_ref, ids_ref, opacity_ref, counts_ref, mine_ref, features_ref = refs[-10:-4]
+    share_ref, table_ref, send_ref, sems = refs[-4:]
     depth, rays = lists_hbm.shape
     gauss = features_hbm.shape[0]
     width = features_hbm.shape[1]
@@ -121,7 +123,7 @@
         shift = lax.div(owner, jnp.int32(2)) - lax.div(me, jnp.int32(2))
         shift = jnp.where(shift < 0, shift + chips, shift)
         flip = jnp.where(lax.rem(owner, jnp.int32(2)) == lax.rem(me, jnp.int32(2)), 0, 1)
-        block = flip * chips + shift
+        block = 2 * shift + flip
     else:
         block = owner
     slot = block * (rays // ray_count) + rank
@@ -130,26 +132,28 @@
     )
 
     piece = 256
-    half = rays // 2
+    span = rays // len(outs)
 
     @pl.loop(0, width // piece)
     def _(step):
         cols = pl.ds(pl.multiple_of(step * piece, piece), piece)
         rendered = dot_tn(table_ref[...], features_ref[:, cols]).astype(BF16)
         ordered = dot_nn(send_ref[...], rendered).astype(BF16)
-        near_ref[:, :, cols] = ordered[:half].reshape(*near_ref.shape[:2], piece)
-        other_ref[:, :, cols] = ordered[half:].reshape(*other_ref.shape[:2], piece)
+        for index, out in enumerate(outs):
+            rows = ordered[index * span:(index + 1) * span]
+            out[:, :, cols] = rows.reshape(*out.shape[:2], piece)
 
 
 def render(ray_count, relative, me, owner, lists, opacity, counts, pixels, features):
     depth, rays = lists.shape
     gauss, width = features.shape
-    shape = jax.ShapeDtypeStruct((ray_count // 2, rays // ray_count, width), BF16)
+    parts = ray_count // 2 if relative else 1
+    shape = jax.ShapeDtypeStruct((ray_count // parts, rays // ray_count, width), BF16)
     return pl.pallas_call(
         functools.partial(render_kernel, ray_count, relative),
-        out_shape=(shape, shape),
+        out_shape=(shape,) * parts,
         in_specs=[SMEM] + [HBM] * 6,
-        out_specs=(VMEM, VMEM),
+        out_specs=(VMEM,) * parts,
         scratch_shapes=[
             pltpu.VMEM(owner.shape, jnp.int32),
             pltpu.VMEM((depth, rays), jnp.int32),
@@ -476,7 +480,7 @@
         ray_count, False, me, block_owner, tile_lists, opacity, tile_counts.reshape(1, rows),
         ray_pixel, gaussian_features,
     )
-    rendered = jnp.concatenate(rendered, axis=0).reshape(rows, width)
+    rendered = rendered[0].reshape(rows, width)
     target = lax.all_to_all(rendered, "ray", split_axis=0, concat_axis=0, tiled=True)
     tokens, normed, normed_t = prepare_tokens(
         ray_count, False, me, block_owner, ray_pixel, image_tokens,
@@ -573,8 +577,8 @@
     mixed_in = None if first else refs.pop(0)
     if last:
         tokens_ref, scale_ref = refs[:2]
-        targets = refs[2:2 + blocks]
-        del refs[:2 + blocks]
+        targets, passed_ref = refs[2:2 + blocks], refs[2 + blocks]
+        del refs[:3 + blocks]
     act_ref, slope_ref = refs[:2]
     del refs[:2]
     width, rows = normed_t_ref.shape
@@ -594,7 +598,7 @@
                 slope_ref[side, start + index] = phi + hidden * density
             downs.append(ref[:, 1].reshape(count * part, width))
             start += count
-    if sides > 1:
+    if sides > 1 or last:
         act = act_ref[...].reshape(2 * start * part, rows)
         part_sum = dot_tn(act, jnp.concatenate(downs, axis=0))
     else:
@@ -613,10 +617,8 @@
     for index, target_ref in enumerate(targets):
         span = pl.ds(index * piece, piece)
         mixed = mixed_ref[span, :]
-        upstream, loss = finish_rows(
-            tokens_ref[span, :].astype(F32), mixed,
-            target_ref[...].reshape(piece, width).astype(F32), scale,
-        )
+        goal = jnp.concatenate([target_ref[0], passed_ref[index]], axis=0).astype(F32)
+        upstream, loss = finish_rows(tokens_ref[span, :].astype(F32), mixed, goal, scale)
         back = (upstream * scale).astype(BF16)
         back_ref[span, :] = back
         back_t_ref[:, span] = back.T
@@ -629,7 +631,7 @@
     part = own[0].shape[2]
     total = sum(array.shape[0] for array in own)
     first, last = mixed is None, finish is not None
-    blocks = len(finish) - 2 if last else 0
+    blocks = len(finish) - 3 if last else 0
     operands = [*after, normed_t, *own, *other]
     if not first:
         operands.append(mixed)
@@ -680,6 +682,29 @@
     )(*pieces, *after)
 
 
+def turn_kernel(y_ref, x_ref, a_ref, b_ref):
+    count = a_ref.shape[0]
+    a_ref[...] = y_ref[:count]
+    b_ref[...] = x_ref[count:]
+
+
+def turn(y, x):
+    count = y.shape[0]
+    first = count // 2
+    return pl.pallas_call(
+        turn_kernel,
+        out_shape=(
+            jax.ShapeDtypeStruct((first, *y.shape[1:]), BF16),
+            jax.ShapeDtypeStruct((count - first, *y.shape[1:]), BF16),
+        ),
+        in_specs=[VMEM] * 2,
+        out_specs=(VMEM, VMEM),
+        compiler_params=params(16),
+        cost_estimate=COST,
+        name="turn",
+    )(y, x)
+
+
 def tie_kernel(*refs):
     pass
 
@@ -697,25 +722,22 @@
     )(array, *after)
 
 
-def mix_kernel(*refs):
-    near_ref, other_ref = refs[:2]
-    outs = refs[-near_ref.shape[0]:]
-    for index, ref in enumerate(outs):
-        ref[0] = near_ref[index]
-        ref[1] = other_ref[index]
-
-
-def mix(near, other, *after):
-    count, each, width = near.shape
-    return pl.pallas_call(
-        mix_kernel,
-        out_shape=tuple([jax.ShapeDtypeStruct((2, each, width), BF16)] * count),
-        in_specs=[VMEM, VMEM] + [ANY] * len(after),
-        out_specs=tuple([VMEM] * count),
+def seconds_kernel(*refs):
+    for index, ref in enumerate(refs[:-1]):
+        refs[-1][index] = ref[1]
+
+
+def seconds(blocks):
+    count, (_, each, width) = len(blocks), blocks[0].shape
+    return pl.pallas_call(
+        seconds_kernel,
+        out_shape=jax.ShapeDtypeStruct((count, each, width), BF16),
+        in_specs=[VMEM] * count,
+        out_specs=VMEM,
         compiler_params=params(16),
         cost_estimate=COST,
-        name="mix",
-    )(near, other, *after)
+        name="seconds",
+    )(*blocks)
 
 
 def joined(refs, pieces, pick):
@@ -749,23 +771,23 @@
 
 
 def down_grad_kernel(side, act_pieces, add, *refs):
-    acts, back_ref = refs[:2], refs[2]
-    arrived = refs[3] if add else None
-    outs = refs[4:] if add else refs[3:]
+    acts, back_ref = refs[:3], refs[3]
+    arrived = refs[4] if add else None
+    outs = refs[5:] if add else refs[4:]
     for quarter in (3, 1, 2, 0):
         act = joined(acts, act_pieces[quarter], lambda ref, a, n: ref[side, a:a + n])
         emit(quarter, dot_nn(act, back_ref[...]), arrived, outs)
 
 
 def up_grad_kernel(side, weight_pieces, act_pieces, add, *refs):
-    weights, slopes = refs[:2], refs[2:4]
-    back_t_ref, normed_ref, gain_in = refs[4:7]
+    weights, slopes = refs[:3], refs[3:6]
+    back_t_ref, normed_ref, gain_in = refs[6:9]
     if add:
-        arrived, scale_ref, small_ref = refs[7:10]
-        outs, vector_ref, gain_ref = refs[10:-2], refs[-2], refs[-1]
+        arrived, scale_ref, small_ref = refs[9:12]
+        outs, vector_ref, gain_ref = refs[12:-2], refs[-2], refs[-1]
     else:
         arrived = None
-        outs, gain_ref = refs[7:-1], refs[-1]
+        outs, gain_ref = refs[9:-1], refs[-1]
     gain_ref[...] = gain_in[...]
     for quarter in (3, 1, 2, 0):
         pieces = weight_pieces[quarter]
@@ -992,37 +1014,44 @@
 
     mine = own_quarter(group, up_weight, down_weight, part)
     arrivals = [along(mine, -shift) for shift in range(1, depth)]
-    rendered, rendered_other = render(
+    rendered = render(
         ray_count, True, me, block_owner, tile_lists, opacity, tile_counts.reshape(1, rows),
         ray_pixel, gaussian_features,
     )
     half = depth // 2
-    low = pack(arrivals[:half - 1], rendered)
-    lows = [low] + [beside(low, flip) for flip in (1, 2, 3)]
+    low = pack(arrivals[:half - 1], rendered[0])
+    x_low, y_low = beside(low, 1), beside(low, 2)
     high = pack(arrivals[half - 1:], low)
-    highs = [high] + [beside(high, flip) for flip in (1, 2, 3)]
-    blocks = mix(rendered, partner(tie(rendered_other, low)), high)
-    targets = [blocks[0]] + [along(blocks[shift], shift) for shift in range(1, depth)]
-    early = pack([own_rows(group, up_weight, down_weight)] + lows, high)
+    x_high, y_high = beside(high, 1), beside(high, 2)
+    y_low = tie(y_low, high)
+    d_low = beside(y_low, 1)
+    targets = [rendered[0]] + [along(rendered[shift], shift) for shift in range(1, depth)]
+    early = pack([own_rows(group, up_weight, down_weight), low, x_low, y_low], high)
     early_other = partner(early)
     tokens, normed, normed_t = prepare_tokens(
         ray_count, True, me, block_owner, ray_pixel, image_tokens,
         layer_norm_gain.reshape(1, width),
     )
     act_early, slope_early, mixed = forward(normed_t, [early], [early_other])
-    late = pack(highs, mixed, *targets[1:-1])
+    late = pack([d_low, high, x_high, y_high], mixed, targets[half])
     late_other = partner(late)
-    act_late, slope_late, back, back_t, small = forward(
-        normed_t, [late], [late_other], mixed,
-        (tokens, layer_scale.reshape(1, width), *targets),
-    )
-    acts, slopes = (act_early, act_late), (slope_early, slope_late)
-    weights = ((early, late), (early_other, late_other))
+    passed_x, passed_y = turn(y_high, x_high)
+    d_high = [beside(passed_x, 1), beside(passed_y, 2)]
+    act_late, slope_late, mixed = forward(normed_t, [late], [late_other], mixed)
+    rest = [target for shift, target in enumerate(targets) if shift not in (0, half)]
+    last = pack(d_high, mixed, *rest)
+    last_other = partner(last)
+    act_last, slope_last, back, back_t, small = forward(
+        normed_t, [last], [last_other], mixed,
+        (tokens, layer_scale.reshape(1, width), *targets, partner(seconds(targets))),
+    )
+    acts, slopes = (act_early, act_late, act_last), (slope_early, slope_late, slope_last)
+    weights = ((early, late, last), (early_other, late_other, last_other))
     count = half - 1
+    rest = depth - half
     pieces = tuple(
-        ((0, q, 1), (0, 4 + q * count, count), (1, q * (depth - half), depth - half))
-        for q in range(4)
-    )
+        ((0, q, 1), (0, 4 + q * count, count), (1, count + q * rest, rest)) for q in range(3)
+    ) + (((0, 3, 1), (1, 0, count), (2, 0, rest)),)
     gain = jnp.zeros((1, width), F32)
     (down_other,) = down_gradient(1, pieces, depth, acts, back)
     down_arrived = partner(down_other)

time: 156 us -> 156 us (level)
  starting transfers between devices: 37.3 us -> 46.4 us
  waiting for transfers between devices: 79.4 us -> 70.5 us
    ppermute x19 -> x20, waiting for transfers between devices: 45.6 us -> 31.9 us  [beside(): lax.ppermute(array, 'grp', [(g, g ^ flip) for g in range(group_count)])]
    ppermute x12, waiting for transfers between devices: 27.1 us -> 32.7 us  [along(): return lax.ppermute(array, 'ray', pairs)]
    ppermute x12, starting transfers between devices: 13 us -> 18.3 us  [along(): return lax.ppermute(array, 'ray', pairs)]
    ppermute x8 -> x9, starting transfers between devices: 3.18 us -> 5.96 us  [partner(): return lax.ppermute(array, 'ray', [(r, r ^ flip) for r in range(ray_count)])]
    ppermute x19 -> x20, starting transfers between devices: 21.1 us -> 22.1 us  [beside(): lax.ppermute(array, 'grp', [(g, g ^ flip) for g in range(group_count)])]
    pallas_call x2 -> x3, Pallas kernels: 7.44 us -> 8.2 us  [forward(): pl.pallas_call(functools.partial(forward_kernel, first, blocks, len(own),...]
    ppermute x8 -> x9, waiting for transfers between devices: 6.6 us -> 5.99 us  [partner(): return lax.ppermute(array, 'ray', [(r, r ^ flip) for r in range(ray_count)])]
  transfers between devices with their start and end apart: 39 -> 41, of which waited for: 28 -> 24; matrix products, arithmetic and copies ran while one was open for 0% -> 0% of each run, Pallas kernels for 16% -> 18%
where the time goes in v11:
time: 156 us
  waiting for transfers between devices  70.5 us (45%)
  starting transfers between devices  46.4 us (30%)
  Pallas kernels  34.3 us (22%)
  local copies, waits for them, and re-layouts  3.45 us (2%)
    ppermute x12, waiting for transfers between devices, along(): return lax.ppermute(array, 'ray', pairs)  32.7 us
    ppermute x20, waiting for transfers between devices, beside(): lax.ppermute(array, 'grp', [(g, g ^ flip) for g in range(group_count)])  31.9 us
    ppermute x20, starting transfers between devices, beside(): lax.ppermute(array, 'grp', [(g, g ^ flip) for g in range(group_count)])  22.1 us
    ppermute x12, starting transfers between devices, along(): return lax.ppermute(array, 'ray', pairs)  18.3 us
    pallas_call x1, Pallas kernels, render(): pl.pallas_call(functools.partial(render_kernel, ray_count, relative), out...  8.38 us
    pallas_call x3, Pallas kernels, forward(): pl.pallas_call(functools.partial(forward_kernel, first, blocks, len(own),...  8.2 us
    ppermute x9, waiting for transfers between devices, partner(): return lax.ppermute(array, 'ray', [(r, r ^ flip) for r in range(ray_count)])  5.99 us
    ppermute x9, starting transfers between devices, partner(): return lax.ppermute(array, 'ray', [(r, r ^ flip) for r in range(ray_count)])  5.96 us
  transfers between devices with their start and end apart: 41, of which 24 were waited for; matrix products, arithmetic and copies ran while one was open for 0% of the time, Pallas kernels for 18%

profile of v11, /device:TPU:8, one launch (start us, length us, event | category | flops | bytes accessed | tf_op | source)
XLA Modules:
  0.0 155.6 jit_solution(2078558023039999673)
XLA Ops:
  3.9 3.0 %collective-permute-start.3 = (bf16[2,64,1024]{2,1,0:T(8,128)(2,1)}, bf16[2,64,1024]{2,1,0:T(8,128)(2,1)S(1)}, u32[]{:S(2)}, u32[]{:S(2)}) collective-permute-start(bf16[2,64,1024]{2,1,0:T(8,128)(2,1)} %quarter.1), channel_id=1, source_target_pairs={{0,4},{1,5},{2,6},{3,7},{4,0},{5,1},{6,2},{7,3},{8,12},{9,13},{10,... | collective-permute-start | bytes 786440 | tf_op jit(solution)/shard_map/ppermute | solution.py:1013
  6.9 2.5 %collective-permute-start.4 = (bf16[2,64,1024]{2,1,0:T(8,128)(2,1)}, bf16[2,64,1024]{2,1,0:T(8,128)(2,1)}, u32[]{:S(2)}, u32[]{:S(2)}) collective-permute-start(bf16[2,64,1024]{2,1,0:T(8,128)(2,1)} %quarter.1), channel_id=1, source_target_pairs={{0,2},{1,3},{2,4},{3,5},{4,6},{5,7},{6,0},{7,1},{8,10},{9,11},{10,... | collective-permute-start | bytes 786440 | tf_op jit(solution)/shard_map/ppermute | solution.py:1013
  10.8 8.4 %render.1 = (bf16[2,64,1024]{2,1,0:T(8,128)(2,1)S(1)}, bf16[2,64,1024]{2,1,0:T(8,128)(2,1)S(1)}, bf16[2,64,1024]{2,1,0:T(8,128)(2,1)S(1)}, bf16[2,64,1024]{2,1,0:T(8,128)(2,1)S(1)}) custom-call(s32[1]{0:T(128)} %bitcast.1.me_ref, s32[1,8]{1,0:T(1,128)S(1)} %copy-done.11, s32[32,512]{1,0:T(8,128)S(1)} %copy-done.7, f32[32,512]{1,0:T(8,128)S(1)} %copy-done.8, ...), custom_call_target="tpu_custom_call" | custom-call | flops 1048576 | bytes 65536 | tf_op jit(solution)/shard_map/render/pallas_call | solution.py:152
  19.2 5.5 %collective-permute-done.refs_0_ = bf16[2,64,1024]{2,1,0:T(8,128)(2,1)} collective-permute-done((bf16[2,64,1024]{2,1,0:T(8,128)(2,1)}, bf16[2,64,1024]{2,1,0:T(8,128)(2,1)}, u32[]{:S(2)}, u32[]{:S(2)}) %collective-permute-start) | collective-permute-done | bytes 262176 | tf_op jit(solution)/shard_map/ppermute | solution.py:1013
  25.6 1.6 %collective-permute-start.2 = (bf16[1,2,64,1024]{3,2,1,0:T(8,128)(2,1)S(1)}, bf16[1,2,64,1024]{3,2,1,0:T(8,128)(2,1)S(1)}, u32[]{:S(2)}, u32[]{:S(2)}) collective-permute-start(bf16[1,2,64,1024]{3,2,1,0:T(8,128)(2,1)S(1)} %pack.5.refs_2_.refs_1_), channel_id=1, source_target_pairs={{0,16},{8,24},{16,0},{24,8},{1,17},{9,25},{17,1},{25,9},{2,18},{10... | collective-permute-start | bytes 786440 | tf_op jit(solution)/shard_map/ppermute | solution.py:1006
  30.4 1.6 %collective-permute-done.2.refs_0_ = bf16[1,2,64,1024]{3,2,1,0:T(8,128)(2,1)S(1)} collective-permute-done((bf16[1,2,64,1024]{3,2,1,0:T(8,128)(2,1)S(1)}, bf16[1,2,64,1024]{3,2,1,0:T(8,128)(2,1)S(1)}, u32[]{:S(2)}, u32[]{:S(2)}) %collective-permute-start.2) | collective-permute-done | bytes 262176 | tf_op jit(solution)/shard_map/ppermute | solution.py:1006
  36.4 3.0 %tokens.1 = (bf16[512,1024]{1,0:T(8,128)(2,1)S(1)}, bf16[512,1024]{1,0:T(8,128)(2,1)S(1)}, bf16[1024,512]{1,0:T(8,128)(2,1)S(1)}) custom-call(s32[1]{0:T(128)} %bitcast.1.me_ref, s32[1,8]{1,0:T(1,128)S(1)} %copy-done.11, s32[1,4096]{1,0:T(1,128)S(1)} %copy-done.6, bf16[512,1024]{1,0:T(8,128)(2,1)S(1)} %copy-done.1, f32[1,1024]{1,0:T(1,128)S(1)} %bitcast.8), custom_call_target="tpu_custom_call" | custom-call | flops 1048576 | bytes 65536 | tf_op jit(solution)/shard_map/tokens/pallas_call | solution.py:238
  39.4 2.9 %forward.3 = (bf16[2,7,64,512]{3,2,1,0:T(8,128)(2,1)S(1)}, f32[2,7,64,512]{3,2,1,0:T(8,128)S(1)}, f32[512,1024]{1,0:T(8,128)S(1)}) custom-call(bf16[1024,512]{1,0:T(8,128)(2,1)S(1)} %get-tuple-element.58.refs_0_, bf16[7,2,64,1024]{3,2,1,0:T(8,128)(2,1)S(1)} %pack.7.refs_1_.refs_0_, bf16[7,2,64,1024]{3,2,1,0:T(8,128)(2,1)S(1)} %collective-permute-done.8.refs_2_.refs_0_), custom_call_target="tpu_custom_call" | custom-call | flops 1048576 | bytes 65536 | tf_op jit(solution)/shard_map/forward/pallas_call | solution.py:652
  42.4 5.0 %collective-permute-done.9.refs_5_.refs_2_.refs_8_ = bf16[2,64,1024]{2,1,0:T(8,128)(2,1)S(1)} collective-permute-done((bf16[2,64,1024]{2,1,0:T(8,128)(2,1)S(1)}, bf16[2,64,1024]{2,1,0:T(8,128)(2,1)S(1)}, u32[]{:S(2)}, u32[]{:S(2)}) %collective-permute-start.9) | collective-permute-done | bytes 262176 | tf_op jit(solution)/shard_map/ppermute | solution.py:1013
  47.4 6.4 %collective-permute-done.5.refs_0_ = bf16[1,2,64,1024]{3,2,1,0:T(8,128)(2,1)S(1)} collective-permute-done((bf16[1,2,64,1024]{3,2,1,0:T(8,128)(2,1)S(1)}, bf16[1,2,64,1024]{3,2,1,0:T(8,128)(2,1)S(1)}, u32[]{:S(2)}, u32[]{:S(2)}) %collective-permute-start.5) | collective-permute-done | bytes 262176 | tf_op jit(solution)/shard_map/ppermute | solution.py:1006
  54.0 2.0 %collective-permute-start.14 = (bf16[2,64,1024]{2,1,0:T(8,128)(2,1)S(1)}, bf16[2,64,1024]{2,1,0:T(8,128)(2,1)S(1)}, u32[]{:S(2)}, u32[]{:S(2)}) collective-permute-start(bf16[2,64,1024]{2,1,0:T(8,128)(2,1)S(1)} %get-tuple-element.65), channel_id=1, source_target_pairs={{0,6},{1,7},{2,0},{3,1},{4,2},{5,3},{6,4},{7,5},{8,14},{9,15},{10,... | collective-permute-start | bytes 786440 | tf_op jit(solution)/shard_map/ppermute | solution.py:1013
  58.1 5.0 %collective-permute-done.13.refs_3_.refs_1_.refs_7_ = bf16[2,64,1024]{2,1,0:T(8,128)(2,1)S(1)} collective-permute-done((bf16[2,64,1024]{2,1,0:T(8,128)(2,1)S(1)}, bf16[2,64,1024]{2,1,0:T(8,128)(2,1)S(1)}, u32[]{:S(2)}, u32[]{:S(2)}) %collective-permute-start.13) | collective-permute-done | bytes 262176 | tf_op jit(solution)/shard_map/ppermute | solution.py:1013
  63.1 3.5 %collective-permute-done.14.refs_4_.refs_3_.refs_9_ = bf16[2,64,1024]{2,1,0:T(8,128)(2,1)S(1)} collective-permute-done((bf16[2,64,1024]{2,1,0:T(8,128)(2,1)S(1)}, bf16[2,64,1024]{2,1,0:T(8,128)(2,1)S(1)}, u32[]{:S(2)}, u32[]{:S(2)}) %collective-permute-start.14) | collective-permute-done | bytes 262176 | tf_op jit(solution)/shard_map/ppermute | solution.py:1013
  66.7 2.9 %forward.4 = (bf16[2,7,64,512]{3,2,1,0:T(8,128)(2,1)S(1)}, f32[2,7,64,512]{3,2,1,0:T(8,128)S(1)}, f32[512,1024]{1,0:T(8,128)S(1)}) custom-call(bf16[1024,512]{1,0:T(8,128)(2,1)S(1)} %get-tuple-element.58.refs_0_, bf16[7,2,64,1024]{3,2,1,0:T(8,128)(2,1)S(1)} %pack.8.refs_1_, bf16[7,2,64,1024]{3,2,1,0:T(8,128)(2,1)S(1)} %collective-permute-done.12.refs_2_.refs_1_, ...), custom_call_target="tpu_custom_call" | custom-call | flops 1048576 | bytes 65536 | tf_op jit(solution)/shard_map/forward/pallas_call | solution.py:652
  71.8 2.4 %forward.5 = (bf16[2,2,64,512]{3,2,1,0:T(8,128)(2,1)S(1)}, f32[2,2,64,512]{3,2,1,0:T(8,128)S(1)}, bf16[512,1024]{1,0:T(8,128)(2,1)S(1)}, bf16[1024,512]{1,0:T(8,128)(2,1)S(1)}, f32[8,1024]{1,0:T(8,128)S(1)}) custom-call(bf16[1024,512]{1,0:T(8,128)(2,1)S(1)} %get-tuple-element.58.refs_0_, bf16[2,2,64,1024]{3,2,1,0:T(8,128)(2,1)S(1)} %pack.9.refs_1_.refs_2_, ...), custom_call_target="tpu_custom_call" | custom-call | flops 1048576 | bytes 65536 | tf_op jit(solution)/shard_map/forward/pallas_call | solution.py:652
  75.9 2.8 %up_gradient.2 = (bf16[4,4,64,1024]{3,2,1,0:T(8,128)(2,1)S(1)}, f32[1,1024]{1,0:T(1,128)S(1)}) custom-call(bf16[7,2,64,1024]{3,2,1,0:T(8,128)(2,1)S(1)} %collective-permute-done.8.refs_2_.refs_0_, bf16[7,2,64,1024]{3,2,1,0:T(8,128)(2,1)S(1)} %collective-permute-done.12.refs_2_.refs_1_, bf16[2,2,64,1024]{3,2,1,0:T(8,128)(2,1)S(1)} %collective-permute-done.15.refs_2_, ...), custom_call_target="tpu_custom_call" | custom-call | flops 1048576 | bytes 65536 | tf_op jit(solution)/shard_map/up_gradient/pallas_call | solution.py:844
  81.0 1.6 %collective-permute-start.29 = (bf16[4,64,1024]{2,1,0:T(8,128)(2,1)S(1)}, bf16[4,64,1024]{2,1,0:T(8,128)(2,1)S(1)}, u32[]{:S(2)}, u32[]{:S(2)}) collective-permute-start(bf16[4,64,1024]{2,1,0:T(8,128)(2,1)S(1)} %get-tuple-element.92), channel_id=1, source_target_pairs={{0,8},{8,0},{16,24},{24,16},{1,9},{9,1},{17,25},{25,17},{2,10},{10... | collective-permute-start | bytes 1572872 | tf_op jit(solution)/shard_map/ppermute | solution.py:1006
  84.1 3.0 %up_gradient.3 = (bf16[4,64,1024]{2,1,0:T(8,128)(2,1)S(1)}, bf16[4,64,1024]{2,1,0:T(8,128)(2,1)S(1)}, bf16[4,64,1024]{2,1,0:T(8,128)(2,1)S(1)}, bf16[2,64,1024]{...) custom-call(bf16[7,2,64,1024]{3,2,1,0:T(8,128)(2,1)S(1)} %pack.7.refs_1_.refs_0_, ...), custom_call_target="tpu_custom_call" | custom-call | flops 1048576 | bytes 65536 | tf_op jit(solution)/shard_map/up_gradient/pallas_call | solution.py:844
  91.7 2.4 %collective-permute-done.23 = f32[8,1024]{1,0:T(8,128)S(1)} collective-permute-done((f32[8,1024]{1,0:T(8,128)S(1)}, f32[8,1024]{1,0:T(8,128)S(1)}, u32[]{:S(2)}, u32[]{:S(2)}) %collective-permute-start.23) | collective-permute-done | bytes 32800 | tf_op jit(solution)/shard_map/ppermute | solution.py:1009
  94.2 1.7 %collective-permute-done.29.x_ref = bf16[4,64,1024]{2,1,0:T(8,128)(2,1)S(1)} collective-permute-done((bf16[4,64,1024]{2,1,0:T(8,128)(2,1)S(1)}, bf16[4,64,1024]{2,1,0:T(8,128)(2,1)S(1)}, u32[]{:S(2)}, u32[]{:S(2)}) %collective-permute-start.29) | collective-permute-done | bytes 524320 | tf_op jit(solution)/shard_map/ppermute | solution.py:1006
  99.7 7.4 %collective-permute-done.18.x_ref = bf16[4,64,1024]{2,1,0:T(8,128)(2,1)S(1)} collective-permute-done((bf16[4,64,1024]{2,1,0:T(8,128)(2,1)S(1)}, bf16[4,64,1024]{2,1,0:T(8,128)(2,1)S(1)}, u32[]{:S(2)}, u32[]{:S(2)}) %collective-permute-start.18) | collective-permute-done | bytes 524320 | tf_op jit(solution)/shard_map/ppermute | solution.py:1006
  110.9 3.1 %collective-permute-start.24 = (f32[8,1024]{1,0:T(8,128)S(1)}, f32[8,1024]{1,0:T(8,128)S(1)}, u32[]{:S(2)}, u32[]{:S(2)}) collective-permute-start(f32[8,1024]{1,0:T(8,128)S(1)} %add.10.refs_0_), channel_id=1, source_target_pairs={{0,4},{1,5},{2,6},{3,7},{4,0},{5,1},{6,2},{7,3},{8,12},{9,13},{10,... | collective-permute-start | bytes 98312 | tf_op jit(solution)/shard_map/ppermute | solution.py:1009
  115.1 3.5 %collective-permute-start.34 = (bf16[64,1024]{1,0:T(8,128)(2,1)S(1)}, bf16[64,1024]{1,0:T(8,128)(2,1)S(1)}, u32[]{:S(2)}, u32[]{:S(2)}) collective-permute-start(bf16[64,1024]{1,0:T(8,128)(2,1)S(1)} %get-tuple-element.100), channel_id=1, source_target_pairs={{0,4},{1,5},{2,6},{3,7},{4,0},{5,1},{6,2},{7,3},{8,12},{9,13},{10,... | collective-permute-start | bytes 393224 | tf_op jit(solution)/shard_map/ppermute | solution.py:1013
  118.7 1.9 %collective-permute-start.35 = (bf16[64,1024]{1,0:T(8,128)(2,1)S(1)}, bf16[64,1024]{1,0:T(8,128)(2,1)S(1)}, u32[]{:S(2)}, u32[]{:S(2)}) collective-permute-start(bf16[64,1024]{1,0:T(8,128)(2,1)S(1)} %get-tuple-element.101), channel_id=1, source_target_pairs={{0,6},{1,7},{2,0},{3,1},{4,2},{5,3},{6,4},{7,5},{8,14},{9,15},{10,... | collective-permute-start | bytes 393224 | tf_op jit(solution)/shard_map/ppermute | solution.py:1013
  121.0 2.4 %collective-permute-start.26 = (bf16[64,1024]{1,0:T(8,128)(2,1)S(1)}, bf16[64,1024]{1,0:T(8,128)(2,1)S(1)}, u32[]{:S(2)}, u32[]{:S(2)}) collective-permute-start(bf16[64,1024]{1,0:T(8,128)(2,1)S(1)} %get-tuple-element.85), channel_id=1, source_target_pairs={{0,4},{1,5},{2,6},{3,7},{4,0},{5,1},{6,2},{7,3},{8,12},{9,13},{10,... | collective-permute-start | bytes 393224 | tf_op jit(solution)/shard_map/ppermute | solution.py:1013
  123.4 1.9 %collective-permute-start.27 = (bf16[64,1024]{1,0:T(8,128)(2,1)S(1)}, bf16[64,1024]{1,0:T(8,128)(2,1)S(1)}, u32[]{:S(2)}, u32[]{:S(2)}) collective-permute-start(bf16[64,1024]{1,0:T(8,128)(2,1)S(1)} %get-tuple-element.86), channel_id=1, source_target_pairs={{0,6},{1,7},{2,0},{3,1},{4,2},{5,3},{6,4},{7,5},{8,14},{9,15},{10,... | collective-permute-start | bytes 393224 | tf_op jit(solution)/shard_map/ppermute | solution.py:1013
  125.3 4.1 %collective-permute-done.34.refs_2_ = bf16[64,1024]{1,0:T(8,128)(2,1)S(1)} collective-permute-done((bf16[64,1024]{1,0:T(8,128)(2,1)S(1)}, bf16[64,1024]{1,0:T(8,128)(2,1)S(1)}, u32[]{:S(2)}, u32[]{:S(2)}) %collective-permute-start.34) | collective-permute-done | bytes 131104 | tf_op jit(solution)/shard_map/ppermute | solution.py:1013
  129.4 5.3 %collective-permute-done.35.refs_3_ = bf16[64,1024]{1,0:T(8,128)(2,1)S(1)} collective-permute-done((bf16[64,1024]{1,0:T(8,128)(2,1)S(1)}, bf16[64,1024]{1,0:T(8,128)(2,1)S(1)}, u32[]{:S(2)}, u32[]{:S(2)}) %collective-permute-start.35) | collective-permute-done | bytes 131104 | tf_op jit(solution)/shard_map/ppermute | solution.py:1013
  137.3 3.0 %collective-permute-done.27.refs_3_ = bf16[64,1024]{1,0:T(8,128)(2,1)S(1)} collective-permute-done((bf16[64,1024]{1,0:T(8,128)(2,1)S(1)}, bf16[64,1024]{1,0:T(8,128)(2,1)S(1)}, u32[]{:S(2)}, u32[]{:S(2)}) %collective-permute-start.27) | collective-permute-done | bytes 131104 | tf_op jit(solution)/shard_map/ppermute | solution.py:1013
  140.7 1.8 %collective-permute-start.40 = (bf16[144,1024]{1,0:T(8,128)(2,1)S(1)}, bf16[144,1024]{1,0:T(8,128)(2,1)S(1)}, u32[]{:S(2)}, u32[]{:S(2)}) collective-permute-start(bf16[144,1024]{1,0:T(8,128)(2,1)S(1)} %get-tuple-element.103), channel_id=1, source_target_pairs={{0,24},{8,16},{16,8},{24,0},{1,25},{9,17},{17,9},{25,1},{2,26},{10... | collective-permute-start | bytes 884744 | tf_op jit(solution)/shard_map/ppermute | solution.py:1006
  144.2 8.7 %collective-permute-done.38.refs_1_ = bf16[80,1024]{1,0:T(8,128)(2,1)S(1)} collective-permute-done((bf16[80,1024]{1,0:T(8,128)(2,1)S(1)}, bf16[80,1024]{1,0:T(8,128)(2,1)S(1)}, u32[]{:S(2)}, u32[]{:S(2)}) %collective-permute-start.38) | collective-permute-done | bytes 163872 | tf_op jit(solution)/shard_map/ppermute | solution.py:1006
  153.8 1.7 %place.1 = (f32[1024,256]{1,0:T(8,128)}, f32[256,1024]{1,0:T(8,128)}, f32[1,1024]{1,0:T(1,128)}, f32[1,1024]{1,0:T(1,128)}, f32[1,1]{1,0:T(1,128)}) custom-call(s32[1]{0:T(128)} %bitcast.group_ref, bf16[80,1024]{1,0:T(8,128)(2,1)S(1)} %get-tuple-element.102.refs_0_, bf16[80,1024]{1,0:T(8,128)(2,1)S(1)} %collective-permute-done.38.refs_1_, ...), custom_call_target="tpu_custom_call" | custom-call | flops 1048576 | bytes 65536 | tf_op jit(solution)/shard_map/place/pallas_call | solution.py:972
  (106 shorter events, 42.4 us)
Async XLA Ops:
  3.8 20.8 %collective-permute-start = (bf16[2,64,1024]{2,1,0:T(8,128)(2,1)}, bf16[2,64,1024]{2,1,0:T(8,128)(2,1)}, u32[]{:S(2)}, u32[]{:S(2)}) collective-permute-start(bf16[2,64,1024]{2,1,0:T(8,128)(2,1)} %quarter.1), channel_id=1, source_target_pairs={{0,6},{1,7},{2,0},{3,1},{4,2},{5,3},{6,4},{7,5},{8,14},{9,15},{10,... | collective-permute-start | bytes 786440 | tf_op jit(solution)/shard_map/ppermute | solution.py:1013
  3.9 25.0 %collective-permute-start.3 = (bf16[2,64,1024]{2,1,0:T(8,128)(2,1)}, bf16[2,64,1024]{2,1,0:T(8,128)(2,1)S(1)}, u32[]{:S(2)}, u32[]{:S(2)}) collective-permute-start(bf16[2,64,1024]{2,1,0:T(8,128)(2,1)} %quarter.1), channel_id=1, source_target_pairs={{0,4},{1,5},{2,6},{3,7},{4,0},{5,1},{6,2},{7,3},{8,12},{9,13},{10,... | collective-permute-start | bytes 786440 | tf_op jit(solution)/shard_map/ppermute | solution.py:1013
  6.9 22.5 %collective-permute-start.4 = (bf16[2,64,1024]{2,1,0:T(8,128)(2,1)}, bf16[2,64,1024]{2,1,0:T(8,128)(2,1)}, u32[]{:S(2)}, u32[]{:S(2)}) collective-permute-start(bf16[2,64,1024]{2,1,0:T(8,128)(2,1)} %quarter.1), channel_id=1, source_target_pairs={{0,2},{1,3},{2,4},{3,5},{4,6},{5,7},{6,0},{7,1},{8,10},{9,11},{10,... | collective-permute-start | bytes 786440 | tf_op jit(solution)/shard_map/ppermute | solution.py:1013
  25.6 6.4 %collective-permute-start.2 = (bf16[1,2,64,1024]{3,2,1,0:T(8,128)(2,1)S(1)}, bf16[1,2,64,1024]{3,2,1,0:T(8,128)(2,1)S(1)}, u32[]{:S(2)}, u32[]{:S(2)}) collective-permute-start(bf16[1,2,64,1024]{3,2,1,0:T(8,128)(2,1)S(1)} %pack.5.refs_2_.refs_1_), channel_id=1, source_target_pairs={{0,16},{8,24},{16,0},{24,8},{1,17},{9,25},{17,1},{25,9},{2,18},{10... | collective-permute-start | bytes 786440 | tf_op jit(solution)/shard_map/ppermute | solution.py:1006
  27.2 6.4 %collective-permute-start.1 = (bf16[1,2,64,1024]{3,2,1,0:T(8,128)(2,1)S(1)}, bf16[1,2,64,1024]{3,2,1,0:T(8,128)(2,1)S(1)}, u32[]{:S(2)}, u32[]{:S(2)}) collective-permute-start(bf16[1,2,64,1024]{3,2,1,0:T(8,128)(2,1)S(1)} %pack.5.refs_2_.refs_1_), channel_id=1, source_target_pairs={{0,8},{8,0},{16,24},{24,16},{1,9},{9,1},{17,25},{25,17},{2,10},{10... | collective-permute-start | bytes 786440 | tf_op jit(solution)/shard_map/ppermute | solution.py:1006
  33.8 20.0 %collective-permute-start.6 = (bf16[2,2,64,1024]{3,2,1,0:T(8,128)(2,1)S(1)}, bf16[2,2,64,1024]{3,2,1,0:T(8,128)(2,1)S(1)}, u32[]{:S(2)}, u32[]{:S(2)}) collective-permute-start(bf16[2,2,64,1024]{3,2,1,0:T(8,128)(2,1)S(1)} %pack.6.refs_1_.refs_4_), channel_id=1, source_target_pairs={{0,8},{8,0},{16,24},{24,16},{1,9},{9,1},{17,25},{25,17},{2,10},{10... | collective-permute-start | bytes 1572872 | tf_op jit(solution)/shard_map/ppermute | solution.py:1006
  35.3 18.4 %collective-permute-start.7 = (bf16[2,2,64,1024]{3,2,1,0:T(8,128)(2,1)S(1)}, bf16[2,2,64,1024]{3,2,1,0:T(8,128)(2,1)S(1)}, u32[]{:S(2)}, u32[]{:S(2)}) collective-permute-start(bf16[2,2,64,1024]{3,2,1,0:T(8,128)(2,1)S(1)} %pack.6.refs_1_.refs_4_), channel_id=1, source_target_pairs={{0,16},{8,24},{16,0},{24,8},{1,17},{9,25},{17,1},{25,9},{2,18},{10... | collective-permute-start | bytes 1572872 | tf_op jit(solution)/shard_map/ppermute | solution.py:1006
  35.8 11.5 %collective-permute-start.9 = (bf16[2,64,1024]{2,1,0:T(8,128)(2,1)S(1)}, bf16[2,64,1024]{2,1,0:T(8,128)(2,1)S(1)}, u32[]{:S(2)}, u32[]{:S(2)}) collective-permute-start(bf16[2,64,1024]{2,1,0:T(8,128)(2,1)S(1)} %get-tuple-element.60), channel_id=1, source_target_pairs={{0,4},{1,5},{2,6},{3,7},{4,0},{5,1},{6,2},{7,3},{8,12},{9,13},{10,... | collective-permute-start | bytes 786440 | tf_op jit(solution)/shard_map/ppermute | solution.py:1013
  35.8 17.9 %collective-permute-start.5 = (bf16[1,2,64,1024]{3,2,1,0:T(8,128)(2,1)S(1)}, bf16[1,2,64,1024]{3,2,1,0:T(8,128)(2,1)S(1)}, u32[]{:S(2)}, u32[]{:S(2)}) collective-permute-start(bf16[1,2,64,1024]{3,2,1,0:T(8,128)(2,1)S(1)} %tie.1.refs_3_), channel_id=1, source_target_pairs={{0,8},{8,0},{16,24},{24,16},{1,9},{9,1},{17,25},{25,17},{2,10},{10... | collective-permute-start | bytes 786440 | tf_op jit(solution)/shard_map/ppermute | solution.py:1006
  53.9 12.8 %collective-permute-start.12 = (bf16[7,2,64,1024]{3,2,1,0:T(8,128)(2,1)S(1)}, bf16[7,2,64,1024]{3,2,1,0:T(8,128)(2,1)S(1)}, u32[]{:S(2)}, u32[]{:S(2)}) collective-permute-start(bf16[7,2,64,1024]{3,2,1,0:T(8,128)(2,1)S(1)} %pack.8.refs_1_), channel_id=1, source_target_pairs={{0,1},{1,0},{2,3},{3,2},{4,5},{5,4},{6,7},{7,6},{8,9},{9,8},{10,11... | collective-permute-start | bytes 5505032 | tf_op jit(solution)/shard_map/ppermute | solution.py:1009
  53.9 9.2 %collective-permute-start.13 = (bf16[2,64,1024]{2,1,0:T(8,128)(2,1)S(1)}, bf16[2,64,1024]{2,1,0:T(8,128)(2,1)S(1)}, u32[]{:S(2)}, u32[]{:S(2)}) collective-permute-start(bf16[2,64,1024]{2,1,0:T(8,128)(2,1)S(1)} %get-tuple-element.64), channel_id=1, source_target_pairs={{0,2},{1,3},{2,4},{3,5},{4,6},{5,7},{6,0},{7,1},{8,10},{9,11},{10,... | collective-permute-start | bytes 786440 | tf_op jit(solution)/shard_map/ppermute | solution.py:1013
  54.0 12.5 %collective-permute-start.14 = (bf16[2,64,1024]{2,1,0:T(8,128)(2,1)S(1)}, bf16[2,64,1024]{2,1,0:T(8,128)(2,1)S(1)}, u32[]{:S(2)}, u32[]{:S(2)}) collective-permute-start(bf16[2,64,1024]{2,1,0:T(8,128)(2,1)S(1)} %get-tuple-element.65), channel_id=1, source_target_pairs={{0,6},{1,7},{2,0},{3,1},{4,2},{5,3},{6,4},{7,5},{8,14},{9,15},{10,... | collective-permute-start | bytes 786440 | tf_op jit(solution)/shard_map/ppermute | solution.py:1013
  56.1 13.6 %collective-permute-start.10 = (bf16[1,2,64,1024]{3,2,1,0:T(8,128)(2,1)S(1)}, bf16[1,2,64,1024]{3,2,1,0:T(8,128)(2,1)S(1)}, u32[]{:S(2)}, u32[]{:S(2)}) collective-permute-start(bf16[1,2,64,1024]{3,2,1,0:T(8,128)(2,1)S(1)} %get-tuple-element.61), channel_id=1, source_target_pairs={{0,8},{8,0},{16,24},{24,16},{1,9},{9,1},{17,25},{25,17},{2,10},{10... | collective-permute-start | bytes 786440 | tf_op jit(solution)/shard_map/ppermute | solution.py:1006
  57.6 12.0 %collective-permute-start.11 = (bf16[1,2,64,1024]{3,2,1,0:T(8,128)(2,1)S(1)}, bf16[1,2,64,1024]{3,2,1,0:T(8,128)(2,1)S(1)}, u32[]{:S(2)}, u32[]{:S(2)}) collective-permute-start(bf16[1,2,64,1024]{3,2,1,0:T(8,128)(2,1)S(1)} %get-tuple-element.62), channel_id=1, source_target_pairs={{0,16},{8,24},{16,0},{24,8},{1,17},{9,25},{17,1},{25,9},{2,18},{10... | collective-permute-start | bytes 786440 | tf_op jit(solution)/shard_map/ppermute | solution.py:1006
  81.0 14.8 %collective-permute-start.29 = (bf16[4,64,1024]{2,1,0:T(8,128)(2,1)S(1)}, bf16[4,64,1024]{2,1,0:T(8,128)(2,1)S(1)}, u32[]{:S(2)}, u32[]{:S(2)}) collective-permute-start(bf16[4,64,1024]{2,1,0:T(8,128)(2,1)S(1)} %get-tuple-element.92), channel_id=1, source_target_pairs={{0,8},{8,0},{16,24},{24,16},{1,9},{9,1},{17,25},{25,17},{2,10},{10... | collective-permute-start | bytes 1572872 | tf_op jit(solution)/shard_map/ppermute | solution.py:1006
  82.6 14.8 %collective-permute-start.30 = (bf16[4,64,1024]{2,1,0:T(8,128)(2,1)S(1)}, bf16[4,64,1024]{2,1,0:T(8,128)(2,1)S(1)}, u32[]{:S(2)}, u32[]{:S(2)}) collective-permute-start(bf16[4,64,1024]{2,1,0:T(8,128)(2,1)S(1)} %get-tuple-element.93), channel_id=1, source_target_pairs={{0,16},{8,24},{16,0},{24,8},{1,17},{9,25},{17,1},{25,9},{2,18},{10... | collective-permute-start | bytes 1572872 | tf_op jit(solution)/shard_map/ppermute | solution.py:1006
  87.2 19.9 %collective-permute-start.18 = (bf16[4,64,1024]{2,1,0:T(8,128)(2,1)S(1)}, bf16[4,64,1024]{2,1,0:T(8,128)(2,1)S(1)}, u32[]{:S(2)}, u32[]{:S(2)}) collective-permute-start(bf16[4,64,1024]{2,1,0:T(8,128)(2,1)S(1)} %get-tuple-element.76), channel_id=1, source_target_pairs={{0,8},{8,0},{16,24},{24,16},{1,9},{9,1},{17,25},{25,17},{2,10},{10... | collective-permute-start | bytes 1572872 | tf_op jit(solution)/shard_map/ppermute | solution.py:1006
  87.8 20.8 %collective-permute-start.19 = (bf16[4,64,1024]{2,1,0:T(8,128)(2,1)S(1)}, bf16[4,64,1024]{2,1,0:T(8,128)(2,1)S(1)}, u32[]{:S(2)}, u32[]{:S(2)}) collective-permute-start(bf16[4,64,1024]{2,1,0:T(8,128)(2,1)S(1)} %get-tuple-element.77), channel_id=1, source_target_pairs={{0,16},{8,24},{16,0},{24,8},{1,17},{9,25},{17,1},{25,9},{2,18},{10... | collective-permute-start | bytes 1572872 | tf_op jit(solution)/shard_map/ppermute | solution.py:1006
  97.5 16.4 %collective-permute-start.31 = (bf16[2,64,1024]{2,1,0:T(8,128)(2,1)S(1)}, bf16[2,64,1024]{2,1,0:T(8,128)(2,1)S(1)}, u32[]{:S(2)}, u32[]{:S(2)}) collective-permute-start(bf16[2,64,1024]{2,1,0:T(8,128)(2,1)S(1)} %get-tuple-element.96), channel_id=1, source_target_pairs={{0,8},{8,0},{16,24},{24,16},{1,9},{9,1},{17,25},{25,17},{2,10},{10... | collective-permute-start | bytes 786440 | tf_op jit(solution)/shard_map/ppermute | solution.py:1006
  98.1 16.1 %collective-permute-start.32 = (bf16[2,64,1024]{2,1,0:T(8,128)(2,1)S(1)}, bf16[2,64,1024]{2,1,0:T(8,128)(2,1)S(1)}, u32[]{:S(2)}, u32[]{:S(2)}) collective-permute-start(bf16[2,64,1024]{2,1,0:T(8,128)(2,1)S(1)} %get-tuple-element.97), channel_id=1, source_target_pairs={{0,16},{8,24},{16,0},{24,8},{1,17},{9,25},{17,1},{25,9},{2,18},{10... | collective-permute-start | bytes 786440 | tf_op jit(solution)/shard_map/ppermute | solution.py:1006
  108.8 11.9 %collective-permute-start.20 = (bf16[2,64,1024]{2,1,0:T(8,128)(2,1)S(1)}, bf16[2,64,1024]{2,1,0:T(8,128)(2,1)S(1)}, u32[]{:S(2)}, u32[]{:S(2)}) collective-permute-start(bf16[2,64,1024]{2,1,0:T(8,128)(2,1)S(1)} %get-tuple-element.80), channel_id=1, source_target_pairs={{0,8},{8,0},{16,24},{24,16},{1,9},{9,1},{17,25},{25,17},{2,10},{10... | collective-permute-start | bytes 786440 | tf_op jit(solution)/shard_map/ppermute | solution.py:1006
  109.4 11.3 %collective-permute-start.21 = (bf16[2,64,1024]{2,1,0:T(8,128)(2,1)S(1)}, bf16[2,64,1024]{2,1,0:T(8,128)(2,1)S(1)}, u32[]{:S(2)}, u32[]{:S(2)}) collective-permute-start(bf16[2,64,1024]{2,1,0:T(8,128)(2,1)S(1)} %get-tuple-element.81), channel_id=1, source_target_pairs={{0,16},{8,24},{16,0},{24,8},{1,17},{9,25},{17,1},{25,9},{2,18},{10... | collective-permute-start | bytes 786440 | tf_op jit(solution)/shard_map/ppermute | solution.py:1006
  110.9 7.8 %collective-permute-start.24 = (f32[8,1024]{1,0:T(8,128)S(1)}, f32[8,1024]{1,0:T(8,128)S(1)}, u32[]{:S(2)}, u32[]{:S(2)}) collective-permute-start(f32[8,1024]{1,0:T(8,128)S(1)} %add.10.refs_0_), channel_id=1, source_target_pairs={{0,4},{1,5},{2,6},{3,7},{4,0},{5,1},{6,2},{7,3},{8,12},{9,13},{10,... | collective-permute-start | bytes 98312 | tf_op jit(solution)/shard_map/ppermute | solution.py:1009
  114.4 8.9 %collective-permute-start.33 = (bf16[64,1024]{1,0:T(8,128)(2,1)S(1)}, bf16[64,1024]{1,0:T(8,128)(2,1)S(1)}, u32[]{:S(2)}, u32[]{:S(2)}) collective-permute-start(bf16[64,1024]{1,0:T(8,128)(2,1)S(1)} %get-tuple-element.99), channel_id=1, source_target_pairs={{0,2},{1,3},{2,4},{3,5},{4,6},{5,7},{6,0},{7,1},{8,10},{9,11},{10,... | collective-permute-start | bytes 393224 | tf_op jit(solution)/shard_map/ppermute | solution.py:1013
  115.1 14.3 %collective-permute-start.34 = (bf16[64,1024]{1,0:T(8,128)(2,1)S(1)}, bf16[64,1024]{1,0:T(8,128)(2,1)S(1)}, u32[]{:S(2)}, u32[]{:S(2)}) collective-permute-start(bf16[64,1024]{1,0:T(8,128)(2,1)S(1)} %get-tuple-element.100), channel_id=1, source_target_pairs={{0,4},{1,5},{2,6},{3,7},{4,0},{5,1},{6,2},{7,3},{8,12},{9,13},{10,... | collective-permute-start | bytes 393224 | tf_op jit(solution)/shard_map/ppermute | solution.py:1013
  118.7 16.1 %collective-permute-start.35 = (bf16[64,1024]{1,0:T(8,128)(2,1)S(1)}, bf16[64,1024]{1,0:T(8,128)(2,1)S(1)}, u32[]{:S(2)}, u32[]{:S(2)}) collective-permute-start(bf16[64,1024]{1,0:T(8,128)(2,1)S(1)} %get-tuple-element.101), channel_id=1, source_target_pairs={{0,6},{1,7},{2,0},{3,1},{4,2},{5,3},{6,4},{7,5},{8,14},{9,15},{10,... | collective-permute-start | bytes 393224 | tf_op jit(solution)/shard_map/ppermute | solution.py:1013
  120.8 15.7 %collective-permute-start.25 = (bf16[64,1024]{1,0:T(8,128)(2,1)S(1)}, bf16[64,1024]{1,0:T(8,128)(2,1)S(1)}, u32[]{:S(2)}, u32[]{:S(2)}) collective-permute-start(bf16[64,1024]{1,0:T(8,128)(2,1)S(1)} %get-tuple-element.84), channel_id=1, source_target_pairs={{0,2},{1,3},{2,4},{3,5},{4,6},{5,7},{6,0},{7,1},{8,10},{9,11},{10,... | collective-permute-start | bytes 393224 | tf_op jit(solution)/shard_map/ppermute | solution.py:1013
  121.0 16.3 %collective-permute-start.26 = (bf16[64,1024]{1,0:T(8,128)(2,1)S(1)}, bf16[64,1024]{1,0:T(8,128)(2,1)S(1)}, u32[]{:S(2)}, u32[]{:S(2)}) collective-permute-start(bf16[64,1024]{1,0:T(8,128)(2,1)S(1)} %get-tuple-element.85), channel_id=1, source_target_pairs={{0,4},{1,5},{2,6},{3,7},{4,0},{5,1},{6,2},{7,3},{8,12},{9,13},{10,... | collective-permute-start | bytes 393224 | tf_op jit(solution)/shard_map/ppermute | solution.py:1013
  123.4 16.9 %collective-permute-start.27 = (bf16[64,1024]{1,0:T(8,128)(2,1)S(1)}, bf16[64,1024]{1,0:T(8,128)(2,1)S(1)}, u32[]{:S(2)}, u32[]{:S(2)}) collective-permute-start(bf16[64,1024]{1,0:T(8,128)(2,1)S(1)} %get-tuple-element.86), channel_id=1, source_target_pairs={{0,6},{1,7},{2,0},{3,1},{4,2},{5,3},{6,4},{7,5},{8,14},{9,15},{10,... | collective-permute-start | bytes 393224 | tf_op jit(solution)/shard_map/ppermute | solution.py:1013
  140.7 13.2 %collective-permute-start.40 = (bf16[144,1024]{1,0:T(8,128)(2,1)S(1)}, bf16[144,1024]{1,0:T(8,128)(2,1)S(1)}, u32[]{:S(2)}, u32[]{:S(2)}) collective-permute-start(bf16[144,1024]{1,0:T(8,128)(2,1)S(1)} %get-tuple-element.103), channel_id=1, source_target_pairs={{0,24},{8,16},{16,8},{24,0},{1,25},{9,17},{17,9},{25,1},{2,26},{10... | collective-permute-start | bytes 884744 | tf_op jit(solution)/shard_map/ppermute | solution.py:1006
  142.5 10.5 %collective-permute-start.38 = (bf16[80,1024]{1,0:T(8,128)(2,1)S(1)}, bf16[80,1024]{1,0:T(8,128)(2,1)S(1)}, u32[]{:S(2)}, u32[]{:S(2)}) collective-permute-start(bf16[80,1024]{1,0:T(8,128)(2,1)S(1)} %get-tuple-element.102.refs_0_), channel_id=1, source_target_pairs={{0,8},{8,0},{16,24},{24,16},{1,9},{9,1},{17,25},{25,17},{2,10},{10... | collective-permute-start | bytes 491528 | tf_op jit(solution)/shard_map/ppermute | solution.py:1006
  143.1 10.7 %collective-permute-start.39 = (bf16[80,1024]{1,0:T(8,128)(2,1)S(1)}, bf16[80,1024]{1,0:T(8,128)(2,1)S(1)}, u32[]{:S(2)}, u32[]{:S(2)}) collective-permute-start(bf16[80,1024]{1,0:T(8,128)(2,1)S(1)} %get-tuple-element.102.refs_0_), channel_id=1, source_target_pairs={{0,16},{8,24},{16,0},{24,8},{1,17},{9,25},{17,1},{25,9},{2,18},{10... | collective-permute-start | bytes 491528 | tf_op jit(solution)/shard_map/ppermute | solution.py:1006
  (22 other events, 127.5 us)

commit v12 on v11

--- a/solution.py
+++ b/solution.py
@@ -771,23 +771,23 @@
 
 
 def down_grad_kernel(side, act_pieces, add, *refs):
-    acts, back_ref = refs[:3], refs[3]
-    arrived = refs[4] if add else None
-    outs = refs[5:] if add else refs[4:]
+    acts, back_ref = refs[:2], refs[2]
+    arrived = refs[3] if add else None
+    outs = refs[4:] if add else refs[3:]
     for quarter in (3, 1, 2, 0):
         act = joined(acts, act_pieces[quarter], lambda ref, a, n: ref[side, a:a + n])
         emit(quarter, dot_nn(act, back_ref[...]), arrived, outs)
 
 
 def up_grad_kernel(side, weight_pieces, act_pieces, add, *refs):
-    weights, slopes = refs[:3], refs[3:6]
-    back_t_ref, normed_ref, gain_in = refs[6:9]
+    weights, slopes = refs[:2], refs[2:4]
+    back_t_ref, normed_ref, gain_in = refs[4:7]
     if add:
-        arrived, scale_ref, small_ref = refs[9:12]
-        outs, vector_ref, gain_ref = refs[12:-2], refs[-2], refs[-1]
+        arrived, scale_ref, small_ref = refs[7:10]
+        outs, vector_ref, gain_ref = refs[10:-2], refs[-2], refs[-1]
     else:
         arrived = None
-        outs, gain_ref = refs[9:-1], refs[-1]
+        outs, gain_ref = refs[7:-1], refs[-1]
     gain_ref[...] = gain_in[...]
     for quarter in (3, 1, 2, 0):
         pieces = weight_pieces[quarter]
@@ -1022,36 +1022,34 @@
     low = pack(arrivals[:half - 1], rendered[0])
     x_low, y_low = beside(low, 1), beside(low, 2)
     high = pack(arrivals[half - 1:], low)
+    high = tie(high, x_low, y_low)
     x_high, y_high = beside(high, 1), beside(high, 2)
-    y_low = tie(y_low, high)
-    d_low = beside(y_low, 1)
     targets = [rendered[0]] + [along(rendered[shift], shift) for shift in range(1, depth)]
-    early = pack([own_rows(group, up_weight, down_weight), low, x_low, y_low], high)
-    early_other = partner(early)
     tokens, normed, normed_t = prepare_tokens(
         ray_count, True, me, block_owner, ray_pixel, image_tokens,
         layer_norm_gain.reshape(1, width),
     )
-    act_early, slope_early, mixed = forward(normed_t, [early], [early_other])
-    late = pack([d_low, high, x_high, y_high], mixed, targets[half])
-    late_other = partner(late)
-    passed_x, passed_y = turn(y_high, x_high)
-    d_high = [beside(passed_x, 1), beside(passed_y, 2)]
-    act_late, slope_late, mixed = forward(normed_t, [late], [late_other], mixed)
-    rest = [target for shift, target in enumerate(targets) if shift not in (0, half)]
-    last = pack(d_high, mixed, *rest)
+    most = pack(
+        [own_rows(group, up_weight, down_weight), low, x_low, y_low, high, x_high, y_high],
+        targets[half],
+    )
+    most_other = partner(most)
+    d_low, d_high = beside(y_low, 1), beside(x_high, 2)
+    act_most, slope_most, mixed = forward(normed_t, [most], [most_other])
+    late = [target for shift, target in enumerate(targets) if shift not in (0, half)]
+    last = pack([d_low, d_high], mixed, *late)
     last_other = partner(last)
     act_last, slope_last, back, back_t, small = forward(
         normed_t, [last], [last_other], mixed,
         (tokens, layer_scale.reshape(1, width), *targets, partner(seconds(targets))),
     )
-    acts, slopes = (act_early, act_late, act_last), (slope_early, slope_late, slope_last)
-    weights = ((early, late, last), (early_other, late_other, last_other))
-    count = half - 1
-    rest = depth - half
+    acts, slopes = (act_most, act_last), (slope_most, slope_last)
+    weights = ((most, last), (most_other, last_other))
+    count, rest = half - 1, depth - half
+    start = 4 + 3 * count
     pieces = tuple(
-        ((0, q, 1), (0, 4 + q * count, count), (1, count + q * rest, rest)) for q in range(3)
-    ) + (((0, 3, 1), (1, 0, count), (2, 0, rest)),)
+        ((0, q, 1), (0, 4 + q * count, count), (0, start + q * rest, rest)) for q in range(3)
+    ) + (((0, 3, 1), (1, 0, depth - 1)),)
     gain = jnp.zeros((1, width), F32)
     (down_other,) = down_gradient(1, pieces, depth, acts, back)
     down_arrived = partner(down_other)
@@ -1065,7 +1063,6 @@
         (up_arrived, layer_norm_gain.reshape(1, width), small),
     )
     vector = vector + partner(vector)
-    vector = vector + partner(vector, 2)
 
     def first_step(to_x, to_y, x_later, y_later, *after):
         from_x, from_y = beside(to_x, 1), beside(to_y, 2)
@@ -1084,11 +1081,13 @@
     shares = totals(own, from_x, from_y, *late)
     (down_total,) = collect(arrive_along(shares))
     down_x, down_y = beside(down_total, 1), beside(down_total, 2)
+    vector = vector + partner(vector, 2)
+    to_x, to_y = tie(to_x, *later), tie(to_y, *later)
+    from_x, from_y, later = first_step(to_x, to_y, *rest_up, vector)
     flip = 4
     while flip < ray_count:
         vector = vector + partner(vector, flip)
         flip *= 2
-    from_x, from_y, later = first_step(to_x, to_y, *rest_up)
     shares = totals(own_up, from_x, from_y, *second_step(later), vector)
     short, long = collect(arrive_along(shares), vector, down_total, (down_x, down_y))
     up_x, up_y, both = beside(short, 1), beside(short, 2), beside(long, 3)

time: 156 us -> 147 us (0.942)
  starting transfers between devices: 46.4 us -> 40.5 us
  Pallas kernels: 34.3 us -> 31.8 us
    ppermute x9 -> x8, starting transfers between devices: 5.96 us -> 3 us  [partner(): return lax.ppermute(array, 'ray', [(r, r ^ flip) for r in range(ray_count)])]
    ppermute x9 -> x8, waiting for transfers between devices: 5.99 us -> 8.27 us  [partner(): return lax.ppermute(array, 'ray', [(r, r ^ flip) for r in range(ray_count)])]
    pallas_call x5 -> x4, Pallas kernels: 2.23 us -> 0.33 us  [pack(): pl.pallas_call(functools.partial(pack_kernel, counts), out_shape=jax.Shap...]
    ppermute x20 -> x19, starting transfers between devices: 22.1 us -> 20.3 us  [beside(): lax.ppermute(array, 'grp', [(g, g ^ flip) for g in range(group_count)])]
    ppermute x20 -> x19, waiting for transfers between devices: 31.9 us -> 30.1 us  [beside(): lax.ppermute(array, 'grp', [(g, g ^ flip) for g in range(group_count)])]
    pallas_call x3 -> x2, Pallas kernels: 8.2 us -> 7.92 us  [forward(): pl.pallas_call(functools.partial(forward_kernel, first, blocks, len(own),...]
  transfers between devices with their start and end apart: 41 -> 39, of which waited for: 24 -> 27; matrix products, arithmetic and copies ran while one was open for 0% -> 0% of each run, Pallas kernels for 18% -> 17%
where the time goes in v12:
time: 147 us
  waiting for transfers between devices  71.8 us (49%)
  starting transfers between devices  40.5 us (28%)
  Pallas kernels  31.8 us (22%)
  local copies, waits for them, and re-layouts  2.13 us (1%)
    ppermute x12, waiting for transfers between devices, along(): return lax.ppermute(array, 'ray', pairs)  33.4 us
    ppermute x19, waiting for transfers between devices, beside(): lax.ppermute(array, 'grp', [(g, g ^ flip) for g in range(group_count)])  30.1 us
    ppermute x19, starting transfers between devices, beside(): lax.ppermute(array, 'grp', [(g, g ^ flip) for g in range(group_count)])  20.3 us
    ppermute x12, starting transfers between devices, along(): return lax.ppermute(array, 'ray', pairs)  17.3 us
    pallas_call x1, Pallas kernels, render(): pl.pallas_call(functools.partial(render_kernel, ray_count, relative), out...  8.41 us
    ppermute x8, waiting for transfers between devices, partner(): return lax.ppermute(array, 'ray', [(r, r ^ flip) for r in range(ray_count)])  8.27 us
    pallas_call x2, Pallas kernels, forward(): pl.pallas_call(functools.partial(forward_kernel, first, blocks, len(own),...  7.92 us
    pallas_call x2, Pallas kernels, up_gradient(): pl.pallas_call(functools.partial(up_grad_kernel, side, weight_pieces, act...  6.05 us
  transfers between devices with their start and end apart: 39, of which 27 were waited for; matrix products, arithmetic and copies ran while one was open for 0% of the time, Pallas kernels for 17%

profile of v12, /device:TPU:8, one launch (start us, length us, event | category | flops | bytes accessed | tf_op | source)
XLA Modules:
  0.0 147.2 jit_solution(6261636706454566118)
XLA Ops:
  3.2 3.0 %collective-permute-start.3 = (bf16[2,64,1024]{2,1,0:T(8,128)(2,1)S(1)}, bf16[2,64,1024]{2,1,0:T(8,128)(2,1)S(1)}, u32[]{:S(2)}, u32[]{:S(2)}) collective-permute-start(bf16[2,64,1024]{2,1,0:T(8,128)(2,1)S(1)} %quarter.1), channel_id=1, source_target_pairs={{0,4},{1,5},{2,6},{3,7},{4,0},{5,1},{6,2},{7,3},{8,12},{9,13},{10,... | collective-permute-start | bytes 786440 | tf_op jit(solution)/shard_map/ppermute | solution.py:1013
  6.2 2.5 %collective-permute-start.4 = (bf16[2,64,1024]{2,1,0:T(8,128)(2,1)S(1)}, bf16[2,64,1024]{2,1,0:T(8,128)(2,1)S(1)}, u32[]{:S(2)}, u32[]{:S(2)}) collective-permute-start(bf16[2,64,1024]{2,1,0:T(8,128)(2,1)S(1)} %quarter.1), channel_id=1, source_target_pairs={{0,2},{1,3},{2,4},{3,5},{4,6},{5,7},{6,0},{7,1},{8,10},{9,11},{10,... | collective-permute-start | bytes 786440 | tf_op jit(solution)/shard_map/ppermute | solution.py:1013
  8.7 8.4 %render.1 = (bf16[2,64,1024]{2,1,0:T(8,128)(2,1)S(1)}, bf16[2,64,1024]{2,1,0:T(8,128)(2,1)S(1)}, bf16[2,64,1024]{2,1,0:T(8,128)(2,1)S(1)}, bf16[2,64,1024]{2,1,0:T(8,128)(2,1)S(1)}) custom-call(s32[1]{0:T(128)} %bitcast.1.me_ref, s32[1,8]{1,0:T(1,128)S(1)} %copy-done.11, s32[32,512]{1,0:T(8,128)S(1)} %copy-done.7, f32[32,512]{1,0:T(8,128)S(1)} %copy-done.8, ...), custom_call_target="tpu_custom_call" | custom-call | flops 1048576 | bytes 65536 | tf_op jit(solution)/shard_map/render/pallas_call | solution.py:152
  17.2 6.4 %collective-permute-done.refs_0_ = bf16[2,64,1024]{2,1,0:T(8,128)(2,1)S(1)} collective-permute-done((bf16[2,64,1024]{2,1,0:T(8,128)(2,1)S(1)}, bf16[2,64,1024]{2,1,0:T(8,128)(2,1)S(1)}, u32[]{:S(2)}, u32[]{:S(2)}) %collective-permute-start) | collective-permute-done | bytes 262176 | tf_op jit(solution)/shard_map/ppermute | solution.py:1013
  23.6 1.6 %collective-permute-start.2 = (bf16[1,2,64,1024]{3,2,1,0:T(8,128)(2,1)S(1)}, bf16[1,2,64,1024]{3,2,1,0:T(8,128)(2,1)S(1)}, u32[]{:S(2)}, u32[]{:S(2)}) collective-permute-start(bf16[1,2,64,1024]{3,2,1,0:T(8,128)(2,1)S(1)} %pack.4.refs_2_.refs_1_), channel_id=1, source_target_pairs={{0,16},{8,24},{16,0},{24,8},{1,17},{9,25},{17,1},{25,9},{2,18},{10... | collective-permute-start | bytes 786440 | tf_op jit(solution)/shard_map/ppermute | solution.py:1006
  26.7 1.7 %collective-permute-done.4.refs_1_ = bf16[2,64,1024]{2,1,0:T(8,128)(2,1)S(1)} collective-permute-done((bf16[2,64,1024]{2,1,0:T(8,128)(2,1)S(1)}, bf16[2,64,1024]{2,1,0:T(8,128)(2,1)S(1)}, u32[]{:S(2)}, u32[]{:S(2)}) %collective-permute-start.4) | collective-permute-done | bytes 262176 | tf_op jit(solution)/shard_map/ppermute | solution.py:1013
  28.5 1.6 %collective-permute-done.2.refs_2_.refs_3_ = bf16[1,2,64,1024]{3,2,1,0:T(8,128)(2,1)S(1)} collective-permute-done((bf16[1,2,64,1024]{3,2,1,0:T(8,128)(2,1)S(1)}, bf16[1,2,64,1024]{3,2,1,0:T(8,128)(2,1)S(1)}, u32[]{:S(2)}, u32[]{:S(2)}) %collective-permute-start.2) | collective-permute-done | bytes 262176 | tf_op jit(solution)/shard_map/ppermute | solution.py:1006
  30.1 2.7 %collective-permute-done.1.refs_1_.refs_2_ = bf16[1,2,64,1024]{3,2,1,0:T(8,128)(2,1)S(1)} collective-permute-done((bf16[1,2,64,1024]{3,2,1,0:T(8,128)(2,1)S(1)}, bf16[1,2,64,1024]{3,2,1,0:T(8,128)(2,1)S(1)}, u32[]{:S(2)}, u32[]{:S(2)}) %collective-permute-start.1) | collective-permute-done | bytes 262176 | tf_op jit(solution)/shard_map/ppermute | solution.py:1006
  34.5 7.6 %collective-permute-done.7.refs_7_.refs_2_.refs_8_ = bf16[2,64,1024]{2,1,0:T(8,128)(2,1)S(1)} collective-permute-done((bf16[2,64,1024]{2,1,0:T(8,128)(2,1)S(1)}, bf16[2,64,1024]{2,1,0:T(8,128)(2,1)S(1)}, u32[]{:S(2)}, u32[]{:S(2)}) %collective-permute-start.7) | collective-permute-done | bytes 262176 | tf_op jit(solution)/shard_map/ppermute | solution.py:1013
  44.7 2.5 %collective-permute-start.11 = (bf16[2,64,1024]{2,1,0:T(8,128)(2,1)S(1)}, bf16[2,64,1024]{2,1,0:T(8,128)(2,1)S(1)}, u32[]{:S(2)}, u32[]{:S(2)}) collective-permute-start(bf16[2,64,1024]{2,1,0:T(8,128)(2,1)S(1)} %get-tuple-element.56), channel_id=1, source_target_pairs={{0,2},{1,3},{2,4},{3,5},{4,6},{5,7},{6,0},{7,1},{8,10},{9,11},{10,... | collective-permute-start | bytes 786440 | tf_op jit(solution)/shard_map/ppermute | solution.py:1013
  47.7 3.2 %tokens.1 = (bf16[512,1024]{1,0:T(8,128)(2,1)S(1)}, bf16[512,1024]{1,0:T(8,128)(2,1)S(1)}, bf16[1024,512]{1,0:T(8,128)(2,1)S(1)}) custom-call(s32[1]{0:T(128)} %bitcast.1.me_ref, s32[1,8]{1,0:T(1,128)S(1)} %copy-done.11, s32[1,4096]{1,0:T(1,128)S(1)} %copy-done.6, bf16[512,1024]{1,0:T(8,128)(2,1)S(1)} %copy-done.1, f32[1,1024]{1,0:T(1,128)S(1)} %bitcast.8), custom_call_target="tpu_custom_call" | custom-call | flops 1048576 | bytes 65536 | tf_op jit(solution)/shard_map/tokens/pallas_call | solution.py:238
  51.0 5.0 %forward.2 = (bf16[2,13,64,512]{3,2,1,0:T(8,128)(2,1)S(1)}, f32[2,13,64,512]{3,2,1,0:T(8,128)S(1)}, f32[512,1024]{1,0:T(8,128)S(1)}) custom-call(bf16[1024,512]{1,0:T(8,128)(2,1)S(1)} %get-tuple-element.54.refs_0_, bf16[13,2,64,1024]{3,2,1,0:T(8,128)(2,1)S(1)} %pack.6.refs_1_.refs_0_, bf16[13,2,64,1024]{3,2,1,0:T(8,128)(2,1)S(1)} %collective-permute-done.10.refs_2_.refs_0_), custom_call_target="tpu_custom_call" | custom-call | flops 1048576 | bytes 65536 | tf_op jit(solution)/shard_map/forward/pallas_call | solution.py:652
  56.0 2.7 %collective-permute-done.11.refs_3_.refs_1_.refs_7_ = bf16[2,64,1024]{2,1,0:T(8,128)(2,1)S(1)} collective-permute-done((bf16[2,64,1024]{2,1,0:T(8,128)(2,1)S(1)}, bf16[2,64,1024]{2,1,0:T(8,128)(2,1)S(1)}, u32[]{:S(2)}, u32[]{:S(2)}) %collective-permute-start.11) | collective-permute-done | bytes 262176 | tf_op jit(solution)/shard_map/ppermute | solution.py:1013
  58.7 2.2 %collective-permute-done.12.refs_4_.refs_3_.refs_9_ = bf16[2,64,1024]{2,1,0:T(8,128)(2,1)S(1)} collective-permute-done((bf16[2,64,1024]{2,1,0:T(8,128)(2,1)S(1)}, bf16[2,64,1024]{2,1,0:T(8,128)(2,1)S(1)}, u32[]{:S(2)}, u32[]{:S(2)}) %collective-permute-start.12) | collective-permute-done | bytes 262176 | tf_op jit(solution)/shard_map/ppermute | solution.py:1013
  61.7 2.4 %collective-permute-done.14.refs_10_ = bf16[4,64,1024]{2,1,0:T(8,128)(2,1)S(1)} collective-permute-done((bf16[4,64,1024]{2,1,0:T(8,128)(2,1)S(1)}, bf16[4,64,1024]{2,1,0:T(8,128)(2,1)S(1)}, u32[]{:S(2)}, u32[]{:S(2)}) %collective-permute-start.14) | collective-permute-done | bytes 524320 | tf_op jit(solution)/shard_map/ppermute | solution.py:1009
  64.1 2.9 %forward.3 = (bf16[2,3,64,512]{3,2,1,0:T(8,128)(2,1)S(1)}, f32[2,3,64,512]{3,2,1,0:T(8,128)S(1)}, bf16[512,1024]{1,0:T(8,128)(2,1)S(1)}, bf16[1024,512]{1,0:T(8,128)(2,1)S(1)}, f32[8,1024]{1,0:T(8,128)S(1)}) custom-call(bf16[1024,512]{1,0:T(8,128)(2,1)S(1)} %get-tuple-element.54.refs_0_, bf16[3,2,64,1024]{3,2,1,0:T(8,128)(2,1)S(1)} %pack.7.refs_1_, ...), custom_call_target="tpu_custom_call" | custom-call | flops 1048576 | bytes 65536 | tf_op jit(solution)/shard_map/forward/pallas_call | solution.py:652
  68.5 2.8 %up_gradient.2 = (bf16[4,4,64,1024]{3,2,1,0:T(8,128)(2,1)S(1)}, f32[1,1024]{1,0:T(1,128)S(1)}) custom-call(bf16[13,2,64,1024]{3,2,1,0:T(8,128)(2,1)S(1)} %collective-permute-done.10.refs_2_.refs_0_, bf16[3,2,64,1024]{3,2,1,0:T(8,128)(2,1)S(1)} %collective-permute-done.13.refs_2_.refs_1_, f32[2,13,64,512]{3,2,1,0:T(8,128)S(1)} %get-tuple-element.58.refs_2_, ...), custom_call_target="tpu_custom_call" | custom-call | flops 1048576 | bytes 65536 | tf_op jit(solution)/shard_map/up_gradient/pallas_call | solution.py:844
  75.5 3.3 %up_gradient.3 = (bf16[4,64,1024]{2,1,0:T(8,128)(2,1)S(1)}, bf16[4,64,1024]{2,1,0:T(8,128)(2,1)S(1)}, bf16[4,64,1024]{2,1,0:T(8,128)(2,1)S(1)}, bf16[2,64,1024]{...) custom-call(bf16[13,2,64,1024]{3,2,1,0:T(8,128)(2,1)S(1)} %pack.6.refs_1_.refs_0_, ...), custom_call_target="tpu_custom_call" | custom-call | flops 1048576 | bytes 65536 | tf_op jit(solution)/shard_map/up_gradient/pallas_call | solution.py:844
  80.1 7.8 %collective-permute-done.17.x_ref = bf16[4,64,1024]{2,1,0:T(8,128)(2,1)S(1)} collective-permute-done((bf16[4,64,1024]{2,1,0:T(8,128)(2,1)S(1)}, bf16[4,64,1024]{2,1,0:T(8,128)(2,1)S(1)}, u32[]{:S(2)}, u32[]{:S(2)}) %collective-permute-start.17) | collective-permute-done | bytes 524320 | tf_op jit(solution)/shard_map/ppermute | solution.py:1006
  92.7 3.6 %collective-permute-done.22 = f32[8,1024]{1,0:T(8,128)S(1)} collective-permute-done((f32[8,1024]{1,0:T(8,128)S(1)}, f32[8,1024]{1,0:T(8,128)S(1)}, u32[]{:S(2)}, u32[]{:S(2)}) %collective-permute-start.22) | collective-permute-done | bytes 32800 | tf_op jit(solution)/shard_map/ppermute | solution.py:1009
  96.3 6.9 %collective-permute-done.21.y_ref = bf16[4,64,1024]{2,1,0:T(8,128)(2,1)S(1)} collective-permute-done((bf16[4,64,1024]{2,1,0:T(8,128)(2,1)S(1)}, bf16[4,64,1024]{2,1,0:T(8,128)(2,1)S(1)}, u32[]{:S(2)}, u32[]{:S(2)}) %collective-permute-start.21) | collective-permute-done | bytes 524320 | tf_op jit(solution)/shard_map/ppermute | solution.py:1006
  103.9 1.6 %collective-permute-start.23 = (bf16[2,64,1024]{2,1,0:T(8,128)(2,1)S(1)}, bf16[2,64,1024]{2,1,0:T(8,128)(2,1)S(1)}, u32[]{:S(2)}, u32[]{:S(2)}) collective-permute-start(bf16[2,64,1024]{2,1,0:T(8,128)(2,1)S(1)} %get-tuple-element.81), channel_id=1, source_target_pairs={{0,8},{8,0},{16,24},{24,16},{1,9},{9,1},{17,25},{25,17},{2,10},{10... | collective-permute-start | bytes 786440 | tf_op jit(solution)/shard_map/ppermute | solution.py:1006
  105.4 1.5 %collective-permute-start.24 = (bf16[2,64,1024]{2,1,0:T(8,128)(2,1)S(1)}, bf16[2,64,1024]{2,1,0:T(8,128)(2,1)S(1)}, u32[]{:S(2)}, u32[]{:S(2)}) collective-permute-start(bf16[2,64,1024]{2,1,0:T(8,128)(2,1)S(1)} %get-tuple-element.82), channel_id=1, source_target_pairs={{0,16},{8,24},{16,0},{24,8},{1,17},{9,25},{17,1},{25,9},{2,18},{10... | collective-permute-start | bytes 786440 | tf_op jit(solution)/shard_map/ppermute | solution.py:1006
  109.5 2.2 %collective-permute-start.31 = (bf16[64,1024]{1,0:T(8,128)(2,1)S(1)}, bf16[64,1024]{1,0:T(8,128)(2,1)S(1)}, u32[]{:S(2)}, u32[]{:S(2)}) collective-permute-start(bf16[64,1024]{1,0:T(8,128)(2,1)S(1)} %get-tuple-element.89), channel_id=1, source_target_pairs={{0,2},{1,3},{2,4},{3,5},{4,6},{5,7},{6,0},{7,1},{8,10},{9,11},{10,... | collective-permute-start | bytes 393224 | tf_op jit(solution)/shard_map/ppermute | solution.py:1013
  113.2 1.6 %collective-permute-start.33 = (bf16[64,1024]{1,0:T(8,128)(2,1)S(1)}, bf16[64,1024]{1,0:T(8,128)(2,1)S(1)}, u32[]{:S(2)}, u32[]{:S(2)}) collective-permute-start(bf16[64,1024]{1,0:T(8,128)(2,1)S(1)} %get-tuple-element.91), channel_id=1, source_target_pairs={{0,6},{1,7},{2,0},{3,1},{4,2},{5,3},{6,4},{7,5},{8,14},{9,15},{10,... | collective-permute-start | bytes 393224 | tf_op jit(solution)/shard_map/ppermute | solution.py:1013
  114.8 1.8 %collective-permute-done.31.refs_1_ = bf16[64,1024]{1,0:T(8,128)(2,1)S(1)} collective-permute-done((bf16[64,1024]{1,0:T(8,128)(2,1)S(1)}, bf16[64,1024]{1,0:T(8,128)(2,1)S(1)}, u32[]{:S(2)}, u32[]{:S(2)}) %collective-permute-start.31) | collective-permute-done | bytes 131104 | tf_op jit(solution)/shard_map/ppermute | solution.py:1013
  118.1 2.9 %collective-permute-done.33.refs_3_ = bf16[64,1024]{1,0:T(8,128)(2,1)S(1)} collective-permute-done((bf16[64,1024]{1,0:T(8,128)(2,1)S(1)}, bf16[64,1024]{1,0:T(8,128)(2,1)S(1)}, u32[]{:S(2)}, u32[]{:S(2)}) %collective-permute-start.33) | collective-permute-done | bytes 131104 | tf_op jit(solution)/shard_map/ppermute | solution.py:1013
  123.6 2.4 %collective-permute-start.27 = (bf16[64,1024]{1,0:T(8,128)(2,1)S(1)}, bf16[64,1024]{1,0:T(8,128)(2,1)S(1)}, u32[]{:S(2)}, u32[]{:S(2)}) collective-permute-start(bf16[64,1024]{1,0:T(8,128)(2,1)S(1)} %get-tuple-element.85), channel_id=1, source_target_pairs={{0,4},{1,5},{2,6},{3,7},{4,0},{5,1},{6,2},{7,3},{8,12},{9,13},{10,... | collective-permute-start | bytes 393224 | tf_op jit(solution)/shard_map/ppermute | solution.py:1013
  129.0 3.4 %collective-permute-done.27.refs_2_ = bf16[64,1024]{1,0:T(8,128)(2,1)S(1)} collective-permute-done((bf16[64,1024]{1,0:T(8,128)(2,1)S(1)}, bf16[64,1024]{1,0:T(8,128)(2,1)S(1)}, u32[]{:S(2)}, u32[]{:S(2)}) %collective-permute-start.27) | collective-permute-done | bytes 131104 | tf_op jit(solution)/shard_map/ppermute | solution.py:1013
  132.4 1.8 %collective-permute-done.28.refs_3_ = bf16[64,1024]{1,0:T(8,128)(2,1)S(1)} collective-permute-done((bf16[64,1024]{1,0:T(8,128)(2,1)S(1)}, bf16[64,1024]{1,0:T(8,128)(2,1)S(1)}, u32[]{:S(2)}, u32[]{:S(2)}) %collective-permute-start.28) | collective-permute-done | bytes 131104 | tf_op jit(solution)/shard_map/ppermute | solution.py:1013
  137.8 7.1 %collective-permute-done.36.refs_1_ = bf16[80,1024]{1,0:T(8,128)(2,1)S(1)} collective-permute-done((bf16[80,1024]{1,0:T(8,128)(2,1)S(1)}, bf16[80,1024]{1,0:T(8,128)(2,1)S(1)}, u32[]{:S(2)}, u32[]{:S(2)}) %collective-permute-start.36) | collective-permute-done | bytes 163872 | tf_op jit(solution)/shard_map/ppermute | solution.py:1006
  145.4 1.7 %place.1 = (f32[1024,256]{1,0:T(8,128)}, f32[256,1024]{1,0:T(8,128)}, f32[1,1024]{1,0:T(1,128)}, f32[1,1024]{1,0:T(1,128)}, f32[1,1]{1,0:T(1,128)}) custom-call(s32[1]{0:T(128)} %bitcast.group_ref, bf16[80,1024]{1,0:T(8,128)(2,1)S(1)} %get-tuple-element.92.refs_0_, bf16[80,1024]{1,0:T(8,128)(2,1)S(1)} %collective-permute-done.36.refs_1_, ...), custom_call_target="tpu_custom_call" | custom-call | flops 1048576 | bytes 65536 | tf_op jit(solution)/shard_map/place/pallas_call | solution.py:972
  (101 shorter events, 37.4 us)
Async XLA Ops:
  3.1 20.5 %collective-permute-start = (bf16[2,64,1024]{2,1,0:T(8,128)(2,1)S(1)}, bf16[2,64,1024]{2,1,0:T(8,128)(2,1)S(1)}, u32[]{:S(2)}, u32[]{:S(2)}) collective-permute-start(bf16[2,64,1024]{2,1,0:T(8,128)(2,1)S(1)} %quarter.1), channel_id=1, source_target_pairs={{0,6},{1,7},{2,0},{3,1},{4,2},{5,3},{6,4},{7,5},{8,14},{9,15},{10,... | collective-permute-start | bytes 786440 | tf_op jit(solution)/shard_map/ppermute | solution.py:1013
  3.2 23.5 %collective-permute-start.3 = (bf16[2,64,1024]{2,1,0:T(8,128)(2,1)S(1)}, bf16[2,64,1024]{2,1,0:T(8,128)(2,1)S(1)}, u32[]{:S(2)}, u32[]{:S(2)}) collective-permute-start(bf16[2,64,1024]{2,1,0:T(8,128)(2,1)S(1)} %quarter.1), channel_id=1, source_target_pairs={{0,4},{1,5},{2,6},{3,7},{4,0},{5,1},{6,2},{7,3},{8,12},{9,13},{10,... | collective-permute-start | bytes 786440 | tf_op jit(solution)/shard_map/ppermute | solution.py:1013
  6.2 22.2 %collective-permute-start.4 = (bf16[2,64,1024]{2,1,0:T(8,128)(2,1)S(1)}, bf16[2,64,1024]{2,1,0:T(8,128)(2,1)S(1)}, u32[]{:S(2)}, u32[]{:S(2)}) collective-permute-start(bf16[2,64,1024]{2,1,0:T(8,128)(2,1)S(1)} %quarter.1), channel_id=1, source_target_pairs={{0,2},{1,3},{2,4},{3,5},{4,6},{5,7},{6,0},{7,1},{8,10},{9,11},{10,... | collective-permute-start | bytes 786440 | tf_op jit(solution)/shard_map/ppermute | solution.py:1013
  23.6 6.4 %collective-permute-start.2 = (bf16[1,2,64,1024]{3,2,1,0:T(8,128)(2,1)S(1)}, bf16[1,2,64,1024]{3,2,1,0:T(8,128)(2,1)S(1)}, u32[]{:S(2)}, u32[]{:S(2)}) collective-permute-start(bf16[1,2,64,1024]{3,2,1,0:T(8,128)(2,1)S(1)} %pack.4.refs_2_.refs_1_), channel_id=1, source_target_pairs={{0,16},{8,24},{16,0},{24,8},{1,17},{9,25},{17,1},{25,9},{2,18},{10... | collective-permute-start | bytes 786440 | tf_op jit(solution)/shard_map/ppermute | solution.py:1006
  25.2 7.5 %collective-permute-start.1 = (bf16[1,2,64,1024]{3,2,1,0:T(8,128)(2,1)S(1)}, bf16[1,2,64,1024]{3,2,1,0:T(8,128)(2,1)S(1)}, u32[]{:S(2)}, u32[]{:S(2)}) collective-permute-start(bf16[1,2,64,1024]{3,2,1,0:T(8,128)(2,1)S(1)} %pack.4.refs_2_.refs_1_), channel_id=1, source_target_pairs={{0,8},{8,0},{16,24},{24,16},{1,9},{9,1},{17,25},{25,17},{2,10},{10... | collective-permute-start | bytes 786440 | tf_op jit(solution)/shard_map/ppermute | solution.py:1006
  32.8 10.1 %collective-permute-start.5 = (bf16[2,2,64,1024]{3,2,1,0:T(8,128)(2,1)S(1)}, bf16[2,2,64,1024]{3,2,1,0:T(8,128)(2,1)S(1)}, u32[]{:S(2)}, u32[]{:S(2)}) collective-permute-start(bf16[2,2,64,1024]{3,2,1,0:T(8,128)(2,1)S(1)} %tie.3.refs_4_), channel_id=1, source_target_pairs={{0,8},{8,0},{16,24},{24,16},{1,9},{9,1},{17,25},{25,17},{2,10},{10... | collective-permute-start | bytes 1572872 | tf_op jit(solution)/shard_map/ppermute | solution.py:1006
  34.3 9.2 %collective-permute-start.6 = (bf16[2,2,64,1024]{3,2,1,0:T(8,128)(2,1)S(1)}, bf16[2,2,64,1024]{3,2,1,0:T(8,128)(2,1)S(1)}, u32[]{:S(2)}, u32[]{:S(2)}) collective-permute-start(bf16[2,2,64,1024]{3,2,1,0:T(8,128)(2,1)S(1)} %tie.3.refs_4_), channel_id=1, source_target_pairs={{0,16},{8,24},{16,0},{24,8},{1,17},{9,25},{17,1},{25,9},{2,18},{10... | collective-permute-start | bytes 1572872 | tf_op jit(solution)/shard_map/ppermute | solution.py:1006
  34.3 7.9 %collective-permute-start.7 = (bf16[2,64,1024]{2,1,0:T(8,128)(2,1)S(1)}, bf16[2,64,1024]{2,1,0:T(8,128)(2,1)S(1)}, u32[]{:S(2)}, u32[]{:S(2)}) collective-permute-start(bf16[2,64,1024]{2,1,0:T(8,128)(2,1)S(1)} %get-tuple-element.53), channel_id=1, source_target_pairs={{0,4},{1,5},{2,6},{3,7},{4,0},{5,1},{6,2},{7,3},{8,12},{9,13},{10,... | collective-permute-start | bytes 786440 | tf_op jit(solution)/shard_map/ppermute | solution.py:1013
  43.7 7.3 %collective-permute-start.10 = (bf16[13,2,64,1024]{3,2,1,0:T(8,128)(2,1)S(1)}, bf16[13,2,64,1024]{3,2,1,0:T(8,128)(2,1)S(1)}, u32[]{:S(2)}, u32[]{:S(2)}) collective-permute-start(bf16[13,2,64,1024]{3,2,1,0:T(8,128)(2,1)S(1)} %pack.6.refs_1_.refs_0_), channel_id=1, source_target_pairs={{0,1},{1,0},{2,3},{3,2},{4,5},{5,4},{6,7},{7,6},{8,9},{9,8},{10,11... | collective-permute-start | bytes 10223624 | tf_op jit(solution)/shard_map/ppermute | solution.py:1009
  43.7 17.2 %collective-permute-start.9 = (bf16[2,2,64,1024]{3,2,1,0:T(8,128)(2,1)S(1)}, bf16[2,2,64,1024]{3,2,1,0:T(8,128)(2,1)S(1)}, u32[]{:S(2)}, u32[]{:S(2)}) collective-permute-start(bf16[2,2,64,1024]{3,2,1,0:T(8,128)(2,1)S(1)} %collective-permute-done.5.refs_5_), channel_id=1, source_target_pairs={{0,16},{8,24},{16,0},{24,8},{1,17},{9,25},{17,1},{25,9},{2,18},{10... | collective-permute-start | bytes 1572872 | tf_op jit(solution)/shard_map/ppermute | solution.py:1006
  44.7 14.0 %collective-permute-start.11 = (bf16[2,64,1024]{2,1,0:T(8,128)(2,1)S(1)}, bf16[2,64,1024]{2,1,0:T(8,128)(2,1)S(1)}, u32[]{:S(2)}, u32[]{:S(2)}) collective-permute-start(bf16[2,64,1024]{2,1,0:T(8,128)(2,1)S(1)} %get-tuple-element.56), channel_id=1, source_target_pairs={{0,2},{1,3},{2,4},{3,5},{4,6},{5,7},{6,0},{7,1},{8,10},{9,11},{10,... | collective-permute-start | bytes 786440 | tf_op jit(solution)/shard_map/ppermute | solution.py:1013
  47.2 13.7 %collective-permute-start.12 = (bf16[2,64,1024]{2,1,0:T(8,128)(2,1)S(1)}, bf16[2,64,1024]{2,1,0:T(8,128)(2,1)S(1)}, u32[]{:S(2)}, u32[]{:S(2)}) collective-permute-start(bf16[2,64,1024]{2,1,0:T(8,128)(2,1)S(1)} %get-tuple-element.57), channel_id=1, source_target_pairs={{0,6},{1,7},{2,0},{3,1},{4,2},{5,3},{6,4},{7,5},{8,14},{9,15},{10,... | collective-permute-start | bytes 786440 | tf_op jit(solution)/shard_map/ppermute | solution.py:1013
  47.2 13.7 %collective-permute-start.8 = (bf16[1,2,64,1024]{3,2,1,0:T(8,128)(2,1)S(1)}, bf16[1,2,64,1024]{3,2,1,0:T(8,128)(2,1)S(1)}, u32[]{:S(2)}, u32[]{:S(2)}) collective-permute-start(bf16[1,2,64,1024]{3,2,1,0:T(8,128)(2,1)S(1)} %collective-permute-done.2.refs_2_.refs_3_), channel_id=1, source_target_pairs={{0,8},{8,0},{16,24},{24,16},{1,9},{9,1},{17,25},{25,17},{2,10},{10... | collective-permute-start | bytes 786440 | tf_op jit(solution)/shard_map/ppermute | solution.py:1006
  73.9 14.0 %collective-permute-start.17 = (bf16[4,64,1024]{2,1,0:T(8,128)(2,1)S(1)}, bf16[4,64,1024]{2,1,0:T(8,128)(2,1)S(1)}, u32[]{:S(2)}, u32[]{:S(2)}) collective-permute-start(bf16[4,64,1024]{2,1,0:T(8,128)(2,1)S(1)} %get-tuple-element.71), channel_id=1, source_target_pairs={{0,8},{8,0},{16,24},{24,16},{1,9},{9,1},{17,25},{25,17},{2,10},{10... | collective-permute-start | bytes 1572872 | tf_op jit(solution)/shard_map/ppermute | solution.py:1006
  74.5 13.7 %collective-permute-start.18 = (bf16[4,64,1024]{2,1,0:T(8,128)(2,1)S(1)}, bf16[4,64,1024]{2,1,0:T(8,128)(2,1)S(1)}, u32[]{:S(2)}, u32[]{:S(2)}) collective-permute-start(bf16[4,64,1024]{2,1,0:T(8,128)(2,1)S(1)} %get-tuple-element.72), channel_id=1, source_target_pairs={{0,16},{8,24},{16,0},{24,8},{1,17},{9,25},{17,1},{25,9},{2,18},{10... | collective-permute-start | bytes 1572872 | tf_op jit(solution)/shard_map/ppermute | solution.py:1006
  88.3 14.9 %collective-permute-start.21 = (bf16[4,64,1024]{2,1,0:T(8,128)(2,1)S(1)}, bf16[4,64,1024]{2,1,0:T(8,128)(2,1)S(1)}, u32[]{:S(2)}, u32[]{:S(2)}) collective-permute-start(bf16[4,64,1024]{2,1,0:T(8,128)(2,1)S(1)} %tie.5), channel_id=1, source_target_pairs={{0,16},{8,24},{16,0},{24,8},{1,17},{9,25},{17,1},{25,9},{2,18},{10... | collective-permute-start | bytes 1572872 | tf_op jit(solution)/shard_map/ppermute | solution.py:1006
  88.9 14.9 %collective-permute-start.20 = (bf16[4,64,1024]{2,1,0:T(8,128)(2,1)S(1)}, bf16[4,64,1024]{2,1,0:T(8,128)(2,1)S(1)}, u32[]{:S(2)}, u32[]{:S(2)}) collective-permute-start(bf16[4,64,1024]{2,1,0:T(8,128)(2,1)S(1)} %tie.4), channel_id=1, source_target_pairs={{0,8},{8,0},{16,24},{24,16},{1,9},{9,1},{17,25},{25,17},{2,10},{10... | collective-permute-start | bytes 1572872 | tf_op jit(solution)/shard_map/ppermute | solution.py:1006
  90.4 19.0 %collective-permute-start.29 = (bf16[2,64,1024]{2,1,0:T(8,128)(2,1)S(1)}, bf16[2,64,1024]{2,1,0:T(8,128)(2,1)S(1)}, u32[]{:S(2)}, u32[]{:S(2)}) collective-permute-start(bf16[2,64,1024]{2,1,0:T(8,128)(2,1)S(1)} %get-tuple-element.76.refs_1_), channel_id=1, source_target_pairs={{0,8},{8,0},{16,24},{24,16},{1,9},{9,1},{17,25},{25,17},{2,10},{10... | collective-permute-start | bytes 786440 | tf_op jit(solution)/shard_map/ppermute | solution.py:1006
  90.9 18.5 %collective-permute-start.30 = (bf16[2,64,1024]{2,1,0:T(8,128)(2,1)S(1)}, bf16[2,64,1024]{2,1,0:T(8,128)(2,1)S(1)}, u32[]{:S(2)}, u32[]{:S(2)}) collective-permute-start(bf16[2,64,1024]{2,1,0:T(8,128)(2,1)S(1)} %get-tuple-element.77.refs_2_), channel_id=1, source_target_pairs={{0,16},{8,24},{16,0},{24,8},{1,17},{9,25},{17,1},{25,9},{2,18},{10... | collective-permute-start | bytes 786440 | tf_op jit(solution)/shard_map/ppermute | solution.py:1006
  103.9 19.5 %collective-permute-start.23 = (bf16[2,64,1024]{2,1,0:T(8,128)(2,1)S(1)}, bf16[2,64,1024]{2,1,0:T(8,128)(2,1)S(1)}, u32[]{:S(2)}, u32[]{:S(2)}) collective-permute-start(bf16[2,64,1024]{2,1,0:T(8,128)(2,1)S(1)} %get-tuple-element.81), channel_id=1, source_target_pairs={{0,8},{8,0},{16,24},{24,16},{1,9},{9,1},{17,25},{25,17},{2,10},{10... | collective-permute-start | bytes 786440 | tf_op jit(solution)/shard_map/ppermute | solution.py:1006
  105.4 18.0 %collective-permute-start.24 = (bf16[2,64,1024]{2,1,0:T(8,128)(2,1)S(1)}, bf16[2,64,1024]{2,1,0:T(8,128)(2,1)S(1)}, u32[]{:S(2)}, u32[]{:S(2)}) collective-permute-start(bf16[2,64,1024]{2,1,0:T(8,128)(2,1)S(1)} %get-tuple-element.82), channel_id=1, source_target_pairs={{0,16},{8,24},{16,0},{24,8},{1,17},{9,25},{17,1},{25,9},{2,18},{10... | collective-permute-start | bytes 786440 | tf_op jit(solution)/shard_map/ppermute | solution.py:1006
  106.9 6.3 %collective-permute-start.25 = (f32[8,1024]{1,0:T(8,128)S(1)}, f32[8,1024]{1,0:T(8,128)S(1)}, u32[]{:S(2)}, u32[]{:S(2)}) collective-permute-start(f32[8,1024]{1,0:T(8,128)S(1)} %add.10.refs_0_), channel_id=1, source_target_pairs={{0,4},{1,5},{2,6},{3,7},{4,0},{5,1},{6,2},{7,3},{8,12},{9,13},{10,... | collective-permute-start | bytes 98312 | tf_op jit(solution)/shard_map/ppermute | solution.py:1009
  109.5 7.1 %collective-permute-start.31 = (bf16[64,1024]{1,0:T(8,128)(2,1)S(1)}, bf16[64,1024]{1,0:T(8,128)(2,1)S(1)}, u32[]{:S(2)}, u32[]{:S(2)}) collective-permute-start(bf16[64,1024]{1,0:T(8,128)(2,1)S(1)} %get-tuple-element.89), channel_id=1, source_target_pairs={{0,2},{1,3},{2,4},{3,5},{4,6},{5,7},{6,0},{7,1},{8,10},{9,11},{10,... | collective-permute-start | bytes 393224 | tf_op jit(solution)/shard_map/ppermute | solution.py:1013
  111.8 6.3 %collective-permute-start.32 = (bf16[64,1024]{1,0:T(8,128)(2,1)S(1)}, bf16[64,1024]{1,0:T(8,128)(2,1)S(1)}, u32[]{:S(2)}, u32[]{:S(2)}) collective-permute-start(bf16[64,1024]{1,0:T(8,128)(2,1)S(1)} %get-tuple-element.90), channel_id=1, source_target_pairs={{0,4},{1,5},{2,6},{3,7},{4,0},{5,1},{6,2},{7,3},{8,12},{9,13},{10,... | collective-permute-start | bytes 393224 | tf_op jit(solution)/shard_map/ppermute | solution.py:1013
  113.2 7.8 %collective-permute-start.33 = (bf16[64,1024]{1,0:T(8,128)(2,1)S(1)}, bf16[64,1024]{1,0:T(8,128)(2,1)S(1)}, u32[]{:S(2)}, u32[]{:S(2)}) collective-permute-start(bf16[64,1024]{1,0:T(8,128)(2,1)S(1)} %get-tuple-element.91), channel_id=1, source_target_pairs={{0,6},{1,7},{2,0},{3,1},{4,2},{5,3},{6,4},{7,5},{8,14},{9,15},{10,... | collective-permute-start | bytes 393224 | tf_op jit(solution)/shard_map/ppermute | solution.py:1013
  121.0 6.5 %collective-permute-start.34 = (bf16[64,1024]{1,0:T(8,128)(2,1)S(1)}, bf16[64,1024]{1,0:T(8,128)(2,1)S(1)}, u32[]{:S(2)}, u32[]{:S(2)}) collective-permute-start(bf16[64,1024]{1,0:T(8,128)(2,1)S(1)} %collect.2.refs_5_.refs_4_), channel_id=1, source_target_pairs={{0,8},{8,0},{16,24},{24,16},{1,9},{9,1},{17,25},{25,17},{2,10},{10... | collective-permute-start | bytes 393224 | tf_op jit(solution)/shard_map/ppermute | solution.py:1006
  123.6 5.4 %collective-permute-start.26 = (bf16[64,1024]{1,0:T(8,128)(2,1)S(1)}, bf16[64,1024]{1,0:T(8,128)(2,1)S(1)}, u32[]{:S(2)}, u32[]{:S(2)}) collective-permute-start(bf16[64,1024]{1,0:T(8,128)(2,1)S(1)} %get-tuple-element.84), channel_id=1, source_target_pairs={{0,2},{1,3},{2,4},{3,5},{4,6},{5,7},{6,0},{7,1},{8,10},{9,11},{10,... | collective-permute-start | bytes 393224 | tf_op jit(solution)/shard_map/ppermute | solution.py:1013
  123.6 8.7 %collective-permute-start.27 = (bf16[64,1024]{1,0:T(8,128)(2,1)S(1)}, bf16[64,1024]{1,0:T(8,128)(2,1)S(1)}, u32[]{:S(2)}, u32[]{:S(2)}) collective-permute-start(bf16[64,1024]{1,0:T(8,128)(2,1)S(1)} %get-tuple-element.85), channel_id=1, source_target_pairs={{0,4},{1,5},{2,6},{3,7},{4,0},{5,1},{6,2},{7,3},{8,12},{9,13},{10,... | collective-permute-start | bytes 393224 | tf_op jit(solution)/shard_map/ppermute | solution.py:1013
  126.1 8.1 %collective-permute-start.28 = (bf16[64,1024]{1,0:T(8,128)(2,1)S(1)}, bf16[64,1024]{1,0:T(8,128)(2,1)S(1)}, u32[]{:S(2)}, u32[]{:S(2)}) collective-permute-start(bf16[64,1024]{1,0:T(8,128)(2,1)S(1)} %get-tuple-element.86), channel_id=1, source_target_pairs={{0,6},{1,7},{2,0},{3,1},{4,2},{5,3},{6,4},{7,5},{8,14},{9,15},{10,... | collective-permute-start | bytes 393224 | tf_op jit(solution)/shard_map/ppermute | solution.py:1013
  134.3 11.2 %collective-permute-start.38 = (bf16[144,1024]{1,0:T(8,128)(2,1)S(1)}, bf16[144,1024]{1,0:T(8,128)(2,1)S(1)}, u32[]{:S(2)}, u32[]{:S(2)}) collective-permute-start(bf16[144,1024]{1,0:T(8,128)(2,1)S(1)} %get-tuple-element.93), channel_id=1, source_target_pairs={{0,24},{8,16},{16,8},{24,0},{1,25},{9,17},{17,9},{25,1},{2,26},{10... | collective-permute-start | bytes 884744 | tf_op jit(solution)/shard_map/ppermute | solution.py:1006
  135.6 9.3 %collective-permute-start.36 = (bf16[80,1024]{1,0:T(8,128)(2,1)S(1)}, bf16[80,1024]{1,0:T(8,128)(2,1)S(1)}, u32[]{:S(2)}, u32[]{:S(2)}) collective-permute-start(bf16[80,1024]{1,0:T(8,128)(2,1)S(1)} %get-tuple-element.92.refs_0_), channel_id=1, source_target_pairs={{0,8},{8,0},{16,24},{24,16},{1,9},{9,1},{17,25},{25,17},{2,10},{10... | collective-permute-start | bytes 491528 | tf_op jit(solution)/shard_map/ppermute | solution.py:1006
  136.8 8.7 %collective-permute-start.37 = (bf16[80,1024]{1,0:T(8,128)(2,1)S(1)}, bf16[80,1024]{1,0:T(8,128)(2,1)S(1)}, u32[]{:S(2)}, u32[]{:S(2)}) collective-permute-start(bf16[80,1024]{1,0:T(8,128)(2,1)S(1)} %get-tuple-element.92.refs_0_), channel_id=1, source_target_pairs={{0,16},{8,24},{16,0},{24,8},{1,17},{9,25},{17,1},{25,9},{2,18},{10... | collective-permute-start | bytes 491528 | tf_op jit(solution)/shard_map/ppermute | solution.py:1006
  (20 other events, 126.6 us)

commit v13 on v12

--- a/solution.py
+++ b/solution.py
@@ -898,16 +898,28 @@
 
 
 def collect_kernel(count, *refs):
-    outs = refs[count:]
-    part, width = refs[0].shape
     total = refs[0][...].astype(F32)
     for ref in refs[1:count]:
         total = total + ref[...].astype(F32)
-    if len(outs) == 1:
-        outs[0][...] = total.astype(BF16)
-        return
-    vector_ref, other_ref, short_ref, long_ref, held_ref = outs[0], outs[1], *outs[-3:]
-    short_ref[pl.ds(0, part), :] = total.astype(BF16)
+    refs[-1][...] = total.astype(BF16)
+
+
+def collect(parts, *after):
+    return pl.pallas_call(
+        functools.partial(collect_kernel, len(parts)),
+        out_shape=jax.ShapeDtypeStruct(parts[0].shape, BF16),
+        in_specs=[VMEM] * len(parts) + [ANY] * len(after),
+        out_specs=VMEM,
+        compiler_params=params(16),
+        cost_estimate=COST,
+        name="collect",
+    )(*parts, *after)
+
+
+def join_kernel(total_ref, vector_ref, other_ref, *refs):
+    short_ref, long_ref, held_ref = refs[-3:]
+    part = total_ref.shape[0]
+    short_ref[pl.ds(0, part), :] = total_ref[...]
     rest = vector_ref[0:3, :]
     held_ref[...] = jnp.zeros_like(held_ref)
     for index in range(3):
@@ -919,26 +931,20 @@
     long_ref[pl.ds(part + 16, part), :] = other_ref[...]
 
 
-def collect(parts, vector=None, other=None, after=()):
-    part, width = parts[0].shape
-    operands = list(parts)
-    if vector is None:
-        counts = (part,)
-        scratch = []
-    else:
-        operands += [vector, other]
-        counts = (part + 16, 2 * part + 16)
-        scratch = [pltpu.VMEM((16, width), F32)]
-    return pl.pallas_call(
-        functools.partial(collect_kernel, len(parts)),
-        out_shape=tuple(jax.ShapeDtypeStruct((rows, width), BF16) for rows in counts),
-        in_specs=[VMEM] * len(operands) + [ANY] * len(after),
-        out_specs=tuple([VMEM] * len(counts)),
-        scratch_shapes=scratch,
+def join(total, vector, other, *after):
+    part, width = total.shape
+    return pl.pallas_call(
+        join_kernel,
+        out_shape=tuple(
+            jax.ShapeDtypeStruct((rows, width), BF16) for rows in (part + 16, 2 * part + 16)
+        ),
+        in_specs=[VMEM] * 3 + [ANY] * len(after),
+        out_specs=(VMEM, VMEM),
+        scratch_shapes=[pltpu.VMEM((16, width), F32)],
         compiler_params=params(16),
         cost_estimate=COST,
-        name="collect",
-    )(*operands, *after)
+        name="join",
+    )(total, vector, other, *after)
 
 
 def place_kernel(part, tokens, group_ref, *refs):
@@ -1079,17 +1085,17 @@
     from_x, from_y, later = first_step(*rest, vector)
     late = second_step(later)
     shares = totals(own, from_x, from_y, *late)
-    (down_total,) = collect(arrive_along(shares))
-    down_x, down_y = beside(down_total, 1), beside(down_total, 2)
-    vector = vector + partner(vector, 2)
-    to_x, to_y = tie(to_x, *later), tie(to_y, *later)
-    from_x, from_y, later = first_step(to_x, to_y, *rest_up, vector)
-    flip = 4
+    flip = 2
     while flip < ray_count:
         vector = vector + partner(vector, flip)
         flip *= 2
-    shares = totals(own_up, from_x, from_y, *second_step(later), vector)
-    short, long = collect(arrive_along(shares), vector, down_total, (down_x, down_y))
+    to_x, to_y = tie(to_x, *later), tie(to_y, *later)
+    from_x, from_y, later = first_step(to_x, to_y, *rest_up, vector, shares[0])
+    up_shares = totals(own_up, from_x, from_y, *second_step(later))
+    down_total = collect(arrive_along(shares), up_shares[0])
+    down_x, down_y = beside(down_total, 1), beside(down_total, 2)
+    up_total = collect(arrive_along(up_shares))
+    short, long = join(up_total, vector, down_total, down_x, down_y)
     up_x, up_y, both = beside(short, 1), beside(short, 2), beside(long, 3)
     grad_up, grad_down, gain, scale, loss = place_quarters(
         group, (short, up_x, up_y, both), (down_total, down_x, down_y, both), part,

time: 147 us -> 150 us (1.020)
  the two profiles are of different devices: /device:TPU:8 before, /device:TPU:26 now
where the time goes in v13:
time: 150 us
  waiting for transfers between devices  66.4 us (44%)
  starting transfers between devices  48.8 us (33%)
  Pallas kernels  31.8 us (21%)
  local copies, waits for them, and re-layouts  2.13 us (1%)
    ppermute x19, waiting for transfers between devices, beside(): lax.ppermute(array, 'grp', [(g, g ^ flip) for g in range(group_count)])  29.1 us
    ppermute x12, waiting for transfers between devices, along(): return lax.ppermute(array, 'ray', pairs)  27.8 us
    ppermute x12, starting transfers between devices, along(): return lax.ppermute(array, 'ray', pairs)  22 us
    ppermute x19, starting transfers between devices, beside(): lax.ppermute(array, 'grp', [(g, g ^ flip) for g in range(group_count)])  21.7 us
    ppermute x8, waiting for transfers between devices, partner(): return lax.ppermute(array, 'ray', [(r, r ^ flip) for r in range(ray_count)])  9.5 us
    pallas_call x1, Pallas kernels, render(): pl.pallas_call(functools.partial(render_kernel, ray_count, relative), out...  8.41 us
    pallas_call x2, Pallas kernels, forward(): pl.pallas_call(functools.partial(forward_kernel, first, blocks, len(own),...  7.92 us
    pallas_call x2, Pallas kernels, up_gradient(): pl.pallas_call(functools.partial(up_grad_kernel, side, weight_pieces, act...  6.04 us
  transfers between devices with their start and end apart: 39, of which 18 were waited for; matrix products, arithmetic and copies ran while one was open for 0% of the time, Pallas kernels for 17%

profile of v13, /device:TPU:26, one launch (start us, length us, event | category | flops | bytes accessed | tf_op | source)
XLA Modules:
  0.0 150.1 jit_solution(10699781299958045043)
XLA Ops:
  4.0 3.0 %collective-permute-start.4 = (bf16[2,64,1024]{2,1,0:T(8,128)(2,1)S(1)}, bf16[2,64,1024]{2,1,0:T(8,128)(2,1)S(1)}, u32[]{:S(2)}, u32[]{:S(2)}) collective-permute-start(bf16[2,64,1024]{2,1,0:T(8,128)(2,1)S(1)} %quarter.1), channel_id=1, source_target_pairs={{0,2},{1,3},{2,4},{3,5},{4,6},{5,7},{6,0},{7,1},{8,10},{9,11},{10,... | collective-permute-start | bytes 786440 | tf_op jit(solution)/shard_map/ppermute | solution.py:1019
  7.1 8.4 %render.1 = (bf16[2,64,1024]{2,1,0:T(8,128)(2,1)S(1)}, bf16[2,64,1024]{2,1,0:T(8,128)(2,1)S(1)}, bf16[2,64,1024]{2,1,0:T(8,128)(2,1)S(1)}, bf16[2,64,1024]{2,1,0:T(8,128)(2,1)S(1)}) custom-call(s32[1]{0:T(128)} %bitcast.1.me_ref, s32[1,8]{1,0:T(1,128)S(1)} %copy-done.11, s32[32,512]{1,0:T(8,128)S(1)} %copy-done.7, f32[32,512]{1,0:T(8,128)S(1)} %copy-done.8, ...), custom_call_target="tpu_custom_call" | custom-call | flops 1048576 | bytes 65536 | tf_op jit(solution)/shard_map/render/pallas_call | solution.py:152
  15.5 1.6 %collective-permute-start.2 = (bf16[1,2,64,1024]{3,2,1,0:T(8,128)(2,1)S(1)}, bf16[1,2,64,1024]{3,2,1,0:T(8,128)(2,1)S(1)}, u32[]{:S(2)}, u32[]{:S(2)}) collective-permute-start(bf16[1,2,64,1024]{3,2,1,0:T(8,128)(2,1)S(1)} %pack.4.refs_2_.refs_1_), channel_id=1, source_target_pairs={{0,16},{8,24},{16,0},{24,8},{1,17},{9,25},{17,1},{25,9},{2,18},{10... | collective-permute-start | bytes 786440 | tf_op jit(solution)/shard_map/ppermute | solution.py:1012
  17.7 6.8 %collective-permute-done.3.refs_0_ = bf16[2,64,1024]{2,1,0:T(8,128)(2,1)S(1)} collective-permute-done((bf16[2,64,1024]{2,1,0:T(8,128)(2,1)S(1)}, bf16[2,64,1024]{2,1,0:T(8,128)(2,1)S(1)}, u32[]{:S(2)}, u32[]{:S(2)}) %collective-permute-start.3) | collective-permute-done | bytes 262176 | tf_op jit(solution)/shard_map/ppermute | solution.py:1019
  25.1 1.5 %collective-permute-start.6 = (bf16[2,2,64,1024]{3,2,1,0:T(8,128)(2,1)S(1)}, bf16[2,2,64,1024]{3,2,1,0:T(8,128)(2,1)S(1)}, u32[]{:S(2)}, u32[]{:S(2)}) collective-permute-start(bf16[2,2,64,1024]{3,2,1,0:T(8,128)(2,1)S(1)} %tie.3.refs_4_), channel_id=1, source_target_pairs={{0,16},{8,24},{16,0},{24,8},{1,17},{9,25},{17,1},{25,9},{2,18},{10... | collective-permute-start | bytes 1572872 | tf_op jit(solution)/shard_map/ppermute | solution.py:1012
  26.7 7.0 %collective-permute-start.7 = (bf16[2,64,1024]{2,1,0:T(8,128)(2,1)S(1)}, bf16[2,64,1024]{2,1,0:T(8,128)(2,1)S(1)}, u32[]{:S(2)}, u32[]{:S(2)}) collective-permute-start(bf16[2,64,1024]{2,1,0:T(8,128)(2,1)S(1)} %get-tuple-element.53), channel_id=1, source_target_pairs={{0,4},{1,5},{2,6},{3,7},{4,0},{5,1},{6,2},{7,3},{8,12},{9,13},{10,... | collective-permute-start | bytes 786440 | tf_op jit(solution)/shard_map/ppermute | solution.py:1019
  33.9 8.1 %collective-permute-done.7.refs_7_.refs_2_.refs_8_ = bf16[2,64,1024]{2,1,0:T(8,128)(2,1)S(1)} collective-permute-done((bf16[2,64,1024]{2,1,0:T(8,128)(2,1)S(1)}, bf16[2,64,1024]{2,1,0:T(8,128)(2,1)S(1)}, u32[]{:S(2)}, u32[]{:S(2)}) %collective-permute-start.7) | collective-permute-done | bytes 262176 | tf_op jit(solution)/shard_map/ppermute | solution.py:1019
  42.9 3.1 %collective-permute-start.11 = (bf16[2,64,1024]{2,1,0:T(8,128)(2,1)S(1)}, bf16[2,64,1024]{2,1,0:T(8,128)(2,1)S(1)}, u32[]{:S(2)}, u32[]{:S(2)}) collective-permute-start(bf16[2,64,1024]{2,1,0:T(8,128)(2,1)S(1)} %get-tuple-element.56), channel_id=1, source_target_pairs={{0,2},{1,3},{2,4},{3,5},{4,6},{5,7},{6,0},{7,1},{8,10},{9,11},{10,... | collective-permute-start | bytes 786440 | tf_op jit(solution)/shard_map/ppermute | solution.py:1019
  47.5 3.2 %tokens.1 = (bf16[512,1024]{1,0:T(8,128)(2,1)S(1)}, bf16[512,1024]{1,0:T(8,128)(2,1)S(1)}, bf16[1024,512]{1,0:T(8,128)(2,1)S(1)}) custom-call(s32[1]{0:T(128)} %bitcast.1.me_ref, s32[1,8]{1,0:T(1,128)S(1)} %copy-done.11, s32[1,4096]{1,0:T(1,128)S(1)} %copy-done.6, bf16[512,1024]{1,0:T(8,128)(2,1)S(1)} %copy-done.1, f32[1,1024]{1,0:T(1,128)S(1)} %bitcast.8), custom_call_target="tpu_custom_call" | custom-call | flops 1048576 | bytes 65536 | tf_op jit(solution)/shard_map/tokens/pallas_call | solution.py:238
  50.7 5.0 %forward.2 = (bf16[2,13,64,512]{3,2,1,0:T(8,128)(2,1)S(1)}, f32[2,13,64,512]{3,2,1,0:T(8,128)S(1)}, f32[512,1024]{1,0:T(8,128)S(1)}) custom-call(bf16[1024,512]{1,0:T(8,128)(2,1)S(1)} %get-tuple-element.54.refs_0_, bf16[13,2,64,1024]{3,2,1,0:T(8,128)(2,1)S(1)} %pack.6.refs_1_.refs_0_, bf16[13,2,64,1024]{3,2,1,0:T(8,128)(2,1)S(1)} %collective-permute-done.10.refs_2_.refs_0_), custom_call_target="tpu_custom_call" | custom-call | flops 1048576 | bytes 65536 | tf_op jit(solution)/shard_map/forward/pallas_call | solution.py:652
  55.7 2.6 %collective-permute-done.12.refs_4_.refs_3_.refs_9_ = bf16[2,64,1024]{2,1,0:T(8,128)(2,1)S(1)} collective-permute-done((bf16[2,64,1024]{2,1,0:T(8,128)(2,1)S(1)}, bf16[2,64,1024]{2,1,0:T(8,128)(2,1)S(1)}, u32[]{:S(2)}, u32[]{:S(2)}) %collective-permute-start.12) | collective-permute-done | bytes 262176 | tf_op jit(solution)/shard_map/ppermute | solution.py:1019
  59.1 2.4 %collective-permute-done.14.refs_10_ = bf16[4,64,1024]{2,1,0:T(8,128)(2,1)S(1)} collective-permute-done((bf16[4,64,1024]{2,1,0:T(8,128)(2,1)S(1)}, bf16[4,64,1024]{2,1,0:T(8,128)(2,1)S(1)}, u32[]{:S(2)}, u32[]{:S(2)}) %collective-permute-start.14) | collective-permute-done | bytes 524320 | tf_op jit(solution)/shard_map/ppermute | solution.py:1015
  61.5 2.9 %forward.3 = (bf16[2,3,64,512]{3,2,1,0:T(8,128)(2,1)S(1)}, f32[2,3,64,512]{3,2,1,0:T(8,128)S(1)}, bf16[512,1024]{1,0:T(8,128)(2,1)S(1)}, bf16[1024,512]{1,0:T(8,128)(2,1)S(1)}, f32[8,1024]{1,0:T(8,128)S(1)}) custom-call(bf16[1024,512]{1,0:T(8,128)(2,1)S(1)} %get-tuple-element.54.refs_0_, bf16[3,2,64,1024]{3,2,1,0:T(8,128)(2,1)S(1)} %pack.7.refs_1_, ...), custom_call_target="tpu_custom_call" | custom-call | flops 1048576 | bytes 65536 | tf_op jit(solution)/shard_map/forward/pallas_call | solution.py:652
  65.9 2.8 %up_gradient.2 = (bf16[4,4,64,1024]{3,2,1,0:T(8,128)(2,1)S(1)}, f32[1,1024]{1,0:T(1,128)S(1)}) custom-call(bf16[13,2,64,1024]{3,2,1,0:T(8,128)(2,1)S(1)} %collective-permute-done.10.refs_2_.refs_0_, bf16[3,2,64,1024]{3,2,1,0:T(8,128)(2,1)S(1)} %collective-permute-done.13.refs_2_.refs_1_, f32[2,13,64,512]{3,2,1,0:T(8,128)S(1)} %get-tuple-element.58.refs_2_, ...), custom_call_target="tpu_custom_call" | custom-call | flops 1048576 | bytes 65536 | tf_op jit(solution)/shard_map/up_gradient/pallas_call | solution.py:844
  71.3 1.6 %collective-permute-start.17 = (bf16[4,64,1024]{2,1,0:T(8,128)(2,1)S(1)}, bf16[4,64,1024]{2,1,0:T(8,128)(2,1)S(1)}, u32[]{:S(2)}, u32[]{:S(2)}) collective-permute-start(bf16[4,64,1024]{2,1,0:T(8,128)(2,1)S(1)} %get-tuple-element.71), channel_id=1, source_target_pairs={{0,8},{8,0},{16,24},{24,16},{1,9},{9,1},{17,25},{25,17},{2,10},{10... | collective-permute-start | bytes 1572872 | tf_op jit(solution)/shard_map/ppermute | solution.py:1012
  74.2 3.3 %up_gradient.3 = (bf16[4,64,1024]{2,1,0:T(8,128)(2,1)S(1)}, bf16[4,64,1024]{2,1,0:T(8,128)(2,1)S(1)}, bf16[4,64,1024]{2,1,0:T(8,128)(2,1)S(1)}, bf16[2,64,1024]{...) custom-call(bf16[13,2,64,1024]{3,2,1,0:T(8,128)(2,1)S(1)} %pack.6.refs_1_.refs_0_, ...), custom_call_target="tpu_custom_call" | custom-call | flops 1048576 | bytes 65536 | tf_op jit(solution)/shard_map/up_gradient/pallas_call | solution.py:844
  78.8 6.5 %collective-permute-done.17.x_ref = bf16[4,64,1024]{2,1,0:T(8,128)(2,1)S(1)} collective-permute-done((bf16[4,64,1024]{2,1,0:T(8,128)(2,1)S(1)}, bf16[4,64,1024]{2,1,0:T(8,128)(2,1)S(1)}, u32[]{:S(2)}, u32[]{:S(2)}) %collective-permute-start.17) | collective-permute-done | bytes 524320 | tf_op jit(solution)/shard_map/ppermute | solution.py:1012
  90.8 1.7 %collective-permute-start.22 = (f32[8,1024]{1,0:T(8,128)S(1)}, f32[8,1024]{1,0:T(8,128)S(1)}, u32[]{:S(2)}, u32[]{:S(2)}) collective-permute-start(f32[8,1024]{1,0:T(8,128)S(1)} %add.9.refs_0_), channel_id=1, source_target_pairs={{0,2},{1,3},{2,0},{3,1},{4,6},{5,7},{6,4},{7,5},{8,10},{9,11},{10,... | collective-permute-start | bytes 98312 | tf_op jit(solution)/shard_map/ppermute | solution.py:1015
  92.5 2.2 %collective-permute-done.22 = f32[8,1024]{1,0:T(8,128)S(1)} collective-permute-done((f32[8,1024]{1,0:T(8,128)S(1)}, f32[8,1024]{1,0:T(8,128)S(1)}, u32[]{:S(2)}, u32[]{:S(2)}) %collective-permute-start.22) | collective-permute-done | bytes 32800 | tf_op jit(solution)/shard_map/ppermute | solution.py:1015
  94.7 2.0 %collective-permute-start.23 = (f32[8,1024]{1,0:T(8,128)S(1)}, f32[8,1024]{1,0:T(8,128)S(1)}, u32[]{:S(2)}, u32[]{:S(2)}) collective-permute-start(f32[8,1024]{1,0:T(8,128)S(1)} %add.10), channel_id=1, source_target_pairs={{0,4},{1,5},{2,6},{3,7},{4,0},{5,1},{6,2},{7,3},{8,12},{9,13},{10,... | collective-permute-start | bytes 98312 | tf_op jit(solution)/shard_map/ppermute | solution.py:1015
  96.7 2.8 %collective-permute-done.23 = f32[8,1024]{1,0:T(8,128)S(1)} collective-permute-done((f32[8,1024]{1,0:T(8,128)S(1)}, f32[8,1024]{1,0:T(8,128)S(1)}, u32[]{:S(2)}, u32[]{:S(2)}) %collective-permute-start.23) | collective-permute-done | bytes 32800 | tf_op jit(solution)/shard_map/ppermute | solution.py:1015
  99.5 6.8 %collective-permute-done.24.x_late_ref = bf16[2,64,1024]{2,1,0:T(8,128)(2,1)S(1)} collective-permute-done((bf16[2,64,1024]{2,1,0:T(8,128)(2,1)S(1)}, bf16[2,64,1024]{2,1,0:T(8,128)(2,1)S(1)}, u32[]{:S(2)}, u32[]{:S(2)}) %collective-permute-start.24) | collective-permute-done | bytes 262176 | tf_op jit(solution)/shard_map/ppermute | solution.py:1012
  107.9 1.7 %collective-permute-start.31 = (bf16[64,1024]{1,0:T(8,128)(2,1)S(1)}, bf16[64,1024]{1,0:T(8,128)(2,1)S(1)}, u32[]{:S(2)}, u32[]{:S(2)}) collective-permute-start(bf16[64,1024]{1,0:T(8,128)(2,1)S(1)} %get-tuple-element.89), channel_id=1, source_target_pairs={{0,2},{1,3},{2,4},{3,5},{4,6},{5,7},{6,0},{7,1},{8,10},{9,11},{10,... | collective-permute-start | bytes 393224 | tf_op jit(solution)/shard_map/ppermute | solution.py:1019
  113.9 1.8 %collective-permute-start.28 = (bf16[64,1024]{1,0:T(8,128)(2,1)S(1)}, bf16[64,1024]{1,0:T(8,128)(2,1)S(1)}, u32[]{:S(2)}, u32[]{:S(2)}) collective-permute-start(bf16[64,1024]{1,0:T(8,128)(2,1)S(1)} %get-tuple-element.86), channel_id=1, source_target_pairs={{0,2},{1,3},{2,4},{3,5},{4,6},{5,7},{6,0},{7,1},{8,10},{9,11},{10,... | collective-permute-start | bytes 393224 | tf_op jit(solution)/shard_map/ppermute | solution.py:1019
  115.7 1.5 collective-permute-start.29
  117.9 9.9 %collective-permute-done.32.refs_2_ = bf16[64,1024]{1,0:T(8,128)(2,1)S(1)} collective-permute-done((bf16[64,1024]{1,0:T(8,128)(2,1)S(1)}, bf16[64,1024]{1,0:T(8,128)(2,1)S(1)}, u32[]{:S(2)}, u32[]{:S(2)}) %collective-permute-start.32) | collective-permute-done | bytes 131104 | tf_op jit(solution)/shard_map/ppermute | solution.py:1019
  129.3 1.7 %collective-permute-start.35 = (bf16[64,1024]{1,0:T(8,128)(2,1)S(1)}, bf16[64,1024]{1,0:T(8,128)(2,1)S(1)}, u32[]{:S(2)}, u32[]{:S(2)}) collective-permute-start(bf16[64,1024]{1,0:T(8,128)(2,1)S(1)} %collect.3.other_ref.refs_4_), channel_id=1, source_target_pairs={{0,16},{8,24},{16,0},{24,8},{1,17},{9,25},{17,1},{25,9},{2,18},{10... | collective-permute-start | bytes 393224 | tf_op jit(solution)/shard_map/ppermute | solution.py:1012
  132.9 5.1 %collective-permute-done.35.refs_1_.refs_6_ = bf16[64,1024]{1,0:T(8,128)(2,1)S(1)} collective-permute-done((bf16[64,1024]{1,0:T(8,128)(2,1)S(1)}, bf16[64,1024]{1,0:T(8,128)(2,1)S(1)}, u32[]{:S(2)}, u32[]{:S(2)}) %collective-permute-start.35) | collective-permute-done | bytes 131104 | tf_op jit(solution)/shard_map/ppermute | solution.py:1012
  138.0 2.1 %collective-permute-start.38 = (bf16[144,1024]{1,0:T(8,128)(2,1)S(1)}, bf16[144,1024]{1,0:T(8,128)(2,1)S(1)}, u32[]{:S(2)}, u32[]{:S(2)}) collective-permute-start(bf16[144,1024]{1,0:T(8,128)(2,1)S(1)} %get-tuple-element.93), channel_id=1, source_target_pairs={{0,24},{8,16},{16,8},{24,0},{1,25},{9,17},{17,9},{25,1},{2,26},{10... | collective-permute-start | bytes 884744 | tf_op jit(solution)/shard_map/ppermute | solution.py:1012
  140.1 1.8 %collective-permute-start.36 = (bf16[80,1024]{1,0:T(8,128)(2,1)S(1)}, bf16[80,1024]{1,0:T(8,128)(2,1)S(1)}, u32[]{:S(2)}, u32[]{:S(2)}) collective-permute-start(bf16[80,1024]{1,0:T(8,128)(2,1)S(1)} %get-tuple-element.92.refs_0_), channel_id=1, source_target_pairs={{0,8},{8,0},{16,24},{24,16},{1,9},{9,1},{17,25},{25,17},{2,10},{10... | collective-permute-start | bytes 491528 | tf_op jit(solution)/shard_map/ppermute | solution.py:1012
  141.9 6.5 %collective-permute-done.36.refs_1_ = bf16[80,1024]{1,0:T(8,128)(2,1)S(1)} collective-permute-done((bf16[80,1024]{1,0:T(8,128)(2,1)S(1)}, bf16[80,1024]{1,0:T(8,128)(2,1)S(1)}, u32[]{:S(2)}, u32[]{:S(2)}) %collective-permute-start.36) | collective-permute-done | bytes 163872 | tf_op jit(solution)/shard_map/ppermute | solution.py:1012
  148.4 1.7 %place.1 = (f32[1024,256]{1,0:T(8,128)}, f32[256,1024]{1,0:T(8,128)}, f32[1,1024]{1,0:T(1,128)}, f32[1,1024]{1,0:T(1,128)}, f32[1,1]{1,0:T(1,128)}) custom-call(s32[1]{0:T(128)} %bitcast.group_ref, bf16[80,1024]{1,0:T(8,128)(2,1)S(1)} %get-tuple-element.92.refs_0_, bf16[80,1024]{1,0:T(8,128)(2,1)S(1)} %collective-permute-done.36.refs_1_, ...), custom_call_target="tpu_custom_call" | custom-call | flops 1048576 | bytes 65536 | tf_op jit(solution)/shard_map/place/pallas_call | solution.py:978
  (102 shorter events, 30.1 us)
Async XLA Ops:
  3.1 12.4 %collective-permute-start = (bf16[2,64,1024]{2,1,0:T(8,128)(2,1)S(1)}, bf16[2,64,1024]{2,1,0:T(8,128)(2,1)S(1)}, u32[]{:S(2)}, u32[]{:S(2)}) collective-permute-start(bf16[2,64,1024]{2,1,0:T(8,128)(2,1)S(1)} %quarter.1), channel_id=1, source_target_pairs={{0,6},{1,7},{2,0},{3,1},{4,2},{5,3},{6,4},{7,5},{8,14},{9,15},{10,... | collective-permute-start | bytes 786440 | tf_op jit(solution)/shard_map/ppermute | solution.py:1019
  3.6 20.8 %collective-permute-start.3 = (bf16[2,64,1024]{2,1,0:T(8,128)(2,1)S(1)}, bf16[2,64,1024]{2,1,0:T(8,128)(2,1)S(1)}, u32[]{:S(2)}, u32[]{:S(2)}) collective-permute-start(bf16[2,64,1024]{2,1,0:T(8,128)(2,1)S(1)} %quarter.1), channel_id=1, source_target_pairs={{0,4},{1,5},{2,6},{3,7},{4,0},{5,1},{6,2},{7,3},{8,12},{9,13},{10,... | collective-permute-start | bytes 786440 | tf_op jit(solution)/shard_map/ppermute | solution.py:1019
  4.0 20.5 %collective-permute-start.4 = (bf16[2,64,1024]{2,1,0:T(8,128)(2,1)S(1)}, bf16[2,64,1024]{2,1,0:T(8,128)(2,1)S(1)}, u32[]{:S(2)}, u32[]{:S(2)}) collective-permute-start(bf16[2,64,1024]{2,1,0:T(8,128)(2,1)S(1)} %quarter.1), channel_id=1, source_target_pairs={{0,2},{1,3},{2,4},{3,5},{4,6},{5,7},{6,0},{7,1},{8,10},{9,11},{10,... | collective-permute-start | bytes 786440 | tf_op jit(solution)/shard_map/ppermute | solution.py:1019
  15.5 9.0 %collective-permute-start.2 = (bf16[1,2,64,1024]{3,2,1,0:T(8,128)(2,1)S(1)}, bf16[1,2,64,1024]{3,2,1,0:T(8,128)(2,1)S(1)}, u32[]{:S(2)}, u32[]{:S(2)}) collective-permute-start(bf16[1,2,64,1024]{3,2,1,0:T(8,128)(2,1)S(1)} %pack.4.refs_2_.refs_1_), channel_id=1, source_target_pairs={{0,16},{8,24},{16,0},{24,8},{1,17},{9,25},{17,1},{25,9},{2,18},{10... | collective-permute-start | bytes 786440 | tf_op jit(solution)/shard_map/ppermute | solution.py:1012
  17.1 7.4 %collective-permute-start.1 = (bf16[1,2,64,1024]{3,2,1,0:T(8,128)(2,1)S(1)}, bf16[1,2,64,1024]{3,2,1,0:T(8,128)(2,1)S(1)}, u32[]{:S(2)}, u32[]{:S(2)}) collective-permute-start(bf16[1,2,64,1024]{3,2,1,0:T(8,128)(2,1)S(1)} %pack.4.refs_2_.refs_1_), channel_id=1, source_target_pairs={{0,8},{8,0},{16,24},{24,16},{1,9},{9,1},{17,25},{25,17},{2,10},{10... | collective-permute-start | bytes 786440 | tf_op jit(solution)/shard_map/ppermute | solution.py:1012
  24.5 17.5 %collective-permute-start.5 = (bf16[2,2,64,1024]{3,2,1,0:T(8,128)(2,1)S(1)}, bf16[2,2,64,1024]{3,2,1,0:T(8,128)(2,1)S(1)}, u32[]{:S(2)}, u32[]{:S(2)}) collective-permute-start(bf16[2,2,64,1024]{3,2,1,0:T(8,128)(2,1)S(1)} %tie.3.refs_4_), channel_id=1, source_target_pairs={{0,8},{8,0},{16,24},{24,16},{1,9},{9,1},{17,25},{25,17},{2,10},{10... | collective-permute-start | bytes 1572872 | tf_op jit(solution)/shard_map/ppermute | solution.py:1012
  25.1 16.9 %collective-permute-start.6 = (bf16[2,2,64,1024]{3,2,1,0:T(8,128)(2,1)S(1)}, bf16[2,2,64,1024]{3,2,1,0:T(8,128)(2,1)S(1)}, u32[]{:S(2)}, u32[]{:S(2)}) collective-permute-start(bf16[2,2,64,1024]{3,2,1,0:T(8,128)(2,1)S(1)} %tie.3.refs_4_), channel_id=1, source_target_pairs={{0,16},{8,24},{16,0},{24,8},{1,17},{9,25},{17,1},{25,9},{2,18},{10... | collective-permute-start | bytes 1572872 | tf_op jit(solution)/shard_map/ppermute | solution.py:1012
  26.7 15.3 %collective-permute-start.7 = (bf16[2,64,1024]{2,1,0:T(8,128)(2,1)S(1)}, bf16[2,64,1024]{2,1,0:T(8,128)(2,1)S(1)}, u32[]{:S(2)}, u32[]{:S(2)}) collective-permute-start(bf16[2,64,1024]{2,1,0:T(8,128)(2,1)S(1)} %get-tuple-element.53), channel_id=1, source_target_pairs={{0,4},{1,5},{2,6},{3,7},{4,0},{5,1},{6,2},{7,3},{8,12},{9,13},{10,... | collective-permute-start | bytes 786440 | tf_op jit(solution)/shard_map/ppermute | solution.py:1019
  42.2 8.5 %collective-permute-start.10 = (bf16[13,2,64,1024]{3,2,1,0:T(8,128)(2,1)S(1)}, bf16[13,2,64,1024]{3,2,1,0:T(8,128)(2,1)S(1)}, u32[]{:S(2)}, u32[]{:S(2)}) collective-permute-start(bf16[13,2,64,1024]{3,2,1,0:T(8,128)(2,1)S(1)} %pack.6.refs_1_.refs_0_), channel_id=1, source_target_pairs={{0,1},{1,0},{2,3},{3,2},{4,5},{5,4},{6,7},{7,6},{8,9},{9,8},{10,11... | collective-permute-start | bytes 10223624 | tf_op jit(solution)/shard_map/ppermute | solution.py:1015
  42.3 16.0 %collective-permute-start.9 = (bf16[2,2,64,1024]{3,2,1,0:T(8,128)(2,1)S(1)}, bf16[2,2,64,1024]{3,2,1,0:T(8,128)(2,1)S(1)}, u32[]{:S(2)}, u32[]{:S(2)}) collective-permute-start(bf16[2,2,64,1024]{3,2,1,0:T(8,128)(2,1)S(1)} %collective-permute-done.5.refs_5_), channel_id=1, source_target_pairs={{0,16},{8,24},{16,0},{24,8},{1,17},{9,25},{17,1},{25,9},{2,18},{10... | collective-permute-start | bytes 1572872 | tf_op jit(solution)/shard_map/ppermute | solution.py:1012
  42.9 12.9 %collective-permute-start.11 = (bf16[2,64,1024]{2,1,0:T(8,128)(2,1)S(1)}, bf16[2,64,1024]{2,1,0:T(8,128)(2,1)S(1)}, u32[]{:S(2)}, u32[]{:S(2)}) collective-permute-start(bf16[2,64,1024]{2,1,0:T(8,128)(2,1)S(1)} %get-tuple-element.56), channel_id=1, source_target_pairs={{0,2},{1,3},{2,4},{3,5},{4,6},{5,7},{6,0},{7,1},{8,10},{9,11},{10,... | collective-permute-start | bytes 786440 | tf_op jit(solution)/shard_map/ppermute | solution.py:1019
  46.0 12.4 %collective-permute-start.12 = (bf16[2,64,1024]{2,1,0:T(8,128)(2,1)S(1)}, bf16[2,64,1024]{2,1,0:T(8,128)(2,1)S(1)}, u32[]{:S(2)}, u32[]{:S(2)}) collective-permute-start(bf16[2,64,1024]{2,1,0:T(8,128)(2,1)S(1)} %get-tuple-element.57), channel_id=1, source_target_pairs={{0,6},{1,7},{2,0},{3,1},{4,2},{5,3},{6,4},{7,5},{8,14},{9,15},{10,... | collective-permute-start | bytes 786440 | tf_op jit(solution)/shard_map/ppermute | solution.py:1019
  46.0 12.4 %collective-permute-start.8 = (bf16[1,2,64,1024]{3,2,1,0:T(8,128)(2,1)S(1)}, bf16[1,2,64,1024]{3,2,1,0:T(8,128)(2,1)S(1)}, u32[]{:S(2)}, u32[]{:S(2)}) collective-permute-start(bf16[1,2,64,1024]{3,2,1,0:T(8,128)(2,1)S(1)} %collective-permute-done.2.refs_2_.refs_3_), channel_id=1, source_target_pairs={{0,8},{8,0},{16,24},{24,16},{1,9},{9,1},{17,25},{25,17},{2,10},{10... | collective-permute-start | bytes 786440 | tf_op jit(solution)/shard_map/ppermute | solution.py:1012
  68.7 5.6 %collective-permute-start.15 = (bf16[4,4,64,1024]{3,2,1,0:T(8,128)(2,1)S(1)}, bf16[4,4,64,1024]{3,2,1,0:T(8,128)(2,1)S(1)}, u32[]{:S(2)}, u32[]{:S(2)}) collective-permute-start(bf16[4,4,64,1024]{3,2,1,0:T(8,128)(2,1)S(1)} %get-tuple-element.64), channel_id=1, source_target_pairs={{0,1},{1,0},{2,3},{3,2},{4,5},{5,4},{6,7},{7,6},{8,9},{9,8},{10,11... | collective-permute-start | bytes 6291464 | tf_op jit(solution)/shard_map/ppermute | solution.py:1015
  71.3 14.0 %collective-permute-start.17 = (bf16[4,64,1024]{2,1,0:T(8,128)(2,1)S(1)}, bf16[4,64,1024]{2,1,0:T(8,128)(2,1)S(1)}, u32[]{:S(2)}, u32[]{:S(2)}) collective-permute-start(bf16[4,64,1024]{2,1,0:T(8,128)(2,1)S(1)} %get-tuple-element.71), channel_id=1, source_target_pairs={{0,8},{8,0},{16,24},{24,16},{1,9},{9,1},{17,25},{25,17},{2,10},{10... | collective-permute-start | bytes 1572872 | tf_op jit(solution)/shard_map/ppermute | solution.py:1012
  72.8 13.7 %collective-permute-start.18 = (bf16[4,64,1024]{2,1,0:T(8,128)(2,1)S(1)}, bf16[4,64,1024]{2,1,0:T(8,128)(2,1)S(1)}, u32[]{:S(2)}, u32[]{:S(2)}) collective-permute-start(bf16[4,64,1024]{2,1,0:T(8,128)(2,1)S(1)} %get-tuple-element.72), channel_id=1, source_target_pairs={{0,16},{8,24},{16,0},{24,8},{1,17},{9,25},{17,1},{25,9},{2,18},{10... | collective-permute-start | bytes 1572872 | tf_op jit(solution)/shard_map/ppermute | solution.py:1012
  86.7 19.8 %collective-permute-start.21 = (bf16[4,64,1024]{2,1,0:T(8,128)(2,1)S(1)}, bf16[4,64,1024]{2,1,0:T(8,128)(2,1)S(1)}, u32[]{:S(2)}, u32[]{:S(2)}) collective-permute-start(bf16[4,64,1024]{2,1,0:T(8,128)(2,1)S(1)} %tie.5), channel_id=1, source_target_pairs={{0,16},{8,24},{16,0},{24,8},{1,17},{9,25},{17,1},{25,9},{2,18},{10... | collective-permute-start | bytes 1572872 | tf_op jit(solution)/shard_map/ppermute | solution.py:1012
  88.1 18.4 %collective-permute-start.20 = (bf16[4,64,1024]{2,1,0:T(8,128)(2,1)S(1)}, bf16[4,64,1024]{2,1,0:T(8,128)(2,1)S(1)}, u32[]{:S(2)}, u32[]{:S(2)}) collective-permute-start(bf16[4,64,1024]{2,1,0:T(8,128)(2,1)S(1)} %tie.4), channel_id=1, source_target_pairs={{0,8},{8,0},{16,24},{24,16},{1,9},{9,1},{17,25},{25,17},{2,10},{10... | collective-permute-start | bytes 1572872 | tf_op jit(solution)/shard_map/ppermute | solution.py:1012
  88.7 17.6 %collective-permute-start.24 = (bf16[2,64,1024]{2,1,0:T(8,128)(2,1)S(1)}, bf16[2,64,1024]{2,1,0:T(8,128)(2,1)S(1)}, u32[]{:S(2)}, u32[]{:S(2)}) collective-permute-start(bf16[2,64,1024]{2,1,0:T(8,128)(2,1)S(1)} %get-tuple-element.76.refs_1_), channel_id=1, source_target_pairs={{0,8},{8,0},{16,24},{24,16},{1,9},{9,1},{17,25},{25,17},{2,10},{10... | collective-permute-start | bytes 786440 | tf_op jit(solution)/shard_map/ppermute | solution.py:1012
  90.2 16.1 %collective-permute-start.25 = (bf16[2,64,1024]{2,1,0:T(8,128)(2,1)S(1)}, bf16[2,64,1024]{2,1,0:T(8,128)(2,1)S(1)}, u32[]{:S(2)}, u32[]{:S(2)}) collective-permute-start(bf16[2,64,1024]{2,1,0:T(8,128)(2,1)S(1)} %get-tuple-element.77.refs_2_), channel_id=1, source_target_pairs={{0,16},{8,24},{16,0},{24,8},{1,17},{9,25},{17,1},{25,9},{2,18},{10... | collective-permute-start | bytes 786440 | tf_op jit(solution)/shard_map/ppermute | solution.py:1012
  106.6 6.4 %collective-permute-start.26 = (bf16[2,64,1024]{2,1,0:T(8,128)(2,1)S(1)}, bf16[2,64,1024]{2,1,0:T(8,128)(2,1)S(1)}, u32[]{:S(2)}, u32[]{:S(2)}) collective-permute-start(bf16[2,64,1024]{2,1,0:T(8,128)(2,1)S(1)} %get-tuple-element.83), channel_id=1, source_target_pairs={{0,8},{8,0},{16,24},{24,16},{1,9},{9,1},{17,25},{25,17},{2,10},{10... | collective-permute-start | bytes 786440 | tf_op jit(solution)/shard_map/ppermute | solution.py:1012
  107.3 6.4 %collective-permute-start.27 = (bf16[2,64,1024]{2,1,0:T(8,128)(2,1)S(1)}, bf16[2,64,1024]{2,1,0:T(8,128)(2,1)S(1)}, u32[]{:S(2)}, u32[]{:S(2)}) collective-permute-start(bf16[2,64,1024]{2,1,0:T(8,128)(2,1)S(1)} %get-tuple-element.84), channel_id=1, source_target_pairs={{0,16},{8,24},{16,0},{24,8},{1,17},{9,25},{17,1},{25,9},{2,18},{10... | collective-permute-start | bytes 786440 | tf_op jit(solution)/shard_map/ppermute | solution.py:1012
  107.9 9.3 %collective-permute-start.31 = (bf16[64,1024]{1,0:T(8,128)(2,1)S(1)}, bf16[64,1024]{1,0:T(8,128)(2,1)S(1)}, u32[]{:S(2)}, u32[]{:S(2)}) collective-permute-start(bf16[64,1024]{1,0:T(8,128)(2,1)S(1)} %get-tuple-element.89), channel_id=1, source_target_pairs={{0,2},{1,3},{2,4},{3,5},{4,6},{5,7},{6,0},{7,1},{8,10},{9,11},{10,... | collective-permute-start | bytes 393224 | tf_op jit(solution)/shard_map/ppermute | solution.py:1019
  109.6 18.1 %collective-permute-start.32 = (bf16[64,1024]{1,0:T(8,128)(2,1)S(1)}, bf16[64,1024]{1,0:T(8,128)(2,1)S(1)}, u32[]{:S(2)}, u32[]{:S(2)}) collective-permute-start(bf16[64,1024]{1,0:T(8,128)(2,1)S(1)} %get-tuple-element.90), channel_id=1, source_target_pairs={{0,4},{1,5},{2,6},{3,7},{4,0},{5,1},{6,2},{7,3},{8,12},{9,13},{10,... | collective-permute-start | bytes 393224 | tf_op jit(solution)/shard_map/ppermute | solution.py:1019
  111.1 16.7 %collective-permute-start.33 = (bf16[64,1024]{1,0:T(8,128)(2,1)S(1)}, bf16[64,1024]{1,0:T(8,128)(2,1)S(1)}, u32[]{:S(2)}, u32[]{:S(2)}) collective-permute-start(bf16[64,1024]{1,0:T(8,128)(2,1)S(1)} %get-tuple-element.91), channel_id=1, source_target_pairs={{0,6},{1,7},{2,0},{3,1},{4,2},{5,3},{6,4},{7,5},{8,14},{9,15},{10,... | collective-permute-start | bytes 393224 | tf_op jit(solution)/shard_map/ppermute | solution.py:1019
  113.9 17.1 %collective-permute-start.28 = (bf16[64,1024]{1,0:T(8,128)(2,1)S(1)}, bf16[64,1024]{1,0:T(8,128)(2,1)S(1)}, u32[]{:S(2)}, u32[]{:S(2)}) collective-permute-start(bf16[64,1024]{1,0:T(8,128)(2,1)S(1)} %get-tuple-element.86), channel_id=1, source_target_pairs={{0,2},{1,3},{2,4},{3,5},{4,6},{5,7},{6,0},{7,1},{8,10},{9,11},{10,... | collective-permute-start | bytes 393224 | tf_op jit(solution)/shard_map/ppermute | solution.py:1019
  115.7 15.8 %collective-permute-start.29 = (bf16[64,1024]{1,0:T(8,128)(2,1)S(1)}, bf16[64,1024]{1,0:T(8,128)(2,1)S(1)}, u32[]{:S(2)}, u32[]{:S(2)}) collective-permute-start(bf16[64,1024]{1,0:T(8,128)(2,1)S(1)} %get-tuple-element.87), channel_id=1, source_target_pairs={{0,4},{1,5},{2,6},{3,7},{4,0},{5,1},{6,2},{7,3},{8,12},{9,13},{10,... | collective-permute-start | bytes 393224 | tf_op jit(solution)/shard_map/ppermute | solution.py:1019
  117.2 14.3 %collective-permute-start.30 = (bf16[64,1024]{1,0:T(8,128)(2,1)S(1)}, bf16[64,1024]{1,0:T(8,128)(2,1)S(1)}, u32[]{:S(2)}, u32[]{:S(2)}) collective-permute-start(bf16[64,1024]{1,0:T(8,128)(2,1)S(1)} %get-tuple-element.88), channel_id=1, source_target_pairs={{0,6},{1,7},{2,0},{3,1},{4,2},{5,3},{6,4},{7,5},{8,14},{9,15},{10,... | collective-permute-start | bytes 393224 | tf_op jit(solution)/shard_map/ppermute | solution.py:1019
  129.3 8.6 %collective-permute-start.35 = (bf16[64,1024]{1,0:T(8,128)(2,1)S(1)}, bf16[64,1024]{1,0:T(8,128)(2,1)S(1)}, u32[]{:S(2)}, u32[]{:S(2)}) collective-permute-start(bf16[64,1024]{1,0:T(8,128)(2,1)S(1)} %collect.3.other_ref.refs_4_), channel_id=1, source_target_pairs={{0,16},{8,24},{16,0},{24,8},{1,17},{9,25},{17,1},{25,9},{2,18},{10... | collective-permute-start | bytes 393224 | tf_op jit(solution)/shard_map/ppermute | solution.py:1012
  138.0 10.4 %collective-permute-start.38 = (bf16[144,1024]{1,0:T(8,128)(2,1)S(1)}, bf16[144,1024]{1,0:T(8,128)(2,1)S(1)}, u32[]{:S(2)}, u32[]{:S(2)}) collective-permute-start(bf16[144,1024]{1,0:T(8,128)(2,1)S(1)} %get-tuple-element.93), channel_id=1, source_target_pairs={{0,24},{8,16},{16,8},{24,0},{1,25},{9,17},{17,9},{25,1},{2,26},{10... | collective-permute-start | bytes 884744 | tf_op jit(solution)/shard_map/ppermute | solution.py:1012
  140.1 8.3 %collective-permute-start.36 = (bf16[80,1024]{1,0:T(8,128)(2,1)S(1)}, bf16[80,1024]{1,0:T(8,128)(2,1)S(1)}, u32[]{:S(2)}, u32[]{:S(2)}) collective-permute-start(bf16[80,1024]{1,0:T(8,128)(2,1)S(1)} %get-tuple-element.92.refs_0_), channel_id=1, source_target_pairs={{0,8},{8,0},{16,24},{24,16},{1,9},{9,1},{17,25},{25,17},{2,10},{10... | collective-permute-start | bytes 491528 | tf_op jit(solution)/shard_map/ppermute | solution.py:1012
  141.9 6.5 %collective-permute-start.37 = (bf16[80,1024]{1,0:T(8,128)(2,1)S(1)}, bf16[80,1024]{1,0:T(8,128)(2,1)S(1)}, u32[]{:S(2)}, u32[]{:S(2)}) collective-permute-start(bf16[80,1024]{1,0:T(8,128)(2,1)S(1)} %get-tuple-element.92.refs_0_), channel_id=1, source_target_pairs={{0,16},{8,24},{16,0},{24,8},{1,17},{9,25},{17,1},{25,9},{2,18},{10... | collective-permute-start | bytes 491528 | tf_op jit(solution)/shard_map/ppermute | solution.py:1012
  (20 other events, 119.9 us)

commit v14 on v13

--- a/solution.py
+++ b/solution.py
@@ -1069,6 +1069,10 @@
         (up_arrived, layer_norm_gain.reshape(1, width), small),
     )
     vector = vector + partner(vector)
+    flip = 2
+    while flip < ray_count:
+        vector = vector + partner(vector, flip)
+        flip *= 2
 
     def first_step(to_x, to_y, x_later, y_later, *after):
         from_x, from_y = beside(to_x, 1), beside(to_y, 2)
@@ -1085,12 +1089,7 @@
     from_x, from_y, later = first_step(*rest, vector)
     late = second_step(later)
     shares = totals(own, from_x, from_y, *late)
-    flip = 2
-    while flip < ray_count:
-        vector = vector + partner(vector, flip)
-        flip *= 2
-    to_x, to_y = tie(to_x, *later), tie(to_y, *later)
-    from_x, from_y, later = first_step(to_x, to_y, *rest_up, vector, shares[0])
+    from_x, from_y, later = first_step(to_x, to_y, *rest_up)
     up_shares = totals(own_up, from_x, from_y, *second_step(later))
     down_total = collect(arrive_along(shares), up_shares[0])
     down_x, down_y = beside(down_total, 1), beside(down_total, 2)

time: 150 us -> 147 us (0.980)
  the two profiles are of different devices: /device:TPU:26 before, /device:TPU:8 now
where the time goes in v14:
time: 147 us; the launch traced here: 145 us
  waiting for transfers between devices  72.8 us (50%)
  starting transfers between devices  37 us (25%)
  Pallas kernels  31.8 us (22%)
  local copies, waits for them, and re-layouts  2.13 us (1%)
    ppermute x12, waiting for transfers between devices, along(): return lax.ppermute(array, 'ray', pairs)  33.4 us
    ppermute x19, waiting for transfers between devices, beside(): lax.ppermute(array, 'grp', [(g, g ^ flip) for g in range(group_count)])  26.9 us
    ppermute x19, starting transfers between devices, beside(): lax.ppermute(array, 'grp', [(g, g ^ flip) for g in range(group_count)])  19.4 us
    ppermute x12, starting transfers between devices, along(): return lax.ppermute(array, 'ray', pairs)  15 us
    ppermute x8, waiting for transfers between devices, partner(): return lax.ppermute(array, 'ray', [(r, r ^ flip) for r in range(ray_count)])  12.5 us
    pallas_call x1, Pallas kernels, render(): pl.pallas_call(functools.partial(render_kernel, ray_count, relative), out...  8.41 us
    pallas_call x2, Pallas kernels, forward(): pl.pallas_call(functools.partial(forward_kernel, first, blocks, len(own),...  7.92 us
    pallas_call x2, Pallas kernels, up_gradient(): pl.pallas_call(functools.partial(up_grad_kernel, side, weight_pieces, act...  6.05 us
  transfers between devices with their start and end apart: 39, of which 29 were waited for; matrix products, arithmetic and copies ran while one was open for 0% of the time, Pallas kernels for 17%

profile of v14, /device:TPU:8, one launch (start us, length us, event | category | flops | bytes accessed | tf_op | source)
XLA Modules:
  0.0 144.7 jit_solution(15202760164887879230)
XLA Ops:
  3.2 3.0 %collective-permute-start.3 = (bf16[2,64,1024]{2,1,0:T(8,128)(2,1)S(1)}, bf16[2,64,1024]{2,1,0:T(8,128)(2,1)S(1)}, u32[]{:S(2)}, u32[]{:S(2)}) collective-permute-start(bf16[2,64,1024]{2,1,0:T(8,128)(2,1)S(1)} %quarter.1), channel_id=1, source_target_pairs={{0,4},{1,5},{2,6},{3,7},{4,0},{5,1},{6,2},{7,3},{8,12},{9,13},{10,... | collective-permute-start | bytes 786440 | tf_op jit(solution)/shard_map/ppermute | solution.py:1019
  6.2 2.5 %collective-permute-start.4 = (bf16[2,64,1024]{2,1,0:T(8,128)(2,1)S(1)}, bf16[2,64,1024]{2,1,0:T(8,128)(2,1)S(1)}, u32[]{:S(2)}, u32[]{:S(2)}) collective-permute-start(bf16[2,64,1024]{2,1,0:T(8,128)(2,1)S(1)} %quarter.1), channel_id=1, source_target_pairs={{0,2},{1,3},{2,4},{3,5},{4,6},{5,7},{6,0},{7,1},{8,10},{9,11},{10,... | collective-permute-start | bytes 786440 | tf_op jit(solution)/shard_map/ppermute | solution.py:1019
  8.7 8.4 %render.1 = (bf16[2,64,1024]{2,1,0:T(8,128)(2,1)S(1)}, bf16[2,64,1024]{2,1,0:T(8,128)(2,1)S(1)}, bf16[2,64,1024]{2,1,0:T(8,128)(2,1)S(1)}, bf16[2,64,1024]{2,1,0:T(8,128)(2,1)S(1)}) custom-call(s32[1]{0:T(128)} %bitcast.1.me_ref, s32[1,8]{1,0:T(1,128)S(1)} %copy-done.11, s32[32,512]{1,0:T(8,128)S(1)} %copy-done.7, f32[32,512]{1,0:T(8,128)S(1)} %copy-done.8, ...), custom_call_target="tpu_custom_call" | custom-call | flops 1048576 | bytes 65536 | tf_op jit(solution)/shard_map/render/pallas_call | solution.py:152
  17.2 6.4 %collective-permute-done.refs_0_ = bf16[2,64,1024]{2,1,0:T(8,128)(2,1)S(1)} collective-permute-done((bf16[2,64,1024]{2,1,0:T(8,128)(2,1)S(1)}, bf16[2,64,1024]{2,1,0:T(8,128)(2,1)S(1)}, u32[]{:S(2)}, u32[]{:S(2)}) %collective-permute-start) | collective-permute-done | bytes 262176 | tf_op jit(solution)/shard_map/ppermute | solution.py:1019
  23.6 1.6 %collective-permute-start.2 = (bf16[1,2,64,1024]{3,2,1,0:T(8,128)(2,1)S(1)}, bf16[1,2,64,1024]{3,2,1,0:T(8,128)(2,1)S(1)}, u32[]{:S(2)}, u32[]{:S(2)}) collective-permute-start(bf16[1,2,64,1024]{3,2,1,0:T(8,128)(2,1)S(1)} %pack.4.refs_2_.refs_1_), channel_id=1, source_target_pairs={{0,16},{8,24},{16,0},{24,8},{1,17},{9,25},{17,1},{25,9},{2,18},{10... | collective-permute-start | bytes 786440 | tf_op jit(solution)/shard_map/ppermute | solution.py:1012
  25.2 1.5 %collective-permute-start.1 = (bf16[1,2,64,1024]{3,2,1,0:T(8,128)(2,1)S(1)}, bf16[1,2,64,1024]{3,2,1,0:T(8,128)(2,1)S(1)}, u32[]{:S(2)}, u32[]{:S(2)}) collective-permute-start(bf16[1,2,64,1024]{3,2,1,0:T(8,128)(2,1)S(1)} %pack.4.refs_2_.refs_1_), channel_id=1, source_target_pairs={{0,8},{8,0},{16,24},{24,16},{1,9},{9,1},{17,25},{25,17},{2,10},{10... | collective-permute-start | bytes 786440 | tf_op jit(solution)/shard_map/ppermute | solution.py:1012
  26.7 1.7 %collective-permute-done.4.refs_1_ = bf16[2,64,1024]{2,1,0:T(8,128)(2,1)S(1)} collective-permute-done((bf16[2,64,1024]{2,1,0:T(8,128)(2,1)S(1)}, bf16[2,64,1024]{2,1,0:T(8,128)(2,1)S(1)}, u32[]{:S(2)}, u32[]{:S(2)}) %collective-permute-start.4) | collective-permute-done | bytes 262176 | tf_op jit(solution)/shard_map/ppermute | solution.py:1019
  28.5 1.6 %collective-permute-done.2.refs_2_.refs_3_ = bf16[1,2,64,1024]{3,2,1,0:T(8,128)(2,1)S(1)} collective-permute-done((bf16[1,2,64,1024]{3,2,1,0:T(8,128)(2,1)S(1)}, bf16[1,2,64,1024]{3,2,1,0:T(8,128)(2,1)S(1)}, u32[]{:S(2)}, u32[]{:S(2)}) %collective-permute-start.2) | collective-permute-done | bytes 262176 | tf_op jit(solution)/shard_map/ppermute | solution.py:1012
  30.1 2.7 %collective-permute-done.1.refs_1_.refs_2_ = bf16[1,2,64,1024]{3,2,1,0:T(8,128)(2,1)S(1)} collective-permute-done((bf16[1,2,64,1024]{3,2,1,0:T(8,128)(2,1)S(1)}, bf16[1,2,64,1024]{3,2,1,0:T(8,128)(2,1)S(1)}, u32[]{:S(2)}, u32[]{:S(2)}) %collective-permute-start.1) | collective-permute-done | bytes 262176 | tf_op jit(solution)/shard_map/ppermute | solution.py:1012
  32.8 1.5 %collective-permute-start.5 = (bf16[2,2,64,1024]{3,2,1,0:T(8,128)(2,1)S(1)}, bf16[2,2,64,1024]{3,2,1,0:T(8,128)(2,1)S(1)}, u32[]{:S(2)}, u32[]{:S(2)}) collective-permute-start(bf16[2,2,64,1024]{3,2,1,0:T(8,128)(2,1)S(1)} %tie.1.refs_4_), channel_id=1, source_target_pairs={{0,8},{8,0},{16,24},{24,16},{1,9},{9,1},{17,25},{25,17},{2,10},{10... | collective-permute-start | bytes 1572872 | tf_op jit(solution)/shard_map/ppermute | solution.py:1012
  34.5 7.6 %collective-permute-done.7.refs_7_.refs_2_.refs_8_ = bf16[2,64,1024]{2,1,0:T(8,128)(2,1)S(1)} collective-permute-done((bf16[2,64,1024]{2,1,0:T(8,128)(2,1)S(1)}, bf16[2,64,1024]{2,1,0:T(8,128)(2,1)S(1)}, u32[]{:S(2)}, u32[]{:S(2)}) %collective-permute-start.7) | collective-permute-done | bytes 262176 | tf_op jit(solution)/shard_map/ppermute | solution.py:1019
  44.7 2.5 %collective-permute-start.11 = (bf16[2,64,1024]{2,1,0:T(8,128)(2,1)S(1)}, bf16[2,64,1024]{2,1,0:T(8,128)(2,1)S(1)}, u32[]{:S(2)}, u32[]{:S(2)}) collective-permute-start(bf16[2,64,1024]{2,1,0:T(8,128)(2,1)S(1)} %get-tuple-element.56), channel_id=1, source_target_pairs={{0,2},{1,3},{2,4},{3,5},{4,6},{5,7},{6,0},{7,1},{8,10},{9,11},{10,... | collective-permute-start | bytes 786440 | tf_op jit(solution)/shard_map/ppermute | solution.py:1019
  47.7 3.2 %tokens.1 = (bf16[512,1024]{1,0:T(8,128)(2,1)S(1)}, bf16[512,1024]{1,0:T(8,128)(2,1)S(1)}, bf16[1024,512]{1,0:T(8,128)(2,1)S(1)}) custom-call(s32[1]{0:T(128)} %bitcast.1.me_ref, s32[1,8]{1,0:T(1,128)S(1)} %copy-done.11, s32[1,4096]{1,0:T(1,128)S(1)} %copy-done.6, bf16[512,1024]{1,0:T(8,128)(2,1)S(1)} %copy-done.1, f32[1,1024]{1,0:T(1,128)S(1)} %bitcast.8), custom_call_target="tpu_custom_call" | custom-call | flops 1048576 | bytes 65536 | tf_op jit(solution)/shard_map/tokens/pallas_call | solution.py:238
  51.0 5.0 %forward.2 = (bf16[2,13,64,512]{3,2,1,0:T(8,128)(2,1)S(1)}, f32[2,13,64,512]{3,2,1,0:T(8,128)S(1)}, f32[512,1024]{1,0:T(8,128)S(1)}) custom-call(bf16[1024,512]{1,0:T(8,128)(2,1)S(1)} %get-tuple-element.54.refs_0_, bf16[13,2,64,1024]{3,2,1,0:T(8,128)(2,1)S(1)} %pack.6.refs_1_.refs_0_, bf16[13,2,64,1024]{3,2,1,0:T(8,128)(2,1)S(1)} %collective-permute-done.10.refs_2_.refs_0_), custom_call_target="tpu_custom_call" | custom-call | flops 1048576 | bytes 65536 | tf_op jit(solution)/shard_map/forward/pallas_call | solution.py:652
  56.0 2.7 %collective-permute-done.11.refs_3_.refs_1_.refs_7_ = bf16[2,64,1024]{2,1,0:T(8,128)(2,1)S(1)} collective-permute-done((bf16[2,64,1024]{2,1,0:T(8,128)(2,1)S(1)}, bf16[2,64,1024]{2,1,0:T(8,128)(2,1)S(1)}, u32[]{:S(2)}, u32[]{:S(2)}) %collective-permute-start.11) | collective-permute-done | bytes 262176 | tf_op jit(solution)/shard_map/ppermute | solution.py:1019
  58.7 2.2 %collective-permute-done.12.refs_4_.refs_3_.refs_9_ = bf16[2,64,1024]{2,1,0:T(8,128)(2,1)S(1)} collective-permute-done((bf16[2,64,1024]{2,1,0:T(8,128)(2,1)S(1)}, bf16[2,64,1024]{2,1,0:T(8,128)(2,1)S(1)}, u32[]{:S(2)}, u32[]{:S(2)}) %collective-permute-start.12) | collective-permute-done | bytes 262176 | tf_op jit(solution)/shard_map/ppermute | solution.py:1019
  61.7 2.4 %collective-permute-done.14.refs_10_ = bf16[4,64,1024]{2,1,0:T(8,128)(2,1)S(1)} collective-permute-done((bf16[4,64,1024]{2,1,0:T(8,128)(2,1)S(1)}, bf16[4,64,1024]{2,1,0:T(8,128)(2,1)S(1)}, u32[]{:S(2)}, u32[]{:S(2)}) %collective-permute-start.14) | collective-permute-done | bytes 524320 | tf_op jit(solution)/shard_map/ppermute | solution.py:1015
  64.1 2.9 %forward.3 = (bf16[2,3,64,512]{3,2,1,0:T(8,128)(2,1)S(1)}, f32[2,3,64,512]{3,2,1,0:T(8,128)S(1)}, bf16[512,1024]{1,0:T(8,128)(2,1)S(1)}, bf16[1024,512]{1,0:T(8,128)(2,1)S(1)}, f32[8,1024]{1,0:T(8,128)S(1)}) custom-call(bf16[1024,512]{1,0:T(8,128)(2,1)S(1)} %get-tuple-element.54.refs_0_, bf16[3,2,64,1024]{3,2,1,0:T(8,128)(2,1)S(1)} %pack.7.refs_1_, ...), custom_call_target="tpu_custom_call" | custom-call | flops 1048576 | bytes 65536 | tf_op jit(solution)/shard_map/forward/pallas_call | solution.py:652
  68.5 2.8 %up_gradient.2 = (bf16[4,4,64,1024]{3,2,1,0:T(8,128)(2,1)S(1)}, f32[1,1024]{1,0:T(1,128)S(1)}) custom-call(bf16[13,2,64,1024]{3,2,1,0:T(8,128)(2,1)S(1)} %collective-permute-done.10.refs_2_.refs_0_, bf16[3,2,64,1024]{3,2,1,0:T(8,128)(2,1)S(1)} %collective-permute-done.13.refs_2_.refs_1_, f32[2,13,64,512]{3,2,1,0:T(8,128)S(1)} %get-tuple-element.58.refs_2_, ...), custom_call_target="tpu_custom_call" | custom-call | flops 1048576 | bytes 65536 | tf_op jit(solution)/shard_map/up_gradient/pallas_call | solution.py:844
  75.5 3.3 %up_gradient.3 = (bf16[4,64,1024]{2,1,0:T(8,128)(2,1)S(1)}, bf16[4,64,1024]{2,1,0:T(8,128)(2,1)S(1)}, bf16[4,64,1024]{2,1,0:T(8,128)(2,1)S(1)}, bf16[2,64,1024]{...) custom-call(bf16[13,2,64,1024]{3,2,1,0:T(8,128)(2,1)S(1)} %pack.6.refs_1_.refs_0_, ...), custom_call_target="tpu_custom_call" | custom-call | flops 1048576 | bytes 65536 | tf_op jit(solution)/shard_map/up_gradient/pallas_call | solution.py:844
  79.8 1.5 %collective-permute-start.17 = (bf16[4,64,1024]{2,1,0:T(8,128)(2,1)S(1)}, bf16[4,64,1024]{2,1,0:T(8,128)(2,1)S(1)}, u32[]{:S(2)}, u32[]{:S(2)}) collective-permute-start(bf16[4,64,1024]{2,1,0:T(8,128)(2,1)S(1)} %get-tuple-element.68), channel_id=1, source_target_pairs={{0,16},{8,24},{16,0},{24,8},{1,17},{9,25},{17,1},{25,9},{2,18},{10... | collective-permute-start | bytes 1572872 | tf_op jit(solution)/shard_map/ppermute | solution.py:1012
  82.8 3.6 %collective-permute-done.24 = f32[8,1024]{1,0:T(8,128)S(1)} collective-permute-done((f32[8,1024]{1,0:T(8,128)S(1)}, f32[8,1024]{1,0:T(8,128)S(1)}, u32[]{:S(2)}, u32[]{:S(2)}) %collective-permute-start.24) | collective-permute-done | bytes 32800 | tf_op jit(solution)/shard_map/ppermute | solution.py:1015
  87.4 3.8 %collective-permute-done.25 = f32[8,1024]{1,0:T(8,128)S(1)} collective-permute-done((f32[8,1024]{1,0:T(8,128)S(1)}, f32[8,1024]{1,0:T(8,128)S(1)}, u32[]{:S(2)}, u32[]{:S(2)}) %collective-permute-start.25) | collective-permute-done | bytes 32800 | tf_op jit(solution)/shard_map/ppermute | solution.py:1015
  93.1 6.8 %collective-permute-done.16.x_ref = bf16[4,64,1024]{2,1,0:T(8,128)(2,1)S(1)} collective-permute-done((bf16[4,64,1024]{2,1,0:T(8,128)(2,1)S(1)}, bf16[4,64,1024]{2,1,0:T(8,128)(2,1)S(1)}, u32[]{:S(2)}, u32[]{:S(2)}) %collective-permute-start.16) | collective-permute-done | bytes 524320 | tf_op jit(solution)/shard_map/ppermute | solution.py:1012
  100.6 1.5 %collective-permute-start.18 = (bf16[2,64,1024]{2,1,0:T(8,128)(2,1)S(1)}, bf16[2,64,1024]{2,1,0:T(8,128)(2,1)S(1)}, u32[]{:S(2)}, u32[]{:S(2)}) collective-permute-start(bf16[2,64,1024]{2,1,0:T(8,128)(2,1)S(1)} %get-tuple-element.71), channel_id=1, source_target_pairs={{0,8},{8,0},{16,24},{24,16},{1,9},{9,1},{17,25},{25,17},{2,10},{10... | collective-permute-start | bytes 786440 | tf_op jit(solution)/shard_map/ppermute | solution.py:1012
  102.7 2.9 %collective-permute-done.29.x_late_ref = bf16[2,64,1024]{2,1,0:T(8,128)(2,1)S(1)} collective-permute-done((bf16[2,64,1024]{2,1,0:T(8,128)(2,1)S(1)}, bf16[2,64,1024]{2,1,0:T(8,128)(2,1)S(1)}, u32[]{:S(2)}, u32[]{:S(2)}) %collective-permute-start.29) | collective-permute-done | bytes 262176 | tf_op jit(solution)/shard_map/ppermute | solution.py:1012
  112.0 2.5 %collective-permute-start.21 = (bf16[64,1024]{1,0:T(8,128)(2,1)S(1)}, bf16[64,1024]{1,0:T(8,128)(2,1)S(1)}, u32[]{:S(2)}, u32[]{:S(2)}) collective-permute-start(bf16[64,1024]{1,0:T(8,128)(2,1)S(1)} %get-tuple-element.75), channel_id=1, source_target_pairs={{0,4},{1,5},{2,6},{3,7},{4,0},{5,1},{6,2},{7,3},{8,12},{9,13},{10,... | collective-permute-start | bytes 393224 | tf_op jit(solution)/shard_map/ppermute | solution.py:1019
  114.7 9.6 %collective-permute-done.32.refs_2_ = bf16[64,1024]{1,0:T(8,128)(2,1)S(1)} collective-permute-done((bf16[64,1024]{1,0:T(8,128)(2,1)S(1)}, bf16[64,1024]{1,0:T(8,128)(2,1)S(1)}, u32[]{:S(2)}, u32[]{:S(2)}) %collective-permute-start.32) | collective-permute-done | bytes 131104 | tf_op jit(solution)/shard_map/ppermute | solution.py:1019
  125.2 1.5 %collective-permute-start.34 = (bf16[64,1024]{1,0:T(8,128)(2,1)S(1)}, bf16[64,1024]{1,0:T(8,128)(2,1)S(1)}, u32[]{:S(2)}, u32[]{:S(2)}) collective-permute-start(bf16[64,1024]{1,0:T(8,128)(2,1)S(1)} %collect.3.other_ref.refs_4_), channel_id=1, source_target_pairs={{0,8},{8,0},{16,24},{24,16},{1,9},{9,1},{17,25},{25,17},{2,10},{10... | collective-permute-start | bytes 393224 | tf_op jit(solution)/shard_map/ppermute | solution.py:1012
  128.1 1.9 %collective-permute-done.22.refs_3_ = bf16[64,1024]{1,0:T(8,128)(2,1)S(1)} collective-permute-done((bf16[64,1024]{1,0:T(8,128)(2,1)S(1)}, bf16[64,1024]{1,0:T(8,128)(2,1)S(1)}, u32[]{:S(2)}, u32[]{:S(2)}) %collective-permute-start.22) | collective-permute-done | bytes 131104 | tf_op jit(solution)/shard_map/ppermute | solution.py:1019
  135.3 7.4 %collective-permute-done.36.refs_1_ = bf16[80,1024]{1,0:T(8,128)(2,1)S(1)} collective-permute-done((bf16[80,1024]{1,0:T(8,128)(2,1)S(1)}, bf16[80,1024]{1,0:T(8,128)(2,1)S(1)}, u32[]{:S(2)}, u32[]{:S(2)}) %collective-permute-start.36) | collective-permute-done | bytes 163872 | tf_op jit(solution)/shard_map/ppermute | solution.py:1012
  142.9 1.7 %place.1 = (f32[1024,256]{1,0:T(8,128)}, f32[256,1024]{1,0:T(8,128)}, f32[1,1024]{1,0:T(1,128)}, f32[1,1024]{1,0:T(1,128)}, f32[1,1]{1,0:T(1,128)}) custom-call(s32[1]{0:T(128)} %bitcast.group_ref, bf16[80,1024]{1,0:T(8,128)(2,1)S(1)} %get-tuple-element.92.refs_0_, bf16[80,1024]{1,0:T(8,128)(2,1)S(1)} %collective-permute-done.36.refs_1_, ...), custom_call_target="tpu_custom_call" | custom-call | flops 1048576 | bytes 65536 | tf_op jit(solution)/shard_map/place/pallas_call | solution.py:978
  (100 shorter events, 33.3 us)
Async XLA Ops:
  3.1 20.5 %collective-permute-start = (bf16[2,64,1024]{2,1,0:T(8,128)(2,1)S(1)}, bf16[2,64,1024]{2,1,0:T(8,128)(2,1)S(1)}, u32[]{:S(2)}, u32[]{:S(2)}) collective-permute-start(bf16[2,64,1024]{2,1,0:T(8,128)(2,1)S(1)} %quarter.1), channel_id=1, source_target_pairs={{0,6},{1,7},{2,0},{3,1},{4,2},{5,3},{6,4},{7,5},{8,14},{9,15},{10,... | collective-permute-start | bytes 786440 | tf_op jit(solution)/shard_map/ppermute | solution.py:1019
  3.2 23.5 %collective-permute-start.3 = (bf16[2,64,1024]{2,1,0:T(8,128)(2,1)S(1)}, bf16[2,64,1024]{2,1,0:T(8,128)(2,1)S(1)}, u32[]{:S(2)}, u32[]{:S(2)}) collective-permute-start(bf16[2,64,1024]{2,1,0:T(8,128)(2,1)S(1)} %quarter.1), channel_id=1, source_target_pairs={{0,4},{1,5},{2,6},{3,7},{4,0},{5,1},{6,2},{7,3},{8,12},{9,13},{10,... | collective-permute-start | bytes 786440 | tf_op jit(solution)/shard_map/ppermute | solution.py:1019
  6.2 22.2 %collective-permute-start.4 = (bf16[2,64,1024]{2,1,0:T(8,128)(2,1)S(1)}, bf16[2,64,1024]{2,1,0:T(8,128)(2,1)S(1)}, u32[]{:S(2)}, u32[]{:S(2)}) collective-permute-start(bf16[2,64,1024]{2,1,0:T(8,128)(2,1)S(1)} %quarter.1), channel_id=1, source_target_pairs={{0,2},{1,3},{2,4},{3,5},{4,6},{5,7},{6,0},{7,1},{8,10},{9,11},{10,... | collective-permute-start | bytes 786440 | tf_op jit(solution)/shard_map/ppermute | solution.py:1019
  23.6 6.4 %collective-permute-start.2 = (bf16[1,2,64,1024]{3,2,1,0:T(8,128)(2,1)S(1)}, bf16[1,2,64,1024]{3,2,1,0:T(8,128)(2,1)S(1)}, u32[]{:S(2)}, u32[]{:S(2)}) collective-permute-start(bf16[1,2,64,1024]{3,2,1,0:T(8,128)(2,1)S(1)} %pack.4.refs_2_.refs_1_), channel_id=1, source_target_pairs={{0,16},{8,24},{16,0},{24,8},{1,17},{9,25},{17,1},{25,9},{2,18},{10... | collective-permute-start | bytes 786440 | tf_op jit(solution)/shard_map/ppermute | solution.py:1012
  25.2 7.5 %collective-permute-start.1 = (bf16[1,2,64,1024]{3,2,1,0:T(8,128)(2,1)S(1)}, bf16[1,2,64,1024]{3,2,1,0:T(8,128)(2,1)S(1)}, u32[]{:S(2)}, u32[]{:S(2)}) collective-permute-start(bf16[1,2,64,1024]{3,2,1,0:T(8,128)(2,1)S(1)} %pack.4.refs_2_.refs_1_), channel_id=1, source_target_pairs={{0,8},{8,0},{16,24},{24,16},{1,9},{9,1},{17,25},{25,17},{2,10},{10... | collective-permute-start | bytes 786440 | tf_op jit(solution)/shard_map/ppermute | solution.py:1012
  32.8 10.1 %collective-permute-start.5 = (bf16[2,2,64,1024]{3,2,1,0:T(8,128)(2,1)S(1)}, bf16[2,2,64,1024]{3,2,1,0:T(8,128)(2,1)S(1)}, u32[]{:S(2)}, u32[]{:S(2)}) collective-permute-start(bf16[2,2,64,1024]{3,2,1,0:T(8,128)(2,1)S(1)} %tie.1.refs_4_), channel_id=1, source_target_pairs={{0,8},{8,0},{16,24},{24,16},{1,9},{9,1},{17,25},{25,17},{2,10},{10... | collective-permute-start | bytes 1572872 | tf_op jit(solution)/shard_map/ppermute | solution.py:1012
  34.3 9.2 %collective-permute-start.6 = (bf16[2,2,64,1024]{3,2,1,0:T(8,128)(2,1)S(1)}, bf16[2,2,64,1024]{3,2,1,0:T(8,128)(2,1)S(1)}, u32[]{:S(2)}, u32[]{:S(2)}) collective-permute-start(bf16[2,2,64,1024]{3,2,1,0:T(8,128)(2,1)S(1)} %tie.1.refs_4_), channel_id=1, source_target_pairs={{0,16},{8,24},{16,0},{24,8},{1,17},{9,25},{17,1},{25,9},{2,18},{10... | collective-permute-start | bytes 1572872 | tf_op jit(solution)/shard_map/ppermute | solution.py:1012
  34.3 7.9 %collective-permute-start.7 = (bf16[2,64,1024]{2,1,0:T(8,128)(2,1)S(1)}, bf16[2,64,1024]{2,1,0:T(8,128)(2,1)S(1)}, u32[]{:S(2)}, u32[]{:S(2)}) collective-permute-start(bf16[2,64,1024]{2,1,0:T(8,128)(2,1)S(1)} %get-tuple-element.53), channel_id=1, source_target_pairs={{0,4},{1,5},{2,6},{3,7},{4,0},{5,1},{6,2},{7,3},{8,12},{9,13},{10,... | collective-permute-start | bytes 786440 | tf_op jit(solution)/shard_map/ppermute | solution.py:1019
  43.7 7.3 %collective-permute-start.10 = (bf16[13,2,64,1024]{3,2,1,0:T(8,128)(2,1)S(1)}, bf16[13,2,64,1024]{3,2,1,0:T(8,128)(2,1)S(1)}, u32[]{:S(2)}, u32[]{:S(2)}) collective-permute-start(bf16[13,2,64,1024]{3,2,1,0:T(8,128)(2,1)S(1)} %pack.6.refs_1_.refs_0_), channel_id=1, source_target_pairs={{0,1},{1,0},{2,3},{3,2},{4,5},{5,4},{6,7},{7,6},{8,9},{9,8},{10,11... | collective-permute-start | bytes 10223624 | tf_op jit(solution)/shard_map/ppermute | solution.py:1015
  43.7 17.2 %collective-permute-start.9 = (bf16[2,2,64,1024]{3,2,1,0:T(8,128)(2,1)S(1)}, bf16[2,2,64,1024]{3,2,1,0:T(8,128)(2,1)S(1)}, u32[]{:S(2)}, u32[]{:S(2)}) collective-permute-start(bf16[2,2,64,1024]{3,2,1,0:T(8,128)(2,1)S(1)} %collective-permute-done.5.refs_5_), channel_id=1, source_target_pairs={{0,16},{8,24},{16,0},{24,8},{1,17},{9,25},{17,1},{25,9},{2,18},{10... | collective-permute-start | bytes 1572872 | tf_op jit(solution)/shard_map/ppermute | solution.py:1012
  44.7 14.0 %collective-permute-start.11 = (bf16[2,64,1024]{2,1,0:T(8,128)(2,1)S(1)}, bf16[2,64,1024]{2,1,0:T(8,128)(2,1)S(1)}, u32[]{:S(2)}, u32[]{:S(2)}) collective-permute-start(bf16[2,64,1024]{2,1,0:T(8,128)(2,1)S(1)} %get-tuple-element.56), channel_id=1, source_target_pairs={{0,2},{1,3},{2,4},{3,5},{4,6},{5,7},{6,0},{7,1},{8,10},{9,11},{10,... | collective-permute-start | bytes 786440 | tf_op jit(solution)/shard_map/ppermute | solution.py:1019
  47.2 13.7 %collective-permute-start.12 = (bf16[2,64,1024]{2,1,0:T(8,128)(2,1)S(1)}, bf16[2,64,1024]{2,1,0:T(8,128)(2,1)S(1)}, u32[]{:S(2)}, u32[]{:S(2)}) collective-permute-start(bf16[2,64,1024]{2,1,0:T(8,128)(2,1)S(1)} %get-tuple-element.57), channel_id=1, source_target_pairs={{0,6},{1,7},{2,0},{3,1},{4,2},{5,3},{6,4},{7,5},{8,14},{9,15},{10,... | collective-permute-start | bytes 786440 | tf_op jit(solution)/shard_map/ppermute | solution.py:1019
  47.2 13.7 %collective-permute-start.8 = (bf16[1,2,64,1024]{3,2,1,0:T(8,128)(2,1)S(1)}, bf16[1,2,64,1024]{3,2,1,0:T(8,128)(2,1)S(1)}, u32[]{:S(2)}, u32[]{:S(2)}) collective-permute-start(bf16[1,2,64,1024]{3,2,1,0:T(8,128)(2,1)S(1)} %collective-permute-done.2.refs_2_.refs_3_), channel_id=1, source_target_pairs={{0,8},{8,0},{16,24},{24,16},{1,9},{9,1},{17,25},{25,17},{2,10},{10... | collective-permute-start | bytes 786440 | tf_op jit(solution)/shard_map/ppermute | solution.py:1012
  73.9 17.4 %collective-permute-start.27 = (bf16[4,64,1024]{2,1,0:T(8,128)(2,1)S(1)}, bf16[4,64,1024]{2,1,0:T(8,128)(2,1)S(1)}, u32[]{:S(2)}, u32[]{:S(2)}) collective-permute-start(bf16[4,64,1024]{2,1,0:T(8,128)(2,1)S(1)} %get-tuple-element.82), channel_id=1, source_target_pairs={{0,8},{8,0},{16,24},{24,16},{1,9},{9,1},{17,25},{25,17},{2,10},{10... | collective-permute-start | bytes 1572872 | tf_op jit(solution)/shard_map/ppermute | solution.py:1012
  74.5 16.8 %collective-permute-start.28 = (bf16[4,64,1024]{2,1,0:T(8,128)(2,1)S(1)}, bf16[4,64,1024]{2,1,0:T(8,128)(2,1)S(1)}, u32[]{:S(2)}, u32[]{:S(2)}) collective-permute-start(bf16[4,64,1024]{2,1,0:T(8,128)(2,1)S(1)} %get-tuple-element.83), channel_id=1, source_target_pairs={{0,16},{8,24},{16,0},{24,8},{1,17},{9,25},{17,1},{25,9},{2,18},{10... | collective-permute-start | bytes 1572872 | tf_op jit(solution)/shard_map/ppermute | solution.py:1012
  78.8 21.1 %collective-permute-start.16 = (bf16[4,64,1024]{2,1,0:T(8,128)(2,1)S(1)}, bf16[4,64,1024]{2,1,0:T(8,128)(2,1)S(1)}, u32[]{:S(2)}, u32[]{:S(2)}) collective-permute-start(bf16[4,64,1024]{2,1,0:T(8,128)(2,1)S(1)} %get-tuple-element.67), channel_id=1, source_target_pairs={{0,8},{8,0},{16,24},{24,16},{1,9},{9,1},{17,25},{25,17},{2,10},{10... | collective-permute-start | bytes 1572872 | tf_op jit(solution)/shard_map/ppermute | solution.py:1012
  79.8 20.7 %collective-permute-start.17 = (bf16[4,64,1024]{2,1,0:T(8,128)(2,1)S(1)}, bf16[4,64,1024]{2,1,0:T(8,128)(2,1)S(1)}, u32[]{:S(2)}, u32[]{:S(2)}) collective-permute-start(bf16[4,64,1024]{2,1,0:T(8,128)(2,1)S(1)} %get-tuple-element.68), channel_id=1, source_target_pairs={{0,16},{8,24},{16,0},{24,8},{1,17},{9,25},{17,1},{25,9},{2,18},{10... | collective-permute-start | bytes 1572872 | tf_op jit(solution)/shard_map/ppermute | solution.py:1012
  91.4 14.1 %collective-permute-start.29 = (bf16[2,64,1024]{2,1,0:T(8,128)(2,1)S(1)}, bf16[2,64,1024]{2,1,0:T(8,128)(2,1)S(1)}, u32[]{:S(2)}, u32[]{:S(2)}) collective-permute-start(bf16[2,64,1024]{2,1,0:T(8,128)(2,1)S(1)} %get-tuple-element.86), channel_id=1, source_target_pairs={{0,8},{8,0},{16,24},{24,16},{1,9},{9,1},{17,25},{25,17},{2,10},{10... | collective-permute-start | bytes 786440 | tf_op jit(solution)/shard_map/ppermute | solution.py:1012
  92.0 14.1 %collective-permute-start.30 = (bf16[2,64,1024]{2,1,0:T(8,128)(2,1)S(1)}, bf16[2,64,1024]{2,1,0:T(8,128)(2,1)S(1)}, u32[]{:S(2)}, u32[]{:S(2)}) collective-permute-start(bf16[2,64,1024]{2,1,0:T(8,128)(2,1)S(1)} %get-tuple-element.87), channel_id=1, source_target_pairs={{0,16},{8,24},{16,0},{24,8},{1,17},{9,25},{17,1},{25,9},{2,18},{10... | collective-permute-start | bytes 786440 | tf_op jit(solution)/shard_map/ppermute | solution.py:1012
  100.6 9.7 %collective-permute-start.18 = (bf16[2,64,1024]{2,1,0:T(8,128)(2,1)S(1)}, bf16[2,64,1024]{2,1,0:T(8,128)(2,1)S(1)}, u32[]{:S(2)}, u32[]{:S(2)}) collective-permute-start(bf16[2,64,1024]{2,1,0:T(8,128)(2,1)S(1)} %get-tuple-element.71), channel_id=1, source_target_pairs={{0,8},{8,0},{16,24},{24,16},{1,9},{9,1},{17,25},{25,17},{2,10},{10... | collective-permute-start | bytes 786440 | tf_op jit(solution)/shard_map/ppermute | solution.py:1012
  102.2 8.4 %collective-permute-start.19 = (bf16[2,64,1024]{2,1,0:T(8,128)(2,1)S(1)}, bf16[2,64,1024]{2,1,0:T(8,128)(2,1)S(1)}, u32[]{:S(2)}, u32[]{:S(2)}) collective-permute-start(bf16[2,64,1024]{2,1,0:T(8,128)(2,1)S(1)} %get-tuple-element.72), channel_id=1, source_target_pairs={{0,16},{8,24},{16,0},{24,8},{1,17},{9,25},{17,1},{25,9},{2,18},{10... | collective-permute-start | bytes 786440 | tf_op jit(solution)/shard_map/ppermute | solution.py:1012
  106.3 8.2 %collective-permute-start.31 = (bf16[64,1024]{1,0:T(8,128)(2,1)S(1)}, bf16[64,1024]{1,0:T(8,128)(2,1)S(1)}, u32[]{:S(2)}, u32[]{:S(2)}) collective-permute-start(bf16[64,1024]{1,0:T(8,128)(2,1)S(1)} %get-tuple-element.89), channel_id=1, source_target_pairs={{0,2},{1,3},{2,4},{3,5},{4,6},{5,7},{6,0},{7,1},{8,10},{9,11},{10,... | collective-permute-start | bytes 393224 | tf_op jit(solution)/shard_map/ppermute | solution.py:1019
  107.5 16.8 %collective-permute-start.32 = (bf16[64,1024]{1,0:T(8,128)(2,1)S(1)}, bf16[64,1024]{1,0:T(8,128)(2,1)S(1)}, u32[]{:S(2)}, u32[]{:S(2)}) collective-permute-start(bf16[64,1024]{1,0:T(8,128)(2,1)S(1)} %get-tuple-element.90), channel_id=1, source_target_pairs={{0,4},{1,5},{2,6},{3,7},{4,0},{5,1},{6,2},{7,3},{8,12},{9,13},{10,... | collective-permute-start | bytes 393224 | tf_op jit(solution)/shard_map/ppermute | solution.py:1019
  109.0 16.1 %collective-permute-start.33 = (bf16[64,1024]{1,0:T(8,128)(2,1)S(1)}, bf16[64,1024]{1,0:T(8,128)(2,1)S(1)}, u32[]{:S(2)}, u32[]{:S(2)}) collective-permute-start(bf16[64,1024]{1,0:T(8,128)(2,1)S(1)} %get-tuple-element.91), channel_id=1, source_target_pairs={{0,6},{1,7},{2,0},{3,1},{4,2},{5,3},{6,4},{7,5},{8,14},{9,15},{10,... | collective-permute-start | bytes 393224 | tf_op jit(solution)/shard_map/ppermute | solution.py:1019
  110.8 16.8 %collective-permute-start.20 = (bf16[64,1024]{1,0:T(8,128)(2,1)S(1)}, bf16[64,1024]{1,0:T(8,128)(2,1)S(1)}, u32[]{:S(2)}, u32[]{:S(2)}) collective-permute-start(bf16[64,1024]{1,0:T(8,128)(2,1)S(1)} %get-tuple-element.74), channel_id=1, source_target_pairs={{0,2},{1,3},{2,4},{3,5},{4,6},{5,7},{6,0},{7,1},{8,10},{9,11},{10,... | collective-permute-start | bytes 393224 | tf_op jit(solution)/shard_map/ppermute | solution.py:1019
  112.0 16.0 %collective-permute-start.21 = (bf16[64,1024]{1,0:T(8,128)(2,1)S(1)}, bf16[64,1024]{1,0:T(8,128)(2,1)S(1)}, u32[]{:S(2)}, u32[]{:S(2)}) collective-permute-start(bf16[64,1024]{1,0:T(8,128)(2,1)S(1)} %get-tuple-element.75), channel_id=1, source_target_pairs={{0,4},{1,5},{2,6},{3,7},{4,0},{5,1},{6,2},{7,3},{8,12},{9,13},{10,... | collective-permute-start | bytes 393224 | tf_op jit(solution)/shard_map/ppermute | solution.py:1019
  114.6 15.5 %collective-permute-start.22 = (bf16[64,1024]{1,0:T(8,128)(2,1)S(1)}, bf16[64,1024]{1,0:T(8,128)(2,1)S(1)}, u32[]{:S(2)}, u32[]{:S(2)}) collective-permute-start(bf16[64,1024]{1,0:T(8,128)(2,1)S(1)} %get-tuple-element.76), channel_id=1, source_target_pairs={{0,6},{1,7},{2,0},{3,1},{4,2},{5,3},{6,4},{7,5},{8,14},{9,15},{10,... | collective-permute-start | bytes 393224 | tf_op jit(solution)/shard_map/ppermute | solution.py:1019
  125.2 5.0 %collective-permute-start.34 = (bf16[64,1024]{1,0:T(8,128)(2,1)S(1)}, bf16[64,1024]{1,0:T(8,128)(2,1)S(1)}, u32[]{:S(2)}, u32[]{:S(2)}) collective-permute-start(bf16[64,1024]{1,0:T(8,128)(2,1)S(1)} %collect.3.other_ref.refs_4_), channel_id=1, source_target_pairs={{0,8},{8,0},{16,24},{24,16},{1,9},{9,1},{17,25},{25,17},{2,10},{10... | collective-permute-start | bytes 393224 | tf_op jit(solution)/shard_map/ppermute | solution.py:1012
  126.8 5.0 %collective-permute-start.35 = (bf16[64,1024]{1,0:T(8,128)(2,1)S(1)}, bf16[64,1024]{1,0:T(8,128)(2,1)S(1)}, u32[]{:S(2)}, u32[]{:S(2)}) collective-permute-start(bf16[64,1024]{1,0:T(8,128)(2,1)S(1)} %collect.3.other_ref.refs_4_), channel_id=1, source_target_pairs={{0,16},{8,24},{16,0},{24,8},{1,17},{9,25},{17,1},{25,9},{2,18},{10... | collective-permute-start | bytes 393224 | tf_op jit(solution)/shard_map/ppermute | solution.py:1012
  131.8 11.2 %collective-permute-start.38 = (bf16[144,1024]{1,0:T(8,128)(2,1)S(1)}, bf16[144,1024]{1,0:T(8,128)(2,1)S(1)}, u32[]{:S(2)}, u32[]{:S(2)}) collective-permute-start(bf16[144,1024]{1,0:T(8,128)(2,1)S(1)} %get-tuple-element.93), channel_id=1, source_target_pairs={{0,24},{8,16},{16,8},{24,0},{1,25},{9,17},{17,9},{25,1},{2,26},{10... | collective-permute-start | bytes 884744 | tf_op jit(solution)/shard_map/ppermute | solution.py:1012
  132.7 10.0 %collective-permute-start.36 = (bf16[80,1024]{1,0:T(8,128)(2,1)S(1)}, bf16[80,1024]{1,0:T(8,128)(2,1)S(1)}, u32[]{:S(2)}, u32[]{:S(2)}) collective-permute-start(bf16[80,1024]{1,0:T(8,128)(2,1)S(1)} %get-tuple-element.92.refs_0_), channel_id=1, source_target_pairs={{0,8},{8,0},{16,24},{24,16},{1,9},{9,1},{17,25},{25,17},{2,10},{10... | collective-permute-start | bytes 491528 | tf_op jit(solution)/shard_map/ppermute | solution.py:1012
  134.2 8.7 %collective-permute-start.37 = (bf16[80,1024]{1,0:T(8,128)(2,1)S(1)}, bf16[80,1024]{1,0:T(8,128)(2,1)S(1)}, u32[]{:S(2)}, u32[]{:S(2)}) collective-permute-start(bf16[80,1024]{1,0:T(8,128)(2,1)S(1)} %get-tuple-element.92.refs_0_), channel_id=1, source_target_pairs={{0,16},{8,24},{16,0},{24,8},{1,17},{9,25},{17,1},{25,9},{2,18},{10... | collective-permute-start | bytes 491528 | tf_op jit(solution)/shard_map/ppermute | solution.py:1012
  (20 other events, 126.3 us)

commit v15 on v14

--- a/solution.py
+++ b/solution.py
@@ -1027,20 +1027,24 @@
     half = depth // 2
     low = pack(arrivals[:half - 1], rendered[0])
     x_low, y_low = beside(low, 1), beside(low, 2)
-    high = pack(arrivals[half - 1:], low)
-    high = tie(high, x_low, y_low)
-    x_high, y_high = beside(high, 1), beside(high, 2)
+    high, x_high, y_high, last_sent = [], [], [], (x_low, y_low)
+    for arrival in arrivals[half - 1:]:
+        arrival = tie(arrival, *last_sent)
+        last_sent = (arrival,)
+        high.append(arrival)
+        x_high.append(beside(arrival, 1))
+        y_high.append(beside(arrival, 2))
     targets = [rendered[0]] + [along(rendered[shift], shift) for shift in range(1, depth)]
     tokens, normed, normed_t = prepare_tokens(
         ray_count, True, me, block_owner, ray_pixel, image_tokens,
         layer_norm_gain.reshape(1, width),
     )
     most = pack(
-        [own_rows(group, up_weight, down_weight), low, x_low, y_low, high, x_high, y_high],
-        targets[half],
+        [own_rows(group, up_weight, down_weight), low, x_low, y_low, *high, *x_high, *y_high],
+        targets[half], normed,
     )
     most_other = partner(most)
-    d_low, d_high = beside(y_low, 1), beside(x_high, 2)
+    d_low, d_high = beside(y_low, 1), beside(pack(x_high), 2)
     act_most, slope_most, mixed = forward(normed_t, [most], [most_other])
     late = [target for shift, target in enumerate(targets) if shift not in (0, half)]
     last = pack([d_low, d_high], mixed, *late)

time: 147 us -> 151 us (1.027)
  starting transfers between devices: 37 us -> 40.1 us
  waiting for transfers between devices: 72.8 us -> 75.3 us
    ppermute x19 -> x21, starting transfers between devices: 19.4 us -> 22.2 us  [beside(): lax.ppermute(array, 'grp', [(g, g ^ flip) for g in range(group_count)])]
    ppermute x12, waiting for transfers between devices: 33.4 us -> 35.7 us  [along(): return lax.ppermute(array, 'ray', pairs)]
    ppermute x19 -> x21, waiting for transfers between devices: 26.9 us -> 26.8 us  [beside(): lax.ppermute(array, 'grp', [(g, g ^ flip) for g in range(group_count)])]
  transfers between devices with their start and end apart: 39 -> 41, of which waited for: 29 -> 29; matrix products, arithmetic and copies ran while one was open for 0% -> 0% of each run, Pallas kernels for 17% -> 17%
where the time goes in v15:
time: 151 us; the launch traced here: 150 us
  waiting for transfers between devices  75.3 us (50%)
  starting transfers between devices  40.1 us (27%)
  Pallas kernels  31.6 us (21%)
  local copies, waits for them, and re-layouts  2.13 us (1%)
    ppermute x12, waiting for transfers between devices, along(): return lax.ppermute(array, 'ray', pairs)  35.7 us
    ppermute x21, waiting for transfers between devices, beside(): lax.ppermute(array, 'grp', [(g, g ^ flip) for g in range(group_count)])  26.8 us
    ppermute x21, starting transfers between devices, beside(): lax.ppermute(array, 'grp', [(g, g ^ flip) for g in range(group_count)])  22.2 us
    ppermute x12, starting transfers between devices, along(): return lax.ppermute(array, 'ray', pairs)  14.1 us
    ppermute x8, waiting for transfers between devices, partner(): return lax.ppermute(array, 'ray', [(r, r ^ flip) for r in range(ray_count)])  12.8 us
    pallas_call x1, Pallas kernels, render(): pl.pallas_call(functools.partial(render_kernel, ray_count, relative), out...  8.41 us
    pallas_call x2, Pallas kernels, forward(): pl.pallas_call(functools.partial(forward_kernel, first, blocks, len(own),...  7.9 us
    pallas_call x2, Pallas kernels, up_gradient(): pl.pallas_call(functools.partial(up_grad_kernel, side, weight_pieces, act...  6.09 us
  transfers between devices with their start and end apart: 41, of which 29 were waited for; matrix products, arithmetic and copies ran while one was open for 0% of the time, Pallas kernels for 17%

profile of v15, /device:TPU:8, one launch (start us, length us, event | category | flops | bytes accessed | tf_op | source)
XLA Modules:
  0.0 150.1 jit_solution(13396956628746976467)
XLA Ops:
  3.2 3.0 %collective-permute-start.3 = (bf16[2,64,1024]{2,1,0:T(8,128)(2,1)S(1)}, bf16[2,64,1024]{2,1,0:T(8,128)(2,1)S(1)}, u32[]{:S(2)}, u32[]{:S(2)}) collective-permute-start(bf16[2,64,1024]{2,1,0:T(8,128)(2,1)S(1)} %quarter.1), channel_id=1, source_target_pairs={{0,4},{1,5},{2,6},{3,7},{4,0},{5,1},{6,2},{7,3},{8,12},{9,13},{10,... | collective-permute-start | bytes 786440 | tf_op jit(solution)/shard_map/ppermute | solution.py:1019
  6.3 8.4 %render.1 = (bf16[2,64,1024]{2,1,0:T(8,128)(2,1)S(1)}, bf16[2,64,1024]{2,1,0:T(8,128)(2,1)S(1)}, bf16[2,64,1024]{2,1,0:T(8,128)(2,1)S(1)}, bf16[2,64,1024]{2,1,0:T(8,128)(2,1)S(1)}) custom-call(s32[1]{0:T(128)} %bitcast.1.me_ref, s32[1,8]{1,0:T(1,128)S(1)} %copy-done.11, s32[32,512]{1,0:T(8,128)S(1)} %copy-done.7, f32[32,512]{1,0:T(8,128)S(1)} %copy-done.8, ...), custom_call_target="tpu_custom_call" | custom-call | flops 1048576 | bytes 65536 | tf_op jit(solution)/shard_map/render/pallas_call | solution.py:152
  14.7 3.3 %collective-permute-done.refs_0_ = bf16[2,64,1024]{2,1,0:T(8,128)(2,1)S(1)} collective-permute-done((bf16[2,64,1024]{2,1,0:T(8,128)(2,1)S(1)}, bf16[2,64,1024]{2,1,0:T(8,128)(2,1)S(1)}, u32[]{:S(2)}, u32[]{:S(2)}) %collective-permute-start) | collective-permute-done | bytes 262176 | tf_op jit(solution)/shard_map/ppermute | solution.py:1019
  18.1 1.6 %collective-permute-start.2 = (bf16[1,2,64,1024]{3,2,1,0:T(8,128)(2,1)S(1)}, bf16[1,2,64,1024]{3,2,1,0:T(8,128)(2,1)S(1)}, u32[]{:S(2)}, u32[]{:S(2)}) collective-permute-start(bf16[1,2,64,1024]{3,2,1,0:T(8,128)(2,1)S(1)} %pack.4.refs_1_), channel_id=1, source_target_pairs={{0,16},{8,24},{16,0},{24,8},{1,17},{9,25},{17,1},{25,9},{2,18},{10... | collective-permute-start | bytes 786440 | tf_op jit(solution)/shard_map/ppermute | solution.py:1012
  21.2 5.2 %collective-permute-done.3.refs_0_ = bf16[2,64,1024]{2,1,0:T(8,128)(2,1)S(1)} collective-permute-done((bf16[2,64,1024]{2,1,0:T(8,128)(2,1)S(1)}, bf16[2,64,1024]{2,1,0:T(8,128)(2,1)S(1)}, u32[]{:S(2)}, u32[]{:S(2)}) %collective-permute-start.3) | collective-permute-done | bytes 262176 | tf_op jit(solution)/shard_map/ppermute | solution.py:1019
  26.5 8.4 %collective-permute-done.4.refs_0_ = bf16[2,64,1024]{2,1,0:T(8,128)(2,1)S(1)} collective-permute-done((bf16[2,64,1024]{2,1,0:T(8,128)(2,1)S(1)}, bf16[2,64,1024]{2,1,0:T(8,128)(2,1)S(1)}, u32[]{:S(2)}, u32[]{:S(2)}) %collective-permute-start.4) | collective-permute-done | bytes 262176 | tf_op jit(solution)/shard_map/ppermute | solution.py:1019
  36.4 1.5 %collective-permute-start.8 = (bf16[2,64,1024]{2,1,0:T(8,128)(2,1)S(1)}, bf16[2,64,1024]{2,1,0:T(8,128)(2,1)S(1)}, u32[]{:S(2)}, u32[]{:S(2)}) collective-permute-start(bf16[2,64,1024]{2,1,0:T(8,128)(2,1)S(1)} %tie.3.refs_5_), channel_id=1, source_target_pairs={{0,16},{8,24},{16,0},{24,8},{1,17},{9,25},{17,1},{25,9},{2,18},{10... | collective-permute-start | bytes 786440 | tf_op jit(solution)/shard_map/ppermute | solution.py:1012
  39.2 3.1 %tokens.1 = (bf16[512,1024]{1,0:T(8,128)(2,1)S(1)}, bf16[512,1024]{1,0:T(8,128)(2,1)S(1)}, bf16[1024,512]{1,0:T(8,128)(2,1)S(1)}) custom-call(s32[1]{0:T(128)} %bitcast.1.me_ref, s32[1,8]{1,0:T(1,128)S(1)} %copy-done.11, s32[1,4096]{1,0:T(1,128)S(1)} %copy-done.6, bf16[512,1024]{1,0:T(8,128)(2,1)S(1)} %copy-done.1, f32[1,1024]{1,0:T(1,128)S(1)} %bitcast.8), custom_call_target="tpu_custom_call" | custom-call | flops 1048576 | bytes 65536 | tf_op jit(solution)/shard_map/tokens/pallas_call | solution.py:238
  42.3 1.8 %collective-permute-done.6.refs_7_.refs_1_ = bf16[2,64,1024]{2,1,0:T(8,128)(2,1)S(1)} collective-permute-done((bf16[2,64,1024]{2,1,0:T(8,128)(2,1)S(1)}, bf16[2,64,1024]{2,1,0:T(8,128)(2,1)S(1)}, u32[]{:S(2)}, u32[]{:S(2)}) %collective-permute-start.6) | collective-permute-done | bytes 262176 | tf_op jit(solution)/shard_map/ppermute | solution.py:1012
  45.5 1.6 %collective-permute-done.5.refs_6_.refs_0_ = bf16[2,64,1024]{2,1,0:T(8,128)(2,1)S(1)} collective-permute-done((bf16[2,64,1024]{2,1,0:T(8,128)(2,1)S(1)}, bf16[2,64,1024]{2,1,0:T(8,128)(2,1)S(1)}, u32[]{:S(2)}, u32[]{:S(2)}) %collective-permute-start.5) | collective-permute-done | bytes 262176 | tf_op jit(solution)/shard_map/ppermute | solution.py:1012
  48.7 1.6 %collective-permute-start.11 = (bf16[2,2,64,1024]{3,2,1,0:T(8,128)(2,1)S(1)}, bf16[2,2,64,1024]{3,2,1,0:T(8,128)(2,1)S(1)}, u32[]{:S(2)}, u32[]{:S(2)}) collective-permute-start(bf16[2,2,64,1024]{3,2,1,0:T(8,128)(2,1)S(1)} %pack.6), channel_id=1, source_target_pairs={{0,16},{8,24},{16,0},{24,8},{1,17},{9,25},{17,1},{25,9},{2,18},{10... | collective-permute-start | bytes 1572872 | tf_op jit(solution)/shard_map/ppermute | solution.py:1012
  50.2 2.5 %collective-permute-start.13 = (bf16[2,64,1024]{2,1,0:T(8,128)(2,1)S(1)}, bf16[2,64,1024]{2,1,0:T(8,128)(2,1)S(1)}, u32[]{:S(2)}, u32[]{:S(2)}) collective-permute-start(bf16[2,64,1024]{2,1,0:T(8,128)(2,1)S(1)} %get-tuple-element.57), channel_id=1, source_target_pairs={{0,2},{1,3},{2,4},{3,5},{4,6},{5,7},{6,0},{7,1},{8,10},{9,11},{10,... | collective-permute-start | bytes 786440 | tf_op jit(solution)/shard_map/ppermute | solution.py:1019
  54.6 5.0 %forward.2 = (bf16[2,13,64,512]{3,2,1,0:T(8,128)(2,1)S(1)}, f32[2,13,64,512]{3,2,1,0:T(8,128)S(1)}, f32[512,1024]{1,0:T(8,128)S(1)}) custom-call(bf16[1024,512]{1,0:T(8,128)(2,1)S(1)} %get-tuple-element.55.refs_0_, bf16[13,2,64,1024]{3,2,1,0:T(8,128)(2,1)S(1)} %pack.5.refs_1_.refs_0_, bf16[13,2,64,1024]{3,2,1,0:T(8,128)(2,1)S(1)} %collective-permute-done.12.refs_2_.refs_0_), custom_call_target="tpu_custom_call" | custom-call | flops 1048576 | bytes 65536 | tf_op jit(solution)/shard_map/forward/pallas_call | solution.py:652
  59.6 4.6 %collective-permute-done.13.refs_3_.refs_1_.refs_7_ = bf16[2,64,1024]{2,1,0:T(8,128)(2,1)S(1)} collective-permute-done((bf16[2,64,1024]{2,1,0:T(8,128)(2,1)S(1)}, bf16[2,64,1024]{2,1,0:T(8,128)(2,1)S(1)}, u32[]{:S(2)}, u32[]{:S(2)}) %collective-permute-start.13) | collective-permute-done | bytes 262176 | tf_op jit(solution)/shard_map/ppermute | solution.py:1019
  66.3 2.4 %collective-permute-done.16.refs_10_ = bf16[4,64,1024]{2,1,0:T(8,128)(2,1)S(1)} collective-permute-done((bf16[4,64,1024]{2,1,0:T(8,128)(2,1)S(1)}, bf16[4,64,1024]{2,1,0:T(8,128)(2,1)S(1)}, u32[]{:S(2)}, u32[]{:S(2)}) %collective-permute-start.16) | collective-permute-done | bytes 524320 | tf_op jit(solution)/shard_map/ppermute | solution.py:1015
  68.8 2.9 %forward.3 = (bf16[2,3,64,512]{3,2,1,0:T(8,128)(2,1)S(1)}, f32[2,3,64,512]{3,2,1,0:T(8,128)S(1)}, bf16[512,1024]{1,0:T(8,128)(2,1)S(1)}, bf16[1024,512]{1,0:T(8,128)(2,1)S(1)}, f32[8,1024]{1,0:T(8,128)S(1)}) custom-call(bf16[1024,512]{1,0:T(8,128)(2,1)S(1)} %get-tuple-element.55.refs_0_, bf16[3,2,64,1024]{3,2,1,0:T(8,128)(2,1)S(1)} %pack.7.refs_1_, ...), custom_call_target="tpu_custom_call" | custom-call | flops 1048576 | bytes 65536 | tf_op jit(solution)/shard_map/forward/pallas_call | solution.py:652
  73.2 2.8 %up_gradient.2 = (bf16[4,4,64,1024]{3,2,1,0:T(8,128)(2,1)S(1)}, f32[1,1024]{1,0:T(1,128)S(1)}) custom-call(bf16[13,2,64,1024]{3,2,1,0:T(8,128)(2,1)S(1)} %collective-permute-done.12.refs_2_.refs_0_, bf16[3,2,64,1024]{3,2,1,0:T(8,128)(2,1)S(1)} %collective-permute-done.15.refs_2_.refs_1_, f32[2,13,64,512]{3,2,1,0:T(8,128)S(1)} %get-tuple-element.59.refs_2_, ...), custom_call_target="tpu_custom_call" | custom-call | flops 1048576 | bytes 65536 | tf_op jit(solution)/shard_map/up_gradient/pallas_call | solution.py:844
  80.2 3.3 %up_gradient.3 = (bf16[4,64,1024]{2,1,0:T(8,128)(2,1)S(1)}, bf16[4,64,1024]{2,1,0:T(8,128)(2,1)S(1)}, bf16[4,64,1024]{2,1,0:T(8,128)(2,1)S(1)}, bf16[2,64,1024]{...) custom-call(bf16[13,2,64,1024]{3,2,1,0:T(8,128)(2,1)S(1)} %pack.5.refs_1_.refs_0_, ...), custom_call_target="tpu_custom_call" | custom-call | flops 1048576 | bytes 65536 | tf_op jit(solution)/shard_map/up_gradient/pallas_call | solution.py:844
  84.5 1.5 %collective-permute-start.19 = (bf16[4,64,1024]{2,1,0:T(8,128)(2,1)S(1)}, bf16[4,64,1024]{2,1,0:T(8,128)(2,1)S(1)}, u32[]{:S(2)}, u32[]{:S(2)}) collective-permute-start(bf16[4,64,1024]{2,1,0:T(8,128)(2,1)S(1)} %get-tuple-element.68), channel_id=1, source_target_pairs={{0,16},{8,24},{16,0},{24,8},{1,17},{9,25},{17,1},{25,9},{2,18},{10... | collective-permute-start | bytes 1572872 | tf_op jit(solution)/shard_map/ppermute | solution.py:1012
  88.4 2.7 %collective-permute-done.26 = f32[8,1024]{1,0:T(8,128)S(1)} collective-permute-done((f32[8,1024]{1,0:T(8,128)S(1)}, f32[8,1024]{1,0:T(8,128)S(1)}, u32[]{:S(2)}, u32[]{:S(2)}) %collective-permute-start.26) | collective-permute-done | bytes 32800 | tf_op jit(solution)/shard_map/ppermute | solution.py:1015
  92.3 3.7 %collective-permute-done.27 = f32[8,1024]{1,0:T(8,128)S(1)} collective-permute-done((f32[8,1024]{1,0:T(8,128)S(1)}, f32[8,1024]{1,0:T(8,128)S(1)}, u32[]{:S(2)}, u32[]{:S(2)}) %collective-permute-start.27) | collective-permute-done | bytes 32800 | tf_op jit(solution)/shard_map/ppermute | solution.py:1015
  97.9 6.7 %collective-permute-done.18.x_ref = bf16[4,64,1024]{2,1,0:T(8,128)(2,1)S(1)} collective-permute-done((bf16[4,64,1024]{2,1,0:T(8,128)(2,1)S(1)}, bf16[4,64,1024]{2,1,0:T(8,128)(2,1)S(1)}, u32[]{:S(2)}, u32[]{:S(2)}) %collective-permute-start.18) | collective-permute-done | bytes 524320 | tf_op jit(solution)/shard_map/ppermute | solution.py:1012
  105.3 1.5 %collective-permute-start.20 = (bf16[2,64,1024]{2,1,0:T(8,128)(2,1)S(1)}, bf16[2,64,1024]{2,1,0:T(8,128)(2,1)S(1)}, u32[]{:S(2)}, u32[]{:S(2)}) collective-permute-start(bf16[2,64,1024]{2,1,0:T(8,128)(2,1)S(1)} %get-tuple-element.71), channel_id=1, source_target_pairs={{0,8},{8,0},{16,24},{24,16},{1,9},{9,1},{17,25},{25,17},{2,10},{10... | collective-permute-start | bytes 786440 | tf_op jit(solution)/shard_map/ppermute | solution.py:1012
  107.4 2.8 %collective-permute-done.31.x_late_ref = bf16[2,64,1024]{2,1,0:T(8,128)(2,1)S(1)} collective-permute-done((bf16[2,64,1024]{2,1,0:T(8,128)(2,1)S(1)}, bf16[2,64,1024]{2,1,0:T(8,128)(2,1)S(1)}, u32[]{:S(2)}, u32[]{:S(2)}) %collective-permute-start.31) | collective-permute-done | bytes 262176 | tf_op jit(solution)/shard_map/ppermute | solution.py:1012
  112.2 2.4 %collective-permute-start.34 = (bf16[64,1024]{1,0:T(8,128)(2,1)S(1)}, bf16[64,1024]{1,0:T(8,128)(2,1)S(1)}, u32[]{:S(2)}, u32[]{:S(2)}) collective-permute-start(bf16[64,1024]{1,0:T(8,128)(2,1)S(1)} %get-tuple-element.90), channel_id=1, source_target_pairs={{0,4},{1,5},{2,6},{3,7},{4,0},{5,1},{6,2},{7,3},{8,12},{9,13},{10,... | collective-permute-start | bytes 393224 | tf_op jit(solution)/shard_map/ppermute | solution.py:1019
  116.9 2.4 %collective-permute-start.23 = (bf16[64,1024]{1,0:T(8,128)(2,1)S(1)}, bf16[64,1024]{1,0:T(8,128)(2,1)S(1)}, u32[]{:S(2)}, u32[]{:S(2)}) collective-permute-start(bf16[64,1024]{1,0:T(8,128)(2,1)S(1)} %get-tuple-element.75), channel_id=1, source_target_pairs={{0,4},{1,5},{2,6},{3,7},{4,0},{5,1},{6,2},{7,3},{8,12},{9,13},{10,... | collective-permute-start | bytes 393224 | tf_op jit(solution)/shard_map/ppermute | solution.py:1019
  120.3 8.6 %collective-permute-done.34.refs_2_ = bf16[64,1024]{1,0:T(8,128)(2,1)S(1)} collective-permute-done((bf16[64,1024]{1,0:T(8,128)(2,1)S(1)}, bf16[64,1024]{1,0:T(8,128)(2,1)S(1)}, u32[]{:S(2)}, u32[]{:S(2)}) %collective-permute-start.34) | collective-permute-done | bytes 131104 | tf_op jit(solution)/shard_map/ppermute | solution.py:1019
  130.3 1.5 %collective-permute-start.36 = (bf16[64,1024]{1,0:T(8,128)(2,1)S(1)}, bf16[64,1024]{1,0:T(8,128)(2,1)S(1)}, u32[]{:S(2)}, u32[]{:S(2)}) collective-permute-start(bf16[64,1024]{1,0:T(8,128)(2,1)S(1)} %collect.3.other_ref.refs_4_), channel_id=1, source_target_pairs={{0,8},{8,0},{16,24},{24,16},{1,9},{9,1},{17,25},{25,17},{2,10},{10... | collective-permute-start | bytes 393224 | tf_op jit(solution)/shard_map/ppermute | solution.py:1012
  133.0 2.2 %collective-permute-done.24.refs_3_ = bf16[64,1024]{1,0:T(8,128)(2,1)S(1)} collective-permute-done((bf16[64,1024]{1,0:T(8,128)(2,1)S(1)}, bf16[64,1024]{1,0:T(8,128)(2,1)S(1)}, u32[]{:S(2)}, u32[]{:S(2)}) %collective-permute-start.24) | collective-permute-done | bytes 131104 | tf_op jit(solution)/shard_map/ppermute | solution.py:1019
  138.9 1.5 %collective-permute-start.39 = (bf16[80,1024]{1,0:T(8,128)(2,1)S(1)}, bf16[80,1024]{1,0:T(8,128)(2,1)S(1)}, u32[]{:S(2)}, u32[]{:S(2)}) collective-permute-start(bf16[80,1024]{1,0:T(8,128)(2,1)S(1)} %get-tuple-element.92.refs_0_), channel_id=1, source_target_pairs={{0,16},{8,24},{16,0},{24,8},{1,17},{9,25},{17,1},{25,9},{2,18},{10... | collective-permute-start | bytes 491528 | tf_op jit(solution)/shard_map/ppermute | solution.py:1012
  140.4 7.0 %collective-permute-done.38.refs_1_ = bf16[80,1024]{1,0:T(8,128)(2,1)S(1)} collective-permute-done((bf16[80,1024]{1,0:T(8,128)(2,1)S(1)}, bf16[80,1024]{1,0:T(8,128)(2,1)S(1)}, u32[]{:S(2)}, u32[]{:S(2)}) %collective-permute-start.38) | collective-permute-done | bytes 163872 | tf_op jit(solution)/shard_map/ppermute | solution.py:1012
  148.4 1.7 %place.1 = (f32[1024,256]{1,0:T(8,128)}, f32[256,1024]{1,0:T(8,128)}, f32[1,1024]{1,0:T(1,128)}, f32[1,1024]{1,0:T(1,128)}, f32[1,1]{1,0:T(1,128)}) custom-call(s32[1]{0:T(128)} %bitcast.group_ref, bf16[80,1024]{1,0:T(8,128)(2,1)S(1)} %get-tuple-element.92.refs_0_, bf16[80,1024]{1,0:T(8,128)(2,1)S(1)} %collective-permute-done.38.refs_1_, ...), custom_call_target="tpu_custom_call" | custom-call | flops 1048576 | bytes 65536 | tf_op jit(solution)/shard_map/place/pallas_call | solution.py:978
  (105 shorter events, 39.6 us)
Async XLA Ops:
  3.1 14.9 %collective-permute-start = (bf16[2,64,1024]{2,1,0:T(8,128)(2,1)S(1)}, bf16[2,64,1024]{2,1,0:T(8,128)(2,1)S(1)}, u32[]{:S(2)}, u32[]{:S(2)}) collective-permute-start(bf16[2,64,1024]{2,1,0:T(8,128)(2,1)S(1)} %quarter.1), channel_id=1, source_target_pairs={{0,6},{1,7},{2,0},{3,1},{4,2},{5,3},{6,4},{7,5},{8,14},{9,15},{10,... | collective-permute-start | bytes 786440 | tf_op jit(solution)/shard_map/ppermute | solution.py:1019
  3.2 23.3 %collective-permute-start.3 = (bf16[2,64,1024]{2,1,0:T(8,128)(2,1)S(1)}, bf16[2,64,1024]{2,1,0:T(8,128)(2,1)S(1)}, u32[]{:S(2)}, u32[]{:S(2)}) collective-permute-start(bf16[2,64,1024]{2,1,0:T(8,128)(2,1)S(1)} %quarter.1), channel_id=1, source_target_pairs={{0,4},{1,5},{2,6},{3,7},{4,0},{5,1},{6,2},{7,3},{8,12},{9,13},{10,... | collective-permute-start | bytes 786440 | tf_op jit(solution)/shard_map/ppermute | solution.py:1019
  18.1 8.4 %collective-permute-start.2 = (bf16[1,2,64,1024]{3,2,1,0:T(8,128)(2,1)S(1)}, bf16[1,2,64,1024]{3,2,1,0:T(8,128)(2,1)S(1)}, u32[]{:S(2)}, u32[]{:S(2)}) collective-permute-start(bf16[1,2,64,1024]{3,2,1,0:T(8,128)(2,1)S(1)} %pack.4.refs_1_), channel_id=1, source_target_pairs={{0,16},{8,24},{16,0},{24,8},{1,17},{9,25},{17,1},{25,9},{2,18},{10... | collective-permute-start | bytes 786440 | tf_op jit(solution)/shard_map/ppermute | solution.py:1012
  19.6 6.9 %collective-permute-start.1 = (bf16[1,2,64,1024]{3,2,1,0:T(8,128)(2,1)S(1)}, bf16[1,2,64,1024]{3,2,1,0:T(8,128)(2,1)S(1)}, u32[]{:S(2)}, u32[]{:S(2)}) collective-permute-start(bf16[1,2,64,1024]{3,2,1,0:T(8,128)(2,1)S(1)} %pack.4.refs_1_), channel_id=1, source_target_pairs={{0,8},{8,0},{16,24},{24,16},{1,9},{9,1},{17,25},{25,17},{2,10},{10... | collective-permute-start | bytes 786440 | tf_op jit(solution)/shard_map/ppermute | solution.py:1012
  21.1 13.8 %collective-permute-start.4 = (bf16[2,64,1024]{2,1,0:T(8,128)(2,1)S(1)}, bf16[2,64,1024]{2,1,0:T(8,128)(2,1)S(1)}, u32[]{:S(2)}, u32[]{:S(2)}) collective-permute-start(bf16[2,64,1024]{2,1,0:T(8,128)(2,1)S(1)} %quarter.1), channel_id=1, source_target_pairs={{0,2},{1,3},{2,4},{3,5},{4,6},{5,7},{6,0},{7,1},{8,10},{9,11},{10,... | collective-permute-start | bytes 786440 | tf_op jit(solution)/shard_map/ppermute | solution.py:1019
  21.1 21.2 %collective-permute-start.9 = (bf16[2,64,1024]{2,1,0:T(8,128)(2,1)S(1)}, bf16[2,64,1024]{2,1,0:T(8,128)(2,1)S(1)}, u32[]{:S(2)}, u32[]{:S(2)}) collective-permute-start(bf16[2,64,1024]{2,1,0:T(8,128)(2,1)S(1)} %get-tuple-element.53), channel_id=1, source_target_pairs={{0,4},{1,5},{2,6},{3,7},{4,0},{5,1},{6,2},{7,3},{8,12},{9,13},{10,... | collective-permute-start | bytes 786440 | tf_op jit(solution)/shard_map/ppermute | solution.py:1019
  34.9 9.2 %collective-permute-start.6 = (bf16[2,64,1024]{2,1,0:T(8,128)(2,1)S(1)}, bf16[2,64,1024]{2,1,0:T(8,128)(2,1)S(1)}, u32[]{:S(2)}, u32[]{:S(2)}) collective-permute-start(bf16[2,64,1024]{2,1,0:T(8,128)(2,1)S(1)} %tie.3.refs_5_), channel_id=1, source_target_pairs={{0,8},{8,0},{16,24},{24,16},{1,9},{9,1},{17,25},{25,17},{2,10},{10... | collective-permute-start | bytes 786440 | tf_op jit(solution)/shard_map/ppermute | solution.py:1012
  36.4 9.1 %collective-permute-start.8 = (bf16[2,64,1024]{2,1,0:T(8,128)(2,1)S(1)}, bf16[2,64,1024]{2,1,0:T(8,128)(2,1)S(1)}, u32[]{:S(2)}, u32[]{:S(2)}) collective-permute-start(bf16[2,64,1024]{2,1,0:T(8,128)(2,1)S(1)} %tie.3.refs_5_), channel_id=1, source_target_pairs={{0,16},{8,24},{16,0},{24,8},{1,17},{9,25},{17,1},{25,9},{2,18},{10... | collective-permute-start | bytes 786440 | tf_op jit(solution)/shard_map/ppermute | solution.py:1012
  37.9 9.2 %collective-permute-start.5 = (bf16[2,64,1024]{2,1,0:T(8,128)(2,1)S(1)}, bf16[2,64,1024]{2,1,0:T(8,128)(2,1)S(1)}, u32[]{:S(2)}, u32[]{:S(2)}) collective-permute-start(bf16[2,64,1024]{2,1,0:T(8,128)(2,1)S(1)} %tie.2.refs_1_.refs_4_), channel_id=1, source_target_pairs={{0,8},{8,0},{16,24},{24,16},{1,9},{9,1},{17,25},{25,17},{2,10},{10... | collective-permute-start | bytes 786440 | tf_op jit(solution)/shard_map/ppermute | solution.py:1012
  38.5 9.9 %collective-permute-start.7 = (bf16[2,64,1024]{2,1,0:T(8,128)(2,1)S(1)}, bf16[2,64,1024]{2,1,0:T(8,128)(2,1)S(1)}, u32[]{:S(2)}, u32[]{:S(2)}) collective-permute-start(bf16[2,64,1024]{2,1,0:T(8,128)(2,1)S(1)} %tie.2.refs_1_.refs_4_), channel_id=1, source_target_pairs={{0,16},{8,24},{16,0},{24,8},{1,17},{9,25},{17,1},{25,9},{2,18},{10... | collective-permute-start | bytes 786440 | tf_op jit(solution)/shard_map/ppermute | solution.py:1012
  48.5 6.1 %collective-permute-start.12 = (bf16[13,2,64,1024]{3,2,1,0:T(8,128)(2,1)S(1)}, bf16[13,2,64,1024]{3,2,1,0:T(8,128)(2,1)S(1)}, u32[]{:S(2)}, u32[]{:S(2)}) collective-permute-start(bf16[13,2,64,1024]{3,2,1,0:T(8,128)(2,1)S(1)} %pack.5.refs_1_.refs_0_), channel_id=1, source_target_pairs={{0,1},{1,0},{2,3},{3,2},{4,5},{5,4},{6,7},{7,6},{8,9},{9,8},{10,11... | collective-permute-start | bytes 10223624 | tf_op jit(solution)/shard_map/ppermute | solution.py:1015
  48.7 16.9 %collective-permute-start.11 = (bf16[2,2,64,1024]{3,2,1,0:T(8,128)(2,1)S(1)}, bf16[2,2,64,1024]{3,2,1,0:T(8,128)(2,1)S(1)}, u32[]{:S(2)}, u32[]{:S(2)}) collective-permute-start(bf16[2,2,64,1024]{3,2,1,0:T(8,128)(2,1)S(1)} %pack.6), channel_id=1, source_target_pairs={{0,16},{8,24},{16,0},{24,8},{1,17},{9,25},{17,1},{25,9},{2,18},{10... | collective-permute-start | bytes 1572872 | tf_op jit(solution)/shard_map/ppermute | solution.py:1012
  50.2 14.0 %collective-permute-start.13 = (bf16[2,64,1024]{2,1,0:T(8,128)(2,1)S(1)}, bf16[2,64,1024]{2,1,0:T(8,128)(2,1)S(1)}, u32[]{:S(2)}, u32[]{:S(2)}) collective-permute-start(bf16[2,64,1024]{2,1,0:T(8,128)(2,1)S(1)} %get-tuple-element.57), channel_id=1, source_target_pairs={{0,2},{1,3},{2,4},{3,5},{4,6},{5,7},{6,0},{7,1},{8,10},{9,11},{10,... | collective-permute-start | bytes 786440 | tf_op jit(solution)/shard_map/ppermute | solution.py:1019
  52.7 12.8 %collective-permute-start.14 = (bf16[2,64,1024]{2,1,0:T(8,128)(2,1)S(1)}, bf16[2,64,1024]{2,1,0:T(8,128)(2,1)S(1)}, u32[]{:S(2)}, u32[]{:S(2)}) collective-permute-start(bf16[2,64,1024]{2,1,0:T(8,128)(2,1)S(1)} %get-tuple-element.58), channel_id=1, source_target_pairs={{0,6},{1,7},{2,0},{3,1},{4,2},{5,3},{6,4},{7,5},{8,14},{9,15},{10,... | collective-permute-start | bytes 786440 | tf_op jit(solution)/shard_map/ppermute | solution.py:1019
  52.7 12.8 %collective-permute-start.10 = (bf16[1,2,64,1024]{3,2,1,0:T(8,128)(2,1)S(1)}, bf16[1,2,64,1024]{3,2,1,0:T(8,128)(2,1)S(1)}, u32[]{:S(2)}, u32[]{:S(2)}) collective-permute-start(bf16[1,2,64,1024]{3,2,1,0:T(8,128)(2,1)S(1)} %collective-permute-done.2.refs_2_.refs_3_), channel_id=1, source_target_pairs={{0,8},{8,0},{16,24},{24,16},{1,9},{9,1},{17,25},{25,17},{2,10},{10... | collective-permute-start | bytes 786440 | tf_op jit(solution)/shard_map/ppermute | solution.py:1012
  78.5 17.6 %collective-permute-start.29 = (bf16[4,64,1024]{2,1,0:T(8,128)(2,1)S(1)}, bf16[4,64,1024]{2,1,0:T(8,128)(2,1)S(1)}, u32[]{:S(2)}, u32[]{:S(2)}) collective-permute-start(bf16[4,64,1024]{2,1,0:T(8,128)(2,1)S(1)} %get-tuple-element.82), channel_id=1, source_target_pairs={{0,8},{8,0},{16,24},{24,16},{1,9},{9,1},{17,25},{25,17},{2,10},{10... | collective-permute-start | bytes 1572872 | tf_op jit(solution)/shard_map/ppermute | solution.py:1012
  79.1 16.9 %collective-permute-start.30 = (bf16[4,64,1024]{2,1,0:T(8,128)(2,1)S(1)}, bf16[4,64,1024]{2,1,0:T(8,128)(2,1)S(1)}, u32[]{:S(2)}, u32[]{:S(2)}) collective-permute-start(bf16[4,64,1024]{2,1,0:T(8,128)(2,1)S(1)} %get-tuple-element.83), channel_id=1, source_target_pairs={{0,16},{8,24},{16,0},{24,8},{1,17},{9,25},{17,1},{25,9},{2,18},{10... | collective-permute-start | bytes 1572872 | tf_op jit(solution)/shard_map/ppermute | solution.py:1012
  83.5 21.1 %collective-permute-start.18 = (bf16[4,64,1024]{2,1,0:T(8,128)(2,1)S(1)}, bf16[4,64,1024]{2,1,0:T(8,128)(2,1)S(1)}, u32[]{:S(2)}, u32[]{:S(2)}) collective-permute-start(bf16[4,64,1024]{2,1,0:T(8,128)(2,1)S(1)} %get-tuple-element.67), channel_id=1, source_target_pairs={{0,8},{8,0},{16,24},{24,16},{1,9},{9,1},{17,25},{25,17},{2,10},{10... | collective-permute-start | bytes 1572872 | tf_op jit(solution)/shard_map/ppermute | solution.py:1012
  84.5 20.7 %collective-permute-start.19 = (bf16[4,64,1024]{2,1,0:T(8,128)(2,1)S(1)}, bf16[4,64,1024]{2,1,0:T(8,128)(2,1)S(1)}, u32[]{:S(2)}, u32[]{:S(2)}) collective-permute-start(bf16[4,64,1024]{2,1,0:T(8,128)(2,1)S(1)} %get-tuple-element.68), channel_id=1, source_target_pairs={{0,16},{8,24},{16,0},{24,8},{1,17},{9,25},{17,1},{25,9},{2,18},{10... | collective-permute-start | bytes 1572872 | tf_op jit(solution)/shard_map/ppermute | solution.py:1012
  96.2 14.0 %collective-permute-start.31 = (bf16[2,64,1024]{2,1,0:T(8,128)(2,1)S(1)}, bf16[2,64,1024]{2,1,0:T(8,128)(2,1)S(1)}, u32[]{:S(2)}, u32[]{:S(2)}) collective-permute-start(bf16[2,64,1024]{2,1,0:T(8,128)(2,1)S(1)} %get-tuple-element.86), channel_id=1, source_target_pairs={{0,8},{8,0},{16,24},{24,16},{1,9},{9,1},{17,25},{25,17},{2,10},{10... | collective-permute-start | bytes 786440 | tf_op jit(solution)/shard_map/ppermute | solution.py:1012
  96.8 14.0 %collective-permute-start.32 = (bf16[2,64,1024]{2,1,0:T(8,128)(2,1)S(1)}, bf16[2,64,1024]{2,1,0:T(8,128)(2,1)S(1)}, u32[]{:S(2)}, u32[]{:S(2)}) collective-permute-start(bf16[2,64,1024]{2,1,0:T(8,128)(2,1)S(1)} %get-tuple-element.87), channel_id=1, source_target_pairs={{0,16},{8,24},{16,0},{24,8},{1,17},{9,25},{17,1},{25,9},{2,18},{10... | collective-permute-start | bytes 786440 | tf_op jit(solution)/shard_map/ppermute | solution.py:1012
  105.3 9.7 %collective-permute-start.20 = (bf16[2,64,1024]{2,1,0:T(8,128)(2,1)S(1)}, bf16[2,64,1024]{2,1,0:T(8,128)(2,1)S(1)}, u32[]{:S(2)}, u32[]{:S(2)}) collective-permute-start(bf16[2,64,1024]{2,1,0:T(8,128)(2,1)S(1)} %get-tuple-element.71), channel_id=1, source_target_pairs={{0,8},{8,0},{16,24},{24,16},{1,9},{9,1},{17,25},{25,17},{2,10},{10... | collective-permute-start | bytes 786440 | tf_op jit(solution)/shard_map/ppermute | solution.py:1012
  106.8 8.4 %collective-permute-start.21 = (bf16[2,64,1024]{2,1,0:T(8,128)(2,1)S(1)}, bf16[2,64,1024]{2,1,0:T(8,128)(2,1)S(1)}, u32[]{:S(2)}, u32[]{:S(2)}) collective-permute-start(bf16[2,64,1024]{2,1,0:T(8,128)(2,1)S(1)} %get-tuple-element.72), channel_id=1, source_target_pairs={{0,16},{8,24},{16,0},{24,8},{1,17},{9,25},{17,1},{25,9},{2,18},{10... | collective-permute-start | bytes 786440 | tf_op jit(solution)/shard_map/ppermute | solution.py:1012
  111.0 8.3 %collective-permute-start.33 = (bf16[64,1024]{1,0:T(8,128)(2,1)S(1)}, bf16[64,1024]{1,0:T(8,128)(2,1)S(1)}, u32[]{:S(2)}, u32[]{:S(2)}) collective-permute-start(bf16[64,1024]{1,0:T(8,128)(2,1)S(1)} %get-tuple-element.89), channel_id=1, source_target_pairs={{0,2},{1,3},{2,4},{3,5},{4,6},{5,7},{6,0},{7,1},{8,10},{9,11},{10,... | collective-permute-start | bytes 393224 | tf_op jit(solution)/shard_map/ppermute | solution.py:1019
  112.2 16.7 %collective-permute-start.34 = (bf16[64,1024]{1,0:T(8,128)(2,1)S(1)}, bf16[64,1024]{1,0:T(8,128)(2,1)S(1)}, u32[]{:S(2)}, u32[]{:S(2)}) collective-permute-start(bf16[64,1024]{1,0:T(8,128)(2,1)S(1)} %get-tuple-element.90), channel_id=1, source_target_pairs={{0,4},{1,5},{2,6},{3,7},{4,0},{5,1},{6,2},{7,3},{8,12},{9,13},{10,... | collective-permute-start | bytes 393224 | tf_op jit(solution)/shard_map/ppermute | solution.py:1019
  114.6 15.6 %collective-permute-start.35 = (bf16[64,1024]{1,0:T(8,128)(2,1)S(1)}, bf16[64,1024]{1,0:T(8,128)(2,1)S(1)}, u32[]{:S(2)}, u32[]{:S(2)}) collective-permute-start(bf16[64,1024]{1,0:T(8,128)(2,1)S(1)} %get-tuple-element.91), channel_id=1, source_target_pairs={{0,6},{1,7},{2,0},{3,1},{4,2},{5,3},{6,4},{7,5},{8,14},{9,15},{10,... | collective-permute-start | bytes 393224 | tf_op jit(solution)/shard_map/ppermute | solution.py:1019
  115.5 16.9 %collective-permute-start.22 = (bf16[64,1024]{1,0:T(8,128)(2,1)S(1)}, bf16[64,1024]{1,0:T(8,128)(2,1)S(1)}, u32[]{:S(2)}, u32[]{:S(2)}) collective-permute-start(bf16[64,1024]{1,0:T(8,128)(2,1)S(1)} %get-tuple-element.74), channel_id=1, source_target_pairs={{0,2},{1,3},{2,4},{3,5},{4,6},{5,7},{6,0},{7,1},{8,10},{9,11},{10,... | collective-permute-start | bytes 393224 | tf_op jit(solution)/shard_map/ppermute | solution.py:1019
  116.9 16.2 %collective-permute-start.23 = (bf16[64,1024]{1,0:T(8,128)(2,1)S(1)}, bf16[64,1024]{1,0:T(8,128)(2,1)S(1)}, u32[]{:S(2)}, u32[]{:S(2)}) collective-permute-start(bf16[64,1024]{1,0:T(8,128)(2,1)S(1)} %get-tuple-element.75), channel_id=1, source_target_pairs={{0,4},{1,5},{2,6},{3,7},{4,0},{5,1},{6,2},{7,3},{8,12},{9,13},{10,... | collective-permute-start | bytes 393224 | tf_op jit(solution)/shard_map/ppermute | solution.py:1019
  119.2 16.0 %collective-permute-start.24 = (bf16[64,1024]{1,0:T(8,128)(2,1)S(1)}, bf16[64,1024]{1,0:T(8,128)(2,1)S(1)}, u32[]{:S(2)}, u32[]{:S(2)}) collective-permute-start(bf16[64,1024]{1,0:T(8,128)(2,1)S(1)} %get-tuple-element.76), channel_id=1, source_target_pairs={{0,6},{1,7},{2,0},{3,1},{4,2},{5,3},{6,4},{7,5},{8,14},{9,15},{10,... | collective-permute-start | bytes 393224 | tf_op jit(solution)/shard_map/ppermute | solution.py:1019
  136.8 11.5 %collective-permute-start.40 = (bf16[144,1024]{1,0:T(8,128)(2,1)S(1)}, bf16[144,1024]{1,0:T(8,128)(2,1)S(1)}, u32[]{:S(2)}, u32[]{:S(2)}) collective-permute-start(bf16[144,1024]{1,0:T(8,128)(2,1)S(1)} %get-tuple-element.93), channel_id=1, source_target_pairs={{0,24},{8,16},{16,8},{24,0},{1,25},{9,17},{17,9},{25,1},{2,26},{10... | collective-permute-start | bytes 884744 | tf_op jit(solution)/shard_map/ppermute | solution.py:1012
  137.4 10.0 %collective-permute-start.38 = (bf16[80,1024]{1,0:T(8,128)(2,1)S(1)}, bf16[80,1024]{1,0:T(8,128)(2,1)S(1)}, u32[]{:S(2)}, u32[]{:S(2)}) collective-permute-start(bf16[80,1024]{1,0:T(8,128)(2,1)S(1)} %get-tuple-element.92.refs_0_), channel_id=1, source_target_pairs={{0,8},{8,0},{16,24},{24,16},{1,9},{9,1},{17,25},{25,17},{2,10},{10... | collective-permute-start | bytes 491528 | tf_op jit(solution)/shard_map/ppermute | solution.py:1012
  138.9 9.5 %collective-permute-start.39 = (bf16[80,1024]{1,0:T(8,128)(2,1)S(1)}, bf16[80,1024]{1,0:T(8,128)(2,1)S(1)}, u32[]{:S(2)}, u32[]{:S(2)}) collective-permute-start(bf16[80,1024]{1,0:T(8,128)(2,1)S(1)} %get-tuple-element.92.refs_0_), channel_id=1, source_target_pairs={{0,16},{8,24},{16,0},{24,8},{1,17},{9,25},{17,1},{25,9},{2,18},{10... | collective-permute-start | bytes 491528 | tf_op jit(solution)/shard_map/ppermute | solution.py:1012
  (22 other events, 168.7 us)

commit v16 on v14

--- a/solution.py
+++ b/solution.py
@@ -1037,12 +1037,12 @@
     )
     most = pack(
         [own_rows(group, up_weight, down_weight), low, x_low, y_low, high, x_high, y_high],
-        targets[half],
+        normed, targets[1], *targets[half + 1:],
     )
     most_other = partner(most)
     d_low, d_high = beside(y_low, 1), beside(x_high, 2)
     act_most, slope_most, mixed = forward(normed_t, [most], [most_other])
-    late = [target for shift, target in enumerate(targets) if shift not in (0, half)]
+    late = targets[2:half + 1]
     last = pack([d_low, d_high], mixed, *late)
     last_other = partner(last)
     act_last, slope_last, back, back_t, small = forward(

time: 147 us -> 145 us (0.986); the launches traced: 145 us -> 145 us
  starting transfers between devices: 37 us -> 46.6 us
  waiting for transfers between devices: 72.8 us -> 63.4 us
    ppermute x12, waiting for transfers between devices: 33.4 us -> 28.2 us  [along(): return lax.ppermute(array, 'ray', pairs)]
    ppermute x12, starting transfers between devices: 15 us -> 19.9 us  [along(): return lax.ppermute(array, 'ray', pairs)]
    ppermute x8, starting transfers between devices: 2.59 us -> 6.59 us  [partner(): return lax.ppermute(array, 'ray', [(r, r ^ flip) for r in range(ray_count)])]
    ppermute x19, waiting for transfers between devices: 26.9 us -> 23.5 us  [beside(): lax.ppermute(array, 'grp', [(g, g ^ flip) for g in range(group_count)])]
  transfers between devices with their start and end apart: 39 -> 39, of which waited for: 29 -> 25; matrix products, arithmetic and copies ran while one was open for 0% -> 0% of each run, Pallas kernels for 17% -> 17%
where the time goes in v16:
time: 145 us
  waiting for transfers between devices  63.4 us (44%)
  starting transfers between devices  46.6 us (32%)
  Pallas kernels  31.8 us (22%)
  local copies, waits for them, and re-layouts  2.13 us (1%)
    ppermute x12, waiting for transfers between devices, along(): return lax.ppermute(array, 'ray', pairs)  28.2 us
    ppermute x19, waiting for transfers between devices, beside(): lax.ppermute(array, 'grp', [(g, g ^ flip) for g in range(group_count)])  23.5 us
    ppermute x19, starting transfers between devices, beside(): lax.ppermute(array, 'grp', [(g, g ^ flip) for g in range(group_count)])  20.1 us
    ppermute x12, starting transfers between devices, along(): return lax.ppermute(array, 'ray', pairs)  19.9 us
    ppermute x8, waiting for transfers between devices, partner(): return lax.ppermute(array, 'ray', [(r, r ^ flip) for r in range(ray_count)])  11.6 us
    pallas_call x1, Pallas kernels, render(): pl.pallas_call(functools.partial(render_kernel, ray_count, relative), out...  8.41 us
    pallas_call x2, Pallas kernels, forward(): pl.pallas_call(functools.partial(forward_kernel, first, blocks, len(own),...  7.89 us
    ppermute x8, starting transfers between devices, partner(): return lax.ppermute(array, 'ray', [(r, r ^ flip) for r in range(ray_count)])  6.59 us
  transfers between devices with their start and end apart: 39, of which 25 were waited for; matrix products, arithmetic and copies ran while one was open for 0% of the time, Pallas kernels for 17%

profile of v16, /device:TPU:8, one launch (start us, length us, event | category | flops | bytes accessed | tf_op | source)
XLA Modules:
  0.0 144.8 jit_solution(8075740615813985270)
XLA Ops:
  3.2 3.0 %collective-permute-start.3 = (bf16[2,64,1024]{2,1,0:T(8,128)(2,1)S(1)}, bf16[2,64,1024]{2,1,0:T(8,128)(2,1)S(1)}, u32[]{:S(2)}, u32[]{:S(2)}) collective-permute-start(bf16[2,64,1024]{2,1,0:T(8,128)(2,1)S(1)} %quarter.1), channel_id=1, source_target_pairs={{0,4},{1,5},{2,6},{3,7},{4,0},{5,1},{6,2},{7,3},{8,12},{9,13},{10,... | collective-permute-start | bytes 786440 | tf_op jit(solution)/shard_map/ppermute | solution.py:1019
  6.2 2.5 %collective-permute-start.4 = (bf16[2,64,1024]{2,1,0:T(8,128)(2,1)S(1)}, bf16[2,64,1024]{2,1,0:T(8,128)(2,1)S(1)}, u32[]{:S(2)}, u32[]{:S(2)}) collective-permute-start(bf16[2,64,1024]{2,1,0:T(8,128)(2,1)S(1)} %quarter.1), channel_id=1, source_target_pairs={{0,2},{1,3},{2,4},{3,5},{4,6},{5,7},{6,0},{7,1},{8,10},{9,11},{10,... | collective-permute-start | bytes 786440 | tf_op jit(solution)/shard_map/ppermute | solution.py:1019
  8.7 8.4 %render.1 = (bf16[2,64,1024]{2,1,0:T(8,128)(2,1)S(1)}, bf16[2,64,1024]{2,1,0:T(8,128)(2,1)S(1)}, bf16[2,64,1024]{2,1,0:T(8,128)(2,1)S(1)}, bf16[2,64,1024]{2,1,0:T(8,128)(2,1)S(1)}) custom-call(s32[1]{0:T(128)} %bitcast.1.me_ref, s32[1,8]{1,0:T(1,128)S(1)} %copy-done.11, s32[32,512]{1,0:T(8,128)S(1)} %copy-done.7, f32[32,512]{1,0:T(8,128)S(1)} %copy-done.8, ...), custom_call_target="tpu_custom_call" | custom-call | flops 1048576 | bytes 65536 | tf_op jit(solution)/shard_map/render/pallas_call | solution.py:152
  17.2 6.4 %collective-permute-done.refs_0_ = bf16[2,64,1024]{2,1,0:T(8,128)(2,1)S(1)} collective-permute-done((bf16[2,64,1024]{2,1,0:T(8,128)(2,1)S(1)}, bf16[2,64,1024]{2,1,0:T(8,128)(2,1)S(1)}, u32[]{:S(2)}, u32[]{:S(2)}) %collective-permute-start) | collective-permute-done | bytes 262176 | tf_op jit(solution)/shard_map/ppermute | solution.py:1019
  23.6 1.6 %collective-permute-start.2 = (bf16[1,2,64,1024]{3,2,1,0:T(8,128)(2,1)S(1)}, bf16[1,2,64,1024]{3,2,1,0:T(8,128)(2,1)S(1)}, u32[]{:S(2)}, u32[]{:S(2)}) collective-permute-start(bf16[1,2,64,1024]{3,2,1,0:T(8,128)(2,1)S(1)} %pack.4.refs_2_.refs_1_), channel_id=1, source_target_pairs={{0,16},{8,24},{16,0},{24,8},{1,17},{9,25},{17,1},{25,9},{2,18},{10... | collective-permute-start | bytes 786440 | tf_op jit(solution)/shard_map/ppermute | solution.py:1012
  26.7 1.7 %collective-permute-done.4.refs_1_ = bf16[2,64,1024]{2,1,0:T(8,128)(2,1)S(1)} collective-permute-done((bf16[2,64,1024]{2,1,0:T(8,128)(2,1)S(1)}, bf16[2,64,1024]{2,1,0:T(8,128)(2,1)S(1)}, u32[]{:S(2)}, u32[]{:S(2)}) %collective-permute-start.4) | collective-permute-done | bytes 262176 | tf_op jit(solution)/shard_map/ppermute | solution.py:1019
  28.5 1.6 %collective-permute-done.2.refs_2_.refs_3_ = bf16[1,2,64,1024]{3,2,1,0:T(8,128)(2,1)S(1)} collective-permute-done((bf16[1,2,64,1024]{3,2,1,0:T(8,128)(2,1)S(1)}, bf16[1,2,64,1024]{3,2,1,0:T(8,128)(2,1)S(1)}, u32[]{:S(2)}, u32[]{:S(2)}) %collective-permute-start.2) | collective-permute-done | bytes 262176 | tf_op jit(solution)/shard_map/ppermute | solution.py:1012
  30.1 2.7 %collective-permute-done.1.refs_1_.refs_2_ = bf16[1,2,64,1024]{3,2,1,0:T(8,128)(2,1)S(1)} collective-permute-done((bf16[1,2,64,1024]{3,2,1,0:T(8,128)(2,1)S(1)}, bf16[1,2,64,1024]{3,2,1,0:T(8,128)(2,1)S(1)}, u32[]{:S(2)}, u32[]{:S(2)}) %collective-permute-start.1) | collective-permute-done | bytes 262176 | tf_op jit(solution)/shard_map/ppermute | solution.py:1012
  34.2 2.0 %collective-permute-start.8 = (bf16[2,64,1024]{2,1,0:T(8,128)(2,1)S(1)}, bf16[2,64,1024]{2,1,0:T(8,128)(2,1)S(1)}, u32[]{:S(2)}, u32[]{:S(2)}) collective-permute-start(bf16[2,64,1024]{2,1,0:T(8,128)(2,1)S(1)} %get-tuple-element.55), channel_id=1, source_target_pairs={{0,6},{1,7},{2,0},{3,1},{4,2},{5,3},{6,4},{7,5},{8,14},{9,15},{10,... | collective-permute-start | bytes 786440 | tf_op jit(solution)/shard_map/ppermute | solution.py:1019
  36.5 3.2 %tokens.1 = (bf16[512,1024]{1,0:T(8,128)(2,1)S(1)}, bf16[512,1024]{1,0:T(8,128)(2,1)S(1)}, bf16[1024,512]{1,0:T(8,128)(2,1)S(1)}) custom-call(s32[1]{0:T(128)} %bitcast.1.me_ref, s32[1,8]{1,0:T(1,128)S(1)} %copy-done.11, s32[1,4096]{1,0:T(1,128)S(1)} %copy-done.6, bf16[512,1024]{1,0:T(8,128)(2,1)S(1)} %copy-done.1, f32[1,1024]{1,0:T(1,128)S(1)} %bitcast.8), custom_call_target="tpu_custom_call" | custom-call | flops 1048576 | bytes 65536 | tf_op jit(solution)/shard_map/tokens/pallas_call | solution.py:238
  39.8 4.3 %collective-permute-done.7.refs_8_.refs_1_.refs_7_ = bf16[2,64,1024]{2,1,0:T(8,128)(2,1)S(1)} collective-permute-done((bf16[2,64,1024]{2,1,0:T(8,128)(2,1)S(1)}, bf16[2,64,1024]{2,1,0:T(8,128)(2,1)S(1)}, u32[]{:S(2)}, u32[]{:S(2)}) %collective-permute-start.7) | collective-permute-done | bytes 262176 | tf_op jit(solution)/shard_map/ppermute | solution.py:1019
  46.2 2.1 %collective-permute-start.12 = (bf16[2,64,1024]{2,1,0:T(8,128)(2,1)S(1)}, bf16[2,64,1024]{2,1,0:T(8,128)(2,1)S(1)}, u32[]{:S(2)}, u32[]{:S(2)}) collective-permute-start(bf16[2,64,1024]{2,1,0:T(8,128)(2,1)S(1)} %get-tuple-element.58), channel_id=1, source_target_pairs={{0,4},{1,5},{2,6},{3,7},{4,0},{5,1},{6,2},{7,3},{8,12},{9,13},{10,... | collective-permute-start | bytes 786440 | tf_op jit(solution)/shard_map/ppermute | solution.py:1019
  48.8 2.8 %collective-permute-done.11.refs_2_.refs_0_ = bf16[13,2,64,1024]{3,2,1,0:T(8,128)(2,1)S(1)} collective-permute-done((bf16[13,2,64,1024]{3,2,1,0:T(8,128)(2,1)S(1)}, bf16[13,2,64,1024]{3,2,1,0:T(8,128)(2,1)S(1)}, u32[]{:S(2)}, u32[]{:S(2)}) %collective-permute-start.11) | collective-permute-done | bytes 3407904 | tf_op jit(solution)/shard_map/ppermute | solution.py:1015
  51.7 5.0 %forward.2 = (bf16[2,13,64,512]{3,2,1,0:T(8,128)(2,1)S(1)}, f32[2,13,64,512]{3,2,1,0:T(8,128)S(1)}, f32[512,1024]{1,0:T(8,128)S(1)}) custom-call(bf16[1024,512]{1,0:T(8,128)(2,1)S(1)} %get-tuple-element.56.refs_0_, bf16[13,2,64,1024]{3,2,1,0:T(8,128)(2,1)S(1)} %pack.6.refs_1_.refs_0_, bf16[13,2,64,1024]{3,2,1,0:T(8,128)(2,1)S(1)} %collective-permute-done.11.refs_2_.refs_0_), custom_call_target="tpu_custom_call" | custom-call | flops 1048576 | bytes 65536 | tf_op jit(solution)/shard_map/forward/pallas_call | solution.py:652
  56.7 3.1 %collective-permute-done.12.refs_3_.refs_2_.refs_8_ = bf16[2,64,1024]{2,1,0:T(8,128)(2,1)S(1)} collective-permute-done((bf16[2,64,1024]{2,1,0:T(8,128)(2,1)S(1)}, bf16[2,64,1024]{2,1,0:T(8,128)(2,1)S(1)}, u32[]{:S(2)}, u32[]{:S(2)}) %collective-permute-start.12) | collective-permute-done | bytes 262176 | tf_op jit(solution)/shard_map/ppermute | solution.py:1019
  60.7 2.4 %collective-permute-done.14.refs_10_ = bf16[4,64,1024]{2,1,0:T(8,128)(2,1)S(1)} collective-permute-done((bf16[4,64,1024]{2,1,0:T(8,128)(2,1)S(1)}, bf16[4,64,1024]{2,1,0:T(8,128)(2,1)S(1)}, u32[]{:S(2)}, u32[]{:S(2)}) %collective-permute-start.14) | collective-permute-done | bytes 524320 | tf_op jit(solution)/shard_map/ppermute | solution.py:1015
  63.1 2.9 %forward.3 = (bf16[2,3,64,512]{3,2,1,0:T(8,128)(2,1)S(1)}, f32[2,3,64,512]{3,2,1,0:T(8,128)S(1)}, bf16[512,1024]{1,0:T(8,128)(2,1)S(1)}, bf16[1024,512]{1,0:T(8,128)(2,1)S(1)}, f32[8,1024]{1,0:T(8,128)S(1)}) custom-call(bf16[1024,512]{1,0:T(8,128)(2,1)S(1)} %get-tuple-element.56.refs_0_, bf16[3,2,64,1024]{3,2,1,0:T(8,128)(2,1)S(1)} %pack.7.refs_1_, ...), custom_call_target="tpu_custom_call" | custom-call | flops 1048576 | bytes 65536 | tf_op jit(solution)/shard_map/forward/pallas_call | solution.py:652
  67.6 2.8 %up_gradient.2 = (bf16[4,4,64,1024]{3,2,1,0:T(8,128)(2,1)S(1)}, f32[1,1024]{1,0:T(1,128)S(1)}) custom-call(bf16[13,2,64,1024]{3,2,1,0:T(8,128)(2,1)S(1)} %collective-permute-done.11.refs_2_.refs_0_, bf16[3,2,64,1024]{3,2,1,0:T(8,128)(2,1)S(1)} %collective-permute-done.13.refs_2_.refs_1_, f32[2,13,64,512]{3,2,1,0:T(8,128)S(1)} %get-tuple-element.59.refs_2_, ...), custom_call_target="tpu_custom_call" | custom-call | flops 1048576 | bytes 65536 | tf_op jit(solution)/shard_map/up_gradient/pallas_call | solution.py:844
  74.6 3.3 %up_gradient.3 = (bf16[4,64,1024]{2,1,0:T(8,128)(2,1)S(1)}, bf16[4,64,1024]{2,1,0:T(8,128)(2,1)S(1)}, bf16[4,64,1024]{2,1,0:T(8,128)(2,1)S(1)}, bf16[2,64,1024]{...) custom-call(bf16[13,2,64,1024]{3,2,1,0:T(8,128)(2,1)S(1)} %pack.6.refs_1_.refs_0_, ...), custom_call_target="tpu_custom_call" | custom-call | flops 1048576 | bytes 65536 | tf_op jit(solution)/shard_map/up_gradient/pallas_call | solution.py:844
  81.6 2.4 %collective-permute-start.24 = (f32[8,1024]{1,0:T(8,128)S(1)}, f32[8,1024]{1,0:T(8,128)S(1)}, u32[]{:S(2)}, u32[]{:S(2)}) collective-permute-start(f32[8,1024]{1,0:T(8,128)S(1)} %add.9), channel_id=1, source_target_pairs={{0,2},{1,3},{2,0},{3,1},{4,6},{5,7},{6,4},{7,5},{8,10},{9,11},{10,... | collective-permute-start | bytes 98312 | tf_op jit(solution)/shard_map/ppermute | solution.py:1015
  84.0 1.9 %collective-permute-done.24 = f32[8,1024]{1,0:T(8,128)S(1)} collective-permute-done((f32[8,1024]{1,0:T(8,128)S(1)}, f32[8,1024]{1,0:T(8,128)S(1)}, u32[]{:S(2)}, u32[]{:S(2)}) %collective-permute-start.24) | collective-permute-done | bytes 32800 | tf_op jit(solution)/shard_map/ppermute | solution.py:1015
  85.9 2.9 %collective-permute-start.25 = (f32[8,1024]{1,0:T(8,128)S(1)}, f32[8,1024]{1,0:T(8,128)S(1)}, u32[]{:S(2)}, u32[]{:S(2)}) collective-permute-start(f32[8,1024]{1,0:T(8,128)S(1)} %add.10), channel_id=1, source_target_pairs={{0,4},{1,5},{2,6},{3,7},{4,0},{5,1},{6,2},{7,3},{8,12},{9,13},{10,... | collective-permute-start | bytes 98312 | tf_op jit(solution)/shard_map/ppermute | solution.py:1015
  88.7 2.0 %collective-permute-done.25 = f32[8,1024]{1,0:T(8,128)S(1)} collective-permute-done((f32[8,1024]{1,0:T(8,128)S(1)}, f32[8,1024]{1,0:T(8,128)S(1)}, u32[]{:S(2)}, u32[]{:S(2)}) %collective-permute-start.25) | collective-permute-done | bytes 32800 | tf_op jit(solution)/shard_map/ppermute | solution.py:1015
  93.0 6.0 %collective-permute-done.16.x_ref = bf16[4,64,1024]{2,1,0:T(8,128)(2,1)S(1)} collective-permute-done((bf16[4,64,1024]{2,1,0:T(8,128)(2,1)S(1)}, bf16[4,64,1024]{2,1,0:T(8,128)(2,1)S(1)}, u32[]{:S(2)}, u32[]{:S(2)}) %collective-permute-start.16) | collective-permute-done | bytes 524320 | tf_op jit(solution)/shard_map/ppermute | solution.py:1012
  101.8 2.8 %collective-permute-done.29.x_late_ref = bf16[2,64,1024]{2,1,0:T(8,128)(2,1)S(1)} collective-permute-done((bf16[2,64,1024]{2,1,0:T(8,128)(2,1)S(1)}, bf16[2,64,1024]{2,1,0:T(8,128)(2,1)S(1)}, u32[]{:S(2)}, u32[]{:S(2)}) %collective-permute-start.29) | collective-permute-done | bytes 262176 | tf_op jit(solution)/shard_map/ppermute | solution.py:1012
  106.7 3.5 %collective-permute-start.32 = (bf16[64,1024]{1,0:T(8,128)(2,1)S(1)}, bf16[64,1024]{1,0:T(8,128)(2,1)S(1)}, u32[]{:S(2)}, u32[]{:S(2)}) collective-permute-start(bf16[64,1024]{1,0:T(8,128)(2,1)S(1)} %get-tuple-element.90), channel_id=1, source_target_pairs={{0,4},{1,5},{2,6},{3,7},{4,0},{5,1},{6,2},{7,3},{8,12},{9,13},{10,... | collective-permute-start | bytes 393224 | tf_op jit(solution)/shard_map/ppermute | solution.py:1019
  110.9 1.6 %collective-permute-start.20 = (bf16[64,1024]{1,0:T(8,128)(2,1)S(1)}, bf16[64,1024]{1,0:T(8,128)(2,1)S(1)}, u32[]{:S(2)}, u32[]{:S(2)}) collective-permute-start(bf16[64,1024]{1,0:T(8,128)(2,1)S(1)} %get-tuple-element.74), channel_id=1, source_target_pairs={{0,2},{1,3},{2,4},{3,5},{4,6},{5,7},{6,0},{7,1},{8,10},{9,11},{10,... | collective-permute-start | bytes 393224 | tf_op jit(solution)/shard_map/ppermute | solution.py:1019
  112.5 2.2 %collective-permute-start.21 = (bf16[64,1024]{1,0:T(8,128)(2,1)S(1)}, bf16[64,1024]{1,0:T(8,128)(2,1)S(1)}, u32[]{:S(2)}, u32[]{:S(2)}) collective-permute-start(bf16[64,1024]{1,0:T(8,128)(2,1)S(1)} %get-tuple-element.75), channel_id=1, source_target_pairs={{0,4},{1,5},{2,6},{3,7},{4,0},{5,1},{6,2},{7,3},{8,12},{9,13},{10,... | collective-permute-start | bytes 393224 | tf_op jit(solution)/shard_map/ppermute | solution.py:1019
  115.8 8.6 %collective-permute-done.32.refs_2_ = bf16[64,1024]{1,0:T(8,128)(2,1)S(1)} collective-permute-done((bf16[64,1024]{1,0:T(8,128)(2,1)S(1)}, bf16[64,1024]{1,0:T(8,128)(2,1)S(1)}, u32[]{:S(2)}, u32[]{:S(2)}) %collective-permute-start.32) | collective-permute-done | bytes 131104 | tf_op jit(solution)/shard_map/ppermute | solution.py:1019
  132.3 1.6 %collective-permute-start.38 = (bf16[144,1024]{1,0:T(8,128)(2,1)S(1)}, bf16[144,1024]{1,0:T(8,128)(2,1)S(1)}, u32[]{:S(2)}, u32[]{:S(2)}) collective-permute-start(bf16[144,1024]{1,0:T(8,128)(2,1)S(1)} %get-tuple-element.93), channel_id=1, source_target_pairs={{0,24},{8,16},{16,8},{24,0},{1,25},{9,17},{17,9},{25,1},{2,26},{10... | collective-permute-start | bytes 884744 | tf_op jit(solution)/shard_map/ppermute | solution.py:1012
  135.8 7.3 %collective-permute-done.36.refs_1_ = bf16[80,1024]{1,0:T(8,128)(2,1)S(1)} collective-permute-done((bf16[80,1024]{1,0:T(8,128)(2,1)S(1)}, bf16[80,1024]{1,0:T(8,128)(2,1)S(1)}, u32[]{:S(2)}, u32[]{:S(2)}) %collective-permute-start.36) | collective-permute-done | bytes 163872 | tf_op jit(solution)/shard_map/ppermute | solution.py:1012
  143.1 1.7 %place.1 = (f32[1024,256]{1,0:T(8,128)}, f32[256,1024]{1,0:T(8,128)}, f32[1,1024]{1,0:T(1,128)}, f32[1,1024]{1,0:T(1,128)}, f32[1,1]{1,0:T(1,128)}) custom-call(s32[1]{0:T(128)} %bitcast.group_ref, bf16[80,1024]{1,0:T(8,128)(2,1)S(1)} %get-tuple-element.92.refs_0_, bf16[80,1024]{1,0:T(8,128)(2,1)S(1)} %collective-permute-done.36.refs_1_, ...), custom_call_target="tpu_custom_call" | custom-call | flops 1048576 | bytes 65536 | tf_op jit(solution)/shard_map/place/pallas_call | solution.py:978
  (100 shorter events, 37.6 us)
Async XLA Ops:
  3.1 20.5 %collective-permute-start = (bf16[2,64,1024]{2,1,0:T(8,128)(2,1)S(1)}, bf16[2,64,1024]{2,1,0:T(8,128)(2,1)S(1)}, u32[]{:S(2)}, u32[]{:S(2)}) collective-permute-start(bf16[2,64,1024]{2,1,0:T(8,128)(2,1)S(1)} %quarter.1), channel_id=1, source_target_pairs={{0,6},{1,7},{2,0},{3,1},{4,2},{5,3},{6,4},{7,5},{8,14},{9,15},{10,... | collective-permute-start | bytes 786440 | tf_op jit(solution)/shard_map/ppermute | solution.py:1019
  3.2 23.5 %collective-permute-start.3 = (bf16[2,64,1024]{2,1,0:T(8,128)(2,1)S(1)}, bf16[2,64,1024]{2,1,0:T(8,128)(2,1)S(1)}, u32[]{:S(2)}, u32[]{:S(2)}) collective-permute-start(bf16[2,64,1024]{2,1,0:T(8,128)(2,1)S(1)} %quarter.1), channel_id=1, source_target_pairs={{0,4},{1,5},{2,6},{3,7},{4,0},{5,1},{6,2},{7,3},{8,12},{9,13},{10,... | collective-permute-start | bytes 786440 | tf_op jit(solution)/shard_map/ppermute | solution.py:1019
  6.2 22.2 %collective-permute-start.4 = (bf16[2,64,1024]{2,1,0:T(8,128)(2,1)S(1)}, bf16[2,64,1024]{2,1,0:T(8,128)(2,1)S(1)}, u32[]{:S(2)}, u32[]{:S(2)}) collective-permute-start(bf16[2,64,1024]{2,1,0:T(8,128)(2,1)S(1)} %quarter.1), channel_id=1, source_target_pairs={{0,2},{1,3},{2,4},{3,5},{4,6},{5,7},{6,0},{7,1},{8,10},{9,11},{10,... | collective-permute-start | bytes 786440 | tf_op jit(solution)/shard_map/ppermute | solution.py:1019
  23.6 6.4 %collective-permute-start.2 = (bf16[1,2,64,1024]{3,2,1,0:T(8,128)(2,1)S(1)}, bf16[1,2,64,1024]{3,2,1,0:T(8,128)(2,1)S(1)}, u32[]{:S(2)}, u32[]{:S(2)}) collective-permute-start(bf16[1,2,64,1024]{3,2,1,0:T(8,128)(2,1)S(1)} %pack.4.refs_2_.refs_1_), channel_id=1, source_target_pairs={{0,16},{8,24},{16,0},{24,8},{1,17},{9,25},{17,1},{25,9},{2,18},{10... | collective-permute-start | bytes 786440 | tf_op jit(solution)/shard_map/ppermute | solution.py:1012
  25.2 7.5 %collective-permute-start.1 = (bf16[1,2,64,1024]{3,2,1,0:T(8,128)(2,1)S(1)}, bf16[1,2,64,1024]{3,2,1,0:T(8,128)(2,1)S(1)}, u32[]{:S(2)}, u32[]{:S(2)}) collective-permute-start(bf16[1,2,64,1024]{3,2,1,0:T(8,128)(2,1)S(1)} %pack.4.refs_2_.refs_1_), channel_id=1, source_target_pairs={{0,8},{8,0},{16,24},{24,16},{1,9},{9,1},{17,25},{25,17},{2,10},{10... | collective-permute-start | bytes 786440 | tf_op jit(solution)/shard_map/ppermute | solution.py:1012
  32.7 12.6 %collective-permute-start.5 = (bf16[2,2,64,1024]{3,2,1,0:T(8,128)(2,1)S(1)}, bf16[2,2,64,1024]{3,2,1,0:T(8,128)(2,1)S(1)}, u32[]{:S(2)}, u32[]{:S(2)}) collective-permute-start(bf16[2,2,64,1024]{3,2,1,0:T(8,128)(2,1)S(1)} %tie.1.refs_4_), channel_id=1, source_target_pairs={{0,8},{8,0},{16,24},{24,16},{1,9},{9,1},{17,25},{25,17},{2,10},{10... | collective-permute-start | bytes 1572872 | tf_op jit(solution)/shard_map/ppermute | solution.py:1012
  34.2 11.1 %collective-permute-start.6 = (bf16[2,2,64,1024]{3,2,1,0:T(8,128)(2,1)S(1)}, bf16[2,2,64,1024]{3,2,1,0:T(8,128)(2,1)S(1)}, u32[]{:S(2)}, u32[]{:S(2)}) collective-permute-start(bf16[2,2,64,1024]{3,2,1,0:T(8,128)(2,1)S(1)} %tie.1.refs_4_), channel_id=1, source_target_pairs={{0,16},{8,24},{16,0},{24,8},{1,17},{9,25},{17,1},{25,9},{2,18},{10... | collective-permute-start | bytes 1572872 | tf_op jit(solution)/shard_map/ppermute | solution.py:1012
  34.2 9.9 %collective-permute-start.7 = (bf16[2,64,1024]{2,1,0:T(8,128)(2,1)S(1)}, bf16[2,64,1024]{2,1,0:T(8,128)(2,1)S(1)}, u32[]{:S(2)}, u32[]{:S(2)}) collective-permute-start(bf16[2,64,1024]{2,1,0:T(8,128)(2,1)S(1)} %get-tuple-element.54), channel_id=1, source_target_pairs={{0,2},{1,3},{2,4},{3,5},{4,6},{5,7},{6,0},{7,1},{8,10},{9,11},{10,... | collective-permute-start | bytes 786440 | tf_op jit(solution)/shard_map/ppermute | solution.py:1019
  34.2 11.1 %collective-permute-start.8 = (bf16[2,64,1024]{2,1,0:T(8,128)(2,1)S(1)}, bf16[2,64,1024]{2,1,0:T(8,128)(2,1)S(1)}, u32[]{:S(2)}, u32[]{:S(2)}) collective-permute-start(bf16[2,64,1024]{2,1,0:T(8,128)(2,1)S(1)} %get-tuple-element.55), channel_id=1, source_target_pairs={{0,6},{1,7},{2,0},{3,1},{4,2},{5,3},{6,4},{7,5},{8,14},{9,15},{10,... | collective-permute-start | bytes 786440 | tf_op jit(solution)/shard_map/ppermute | solution.py:1019
  45.6 6.1 %collective-permute-start.11 = (bf16[13,2,64,1024]{3,2,1,0:T(8,128)(2,1)S(1)}, bf16[13,2,64,1024]{3,2,1,0:T(8,128)(2,1)S(1)}, u32[]{:S(2)}, u32[]{:S(2)}) collective-permute-start(bf16[13,2,64,1024]{3,2,1,0:T(8,128)(2,1)S(1)} %pack.6.refs_1_.refs_0_), channel_id=1, source_target_pairs={{0,1},{1,0},{2,3},{3,2},{4,5},{5,4},{6,7},{7,6},{8,9},{9,8},{10,11... | collective-permute-start | bytes 10223624 | tf_op jit(solution)/shard_map/ppermute | solution.py:1015
  45.6 14.3 %collective-permute-start.10 = (bf16[2,2,64,1024]{3,2,1,0:T(8,128)(2,1)S(1)}, bf16[2,2,64,1024]{3,2,1,0:T(8,128)(2,1)S(1)}, u32[]{:S(2)}, u32[]{:S(2)}) collective-permute-start(bf16[2,2,64,1024]{3,2,1,0:T(8,128)(2,1)S(1)} %collective-permute-done.5.refs_5_), channel_id=1, source_target_pairs={{0,16},{8,24},{16,0},{24,8},{1,17},{9,25},{17,1},{25,9},{2,18},{10... | collective-permute-start | bytes 1572872 | tf_op jit(solution)/shard_map/ppermute | solution.py:1012
  46.2 13.6 %collective-permute-start.12 = (bf16[2,64,1024]{2,1,0:T(8,128)(2,1)S(1)}, bf16[2,64,1024]{2,1,0:T(8,128)(2,1)S(1)}, u32[]{:S(2)}, u32[]{:S(2)}) collective-permute-start(bf16[2,64,1024]{2,1,0:T(8,128)(2,1)S(1)} %get-tuple-element.58), channel_id=1, source_target_pairs={{0,4},{1,5},{2,6},{3,7},{4,0},{5,1},{6,2},{7,3},{8,12},{9,13},{10,... | collective-permute-start | bytes 786440 | tf_op jit(solution)/shard_map/ppermute | solution.py:1019
  48.3 11.5 %collective-permute-start.9 = (bf16[1,2,64,1024]{3,2,1,0:T(8,128)(2,1)S(1)}, bf16[1,2,64,1024]{3,2,1,0:T(8,128)(2,1)S(1)}, u32[]{:S(2)}, u32[]{:S(2)}) collective-permute-start(bf16[1,2,64,1024]{3,2,1,0:T(8,128)(2,1)S(1)} %collective-permute-done.2.refs_2_.refs_3_), channel_id=1, source_target_pairs={{0,8},{8,0},{16,24},{24,16},{1,9},{9,1},{17,25},{25,17},{2,10},{10... | collective-permute-start | bytes 786440 | tf_op jit(solution)/shard_map/ppermute | solution.py:1012
  72.9 17.8 %collective-permute-start.27 = (bf16[4,64,1024]{2,1,0:T(8,128)(2,1)S(1)}, bf16[4,64,1024]{2,1,0:T(8,128)(2,1)S(1)}, u32[]{:S(2)}, u32[]{:S(2)}) collective-permute-start(bf16[4,64,1024]{2,1,0:T(8,128)(2,1)S(1)} %get-tuple-element.82), channel_id=1, source_target_pairs={{0,8},{8,0},{16,24},{24,16},{1,9},{9,1},{17,25},{25,17},{2,10},{10... | collective-permute-start | bytes 1572872 | tf_op jit(solution)/shard_map/ppermute | solution.py:1012
  73.5 17.2 %collective-permute-start.28 = (bf16[4,64,1024]{2,1,0:T(8,128)(2,1)S(1)}, bf16[4,64,1024]{2,1,0:T(8,128)(2,1)S(1)}, u32[]{:S(2)}, u32[]{:S(2)}) collective-permute-start(bf16[4,64,1024]{2,1,0:T(8,128)(2,1)S(1)} %get-tuple-element.83), channel_id=1, source_target_pairs={{0,16},{8,24},{16,0},{24,8},{1,17},{9,25},{17,1},{25,9},{2,18},{10... | collective-permute-start | bytes 1572872 | tf_op jit(solution)/shard_map/ppermute | solution.py:1012
  77.9 21.1 %collective-permute-start.16 = (bf16[4,64,1024]{2,1,0:T(8,128)(2,1)S(1)}, bf16[4,64,1024]{2,1,0:T(8,128)(2,1)S(1)}, u32[]{:S(2)}, u32[]{:S(2)}) collective-permute-start(bf16[4,64,1024]{2,1,0:T(8,128)(2,1)S(1)} %get-tuple-element.67), channel_id=1, source_target_pairs={{0,8},{8,0},{16,24},{24,16},{1,9},{9,1},{17,25},{25,17},{2,10},{10... | collective-permute-start | bytes 1572872 | tf_op jit(solution)/shard_map/ppermute | solution.py:1012
  78.9 20.7 %collective-permute-start.17 = (bf16[4,64,1024]{2,1,0:T(8,128)(2,1)S(1)}, bf16[4,64,1024]{2,1,0:T(8,128)(2,1)S(1)}, u32[]{:S(2)}, u32[]{:S(2)}) collective-permute-start(bf16[4,64,1024]{2,1,0:T(8,128)(2,1)S(1)} %get-tuple-element.68), channel_id=1, source_target_pairs={{0,16},{8,24},{16,0},{24,8},{1,17},{9,25},{17,1},{25,9},{2,18},{10... | collective-permute-start | bytes 1572872 | tf_op jit(solution)/shard_map/ppermute | solution.py:1012
  90.9 13.7 %collective-permute-start.29 = (bf16[2,64,1024]{2,1,0:T(8,128)(2,1)S(1)}, bf16[2,64,1024]{2,1,0:T(8,128)(2,1)S(1)}, u32[]{:S(2)}, u32[]{:S(2)}) collective-permute-start(bf16[2,64,1024]{2,1,0:T(8,128)(2,1)S(1)} %get-tuple-element.86), channel_id=1, source_target_pairs={{0,8},{8,0},{16,24},{24,16},{1,9},{9,1},{17,25},{25,17},{2,10},{10... | collective-permute-start | bytes 786440 | tf_op jit(solution)/shard_map/ppermute | solution.py:1012
  92.0 13.1 %collective-permute-start.30 = (bf16[2,64,1024]{2,1,0:T(8,128)(2,1)S(1)}, bf16[2,64,1024]{2,1,0:T(8,128)(2,1)S(1)}, u32[]{:S(2)}, u32[]{:S(2)}) collective-permute-start(bf16[2,64,1024]{2,1,0:T(8,128)(2,1)S(1)} %get-tuple-element.87), channel_id=1, source_target_pairs={{0,16},{8,24},{16,0},{24,8},{1,17},{9,25},{17,1},{25,9},{2,18},{10... | collective-permute-start | bytes 786440 | tf_op jit(solution)/shard_map/ppermute | solution.py:1012
  99.7 11.0 %collective-permute-start.18 = (bf16[2,64,1024]{2,1,0:T(8,128)(2,1)S(1)}, bf16[2,64,1024]{2,1,0:T(8,128)(2,1)S(1)}, u32[]{:S(2)}, u32[]{:S(2)}) collective-permute-start(bf16[2,64,1024]{2,1,0:T(8,128)(2,1)S(1)} %get-tuple-element.71), channel_id=1, source_target_pairs={{0,8},{8,0},{16,24},{24,16},{1,9},{9,1},{17,25},{25,17},{2,10},{10... | collective-permute-start | bytes 786440 | tf_op jit(solution)/shard_map/ppermute | solution.py:1012
  101.2 9.5 %collective-permute-start.19 = (bf16[2,64,1024]{2,1,0:T(8,128)(2,1)S(1)}, bf16[2,64,1024]{2,1,0:T(8,128)(2,1)S(1)}, u32[]{:S(2)}, u32[]{:S(2)}) collective-permute-start(bf16[2,64,1024]{2,1,0:T(8,128)(2,1)S(1)} %get-tuple-element.72), channel_id=1, source_target_pairs={{0,16},{8,24},{16,0},{24,8},{1,17},{9,25},{17,1},{25,9},{2,18},{10... | collective-permute-start | bytes 786440 | tf_op jit(solution)/shard_map/ppermute | solution.py:1012
  105.4 9.3 %collective-permute-start.31 = (bf16[64,1024]{1,0:T(8,128)(2,1)S(1)}, bf16[64,1024]{1,0:T(8,128)(2,1)S(1)}, u32[]{:S(2)}, u32[]{:S(2)}) collective-permute-start(bf16[64,1024]{1,0:T(8,128)(2,1)S(1)} %get-tuple-element.89), channel_id=1, source_target_pairs={{0,2},{1,3},{2,4},{3,5},{4,6},{5,7},{6,0},{7,1},{8,10},{9,11},{10,... | collective-permute-start | bytes 393224 | tf_op jit(solution)/shard_map/ppermute | solution.py:1019
  106.7 17.8 %collective-permute-start.32 = (bf16[64,1024]{1,0:T(8,128)(2,1)S(1)}, bf16[64,1024]{1,0:T(8,128)(2,1)S(1)}, u32[]{:S(2)}, u32[]{:S(2)}) collective-permute-start(bf16[64,1024]{1,0:T(8,128)(2,1)S(1)} %get-tuple-element.90), channel_id=1, source_target_pairs={{0,4},{1,5},{2,6},{3,7},{4,0},{5,1},{6,2},{7,3},{8,12},{9,13},{10,... | collective-permute-start | bytes 393224 | tf_op jit(solution)/shard_map/ppermute | solution.py:1019
  110.2 15.5 %collective-permute-start.33 = (bf16[64,1024]{1,0:T(8,128)(2,1)S(1)}, bf16[64,1024]{1,0:T(8,128)(2,1)S(1)}, u32[]{:S(2)}, u32[]{:S(2)}) collective-permute-start(bf16[64,1024]{1,0:T(8,128)(2,1)S(1)} %get-tuple-element.91), channel_id=1, source_target_pairs={{0,6},{1,7},{2,0},{3,1},{4,2},{5,3},{6,4},{7,5},{8,14},{9,15},{10,... | collective-permute-start | bytes 393224 | tf_op jit(solution)/shard_map/ppermute | solution.py:1019
  110.9 17.9 %collective-permute-start.20 = (bf16[64,1024]{1,0:T(8,128)(2,1)S(1)}, bf16[64,1024]{1,0:T(8,128)(2,1)S(1)}, u32[]{:S(2)}, u32[]{:S(2)}) collective-permute-start(bf16[64,1024]{1,0:T(8,128)(2,1)S(1)} %get-tuple-element.74), channel_id=1, source_target_pairs={{0,2},{1,3},{2,4},{3,5},{4,6},{5,7},{6,0},{7,1},{8,10},{9,11},{10,... | collective-permute-start | bytes 393224 | tf_op jit(solution)/shard_map/ppermute | solution.py:1019
  112.5 16.4 %collective-permute-start.21 = (bf16[64,1024]{1,0:T(8,128)(2,1)S(1)}, bf16[64,1024]{1,0:T(8,128)(2,1)S(1)}, u32[]{:S(2)}, u32[]{:S(2)}) collective-permute-start(bf16[64,1024]{1,0:T(8,128)(2,1)S(1)} %get-tuple-element.75), channel_id=1, source_target_pairs={{0,4},{1,5},{2,6},{3,7},{4,0},{5,1},{6,2},{7,3},{8,12},{9,13},{10,... | collective-permute-start | bytes 393224 | tf_op jit(solution)/shard_map/ppermute | solution.py:1019
  114.7 15.7 %collective-permute-start.22 = (bf16[64,1024]{1,0:T(8,128)(2,1)S(1)}, bf16[64,1024]{1,0:T(8,128)(2,1)S(1)}, u32[]{:S(2)}, u32[]{:S(2)}) collective-permute-start(bf16[64,1024]{1,0:T(8,128)(2,1)S(1)} %get-tuple-element.76), channel_id=1, source_target_pairs={{0,6},{1,7},{2,0},{3,1},{4,2},{5,3},{6,4},{7,5},{8,14},{9,15},{10,... | collective-permute-start | bytes 393224 | tf_op jit(solution)/shard_map/ppermute | solution.py:1019
  125.8 5.0 %collective-permute-start.34 = (bf16[64,1024]{1,0:T(8,128)(2,1)S(1)}, bf16[64,1024]{1,0:T(8,128)(2,1)S(1)}, u32[]{:S(2)}, u32[]{:S(2)}) collective-permute-start(bf16[64,1024]{1,0:T(8,128)(2,1)S(1)} %collect.3.other_ref.refs_4_), channel_id=1, source_target_pairs={{0,8},{8,0},{16,24},{24,16},{1,9},{9,1},{17,25},{25,17},{2,10},{10... | collective-permute-start | bytes 393224 | tf_op jit(solution)/shard_map/ppermute | solution.py:1012
  127.2 5.0 %collective-permute-start.35 = (bf16[64,1024]{1,0:T(8,128)(2,1)S(1)}, bf16[64,1024]{1,0:T(8,128)(2,1)S(1)}, u32[]{:S(2)}, u32[]{:S(2)}) collective-permute-start(bf16[64,1024]{1,0:T(8,128)(2,1)S(1)} %collect.3.other_ref.refs_4_), channel_id=1, source_target_pairs={{0,16},{8,24},{16,0},{24,8},{1,17},{9,25},{17,1},{25,9},{2,18},{10... | collective-permute-start | bytes 393224 | tf_op jit(solution)/shard_map/ppermute | solution.py:1012
  132.3 10.8 %collective-permute-start.38 = (bf16[144,1024]{1,0:T(8,128)(2,1)S(1)}, bf16[144,1024]{1,0:T(8,128)(2,1)S(1)}, u32[]{:S(2)}, u32[]{:S(2)}) collective-permute-start(bf16[144,1024]{1,0:T(8,128)(2,1)S(1)} %get-tuple-element.93), channel_id=1, source_target_pairs={{0,24},{8,16},{16,8},{24,0},{1,25},{9,17},{17,9},{25,1},{2,26},{10... | collective-permute-start | bytes 884744 | tf_op jit(solution)/shard_map/ppermute | solution.py:1012
  133.9 9.2 %collective-permute-start.36 = (bf16[80,1024]{1,0:T(8,128)(2,1)S(1)}, bf16[80,1024]{1,0:T(8,128)(2,1)S(1)}, u32[]{:S(2)}, u32[]{:S(2)}) collective-permute-start(bf16[80,1024]{1,0:T(8,128)(2,1)S(1)} %get-tuple-element.92.refs_0_), channel_id=1, source_target_pairs={{0,8},{8,0},{16,24},{24,16},{1,9},{9,1},{17,25},{25,17},{2,10},{10... | collective-permute-start | bytes 491528 | tf_op jit(solution)/shard_map/ppermute | solution.py:1012
  135.3 7.8 %collective-permute-start.37 = (bf16[80,1024]{1,0:T(8,128)(2,1)S(1)}, bf16[80,1024]{1,0:T(8,128)(2,1)S(1)}, u32[]{:S(2)}, u32[]{:S(2)}) collective-permute-start(bf16[80,1024]{1,0:T(8,128)(2,1)S(1)} %get-tuple-element.92.refs_0_), channel_id=1, source_target_pairs={{0,16},{8,24},{16,0},{24,8},{1,17},{9,25},{17,1},{25,9},{2,18},{10... | collective-permute-start | bytes 491528 | tf_op jit(solution)/shard_map/ppermute | solution.py:1012
  (20 other events, 120.3 us)

commit v17 on v16

--- a/solution.py
+++ b/solution.py
@@ -528,7 +528,7 @@
             pltpu.VMEM((lanes, width), BF16),
             pltpu.SemaphoreType.DMA((2,)),
         ],
-        compiler_params=params(16),
+        compiler_params=params(56),
         cost_estimate=LONG,
         name="quarter",
     )(group, up, down)

time: 145 us -> 145 us (level)
  local copies, waits for them, and re-layouts: 2.13 us -> 0.06 us
    unnamed x26 -> x22, local copies, waits for them, and re-layouts: 2.13 us -> 0.05 us
    pallas_call x1, Pallas kernels: 0.38 us -> 1.95 us  [own_quarter(): pl.pallas_call(quarter_kernel, out_shape=jax.ShapeDtypeStruct((2, part, w...]
  transfers between devices with their start and end apart: 39 -> 39, of which waited for: 25 -> 27; matrix products, arithmetic and copies ran while one was open for 0% -> 0% of each run, Pallas kernels for 17% -> 17%
where the time goes in v17:
time: 145 us
  waiting for transfers between devices  64.3 us (44%)
  starting transfers between devices  46.1 us (32%)
  Pallas kernels  33.2 us (23%)
    ppermute x12, waiting for transfers between devices, along(): return lax.ppermute(array, 'ray', pairs)  29 us
    ppermute x19, waiting for transfers between devices, beside(): lax.ppermute(array, 'grp', [(g, g ^ flip) for g in range(group_count)])  23.4 us
    ppermute x19, starting transfers between devices, beside(): lax.ppermute(array, 'grp', [(g, g ^ flip) for g in range(group_count)])  20.3 us
    ppermute x12, starting transfers between devices, along(): return lax.ppermute(array, 'ray', pairs)  19.3 us
    ppermute x8, waiting for transfers between devices, partner(): return lax.ppermute(array, 'ray', [(r, r ^ flip) for r in range(ray_count)])  11.8 us
    pallas_call x1, Pallas kernels, render(): pl.pallas_call(functools.partial(render_kernel, ray_count, relative), out...  8.41 us
    pallas_call x2, Pallas kernels, forward(): pl.pallas_call(functools.partial(forward_kernel, first, blocks, len(own),...  7.95 us
    ppermute x8, starting transfers between devices, partner(): return lax.ppermute(array, 'ray', [(r, r ^ flip) for r in range(ray_count)])  6.47 us
  transfers between devices with their start and end apart: 39, of which 27 were waited for; matrix products, arithmetic and copies ran while one was open for 0% of the time, Pallas kernels for 17%

profile of v17, /device:TPU:8, one launch (start us, length us, event | category | flops | bytes accessed | tf_op | source)
XLA Modules:
  0.0 144.5 jit_solution(15270112922305227739)
XLA Ops:
  0.7 2.0 %quarter.1 = bf16[2,64,1024]{2,1,0:T(8,128)(2,1)} custom-call(s32[1]{0:T(128)} %bitcast.group_ref, bf16[1024,256]{1,0:T(8,128)(2,1)} %up_hbm.1, bf16[256,1024]{1,0:T(8,128)(2,1)} %down_hbm.1), custom_call_target="tpu_custom_call" | custom-call | flops 10000000000 | bytes 1048576 | tf_op jit(solution)/shard_map/quarter/pallas_call | solution.py:521
  2.7 3.0 %collective-permute-start.3 = (bf16[2,64,1024]{2,1,0:T(8,128)(2,1)}, bf16[2,64,1024]{2,1,0:T(8,128)(2,1)S(1)}, u32[]{:S(2)}, u32[]{:S(2)}) collective-permute-start(bf16[2,64,1024]{2,1,0:T(8,128)(2,1)} %quarter.1), channel_id=1, source_target_pairs={{0,4},{1,5},{2,6},{3,7},{4,0},{5,1},{6,2},{7,3},{8,12},{9,13},{10,... | collective-permute-start | bytes 786440 | tf_op jit(solution)/shard_map/ppermute | solution.py:1019
  5.8 2.5 %collective-permute-start.4 = (bf16[2,64,1024]{2,1,0:T(8,128)(2,1)}, bf16[2,64,1024]{2,1,0:T(8,128)(2,1)S(1)}, u32[]{:S(2)}, u32[]{:S(2)}) collective-permute-start(bf16[2,64,1024]{2,1,0:T(8,128)(2,1)} %quarter.1), channel_id=1, source_target_pairs={{0,2},{1,3},{2,4},{3,5},{4,6},{5,7},{6,0},{7,1},{8,10},{9,11},{10,... | collective-permute-start | bytes 786440 | tf_op jit(solution)/shard_map/ppermute | solution.py:1019
  8.3 8.4 %render.1 = (bf16[2,64,1024]{2,1,0:T(8,128)(2,1)S(1)}, bf16[2,64,1024]{2,1,0:T(8,128)(2,1)S(1)}, bf16[2,64,1024]{2,1,0:T(8,128)(2,1)S(1)}, bf16[2,64,1024]{2,1,0:T(8,128)(2,1)S(1)}) custom-call(s32[1]{0:T(128)} %bitcast.1.me_ref, s32[1,8]{1,0:T(1,128)S(1)} %copy-done.9, s32[32,512]{1,0:T(8,128)S(1)} %copy-done.5, f32[32,512]{1,0:T(8,128)S(1)} %copy-done.6, ...), custom_call_target="tpu_custom_call" | custom-call | flops 1048576 | bytes 65536 | tf_op jit(solution)/shard_map/render/pallas_call | solution.py:152
  16.7 6.6 %collective-permute-done.refs_0_ = bf16[2,64,1024]{2,1,0:T(8,128)(2,1)S(1)} collective-permute-done((bf16[2,64,1024]{2,1,0:T(8,128)(2,1)}, bf16[2,64,1024]{2,1,0:T(8,128)(2,1)S(1)}, u32[]{:S(2)}, u32[]{:S(2)}) %collective-permute-start) | collective-permute-done | bytes 262176 | tf_op jit(solution)/shard_map/ppermute | solution.py:1019
  23.4 1.6 %collective-permute-start.2 = (bf16[1,2,64,1024]{3,2,1,0:T(8,128)(2,1)S(1)}, bf16[1,2,64,1024]{3,2,1,0:T(8,128)(2,1)S(1)}, u32[]{:S(2)}, u32[]{:S(2)}) collective-permute-start(bf16[1,2,64,1024]{3,2,1,0:T(8,128)(2,1)S(1)} %pack.4.refs_2_.refs_1_), channel_id=1, source_target_pairs={{0,16},{8,24},{16,0},{24,8},{1,17},{9,25},{17,1},{25,9},{2,18},{10... | collective-permute-start | bytes 786440 | tf_op jit(solution)/shard_map/ppermute | solution.py:1012
  26.5 1.8 %collective-permute-done.4.refs_1_ = bf16[2,64,1024]{2,1,0:T(8,128)(2,1)S(1)} collective-permute-done((bf16[2,64,1024]{2,1,0:T(8,128)(2,1)}, bf16[2,64,1024]{2,1,0:T(8,128)(2,1)S(1)}, u32[]{:S(2)}, u32[]{:S(2)}) %collective-permute-start.4) | collective-permute-done | bytes 262176 | tf_op jit(solution)/shard_map/ppermute | solution.py:1019
  29.8 2.5 %collective-permute-done.1.refs_1_.refs_2_ = bf16[1,2,64,1024]{3,2,1,0:T(8,128)(2,1)S(1)} collective-permute-done((bf16[1,2,64,1024]{3,2,1,0:T(8,128)(2,1)S(1)}, bf16[1,2,64,1024]{3,2,1,0:T(8,128)(2,1)S(1)}, u32[]{:S(2)}, u32[]{:S(2)}) %collective-permute-start.1) | collective-permute-done | bytes 262176 | tf_op jit(solution)/shard_map/ppermute | solution.py:1012
  33.9 2.0 %collective-permute-start.8 = (bf16[2,64,1024]{2,1,0:T(8,128)(2,1)S(1)}, bf16[2,64,1024]{2,1,0:T(8,128)(2,1)S(1)}, u32[]{:S(2)}, u32[]{:S(2)}) collective-permute-start(bf16[2,64,1024]{2,1,0:T(8,128)(2,1)S(1)} %get-tuple-element.55), channel_id=1, source_target_pairs={{0,6},{1,7},{2,0},{3,1},{4,2},{5,3},{6,4},{7,5},{8,14},{9,15},{10,... | collective-permute-start | bytes 786440 | tf_op jit(solution)/shard_map/ppermute | solution.py:1019
  36.1 3.2 %tokens.1 = (bf16[512,1024]{1,0:T(8,128)(2,1)S(1)}, bf16[512,1024]{1,0:T(8,128)(2,1)S(1)}, bf16[1024,512]{1,0:T(8,128)(2,1)S(1)}) custom-call(s32[1]{0:T(128)} %bitcast.1.me_ref, s32[1,8]{1,0:T(1,128)S(1)} %copy-done.9, s32[1,4096]{1,0:T(1,128)S(1)} %copy-done.4, bf16[512,1024]{1,0:T(8,128)(2,1)S(1)} %copy-done.1, f32[1,1024]{1,0:T(1,128)S(1)} %bitcast.8), custom_call_target="tpu_custom_call" | custom-call | flops 1048576 | bytes 65536 | tf_op jit(solution)/shard_map/tokens/pallas_call | solution.py:238
  39.4 4.4 %collective-permute-done.7.refs_8_.refs_1_.refs_7_ = bf16[2,64,1024]{2,1,0:T(8,128)(2,1)S(1)} collective-permute-done((bf16[2,64,1024]{2,1,0:T(8,128)(2,1)S(1)}, bf16[2,64,1024]{2,1,0:T(8,128)(2,1)S(1)}, u32[]{:S(2)}, u32[]{:S(2)}) %collective-permute-start.7) | collective-permute-done | bytes 262176 | tf_op jit(solution)/shard_map/ppermute | solution.py:1019
  45.9 2.0 %collective-permute-start.12 = (bf16[2,64,1024]{2,1,0:T(8,128)(2,1)S(1)}, bf16[2,64,1024]{2,1,0:T(8,128)(2,1)S(1)}, u32[]{:S(2)}, u32[]{:S(2)}) collective-permute-start(bf16[2,64,1024]{2,1,0:T(8,128)(2,1)S(1)} %get-tuple-element.58), channel_id=1, source_target_pairs={{0,4},{1,5},{2,6},{3,7},{4,0},{5,1},{6,2},{7,3},{8,12},{9,13},{10,... | collective-permute-start | bytes 786440 | tf_op jit(solution)/shard_map/ppermute | solution.py:1019
  48.4 2.9 %collective-permute-done.11.refs_2_.refs_0_ = bf16[13,2,64,1024]{3,2,1,0:T(8,128)(2,1)S(1)} collective-permute-done((bf16[13,2,64,1024]{3,2,1,0:T(8,128)(2,1)S(1)}, bf16[13,2,64,1024]{3,2,1,0:T(8,128)(2,1)S(1)}, u32[]{:S(2)}, u32[]{:S(2)}) %collective-permute-start.11) | collective-permute-done | bytes 3407904 | tf_op jit(solution)/shard_map/ppermute | solution.py:1015
  51.4 5.0 %forward.2 = (bf16[2,13,64,512]{3,2,1,0:T(8,128)(2,1)S(1)}, f32[2,13,64,512]{3,2,1,0:T(8,128)S(1)}, f32[512,1024]{1,0:T(8,128)S(1)}) custom-call(bf16[1024,512]{1,0:T(8,128)(2,1)S(1)} %get-tuple-element.56.refs_0_, bf16[13,2,64,1024]{3,2,1,0:T(8,128)(2,1)S(1)} %pack.6.refs_1_.refs_0_, bf16[13,2,64,1024]{3,2,1,0:T(8,128)(2,1)S(1)} %collective-permute-done.11.refs_2_.refs_0_), custom_call_target="tpu_custom_call" | custom-call | flops 1048576 | bytes 65536 | tf_op jit(solution)/shard_map/forward/pallas_call | solution.py:652
  56.4 3.0 %collective-permute-done.12.refs_3_.refs_2_.refs_8_ = bf16[2,64,1024]{2,1,0:T(8,128)(2,1)S(1)} collective-permute-done((bf16[2,64,1024]{2,1,0:T(8,128)(2,1)S(1)}, bf16[2,64,1024]{2,1,0:T(8,128)(2,1)S(1)}, u32[]{:S(2)}, u32[]{:S(2)}) %collective-permute-start.12) | collective-permute-done | bytes 262176 | tf_op jit(solution)/shard_map/ppermute | solution.py:1019
  60.4 2.4 %collective-permute-done.14.refs_10_ = bf16[4,64,1024]{2,1,0:T(8,128)(2,1)S(1)} collective-permute-done((bf16[4,64,1024]{2,1,0:T(8,128)(2,1)S(1)}, bf16[4,64,1024]{2,1,0:T(8,128)(2,1)S(1)}, u32[]{:S(2)}, u32[]{:S(2)}) %collective-permute-start.14) | collective-permute-done | bytes 524320 | tf_op jit(solution)/shard_map/ppermute | solution.py:1015
  62.9 2.9 %forward.3 = (bf16[2,3,64,512]{3,2,1,0:T(8,128)(2,1)S(1)}, f32[2,3,64,512]{3,2,1,0:T(8,128)S(1)}, bf16[512,1024]{1,0:T(8,128)(2,1)S(1)}, bf16[1024,512]{1,0:T(8,128)(2,1)S(1)}, f32[8,1024]{1,0:T(8,128)S(1)}) custom-call(bf16[1024,512]{1,0:T(8,128)(2,1)S(1)} %get-tuple-element.56.refs_0_, bf16[3,2,64,1024]{3,2,1,0:T(8,128)(2,1)S(1)} %pack.7.refs_1_, ...), custom_call_target="tpu_custom_call" | custom-call | flops 1048576 | bytes 65536 | tf_op jit(solution)/shard_map/forward/pallas_call | solution.py:652
  67.3 2.7 %up_gradient.2 = (bf16[4,4,64,1024]{3,2,1,0:T(8,128)(2,1)S(1)}, f32[1,1024]{1,0:T(1,128)S(1)}) custom-call(bf16[13,2,64,1024]{3,2,1,0:T(8,128)(2,1)S(1)} %collective-permute-done.11.refs_2_.refs_0_, bf16[3,2,64,1024]{3,2,1,0:T(8,128)(2,1)S(1)} %collective-permute-done.13.refs_2_.refs_1_, f32[2,13,64,512]{3,2,1,0:T(8,128)S(1)} %get-tuple-element.59.refs_2_, ...), custom_call_target="tpu_custom_call" | custom-call | flops 1048576 | bytes 65536 | tf_op jit(solution)/shard_map/up_gradient/pallas_call | solution.py:844
  74.3 3.2 %up_gradient.3 = (bf16[4,64,1024]{2,1,0:T(8,128)(2,1)S(1)}, bf16[4,64,1024]{2,1,0:T(8,128)(2,1)S(1)}, bf16[4,64,1024]{2,1,0:T(8,128)(2,1)S(1)}, bf16[2,64,1024]{...) custom-call(bf16[13,2,64,1024]{3,2,1,0:T(8,128)(2,1)S(1)} %pack.6.refs_1_.refs_0_, ...), custom_call_target="tpu_custom_call" | custom-call | flops 1048576 | bytes 65536 | tf_op jit(solution)/shard_map/up_gradient/pallas_call | solution.py:844
  81.2 2.4 %collective-permute-start.24 = (f32[8,1024]{1,0:T(8,128)S(1)}, f32[8,1024]{1,0:T(8,128)S(1)}, u32[]{:S(2)}, u32[]{:S(2)}) collective-permute-start(f32[8,1024]{1,0:T(8,128)S(1)} %add.9), channel_id=1, source_target_pairs={{0,2},{1,3},{2,0},{3,1},{4,6},{5,7},{6,4},{7,5},{8,10},{9,11},{10,... | collective-permute-start | bytes 98312 | tf_op jit(solution)/shard_map/ppermute | solution.py:1015
  83.6 1.9 %collective-permute-done.24 = f32[8,1024]{1,0:T(8,128)S(1)} collective-permute-done((f32[8,1024]{1,0:T(8,128)S(1)}, f32[8,1024]{1,0:T(8,128)S(1)}, u32[]{:S(2)}, u32[]{:S(2)}) %collective-permute-start.24) | collective-permute-done | bytes 32800 | tf_op jit(solution)/shard_map/ppermute | solution.py:1015
  85.5 2.7 %collective-permute-start.25 = (f32[8,1024]{1,0:T(8,128)S(1)}, f32[8,1024]{1,0:T(8,128)S(1)}, u32[]{:S(2)}, u32[]{:S(2)}) collective-permute-start(f32[8,1024]{1,0:T(8,128)S(1)} %add.10), channel_id=1, source_target_pairs={{0,4},{1,5},{2,6},{3,7},{4,0},{5,1},{6,2},{7,3},{8,12},{9,13},{10,... | collective-permute-start | bytes 98312 | tf_op jit(solution)/shard_map/ppermute | solution.py:1015
  88.2 2.1 %collective-permute-done.25 = f32[8,1024]{1,0:T(8,128)S(1)} collective-permute-done((f32[8,1024]{1,0:T(8,128)S(1)}, f32[8,1024]{1,0:T(8,128)S(1)}, u32[]{:S(2)}, u32[]{:S(2)}) %collective-permute-start.25) | collective-permute-done | bytes 32800 | tf_op jit(solution)/shard_map/ppermute | solution.py:1015
  92.6 6.1 %collective-permute-done.16.x_ref = bf16[4,64,1024]{2,1,0:T(8,128)(2,1)S(1)} collective-permute-done((bf16[4,64,1024]{2,1,0:T(8,128)(2,1)S(1)}, bf16[4,64,1024]{2,1,0:T(8,128)(2,1)S(1)}, u32[]{:S(2)}, u32[]{:S(2)}) %collective-permute-start.16) | collective-permute-done | bytes 524320 | tf_op jit(solution)/shard_map/ppermute | solution.py:1012
  101.6 2.7 %collective-permute-done.29.x_late_ref = bf16[2,64,1024]{2,1,0:T(8,128)(2,1)S(1)} collective-permute-done((bf16[2,64,1024]{2,1,0:T(8,128)(2,1)S(1)}, bf16[2,64,1024]{2,1,0:T(8,128)(2,1)S(1)}, u32[]{:S(2)}, u32[]{:S(2)}) %collective-permute-start.29) | collective-permute-done | bytes 262176 | tf_op jit(solution)/shard_map/ppermute | solution.py:1012
  106.4 3.5 %collective-permute-start.32 = (bf16[64,1024]{1,0:T(8,128)(2,1)S(1)}, bf16[64,1024]{1,0:T(8,128)(2,1)S(1)}, u32[]{:S(2)}, u32[]{:S(2)}) collective-permute-start(bf16[64,1024]{1,0:T(8,128)(2,1)S(1)} %get-tuple-element.90), channel_id=1, source_target_pairs={{0,4},{1,5},{2,6},{3,7},{4,0},{5,1},{6,2},{7,3},{8,12},{9,13},{10,... | collective-permute-start | bytes 393224 | tf_op jit(solution)/shard_map/ppermute | solution.py:1019
  110.4 1.7 %collective-permute-start.20 = (bf16[64,1024]{1,0:T(8,128)(2,1)S(1)}, bf16[64,1024]{1,0:T(8,128)(2,1)S(1)}, u32[]{:S(2)}, u32[]{:S(2)}) collective-permute-start(bf16[64,1024]{1,0:T(8,128)(2,1)S(1)} %get-tuple-element.74), channel_id=1, source_target_pairs={{0,2},{1,3},{2,4},{3,5},{4,6},{5,7},{6,0},{7,1},{8,10},{9,11},{10,... | collective-permute-start | bytes 393224 | tf_op jit(solution)/shard_map/ppermute | solution.py:1019
  112.1 2.2 %collective-permute-start.21 = (bf16[64,1024]{1,0:T(8,128)(2,1)S(1)}, bf16[64,1024]{1,0:T(8,128)(2,1)S(1)}, u32[]{:S(2)}, u32[]{:S(2)}) collective-permute-start(bf16[64,1024]{1,0:T(8,128)(2,1)S(1)} %get-tuple-element.75), channel_id=1, source_target_pairs={{0,4},{1,5},{2,6},{3,7},{4,0},{5,1},{6,2},{7,3},{8,12},{9,13},{10,... | collective-permute-start | bytes 393224 | tf_op jit(solution)/shard_map/ppermute | solution.py:1019
  115.5 8.8 %collective-permute-done.32.refs_2_ = bf16[64,1024]{1,0:T(8,128)(2,1)S(1)} collective-permute-done((bf16[64,1024]{1,0:T(8,128)(2,1)S(1)}, bf16[64,1024]{1,0:T(8,128)(2,1)S(1)}, u32[]{:S(2)}, u32[]{:S(2)}) %collective-permute-start.32) | collective-permute-done | bytes 131104 | tf_op jit(solution)/shard_map/ppermute | solution.py:1019
  132.0 1.6 %collective-permute-start.38 = (bf16[144,1024]{1,0:T(8,128)(2,1)S(1)}, bf16[144,1024]{1,0:T(8,128)(2,1)S(1)}, u32[]{:S(2)}, u32[]{:S(2)}) collective-permute-start(bf16[144,1024]{1,0:T(8,128)(2,1)S(1)} %get-tuple-element.93), channel_id=1, source_target_pairs={{0,24},{8,16},{16,8},{24,0},{1,25},{9,17},{17,9},{25,1},{2,26},{10... | collective-permute-start | bytes 884744 | tf_op jit(solution)/shard_map/ppermute | solution.py:1012
  135.5 7.3 %collective-permute-done.36.refs_1_ = bf16[80,1024]{1,0:T(8,128)(2,1)S(1)} collective-permute-done((bf16[80,1024]{1,0:T(8,128)(2,1)S(1)}, bf16[80,1024]{1,0:T(8,128)(2,1)S(1)}, u32[]{:S(2)}, u32[]{:S(2)}) %collective-permute-start.36) | collective-permute-done | bytes 163872 | tf_op jit(solution)/shard_map/ppermute | solution.py:1012
  142.8 1.7 %place.1 = (f32[1024,256]{1,0:T(8,128)}, f32[256,1024]{1,0:T(8,128)}, f32[1,1024]{1,0:T(1,128)}, f32[1,1024]{1,0:T(1,128)}, f32[1,1]{1,0:T(1,128)}) custom-call(s32[1]{0:T(128)} %bitcast.group_ref, bf16[80,1024]{1,0:T(8,128)(2,1)S(1)} %get-tuple-element.92.refs_0_, bf16[80,1024]{1,0:T(8,128)(2,1)S(1)} %collective-permute-done.36.refs_1_, ...), custom_call_target="tpu_custom_call" | custom-call | flops 1048576 | bytes 65536 | tf_op jit(solution)/shard_map/place/pallas_call | solution.py:978
  (96 shorter events, 36.6 us)
Async XLA Ops:
  2.7 20.7 %collective-permute-start = (bf16[2,64,1024]{2,1,0:T(8,128)(2,1)}, bf16[2,64,1024]{2,1,0:T(8,128)(2,1)S(1)}, u32[]{:S(2)}, u32[]{:S(2)}) collective-permute-start(bf16[2,64,1024]{2,1,0:T(8,128)(2,1)} %quarter.1), channel_id=1, source_target_pairs={{0,6},{1,7},{2,0},{3,1},{4,2},{5,3},{6,4},{7,5},{8,14},{9,15},{10,... | collective-permute-start | bytes 786440 | tf_op jit(solution)/shard_map/ppermute | solution.py:1019
  2.7 23.7 %collective-permute-start.3 = (bf16[2,64,1024]{2,1,0:T(8,128)(2,1)}, bf16[2,64,1024]{2,1,0:T(8,128)(2,1)S(1)}, u32[]{:S(2)}, u32[]{:S(2)}) collective-permute-start(bf16[2,64,1024]{2,1,0:T(8,128)(2,1)} %quarter.1), channel_id=1, source_target_pairs={{0,4},{1,5},{2,6},{3,7},{4,0},{5,1},{6,2},{7,3},{8,12},{9,13},{10,... | collective-permute-start | bytes 786440 | tf_op jit(solution)/shard_map/ppermute | solution.py:1019
  5.8 22.5 %collective-permute-start.4 = (bf16[2,64,1024]{2,1,0:T(8,128)(2,1)}, bf16[2,64,1024]{2,1,0:T(8,128)(2,1)S(1)}, u32[]{:S(2)}, u32[]{:S(2)}) collective-permute-start(bf16[2,64,1024]{2,1,0:T(8,128)(2,1)} %quarter.1), channel_id=1, source_target_pairs={{0,2},{1,3},{2,4},{3,5},{4,6},{5,7},{6,0},{7,1},{8,10},{9,11},{10,... | collective-permute-start | bytes 786440 | tf_op jit(solution)/shard_map/ppermute | solution.py:1019
  23.4 6.4 %collective-permute-start.2 = (bf16[1,2,64,1024]{3,2,1,0:T(8,128)(2,1)S(1)}, bf16[1,2,64,1024]{3,2,1,0:T(8,128)(2,1)S(1)}, u32[]{:S(2)}, u32[]{:S(2)}) collective-permute-start(bf16[1,2,64,1024]{3,2,1,0:T(8,128)(2,1)S(1)} %pack.4.refs_2_.refs_1_), channel_id=1, source_target_pairs={{0,16},{8,24},{16,0},{24,8},{1,17},{9,25},{17,1},{25,9},{2,18},{10... | collective-permute-start | bytes 786440 | tf_op jit(solution)/shard_map/ppermute | solution.py:1012
  25.0 7.4 %collective-permute-start.1 = (bf16[1,2,64,1024]{3,2,1,0:T(8,128)(2,1)S(1)}, bf16[1,2,64,1024]{3,2,1,0:T(8,128)(2,1)S(1)}, u32[]{:S(2)}, u32[]{:S(2)}) collective-permute-start(bf16[1,2,64,1024]{3,2,1,0:T(8,128)(2,1)S(1)} %pack.4.refs_2_.refs_1_), channel_id=1, source_target_pairs={{0,8},{8,0},{16,24},{24,16},{1,9},{9,1},{17,25},{25,17},{2,10},{10... | collective-permute-start | bytes 786440 | tf_op jit(solution)/shard_map/ppermute | solution.py:1012
  32.4 12.7 %collective-permute-start.5 = (bf16[2,2,64,1024]{3,2,1,0:T(8,128)(2,1)S(1)}, bf16[2,2,64,1024]{3,2,1,0:T(8,128)(2,1)S(1)}, u32[]{:S(2)}, u32[]{:S(2)}) collective-permute-start(bf16[2,2,64,1024]{3,2,1,0:T(8,128)(2,1)S(1)} %tie.1.refs_4_), channel_id=1, source_target_pairs={{0,8},{8,0},{16,24},{24,16},{1,9},{9,1},{17,25},{25,17},{2,10},{10... | collective-permute-start | bytes 1572872 | tf_op jit(solution)/shard_map/ppermute | solution.py:1012
  33.9 11.2 %collective-permute-start.6 = (bf16[2,2,64,1024]{3,2,1,0:T(8,128)(2,1)S(1)}, bf16[2,2,64,1024]{3,2,1,0:T(8,128)(2,1)S(1)}, u32[]{:S(2)}, u32[]{:S(2)}) collective-permute-start(bf16[2,2,64,1024]{3,2,1,0:T(8,128)(2,1)S(1)} %tie.1.refs_4_), channel_id=1, source_target_pairs={{0,16},{8,24},{16,0},{24,8},{1,17},{9,25},{17,1},{25,9},{2,18},{10... | collective-permute-start | bytes 1572872 | tf_op jit(solution)/shard_map/ppermute | solution.py:1012
  33.9 10.0 %collective-permute-start.7 = (bf16[2,64,1024]{2,1,0:T(8,128)(2,1)S(1)}, bf16[2,64,1024]{2,1,0:T(8,128)(2,1)S(1)}, u32[]{:S(2)}, u32[]{:S(2)}) collective-permute-start(bf16[2,64,1024]{2,1,0:T(8,128)(2,1)S(1)} %get-tuple-element.54), channel_id=1, source_target_pairs={{0,2},{1,3},{2,4},{3,5},{4,6},{5,7},{6,0},{7,1},{8,10},{9,11},{10,... | collective-permute-start | bytes 786440 | tf_op jit(solution)/shard_map/ppermute | solution.py:1019
  33.9 11.2 %collective-permute-start.8 = (bf16[2,64,1024]{2,1,0:T(8,128)(2,1)S(1)}, bf16[2,64,1024]{2,1,0:T(8,128)(2,1)S(1)}, u32[]{:S(2)}, u32[]{:S(2)}) collective-permute-start(bf16[2,64,1024]{2,1,0:T(8,128)(2,1)S(1)} %get-tuple-element.55), channel_id=1, source_target_pairs={{0,6},{1,7},{2,0},{3,1},{4,2},{5,3},{6,4},{7,5},{8,14},{9,15},{10,... | collective-permute-start | bytes 786440 | tf_op jit(solution)/shard_map/ppermute | solution.py:1019
  45.3 6.1 %collective-permute-start.11 = (bf16[13,2,64,1024]{3,2,1,0:T(8,128)(2,1)S(1)}, bf16[13,2,64,1024]{3,2,1,0:T(8,128)(2,1)S(1)}, u32[]{:S(2)}, u32[]{:S(2)}) collective-permute-start(bf16[13,2,64,1024]{3,2,1,0:T(8,128)(2,1)S(1)} %pack.6.refs_1_.refs_0_), channel_id=1, source_target_pairs={{0,1},{1,0},{2,3},{3,2},{4,5},{5,4},{6,7},{7,6},{8,9},{9,8},{10,11... | collective-permute-start | bytes 10223624 | tf_op jit(solution)/shard_map/ppermute | solution.py:1015
  45.4 14.3 %collective-permute-start.10 = (bf16[2,2,64,1024]{3,2,1,0:T(8,128)(2,1)S(1)}, bf16[2,2,64,1024]{3,2,1,0:T(8,128)(2,1)S(1)}, u32[]{:S(2)}, u32[]{:S(2)}) collective-permute-start(bf16[2,2,64,1024]{3,2,1,0:T(8,128)(2,1)S(1)} %collective-permute-done.5.refs_5_), channel_id=1, source_target_pairs={{0,16},{8,24},{16,0},{24,8},{1,17},{9,25},{17,1},{25,9},{2,18},{10... | collective-permute-start | bytes 1572872 | tf_op jit(solution)/shard_map/ppermute | solution.py:1012
  45.9 13.5 %collective-permute-start.12 = (bf16[2,64,1024]{2,1,0:T(8,128)(2,1)S(1)}, bf16[2,64,1024]{2,1,0:T(8,128)(2,1)S(1)}, u32[]{:S(2)}, u32[]{:S(2)}) collective-permute-start(bf16[2,64,1024]{2,1,0:T(8,128)(2,1)S(1)} %get-tuple-element.58), channel_id=1, source_target_pairs={{0,4},{1,5},{2,6},{3,7},{4,0},{5,1},{6,2},{7,3},{8,12},{9,13},{10,... | collective-permute-start | bytes 786440 | tf_op jit(solution)/shard_map/ppermute | solution.py:1019
  47.9 11.5 %collective-permute-start.9 = (bf16[1,2,64,1024]{3,2,1,0:T(8,128)(2,1)S(1)}, bf16[1,2,64,1024]{3,2,1,0:T(8,128)(2,1)S(1)}, u32[]{:S(2)}, u32[]{:S(2)}) collective-permute-start(bf16[1,2,64,1024]{3,2,1,0:T(8,128)(2,1)S(1)} %collective-permute-done.2.refs_2_.refs_3_), channel_id=1, source_target_pairs={{0,8},{8,0},{16,24},{24,16},{1,9},{9,1},{17,25},{25,17},{2,10},{10... | collective-permute-start | bytes 786440 | tf_op jit(solution)/shard_map/ppermute | solution.py:1012
  72.6 17.7 %collective-permute-start.27 = (bf16[4,64,1024]{2,1,0:T(8,128)(2,1)S(1)}, bf16[4,64,1024]{2,1,0:T(8,128)(2,1)S(1)}, u32[]{:S(2)}, u32[]{:S(2)}) collective-permute-start(bf16[4,64,1024]{2,1,0:T(8,128)(2,1)S(1)} %get-tuple-element.82), channel_id=1, source_target_pairs={{0,8},{8,0},{16,24},{24,16},{1,9},{9,1},{17,25},{25,17},{2,10},{10... | collective-permute-start | bytes 1572872 | tf_op jit(solution)/shard_map/ppermute | solution.py:1012
  73.2 17.1 %collective-permute-start.28 = (bf16[4,64,1024]{2,1,0:T(8,128)(2,1)S(1)}, bf16[4,64,1024]{2,1,0:T(8,128)(2,1)S(1)}, u32[]{:S(2)}, u32[]{:S(2)}) collective-permute-start(bf16[4,64,1024]{2,1,0:T(8,128)(2,1)S(1)} %get-tuple-element.83), channel_id=1, source_target_pairs={{0,16},{8,24},{16,0},{24,8},{1,17},{9,25},{17,1},{25,9},{2,18},{10... | collective-permute-start | bytes 1572872 | tf_op jit(solution)/shard_map/ppermute | solution.py:1012
  77.5 21.2 %collective-permute-start.16 = (bf16[4,64,1024]{2,1,0:T(8,128)(2,1)S(1)}, bf16[4,64,1024]{2,1,0:T(8,128)(2,1)S(1)}, u32[]{:S(2)}, u32[]{:S(2)}) collective-permute-start(bf16[4,64,1024]{2,1,0:T(8,128)(2,1)S(1)} %get-tuple-element.67), channel_id=1, source_target_pairs={{0,8},{8,0},{16,24},{24,16},{1,9},{9,1},{17,25},{25,17},{2,10},{10... | collective-permute-start | bytes 1572872 | tf_op jit(solution)/shard_map/ppermute | solution.py:1012
  78.6 20.6 %collective-permute-start.17 = (bf16[4,64,1024]{2,1,0:T(8,128)(2,1)S(1)}, bf16[4,64,1024]{2,1,0:T(8,128)(2,1)S(1)}, u32[]{:S(2)}, u32[]{:S(2)}) collective-permute-start(bf16[4,64,1024]{2,1,0:T(8,128)(2,1)S(1)} %get-tuple-element.68), channel_id=1, source_target_pairs={{0,16},{8,24},{16,0},{24,8},{1,17},{9,25},{17,1},{25,9},{2,18},{10... | collective-permute-start | bytes 1572872 | tf_op jit(solution)/shard_map/ppermute | solution.py:1012
  90.5 13.8 %collective-permute-start.29 = (bf16[2,64,1024]{2,1,0:T(8,128)(2,1)S(1)}, bf16[2,64,1024]{2,1,0:T(8,128)(2,1)S(1)}, u32[]{:S(2)}, u32[]{:S(2)}) collective-permute-start(bf16[2,64,1024]{2,1,0:T(8,128)(2,1)S(1)} %get-tuple-element.86), channel_id=1, source_target_pairs={{0,8},{8,0},{16,24},{24,16},{1,9},{9,1},{17,25},{25,17},{2,10},{10... | collective-permute-start | bytes 786440 | tf_op jit(solution)/shard_map/ppermute | solution.py:1012
  91.6 13.2 %collective-permute-start.30 = (bf16[2,64,1024]{2,1,0:T(8,128)(2,1)S(1)}, bf16[2,64,1024]{2,1,0:T(8,128)(2,1)S(1)}, u32[]{:S(2)}, u32[]{:S(2)}) collective-permute-start(bf16[2,64,1024]{2,1,0:T(8,128)(2,1)S(1)} %get-tuple-element.87), channel_id=1, source_target_pairs={{0,16},{8,24},{16,0},{24,8},{1,17},{9,25},{17,1},{25,9},{2,18},{10... | collective-permute-start | bytes 786440 | tf_op jit(solution)/shard_map/ppermute | solution.py:1012
  99.4 10.9 %collective-permute-start.18 = (bf16[2,64,1024]{2,1,0:T(8,128)(2,1)S(1)}, bf16[2,64,1024]{2,1,0:T(8,128)(2,1)S(1)}, u32[]{:S(2)}, u32[]{:S(2)}) collective-permute-start(bf16[2,64,1024]{2,1,0:T(8,128)(2,1)S(1)} %get-tuple-element.71), channel_id=1, source_target_pairs={{0,8},{8,0},{16,24},{24,16},{1,9},{9,1},{17,25},{25,17},{2,10},{10... | collective-permute-start | bytes 786440 | tf_op jit(solution)/shard_map/ppermute | solution.py:1012
  100.9 9.3 %collective-permute-start.19 = (bf16[2,64,1024]{2,1,0:T(8,128)(2,1)S(1)}, bf16[2,64,1024]{2,1,0:T(8,128)(2,1)S(1)}, u32[]{:S(2)}, u32[]{:S(2)}) collective-permute-start(bf16[2,64,1024]{2,1,0:T(8,128)(2,1)S(1)} %get-tuple-element.72), channel_id=1, source_target_pairs={{0,16},{8,24},{16,0},{24,8},{1,17},{9,25},{17,1},{25,9},{2,18},{10... | collective-permute-start | bytes 786440 | tf_op jit(solution)/shard_map/ppermute | solution.py:1012
  105.1 9.8 %collective-permute-start.31 = (bf16[64,1024]{1,0:T(8,128)(2,1)S(1)}, bf16[64,1024]{1,0:T(8,128)(2,1)S(1)}, u32[]{:S(2)}, u32[]{:S(2)}) collective-permute-start(bf16[64,1024]{1,0:T(8,128)(2,1)S(1)} %get-tuple-element.89), channel_id=1, source_target_pairs={{0,2},{1,3},{2,4},{3,5},{4,6},{5,7},{6,0},{7,1},{8,10},{9,11},{10,... | collective-permute-start | bytes 393224 | tf_op jit(solution)/shard_map/ppermute | solution.py:1019
  106.4 17.9 %collective-permute-start.32 = (bf16[64,1024]{1,0:T(8,128)(2,1)S(1)}, bf16[64,1024]{1,0:T(8,128)(2,1)S(1)}, u32[]{:S(2)}, u32[]{:S(2)}) collective-permute-start(bf16[64,1024]{1,0:T(8,128)(2,1)S(1)} %get-tuple-element.90), channel_id=1, source_target_pairs={{0,4},{1,5},{2,6},{3,7},{4,0},{5,1},{6,2},{7,3},{8,12},{9,13},{10,... | collective-permute-start | bytes 393224 | tf_op jit(solution)/shard_map/ppermute | solution.py:1019
  109.9 15.5 %collective-permute-start.33 = (bf16[64,1024]{1,0:T(8,128)(2,1)S(1)}, bf16[64,1024]{1,0:T(8,128)(2,1)S(1)}, u32[]{:S(2)}, u32[]{:S(2)}) collective-permute-start(bf16[64,1024]{1,0:T(8,128)(2,1)S(1)} %get-tuple-element.91), channel_id=1, source_target_pairs={{0,6},{1,7},{2,0},{3,1},{4,2},{5,3},{6,4},{7,5},{8,14},{9,15},{10,... | collective-permute-start | bytes 393224 | tf_op jit(solution)/shard_map/ppermute | solution.py:1019
  110.4 18.0 %collective-permute-start.20 = (bf16[64,1024]{1,0:T(8,128)(2,1)S(1)}, bf16[64,1024]{1,0:T(8,128)(2,1)S(1)}, u32[]{:S(2)}, u32[]{:S(2)}) collective-permute-start(bf16[64,1024]{1,0:T(8,128)(2,1)S(1)} %get-tuple-element.74), channel_id=1, source_target_pairs={{0,2},{1,3},{2,4},{3,5},{4,6},{5,7},{6,0},{7,1},{8,10},{9,11},{10,... | collective-permute-start | bytes 393224 | tf_op jit(solution)/shard_map/ppermute | solution.py:1019
  112.1 16.4 %collective-permute-start.21 = (bf16[64,1024]{1,0:T(8,128)(2,1)S(1)}, bf16[64,1024]{1,0:T(8,128)(2,1)S(1)}, u32[]{:S(2)}, u32[]{:S(2)}) collective-permute-start(bf16[64,1024]{1,0:T(8,128)(2,1)S(1)} %get-tuple-element.75), channel_id=1, source_target_pairs={{0,4},{1,5},{2,6},{3,7},{4,0},{5,1},{6,2},{7,3},{8,12},{9,13},{10,... | collective-permute-start | bytes 393224 | tf_op jit(solution)/shard_map/ppermute | solution.py:1019
  114.8 15.2 %collective-permute-start.22 = (bf16[64,1024]{1,0:T(8,128)(2,1)S(1)}, bf16[64,1024]{1,0:T(8,128)(2,1)S(1)}, u32[]{:S(2)}, u32[]{:S(2)}) collective-permute-start(bf16[64,1024]{1,0:T(8,128)(2,1)S(1)} %get-tuple-element.76), channel_id=1, source_target_pairs={{0,6},{1,7},{2,0},{3,1},{4,2},{5,3},{6,4},{7,5},{8,14},{9,15},{10,... | collective-permute-start | bytes 393224 | tf_op jit(solution)/shard_map/ppermute | solution.py:1019
  125.5 5.0 %collective-permute-start.34 = (bf16[64,1024]{1,0:T(8,128)(2,1)S(1)}, bf16[64,1024]{1,0:T(8,128)(2,1)S(1)}, u32[]{:S(2)}, u32[]{:S(2)}) collective-permute-start(bf16[64,1024]{1,0:T(8,128)(2,1)S(1)} %collect.3.other_ref.refs_4_), channel_id=1, source_target_pairs={{0,8},{8,0},{16,24},{24,16},{1,9},{9,1},{17,25},{25,17},{2,10},{10... | collective-permute-start | bytes 393224 | tf_op jit(solution)/shard_map/ppermute | solution.py:1012
  126.9 5.0 %collective-permute-start.35 = (bf16[64,1024]{1,0:T(8,128)(2,1)S(1)}, bf16[64,1024]{1,0:T(8,128)(2,1)S(1)}, u32[]{:S(2)}, u32[]{:S(2)}) collective-permute-start(bf16[64,1024]{1,0:T(8,128)(2,1)S(1)} %collect.3.other_ref.refs_4_), channel_id=1, source_target_pairs={{0,16},{8,24},{16,0},{24,8},{1,17},{9,25},{17,1},{25,9},{2,18},{10... | collective-permute-start | bytes 393224 | tf_op jit(solution)/shard_map/ppermute | solution.py:1012
  132.0 10.8 %collective-permute-start.38 = (bf16[144,1024]{1,0:T(8,128)(2,1)S(1)}, bf16[144,1024]{1,0:T(8,128)(2,1)S(1)}, u32[]{:S(2)}, u32[]{:S(2)}) collective-permute-start(bf16[144,1024]{1,0:T(8,128)(2,1)S(1)} %get-tuple-element.93), channel_id=1, source_target_pairs={{0,24},{8,16},{16,8},{24,0},{1,25},{9,17},{17,9},{25,1},{2,26},{10... | collective-permute-start | bytes 884744 | tf_op jit(solution)/shard_map/ppermute | solution.py:1012
  133.6 9.2 %collective-permute-start.36 = (bf16[80,1024]{1,0:T(8,128)(2,1)S(1)}, bf16[80,1024]{1,0:T(8,128)(2,1)S(1)}, u32[]{:S(2)}, u32[]{:S(2)}) collective-permute-start(bf16[80,1024]{1,0:T(8,128)(2,1)S(1)} %get-tuple-element.92.refs_0_), channel_id=1, source_target_pairs={{0,8},{8,0},{16,24},{24,16},{1,9},{9,1},{17,25},{25,17},{2,10},{10... | collective-permute-start | bytes 491528 | tf_op jit(solution)/shard_map/ppermute | solution.py:1012
  135.0 7.8 %collective-permute-start.37 = (bf16[80,1024]{1,0:T(8,128)(2,1)S(1)}, bf16[80,1024]{1,0:T(8,128)(2,1)S(1)}, u32[]{:S(2)}, u32[]{:S(2)}) collective-permute-start(bf16[80,1024]{1,0:T(8,128)(2,1)S(1)} %get-tuple-element.92.refs_0_), channel_id=1, source_target_pairs={{0,16},{8,24},{16,0},{24,8},{1,17},{9,25},{17,1},{25,9},{2,18},{10... | collective-permute-start | bytes 491528 | tf_op jit(solution)/shard_map/ppermute | solution.py:1012
  (18 other events, 127.6 us)

commit v18 on v17

--- a/solution.py
+++ b/solution.py
@@ -954,12 +954,12 @@
     vectors = []
     for index, (up, down) in enumerate(zip(ups, downs)):
         first = pl.multiple_of(jnp.bitwise_xor(group, index) * part, part)
-        held_ref[pl.ds(first, part), :] = up[pl.ds(0, part), :].astype(F32)
+        held_ref[pl.ds(first, part), :] = up[pl.ds(0, part), :]
         start = down.shape[0] - part
         down_ref[pl.ds(first, part), :] = down[pl.ds(start, part), :].astype(F32)
         rows = up[pl.ds(part, 16), :].astype(F32)
         vectors.append((rows[0:3] + rows[3:6]) + rows[6:9])
-    up_ref[...] = held_ref[...].T
+    up_ref[...] = held_ref[...].T.astype(F32)
     vector = (vectors[0] + vectors[1]) + (vectors[2] + vectors[3])
     gain_ref[...] = vector[0:1]
     scale_ref[...] = vector[1:2]
@@ -980,7 +980,7 @@
         out_shape=tuple(shapes),
         in_specs=[SMEM] + [VMEM] * 8,
         out_specs=tuple([VMEM] * len(shapes)),
-        scratch_shapes=[pltpu.VMEM((4 * part, width), F32)],
+        scratch_shapes=[pltpu.VMEM((4 * part, width), BF16)],
         compiler_params=params(16),
         cost_estimate=COST,
         name="place",
@@ -1037,12 +1037,12 @@
     )
     most = pack(
         [own_rows(group, up_weight, down_weight), low, x_low, y_low, high, x_high, y_high],
-        normed, targets[1], *targets[half + 1:],
+        normed, targets[half],
     )
     most_other = partner(most)
     d_low, d_high = beside(y_low, 1), beside(x_high, 2)
     act_most, slope_most, mixed = forward(normed_t, [most], [most_other])
-    late = targets[2:half + 1]
+    late = targets[1:half] + targets[half + 1:]
     last = pack([d_low, d_high], mixed, *late)
     last_other = partner(last)
     act_last, slope_last, back, back_t, small = forward(

time: 145 us -> 146 us (level)
  starting transfers between devices: 46.1 us -> 37.2 us
  waiting for transfers between devices: 64.3 us -> 73.1 us
    ppermute x12, starting transfers between devices: 19.3 us -> 14.9 us  [along(): return lax.ppermute(array, 'ray', pairs)]
    ppermute x8, starting transfers between devices: 6.47 us -> 2.58 us  [partner(): return lax.ppermute(array, 'ray', [(r, r ^ flip) for r in range(ray_count)])]
    ppermute x12, waiting for transfers between devices: 29 us -> 32.2 us  [along(): return lax.ppermute(array, 'ray', pairs)]
    ppermute x19, waiting for transfers between devices: 23.4 us -> 26.5 us  [beside(): lax.ppermute(array, 'grp', [(g, g ^ flip) for g in range(group_count)])]
    ppermute x8, waiting for transfers between devices: 11.8 us -> 14.5 us  [partner(): return lax.ppermute(array, 'ray', [(r, r ^ flip) for r in range(ray_count)])]
  transfers between devices with their start and end apart: 39 -> 39, of which waited for: 27 -> 30; matrix products, arithmetic and copies ran while one was open for 0% -> 0% of each run, Pallas kernels for 17% -> 17%
where the time goes in v18:
time: 146 us; the launch traced here: 144 us
  waiting for transfers between devices  73.1 us (50%)
  starting transfers between devices  37.2 us (25%)
  Pallas kernels  32.8 us (22%)
    ppermute x12, waiting for transfers between devices, along(): return lax.ppermute(array, 'ray', pairs)  32.2 us
    ppermute x19, waiting for transfers between devices, beside(): lax.ppermute(array, 'grp', [(g, g ^ flip) for g in range(group_count)])  26.5 us
    ppermute x19, starting transfers between devices, beside(): lax.ppermute(array, 'grp', [(g, g ^ flip) for g in range(group_count)])  19.7 us
    ppermute x12, starting transfers between devices, along(): return lax.ppermute(array, 'ray', pairs)  14.9 us
    ppermute x8, waiting for transfers between devices, partner(): return lax.ppermute(array, 'ray', [(r, r ^ flip) for r in range(ray_count)])  14.5 us
    pallas_call x1, Pallas kernels, render(): pl.pallas_call(functools.partial(render_kernel, ray_count, relative), out...  8.42 us
    pallas_call x2, Pallas kernels, forward(): pl.pallas_call(functools.partial(forward_kernel, first, blocks, len(own),...  7.95 us
    pallas_call x2, Pallas kernels, up_gradient(): pl.pallas_call(functools.partial(up_grad_kernel, side, weight_pieces, act...  5.93 us
  transfers between devices with their start and end apart: 39, of which 30 were waited for; matrix products, arithmetic and copies ran while one was open for 0% of the time, Pallas kernels for 17%

profile of v18, /device:TPU:8, one launch (start us, length us, event | category | flops | bytes accessed | tf_op | source)
XLA Modules:
  0.0 144.1 jit_solution(11979418493827123738)
XLA Ops:
  0.7 2.0 %quarter.1 = bf16[2,64,1024]{2,1,0:T(8,128)(2,1)} custom-call(s32[1]{0:T(128)} %bitcast.group_ref, bf16[1024,256]{1,0:T(8,128)(2,1)} %up_hbm.1, bf16[256,1024]{1,0:T(8,128)(2,1)} %down_hbm.1), custom_call_target="tpu_custom_call" | custom-call | flops 10000000000 | bytes 1048576 | tf_op jit(solution)/shard_map/quarter/pallas_call | solution.py:521
  2.7 3.0 %collective-permute-start.3 = (bf16[2,64,1024]{2,1,0:T(8,128)(2,1)}, bf16[2,64,1024]{2,1,0:T(8,128)(2,1)S(1)}, u32[]{:S(2)}, u32[]{:S(2)}) collective-permute-start(bf16[2,64,1024]{2,1,0:T(8,128)(2,1)} %quarter.1), channel_id=1, source_target_pairs={{0,4},{1,5},{2,6},{3,7},{4,0},{5,1},{6,2},{7,3},{8,12},{9,13},{10,... | collective-permute-start | bytes 786440 | tf_op jit(solution)/shard_map/ppermute | solution.py:1019
  5.8 2.5 %collective-permute-start.4 = (bf16[2,64,1024]{2,1,0:T(8,128)(2,1)}, bf16[2,64,1024]{2,1,0:T(8,128)(2,1)S(1)}, u32[]{:S(2)}, u32[]{:S(2)}) collective-permute-start(bf16[2,64,1024]{2,1,0:T(8,128)(2,1)} %quarter.1), channel_id=1, source_target_pairs={{0,2},{1,3},{2,4},{3,5},{4,6},{5,7},{6,0},{7,1},{8,10},{9,11},{10,... | collective-permute-start | bytes 786440 | tf_op jit(solution)/shard_map/ppermute | solution.py:1019
  8.3 8.4 %render.1 = (bf16[2,64,1024]{2,1,0:T(8,128)(2,1)S(1)}, bf16[2,64,1024]{2,1,0:T(8,128)(2,1)S(1)}, bf16[2,64,1024]{2,1,0:T(8,128)(2,1)S(1)}, bf16[2,64,1024]{2,1,0:T(8,128)(2,1)S(1)}) custom-call(s32[1]{0:T(128)} %bitcast.1.me_ref, s32[1,8]{1,0:T(1,128)S(1)} %copy-done.9, s32[32,512]{1,0:T(8,128)S(1)} %copy-done.5, f32[32,512]{1,0:T(8,128)S(1)} %copy-done.6, ...), custom_call_target="tpu_custom_call" | custom-call | flops 1048576 | bytes 65536 | tf_op jit(solution)/shard_map/render/pallas_call | solution.py:152
  16.7 6.6 %collective-permute-done.refs_0_ = bf16[2,64,1024]{2,1,0:T(8,128)(2,1)S(1)} collective-permute-done((bf16[2,64,1024]{2,1,0:T(8,128)(2,1)}, bf16[2,64,1024]{2,1,0:T(8,128)(2,1)S(1)}, u32[]{:S(2)}, u32[]{:S(2)}) %collective-permute-start) | collective-permute-done | bytes 262176 | tf_op jit(solution)/shard_map/ppermute | solution.py:1019
  23.4 1.6 %collective-permute-start.2 = (bf16[1,2,64,1024]{3,2,1,0:T(8,128)(2,1)S(1)}, bf16[1,2,64,1024]{3,2,1,0:T(8,128)(2,1)S(1)}, u32[]{:S(2)}, u32[]{:S(2)}) collective-permute-start(bf16[1,2,64,1024]{3,2,1,0:T(8,128)(2,1)S(1)} %pack.4.refs_2_.refs_1_), channel_id=1, source_target_pairs={{0,16},{8,24},{16,0},{24,8},{1,17},{9,25},{17,1},{25,9},{2,18},{10... | collective-permute-start | bytes 786440 | tf_op jit(solution)/shard_map/ppermute | solution.py:1012
  26.5 1.8 %collective-permute-done.4.refs_1_ = bf16[2,64,1024]{2,1,0:T(8,128)(2,1)S(1)} collective-permute-done((bf16[2,64,1024]{2,1,0:T(8,128)(2,1)}, bf16[2,64,1024]{2,1,0:T(8,128)(2,1)S(1)}, u32[]{:S(2)}, u32[]{:S(2)}) %collective-permute-start.4) | collective-permute-done | bytes 262176 | tf_op jit(solution)/shard_map/ppermute | solution.py:1019
  28.3 1.5 %collective-permute-done.2.refs_2_.refs_3_ = bf16[1,2,64,1024]{3,2,1,0:T(8,128)(2,1)S(1)} collective-permute-done((bf16[1,2,64,1024]{3,2,1,0:T(8,128)(2,1)S(1)}, bf16[1,2,64,1024]{3,2,1,0:T(8,128)(2,1)S(1)}, u32[]{:S(2)}, u32[]{:S(2)}) %collective-permute-start.2) | collective-permute-done | bytes 262176 | tf_op jit(solution)/shard_map/ppermute | solution.py:1012
  29.8 2.5 %collective-permute-done.1.refs_1_.refs_2_ = bf16[1,2,64,1024]{3,2,1,0:T(8,128)(2,1)S(1)} collective-permute-done((bf16[1,2,64,1024]{3,2,1,0:T(8,128)(2,1)S(1)}, bf16[1,2,64,1024]{3,2,1,0:T(8,128)(2,1)S(1)}, u32[]{:S(2)}, u32[]{:S(2)}) %collective-permute-start.1) | collective-permute-done | bytes 262176 | tf_op jit(solution)/shard_map/ppermute | solution.py:1012
  34.1 3.1 %tokens.1 = (bf16[512,1024]{1,0:T(8,128)(2,1)S(1)}, bf16[512,1024]{1,0:T(8,128)(2,1)S(1)}, bf16[1024,512]{1,0:T(8,128)(2,1)S(1)}) custom-call(s32[1]{0:T(128)} %bitcast.1.me_ref, s32[1,8]{1,0:T(1,128)S(1)} %copy-done.9, s32[1,4096]{1,0:T(1,128)S(1)} %copy-done.4, bf16[512,1024]{1,0:T(8,128)(2,1)S(1)} %copy-done.1, f32[1,1024]{1,0:T(1,128)S(1)} %bitcast.8), custom_call_target="tpu_custom_call" | custom-call | flops 1048576 | bytes 65536 | tf_op jit(solution)/shard_map/tokens/pallas_call | solution.py:238
  37.2 4.7 %collective-permute-done.7.refs_8_.refs_2_ = bf16[2,64,1024]{2,1,0:T(8,128)(2,1)S(1)} collective-permute-done((bf16[2,64,1024]{2,1,0:T(8,128)(2,1)S(1)}, bf16[2,64,1024]{2,1,0:T(8,128)(2,1)S(1)}, u32[]{:S(2)}, u32[]{:S(2)}) %collective-permute-start.7) | collective-permute-done | bytes 262176 | tf_op jit(solution)/shard_map/ppermute | solution.py:1019
  44.6 2.4 %collective-permute-start.11 = (bf16[2,64,1024]{2,1,0:T(8,128)(2,1)S(1)}, bf16[2,64,1024]{2,1,0:T(8,128)(2,1)S(1)}, u32[]{:S(2)}, u32[]{:S(2)}) collective-permute-start(bf16[2,64,1024]{2,1,0:T(8,128)(2,1)S(1)} %get-tuple-element.57), channel_id=1, source_target_pairs={{0,2},{1,3},{2,4},{3,5},{4,6},{5,7},{6,0},{7,1},{8,10},{9,11},{10,... | collective-permute-start | bytes 786440 | tf_op jit(solution)/shard_map/ppermute | solution.py:1019
  47.5 1.9 %collective-permute-done.10.refs_2_.refs_0_ = bf16[13,2,64,1024]{3,2,1,0:T(8,128)(2,1)S(1)} collective-permute-done((bf16[13,2,64,1024]{3,2,1,0:T(8,128)(2,1)S(1)}, bf16[13,2,64,1024]{3,2,1,0:T(8,128)(2,1)S(1)}, u32[]{:S(2)}, u32[]{:S(2)}) %collective-permute-start.10) | collective-permute-done | bytes 3407904 | tf_op jit(solution)/shard_map/ppermute | solution.py:1015
  49.4 5.0 %forward.2 = (bf16[2,13,64,512]{3,2,1,0:T(8,128)(2,1)S(1)}, f32[2,13,64,512]{3,2,1,0:T(8,128)S(1)}, f32[512,1024]{1,0:T(8,128)S(1)}) custom-call(bf16[1024,512]{1,0:T(8,128)(2,1)S(1)} %get-tuple-element.55.refs_0_, bf16[13,2,64,1024]{3,2,1,0:T(8,128)(2,1)S(1)} %pack.6.refs_1_.refs_0_, bf16[13,2,64,1024]{3,2,1,0:T(8,128)(2,1)S(1)} %collective-permute-done.10.refs_2_.refs_0_), custom_call_target="tpu_custom_call" | custom-call | flops 1048576 | bytes 65536 | tf_op jit(solution)/shard_map/forward/pallas_call | solution.py:652
  54.4 4.1 %collective-permute-done.11.refs_3_.refs_1_.refs_7_ = bf16[2,64,1024]{2,1,0:T(8,128)(2,1)S(1)} collective-permute-done((bf16[2,64,1024]{2,1,0:T(8,128)(2,1)S(1)}, bf16[2,64,1024]{2,1,0:T(8,128)(2,1)S(1)}, u32[]{:S(2)}, u32[]{:S(2)}) %collective-permute-start.11) | collective-permute-done | bytes 262176 | tf_op jit(solution)/shard_map/ppermute | solution.py:1019
  58.5 2.2 %collective-permute-done.12.refs_4_.refs_3_.refs_9_ = bf16[2,64,1024]{2,1,0:T(8,128)(2,1)S(1)} collective-permute-done((bf16[2,64,1024]{2,1,0:T(8,128)(2,1)S(1)}, bf16[2,64,1024]{2,1,0:T(8,128)(2,1)S(1)}, u32[]{:S(2)}, u32[]{:S(2)}) %collective-permute-start.12) | collective-permute-done | bytes 262176 | tf_op jit(solution)/shard_map/ppermute | solution.py:1019
  61.4 2.4 %collective-permute-done.14.refs_10_ = bf16[4,64,1024]{2,1,0:T(8,128)(2,1)S(1)} collective-permute-done((bf16[4,64,1024]{2,1,0:T(8,128)(2,1)S(1)}, bf16[4,64,1024]{2,1,0:T(8,128)(2,1)S(1)}, u32[]{:S(2)}, u32[]{:S(2)}) %collective-permute-start.14) | collective-permute-done | bytes 524320 | tf_op jit(solution)/shard_map/ppermute | solution.py:1015
  63.8 2.9 %forward.3 = (bf16[2,3,64,512]{3,2,1,0:T(8,128)(2,1)S(1)}, f32[2,3,64,512]{3,2,1,0:T(8,128)S(1)}, bf16[512,1024]{1,0:T(8,128)(2,1)S(1)}, bf16[1024,512]{1,0:T(8,128)(2,1)S(1)}, f32[8,1024]{1,0:T(8,128)S(1)}) custom-call(bf16[1024,512]{1,0:T(8,128)(2,1)S(1)} %get-tuple-element.55.refs_0_, bf16[3,2,64,1024]{3,2,1,0:T(8,128)(2,1)S(1)} %pack.7.refs_1_, ...), custom_call_target="tpu_custom_call" | custom-call | flops 1048576 | bytes 65536 | tf_op jit(solution)/shard_map/forward/pallas_call | solution.py:652
  68.2 2.7 %up_gradient.2 = (bf16[4,4,64,1024]{3,2,1,0:T(8,128)(2,1)S(1)}, f32[1,1024]{1,0:T(1,128)S(1)}) custom-call(bf16[13,2,64,1024]{3,2,1,0:T(8,128)(2,1)S(1)} %collective-permute-done.10.refs_2_.refs_0_, bf16[3,2,64,1024]{3,2,1,0:T(8,128)(2,1)S(1)} %collective-permute-done.13.refs_2_.refs_1_, f32[2,13,64,512]{3,2,1,0:T(8,128)S(1)} %get-tuple-element.59.refs_2_, ...), custom_call_target="tpu_custom_call" | custom-call | flops 1048576 | bytes 65536 | tf_op jit(solution)/shard_map/up_gradient/pallas_call | solution.py:844
  75.3 3.2 %up_gradient.3 = (bf16[4,64,1024]{2,1,0:T(8,128)(2,1)S(1)}, bf16[4,64,1024]{2,1,0:T(8,128)(2,1)S(1)}, bf16[4,64,1024]{2,1,0:T(8,128)(2,1)S(1)}, bf16[2,64,1024]{...) custom-call(bf16[13,2,64,1024]{3,2,1,0:T(8,128)(2,1)S(1)} %pack.6.refs_1_.refs_0_, ...), custom_call_target="tpu_custom_call" | custom-call | flops 1048576 | bytes 65536 | tf_op jit(solution)/shard_map/up_gradient/pallas_call | solution.py:844
  79.4 1.5 %collective-permute-start.17 = (bf16[4,64,1024]{2,1,0:T(8,128)(2,1)S(1)}, bf16[4,64,1024]{2,1,0:T(8,128)(2,1)S(1)}, u32[]{:S(2)}, u32[]{:S(2)}) collective-permute-start(bf16[4,64,1024]{2,1,0:T(8,128)(2,1)S(1)} %get-tuple-element.68), channel_id=1, source_target_pairs={{0,16},{8,24},{16,0},{24,8},{1,17},{9,25},{17,1},{25,9},{2,18},{10... | collective-permute-start | bytes 1572872 | tf_op jit(solution)/shard_map/ppermute | solution.py:1012
  82.4 3.6 %collective-permute-done.24 = f32[8,1024]{1,0:T(8,128)S(1)} collective-permute-done((f32[8,1024]{1,0:T(8,128)S(1)}, f32[8,1024]{1,0:T(8,128)S(1)}, u32[]{:S(2)}, u32[]{:S(2)}) %collective-permute-start.24) | collective-permute-done | bytes 32800 | tf_op jit(solution)/shard_map/ppermute | solution.py:1015
  87.0 3.8 %collective-permute-done.25 = f32[8,1024]{1,0:T(8,128)S(1)} collective-permute-done((f32[8,1024]{1,0:T(8,128)S(1)}, f32[8,1024]{1,0:T(8,128)S(1)}, u32[]{:S(2)}, u32[]{:S(2)}) %collective-permute-start.25) | collective-permute-done | bytes 32800 | tf_op jit(solution)/shard_map/ppermute | solution.py:1015
  92.8 6.8 %collective-permute-done.16.x_ref = bf16[4,64,1024]{2,1,0:T(8,128)(2,1)S(1)} collective-permute-done((bf16[4,64,1024]{2,1,0:T(8,128)(2,1)S(1)}, bf16[4,64,1024]{2,1,0:T(8,128)(2,1)S(1)}, u32[]{:S(2)}, u32[]{:S(2)}) %collective-permute-start.16) | collective-permute-done | bytes 524320 | tf_op jit(solution)/shard_map/ppermute | solution.py:1012
  100.3 1.6 %collective-permute-start.18 = (bf16[2,64,1024]{2,1,0:T(8,128)(2,1)S(1)}, bf16[2,64,1024]{2,1,0:T(8,128)(2,1)S(1)}, u32[]{:S(2)}, u32[]{:S(2)}) collective-permute-start(bf16[2,64,1024]{2,1,0:T(8,128)(2,1)S(1)} %get-tuple-element.71), channel_id=1, source_target_pairs={{0,8},{8,0},{16,24},{24,16},{1,9},{9,1},{17,25},{25,17},{2,10},{10... | collective-permute-start | bytes 786440 | tf_op jit(solution)/shard_map/ppermute | solution.py:1012
  102.3 2.9 %collective-permute-done.29.x_late_ref = bf16[2,64,1024]{2,1,0:T(8,128)(2,1)S(1)} collective-permute-done((bf16[2,64,1024]{2,1,0:T(8,128)(2,1)S(1)}, bf16[2,64,1024]{2,1,0:T(8,128)(2,1)S(1)}, u32[]{:S(2)}, u32[]{:S(2)}) %collective-permute-start.29) | collective-permute-done | bytes 262176 | tf_op jit(solution)/shard_map/ppermute | solution.py:1012
  111.7 2.5 %collective-permute-start.21 = (bf16[64,1024]{1,0:T(8,128)(2,1)S(1)}, bf16[64,1024]{1,0:T(8,128)(2,1)S(1)}, u32[]{:S(2)}, u32[]{:S(2)}) collective-permute-start(bf16[64,1024]{1,0:T(8,128)(2,1)S(1)} %get-tuple-element.75), channel_id=1, source_target_pairs={{0,4},{1,5},{2,6},{3,7},{4,0},{5,1},{6,2},{7,3},{8,12},{9,13},{10,... | collective-permute-start | bytes 393224 | tf_op jit(solution)/shard_map/ppermute | solution.py:1019
  114.4 9.6 %collective-permute-done.32.refs_2_ = bf16[64,1024]{1,0:T(8,128)(2,1)S(1)} collective-permute-done((bf16[64,1024]{1,0:T(8,128)(2,1)S(1)}, bf16[64,1024]{1,0:T(8,128)(2,1)S(1)}, u32[]{:S(2)}, u32[]{:S(2)}) %collective-permute-start.32) | collective-permute-done | bytes 131104 | tf_op jit(solution)/shard_map/ppermute | solution.py:1019
  124.9 1.5 %collective-permute-start.34 = (bf16[64,1024]{1,0:T(8,128)(2,1)S(1)}, bf16[64,1024]{1,0:T(8,128)(2,1)S(1)}, u32[]{:S(2)}, u32[]{:S(2)}) collective-permute-start(bf16[64,1024]{1,0:T(8,128)(2,1)S(1)} %collect.3.other_ref.refs_4_), channel_id=1, source_target_pairs={{0,8},{8,0},{16,24},{24,16},{1,9},{9,1},{17,25},{25,17},{2,10},{10... | collective-permute-start | bytes 393224 | tf_op jit(solution)/shard_map/ppermute | solution.py:1012
  127.7 1.9 %collective-permute-done.22.refs_3_ = bf16[64,1024]{1,0:T(8,128)(2,1)S(1)} collective-permute-done((bf16[64,1024]{1,0:T(8,128)(2,1)S(1)}, bf16[64,1024]{1,0:T(8,128)(2,1)S(1)}, u32[]{:S(2)}, u32[]{:S(2)}) %collective-permute-start.22) | collective-permute-done | bytes 131104 | tf_op jit(solution)/shard_map/ppermute | solution.py:1019
  135.0 7.4 %collective-permute-done.36.refs_1_ = bf16[80,1024]{1,0:T(8,128)(2,1)S(1)} collective-permute-done((bf16[80,1024]{1,0:T(8,128)(2,1)S(1)}, bf16[80,1024]{1,0:T(8,128)(2,1)S(1)}, u32[]{:S(2)}, u32[]{:S(2)}) %collective-permute-start.36) | collective-permute-done | bytes 163872 | tf_op jit(solution)/shard_map/ppermute | solution.py:1012
  142.6 1.6 %place.1 = (f32[1024,256]{1,0:T(8,128)}, f32[256,1024]{1,0:T(8,128)}, f32[1,1024]{1,0:T(1,128)}, f32[1,1024]{1,0:T(1,128)}, f32[1,1]{1,0:T(1,128)}) custom-call(s32[1]{0:T(128)} %bitcast.group_ref, bf16[80,1024]{1,0:T(8,128)(2,1)S(1)} %get-tuple-element.92.refs_0_, bf16[80,1024]{1,0:T(8,128)(2,1)S(1)} %collective-permute-done.36.refs_1_, ...), custom_call_target="tpu_custom_call" | custom-call | flops 1048576 | bytes 65536 | tf_op jit(solution)/shard_map/place/pallas_call | solution.py:978
  (96 shorter events, 33.9 us)
Async XLA Ops:
  2.7 20.7 %collective-permute-start = (bf16[2,64,1024]{2,1,0:T(8,128)(2,1)}, bf16[2,64,1024]{2,1,0:T(8,128)(2,1)S(1)}, u32[]{:S(2)}, u32[]{:S(2)}) collective-permute-start(bf16[2,64,1024]{2,1,0:T(8,128)(2,1)} %quarter.1), channel_id=1, source_target_pairs={{0,6},{1,7},{2,0},{3,1},{4,2},{5,3},{6,4},{7,5},{8,14},{9,15},{10,... | collective-permute-start | bytes 786440 | tf_op jit(solution)/shard_map/ppermute | solution.py:1019
  2.7 23.7 %collective-permute-start.3 = (bf16[2,64,1024]{2,1,0:T(8,128)(2,1)}, bf16[2,64,1024]{2,1,0:T(8,128)(2,1)S(1)}, u32[]{:S(2)}, u32[]{:S(2)}) collective-permute-start(bf16[2,64,1024]{2,1,0:T(8,128)(2,1)} %quarter.1), channel_id=1, source_target_pairs={{0,4},{1,5},{2,6},{3,7},{4,0},{5,1},{6,2},{7,3},{8,12},{9,13},{10,... | collective-permute-start | bytes 786440 | tf_op jit(solution)/shard_map/ppermute | solution.py:1019
  5.8 22.5 %collective-permute-start.4 = (bf16[2,64,1024]{2,1,0:T(8,128)(2,1)}, bf16[2,64,1024]{2,1,0:T(8,128)(2,1)S(1)}, u32[]{:S(2)}, u32[]{:S(2)}) collective-permute-start(bf16[2,64,1024]{2,1,0:T(8,128)(2,1)} %quarter.1), channel_id=1, source_target_pairs={{0,2},{1,3},{2,4},{3,5},{4,6},{5,7},{6,0},{7,1},{8,10},{9,11},{10,... | collective-permute-start | bytes 786440 | tf_op jit(solution)/shard_map/ppermute | solution.py:1019
  23.4 6.4 %collective-permute-start.2 = (bf16[1,2,64,1024]{3,2,1,0:T(8,128)(2,1)S(1)}, bf16[1,2,64,1024]{3,2,1,0:T(8,128)(2,1)S(1)}, u32[]{:S(2)}, u32[]{:S(2)}) collective-permute-start(bf16[1,2,64,1024]{3,2,1,0:T(8,128)(2,1)S(1)} %pack.4.refs_2_.refs_1_), channel_id=1, source_target_pairs={{0,16},{8,24},{16,0},{24,8},{1,17},{9,25},{17,1},{25,9},{2,18},{10... | collective-permute-start | bytes 786440 | tf_op jit(solution)/shard_map/ppermute | solution.py:1012
  25.0 7.4 %collective-permute-start.1 = (bf16[1,2,64,1024]{3,2,1,0:T(8,128)(2,1)S(1)}, bf16[1,2,64,1024]{3,2,1,0:T(8,128)(2,1)S(1)}, u32[]{:S(2)}, u32[]{:S(2)}) collective-permute-start(bf16[1,2,64,1024]{3,2,1,0:T(8,128)(2,1)S(1)} %pack.4.refs_2_.refs_1_), channel_id=1, source_target_pairs={{0,8},{8,0},{16,24},{24,16},{1,9},{9,1},{17,25},{25,17},{2,10},{10... | collective-permute-start | bytes 786440 | tf_op jit(solution)/shard_map/ppermute | solution.py:1012
  32.4 10.2 %collective-permute-start.5 = (bf16[2,2,64,1024]{3,2,1,0:T(8,128)(2,1)S(1)}, bf16[2,2,64,1024]{3,2,1,0:T(8,128)(2,1)S(1)}, u32[]{:S(2)}, u32[]{:S(2)}) collective-permute-start(bf16[2,2,64,1024]{3,2,1,0:T(8,128)(2,1)S(1)} %tie.1.refs_4_), channel_id=1, source_target_pairs={{0,8},{8,0},{16,24},{24,16},{1,9},{9,1},{17,25},{25,17},{2,10},{10... | collective-permute-start | bytes 1572872 | tf_op jit(solution)/shard_map/ppermute | solution.py:1012
  33.9 9.2 %collective-permute-start.6 = (bf16[2,2,64,1024]{3,2,1,0:T(8,128)(2,1)S(1)}, bf16[2,2,64,1024]{3,2,1,0:T(8,128)(2,1)S(1)}, u32[]{:S(2)}, u32[]{:S(2)}) collective-permute-start(bf16[2,2,64,1024]{3,2,1,0:T(8,128)(2,1)S(1)} %tie.1.refs_4_), channel_id=1, source_target_pairs={{0,16},{8,24},{16,0},{24,8},{1,17},{9,25},{17,1},{25,9},{2,18},{10... | collective-permute-start | bytes 1572872 | tf_op jit(solution)/shard_map/ppermute | solution.py:1012
  33.9 8.1 %collective-permute-start.7 = (bf16[2,64,1024]{2,1,0:T(8,128)(2,1)S(1)}, bf16[2,64,1024]{2,1,0:T(8,128)(2,1)S(1)}, u32[]{:S(2)}, u32[]{:S(2)}) collective-permute-start(bf16[2,64,1024]{2,1,0:T(8,128)(2,1)S(1)} %get-tuple-element.54), channel_id=1, source_target_pairs={{0,4},{1,5},{2,6},{3,7},{4,0},{5,1},{6,2},{7,3},{8,12},{9,13},{10,... | collective-permute-start | bytes 786440 | tf_op jit(solution)/shard_map/ppermute | solution.py:1019
  43.3 6.1 %collective-permute-start.10 = (bf16[13,2,64,1024]{3,2,1,0:T(8,128)(2,1)S(1)}, bf16[13,2,64,1024]{3,2,1,0:T(8,128)(2,1)S(1)}, u32[]{:S(2)}, u32[]{:S(2)}) collective-permute-start(bf16[13,2,64,1024]{3,2,1,0:T(8,128)(2,1)S(1)} %pack.6.refs_1_.refs_0_), channel_id=1, source_target_pairs={{0,1},{1,0},{2,3},{3,2},{4,5},{5,4},{6,7},{7,6},{8,9},{9,8},{10,11... | collective-permute-start | bytes 10223624 | tf_op jit(solution)/shard_map/ppermute | solution.py:1015
  43.3 17.3 %collective-permute-start.9 = (bf16[2,2,64,1024]{3,2,1,0:T(8,128)(2,1)S(1)}, bf16[2,2,64,1024]{3,2,1,0:T(8,128)(2,1)S(1)}, u32[]{:S(2)}, u32[]{:S(2)}) collective-permute-start(bf16[2,2,64,1024]{3,2,1,0:T(8,128)(2,1)S(1)} %collective-permute-done.5.refs_5_), channel_id=1, source_target_pairs={{0,16},{8,24},{16,0},{24,8},{1,17},{9,25},{17,1},{25,9},{2,18},{10... | collective-permute-start | bytes 1572872 | tf_op jit(solution)/shard_map/ppermute | solution.py:1012
  44.6 13.9 %collective-permute-start.11 = (bf16[2,64,1024]{2,1,0:T(8,128)(2,1)S(1)}, bf16[2,64,1024]{2,1,0:T(8,128)(2,1)S(1)}, u32[]{:S(2)}, u32[]{:S(2)}) collective-permute-start(bf16[2,64,1024]{2,1,0:T(8,128)(2,1)S(1)} %get-tuple-element.57), channel_id=1, source_target_pairs={{0,2},{1,3},{2,4},{3,5},{4,6},{5,7},{6,0},{7,1},{8,10},{9,11},{10,... | collective-permute-start | bytes 786440 | tf_op jit(solution)/shard_map/ppermute | solution.py:1019
  46.9 13.7 %collective-permute-start.12 = (bf16[2,64,1024]{2,1,0:T(8,128)(2,1)S(1)}, bf16[2,64,1024]{2,1,0:T(8,128)(2,1)S(1)}, u32[]{:S(2)}, u32[]{:S(2)}) collective-permute-start(bf16[2,64,1024]{2,1,0:T(8,128)(2,1)S(1)} %get-tuple-element.58), channel_id=1, source_target_pairs={{0,6},{1,7},{2,0},{3,1},{4,2},{5,3},{6,4},{7,5},{8,14},{9,15},{10,... | collective-permute-start | bytes 786440 | tf_op jit(solution)/shard_map/ppermute | solution.py:1019
  46.9 13.7 %collective-permute-start.8 = (bf16[1,2,64,1024]{3,2,1,0:T(8,128)(2,1)S(1)}, bf16[1,2,64,1024]{3,2,1,0:T(8,128)(2,1)S(1)}, u32[]{:S(2)}, u32[]{:S(2)}) collective-permute-start(bf16[1,2,64,1024]{3,2,1,0:T(8,128)(2,1)S(1)} %collective-permute-done.2.refs_2_.refs_3_), channel_id=1, source_target_pairs={{0,8},{8,0},{16,24},{24,16},{1,9},{9,1},{17,25},{25,17},{2,10},{10... | collective-permute-start | bytes 786440 | tf_op jit(solution)/shard_map/ppermute | solution.py:1012
  73.5 17.4 %collective-permute-start.27 = (bf16[4,64,1024]{2,1,0:T(8,128)(2,1)S(1)}, bf16[4,64,1024]{2,1,0:T(8,128)(2,1)S(1)}, u32[]{:S(2)}, u32[]{:S(2)}) collective-permute-start(bf16[4,64,1024]{2,1,0:T(8,128)(2,1)S(1)} %get-tuple-element.82), channel_id=1, source_target_pairs={{0,8},{8,0},{16,24},{24,16},{1,9},{9,1},{17,25},{25,17},{2,10},{10... | collective-permute-start | bytes 1572872 | tf_op jit(solution)/shard_map/ppermute | solution.py:1012
  74.1 16.8 %collective-permute-start.28 = (bf16[4,64,1024]{2,1,0:T(8,128)(2,1)S(1)}, bf16[4,64,1024]{2,1,0:T(8,128)(2,1)S(1)}, u32[]{:S(2)}, u32[]{:S(2)}) collective-permute-start(bf16[4,64,1024]{2,1,0:T(8,128)(2,1)S(1)} %get-tuple-element.83), channel_id=1, source_target_pairs={{0,16},{8,24},{16,0},{24,8},{1,17},{9,25},{17,1},{25,9},{2,18},{10... | collective-permute-start | bytes 1572872 | tf_op jit(solution)/shard_map/ppermute | solution.py:1012
  78.5 21.1 %collective-permute-start.16 = (bf16[4,64,1024]{2,1,0:T(8,128)(2,1)S(1)}, bf16[4,64,1024]{2,1,0:T(8,128)(2,1)S(1)}, u32[]{:S(2)}, u32[]{:S(2)}) collective-permute-start(bf16[4,64,1024]{2,1,0:T(8,128)(2,1)S(1)} %get-tuple-element.67), channel_id=1, source_target_pairs={{0,8},{8,0},{16,24},{24,16},{1,9},{9,1},{17,25},{25,17},{2,10},{10... | collective-permute-start | bytes 1572872 | tf_op jit(solution)/shard_map/ppermute | solution.py:1012
  79.4 20.7 %collective-permute-start.17 = (bf16[4,64,1024]{2,1,0:T(8,128)(2,1)S(1)}, bf16[4,64,1024]{2,1,0:T(8,128)(2,1)S(1)}, u32[]{:S(2)}, u32[]{:S(2)}) collective-permute-start(bf16[4,64,1024]{2,1,0:T(8,128)(2,1)S(1)} %get-tuple-element.68), channel_id=1, source_target_pairs={{0,16},{8,24},{16,0},{24,8},{1,17},{9,25},{17,1},{25,9},{2,18},{10... | collective-permute-start | bytes 1572872 | tf_op jit(solution)/shard_map/ppermute | solution.py:1012
  91.0 14.2 %collective-permute-start.29 = (bf16[2,64,1024]{2,1,0:T(8,128)(2,1)S(1)}, bf16[2,64,1024]{2,1,0:T(8,128)(2,1)S(1)}, u32[]{:S(2)}, u32[]{:S(2)}) collective-permute-start(bf16[2,64,1024]{2,1,0:T(8,128)(2,1)S(1)} %get-tuple-element.86), channel_id=1, source_target_pairs={{0,8},{8,0},{16,24},{24,16},{1,9},{9,1},{17,25},{25,17},{2,10},{10... | collective-permute-start | bytes 786440 | tf_op jit(solution)/shard_map/ppermute | solution.py:1012
  91.6 14.1 %collective-permute-start.30 = (bf16[2,64,1024]{2,1,0:T(8,128)(2,1)S(1)}, bf16[2,64,1024]{2,1,0:T(8,128)(2,1)S(1)}, u32[]{:S(2)}, u32[]{:S(2)}) collective-permute-start(bf16[2,64,1024]{2,1,0:T(8,128)(2,1)S(1)} %get-tuple-element.87), channel_id=1, source_target_pairs={{0,16},{8,24},{16,0},{24,8},{1,17},{9,25},{17,1},{25,9},{2,18},{10... | collective-permute-start | bytes 786440 | tf_op jit(solution)/shard_map/ppermute | solution.py:1012
  100.3 9.7 %collective-permute-start.18 = (bf16[2,64,1024]{2,1,0:T(8,128)(2,1)S(1)}, bf16[2,64,1024]{2,1,0:T(8,128)(2,1)S(1)}, u32[]{:S(2)}, u32[]{:S(2)}) collective-permute-start(bf16[2,64,1024]{2,1,0:T(8,128)(2,1)S(1)} %get-tuple-element.71), channel_id=1, source_target_pairs={{0,8},{8,0},{16,24},{24,16},{1,9},{9,1},{17,25},{25,17},{2,10},{10... | collective-permute-start | bytes 786440 | tf_op jit(solution)/shard_map/ppermute | solution.py:1012
  101.8 8.4 %collective-permute-start.19 = (bf16[2,64,1024]{2,1,0:T(8,128)(2,1)S(1)}, bf16[2,64,1024]{2,1,0:T(8,128)(2,1)S(1)}, u32[]{:S(2)}, u32[]{:S(2)}) collective-permute-start(bf16[2,64,1024]{2,1,0:T(8,128)(2,1)S(1)} %get-tuple-element.72), channel_id=1, source_target_pairs={{0,16},{8,24},{16,0},{24,8},{1,17},{9,25},{17,1},{25,9},{2,18},{10... | collective-permute-start | bytes 786440 | tf_op jit(solution)/shard_map/ppermute | solution.py:1012
  106.0 8.2 %collective-permute-start.31 = (bf16[64,1024]{1,0:T(8,128)(2,1)S(1)}, bf16[64,1024]{1,0:T(8,128)(2,1)S(1)}, u32[]{:S(2)}, u32[]{:S(2)}) collective-permute-start(bf16[64,1024]{1,0:T(8,128)(2,1)S(1)} %get-tuple-element.89), channel_id=1, source_target_pairs={{0,2},{1,3},{2,4},{3,5},{4,6},{5,7},{6,0},{7,1},{8,10},{9,11},{10,... | collective-permute-start | bytes 393224 | tf_op jit(solution)/shard_map/ppermute | solution.py:1019
  107.2 16.8 %collective-permute-start.32 = (bf16[64,1024]{1,0:T(8,128)(2,1)S(1)}, bf16[64,1024]{1,0:T(8,128)(2,1)S(1)}, u32[]{:S(2)}, u32[]{:S(2)}) collective-permute-start(bf16[64,1024]{1,0:T(8,128)(2,1)S(1)} %get-tuple-element.90), channel_id=1, source_target_pairs={{0,4},{1,5},{2,6},{3,7},{4,0},{5,1},{6,2},{7,3},{8,12},{9,13},{10,... | collective-permute-start | bytes 393224 | tf_op jit(solution)/shard_map/ppermute | solution.py:1019
  108.7 16.1 %collective-permute-start.33 = (bf16[64,1024]{1,0:T(8,128)(2,1)S(1)}, bf16[64,1024]{1,0:T(8,128)(2,1)S(1)}, u32[]{:S(2)}, u32[]{:S(2)}) collective-permute-start(bf16[64,1024]{1,0:T(8,128)(2,1)S(1)} %get-tuple-element.91), channel_id=1, source_target_pairs={{0,6},{1,7},{2,0},{3,1},{4,2},{5,3},{6,4},{7,5},{8,14},{9,15},{10,... | collective-permute-start | bytes 393224 | tf_op jit(solution)/shard_map/ppermute | solution.py:1019
  110.5 16.9 %collective-permute-start.20 = (bf16[64,1024]{1,0:T(8,128)(2,1)S(1)}, bf16[64,1024]{1,0:T(8,128)(2,1)S(1)}, u32[]{:S(2)}, u32[]{:S(2)}) collective-permute-start(bf16[64,1024]{1,0:T(8,128)(2,1)S(1)} %get-tuple-element.74), channel_id=1, source_target_pairs={{0,2},{1,3},{2,4},{3,5},{4,6},{5,7},{6,0},{7,1},{8,10},{9,11},{10,... | collective-permute-start | bytes 393224 | tf_op jit(solution)/shard_map/ppermute | solution.py:1019
  111.7 16.0 %collective-permute-start.21 = (bf16[64,1024]{1,0:T(8,128)(2,1)S(1)}, bf16[64,1024]{1,0:T(8,128)(2,1)S(1)}, u32[]{:S(2)}, u32[]{:S(2)}) collective-permute-start(bf16[64,1024]{1,0:T(8,128)(2,1)S(1)} %get-tuple-element.75), channel_id=1, source_target_pairs={{0,4},{1,5},{2,6},{3,7},{4,0},{5,1},{6,2},{7,3},{8,12},{9,13},{10,... | collective-permute-start | bytes 393224 | tf_op jit(solution)/shard_map/ppermute | solution.py:1019
  114.2 15.5 %collective-permute-start.22 = (bf16[64,1024]{1,0:T(8,128)(2,1)S(1)}, bf16[64,1024]{1,0:T(8,128)(2,1)S(1)}, u32[]{:S(2)}, u32[]{:S(2)}) collective-permute-start(bf16[64,1024]{1,0:T(8,128)(2,1)S(1)} %get-tuple-element.76), channel_id=1, source_target_pairs={{0,6},{1,7},{2,0},{3,1},{4,2},{5,3},{6,4},{7,5},{8,14},{9,15},{10,... | collective-permute-start | bytes 393224 | tf_op jit(solution)/shard_map/ppermute | solution.py:1019
  124.9 5.0 %collective-permute-start.34 = (bf16[64,1024]{1,0:T(8,128)(2,1)S(1)}, bf16[64,1024]{1,0:T(8,128)(2,1)S(1)}, u32[]{:S(2)}, u32[]{:S(2)}) collective-permute-start(bf16[64,1024]{1,0:T(8,128)(2,1)S(1)} %collect.3.other_ref.refs_4_), channel_id=1, source_target_pairs={{0,8},{8,0},{16,24},{24,16},{1,9},{9,1},{17,25},{25,17},{2,10},{10... | collective-permute-start | bytes 393224 | tf_op jit(solution)/shard_map/ppermute | solution.py:1012
  126.4 5.0 %collective-permute-start.35 = (bf16[64,1024]{1,0:T(8,128)(2,1)S(1)}, bf16[64,1024]{1,0:T(8,128)(2,1)S(1)}, u32[]{:S(2)}, u32[]{:S(2)}) collective-permute-start(bf16[64,1024]{1,0:T(8,128)(2,1)S(1)} %collect.3.other_ref.refs_4_), channel_id=1, source_target_pairs={{0,16},{8,24},{16,0},{24,8},{1,17},{9,25},{17,1},{25,9},{2,18},{10... | collective-permute-start | bytes 393224 | tf_op jit(solution)/shard_map/ppermute | solution.py:1012
  131.4 11.2 %collective-permute-start.38 = (bf16[144,1024]{1,0:T(8,128)(2,1)S(1)}, bf16[144,1024]{1,0:T(8,128)(2,1)S(1)}, u32[]{:S(2)}, u32[]{:S(2)}) collective-permute-start(bf16[144,1024]{1,0:T(8,128)(2,1)S(1)} %get-tuple-element.93), channel_id=1, source_target_pairs={{0,24},{8,16},{16,8},{24,0},{1,25},{9,17},{17,9},{25,1},{2,26},{10... | collective-permute-start | bytes 884744 | tf_op jit(solution)/shard_map/ppermute | solution.py:1012
  132.4 10.0 %collective-permute-start.36 = (bf16[80,1024]{1,0:T(8,128)(2,1)S(1)}, bf16[80,1024]{1,0:T(8,128)(2,1)S(1)}, u32[]{:S(2)}, u32[]{:S(2)}) collective-permute-start(bf16[80,1024]{1,0:T(8,128)(2,1)S(1)} %get-tuple-element.92.refs_0_), channel_id=1, source_target_pairs={{0,8},{8,0},{16,24},{24,16},{1,9},{9,1},{17,25},{25,17},{2,10},{10... | collective-permute-start | bytes 491528 | tf_op jit(solution)/shard_map/ppermute | solution.py:1012
  133.9 8.7 %collective-permute-start.37 = (bf16[80,1024]{1,0:T(8,128)(2,1)S(1)}, bf16[80,1024]{1,0:T(8,128)(2,1)S(1)}, u32[]{:S(2)}, u32[]{:S(2)}) collective-permute-start(bf16[80,1024]{1,0:T(8,128)(2,1)S(1)} %get-tuple-element.92.refs_0_), channel_id=1, source_target_pairs={{0,16},{8,24},{16,0},{24,8},{1,17},{9,25},{17,1},{25,9},{2,18},{10... | collective-permute-start | bytes 491528 | tf_op jit(solution)/shard_map/ppermute | solution.py:1012
  (18 other events, 119.2 us)

commit v19 on v18

--- a/solution.py
+++ b/solution.py
@@ -1037,12 +1037,12 @@
     )
     most = pack(
         [own_rows(group, up_weight, down_weight), low, x_low, y_low, high, x_high, y_high],
-        normed, targets[half],
+        normed, targets[1], *targets[half + 1:],
     )
     most_other = partner(most)
     d_low, d_high = beside(y_low, 1), beside(x_high, 2)
     act_most, slope_most, mixed = forward(normed_t, [most], [most_other])
-    late = targets[1:half] + targets[half + 1:]
+    late = targets[2:half + 1]
     last = pack([d_low, d_high], mixed, *late)
     last_other = partner(last)
     act_last, slope_last, back, back_t, small = forward(

time: 146 us -> 145 us (level)
  starting transfers between devices: 37.2 us -> 46.1 us
  waiting for transfers between devices: 73.1 us -> 64.3 us
    ppermute x12, starting transfers between devices: 14.9 us -> 19.3 us  [along(): return lax.ppermute(array, 'ray', pairs)]
    ppermute x8, starting transfers between devices: 2.58 us -> 6.47 us  [partner(): return lax.ppermute(array, 'ray', [(r, r ^ flip) for r in range(ray_count)])]
    ppermute x12, waiting for transfers between devices: 32.2 us -> 29 us  [along(): return lax.ppermute(array, 'ray', pairs)]
    ppermute x19, waiting for transfers between devices: 26.5 us -> 23.4 us  [beside(): lax.ppermute(array, 'grp', [(g, g ^ flip) for g in range(group_count)])]
    ppermute x8, waiting for transfers between devices: 14.5 us -> 11.8 us  [partner(): return lax.ppermute(array, 'ray', [(r, r ^ flip) for r in range(ray_count)])]
  transfers between devices with their start and end apart: 39 -> 39, of which waited for: 30 -> 27; matrix products, arithmetic and copies ran while one was open for 0% -> 0% of each run, Pallas kernels for 17% -> 17%
where the time goes in v19:
time: 145 us; the launch traced here: 144 us
  waiting for transfers between devices  64.3 us (44%)
  starting transfers between devices  46.1 us (32%)
  Pallas kernels  33 us (23%)
    ppermute x12, waiting for transfers between devices, along(): return lax.ppermute(array, 'ray', pairs)  29 us
    ppermute x19, waiting for transfers between devices, beside(): lax.ppermute(array, 'grp', [(g, g ^ flip) for g in range(group_count)])  23.4 us
    ppermute x19, starting transfers between devices, beside(): lax.ppermute(array, 'grp', [(g, g ^ flip) for g in range(group_count)])  20.3 us
    ppermute x12, starting transfers between devices, along(): return lax.ppermute(array, 'ray', pairs)  19.3 us
    ppermute x8, waiting for transfers between devices, partner(): return lax.ppermute(array, 'ray', [(r, r ^ flip) for r in range(ray_count)])  11.8 us
    pallas_call x1, Pallas kernels, render(): pl.pallas_call(functools.partial(render_kernel, ray_count, relative), out...  8.41 us
    pallas_call x2, Pallas kernels, forward(): pl.pallas_call(functools.partial(forward_kernel, first, blocks, len(own),...  7.95 us
    ppermute x8, starting transfers between devices, partner(): return lax.ppermute(array, 'ray', [(r, r ^ flip) for r in range(ray_count)])  6.47 us
  transfers between devices with their start and end apart: 39, of which 27 were waited for; matrix products, arithmetic and copies ran while one was open for 0% of the time, Pallas kernels for 17%

profile of v19, /device:TPU:8, one launch (start us, length us, event | category | flops | bytes accessed | tf_op | source)
XLA Modules:
  0.0 144.4 jit_solution(17463859619350513111)
XLA Ops:
  0.7 2.0 %quarter.1 = bf16[2,64,1024]{2,1,0:T(8,128)(2,1)} custom-call(s32[1]{0:T(128)} %bitcast.group_ref, bf16[1024,256]{1,0:T(8,128)(2,1)} %up_hbm.1, bf16[256,1024]{1,0:T(8,128)(2,1)} %down_hbm.1), custom_call_target="tpu_custom_call" | custom-call | flops 10000000000 | bytes 1048576 | tf_op jit(solution)/shard_map/quarter/pallas_call | solution.py:521
  2.7 3.0 %collective-permute-start.3 = (bf16[2,64,1024]{2,1,0:T(8,128)(2,1)}, bf16[2,64,1024]{2,1,0:T(8,128)(2,1)S(1)}, u32[]{:S(2)}, u32[]{:S(2)}) collective-permute-start(bf16[2,64,1024]{2,1,0:T(8,128)(2,1)} %quarter.1), channel_id=1, source_target_pairs={{0,4},{1,5},{2,6},{3,7},{4,0},{5,1},{6,2},{7,3},{8,12},{9,13},{10,... | collective-permute-start | bytes 786440 | tf_op jit(solution)/shard_map/ppermute | solution.py:1019
  5.8 2.5 %collective-permute-start.4 = (bf16[2,64,1024]{2,1,0:T(8,128)(2,1)}, bf16[2,64,1024]{2,1,0:T(8,128)(2,1)S(1)}, u32[]{:S(2)}, u32[]{:S(2)}) collective-permute-start(bf16[2,64,1024]{2,1,0:T(8,128)(2,1)} %quarter.1), channel_id=1, source_target_pairs={{0,2},{1,3},{2,4},{3,5},{4,6},{5,7},{6,0},{7,1},{8,10},{9,11},{10,... | collective-permute-start | bytes 786440 | tf_op jit(solution)/shard_map/ppermute | solution.py:1019
  8.3 8.4 %render.1 = (bf16[2,64,1024]{2,1,0:T(8,128)(2,1)S(1)}, bf16[2,64,1024]{2,1,0:T(8,128)(2,1)S(1)}, bf16[2,64,1024]{2,1,0:T(8,128)(2,1)S(1)}, bf16[2,64,1024]{2,1,0:T(8,128)(2,1)S(1)}) custom-call(s32[1]{0:T(128)} %bitcast.1.me_ref, s32[1,8]{1,0:T(1,128)S(1)} %copy-done.9, s32[32,512]{1,0:T(8,128)S(1)} %copy-done.5, f32[32,512]{1,0:T(8,128)S(1)} %copy-done.6, ...), custom_call_target="tpu_custom_call" | custom-call | flops 1048576 | bytes 65536 | tf_op jit(solution)/shard_map/render/pallas_call | solution.py:152
  16.7 6.6 %collective-permute-done.refs_0_ = bf16[2,64,1024]{2,1,0:T(8,128)(2,1)S(1)} collective-permute-done((bf16[2,64,1024]{2,1,0:T(8,128)(2,1)}, bf16[2,64,1024]{2,1,0:T(8,128)(2,1)S(1)}, u32[]{:S(2)}, u32[]{:S(2)}) %collective-permute-start) | collective-permute-done | bytes 262176 | tf_op jit(solution)/shard_map/ppermute | solution.py:1019
  23.4 1.6 %collective-permute-start.2 = (bf16[1,2,64,1024]{3,2,1,0:T(8,128)(2,1)S(1)}, bf16[1,2,64,1024]{3,2,1,0:T(8,128)(2,1)S(1)}, u32[]{:S(2)}, u32[]{:S(2)}) collective-permute-start(bf16[1,2,64,1024]{3,2,1,0:T(8,128)(2,1)S(1)} %pack.4.refs_2_.refs_1_), channel_id=1, source_target_pairs={{0,16},{8,24},{16,0},{24,8},{1,17},{9,25},{17,1},{25,9},{2,18},{10... | collective-permute-start | bytes 786440 | tf_op jit(solution)/shard_map/ppermute | solution.py:1012
  26.5 1.8 %collective-permute-done.4.refs_1_ = bf16[2,64,1024]{2,1,0:T(8,128)(2,1)S(1)} collective-permute-done((bf16[2,64,1024]{2,1,0:T(8,128)(2,1)}, bf16[2,64,1024]{2,1,0:T(8,128)(2,1)S(1)}, u32[]{:S(2)}, u32[]{:S(2)}) %collective-permute-start.4) | collective-permute-done | bytes 262176 | tf_op jit(solution)/shard_map/ppermute | solution.py:1019
  29.8 2.5 %collective-permute-done.1.refs_1_.refs_2_ = bf16[1,2,64,1024]{3,2,1,0:T(8,128)(2,1)S(1)} collective-permute-done((bf16[1,2,64,1024]{3,2,1,0:T(8,128)(2,1)S(1)}, bf16[1,2,64,1024]{3,2,1,0:T(8,128)(2,1)S(1)}, u32[]{:S(2)}, u32[]{:S(2)}) %collective-permute-start.1) | collective-permute-done | bytes 262176 | tf_op jit(solution)/shard_map/ppermute | solution.py:1012
  33.9 2.0 %collective-permute-start.8 = (bf16[2,64,1024]{2,1,0:T(8,128)(2,1)S(1)}, bf16[2,64,1024]{2,1,0:T(8,128)(2,1)S(1)}, u32[]{:S(2)}, u32[]{:S(2)}) collective-permute-start(bf16[2,64,1024]{2,1,0:T(8,128)(2,1)S(1)} %get-tuple-element.55), channel_id=1, source_target_pairs={{0,6},{1,7},{2,0},{3,1},{4,2},{5,3},{6,4},{7,5},{8,14},{9,15},{10,... | collective-permute-start | bytes 786440 | tf_op jit(solution)/shard_map/ppermute | solution.py:1019
  36.1 3.2 %tokens.1 = (bf16[512,1024]{1,0:T(8,128)(2,1)S(1)}, bf16[512,1024]{1,0:T(8,128)(2,1)S(1)}, bf16[1024,512]{1,0:T(8,128)(2,1)S(1)}) custom-call(s32[1]{0:T(128)} %bitcast.1.me_ref, s32[1,8]{1,0:T(1,128)S(1)} %copy-done.9, s32[1,4096]{1,0:T(1,128)S(1)} %copy-done.4, bf16[512,1024]{1,0:T(8,128)(2,1)S(1)} %copy-done.1, f32[1,1024]{1,0:T(1,128)S(1)} %bitcast.8), custom_call_target="tpu_custom_call" | custom-call | flops 1048576 | bytes 65536 | tf_op jit(solution)/shard_map/tokens/pallas_call | solution.py:238
  39.4 4.4 %collective-permute-done.7.refs_8_.refs_1_.refs_7_ = bf16[2,64,1024]{2,1,0:T(8,128)(2,1)S(1)} collective-permute-done((bf16[2,64,1024]{2,1,0:T(8,128)(2,1)S(1)}, bf16[2,64,1024]{2,1,0:T(8,128)(2,1)S(1)}, u32[]{:S(2)}, u32[]{:S(2)}) %collective-permute-start.7) | collective-permute-done | bytes 262176 | tf_op jit(solution)/shard_map/ppermute | solution.py:1019
  45.9 2.0 %collective-permute-start.12 = (bf16[2,64,1024]{2,1,0:T(8,128)(2,1)S(1)}, bf16[2,64,1024]{2,1,0:T(8,128)(2,1)S(1)}, u32[]{:S(2)}, u32[]{:S(2)}) collective-permute-start(bf16[2,64,1024]{2,1,0:T(8,128)(2,1)S(1)} %get-tuple-element.58), channel_id=1, source_target_pairs={{0,4},{1,5},{2,6},{3,7},{4,0},{5,1},{6,2},{7,3},{8,12},{9,13},{10,... | collective-permute-start | bytes 786440 | tf_op jit(solution)/shard_map/ppermute | solution.py:1019
  48.4 2.9 %collective-permute-done.11.refs_2_.refs_0_ = bf16[13,2,64,1024]{3,2,1,0:T(8,128)(2,1)S(1)} collective-permute-done((bf16[13,2,64,1024]{3,2,1,0:T(8,128)(2,1)S(1)}, bf16[13,2,64,1024]{3,2,1,0:T(8,128)(2,1)S(1)}, u32[]{:S(2)}, u32[]{:S(2)}) %collective-permute-start.11) | collective-permute-done | bytes 3407904 | tf_op jit(solution)/shard_map/ppermute | solution.py:1015
  51.4 5.0 %forward.2 = (bf16[2,13,64,512]{3,2,1,0:T(8,128)(2,1)S(1)}, f32[2,13,64,512]{3,2,1,0:T(8,128)S(1)}, f32[512,1024]{1,0:T(8,128)S(1)}) custom-call(bf16[1024,512]{1,0:T(8,128)(2,1)S(1)} %get-tuple-element.56.refs_0_, bf16[13,2,64,1024]{3,2,1,0:T(8,128)(2,1)S(1)} %pack.6.refs_1_.refs_0_, bf16[13,2,64,1024]{3,2,1,0:T(8,128)(2,1)S(1)} %collective-permute-done.11.refs_2_.refs_0_), custom_call_target="tpu_custom_call" | custom-call | flops 1048576 | bytes 65536 | tf_op jit(solution)/shard_map/forward/pallas_call | solution.py:652
  56.4 3.0 %collective-permute-done.12.refs_3_.refs_2_.refs_8_ = bf16[2,64,1024]{2,1,0:T(8,128)(2,1)S(1)} collective-permute-done((bf16[2,64,1024]{2,1,0:T(8,128)(2,1)S(1)}, bf16[2,64,1024]{2,1,0:T(8,128)(2,1)S(1)}, u32[]{:S(2)}, u32[]{:S(2)}) %collective-permute-start.12) | collective-permute-done | bytes 262176 | tf_op jit(solution)/shard_map/ppermute | solution.py:1019
  60.4 2.4 %collective-permute-done.14.refs_10_ = bf16[4,64,1024]{2,1,0:T(8,128)(2,1)S(1)} collective-permute-done((bf16[4,64,1024]{2,1,0:T(8,128)(2,1)S(1)}, bf16[4,64,1024]{2,1,0:T(8,128)(2,1)S(1)}, u32[]{:S(2)}, u32[]{:S(2)}) %collective-permute-start.14) | collective-permute-done | bytes 524320 | tf_op jit(solution)/shard_map/ppermute | solution.py:1015
  62.9 2.9 %forward.3 = (bf16[2,3,64,512]{3,2,1,0:T(8,128)(2,1)S(1)}, f32[2,3,64,512]{3,2,1,0:T(8,128)S(1)}, bf16[512,1024]{1,0:T(8,128)(2,1)S(1)}, bf16[1024,512]{1,0:T(8,128)(2,1)S(1)}, f32[8,1024]{1,0:T(8,128)S(1)}) custom-call(bf16[1024,512]{1,0:T(8,128)(2,1)S(1)} %get-tuple-element.56.refs_0_, bf16[3,2,64,1024]{3,2,1,0:T(8,128)(2,1)S(1)} %pack.7.refs_1_, ...), custom_call_target="tpu_custom_call" | custom-call | flops 1048576 | bytes 65536 | tf_op jit(solution)/shard_map/forward/pallas_call | solution.py:652
  67.3 2.7 %up_gradient.2 = (bf16[4,4,64,1024]{3,2,1,0:T(8,128)(2,1)S(1)}, f32[1,1024]{1,0:T(1,128)S(1)}) custom-call(bf16[13,2,64,1024]{3,2,1,0:T(8,128)(2,1)S(1)} %collective-permute-done.11.refs_2_.refs_0_, bf16[3,2,64,1024]{3,2,1,0:T(8,128)(2,1)S(1)} %collective-permute-done.13.refs_2_.refs_1_, f32[2,13,64,512]{3,2,1,0:T(8,128)S(1)} %get-tuple-element.59.refs_2_, ...), custom_call_target="tpu_custom_call" | custom-call | flops 1048576 | bytes 65536 | tf_op jit(solution)/shard_map/up_gradient/pallas_call | solution.py:844
  74.3 3.2 %up_gradient.3 = (bf16[4,64,1024]{2,1,0:T(8,128)(2,1)S(1)}, bf16[4,64,1024]{2,1,0:T(8,128)(2,1)S(1)}, bf16[4,64,1024]{2,1,0:T(8,128)(2,1)S(1)}, bf16[2,64,1024]{...) custom-call(bf16[13,2,64,1024]{3,2,1,0:T(8,128)(2,1)S(1)} %pack.6.refs_1_.refs_0_, ...), custom_call_target="tpu_custom_call" | custom-call | flops 1048576 | bytes 65536 | tf_op jit(solution)/shard_map/up_gradient/pallas_call | solution.py:844
  81.2 2.4 %collective-permute-start.24 = (f32[8,1024]{1,0:T(8,128)S(1)}, f32[8,1024]{1,0:T(8,128)S(1)}, u32[]{:S(2)}, u32[]{:S(2)}) collective-permute-start(f32[8,1024]{1,0:T(8,128)S(1)} %add.9), channel_id=1, source_target_pairs={{0,2},{1,3},{2,0},{3,1},{4,6},{5,7},{6,4},{7,5},{8,10},{9,11},{10,... | collective-permute-start | bytes 98312 | tf_op jit(solution)/shard_map/ppermute | solution.py:1015
  83.6 1.9 %collective-permute-done.24 = f32[8,1024]{1,0:T(8,128)S(1)} collective-permute-done((f32[8,1024]{1,0:T(8,128)S(1)}, f32[8,1024]{1,0:T(8,128)S(1)}, u32[]{:S(2)}, u32[]{:S(2)}) %collective-permute-start.24) | collective-permute-done | bytes 32800 | tf_op jit(solution)/shard_map/ppermute | solution.py:1015
  85.5 2.7 %collective-permute-start.25 = (f32[8,1024]{1,0:T(8,128)S(1)}, f32[8,1024]{1,0:T(8,128)S(1)}, u32[]{:S(2)}, u32[]{:S(2)}) collective-permute-start(f32[8,1024]{1,0:T(8,128)S(1)} %add.10), channel_id=1, source_target_pairs={{0,4},{1,5},{2,6},{3,7},{4,0},{5,1},{6,2},{7,3},{8,12},{9,13},{10,... | collective-permute-start | bytes 98312 | tf_op jit(solution)/shard_map/ppermute | solution.py:1015
  88.2 2.1 %collective-permute-done.25 = f32[8,1024]{1,0:T(8,128)S(1)} collective-permute-done((f32[8,1024]{1,0:T(8,128)S(1)}, f32[8,1024]{1,0:T(8,128)S(1)}, u32[]{:S(2)}, u32[]{:S(2)}) %collective-permute-start.25) | collective-permute-done | bytes 32800 | tf_op jit(solution)/shard_map/ppermute | solution.py:1015
  92.6 6.1 %collective-permute-done.16.x_ref = bf16[4,64,1024]{2,1,0:T(8,128)(2,1)S(1)} collective-permute-done((bf16[4,64,1024]{2,1,0:T(8,128)(2,1)S(1)}, bf16[4,64,1024]{2,1,0:T(8,128)(2,1)S(1)}, u32[]{:S(2)}, u32[]{:S(2)}) %collective-permute-start.16) | collective-permute-done | bytes 524320 | tf_op jit(solution)/shard_map/ppermute | solution.py:1012
  101.6 2.7 %collective-permute-done.29.x_late_ref = bf16[2,64,1024]{2,1,0:T(8,128)(2,1)S(1)} collective-permute-done((bf16[2,64,1024]{2,1,0:T(8,128)(2,1)S(1)}, bf16[2,64,1024]{2,1,0:T(8,128)(2,1)S(1)}, u32[]{:S(2)}, u32[]{:S(2)}) %collective-permute-start.29) | collective-permute-done | bytes 262176 | tf_op jit(solution)/shard_map/ppermute | solution.py:1012
  106.4 3.5 %collective-permute-start.32 = (bf16[64,1024]{1,0:T(8,128)(2,1)S(1)}, bf16[64,1024]{1,0:T(8,128)(2,1)S(1)}, u32[]{:S(2)}, u32[]{:S(2)}) collective-permute-start(bf16[64,1024]{1,0:T(8,128)(2,1)S(1)} %get-tuple-element.90), channel_id=1, source_target_pairs={{0,4},{1,5},{2,6},{3,7},{4,0},{5,1},{6,2},{7,3},{8,12},{9,13},{10,... | collective-permute-start | bytes 393224 | tf_op jit(solution)/shard_map/ppermute | solution.py:1019
  110.4 1.7 %collective-permute-start.20 = (bf16[64,1024]{1,0:T(8,128)(2,1)S(1)}, bf16[64,1024]{1,0:T(8,128)(2,1)S(1)}, u32[]{:S(2)}, u32[]{:S(2)}) collective-permute-start(bf16[64,1024]{1,0:T(8,128)(2,1)S(1)} %get-tuple-element.74), channel_id=1, source_target_pairs={{0,2},{1,3},{2,4},{3,5},{4,6},{5,7},{6,0},{7,1},{8,10},{9,11},{10,... | collective-permute-start | bytes 393224 | tf_op jit(solution)/shard_map/ppermute | solution.py:1019
  112.1 2.2 %collective-permute-start.21 = (bf16[64,1024]{1,0:T(8,128)(2,1)S(1)}, bf16[64,1024]{1,0:T(8,128)(2,1)S(1)}, u32[]{:S(2)}, u32[]{:S(2)}) collective-permute-start(bf16[64,1024]{1,0:T(8,128)(2,1)S(1)} %get-tuple-element.75), channel_id=1, source_target_pairs={{0,4},{1,5},{2,6},{3,7},{4,0},{5,1},{6,2},{7,3},{8,12},{9,13},{10,... | collective-permute-start | bytes 393224 | tf_op jit(solution)/shard_map/ppermute | solution.py:1019
  115.5 8.8 %collective-permute-done.32.refs_2_ = bf16[64,1024]{1,0:T(8,128)(2,1)S(1)} collective-permute-done((bf16[64,1024]{1,0:T(8,128)(2,1)S(1)}, bf16[64,1024]{1,0:T(8,128)(2,1)S(1)}, u32[]{:S(2)}, u32[]{:S(2)}) %collective-permute-start.32) | collective-permute-done | bytes 131104 | tf_op jit(solution)/shard_map/ppermute | solution.py:1019
  132.0 1.6 %collective-permute-start.38 = (bf16[144,1024]{1,0:T(8,128)(2,1)S(1)}, bf16[144,1024]{1,0:T(8,128)(2,1)S(1)}, u32[]{:S(2)}, u32[]{:S(2)}) collective-permute-start(bf16[144,1024]{1,0:T(8,128)(2,1)S(1)} %get-tuple-element.93), channel_id=1, source_target_pairs={{0,24},{8,16},{16,8},{24,0},{1,25},{9,17},{17,9},{25,1},{2,26},{10... | collective-permute-start | bytes 884744 | tf_op jit(solution)/shard_map/ppermute | solution.py:1012
  135.5 7.3 %collective-permute-done.36.refs_1_ = bf16[80,1024]{1,0:T(8,128)(2,1)S(1)} collective-permute-done((bf16[80,1024]{1,0:T(8,128)(2,1)S(1)}, bf16[80,1024]{1,0:T(8,128)(2,1)S(1)}, u32[]{:S(2)}, u32[]{:S(2)}) %collective-permute-start.36) | collective-permute-done | bytes 163872 | tf_op jit(solution)/shard_map/ppermute | solution.py:1012
  142.8 1.6 %place.1 = (f32[1024,256]{1,0:T(8,128)}, f32[256,1024]{1,0:T(8,128)}, f32[1,1024]{1,0:T(1,128)}, f32[1,1024]{1,0:T(1,128)}, f32[1,1]{1,0:T(1,128)}) custom-call(s32[1]{0:T(128)} %bitcast.group_ref, bf16[80,1024]{1,0:T(8,128)(2,1)S(1)} %get-tuple-element.92.refs_0_, bf16[80,1024]{1,0:T(8,128)(2,1)S(1)} %collective-permute-done.36.refs_1_, ...), custom_call_target="tpu_custom_call" | custom-call | flops 1048576 | bytes 65536 | tf_op jit(solution)/shard_map/place/pallas_call | solution.py:978
  (96 shorter events, 36.6 us)
Async XLA Ops:
  2.7 20.7 %collective-permute-start = (bf16[2,64,1024]{2,1,0:T(8,128)(2,1)}, bf16[2,64,1024]{2,1,0:T(8,128)(2,1)S(1)}, u32[]{:S(2)}, u32[]{:S(2)}) collective-permute-start(bf16[2,64,1024]{2,1,0:T(8,128)(2,1)} %quarter.1), channel_id=1, source_target_pairs={{0,6},{1,7},{2,0},{3,1},{4,2},{5,3},{6,4},{7,5},{8,14},{9,15},{10,... | collective-permute-start | bytes 786440 | tf_op jit(solution)/shard_map/ppermute | solution.py:1019
  2.7 23.7 %collective-permute-start.3 = (bf16[2,64,1024]{2,1,0:T(8,128)(2,1)}, bf16[2,64,1024]{2,1,0:T(8,128)(2,1)S(1)}, u32[]{:S(2)}, u32[]{:S(2)}) collective-permute-start(bf16[2,64,1024]{2,1,0:T(8,128)(2,1)} %quarter.1), channel_id=1, source_target_pairs={{0,4},{1,5},{2,6},{3,7},{4,0},{5,1},{6,2},{7,3},{8,12},{9,13},{10,... | collective-permute-start | bytes 786440 | tf_op jit(solution)/shard_map/ppermute | solution.py:1019
  5.8 22.5 %collective-permute-start.4 = (bf16[2,64,1024]{2,1,0:T(8,128)(2,1)}, bf16[2,64,1024]{2,1,0:T(8,128)(2,1)S(1)}, u32[]{:S(2)}, u32[]{:S(2)}) collective-permute-start(bf16[2,64,1024]{2,1,0:T(8,128)(2,1)} %quarter.1), channel_id=1, source_target_pairs={{0,2},{1,3},{2,4},{3,5},{4,6},{5,7},{6,0},{7,1},{8,10},{9,11},{10,... | collective-permute-start | bytes 786440 | tf_op jit(solution)/shard_map/ppermute | solution.py:1019
  23.4 6.4 %collective-permute-start.2 = (bf16[1,2,64,1024]{3,2,1,0:T(8,128)(2,1)S(1)}, bf16[1,2,64,1024]{3,2,1,0:T(8,128)(2,1)S(1)}, u32[]{:S(2)}, u32[]{:S(2)}) collective-permute-start(bf16[1,2,64,1024]{3,2,1,0:T(8,128)(2,1)S(1)} %pack.4.refs_2_.refs_1_), channel_id=1, source_target_pairs={{0,16},{8,24},{16,0},{24,8},{1,17},{9,25},{17,1},{25,9},{2,18},{10... | collective-permute-start | bytes 786440 | tf_op jit(solution)/shard_map/ppermute | solution.py:1012
  25.0 7.4 %collective-permute-start.1 = (bf16[1,2,64,1024]{3,2,1,0:T(8,128)(2,1)S(1)}, bf16[1,2,64,1024]{3,2,1,0:T(8,128)(2,1)S(1)}, u32[]{:S(2)}, u32[]{:S(2)}) collective-permute-start(bf16[1,2,64,1024]{3,2,1,0:T(8,128)(2,1)S(1)} %pack.4.refs_2_.refs_1_), channel_id=1, source_target_pairs={{0,8},{8,0},{16,24},{24,16},{1,9},{9,1},{17,25},{25,17},{2,10},{10... | collective-permute-start | bytes 786440 | tf_op jit(solution)/shard_map/ppermute | solution.py:1012
  32.4 12.7 %collective-permute-start.5 = (bf16[2,2,64,1024]{3,2,1,0:T(8,128)(2,1)S(1)}, bf16[2,2,64,1024]{3,2,1,0:T(8,128)(2,1)S(1)}, u32[]{:S(2)}, u32[]{:S(2)}) collective-permute-start(bf16[2,2,64,1024]{3,2,1,0:T(8,128)(2,1)S(1)} %tie.1.refs_4_), channel_id=1, source_target_pairs={{0,8},{8,0},{16,24},{24,16},{1,9},{9,1},{17,25},{25,17},{2,10},{10... | collective-permute-start | bytes 1572872 | tf_op jit(solution)/shard_map/ppermute | solution.py:1012
  33.9 11.2 %collective-permute-start.6 = (bf16[2,2,64,1024]{3,2,1,0:T(8,128)(2,1)S(1)}, bf16[2,2,64,1024]{3,2,1,0:T(8,128)(2,1)S(1)}, u32[]{:S(2)}, u32[]{:S(2)}) collective-permute-start(bf16[2,2,64,1024]{3,2,1,0:T(8,128)(2,1)S(1)} %tie.1.refs_4_), channel_id=1, source_target_pairs={{0,16},{8,24},{16,0},{24,8},{1,17},{9,25},{17,1},{25,9},{2,18},{10... | collective-permute-start | bytes 1572872 | tf_op jit(solution)/shard_map/ppermute | solution.py:1012
  33.9 10.0 %collective-permute-start.7 = (bf16[2,64,1024]{2,1,0:T(8,128)(2,1)S(1)}, bf16[2,64,1024]{2,1,0:T(8,128)(2,1)S(1)}, u32[]{:S(2)}, u32[]{:S(2)}) collective-permute-start(bf16[2,64,1024]{2,1,0:T(8,128)(2,1)S(1)} %get-tuple-element.54), channel_id=1, source_target_pairs={{0,2},{1,3},{2,4},{3,5},{4,6},{5,7},{6,0},{7,1},{8,10},{9,11},{10,... | collective-permute-start | bytes 786440 | tf_op jit(solution)/shard_map/ppermute | solution.py:1019
  33.9 11.2 %collective-permute-start.8 = (bf16[2,64,1024]{2,1,0:T(8,128)(2,1)S(1)}, bf16[2,64,1024]{2,1,0:T(8,128)(2,1)S(1)}, u32[]{:S(2)}, u32[]{:S(2)}) collective-permute-start(bf16[2,64,1024]{2,1,0:T(8,128)(2,1)S(1)} %get-tuple-element.55), channel_id=1, source_target_pairs={{0,6},{1,7},{2,0},{3,1},{4,2},{5,3},{6,4},{7,5},{8,14},{9,15},{10,... | collective-permute-start | bytes 786440 | tf_op jit(solution)/shard_map/ppermute | solution.py:1019
  45.3 6.1 %collective-permute-start.11 = (bf16[13,2,64,1024]{3,2,1,0:T(8,128)(2,1)S(1)}, bf16[13,2,64,1024]{3,2,1,0:T(8,128)(2,1)S(1)}, u32[]{:S(2)}, u32[]{:S(2)}) collective-permute-start(bf16[13,2,64,1024]{3,2,1,0:T(8,128)(2,1)S(1)} %pack.6.refs_1_.refs_0_), channel_id=1, source_target_pairs={{0,1},{1,0},{2,3},{3,2},{4,5},{5,4},{6,7},{7,6},{8,9},{9,8},{10,11... | collective-permute-start | bytes 10223624 | tf_op jit(solution)/shard_map/ppermute | solution.py:1015
  45.4 14.3 %collective-permute-start.10 = (bf16[2,2,64,1024]{3,2,1,0:T(8,128)(2,1)S(1)}, bf16[2,2,64,1024]{3,2,1,0:T(8,128)(2,1)S(1)}, u32[]{:S(2)}, u32[]{:S(2)}) collective-permute-start(bf16[2,2,64,1024]{3,2,1,0:T(8,128)(2,1)S(1)} %collective-permute-done.5.refs_5_), channel_id=1, source_target_pairs={{0,16},{8,24},{16,0},{24,8},{1,17},{9,25},{17,1},{25,9},{2,18},{10... | collective-permute-start | bytes 1572872 | tf_op jit(solution)/shard_map/ppermute | solution.py:1012
  45.9 13.5 %collective-permute-start.12 = (bf16[2,64,1024]{2,1,0:T(8,128)(2,1)S(1)}, bf16[2,64,1024]{2,1,0:T(8,128)(2,1)S(1)}, u32[]{:S(2)}, u32[]{:S(2)}) collective-permute-start(bf16[2,64,1024]{2,1,0:T(8,128)(2,1)S(1)} %get-tuple-element.58), channel_id=1, source_target_pairs={{0,4},{1,5},{2,6},{3,7},{4,0},{5,1},{6,2},{7,3},{8,12},{9,13},{10,... | collective-permute-start | bytes 786440 | tf_op jit(solution)/shard_map/ppermute | solution.py:1019
  47.9 11.5 %collective-permute-start.9 = (bf16[1,2,64,1024]{3,2,1,0:T(8,128)(2,1)S(1)}, bf16[1,2,64,1024]{3,2,1,0:T(8,128)(2,1)S(1)}, u32[]{:S(2)}, u32[]{:S(2)}) collective-permute-start(bf16[1,2,64,1024]{3,2,1,0:T(8,128)(2,1)S(1)} %collective-permute-done.2.refs_2_.refs_3_), channel_id=1, source_target_pairs={{0,8},{8,0},{16,24},{24,16},{1,9},{9,1},{17,25},{25,17},{2,10},{10... | collective-permute-start | bytes 786440 | tf_op jit(solution)/shard_map/ppermute | solution.py:1012
  72.6 17.7 %collective-permute-start.27 = (bf16[4,64,1024]{2,1,0:T(8,128)(2,1)S(1)}, bf16[4,64,1024]{2,1,0:T(8,128)(2,1)S(1)}, u32[]{:S(2)}, u32[]{:S(2)}) collective-permute-start(bf16[4,64,1024]{2,1,0:T(8,128)(2,1)S(1)} %get-tuple-element.82), channel_id=1, source_target_pairs={{0,8},{8,0},{16,24},{24,16},{1,9},{9,1},{17,25},{25,17},{2,10},{10... | collective-permute-start | bytes 1572872 | tf_op jit(solution)/shard_map/ppermute | solution.py:1012
  73.2 17.1 %collective-permute-start.28 = (bf16[4,64,1024]{2,1,0:T(8,128)(2,1)S(1)}, bf16[4,64,1024]{2,1,0:T(8,128)(2,1)S(1)}, u32[]{:S(2)}, u32[]{:S(2)}) collective-permute-start(bf16[4,64,1024]{2,1,0:T(8,128)(2,1)S(1)} %get-tuple-element.83), channel_id=1, source_target_pairs={{0,16},{8,24},{16,0},{24,8},{1,17},{9,25},{17,1},{25,9},{2,18},{10... | collective-permute-start | bytes 1572872 | tf_op jit(solution)/shard_map/ppermute | solution.py:1012
  77.5 21.2 %collective-permute-start.16 = (bf16[4,64,1024]{2,1,0:T(8,128)(2,1)S(1)}, bf16[4,64,1024]{2,1,0:T(8,128)(2,1)S(1)}, u32[]{:S(2)}, u32[]{:S(2)}) collective-permute-start(bf16[4,64,1024]{2,1,0:T(8,128)(2,1)S(1)} %get-tuple-element.67), channel_id=1, source_target_pairs={{0,8},{8,0},{16,24},{24,16},{1,9},{9,1},{17,25},{25,17},{2,10},{10... | collective-permute-start | bytes 1572872 | tf_op jit(solution)/shard_map/ppermute | solution.py:1012
  78.6 20.6 %collective-permute-start.17 = (bf16[4,64,1024]{2,1,0:T(8,128)(2,1)S(1)}, bf16[4,64,1024]{2,1,0:T(8,128)(2,1)S(1)}, u32[]{:S(2)}, u32[]{:S(2)}) collective-permute-start(bf16[4,64,1024]{2,1,0:T(8,128)(2,1)S(1)} %get-tuple-element.68), channel_id=1, source_target_pairs={{0,16},{8,24},{16,0},{24,8},{1,17},{9,25},{17,1},{25,9},{2,18},{10... | collective-permute-start | bytes 1572872 | tf_op jit(solution)/shard_map/ppermute | solution.py:1012
  90.5 13.8 %collective-permute-start.29 = (bf16[2,64,1024]{2,1,0:T(8,128)(2,1)S(1)}, bf16[2,64,1024]{2,1,0:T(8,128)(2,1)S(1)}, u32[]{:S(2)}, u32[]{:S(2)}) collective-permute-start(bf16[2,64,1024]{2,1,0:T(8,128)(2,1)S(1)} %get-tuple-element.86), channel_id=1, source_target_pairs={{0,8},{8,0},{16,24},{24,16},{1,9},{9,1},{17,25},{25,17},{2,10},{10... | collective-permute-start | bytes 786440 | tf_op jit(solution)/shard_map/ppermute | solution.py:1012
  91.6 13.2 %collective-permute-start.30 = (bf16[2,64,1024]{2,1,0:T(8,128)(2,1)S(1)}, bf16[2,64,1024]{2,1,0:T(8,128)(2,1)S(1)}, u32[]{:S(2)}, u32[]{:S(2)}) collective-permute-start(bf16[2,64,1024]{2,1,0:T(8,128)(2,1)S(1)} %get-tuple-element.87), channel_id=1, source_target_pairs={{0,16},{8,24},{16,0},{24,8},{1,17},{9,25},{17,1},{25,9},{2,18},{10... | collective-permute-start | bytes 786440 | tf_op jit(solution)/shard_map/ppermute | solution.py:1012
  99.4 10.9 %collective-permute-start.18 = (bf16[2,64,1024]{2,1,0:T(8,128)(2,1)S(1)}, bf16[2,64,1024]{2,1,0:T(8,128)(2,1)S(1)}, u32[]{:S(2)}, u32[]{:S(2)}) collective-permute-start(bf16[2,64,1024]{2,1,0:T(8,128)(2,1)S(1)} %get-tuple-element.71), channel_id=1, source_target_pairs={{0,8},{8,0},{16,24},{24,16},{1,9},{9,1},{17,25},{25,17},{2,10},{10... | collective-permute-start | bytes 786440 | tf_op jit(solution)/shard_map/ppermute | solution.py:1012
  100.9 9.3 %collective-permute-start.19 = (bf16[2,64,1024]{2,1,0:T(8,128)(2,1)S(1)}, bf16[2,64,1024]{2,1,0:T(8,128)(2,1)S(1)}, u32[]{:S(2)}, u32[]{:S(2)}) collective-permute-start(bf16[2,64,1024]{2,1,0:T(8,128)(2,1)S(1)} %get-tuple-element.72), channel_id=1, source_target_pairs={{0,16},{8,24},{16,0},{24,8},{1,17},{9,25},{17,1},{25,9},{2,18},{10... | collective-permute-start | bytes 786440 | tf_op jit(solution)/shard_map/ppermute | solution.py:1012
  105.1 9.8 %collective-permute-start.31 = (bf16[64,1024]{1,0:T(8,128)(2,1)S(1)}, bf16[64,1024]{1,0:T(8,128)(2,1)S(1)}, u32[]{:S(2)}, u32[]{:S(2)}) collective-permute-start(bf16[64,1024]{1,0:T(8,128)(2,1)S(1)} %get-tuple-element.89), channel_id=1, source_target_pairs={{0,2},{1,3},{2,4},{3,5},{4,6},{5,7},{6,0},{7,1},{8,10},{9,11},{10,... | collective-permute-start | bytes 393224 | tf_op jit(solution)/shard_map/ppermute | solution.py:1019
  106.4 17.9 %collective-permute-start.32 = (bf16[64,1024]{1,0:T(8,128)(2,1)S(1)}, bf16[64,1024]{1,0:T(8,128)(2,1)S(1)}, u32[]{:S(2)}, u32[]{:S(2)}) collective-permute-start(bf16[64,1024]{1,0:T(8,128)(2,1)S(1)} %get-tuple-element.90), channel_id=1, source_target_pairs={{0,4},{1,5},{2,6},{3,7},{4,0},{5,1},{6,2},{7,3},{8,12},{9,13},{10,... | collective-permute-start | bytes 393224 | tf_op jit(solution)/shard_map/ppermute | solution.py:1019
  109.9 15.5 %collective-permute-start.33 = (bf16[64,1024]{1,0:T(8,128)(2,1)S(1)}, bf16[64,1024]{1,0:T(8,128)(2,1)S(1)}, u32[]{:S(2)}, u32[]{:S(2)}) collective-permute-start(bf16[64,1024]{1,0:T(8,128)(2,1)S(1)} %get-tuple-element.91), channel_id=1, source_target_pairs={{0,6},{1,7},{2,0},{3,1},{4,2},{5,3},{6,4},{7,5},{8,14},{9,15},{10,... | collective-permute-start | bytes 393224 | tf_op jit(solution)/shard_map/ppermute | solution.py:1019
  110.4 18.0 %collective-permute-start.20 = (bf16[64,1024]{1,0:T(8,128)(2,1)S(1)}, bf16[64,1024]{1,0:T(8,128)(2,1)S(1)}, u32[]{:S(2)}, u32[]{:S(2)}) collective-permute-start(bf16[64,1024]{1,0:T(8,128)(2,1)S(1)} %get-tuple-element.74), channel_id=1, source_target_pairs={{0,2},{1,3},{2,4},{3,5},{4,6},{5,7},{6,0},{7,1},{8,10},{9,11},{10,... | collective-permute-start | bytes 393224 | tf_op jit(solution)/shard_map/ppermute | solution.py:1019
  112.1 16.4 %collective-permute-start.21 = (bf16[64,1024]{1,0:T(8,128)(2,1)S(1)}, bf16[64,1024]{1,0:T(8,128)(2,1)S(1)}, u32[]{:S(2)}, u32[]{:S(2)}) collective-permute-start(bf16[64,1024]{1,0:T(8,128)(2,1)S(1)} %get-tuple-element.75), channel_id=1, source_target_pairs={{0,4},{1,5},{2,6},{3,7},{4,0},{5,1},{6,2},{7,3},{8,12},{9,13},{10,... | collective-permute-start | bytes 393224 | tf_op jit(solution)/shard_map/ppermute | solution.py:1019
  114.8 15.2 %collective-permute-start.22 = (bf16[64,1024]{1,0:T(8,128)(2,1)S(1)}, bf16[64,1024]{1,0:T(8,128)(2,1)S(1)}, u32[]{:S(2)}, u32[]{:S(2)}) collective-permute-start(bf16[64,1024]{1,0:T(8,128)(2,1)S(1)} %get-tuple-element.76), channel_id=1, source_target_pairs={{0,6},{1,7},{2,0},{3,1},{4,2},{5,3},{6,4},{7,5},{8,14},{9,15},{10,... | collective-permute-start | bytes 393224 | tf_op jit(solution)/shard_map/ppermute | solution.py:1019
  125.5 5.0 %collective-permute-start.34 = (bf16[64,1024]{1,0:T(8,128)(2,1)S(1)}, bf16[64,1024]{1,0:T(8,128)(2,1)S(1)}, u32[]{:S(2)}, u32[]{:S(2)}) collective-permute-start(bf16[64,1024]{1,0:T(8,128)(2,1)S(1)} %collect.3.other_ref.refs_4_), channel_id=1, source_target_pairs={{0,8},{8,0},{16,24},{24,16},{1,9},{9,1},{17,25},{25,17},{2,10},{10... | collective-permute-start | bytes 393224 | tf_op jit(solution)/shard_map/ppermute | solution.py:1012
  126.9 5.0 %collective-permute-start.35 = (bf16[64,1024]{1,0:T(8,128)(2,1)S(1)}, bf16[64,1024]{1,0:T(8,128)(2,1)S(1)}, u32[]{:S(2)}, u32[]{:S(2)}) collective-permute-start(bf16[64,1024]{1,0:T(8,128)(2,1)S(1)} %collect.3.other_ref.refs_4_), channel_id=1, source_target_pairs={{0,16},{8,24},{16,0},{24,8},{1,17},{9,25},{17,1},{25,9},{2,18},{10... | collective-permute-start | bytes 393224 | tf_op jit(solution)/shard_map/ppermute | solution.py:1012
  132.0 10.8 %collective-permute-start.38 = (bf16[144,1024]{1,0:T(8,128)(2,1)S(1)}, bf16[144,1024]{1,0:T(8,128)(2,1)S(1)}, u32[]{:S(2)}, u32[]{:S(2)}) collective-permute-start(bf16[144,1024]{1,0:T(8,128)(2,1)S(1)} %get-tuple-element.93), channel_id=1, source_target_pairs={{0,24},{8,16},{16,8},{24,0},{1,25},{9,17},{17,9},{25,1},{2,26},{10... | collective-permute-start | bytes 884744 | tf_op jit(solution)/shard_map/ppermute | solution.py:1012
  133.6 9.2 %collective-permute-start.36 = (bf16[80,1024]{1,0:T(8,128)(2,1)S(1)}, bf16[80,1024]{1,0:T(8,128)(2,1)S(1)}, u32[]{:S(2)}, u32[]{:S(2)}) collective-permute-start(bf16[80,1024]{1,0:T(8,128)(2,1)S(1)} %get-tuple-element.92.refs_0_), channel_id=1, source_target_pairs={{0,8},{8,0},{16,24},{24,16},{1,9},{9,1},{17,25},{25,17},{2,10},{10... | collective-permute-start | bytes 491528 | tf_op jit(solution)/shard_map/ppermute | solution.py:1012
  135.0 7.8 %collective-permute-start.37 = (bf16[80,1024]{1,0:T(8,128)(2,1)S(1)}, bf16[80,1024]{1,0:T(8,128)(2,1)S(1)}, u32[]{:S(2)}, u32[]{:S(2)}) collective-permute-start(bf16[80,1024]{1,0:T(8,128)(2,1)S(1)} %get-tuple-element.92.refs_0_), channel_id=1, source_target_pairs={{0,16},{8,24},{16,0},{24,8},{1,17},{9,25},{17,1},{25,9},{2,18},{10... | collective-permute-start | bytes 491528 | tf_op jit(solution)/shard_map/ppermute | solution.py:1012
  (18 other events, 127.6 us)
